TPU v7x, 32 devices: a whole 2x2x4 slice. The times are simulated.
32 devices in a mesh: dp: 8 (over y, x, core), tm: 4 (over z).
Axes of the slice: x: 2, y: 2, z: 4, core: 2. Of those that a mesh axis runs over, the one named last changes fastest.
Arguments:
- feats: bfloat16 [24576, 512], P(('dp', 'tm')), may hold values from -40 to 40, as said below
- codes: int32 [8, 2, 1536], P('dp', None, 'tm'), may hold values from 0 to 1023, as said below
- conv_weight: bfloat16 [2048, 512], replicated, may hold values from -0.125 to 0.125
- conv_bias: float32 [512], replicated, may hold values from -3 to 3
- proj_weight: bfloat16 [512, 256], replicated, may hold values from -0.25 to 0.25
- codebooks: bfloat16 [2, 1024, 256], replicated, may hold values from -4.1875 to 4.1875
Outputs:
- feat_grad: bfloat16 [24576, 512], P(('dp', 'tm'))
- conv_grad: float32 [2048, 512], P(('dp', 'tm'))
- bias_grad: float32 [512], replicated
- proj_grad: float32 [512, 256], replicated
- code_means: bfloat16 [2, 1024, 256], P(None, 'tm')
- code_usage: float32 [2, 1024], P(None, 'tm')
Inputs may be any that keep to these rules, and one draw needn't show every extreme that they name: `feats`: each clip has its own overall scale, and rows vary in scale within a clip. Codes are used with strongly unequal frequencies; on every level some codes occur in no frame.
All inputs are finite; a program needn't handle non-finite values.
Results may differ from a plain program's by a relative error of at most 0.0075.
Values may be sent and summed in bfloat16 or wider, within the bound.
No kernel may reach another device: no remote copies, remote signals or barrier semaphores. Data moves between devices by JAX's collectives and lax.ppermute only.
A program may use at most 64 MiB of HBM per device.

v0:
```python
import jax
import jax.numpy as jnp
from jax import lax
from jax.sharding import PartitionSpec as P


def shifted(block, axis, distance):
    devices = range(lax.axis_size(axis))
    route = [(i - distance, i) for i in devices if i - distance in devices]
    return lax.ppermute(block, axis, route)


def own_codes(whole, per_shard):
    return lax.dynamic_slice_in_dim(whole, lax.axis_index("tm") * per_shard, per_shard, 1)


def shards(feats, codes, conv_weight, conv_bias, proj_weight, codebooks):
    frame_count = feats.shape[0] // 2
    channels = feats.shape[1]
    levels = codebooks.shape[0]
    book_size = codebooks.shape[1]
    devices_all = lax.axis_size("dp") * lax.axis_size("tm")
    total_frames = codes.shape[2] * devices_all
    per_shard = book_size // lax.axis_size("tm")
    left_rows = shifted(feats[-2:], "tm", 1)
    paired = jnp.concatenate([left_rows, feats], 0).reshape(frame_count + 1, 2 * channels)
    unfold = jnp.concatenate([paired[:-1], paired[1:]], 1)
    conv_out = jnp.dot(unfold, conv_weight, preferred_element_type=jnp.float32)
    hidden = (conv_out + conv_bias).astype(jnp.bfloat16)
    latent = jnp.dot(hidden, proj_weight, preferred_element_type=jnp.float32)
    residual = latent
    grad_total = jnp.zeros(latent.shape, jnp.float32)
    sums_list = []
    counts_list = []
    code_ids = lax.broadcasted_iota(jnp.int32, (1, book_size), 1)
    for level_index in range(levels):
        matches = codes[0, level_index][:, None] == code_ids
        onehot = matches.astype(jnp.float32)
        sums_list.append(jnp.dot(onehot.T, residual, precision=lax.Precision.HIGHEST))
        counts_list.append(jnp.sum(onehot, 0))
        chosen = jnp.dot(
            matches.astype(jnp.bfloat16), codebooks[level_index], preferred_element_type=jnp.float32
        )
        residual = residual - chosen
        grad_total = grad_total + residual
    local_sums = jnp.stack(sums_list)
    local_counts = jnp.stack(counts_list)
    time_sums = lax.psum_scatter(
        local_sums.astype(jnp.bfloat16), "tm", scatter_dimension=1, tiled=True
    ).astype(jnp.float32)
    code_sums = lax.psum(time_sums, "dp")
    latent_grad = grad_total.astype(jnp.bfloat16)
    proj_term = jnp.dot(hidden.T, latent_grad, preferred_element_type=jnp.float32)
    hidden_grad = jnp.dot(latent_grad, proj_weight.T, preferred_element_type=jnp.float32).astype(
        jnp.bfloat16
    )
    bias_term = jnp.sum(hidden_grad.astype(jnp.float32), 0)
    next_row = shifted(hidden_grad[:1], "tm", -1)
    extended = jnp.concatenate([hidden_grad, next_row], 0)
    grad_unfold = jnp.dot(extended, conv_weight.T, preferred_element_type=jnp.float32)
    grad_paired = grad_unfold[1:, : 2 * channels] + grad_unfold[:-1, 2 * channels :]
    feat_grad = grad_paired.reshape(2 * frame_count, channels).astype(jnp.bfloat16)
    proj_float = proj_weight.astype(jnp.float32)
    owned_corr = lax.psum_scatter(
        jnp.dot(unfold.T, latent_grad, preferred_element_type=jnp.float32),
        ("dp", "tm"),
        scatter_dimension=0,
        tiled=True,
    )
    conv_sum = jnp.dot(owned_corr, proj_float.T, precision=lax.Precision.HIGHEST)
    whole_counts, proj_sum, bias_sum = lax.psum((local_counts, proj_term, bias_term), ("dp", "tm"))
    code_counts = own_codes(whole_counts, per_shard)
    conv_grad = conv_sum / total_frames
    proj_grad = proj_sum / total_frames
    bias_grad = bias_sum / total_frames
    code_means = (code_sums / jnp.maximum(code_counts, 1.0)[:, :, None]).astype(jnp.bfloat16)
    code_usage = code_counts * (book_size / total_frames)
    return (feat_grad, conv_grad, bias_grad, proj_grad, code_means, code_usage)


def solution(mesh):
    placed = (P(("dp", "tm"), None), P("dp", None, "tm"), P(), P(), P(), P())
    return jax.shard_map(
        shards,
        mesh=mesh,
        in_specs=placed,
        out_specs=(
            P(("dp", "tm"), None),
            P(("dp", "tm"), None),
            P(),
            P(),
            P(None, "tm", None),
            P(None, "tm"),
        ),
        check_vma=False,
    )
```

profile of v0, /device:TPU:0, one launch (start us, length us, event | category | flops | bytes accessed | tf_op | source)
XLA Modules:
  0.0 210.2 jit_solution(13504972369355095866)
XLA Ops:
  8.1 0.9 slice.34
  9.0 4.9 %collective-permute-start = (bf16[2,512]{1,0:T(2,128)(2,1)S(1)}, bf16[2,512]{1,0:T(2,128)(2,1)S(1)}, u32[]{:S(2)}, u32[]{:S(2)}) collective-permute-start(bf16[2,512]{1,0:T(2,128)(2,1)S(1)} %slice.34), channel_id=1, source_target_pairs={{0,1},{1,2},{2,3},{4,5},{5,6},{6,7},{8,9},{9,10},{10,11},{12,13},{... | collective-permute-start | bytes 6152 | tf_op jit(solution)/shard_map/ppermute | solution.py:10
  13.9 0.8 slice_reduce_fusion
  14.7 2.1 %slice.37 = bf16[384,1024]{1,0:T(8,128)(2,1)} reshape(bf16[768,512]{1,0:T(8,128)(2,1)} %param.6) | data formatting | bytes 1572864 | tf_op jit(solution)/shard_map/slice | solution.py:27
  16.8 1.1 pad_maximum_fusion.1
  17.8 2.2 %slice.36 = bf16[384,1024]{1,0:T(8,128)(2,1)} reshape(bf16[768,512]{1,0:T(8,128)(2,1)} %pad_maximum_fusion.1) | data formatting | bytes 1572864 | tf_op jit(solution)/shard_map/slice | solution.py:27
  20.0 1.2 constant_dynamic-update-slice_fusion.1
  21.4 1.0 fusion.7
  22.4 0.1 copy-done.1
  22.5 0.3 fusion.27
  22.8 1.5 fusion.9
  24.3 0.4 fusion.10
  24.8 0.4 fusion.13
  25.2 0.3 copy-done.7
  25.5 1.1 fusion.29
  26.7 2.5 %fusion.8 = bf16[1,1024,256]{2,1,0:T(8,128)(2,1)S(1)} fusion(f32[384,256]{1,0:T(8,128)} %copy-done.7, s32[384]{0:T(512)S(1)} %get-tuple-element.6), kind=kOutput, calls=%fused_computation.15 | convolution fusion | flops 1208614912 | bytes 919040 | tf_op jit(solution)/shard_map/dot_general | solution.py:39
  29.2 1.1 pad_maximum_fusion
  30.4 3.5 %fusion.28 = f32[2048,256]{1,0:T(8,128)} fusion(bf16[384,2048]{1,0:T(8,128)(2,1)} %copy-done.1, bf16[384,256]{1,0:T(8,128)(2,1)S(1)} %fusion.13), kind=kOutput, calls=%fused_computation.49 | convolution fusion | flops 402653184 | bytes 3866624 | tf_op jit(solution)/shard_map/dot_general | solution.py:65
  33.9 0.4 convert_reduce_fusion
  34.3 0.3 convert_reduce_fusion.2
  34.6 1.3 collective-permute-start.1
  35.9 42.1 %all-reduce = (f32[512]{0:T(512)S(1)}, f32[2,1024]{1,0:T(2,128)S(1)}) all-reduce(f32[512]{0:T(512)S(1)} %get-tuple-element.12, f32[2,1024]{1,0:T(2,128)S(1)} %pad_maximum_fusion.2), channel_id=1, replica_groups=mesh['dp'=8,'tm'=4] {'dp','tm'}, use_global_device_ids=true, to_apply=%region_2.0 | all-reduce | flops 2560 | bytes 20480 | tf_op jit(solution)/shard_map/psum | solution.py:71
  78.0 0.6 broadcast_multiply_fusion.1
  78.6 0.6 dynamic-slice_multiply_fusion
  79.2 1.0 fusion.22
  80.2 0.4 fusion
  80.6 1.1 convert_element_type.38
  81.7 85.8 %all-reduce.4.cloned.1.call-done = f32[512,256]{1,0:T(8,128)} async-done(((f32[512,256]{1,0:T(8,128)}), f32[512,256]{1,0:T(8,128)}) %all-reduce.4.cloned.1.call-update) | async-done | bytes 524304 | tf_op jit(solution)/shard_map/psum | solution.py:71
  167.5 1.9 broadcast_multiply_fusion
  169.4 30.6 %all-reduce.5 = f32[2,256,256]{2,1,0:T(8,128)S(1)} all-reduce(bf16[2,256,256]{2,1,0:T(8,128)(2,1)} %reduce-scatter.5.cloned.1.call-done), channel_id=1, replica_groups=mesh['dp'=8,'tm'=4] {'dp'}, use_global_device_ids=true, to_apply=%region_5.0 | all-reduce | flops 131072 | bytes 786432 | tf_op jit(solution)/shard_map/psum | solution.py:51
  200.0 0.8 divide_convert_fusion
  200.9 1.9 convolution_multiply_fusion
  (27 shorter events, 0.3 us)
Async XLA Ops:
  8.0 13.3 %copy-start = (bf16[2048,512]{1,0:T(8,128)(2,1)S(1)}, bf16[2048,512]{1,0:T(8,128)(2,1)}, u32[]{:S(2)}) copy-start(bf16[2048,512]{1,0:T(8,128)(2,1)} %param.8) | copy-start | bytes 6291460
  8.0 8.8 %copy-start.2 = (bf16[768,512]{1,0:T(8,128)(2,1)S(1)}, bf16[768,512]{1,0:T(8,128)(2,1)}, u32[]{:S(2)}) copy-start(bf16[768,512]{1,0:T(8,128)(2,1)} %param.6) | copy-start | bytes 2359300
  8.0 159.5 %all-reduce.4.cloned.1.call-start = ((), (), s32[]{:S(2)}) async-start(), calls=%async_computation.3 | async-start | bytes 1048576 | tf_op jit(solution)/shard_map/psum | solution.py:71
  9.0 7.8 %collective-permute-start = (bf16[2,512]{1,0:T(2,128)(2,1)S(1)}, bf16[2,512]{1,0:T(2,128)(2,1)S(1)}, u32[]{:S(2)}, u32[]{:S(2)}) collective-permute-start(bf16[2,512]{1,0:T(2,128)(2,1)S(1)} %slice.34), channel_id=1, source_target_pairs={{0,1},{1,2},{2,3},{4,5},{5,6},{6,7},{8,9},{9,10},{10,11},{12,13},{... | collective-permute-start | bytes 6152 | tf_op jit(solution)/shard_map/ppermute | solution.py:10
  17.8 3.4 %copy-start.3 = (bf16[384,1024]{1,0:T(8,128)(2,1)S(1)}, bf16[384,1024]{1,0:T(8,128)(2,1)}, u32[]{:S(2)}) copy-start(bf16[384,1024]{1,0:T(8,128)(2,1)} %slice.37) | copy-start | bytes 2359300
  20.0 1.3 copy-start.6
  21.4 1.2 copy-start.1
  21.4 1.1 copy-start.4
  22.5 1.8 copy-start.5
  24.8 0.7 copy-start.7
  26.7 142.7 %reduce-scatter.5.cloned.1.call-start = ((), (), s32[]{:S(2)}) async-start(), calls=%async_computation.4 | async-start | bytes 1310720 | tf_op jit(solution)/shard_map/reduce_scatter | solution.py:48
  30.3 170.6 %reduce-scatter.3.cloned.1.call-start = ((), (), s32[]{:S(2)}) async-start(), calls=%async_computation.2 | async-start | bytes 2162688 | tf_op jit(solution)/shard_map/reduce_scatter | solution.py:64
  34.6 44.6 %collective-permute-start.1 = (bf16[1,512]{1,0:T(2,128)(2,1)S(1)}, bf16[1,512]{1,0:T(2,128)(2,1)S(1)}, u32[]{:S(2)}, u32[]{:S(2)}) collective-permute-start(bf16[1,512]{1,0:T(2,128)(2,1)S(1)} %slice.45), channel_id=1, source_target_pairs={{1,0},{2,1},{3,2},{5,4},{6,5},{7,6},{9,8},{10,9},{11,10},{13,12},{... | collective-permute-start | bytes 3080 | tf_op jit(solution)/shard_map/ppermute | solution.py:10
Sparse Core Ops, SparseCore 0:
  26.8 140.6 all-reduce.3
Sparse Core Ops, SparseCore 1:
  30.4 28.5 reduce-scatter.4
  61.1 137.5 reduce-scatter.2
where the time goes:
time: 211 us; the launch traced here: 210 us
  waiting for transfers between devices  85.8 us (41%)
  blocking collectives  72.7 us (34%)
  between operations  15.7 us (7%)
  matrix products  14 us (7%)
  local copies, waits for them, and re-layouts  8.87 us (4%)
  other arithmetic  6.76 us (3%)
  starting transfers between devices  6.33 us (3%)
    psum x1, waiting for transfers between devices, shards(): lax.psum((local_counts, proj_term, bias_term), ('dp', 'tm'))  85.8 us
    psum x1, blocking collectives, shards(): lax.psum((local_counts, proj_term, bias_term), ('dp', 'tm'))  42.1 us
    psum x1, blocking collectives, shards(): code_sums = lax.psum(time_sums, 'dp')  30.6 us
    ppermute x2, starting transfers between devices, shifted(): return lax.ppermute(block, axis, route)  6.21 us
    slice x2, local copies, waits for them, and re-layouts, shards(): unfold = jnp.concatenate([paired[:-1], paired[1:]], 1)  4.31 us
  transfers between devices with their start and end apart: 5, of which 1 were waited for; matrix products, arithmetic and copies ran while one was open for 8% of the time, Pallas kernels for 0%

commit v1 on v0

v1 whole, which is shorter than its diff:
```python
import functools

import jax
import jax.numpy as jnp
from jax import lax
from jax.experimental import pallas as pl
from jax.experimental.pallas import tpu as pltpu
from jax.sharding import PartitionSpec as P

BF16 = jnp.bfloat16
F32 = jnp.float32
LANES = 128
VMEM_LIMIT = 48 * 1024 * 1024


def log2(value):
    assert value & (value - 1) == 0
    return value.bit_length() - 1


def nn(a, b):
    return lax.dot_general(a, b, (((1,), (0,)), ((), ())), preferred_element_type=F32)


def nt(a, b):
    return lax.dot_general(a, b, (((1,), (1,)), ((), ())), preferred_element_type=F32)


def call(body, out_shape, args, scalars=0, scratch=(), aliases=None, flops=0):
    specs = [pl.BlockSpec(memory_space=pltpu.SMEM)] * scalars
    specs += [pl.BlockSpec(memory_space=pltpu.VMEM)] * (len(args) - scalars)
    many = isinstance(out_shape, (list, tuple))
    out_specs = [pl.BlockSpec(memory_space=pltpu.VMEM)] * len(out_shape) if many else pl.BlockSpec(
        memory_space=pltpu.VMEM)
    moved = sum(a.size * a.dtype.itemsize for a in args)
    return pl.pallas_call(
        body,
        out_shape=out_shape,
        in_specs=specs,
        out_specs=out_specs,
        scratch_shapes=list(scratch),
        input_output_aliases=aliases or {},
        compiler_params=pltpu.CompilerParams(vmem_limit_bytes=VMEM_LIMIT),
        cost_estimate=pl.CostEstimate(flops=flops, bytes_accessed=moved, transcendentals=0),
    )(*args)


def shape(dims, dtype):
    return jax.ShapeDtypeStruct(dims, dtype)


def digits_of(value):
    high = value.astype(BF16).astype(F32)
    rest = value - high
    middle = rest.astype(BF16).astype(F32)
    low = (rest - middle).astype(BF16).astype(F32)
    return high, middle, low


def one_hot(codes, axis_codes, first, count):
    frames = codes.shape[1 - axis_codes]
    dims = (count, frames) if axis_codes == 0 else (frames, count)
    places = lax.broadcasted_iota(jnp.int32, dims, axis_codes) + first
    return jnp.where(codes == places, 1.0, 0.0).astype(BF16)


def local_kernel(feats, weight, bias, codes, books, unfold, conv, chosen, wide):
    rows, channels = feats.shape
    frames = rows // 2
    for j in range(channels // LANES):
        wide[j, 0:8, :] = jnp.zeros((8, LANES), F32)
        wide[j, 8:, :] = feats[:, j * LANES:(j + 1) * LANES].astype(F32)
        for tap in range(4):
            start = tap * channels + j * LANES
            unfold[:, start:start + LANES] = wide[j, pl.ds(6 + tap, frames, stride=2), :].astype(BF16)
    conv[...] = nn(unfold[...], weight[...]) + bias[...]
    for level in range(books.shape[0]):
        matches = one_hot(codes[:, level:level + 1], 1, 0, books.shape[1])
        chosen[level] = nn(matches, books[level]).astype(BF16)


def pack_extras(block, values, stride):
    block[...] = jnp.zeros(block.shape, F32)
    for digit, part in enumerate(digits_of(values)):
        for j in range(values.shape[1] // LANES):
            block[digit * stride + j:digit * stride + j + 1, :] = part[:, j * LANES:(j + 1) * LANES]


def forward_kernel(split, place, halo, unfold_in, conv, chosen, weight, proj, codes,
                   unfold, latent_out, hidden_grad, send, keep, corr, block):
    frames, width = unfold.shape
    half = width // 2
    levels = chosen.shape[0]
    dz = proj.shape[1]
    row = lax.broadcasted_iota(jnp.int32, (16, half), 0)
    left = jnp.concatenate([halo[0:1, :], halo[1:2, :]], 1).astype(F32)
    head = jnp.where(row == 0, jnp.broadcast_to(left, (16, half)), 0.0)
    unfold[0:16, 0:half] = (unfold_in[0:16, 0:half].astype(F32) + head).astype(BF16)
    fix = nn(head.astype(BF16), weight[0:half, :])
    hidden = jnp.concatenate([conv[0:16, :] + fix, conv[16:, :]], 0).astype(BF16)
    latent = nn(hidden, proj[...])
    latent_out[0:frames, :] = latent.astype(BF16)
    residual = latent
    total = jnp.zeros_like(latent)
    for level in range(levels):
        residual = residual - chosen[level].astype(F32)
        total = total + residual
    latent_grad = total.astype(BF16)
    back = nt(latent_grad, proj[...]).astype(BF16)
    hidden_grad[...] = back
    flipped = jnp.transpose(latent_grad.astype(F32)).astype(BF16)
    pieces_a = width // LANES
    chunk = 512
    for start in range(0, width, chunk):
        product = nn(flipped, unfold[:, start:start + chunk])
        for j in range(chunk // LANES):
            corr[start // LANES + j] = product[:, j * LANES:(j + 1) * LANES]
    product = nn(flipped, hidden)
    pieces_c = hidden.shape[1] // LANES
    for j in range(pieces_c):
        corr[pieces_a + j] = product[:, j * LANES:(j + 1) * LANES]
    at = 0
    for first, count, bits, halved in place:
        shown = count // 2 if halved else count
        for position in range(shown):
            rest = 0
            others = bits[1:] if halved else bits
            for k, bit in enumerate(others):
                rest += ((position >> (len(others) - 1 - k)) & 1) << bit
            where_send = first + rest
            where_keep = first + rest
            if halved:
                where_send = where_send + (1 - split[0]) * (1 << bits[0])
                where_keep = where_keep + split[0] * (1 << bits[0])
            send[at * dz:(at + 1) * dz, :] = corr[where_send].astype(BF16)
            keep[at * dz:(at + 1) * dz, :] = corr[where_keep]
            at += 1
    extra = block.shape[0]
    pack_extras(block, jnp.sum(back.astype(F32), 0, keepdims=True), extra // 4)
    send[at * dz:at * dz + extra, :] = block[...].astype(BF16)
    keep[at * dz:at * dz + extra, :] = block[...]
    block_codes = codes[...]
    rows = []
    for level in range(levels):
        for part in (block_codes[level:level + 1] >> 8, block_codes[level:level + 1] & 255):
            for start in range(0, frames, dz):
                piece = part[:, start:start + dz].astype(F32)
                if piece.shape[1] < dz:
                    piece = jnp.concatenate([piece, jnp.zeros((1, dz - piece.shape[1]), F32)], 1)
                rows.append(piece)
    rows.append(jnp.zeros((latent_out.shape[0] - frames - len(rows), dz), F32))
    latent_out[frames:, :] = jnp.concatenate(rows, 0).astype(BF16)


def step_kernel(halves, extra, bit, got, kept, send, keep):
    at_in = 0
    at_out = 0
    for rows, halved in halves:
        if halved:
            half = rows // 2
            away = pl.multiple_of(at_in + (1 - bit[0]) * half, 16)
            home = pl.multiple_of(at_in + bit[0] * half, 16)
            send[at_out:at_out + half, :] = (
                kept[pl.ds(away, half), :] + got[pl.ds(away, half), :].astype(F32)).astype(BF16)
            keep[at_out:at_out + half, :] = kept[pl.ds(home, half), :] + got[pl.ds(home, half), :].astype(F32)
            at_out += half
        else:
            total = (kept[at_in:at_in + rows, :] + got[at_in:at_in + rows, :].astype(F32)).astype(BF16)
            send[at_out:at_out + rows, :] = total
            keep[at_out:at_out + rows, :] = total.astype(F32)
            at_out += rows
        at_in += rows
    stride = extra // 4
    mine = kept[at_in:at_in + extra, :]
    theirs = got[at_in:at_in + extra, :].astype(F32)
    value = ((mine[0:stride] + mine[stride:2 * stride]) + mine[2 * stride:3 * stride]) + (
        (theirs[0:stride] + theirs[stride:2 * stride]) + theirs[2 * stride:3 * stride])
    parts = digits_of(value)
    block = jnp.concatenate(list(parts) + [jnp.zeros_like(value)], 0)
    send[at_out:at_out + extra, :] = block.astype(BF16)
    keep[at_out:at_out + extra, :] = block


def feat_kernel(grad, after, weight, out, wide, inter):
    frames, channels = grad.shape
    half = weight.shape[0] // 2
    wide[0:frames, :] = grad[...].astype(F32)
    wide[frames:, :] = jnp.broadcast_to(after[0:1, :].astype(F32), (8, channels))
    ahead = wide[pl.ds(1, frames), :].astype(BF16)
    for parity in range(2):
        rows = pl.ds(parity * (half // 2), half // 2)
        rows_after = pl.ds(half + parity * (half // 2), half // 2)
        both = nt(ahead, weight[rows, :]) + nt(grad[...], weight[rows_after, :])
        for j in range(channels // LANES):
            inter[j, pl.ds(parity, frames, stride=2), :] = both[:, j * LANES:(j + 1) * LANES]
    for j in range(channels // LANES):
        out[:, j * LANES:(j + 1) * LANES] = inter[j].astype(BF16)


def sums_kernel(frames, count_blocks, info, *refs):
    blocks, books, send, keep = refs[:count_blocks], refs[-3], refs[-2], refs[-1]
    levels, size, dz = books.shape
    own = send.shape[0] - 16
    first = info[1]
    sums = [jnp.zeros((own, dz), F32) for _ in range(levels)]
    counts = [jnp.zeros((8, own), F32) for _ in range(levels)]
    pairs = {}
    per = -(-frames // dz)
    ones = jnp.ones((8, frames), BF16)
    for ref in blocks:
        digits = ref[frames:, :].astype(F32)
        latent = ref[0:frames, :]
        mine = []
        every = []
        for level in range(levels):
            parts = []
            for digit in range(2):
                base = (level * 2 + digit) * per
                row = jnp.concatenate([digits[base + j:base + j + 1, :] for j in range(per)], 1)[:, :frames]
                parts.append(row)
            codes = (parts[0] * 256.0 + parts[1]).astype(jnp.int32)
            mine.append(one_hot(codes, 0, first, own))
            every.append(one_hot(codes, 0, 0, size) if level < levels - 1 else None)
        for level in range(levels):
            sums[level] = sums[level] + nn(mine[level], latent)
            counts[level] = counts[level] + nt(ones, mine[level])
            for earlier in range(level):
                product = nt(mine[level], every[earlier])
                key = (level, earlier)
                pairs[key] = pairs[key] + product if key in pairs else product
    for (level, earlier), table in pairs.items():
        high = jnp.floor(table * (1.0 / 256.0)) * 256.0
        low = table - high
        sums[level] = sums[level] - nn(high.astype(BF16), books[earlier]) - nn(low.astype(BF16), books[earlier])
    bit = info[0]
    for out, chosen in ((send, 1 - bit), (keep, bit)):
        value = jnp.where(chosen == 1, sums[1], sums[0])
        count = jnp.where(chosen == 1, counts[1], counts[0])
        out[0:own, :] = value.astype(out.dtype)
        out[own:, :] = count_rows(count[0:1], dz).astype(out.dtype)


def count_rows(count, width):
    high = jnp.floor(count * (1.0 / 65536.0))
    rest = count - high * 65536.0
    middle = jnp.floor(rest * (1.0 / 256.0))
    low = rest - middle * 256.0
    block = jnp.concatenate([high, middle, low, jnp.zeros((13, count.shape[1]), F32)], 0)
    if count.shape[1] < width:
        block = jnp.concatenate([block, jnp.zeros((16, width - count.shape[1]), F32)], 1)
    return block


def count_of(block, own):
    return (block[0:1] * 65536.0 + block[1:2] * 256.0 + block[2:3])[:, :own]


def sums_step_kernel(got, kept, out):
    own = out.shape[0] - 16
    out[0:own, :] = (kept[0:own, :].astype(F32) + got[0:own, :].astype(F32)).astype(BF16)
    mine = kept[own:, :].astype(F32)
    theirs = got[own:, :].astype(F32)
    out[own:, :] = count_rows(count_of(mine, own) + count_of(theirs, own), out.shape[1]).astype(BF16)


def means_kernel(got, kept, out):
    own = out.shape[0] - 16
    mine = kept[own:, :].astype(F32)
    theirs = got[own:, :].astype(F32)
    count = count_of(mine, own) + count_of(theirs, own)
    square = (own, own)
    same = lax.broadcasted_iota(jnp.int32, square, 0) == lax.broadcasted_iota(jnp.int32, square, 1)
    tall = jnp.sum(jnp.where(same, jnp.broadcast_to(count, square), 0.0), 1, keepdims=True)
    total = kept[0:own, :].astype(F32) + got[0:own, :].astype(F32)
    out[0:own, :] = (total / jnp.maximum(tall, 1.0)).astype(BF16)
    out[own:, :] = count_rows(count, out.shape[1]).astype(BF16)


def means_out_kernel(scale, bit, mine, theirs, means, usage):
    own = mine.shape[0] - 16
    means[bit[0]] = mine[0:own, :]
    means[1 - bit[0]] = theirs[0:own, :]
    first = count_of(mine[own:, :].astype(F32), own) * scale
    second = count_of(theirs[own:, :].astype(F32), own) * scale
    swap = bit[0] == 1
    usage[0:1, :] = jnp.where(swap, second, first)
    usage[1:2, :] = jnp.where(swap, first, second)


def conv_out_kernel(total_frames, info, got, kept, proj, out, wide):
    rows = out.shape[0]
    corr = kept[...] + got[...].astype(F32)
    flipped = jnp.transpose(corr)
    high = flipped.astype(BF16)
    low = (flipped - high.astype(F32)).astype(BF16)
    wide[...] = (nt(high, proj[...]) + nt(low, proj[...])) * (1.0 / total_frames)
    start = info[0]
    if rows % 8 == 0:
        out[...] = wide[pl.ds(pl.multiple_of(start, 8), rows), :]
    else:
        taken = wide[0:rows, :]
        for other in range(rows, wide.shape[0], rows):
            taken = jnp.where(start == other, wide[other:other + rows, :], taken)
        out[...] = taken


def proj_out_kernel(total_frames, dz, order, refs_count, info, *refs):
    parts, out = refs[:refs_count], refs[-1]
    scale = 1.0 / total_frames
    for j, (ref, places) in enumerate(zip(parts, order)):
        for k, index in enumerate(places):
            start = pl.multiple_of(info[index] * LANES, LANES)
            out[pl.ds(start, LANES), :] = jnp.transpose(ref[k * dz:(k + 1) * dz, :].astype(F32)) * scale


def shifted(block, axis, distance):
    devices = range(lax.axis_size(axis))
    route = [(i - distance, i) for i in devices if i - distance in devices]
    return lax.ppermute(block, axis, route)


def swapped(block, axis, bit):
    route = [(i, i ^ (1 << bit)) for i in range(lax.axis_size(axis))]
    return lax.ppermute(block, axis, route)


def shards(feats, codes, conv_weight, conv_bias, proj_weight, codebooks):
    dp, tm = lax.axis_size("dp"), lax.axis_size("tm")
    rows_in, channels = feats.shape
    frames = rows_in // 2
    levels, book_size, dz = codebooks.shape
    width = conv_weight.shape[0]
    total_frames = frames * dp * tm
    per_shard = book_size // tm
    dp_bits, tm_bits = log2(dp), log2(tm)
    at_dp, at_tm = lax.axis_index("dp"), lax.axis_index("tm")
    me = at_dp * tm + at_tm

    exchanges = [("dp", b, b + tm_bits) for b in range(dp_bits)]
    exchanges += [("tm", b, b) for b in reversed(range(tm_bits))]
    owner_bits = dp_bits + tm_bits
    pieces_a = width // LANES
    under = max(owner_bits - log2(pieces_a), 0)
    pieces_c = channels // LANES
    c_bits = min(log2(pieces_c), 2, dp_bits)
    a_split = [bit - under if bit >= under else None for _, _, bit in exchanges]
    c_split = [log2(pieces_c) - 1 - k if k < c_bits else None for k in range(len(exchanges))]

    def order_of(split, count):
        used = [b for b in split if b is not None]
        rest = [b for b in reversed(range(log2(count))) if b not in used]
        return used + rest

    order_a, order_c = order_of(a_split, pieces_a), order_of(c_split, pieces_c)

    def bit_of(axis, b):
        return ((at_dp if axis == "dp" else at_tm) >> b) & 1

    def bits_array(*values):
        return jnp.stack([jnp.asarray(v, jnp.int32) for v in values])

    halo = shifted(feats[-2:], "tm", 1)
    codes = codes[0]
    codes_tall = codes.T
    unfold, conv, chosen = call(
        local_kernel,
        [shape((frames, width), BF16), shape((frames, channels), F32), shape((levels, frames, dz), BF16)],
        [feats, conv_weight, conv_bias[None, :], codes_tall, codebooks],
        scratch=[pltpu.VMEM((channels // LANES, rows_in + 8, LANES), F32)],
        flops=2 * frames * (width * channels + levels * book_size * dz),
    )

    extra = 4 * (-(-channels // LANES // 8) * 8)
    first_a = a_split[0] is not None
    first_c = c_split[0] is not None
    plan = [(0, pieces_a, order_a, first_a), (pieces_a, pieces_c, order_c, first_c)]
    now_a = pieces_a // 2 if first_a else pieces_a
    now_c = pieces_c // 2 if first_c else pieces_c
    sent_rows = (now_a + now_c) * dz + extra
    code_rows = -(-(levels * 2 * -(-frames // dz)) // 16) * 16
    axis, b, _ = exchanges[0]
    _, latent, hidden_grad, send, keep = call(
        lambda split, *refs: forward_kernel(split, plan, *refs),
        [shape((frames, width), BF16), shape((frames + code_rows, dz), BF16), shape((frames, channels), BF16),
         shape((sent_rows, LANES), BF16), shape((sent_rows, LANES), F32)],
        [bits_array(bit_of(axis, b)), halo, unfold, conv, chosen, conv_weight, proj_weight, codes],
        scalars=1,
        scratch=[pltpu.VMEM((pieces_a + pieces_c, dz, LANES), F32), pltpu.VMEM((extra, LANES), F32)],
        aliases={2: 0},
        flops=2 * frames * (width * dz + 3 * channels * dz),
    )

    got = swapped(send, axis, b)
    blocks = [latent]
    for distance in range(1, tm):
        blocks.append(lax.ppermute(latent, "tm", [(i, (i + distance) % tm) for i in range(tm)]))
    after = shifted(hidden_grad[:16], "tm", -1)
    feat_grad = call(
        feat_kernel,
        shape((rows_in, channels), BF16),
        [hidden_grad, after, conv_weight],
        scratch=[pltpu.VMEM((frames + 8, channels), F32), pltpu.VMEM((channels // LANES, rows_in, LANES), F32)],
        flops=2 * frames * width * channels,
    )

    for k in range(1, len(exchanges)):
        axis, b, _ = exchanges[k]
        halves = [(now_a * dz, a_split[k] is not None), (now_c * dz, c_split[k] is not None)]
        now_a = now_a // 2 if halves[0][1] else now_a
        now_c = now_c // 2 if halves[1][1] else now_c
        sent_rows = (now_a + now_c) * dz + extra
        send, keep = call(
            functools.partial(step_kernel, halves, extra),
            [shape((sent_rows, LANES), BF16), shape((sent_rows, LANES), F32)],
            [bits_array(bit_of(axis, b)), got, keep],
            scalars=1,
        )
        got = swapped(send, axis, b)
    assert now_a == 1
    mid_c = now_a * dz
    mid_x = mid_c + now_c * dz

    owner_rows = width // (dp * tm)
    conv_grad = call(
        functools.partial(conv_out_kernel, total_frames),
        shape((owner_rows, channels), F32),
        [bits_array((me * owner_rows) % LANES), got[:mid_c], keep[:mid_c], proj_weight],
        scalars=1,
        scratch=[pltpu.VMEM((LANES, channels), F32)],
    )
    parts = [(got[mid_c:mid_x].astype(F32) + keep[mid_c:mid_x]).astype(BF16)]
    value = got[mid_x:].astype(F32), keep[mid_x:]
    stride = extra // 4
    bias_sum = sum((v[:stride] + v[stride:2 * stride]) + v[2 * stride:3 * stride] for v in value)
    bias_grad = bias_sum[:channels // LANES].reshape(channels) / total_frames

    names = [[0]] if now_c == 1 else [list(range(now_c))]
    masks = [0]
    for k in reversed(range(c_bits)):
        axis, b, _ = exchanges[k]
        arrived = [swapped(part, axis, b) for part in parts]
        parts = parts + arrived
        masks = masks + [m | (1 << k) for m in masks]
    own_piece = 0
    for k in range(c_bits):
        axis, b, _ = exchanges[k]
        own_piece = own_piece + (bit_of(axis, b) << c_split[k])
    places, order = [], []
    for m in masks:
        flip = sum(1 << c_split[k] for k in range(c_bits) if m >> k & 1)
        group = []
        for inner in range(now_c):
            group.append(len(places))
            places.append((own_piece ^ flip) + inner)
        order.append(group)
    proj_grad = call(
        functools.partial(proj_out_kernel, total_frames, dz, order, len(parts)),
        shape((channels, dz), F32),
        [bits_array(*places)] + parts,
        scalars=1,
    )

    core = bit_of("dp", 0)
    send_sums, keep_sums = call(
        functools.partial(sums_kernel, frames, len(blocks)),
        [shape((per_shard + 16, dz), BF16), shape((per_shard + 16, dz), F32)],
        [bits_array(core, at_tm * per_shard)] + blocks + [codebooks],
        scalars=1,
        flops=2 * len(blocks) * frames * per_shard * (book_size + 2 * dz),
    )
    for b in range(dp_bits):
        got_sums = swapped(send_sums, "dp", b)
        last = b == dp_bits - 1
        send_sums = call(
            means_kernel if last else sums_step_kernel,
            shape((per_shard + 16, dz), BF16),
            [got_sums, keep_sums],
        )
        keep_sums = send_sums
    other = swapped(send_sums, "dp", 0)
    code_means, code_usage = call(
        functools.partial(means_out_kernel, book_size / total_frames),
        [shape((levels, per_shard, dz), BF16), shape((levels, per_shard), F32)],
        [bits_array(core), send_sums, other],
        scalars=1,
    )
    return feat_grad, conv_grad, bias_grad, proj_grad, code_means, code_usage


def solution(mesh):
    placed = (P(("dp", "tm"), None), P("dp", None, "tm"), P(), P(), P(), P())
    return jax.shard_map(
        shards,
        mesh=mesh,
        in_specs=placed,
        out_specs=(
            P(("dp", "tm"), None),
            P(("dp", "tm"), None),
            P(),
            P(),
            P(None, "tm", None),
            P(None, "tm"),
        ),
        check_vma=False,
    )
```

time: 211 us -> 87 us (0.41)
  blocking collectives: 72.7 us -> 0 us
  waiting for transfers between devices: 85.8 us -> 17.6 us
  Pallas kernels: 0 us -> 20.9 us
  starting transfers between devices: 6.33 us -> 26.5 us
  between operations: 15.7 us -> 0.78 us
  matrix products: 14 us -> 0 us
  local copies, waits for them, and re-layouts: 8.87 us -> 19.7 us
  other arithmetic: 6.76 us -> 0.77 us
    psum x1 -> x0, waiting for transfers between devices: 85.8 us -> none  [shards(): lax.psum((local_counts, proj_term, bias_term), ('dp', 'tm'))]
    psum x2 -> x0, blocking collectives: 72.7 us -> none  [the longest x1 42.1 us: shards(): lax.psum((local_counts, proj_term, bias_term), ('dp', 'tm'))]
    pallas_call x0 -> x14, Pallas kernels: none -> 20.9 us  [call(): pl.pallas_call(body, out_shape=out_shape, in_specs=specs, out_specs=out_s...]
    ppermute x0 -> x15, starting transfers between devices: none -> 20.3 us  [the longest x12 14.8 us: swapped(): return lax.ppermute(block, axis, route)]
    ppermute x0 -> x15, waiting for transfers between devices: none -> 17.6 us  [the longest x3 10.3 us: shards(): lax.ppermute(latent, 'tm', [(i, (i + distance) % tm) for i in range(tm)])]
    unnamed x17 -> x50, local copies, waits for them, and re-layouts: 1.69 us -> 18.2 us
    dot_general x11 -> x0, matrix products: 14 us -> none  [the longest x2 4.04 us: shards(): jnp.dot(onehot.T, residual, precision=lax.Precision.HIGHEST)]
    slice x5 -> x3, local copies, waits for them, and re-layouts: 5.98 us -> 0.71 us  [the longest x1 0.71 us: shards(): halo = shifted(feats[-2:], 'tm', 1)]
  transfers between devices with their start and end apart: 5 -> 17, of which waited for: 1 -> 5; matrix products, arithmetic and copies ran while one was open for 8% -> 2% of each run, Pallas kernels for 0% -> 18%
where the time goes in v1:
time: 87 us; the launch traced here: 86.2 us
  starting transfers between devices  26.5 us (30%)
  Pallas kernels  20.9 us (24%)
  local copies, waits for them, and re-layouts  19.7 us (23%)
  waiting for transfers between devices  17.6 us (20%)
    pallas_call x14, Pallas kernels, call(): pl.pallas_call(body, out_shape=out_shape, in_specs=specs, out_specs=out_s...  20.9 us
    unnamed x50, local copies, waits for them, and re-layouts  18.2 us
    ppermute x12, starting transfers between devices, swapped(): return lax.ppermute(block, axis, route)  14.8 us
    ppermute x3, waiting for transfers between devices, shards(): lax.ppermute(latent, 'tm', [(i, (i + distance) % tm) for i in range(tm)])  10.3 us
    ppermute x12, waiting for transfers between devices, swapped(): return lax.ppermute(block, axis, route)  7.26 us
    ppermute x2, starting transfers between devices, shifted(): return lax.ppermute(block, axis, route)  6.2 us
    ppermute x3, starting transfers between devices, shards(): lax.ppermute(latent, 'tm', [(i, (i + distance) % tm) for i in range(tm)])  5.52 us
  transfers between devices with their start and end apart: 17, of which 5 were waited for; matrix products, arithmetic and copies ran while one was open for 2% of the time, Pallas kernels for 18%

profile of v1, /device:TPU:0, one launch (start us, length us, event | category | flops | bytes accessed | tf_op | source)
XLA Modules:
  0.0 86.2 jit_solution(9944549422389033660)
XLA Ops:
  1.3 4.9 %collective-permute-start = (bf16[2,512]{1,0:T(2,128)(2,1)S(1)}, bf16[2,512]{1,0:T(2,128)(2,1)S(1)}, u32[]{:S(2)}, u32[]{:S(2)}) collective-permute-start(bf16[2,512]{1,0:T(2,128)(2,1)S(1)} %slice.46), channel_id=1, source_target_pairs={{0,1},{1,2},{2,3},{4,5},{5,6},{6,7},{8,9},{9,10},{10,11},{12,13},{... | collective-permute-start | bytes 6152 | tf_op jit(solution)/shard_map/ppermute | solution.py:319
  7.1 1.1 %copy-done.21 = bf16[768,512]{1,0:T(8,128)(2,1)S(1)} copy-done((bf16[768,512]{1,0:T(8,128)(2,1)S(1)}, bf16[768,512]{1,0:T(8,128)(2,1)}, u32[]{:S(2)}) %copy-start.21) | copy-done | bytes 786456
  8.2 1.2 %copy-done.22 = bf16[2,1024,256]{2,1,0:T(8,128)(2,1)S(1)} copy-done((bf16[2,1024,256]{2,1,0:T(8,128)(2,1)S(1)}, bf16[2,1024,256]{2,1,0:T(8,128)(2,1)}, u32[]{:S(2)}) %copy-start.22) | copy-done | bytes 1048600
  10.1 3.1 %shard_map.109 = (bf16[384,2048]{1,0:T(8,128)(2,1)S(1)}, f32[384,512]{1,0:T(8,128)S(1)}, bf16[2,384,256]{2,1,0:T(8,128)(2,1)S(1)}) custom-call(bf16[768,512]{1,0:T(8,128)(2,1)S(1)} %copy-done.21, bf16[2048,512]{1,0:T(8,128)(2,1)} %weight.3, f32[1,512]{1,0:T(1,128)S(1)} %bitcast.19, s32[384,2]{1,0:T(8,128)S(1)} %copy.13.codes, ...), custom_call_target="tpu_custom_call" | custom-call | flops 1207959552 | bytes 3937280 | tf_op jit(solution)/shard_map/pallas_call | solution.py:36
  15.5 1.1 %copy-done.3 = f32[384,512]{1,0:T(8,128)S(1)} copy-done((f32[384,512]{1,0:T(8,128)S(1)}, f32[384,512]{1,0:T(8,128)}, u32[]{:S(2)}) %copy-start.3) | copy-done | bytes 786456
  16.6 1.0 %copy-done.9 = bf16[2,384,256]{2,1,0:T(8,128)(2,1)S(1)} copy-done((bf16[2,384,256]{2,1,0:T(8,128)(2,1)S(1)}, bf16[2,384,256]{2,1,0:T(8,128)(2,1)}, u32[]{:S(2)}) %copy-start.9) | copy-done | bytes 393240
  19.0 4.0 %shard_map.110 = (bf16[384,2048]{1,0:T(8,128)(2,1)S(1)}, bf16[400,256]{1,0:T(8,128)(2,1)}, bf16[384,512]{1,0:T(8,128)(2,1)S(1)}, bf16[2592,128]{1,0:T(8,128)(2,1)}, f32[2592,128]{1,0:T(8,128)S(1)}) custom-call(s32[1]{0:T(128)} %bitcast.split.bit, bf16[2,512]{1,0:T(2,128)(2,1)S(1)} %copy-done.20, ...), custom_call_target="tpu_custom_call", output_to_operand_aliasing={{0}: (2, {})} | custom-call | flops 704643072 | bytes 5116932 | tf_op jit(solution)/shard_map/pallas_call | solution.py:36
  23.0 1.6 %collective-permute-start.10 = (bf16[400,256]{1,0:T(8,128)(2,1)}, bf16[400,256]{1,0:T(8,128)(2,1)S(1)}, u32[]{:S(2)}, u32[]{:S(2)}) collective-permute-start(bf16[400,256]{1,0:T(8,128)(2,1)} %get-tuple-element.39.refs_0_), channel_id=1, source_target_pairs={{0,1},{1,2},{2,3},{3,0},{4,5},{5,6},{6,7},{7,4},{8,9},{9,10},{10,1... | collective-permute-start | bytes 614408 | tf_op jit(solution)/shard_map/ppermute | solution.py:396
  24.6 1.0 %collective-permute-start.11 = (bf16[400,256]{1,0:T(8,128)(2,1)}, bf16[400,256]{1,0:T(8,128)(2,1)S(1)}, u32[]{:S(2)}, u32[]{:S(2)}) collective-permute-start(bf16[400,256]{1,0:T(8,128)(2,1)} %get-tuple-element.39.refs_0_), channel_id=1, source_target_pairs={{0,2},{1,3},{2,0},{3,1},{4,6},{5,7},{6,4},{7,5},{8,10},{9,11},{10,... | collective-permute-start | bytes 614408 | tf_op jit(solution)/shard_map/ppermute | solution.py:396
  25.6 2.9 %collective-permute-start.12 = (bf16[400,256]{1,0:T(8,128)(2,1)}, bf16[400,256]{1,0:T(8,128)(2,1)}, u32[]{:S(2)}, u32[]{:S(2)}) collective-permute-start(bf16[400,256]{1,0:T(8,128)(2,1)} %get-tuple-element.39.refs_0_), channel_id=1, source_target_pairs={{0,3},{1,0},{2,1},{3,2},{4,7},{5,4},{6,5},{7,6},{8,11},{9,8},{10,9... | collective-permute-start | bytes 614408 | tf_op jit(solution)/shard_map/ppermute | solution.py:396
  29.5 1.5 %collective-permute-start.3 = (bf16[1312,128]{1,0:T(8,128)(2,1)S(1)}, bf16[1312,128]{1,0:T(8,128)(2,1)S(1)}, u32[]{:S(2)}, u32[]{:S(2)}) collective-permute-start(bf16[1312,128]{1,0:T(8,128)(2,1)S(1)} %get-tuple-element.31), channel_id=1, source_target_pairs={{0,8},{4,12},{8,0},{12,4},{16,24},{20,28},{24,16},{28,20},{1,9},{5... | collective-permute-start | bytes 1007624 | tf_op jit(solution)/shard_map/ppermute | solution.py:324
  31.1 1.9 %collective-permute-done.10.refs_1_ = bf16[400,256]{1,0:T(8,128)(2,1)S(1)} collective-permute-done((bf16[400,256]{1,0:T(8,128)(2,1)}, bf16[400,256]{1,0:T(8,128)(2,1)S(1)}, u32[]{:S(2)}, u32[]{:S(2)}) %collective-permute-start.10) | collective-permute-done | bytes 204832 | tf_op jit(solution)/shard_map/ppermute | solution.py:396
  33.0 8.4 %collective-permute-done.11.refs_2_ = bf16[400,256]{1,0:T(8,128)(2,1)S(1)} collective-permute-done((bf16[400,256]{1,0:T(8,128)(2,1)}, bf16[400,256]{1,0:T(8,128)(2,1)S(1)}, u32[]{:S(2)}, u32[]{:S(2)}) %collective-permute-start.11) | collective-permute-done | bytes 204832 | tf_op jit(solution)/shard_map/ppermute | solution.py:396
  41.4 1.2 %copy-done.23 = bf16[2,1024,256]{2,1,0:T(8,128)(2,1)S(1)} copy-done((bf16[2,1024,256]{2,1,0:T(8,128)(2,1)S(1)}, bf16[2,1024,256]{2,1,0:T(8,128)(2,1)}, u32[]{:S(2)}) %copy-start.23) | copy-done | bytes 1048600
  42.6 4.1 %shard_map.118 = (bf16[272,256]{1,0:T(8,128)(2,1)}, f32[272,256]{1,0:T(8,128)S(1)}) custom-call(s32[2]{0:T(128)S(1)} %pad_add_fusion.1.info, bf16[400,256]{1,0:T(8,128)(2,1)} %get-tuple-element.39.refs_0_, bf16[400,256]{1,0:T(8,128)(2,1)S(1)} %collective-permute-done.10.refs_1_, bf16[400,256]{1,0:T(8,128)(2,1)S(1)} %collective-permute-done.11.refs_2_, ...), custom_call_target="tpu_custom_call" | custom-call | flops 1207959552 | bytes 1867784 | tf_op jit(solution)/shard_map/pallas_call | solution.py:36
  48.2 1.0 %copy-done.11 = bf16[1312,128]{1,0:T(8,128)(2,1)S(1)} copy-done((bf16[1312,128]{1,0:T(8,128)(2,1)S(1)}, bf16[1312,128]{1,0:T(8,128)(2,1)}, u32[]{:S(2)}) %copy-start.11) | copy-done | bytes 335896
  50.7 1.5 %collective-permute-start.4 = (bf16[800,128]{1,0:T(8,128)(2,1)}, bf16[800,128]{1,0:T(8,128)(2,1)S(1)}, u32[]{:S(2)}, u32[]{:S(2)}) collective-permute-start(bf16[800,128]{1,0:T(8,128)(2,1)} %get-tuple-element.33), channel_id=1, source_target_pairs={{0,16},{4,20},{8,24},{12,28},{16,0},{20,4},{24,8},{28,12},{1,17},{... | collective-permute-start | bytes 614408 | tf_op jit(solution)/shard_map/ppermute | solution.py:324
  52.2 1.0 %copy-done.13 = f32[272,256]{1,0:T(8,128)S(1)} copy-done((f32[272,256]{1,0:T(8,128)S(1)}, f32[272,256]{1,0:T(8,128)}, u32[]{:S(2)}) %copy-start.13) | copy-done | bytes 278552
  53.2 1.0 %shard_map.119.kept = bf16[272,256]{1,0:T(8,128)(2,1)S(1)} custom-call(bf16[272,256]{1,0:T(8,128)(2,1)} %collective-permute-done.13.got, f32[272,256]{1,0:T(8,128)S(1)} %copy-done.13), custom_call_target="tpu_custom_call" | custom-call | bytes 417792 | tf_op jit(solution)/shard_map/pallas_call | solution.py:36
  54.1 1.6 %collective-permute-start.14 = (bf16[272,256]{1,0:T(8,128)(2,1)S(1)}, bf16[272,256]{1,0:T(8,128)(2,1)S(1)}, u32[]{:S(2)}, u32[]{:S(2)}) collective-permute-start(bf16[272,256]{1,0:T(8,128)(2,1)S(1)} %shard_map.119.kept), channel_id=1, source_target_pairs={{0,8},{4,12},{8,0},{12,4},{16,24},{20,28},{24,16},{28,20},{1,9},{5... | collective-permute-start | bytes 417800 | tf_op jit(solution)/shard_map/ppermute | solution.py:324
  55.7 4.3 %collective-permute-done.14.got = bf16[272,256]{1,0:T(8,128)(2,1)S(1)} collective-permute-done((bf16[272,256]{1,0:T(8,128)(2,1)S(1)}, bf16[272,256]{1,0:T(8,128)(2,1)S(1)}, u32[]{:S(2)}, u32[]{:S(2)}) %collective-permute-start.14) | collective-permute-done | bytes 139296 | tf_op jit(solution)/shard_map/ppermute | solution.py:324
  60.6 1.0 %copy-done.7 = f32[800,128]{1,0:T(8,128)S(1)} copy-done((f32[800,128]{1,0:T(8,128)S(1)}, f32[800,128]{1,0:T(8,128)}, u32[]{:S(2)}) %copy-start.7) | copy-done | bytes 409624
  62.3 4.0 %collective-permute-start.5 = (bf16[544,128]{1,0:T(8,128)(2,1)}, bf16[544,128]{1,0:T(8,128)(2,1)S(1)}, u32[]{:S(2)}, u32[]{:S(2)}) collective-permute-start(bf16[544,128]{1,0:T(8,128)(2,1)} %get-tuple-element.35), channel_id=1, source_target_pairs={{0,2},{1,3},{2,0},{3,1},{4,6},{5,7},{6,4},{7,5},{8,10},{9,11},{10,... | collective-permute-start | bytes 417800 | tf_op jit(solution)/shard_map/ppermute | solution.py:324
  66.3 1.3 %collective-permute-start.1 = (bf16[16,512]{1,0:T(8,128)(2,1)S(1)}, bf16[16,512]{1,0:T(8,128)(2,1)S(1)}, u32[]{:S(2)}, u32[]{:S(2)}) collective-permute-start(bf16[16,512]{1,0:T(8,128)(2,1)S(1)} %slice.47), channel_id=1, source_target_pairs={{1,0},{2,1},{3,2},{5,4},{6,5},{7,6},{9,8},{10,9},{11,10},{13,12},{... | collective-permute-start | bytes 49160 | tf_op jit(solution)/shard_map/ppermute | solution.py:319
  68.2 0.9 %copy-done.17 = bf16[272,256]{1,0:T(8,128)(2,1)S(1)} copy-done((bf16[272,256]{1,0:T(8,128)(2,1)S(1)}, bf16[272,256]{1,0:T(8,128)(2,1)}, u32[]{:S(2)}) %copy-start.17) | copy-done | bytes 139288
  71.0 4.1 %collective-permute-start.6 = (bf16[544,128]{1,0:T(8,128)(2,1)}, bf16[544,128]{1,0:T(8,128)(2,1)S(1)}, u32[]{:S(2)}, u32[]{:S(2)}) collective-permute-start(bf16[544,128]{1,0:T(8,128)(2,1)} %get-tuple-element.37), channel_id=1, source_target_pairs={{0,1},{1,0},{2,3},{3,2},{4,5},{5,4},{6,7},{7,6},{8,9},{9,8},{10,11... | collective-permute-start | bytes 417800 | tf_op jit(solution)/shard_map/ppermute | solution.py:324
  75.1 2.0 %shard_map.111 = bf16[768,512]{1,0:T(8,128)(2,1)} custom-call(bf16[384,512]{1,0:T(8,128)(2,1)S(1)} %get-tuple-element.28.grad, bf16[16,512]{1,0:T(8,128)(2,1)S(1)} %collective-permute-done.1.after, bf16[2048,512]{1,0:T(8,128)(2,1)S(1)} %copy-done), custom_call_target="tpu_custom_call" | custom-call | flops 805306368 | bytes 2506752 | tf_op jit(solution)/shard_map/pallas_call | solution.py:36
  77.1 1.6 %shard_map.122 = (bf16[2,256,256]{2,1,0:T(8,128)(2,1)}, f32[2,256]{1,0:T(2,128)}) custom-call(s32[1]{0:T(128)} %bitcast.split.bit, bf16[272,256]{1,0:T(8,128)(2,1)S(1)} %shard_map.121.mine, bf16[272,256]{1,0:T(8,128)(2,1)} %collective-permute-done.16.theirs), custom_call_target="tpu_custom_call" | custom-call | bytes 278532 | tf_op jit(solution)/shard_map/pallas_call | solution.py:36
  78.8 1.6 %collective-permute-start.7 = (bf16[256,128]{1,0:T(8,128)(2,1)S(1)}, bf16[256,128]{1,0:T(8,128)(2,1)S(1)}, u32[]{:S(2)}, u32[]{:S(2)}) collective-permute-start(bf16[256,128]{1,0:T(8,128)(2,1)S(1)} %get-tuple-element.44.refs_0_), channel_id=1, source_target_pairs={{0,8},{4,12},{8,0},{12,4},{16,24},{20,28},{24,16},{28,20},{1,9},{5... | collective-permute-start | bytes 196616 | tf_op jit(solution)/shard_map/ppermute | solution.py:324
  80.4 2.8 %collective-permute-done.7.refs_1_ = bf16[256,128]{1,0:T(8,128)(2,1)S(1)} collective-permute-done((bf16[256,128]{1,0:T(8,128)(2,1)S(1)}, bf16[256,128]{1,0:T(8,128)(2,1)S(1)}, u32[]{:S(2)}, u32[]{:S(2)}) %collective-permute-start.7) | collective-permute-done | bytes 65568 | tf_op jit(solution)/shard_map/ppermute | solution.py:324
  83.7 1.0 %shard_map.116 = f32[64,512]{1,0:T(8,128)} custom-call(s32[1]{0:T(128)} %bitcast.4.info, bf16[256,128]{1,0:T(8,128)(2,1)S(1)} %slice.60.got, f32[256,128]{1,0:T(8,128)S(1)} %get-tuple-element.45.kept, bf16[512,256]{1,0:T(8,128)(2,1)S(1)} %copy-done.1), custom_call_target="tpu_custom_call" | custom-call | bytes 458756 | tf_op jit(solution)/shard_map/pallas_call | solution.py:36
  84.7 1.5 %shard_map.117 = f32[512,256]{1,0:T(8,128)} custom-call(s32[4]{0:T(128)S(1)} %pad_add_fusion.info, bf16[256,128]{1,0:T(8,128)(2,1)S(1)} %get-tuple-element.44.refs_0_, bf16[256,128]{1,0:T(8,128)(2,1)S(1)} %collective-permute-done.7.refs_1_, bf16[256,128]{1,0:T(8,128)(2,1)S(1)} %collective-permute-done.8.refs_2_, ...), custom_call_target="tpu_custom_call" | custom-call | bytes 262160 | tf_op jit(solution)/shard_map/pallas_call | solution.py:36
  (76 shorter events, 14.3 us)
Async XLA Ops:
  1.3 13.6 %collective-permute-start = (bf16[2,512]{1,0:T(2,128)(2,1)S(1)}, bf16[2,512]{1,0:T(2,128)(2,1)S(1)}, u32[]{:S(2)}, u32[]{:S(2)}) collective-permute-start(bf16[2,512]{1,0:T(2,128)(2,1)S(1)} %slice.46), channel_id=1, source_target_pairs={{0,1},{1,2},{2,3},{4,5},{5,6},{6,7},{8,9},{9,10},{10,11},{12,13},{... | collective-permute-start | bytes 6152 | tf_op jit(solution)/shard_map/ppermute | solution.py:319
  7.1 1.1 %copy-start.21 = (bf16[768,512]{1,0:T(8,128)(2,1)S(1)}, bf16[768,512]{1,0:T(8,128)(2,1)}, u32[]{:S(2)}) copy-start(bf16[768,512]{1,0:T(8,128)(2,1)} %feats.1) | copy-start | bytes 2359300
  8.2 1.2 %copy-start.22 = (bf16[2,1024,256]{2,1,0:T(8,128)(2,1)S(1)}, bf16[2,1024,256]{2,1,0:T(8,128)(2,1)}, u32[]{:S(2)}) copy-start(bf16[2,1024,256]{2,1,0:T(8,128)(2,1)} %refs_4_.3) | copy-start | bytes 3145732
  10.1 5.3 %copy-start.1 = (bf16[512,256]{1,0:T(8,128)(2,1)S(1)}, bf16[512,256]{1,0:T(8,128)(2,1)}, u32[]{:S(2)}) copy-start(bf16[512,256]{1,0:T(8,128)(2,1)} %proj.1) | copy-start | bytes 786436
  13.3 0.9 %copy-start.2 = (f32[384,512]{1,0:T(8,128)}, f32[384,512]{1,0:T(8,128)S(1)}, u32[]{:S(2)}) copy-start(f32[384,512]{1,0:T(8,128)S(1)} %get-tuple-element.26.refs_2_) | copy-start | bytes 2359300
  15.5 1.1 %copy-start.3 = (f32[384,512]{1,0:T(8,128)S(1)}, f32[384,512]{1,0:T(8,128)}, u32[]{:S(2)}) copy-start(f32[384,512]{1,0:T(8,128)} %copy-done.2) | copy-start | bytes 2359300
  16.6 1.0 %copy-start.9 = (bf16[2,384,256]{2,1,0:T(8,128)(2,1)S(1)}, bf16[2,384,256]{2,1,0:T(8,128)(2,1)}, u32[]{:S(2)}) copy-start(bf16[2,384,256]{2,1,0:T(8,128)(2,1)} %copy-done.8) | copy-start | bytes 1179652
  23.0 5.5 %collective-permute-start.2 = (bf16[2592,128]{1,0:T(8,128)(2,1)}, bf16[2592,128]{1,0:T(8,128)(2,1)S(1)}, u32[]{:S(2)}, u32[]{:S(2)}) collective-permute-start(bf16[2592,128]{1,0:T(8,128)(2,1)} %get-tuple-element.29), channel_id=1, source_target_pairs={{0,4},{4,0},{8,12},{12,8},{16,20},{20,16},{24,28},{28,24},{1,5},{5... | collective-permute-start | bytes 1990664 | tf_op jit(solution)/shard_map/ppermute | solution.py:324
  23.0 10.0 %collective-permute-start.10 = (bf16[400,256]{1,0:T(8,128)(2,1)}, bf16[400,256]{1,0:T(8,128)(2,1)S(1)}, u32[]{:S(2)}, u32[]{:S(2)}) collective-permute-start(bf16[400,256]{1,0:T(8,128)(2,1)} %get-tuple-element.39.refs_0_), channel_id=1, source_target_pairs={{0,1},{1,2},{2,3},{3,0},{4,5},{5,6},{6,7},{7,4},{8,9},{9,10},{10,1... | collective-permute-start | bytes 614408 | tf_op jit(solution)/shard_map/ppermute | solution.py:396
  24.6 16.8 %collective-permute-start.11 = (bf16[400,256]{1,0:T(8,128)(2,1)}, bf16[400,256]{1,0:T(8,128)(2,1)S(1)}, u32[]{:S(2)}, u32[]{:S(2)}) collective-permute-start(bf16[400,256]{1,0:T(8,128)(2,1)} %get-tuple-element.39.refs_0_), channel_id=1, source_target_pairs={{0,2},{1,3},{2,0},{3,1},{4,6},{5,7},{6,4},{7,5},{8,10},{9,11},{10,... | collective-permute-start | bytes 614408 | tf_op jit(solution)/shard_map/ppermute | solution.py:396
  25.6 15.8 %collective-permute-start.12 = (bf16[400,256]{1,0:T(8,128)(2,1)}, bf16[400,256]{1,0:T(8,128)(2,1)}, u32[]{:S(2)}, u32[]{:S(2)}) collective-permute-start(bf16[400,256]{1,0:T(8,128)(2,1)} %get-tuple-element.39.refs_0_), channel_id=1, source_target_pairs={{0,3},{1,0},{2,1},{3,2},{4,7},{5,4},{6,5},{7,6},{8,11},{9,8},{10,9... | collective-permute-start | bytes 614408 | tf_op jit(solution)/shard_map/ppermute | solution.py:396
  28.7 0.8 copy-start.4
  29.5 18.0 %collective-permute-start.3 = (bf16[1312,128]{1,0:T(8,128)(2,1)S(1)}, bf16[1312,128]{1,0:T(8,128)(2,1)S(1)}, u32[]{:S(2)}, u32[]{:S(2)}) collective-permute-start(bf16[1312,128]{1,0:T(8,128)(2,1)S(1)} %get-tuple-element.31), channel_id=1, source_target_pairs={{0,8},{4,12},{8,0},{12,4},{16,24},{20,28},{24,16},{28,20},{1,9},{5... | collective-permute-start | bytes 1007624 | tf_op jit(solution)/shard_map/ppermute | solution.py:324
  31.1 17.1 %copy-start.5 = (f32[1312,128]{1,0:T(8,128)S(1)}, f32[1312,128]{1,0:T(8,128)}, u32[]{:S(2)}) copy-start(f32[1312,128]{1,0:T(8,128)} %copy-done.4) | copy-start | bytes 2015236
  41.4 1.2 %copy-start.23 = (bf16[2,1024,256]{2,1,0:T(8,128)(2,1)S(1)}, bf16[2,1024,256]{2,1,0:T(8,128)(2,1)}, u32[]{:S(2)}) copy-start(bf16[2,1024,256]{2,1,0:T(8,128)(2,1)} %refs_4_.3) | copy-start | bytes 3145732
  47.5 4.7 %collective-permute-start.13 = (bf16[272,256]{1,0:T(8,128)(2,1)}, bf16[272,256]{1,0:T(8,128)(2,1)}, u32[]{:S(2)}, u32[]{:S(2)}) collective-permute-start(bf16[272,256]{1,0:T(8,128)(2,1)} %get-tuple-element.40), channel_id=1, source_target_pairs={{0,4},{4,0},{8,12},{12,8},{16,20},{20,16},{24,28},{28,24},{1,5},{5... | collective-permute-start | bytes 417800 | tf_op jit(solution)/shard_map/ppermute | solution.py:324
  48.2 1.0 %copy-start.11 = (bf16[1312,128]{1,0:T(8,128)(2,1)S(1)}, bf16[1312,128]{1,0:T(8,128)(2,1)}, u32[]{:S(2)}) copy-start(bf16[1312,128]{1,0:T(8,128)(2,1)} %copy-done.10) | copy-start | bytes 1007620
  49.2 25.9 %copy-start = (bf16[2048,512]{1,0:T(8,128)(2,1)S(1)}, bf16[2048,512]{1,0:T(8,128)(2,1)}, u32[]{:S(2)}) copy-start(bf16[2048,512]{1,0:T(8,128)(2,1)} %weight.3) | copy-start | bytes 6291460
  50.7 9.9 %collective-permute-start.4 = (bf16[800,128]{1,0:T(8,128)(2,1)}, bf16[800,128]{1,0:T(8,128)(2,1)S(1)}, u32[]{:S(2)}, u32[]{:S(2)}) collective-permute-start(bf16[800,128]{1,0:T(8,128)(2,1)} %get-tuple-element.33), channel_id=1, source_target_pairs={{0,16},{4,20},{8,24},{12,28},{16,0},{20,4},{24,8},{28,12},{1,17},{... | collective-permute-start | bytes 614408 | tf_op jit(solution)/shard_map/ppermute | solution.py:324
  52.2 1.0 %copy-start.13 = (f32[272,256]{1,0:T(8,128)S(1)}, f32[272,256]{1,0:T(8,128)}, u32[]{:S(2)}) copy-start(f32[272,256]{1,0:T(8,128)} %copy-done.12) | copy-start | bytes 835588
  54.1 5.9 %collective-permute-start.14 = (bf16[272,256]{1,0:T(8,128)(2,1)S(1)}, bf16[272,256]{1,0:T(8,128)(2,1)S(1)}, u32[]{:S(2)}, u32[]{:S(2)}) collective-permute-start(bf16[272,256]{1,0:T(8,128)(2,1)S(1)} %shard_map.119.kept), channel_id=1, source_target_pairs={{0,8},{4,12},{8,0},{12,4},{16,24},{20,28},{24,16},{28,20},{1,9},{5... | collective-permute-start | bytes 417800 | tf_op jit(solution)/shard_map/ppermute | solution.py:324
  60.0 7.5 %collective-permute-start.15 = (bf16[272,256]{1,0:T(8,128)(2,1)S(1)}, bf16[272,256]{1,0:T(8,128)(2,1)S(1)}, u32[]{:S(2)}, u32[]{:S(2)}) collective-permute-start(bf16[272,256]{1,0:T(8,128)(2,1)S(1)} %shard_map.120.kept), channel_id=1, source_target_pairs={{0,16},{4,20},{8,24},{12,28},{16,0},{20,4},{24,8},{28,12},{1,17},{... | collective-permute-start | bytes 417800 | tf_op jit(solution)/shard_map/ppermute | solution.py:324
  60.6 1.0 %copy-start.7 = (f32[800,128]{1,0:T(8,128)S(1)}, f32[800,128]{1,0:T(8,128)}, u32[]{:S(2)}) copy-start(f32[800,128]{1,0:T(8,128)} %copy-done.6) | copy-start | bytes 1228804
  62.3 7.2 %collective-permute-start.5 = (bf16[544,128]{1,0:T(8,128)(2,1)}, bf16[544,128]{1,0:T(8,128)(2,1)S(1)}, u32[]{:S(2)}, u32[]{:S(2)}) collective-permute-start(bf16[544,128]{1,0:T(8,128)(2,1)} %get-tuple-element.35), channel_id=1, source_target_pairs={{0,2},{1,3},{2,0},{3,1},{4,6},{5,7},{6,4},{7,5},{8,10},{9,11},{10,... | collective-permute-start | bytes 417800 | tf_op jit(solution)/shard_map/ppermute | solution.py:324
  66.3 8.8 %collective-permute-start.1 = (bf16[16,512]{1,0:T(8,128)(2,1)S(1)}, bf16[16,512]{1,0:T(8,128)(2,1)S(1)}, u32[]{:S(2)}, u32[]{:S(2)}) collective-permute-start(bf16[16,512]{1,0:T(8,128)(2,1)S(1)} %slice.47), channel_id=1, source_target_pairs={{1,0},{2,1},{3,2},{5,4},{6,5},{7,6},{9,8},{10,9},{11,10},{13,12},{... | collective-permute-start | bytes 49160 | tf_op jit(solution)/shard_map/ppermute | solution.py:319
  68.2 0.9 %copy-start.17 = (bf16[272,256]{1,0:T(8,128)(2,1)S(1)}, bf16[272,256]{1,0:T(8,128)(2,1)}, u32[]{:S(2)}) copy-start(bf16[272,256]{1,0:T(8,128)(2,1)} %copy-done.16) | copy-start | bytes 417796
  69.3 7.8 %collective-permute-start.16 = (bf16[272,256]{1,0:T(8,128)(2,1)S(1)}, bf16[272,256]{1,0:T(8,128)(2,1)}, u32[]{:S(2)}, u32[]{:S(2)}) collective-permute-start(bf16[272,256]{1,0:T(8,128)(2,1)S(1)} %shard_map.121.mine), channel_id=1, source_target_pairs={{0,4},{4,0},{8,12},{12,8},{16,20},{20,16},{24,28},{28,24},{1,5},{5... | collective-permute-start | bytes 417800 | tf_op jit(solution)/shard_map/ppermute | solution.py:324
  71.0 7.8 %collective-permute-start.6 = (bf16[544,128]{1,0:T(8,128)(2,1)}, bf16[544,128]{1,0:T(8,128)(2,1)S(1)}, u32[]{:S(2)}, u32[]{:S(2)}) collective-permute-start(bf16[544,128]{1,0:T(8,128)(2,1)} %get-tuple-element.37), channel_id=1, source_target_pairs={{0,1},{1,0},{2,3},{3,2},{4,5},{5,4},{6,7},{7,6},{8,9},{9,8},{10,11... | collective-permute-start | bytes 417800 | tf_op jit(solution)/shard_map/ppermute | solution.py:324
  75.1 3.7 %copy-start.15 = (f32[544,128]{1,0:T(8,128)S(1)}, f32[544,128]{1,0:T(8,128)}, u32[]{:S(2)}) copy-start(f32[544,128]{1,0:T(8,128)} %copy-done.14) | copy-start | bytes 835588
  78.8 4.3 %collective-permute-start.7 = (bf16[256,128]{1,0:T(8,128)(2,1)S(1)}, bf16[256,128]{1,0:T(8,128)(2,1)S(1)}, u32[]{:S(2)}, u32[]{:S(2)}) collective-permute-start(bf16[256,128]{1,0:T(8,128)(2,1)S(1)} %get-tuple-element.44.refs_0_), channel_id=1, source_target_pairs={{0,8},{4,12},{8,0},{12,4},{16,24},{20,28},{24,16},{28,20},{1,9},{5... | collective-permute-start | bytes 196616 | tf_op jit(solution)/shard_map/ppermute | solution.py:324
  80.3 4.4 %collective-permute-start.8 = (bf16[256,128]{1,0:T(8,128)(2,1)S(1)}, bf16[256,128]{1,0:T(8,128)(2,1)S(1)}, u32[]{:S(2)}, u32[]{:S(2)}) collective-permute-start(bf16[256,128]{1,0:T(8,128)(2,1)S(1)} %get-tuple-element.44.refs_0_), channel_id=1, source_target_pairs={{0,4},{4,0},{8,12},{12,8},{16,20},{20,16},{24,28},{28,24},{1,5},{5... | collective-permute-start | bytes 196616 | tf_op jit(solution)/shard_map/ppermute | solution.py:324
  83.1 1.6 %collective-permute-start.9 = (bf16[256,128]{1,0:T(8,128)(2,1)S(1)}, bf16[256,128]{1,0:T(8,128)(2,1)S(1)}, u32[]{:S(2)}, u32[]{:S(2)}) collective-permute-start(bf16[256,128]{1,0:T(8,128)(2,1)S(1)} %collective-permute-done.7.refs_1_), channel_id=1, source_target_pairs={{0,4},{4,0},{8,12},{12,8},{16,20},{20,16},{24,28},{28,24},{1,5},{5... | collective-permute-start | bytes 196616 | tf_op jit(solution)/shard_map/ppermute | solution.py:324
  (10 other events, 6.9 us)

commit v2 on v0

v2 whole, which is shorter than its diff:
```python
import functools

import jax
import jax.numpy as jnp
from jax import lax
from jax.experimental import pallas as pl
from jax.experimental.pallas import tpu as pltpu
from jax.sharding import PartitionSpec as P

BF16 = jnp.bfloat16
F32 = jnp.float32
LANES = 128
VMEM_LIMIT = 16 * 1024 * 1024


def log2(value):
    assert value & (value - 1) == 0
    return value.bit_length() - 1


def nn(a, b):
    return lax.dot_general(a, b, (((1,), (0,)), ((), ())), preferred_element_type=F32)


def nt(a, b):
    return lax.dot_general(a, b, (((1,), (1,)), ((), ())), preferred_element_type=F32)


ANY = pl.ANY
VMEM = pltpu.VMEM


def call(body, out_shape, args, after=(), anywhere=(), scratch=(), aliases=None, flops=0):
    count = len(args)

    def kernel(*refs):
        body(*refs[:count], *refs[count + len(after):])

    specs = [pl.BlockSpec(memory_space=pltpu.SMEM)]
    specs += [pl.BlockSpec(memory_space=ANY if k in anywhere else VMEM) for k in range(1, count)]
    specs += [pl.BlockSpec(memory_space=ANY)] * len(after)
    moved = sum(a.size * a.dtype.itemsize for a in args)
    many = isinstance(out_shape, (list, tuple))
    return pl.pallas_call(
        kernel,
        out_shape=out_shape,
        in_specs=specs,
        out_specs=[pl.BlockSpec(memory_space=VMEM)] * len(out_shape) if many else pl.BlockSpec(memory_space=VMEM),
        scratch_shapes=list(scratch),
        input_output_aliases=aliases or {},
        compiler_params=pltpu.CompilerParams(vmem_limit_bytes=VMEM_LIMIT),
        cost_estimate=pl.CostEstimate(flops=flops, bytes_accessed=moved, transcendentals=0),
    )(*args, *after)


def shape(dims, dtype):
    return jax.ShapeDtypeStruct(dims, dtype)


def digits_of(value):
    high = value.astype(BF16).astype(F32)
    rest = value - high
    middle = rest.astype(BF16).astype(F32)
    low = (rest - middle).astype(BF16).astype(F32)
    return high, middle, low


def one_hot(codes, axis_codes, first, count):
    frames = codes.shape[1 - axis_codes]
    dims = (count, frames) if axis_codes == 0 else (frames, count)
    places = lax.broadcasted_iota(jnp.int32, dims, axis_codes) + first
    return jnp.where(codes == places, 1.0, 0.0).astype(BF16)


def local_kernel(info, feats_in, weight_in, bias, codes, books_in, proj_in,
                 unfold, conv, chosen, weight, proj, feats, books, wide, sems):
    loads = [pltpu.make_async_copy(src, dst, sems.at[k]) for k, (src, dst) in enumerate(
        [(feats_in, feats), (weight_in, weight), (books_in, books), (proj_in, proj)])]
    for load in loads:
        load.start()
    rows, channels = feats.shape
    frames = rows // 2
    loads[0].wait()
    for j in range(channels // LANES):
        wide[j, 0:8, :] = jnp.zeros((8, LANES), F32)
        wide[j, 8:, :] = feats[:, j * LANES:(j + 1) * LANES].astype(F32)
        for tap in range(4):
            start = tap * channels + j * LANES
            unfold[:, start:start + LANES] = wide[j, pl.ds(6 + tap, frames, stride=2), :].astype(BF16)
    loads[1].wait()
    conv[...] = nn(unfold[...], weight[...]) + bias[...]
    loads[2].wait()
    levels = books.shape[0]
    padded = jnp.concatenate([codes[...].astype(F32), jnp.zeros((8 - levels, frames), F32)], 0)
    tall = jnp.transpose(padded).astype(jnp.int32)
    for level in range(levels):
        matches = one_hot(tall[:, level:level + 1], 1, 0, books.shape[1])
        chosen[level] = nn(matches, books[level]).astype(BF16)
    loads[3].wait()


def walk(order, halved, count):
    others = order[1:] if halved else order
    shown = count // 2 if halved else count
    step = 2 if shown > 1 and others[-1] == 0 else 1
    for position in range(0, shown, step):
        piece = 0
        for k, bit in enumerate(others):
            piece += ((position >> (len(others) - 1 - k)) & 1) << bit
        yield position, piece, step


def correlate(flipped, sources, plan, bit, out):
    dz = flipped.shape[0]
    at = 0
    for source, (count, order, halved) in zip(sources, plan):
        shown = count // 2 if halved else count
        for position, piece, step in walk(order, halved, count):
            if halved:
                column = pl.multiple_of((piece + (bit << order[0])) * LANES, LANES)
                product = nn(flipped, source[:, pl.ds(column, step * LANES)])
            else:
                product = nn(flipped, source[:, piece * LANES:(piece + step) * LANES])
            for j in range(step):
                top = (at + position + j) * dz
                out[top:top + dz, :] = product[:, j * LANES:(j + 1) * LANES].astype(out.dtype)
        at += shown
    return at * dz


def code_digits(codes, dz, rows):
    parts = []
    for part in (codes >> 8, codes & 255):
        for start in range(0, codes.shape[1], dz):
            piece = part[:, start:start + dz].astype(F32)
            if piece.shape[1] < dz:
                piece = jnp.concatenate([piece, jnp.zeros((1, dz - piece.shape[1]), F32)], 1)
            parts.append(piece)
    parts.append(jnp.zeros((rows - len(parts), dz), F32))
    return jnp.concatenate(parts, 0).astype(BF16)


def codes_of(block, frames):
    dz = block.shape[1]
    per = -(-frames // dz)
    digits = block[...].astype(F32)
    parts = [jnp.concatenate([digits[k * per + j:k * per + j + 1, :] for j in range(per)], 1)[:, :frames]
             for k in range(2)]
    return (parts[0] * 256.0 + parts[1]).astype(jnp.int32)


def forward_kernel(plan, info, halo, unfold_in, conv, chosen, weight, proj, codes,
                   unfold, hidden, latent_grad, flipped, own, send):
    frames, width = unfold.shape
    half = width // 2
    dz = proj.shape[1]
    row = lax.broadcasted_iota(jnp.int32, (16, half), 0)
    left = jnp.concatenate([halo[0:1, :], halo[1:2, :]], 1).astype(F32)
    head = jnp.where(row == 0, jnp.broadcast_to(left, (16, half)), 0.0)
    unfold[0:16, 0:half] = (unfold_in[0:16, 0:half].astype(F32) + head).astype(BF16)
    fix = nn(head.astype(BF16), weight[0:half, :])
    hidden[...] = jnp.concatenate([conv[0:16, :] + fix, conv[16:, :]], 0).astype(BF16)
    latent = nn(hidden[...], proj[...])
    once = latent - chosen[0].astype(F32)
    total = once + (once - chosen[1].astype(F32))
    latent_grad[...] = total.astype(BF16)
    flipped[...] = jnp.transpose(latent_grad[...].astype(F32)).astype(BF16)
    bit = info[0]
    at = correlate(flipped[...], (unfold, hidden), plan, 1 - bit, send)
    code_rows = own.shape[0] - frames
    digits = [code_digits(codes[level:level + 1], dz, code_rows) for level in range(2)]
    own[0:frames, :] = jnp.where(bit == 1, once, latent).astype(BF16)
    own[frames:, :] = jnp.where(bit == 1, digits[1], digits[0])
    other = jnp.where(bit == 1, latent, once).astype(BF16)
    other_digits = jnp.where(bit == 1, digits[0], digits[1])
    for j in range(dz // LANES):
        send[at:at + frames, :] = other[:, j * LANES:(j + 1) * LANES]
        send[at + frames:at + frames + code_rows, :] = other_digits[:, j * LANES:(j + 1) * LANES]
        at += frames + code_rows


def rest_kernel(plan, info, flipped, unfold, hidden, latent_grad, proj, keep, hidden_grad, extras):
    correlate(flipped[...], (unfold, hidden), plan, info[0], keep)
    back = nt(latent_grad[...], proj[...]).astype(BF16)
    hidden_grad[...] = back
    stride = extras.shape[0] // 4
    extras[...] = jnp.zeros(extras.shape, F32)
    sums = jnp.sum(back.astype(F32), 0, keepdims=True)
    for digit, part in enumerate(digits_of(sums)):
        for j in range(sums.shape[1] // LANES):
            extras[digit * stride + j:digit * stride + j + 1, :] = part[:, j * LANES:(j + 1) * LANES]


def split_sum(halves, bit, got, kept, send, keep):
    at_in = 0
    at_out = 0
    for rows, halved in halves:
        if halved:
            half = rows // 2
            away = pl.multiple_of(at_in + (1 - bit) * half, 16)
            home = pl.multiple_of(at_in + bit * half, 16)
            send[at_out:at_out + half, :] = (
                kept[pl.ds(away, half), :] + got[pl.ds(away, half), :].astype(F32)).astype(BF16)
            keep[at_out:at_out + half, :] = kept[pl.ds(home, half), :] + got[pl.ds(home, half), :].astype(F32)
            at_out += half
        else:
            total = (kept[at_in:at_in + rows, :] + got[at_in:at_in + rows, :].astype(F32)).astype(BF16)
            send[at_out:at_out + rows, :] = total
            keep[at_out:at_out + rows, :] = total.astype(F32)
            at_out += rows
        at_in += rows
    return at_in, at_out


def add_digits(mine, theirs):
    stride = mine.shape[0] // 4
    return ((mine[0:stride] + mine[stride:2 * stride]) + mine[2 * stride:3 * stride]) + (
        (theirs[0:stride] + theirs[stride:2 * stride]) + theirs[2 * stride:3 * stride])


def digit_block(value):
    return jnp.concatenate(list(digits_of(value)) + [jnp.zeros_like(value)], 0)


def first_step_kernel(halves, place, info, got, kept, extras, send, keep):
    _, at = split_sum(halves, info[place], got, kept, send, keep)
    send[at:, :] = extras[...].astype(BF16)
    keep[at:, :] = extras[...]


def step_kernel(halves, place, info, got, kept, send, keep):
    at_in, at_out = split_sum(halves, info[place], got, kept, send, keep)
    block = digit_block(add_digits(kept[at_in:, :], got[at_in:, :].astype(F32)))
    send[at_out:, :] = block.astype(BF16)
    keep[at_out:, :] = block


def feat_kernel(info, grad, after, weight, out, wide, inter):
    frames, channels = grad.shape
    half = weight.shape[0] // 2
    wide[0:frames, :] = grad[...].astype(F32)
    wide[frames:, :] = jnp.broadcast_to(after[0:1, :].astype(F32), (8, channels))
    ahead = wide[pl.ds(1, frames), :].astype(BF16)
    for parity in range(2):
        rows = pl.ds(parity * (half // 2), half // 2)
        rows_after = pl.ds(half + parity * (half // 2), half // 2)
        both = nt(ahead, weight[rows, :]) + nt(grad[...], weight[rows_after, :])
        for j in range(channels // LANES):
            inter[j, pl.ds(parity, frames, stride=2), :] = both[:, j * LANES:(j + 1) * LANES]
    for j in range(channels // LANES):
        out[:, j * LANES:(j + 1) * LANES] = inter[j].astype(BF16)


def sums_kernel(first, place, info, got, own, hidden_grad, keep, *sends):
    row, sends = sends[-1], sends[:-1]
    row[...] = hidden_grad[0:16, :]
    rows, dz = own.shape
    theirs = jnp.concatenate([got[first + j * rows:first + (j + 1) * rows, :] for j in range(dz // LANES)], 1)
    frames = hidden_grad.shape[0]
    ones = jnp.ones((8, frames), BF16)
    parts = []
    for block in (own[...], theirs):
        parts.append((block[0:frames, :], codes_of(block[frames:, :], frames)))
    for shift, out in enumerate((keep,) + sends):
        count = out.shape[0] - 16
        total = jnp.zeros((count, dz), F32)
        counts = jnp.zeros((8, count), F32)
        for values, codes in parts:
            matches = one_hot(codes, 0, info[place + shift], count)
            total = total + nn(matches, values)
            counts = counts + nt(ones, matches)
        out[0:count, :] = total.astype(out.dtype)
        out[count:, :] = count_rows(counts[0:1], dz).astype(out.dtype)


def count_rows(count, width):
    high = jnp.floor(count * (1.0 / 65536.0))
    rest = count - high * 65536.0
    middle = jnp.floor(rest * (1.0 / 256.0))
    low = rest - middle * 256.0
    block = jnp.concatenate([high, middle, low, jnp.zeros((13, count.shape[1]), F32)], 0)
    if count.shape[1] < width:
        block = jnp.concatenate([block, jnp.zeros((16, width - count.shape[1]), F32)], 1)
    return block


def count_of(block, own):
    return (block[0:1] * 65536.0 + block[1:2] * 256.0 + block[2:3])[:, :own]


def sums_step_kernel(info, kept, *refs):
    gots, out = refs[:-1], refs[-1]
    own = out.shape[0] - 16
    total = kept[0:own, :].astype(F32)
    count = count_of(kept[own:, :].astype(F32), own)
    for got in gots:
        total = total + got[0:own, :].astype(F32)
        count = count + count_of(got[own:, :].astype(F32), own)
    out[0:own, :] = total.astype(BF16)
    out[own:, :] = count_rows(count, out.shape[1]).astype(BF16)


def means_kernel(info, kept, got, out):
    own = out.shape[0] - 16
    count = count_of(kept[own:, :].astype(F32), own) + count_of(got[own:, :].astype(F32), own)
    square = (own, own)
    same = lax.broadcasted_iota(jnp.int32, square, 0) == lax.broadcasted_iota(jnp.int32, square, 1)
    tall = jnp.sum(jnp.where(same, jnp.broadcast_to(count, square), 0.0), 1, keepdims=True)
    total = kept[0:own, :].astype(F32) + got[0:own, :].astype(F32)
    out[0:own, :] = (total / jnp.maximum(tall, 1.0)).astype(BF16)
    out[own:, :] = count_rows(count, out.shape[1]).astype(BF16)


def means_out_kernel(scale, info, mine, theirs, means, usage):
    own = mine.shape[0] - 16
    bit = info[0]
    means[bit] = mine[0:own, :]
    means[1 - bit] = theirs[0:own, :]
    first = count_of(mine[own:, :].astype(F32), own) * scale
    second = count_of(theirs[own:, :].astype(F32), own) * scale
    usage[0:1, :] = jnp.where(bit == 1, second, first)
    usage[1:2, :] = jnp.where(bit == 1, first, second)


def last_kernel(first, second, got, kept, pieces, extras):
    pieces[...] = (kept[first:second, :] + got[first:second, :].astype(F32)).astype(BF16)
    block = digit_block(add_digits(kept[second:, :], got[second:, :].astype(F32)))
    extras[0:second - first, :] = pieces[...]
    extras[second - first:, :] = block.astype(BF16)


def conv_out_kernel(total_frames, place, info, got, kept, proj, out, wide):
    rows = out.shape[0]
    corr = kept[0:proj.shape[1], :] + got[0:proj.shape[1], :].astype(F32)
    flipped = jnp.transpose(corr)
    high = flipped.astype(BF16)
    low = (flipped - high.astype(F32)).astype(BF16)
    wide[...] = (nt(high, proj[...]) + nt(low, proj[...])) * (1.0 / total_frames)
    start = info[place]
    if rows % 8 == 0:
        out[...] = wide[pl.ds(pl.multiple_of(start, 8), rows), :]
    else:
        taken = wide[0:rows, :]
        for other in range(rows, wide.shape[0], rows):
            taken = jnp.where(start == other, wide[other:other + rows, :], taken)
        out[...] = taken


def proj_out_kernel(total_frames, dz, place, inner, info, mine, *refs):
    parts, out, bias = refs[:-2], refs[-2], refs[-1]
    scale = 1.0 / total_frames
    for j, ref in enumerate(parts):
        for k in range(inner):
            start = pl.multiple_of((info[place + j] + k) * LANES, LANES)
            out[pl.ds(start, LANES), :] = jnp.transpose(ref[k * dz:(k + 1) * dz, :].astype(F32)) * scale
    top = inner * dz
    value = add_digits(mine[top:, :].astype(F32), parts[1][top:, :].astype(F32)) * scale
    for j in range(bias.shape[1] // LANES):
        bias[:, j * LANES:(j + 1) * LANES] = value[j:j + 1, :]


def shifted(block, axis, distance):
    devices = range(lax.axis_size(axis))
    route = [(i - distance, i) for i in devices if i - distance in devices]
    return lax.ppermute(block, axis, route)


def swapped(block, axis, mask):
    return lax.ppermute(block, axis, [(i, i ^ mask) for i in range(lax.axis_size(axis))])


def shards(feats, codes, conv_weight, conv_bias, proj_weight, codebooks):
    dp, tm = lax.axis_size("dp"), lax.axis_size("tm")
    rows_in, channels = feats.shape
    frames = rows_in // 2
    levels, book_size, dz = codebooks.shape
    assert levels == 2
    width = conv_weight.shape[0]
    total_frames = frames * dp * tm
    per_shard = book_size // tm
    dp_bits, tm_bits = log2(dp), log2(tm)
    owner_rows = width // (dp * tm)

    exchanges = [("dp", b, b + tm_bits) for b in range(dp_bits)]
    exchanges += [("tm", b, b) for b in reversed(range(tm_bits))]
    pieces_a, pieces_c = width // LANES, channels // LANES
    under = max(dp_bits + tm_bits - log2(pieces_a), 0)
    c_bits = min(log2(pieces_c), 2, dp_bits)
    a_split = [bit - under if bit >= under else None for _, _, bit in exchanges]
    c_split = [log2(pieces_c) - 1 - k if k < c_bits else None for k in range(len(exchanges))]

    def order_of(split, count):
        used = [b for b in split if b is not None]
        return used + [b for b in reversed(range(log2(count))) if b not in used]

    plan = [(pieces_a, order_of(a_split, pieces_a), a_split[0] is not None),
            (pieces_c, order_of(c_split, pieces_c), c_split[0] is not None)]
    now_a = pieces_a // 2 if plan[0][2] else pieces_a
    now_c = pieces_c // 2 if plan[1][2] else pieces_c

    at_dp, at_tm = lax.axis_index("dp"), lax.axis_index("tm")
    bits = [((at_dp if axis == "dp" else at_tm) >> b) & 1 for axis, b, _ in exchanges]
    masks = list(range(1 << c_bits))
    own_piece = sum((bits[k] << c_split[k]) for k in range(c_bits))
    flips = [sum(1 << c_split[k] for k in range(c_bits) if m >> k & 1) for m in masks]
    at_start = len(bits)
    at_codes = at_start + 1
    at_pieces = at_codes + tm
    info = jnp.stack(
        bits + [((at_dp * tm + at_tm) * owner_rows) & (LANES - 1)]
        + [((at_tm + shift) & (tm - 1)) * per_shard for shift in range(tm)]
        + [own_piece ^ flip for flip in flips]).astype(jnp.int32)

    halo = shifted(feats[-2:], "tm", 1)
    codes = codes[0]
    unfold, conv, chosen, weight, proj = call(
        local_kernel,
        [shape((frames, width), BF16), shape((frames, channels), F32), shape((levels, frames, dz), BF16),
         shape(conv_weight.shape, BF16), shape(proj_weight.shape, BF16)],
        [info, feats, conv_weight, conv_bias[None, :], codes, codebooks, proj_weight],
        anywhere=(1, 2, 5, 6),
        scratch=[VMEM((rows_in, channels), BF16), VMEM(codebooks.shape, BF16),
                 VMEM((channels // LANES, rows_in + 8, LANES), F32), pltpu.SemaphoreType.DMA((4,))],
        flops=2 * frames * (width * channels + levels * book_size * dz),
    )

    extra = 4 * (-(-channels // LANES // 8) * 8)
    code_rows = -(-(2 * -(-frames // dz)) // 16) * 16
    corr_rows = (now_a + now_c) * dz
    rows_b = frames + code_rows
    unfold, hidden, latent_grad, flipped, own, send = call(
        functools.partial(forward_kernel, plan),
        [shape((frames, width), BF16), shape((frames, channels), BF16), shape((frames, dz), BF16),
         shape((dz, frames), BF16), shape((rows_b, dz), BF16),
         shape((corr_rows + rows_b * (dz // LANES), LANES), BF16)],
        [info, halo, unfold, conv, chosen, weight, proj, codes],
        aliases={2: 0},
        flops=2 * frames * (width * dz + 3 * channels * dz),
    )
    got = swapped(send, "dp", 1)
    keep, hidden_grad, extras = call(
        functools.partial(rest_kernel, plan),
        [shape((corr_rows, LANES), F32), shape((frames, channels), BF16), shape((extra, LANES), F32)],
        [info, flipped, unfold, hidden, latent_grad, proj],
        after=[send],
        flops=2 * frames * (width * dz // 2 + channels * dz),
    )

    def step(k, body, args, after):
        nonlocal now_a, now_c
        halves = [(now_a * dz, a_split[k] is not None), (now_c * dz, c_split[k] is not None)]
        now_a = now_a // 2 if halves[0][1] else now_a
        now_c = now_c // 2 if halves[1][1] else now_c
        rows = (now_a + now_c) * dz + extra
        return call(
            functools.partial(body, halves, k),
            [shape((rows, LANES), BF16), shape((rows, LANES), F32)],
            [info] + args, after=after)

    def exchange(k, block):
        axis, b, _ = exchanges[k]
        return swapped(block, axis, 1 << b)

    send, keep = step(1, first_step_kernel, [got, keep, extras], [])
    got_x = exchange(1, send)
    sums = call(
        functools.partial(sums_kernel, corr_rows, at_codes),
        [shape((per_shard + 16, dz), F32)] + [shape((per_shard + 16, dz), BF16)] * (tm - 1)
        + [shape((16, channels), BF16)],
        [info, got, own, hidden_grad],
        after=[send],
        flops=4 * frames * book_size * dz,
    )
    ring = [lax.ppermute(sums[shift], "tm", [(i, (i + shift) % tm) for i in range(tm)]) for shift in range(1, tm)]
    after = shifted(sums[-1], "tm", -1)
    send, keep = step(2, step_kernel, [got_x, keep], [sums[0]])
    got = exchange(2, send)
    feat_grad = call(
        feat_kernel,
        shape((rows_in, channels), BF16),
        [info, hidden_grad, after, weight],
        after=[send],
        scratch=[VMEM((frames + 8, channels), F32), VMEM((channels // LANES, rows_in, LANES), F32)],
        flops=2 * frames * width * channels,
    )
    last = feat_grad
    sums_bits = list(range(1, dp_bits))
    sums_now = None
    for k in range(3, len(exchanges)):
        send, keep = step(k, step_kernel, [got, keep], [last])
        got = exchange(k, send)
        if sums_now is None:
            sums_now = call(sums_step_kernel, shape((per_shard + 16, dz), BF16),
                            [info, sums[0]] + ring, after=[send])
            last = sums_now
        elif len(sums_bits) > 1:
            sums_got = swapped(sums_now, "dp", 1 << sums_bits.pop(0))
            sums_now = call(sums_step_kernel, shape((per_shard + 16, dz), BF16),
                            [info, sums_now, sums_got], after=[send])
            last = sums_now
    assert now_a == 1
    first = now_a * dz
    second = first + now_c * dz

    piece, mine = call(
        lambda info, *refs: last_kernel(first, second, *refs),
        [shape((second - first, LANES), BF16), shape((second - first + extra, LANES), BF16)],
        [info, got, keep], after=[last])
    parts = [piece] + [swapped(mine if m == 1 else piece, "dp", m) for m in masks[1:]]
    conv_grad = call(
        functools.partial(conv_out_kernel, total_frames, at_start),
        shape((owner_rows, channels), F32),
        [info, got, keep, proj],
        after=[piece],
        scratch=[VMEM((LANES, channels), F32)],
    )
    while len(sums_bits) > 1:
        sums_got = swapped(sums_now, "dp", 1 << sums_bits.pop(0))
        sums_now = call(sums_step_kernel, shape((per_shard + 16, dz), BF16),
                        [info, sums_now, sums_got], after=[conv_grad])
    sums_got = swapped(sums_now, "dp", 1 << sums_bits.pop(0))
    means = call(means_kernel, shape((per_shard + 16, dz), BF16), [info, sums_now, sums_got], after=[conv_grad])
    other = swapped(means, "dp", 1)
    proj_grad, bias_grad = call(
        functools.partial(proj_out_kernel, total_frames, dz, at_pieces, now_c),
        [shape((channels, dz), F32), shape((1, channels), F32)],
        [info, mine] + parts,
        after=[means],
    )
    code_means, code_usage = call(
        functools.partial(means_out_kernel, book_size / total_frames),
        [shape((levels, per_shard, dz), BF16), shape((levels, per_shard), F32)],
        [info, means, other],
        after=[proj_grad],
    )
    return feat_grad, conv_grad, bias_grad[0], proj_grad, code_means, code_usage


def solution(mesh):
    placed = (P(("dp", "tm"), None), P("dp", None, "tm"), P(), P(), P(), P())
    return jax.shard_map(
        shards,
        mesh=mesh,
        in_specs=placed,
        out_specs=(
            P(("dp", "tm"), None),
            P(("dp", "tm"), None),
            P(),
            P(),
            P(None, "tm", None),
            P(None, "tm"),
        ),
        check_vma=False,
    )
```

time: 211 us -> 78.7 us (0.37)
  blocking collectives: 72.7 us -> 0 us
  waiting for transfers between devices: 85.8 us -> 22.1 us
  Pallas kernels: 0 us -> 19.5 us
  starting transfers between devices: 6.33 us -> 25.6 us
  between operations: 15.7 us -> 0.78 us
  matrix products: 14 us -> 0 us
  other arithmetic: 6.76 us -> 0 us
    psum x1 -> x0, waiting for transfers between devices: 85.8 us -> none  [shards(): lax.psum((local_counts, proj_term, bias_term), ('dp', 'tm'))]
    psum x2 -> x0, blocking collectives: 72.7 us -> none  [the longest x1 42.1 us: shards(): lax.psum((local_counts, proj_term, bias_term), ('dp', 'tm'))]
    pallas_call x0 -> x16, Pallas kernels: none -> 19.5 us  [call(): pl.pallas_call(kernel, out_shape=out_shape, in_specs=specs, out_specs=[pl...]
    ppermute x0 -> x14, starting transfers between devices: none -> 19.4 us  [the longest x11 13.9 us: swapped(): lax.ppermute(block, axis, [(i, i ^ mask) for i in range(lax.axis_size(axi...]
    ppermute x0 -> x14, waiting for transfers between devices: none -> 16.2 us  [the longest x11 16.2 us: swapped(): lax.ppermute(block, axis, [(i, i ^ mask) for i in range(lax.axis_size(axi...]
    dot_general x11 -> x0, matrix products: 14 us -> none  [the longest x2 4.04 us: shards(): jnp.dot(onehot.T, residual, precision=lax.Precision.HIGHEST)]
    unnamed x17 -> x18, local copies, waits for them, and re-layouts: 1.69 us -> 9.34 us
    ppermute x2, waiting for transfers between devices: 0.01 us -> 5.92 us  [shifted(): return lax.ppermute(block, axis, route)]
  transfers between devices with their start and end apart: 5 -> 16, of which waited for: 1 -> 7; matrix products, arithmetic and copies ran while one was open for 8% -> 0% of each run, Pallas kernels for 0% -> 19%
where the time goes in v2:
time: 78.7 us; the launch traced here: 78.2 us
  starting transfers between devices  25.6 us (33%)
  waiting for transfers between devices  22.1 us (28%)
  Pallas kernels  19.5 us (25%)
  local copies, waits for them, and re-layouts  10.1 us (13%)
    pallas_call x16, Pallas kernels, call(): pl.pallas_call(kernel, out_shape=out_shape, in_specs=specs, out_specs=[pl...  19.5 us
    ppermute x11, waiting for transfers between devices, swapped(): lax.ppermute(block, axis, [(i, i ^ mask) for i in range(lax.axis_size(axi...  16.2 us
    ppermute x11, starting transfers between devices, swapped(): lax.ppermute(block, axis, [(i, i ^ mask) for i in range(lax.axis_size(axi...  13.9 us
    unnamed x18, local copies, waits for them, and re-layouts  9.34 us
    ppermute x2, starting transfers between devices, shifted(): return lax.ppermute(block, axis, route)  6.2 us
    ppermute x2, waiting for transfers between devices, shifted(): return lax.ppermute(block, axis, route)  5.92 us
    ppermute x3, starting transfers between devices, shards(): lax.ppermute(sums[shift], 'tm', [(i, (i + shift) % tm) for i in range(tm)])  5.51 us
  transfers between devices with their start and end apart: 16, of which 7 were waited for; matrix products, arithmetic and copies ran while one was open for 0% of the time, Pallas kernels for 19%

profile of v2, /device:TPU:0, one launch (start us, length us, event | category | flops | bytes accessed | tf_op | source)
XLA Modules:
  0.0 78.2 jit_solution(5026820260816408473)
XLA Ops:
  1.3 4.9 %collective-permute-start = (bf16[2,512]{1,0:T(2,128)(2,1)S(1)}, bf16[2,512]{1,0:T(2,128)(2,1)S(1)}, u32[]{:S(2)}, u32[]{:S(2)}) collective-permute-start(bf16[2,512]{1,0:T(2,128)(2,1)S(1)} %slice.3), channel_id=1, source_target_pairs={{0,1},{1,2},{2,3},{4,5},{5,6},{6,7},{8,9},{9,10},{10,11},{12,13},{... | collective-permute-start | bytes 6152 | tf_op jit(solution)/shard_map/ppermute | solution.py:365
  7.1 1.1 %copy-done.4 = bf16[768,512]{1,0:T(8,128)(2,1)S(1)} copy-done((bf16[768,512]{1,0:T(8,128)(2,1)S(1)}, bf16[768,512]{1,0:T(8,128)(2,1)}, u32[]{:S(2)}) %copy-start.4) | copy-done | bytes 786456
  8.2 1.6 %copy-done.5 = bf16[2048,512]{1,0:T(8,128)(2,1)S(1)} copy-done((bf16[2048,512]{1,0:T(8,128)(2,1)S(1)}, bf16[2048,512]{1,0:T(8,128)(2,1)}, u32[]{:S(2)}) %copy-start.5) | copy-done | bytes 2097176
  9.8 1.2 %copy-done.6 = bf16[2,1024,256]{2,1,0:T(8,128)(2,1)S(1)} copy-done((bf16[2,1024,256]{2,1,0:T(8,128)(2,1)S(1)}, bf16[2,1024,256]{2,1,0:T(8,128)(2,1)}, u32[]{:S(2)}) %copy-start.6) | copy-done | bytes 1048600
  11.0 0.9 %copy-done.7 = bf16[512,256]{1,0:T(8,128)(2,1)S(1)} copy-done((bf16[512,256]{1,0:T(8,128)(2,1)S(1)}, bf16[512,256]{1,0:T(8,128)(2,1)}, u32[]{:S(2)}) %copy-start.7) | copy-done | bytes 262168
  12.6 3.2 %shard_map.109 = (bf16[384,2048]{1,0:T(8,128)(2,1)S(1)}, f32[384,512]{1,0:T(8,128)S(1)}, bf16[2,384,256]{2,1,0:T(8,128)(2,1)S(1)}, bf16[2048,512]{1,0:T(8,128)(2,1)S(1)}, bf16[512,256]{1,0:T(8,128)(2,1)S(1)}) custom-call(s32[14]{0:T(128)S(1)} %stack.59.refs_0_, bf16[768,512]{1,0:T(8,128)(2,1)S(1)} %copy-done.4, bf16[2048,512]{1,0:T(8,128)(2,1)S(1)} %copy-done.5, ...), custom_call_target="tpu_custom_call" | custom-call | flops 1207959552 | bytes 4199480 | tf_op jit(solution)/shard_map/pallas_call | solution.py:44
  15.9 1.7 %shard_map.110 = (bf16[384,2048]{1,0:T(8,128)(2,1)S(1)}, bf16[384,512]{1,0:T(8,128)(2,1)S(1)}, bf16[384,256]{1,0:T(8,128)(2,1)S(1)}, bf16[256,384]{1,0:T(8,128)(...) custom-call(s32[14]{0:T(128)S(1)} %stack.59.refs_0_, ...), custom_call_target="tpu_custom_call", output_to_operand_aliasing={{0}: (2, {})} | custom-call | flops 704643072 | bytes 5116984 | tf_op jit(solution)/shard_map/pallas_call | solution.py:44
  17.7 1.2 %shard_map.111 = (f32[2560,128]{1,0:T(8,128)S(1)}, bf16[384,512]{1,0:T(8,128)(2,1)S(1)}, f32[32,128]{1,0:T(8,128)S(1)}) custom-call(s32[14]{0:T(128)S(1)} %stack.59.refs_0_, bf16[256,384]{1,0:T(8,128)(2,1)S(1)} %get-tuple-element.44.refs_1_, bf16[384,2048]{1,0:T(8,128)(2,1)S(1)} %get-tuple-element.45.refs_2_, ...), custom_call_target="tpu_custom_call" | custom-call | flops 301989888 | bytes 2621496 | tf_op jit(solution)/shard_map/pallas_call | solution.py:44
  18.9 1.2 %collective-permute-done.1.refs_1_ = bf16[3360,128]{1,0:T(8,128)(2,1)S(1)} collective-permute-done((bf16[3360,128]{1,0:T(8,128)(2,1)S(1)}, bf16[3360,128]{1,0:T(8,128)(2,1)S(1)}, u32[]{:S(2)}, u32[]{:S(2)}) %collective-permute-start.1) | collective-permute-done | bytes 860192 | tf_op jit(solution)/shard_map/ppermute | solution.py:369
  20.7 1.6 %collective-permute-start.3 = (bf16[1312,128]{1,0:T(8,128)(2,1)S(1)}, bf16[1312,128]{1,0:T(8,128)(2,1)S(1)}, u32[]{:S(2)}, u32[]{:S(2)}) collective-permute-start(bf16[1312,128]{1,0:T(8,128)(2,1)S(1)} %get-tuple-element.53.refs_4_), channel_id=1, source_target_pairs={{0,8},{4,12},{8,0},{12,4},{16,24},{20,28},{24,16},{28,20},{1,9},{5... | collective-permute-start | bytes 1007624 | tf_op jit(solution)/shard_map/ppermute | solution.py:369
  22.3 1.6 %shard_map.113 = (f32[272,256]{1,0:T(8,128)S(1)}, bf16[272,256]{1,0:T(8,128)(2,1)S(1)}, bf16[272,256]{1,0:T(8,128)(2,1)S(1)}, bf16[272,256]{1,0:T(8,128)(2,1)S(1)}, bf16[16,512]{1,0:T(8,128)(2,1)S(1)}) custom-call(s32[14]{0:T(128)S(1)} %stack.59.refs_0_, bf16[3360,128]{1,0:T(8,128)(2,1)S(1)} %collective-permute-done.1.refs_1_, ...), custom_call_target="tpu_custom_call" | custom-call | flops 402653184 | bytes 1458232 | tf_op jit(solution)/shard_map/pallas_call | solution.py:44
  23.9 6.8 %collective-permute-done.3.refs_1_ = bf16[1312,128]{1,0:T(8,128)(2,1)S(1)} collective-permute-done((bf16[1312,128]{1,0:T(8,128)(2,1)S(1)}, bf16[1312,128]{1,0:T(8,128)(2,1)S(1)}, u32[]{:S(2)}, u32[]{:S(2)}) %collective-permute-start.3) | collective-permute-done | bytes 335904 | tf_op jit(solution)/shard_map/ppermute | solution.py:369
  31.3 1.6 %collective-permute-start.4 = (bf16[800,128]{1,0:T(8,128)(2,1)S(1)}, bf16[800,128]{1,0:T(8,128)(2,1)S(1)}, u32[]{:S(2)}, u32[]{:S(2)}) collective-permute-start(bf16[800,128]{1,0:T(8,128)(2,1)S(1)} %get-tuple-element.57.refs_4_), channel_id=1, source_target_pairs={{0,16},{4,20},{8,24},{12,28},{16,0},{20,4},{24,8},{28,12},{1,17},{... | collective-permute-start | bytes 614408 | tf_op jit(solution)/shard_map/ppermute | solution.py:369
  32.9 1.6 %collective-permute-start.6 = (bf16[272,256]{1,0:T(8,128)(2,1)S(1)}, bf16[272,256]{1,0:T(8,128)(2,1)S(1)}, u32[]{:S(2)}, u32[]{:S(2)}) collective-permute-start(bf16[272,256]{1,0:T(8,128)(2,1)S(1)} %get-tuple-element.61), channel_id=1, source_target_pairs={{0,1},{1,2},{2,3},{3,0},{4,5},{5,6},{6,7},{7,4},{8,9},{9,10},{10,1... | collective-permute-start | bytes 417800 | tf_op jit(solution)/shard_map/ppermute | solution.py:474
  34.5 1.0 %collective-permute-start.7 = (bf16[272,256]{1,0:T(8,128)(2,1)S(1)}, bf16[272,256]{1,0:T(8,128)(2,1)S(1)}, u32[]{:S(2)}, u32[]{:S(2)}) collective-permute-start(bf16[272,256]{1,0:T(8,128)(2,1)S(1)} %get-tuple-element.62), channel_id=1, source_target_pairs={{0,2},{1,3},{2,0},{3,1},{4,6},{5,7},{6,4},{7,5},{8,10},{9,11},{10,... | collective-permute-start | bytes 417800 | tf_op jit(solution)/shard_map/ppermute | solution.py:474
  35.5 2.9 %collective-permute-start.8 = (bf16[272,256]{1,0:T(8,128)(2,1)S(1)}, bf16[272,256]{1,0:T(8,128)(2,1)S(1)}, u32[]{:S(2)}, u32[]{:S(2)}) collective-permute-start(bf16[272,256]{1,0:T(8,128)(2,1)S(1)} %get-tuple-element.63), channel_id=1, source_target_pairs={{0,3},{1,0},{2,1},{3,2},{4,7},{5,4},{6,5},{7,6},{8,11},{9,8},{10,9... | collective-permute-start | bytes 417800 | tf_op jit(solution)/shard_map/ppermute | solution.py:474
  38.4 1.3 %collective-permute-start.2 = (bf16[16,512]{1,0:T(8,128)(2,1)S(1)}, bf16[16,512]{1,0:T(8,128)(2,1)S(1)}, u32[]{:S(2)}, u32[]{:S(2)}) collective-permute-start(bf16[16,512]{1,0:T(8,128)(2,1)S(1)} %get-tuple-element.54), channel_id=1, source_target_pairs={{1,0},{2,1},{3,2},{5,4},{6,5},{7,6},{9,8},{10,9},{11,10},{13,12},{... | collective-permute-start | bytes 49160 | tf_op jit(solution)/shard_map/ppermute | solution.py:365
  39.7 5.9 %collective-permute-done.2.refs_2_ = bf16[16,512]{1,0:T(8,128)(2,1)S(1)} collective-permute-done((bf16[16,512]{1,0:T(8,128)(2,1)S(1)}, bf16[16,512]{1,0:T(8,128)(2,1)S(1)}, u32[]{:S(2)}, u32[]{:S(2)}) %collective-permute-start.2) | collective-permute-done | bytes 16416 | tf_op jit(solution)/shard_map/ppermute | solution.py:365
  45.6 2.6 %shard_map.115.refs_3_ = bf16[768,512]{1,0:T(8,128)(2,1)} custom-call(s32[14]{0:T(128)S(1)} %stack.59.refs_0_, bf16[384,512]{1,0:T(8,128)(2,1)S(1)} %get-tuple-element.49.refs_3_.refs_1_, bf16[16,512]{1,0:T(8,128)(2,1)S(1)} %collective-permute-done.2.refs_2_, bf16[2048,512]{1,0:T(8,128)(2,1)S(1)} %get-tuple-element.42.refs_5_.refs_3_, ...), custom_call_target="tpu_custom_call" | custom-call | flops 805306368 | bytes 2506808 | tf_op jit(solution)/shard_map/pallas_call | solution.py:44
  48.2 1.1 %copy-done = bf16[768,512]{1,0:T(8,128)(2,1)S(1)} copy-done((bf16[768,512]{1,0:T(8,128)(2,1)S(1)}, bf16[768,512]{1,0:T(8,128)(2,1)}, u32[]{:S(2)}) %copy-start) | copy-done | bytes 786456
  49.9 2.6 %collective-permute-start.5 = (bf16[544,128]{1,0:T(8,128)(2,1)S(1)}, bf16[544,128]{1,0:T(8,128)(2,1)S(1)}, u32[]{:S(2)}, u32[]{:S(2)}) collective-permute-start(bf16[544,128]{1,0:T(8,128)(2,1)S(1)} %get-tuple-element.59.refs_5_), channel_id=1, source_target_pairs={{0,2},{1,3},{2,0},{3,1},{4,6},{5,7},{6,4},{7,5},{8,10},{9,11},{10,... | collective-permute-start | bytes 417800 | tf_op jit(solution)/shard_map/ppermute | solution.py:369
  53.2 1.6 %collective-permute-start.10 = (bf16[272,256]{1,0:T(8,128)(2,1)S(1)}, bf16[272,256]{1,0:T(8,128)(2,1)S(1)}, u32[]{:S(2)}, u32[]{:S(2)}) collective-permute-start(bf16[272,256]{1,0:T(8,128)(2,1)S(1)} %shard_map.117.refs_3_.refs_1_), channel_id=1, source_target_pairs={{0,8},{4,12},{8,0},{12,4},{16,24},{20,28},{24,16},{28,20},{1,9},{5... | collective-permute-start | bytes 417800 | tf_op jit(solution)/shard_map/ppermute | solution.py:369
  54.7 1.7 %collective-permute-done.5.refs_1_ = bf16[544,128]{1,0:T(8,128)(2,1)S(1)} collective-permute-done((bf16[544,128]{1,0:T(8,128)(2,1)S(1)}, bf16[544,128]{1,0:T(8,128)(2,1)S(1)}, u32[]{:S(2)}, u32[]{:S(2)}) %collective-permute-start.5) | collective-permute-done | bytes 139296 | tf_op jit(solution)/shard_map/ppermute | solution.py:369
  57.0 3.7 %collective-permute-start.9 = (bf16[544,128]{1,0:T(8,128)(2,1)S(1)}, bf16[544,128]{1,0:T(8,128)(2,1)S(1)}, u32[]{:S(2)}, u32[]{:S(2)}) collective-permute-start(bf16[544,128]{1,0:T(8,128)(2,1)S(1)} %get-tuple-element.64.refs_3_), channel_id=1, source_target_pairs={{0,1},{1,0},{2,3},{3,2},{4,5},{5,4},{6,7},{7,6},{8,9},{9,8},{10,11... | collective-permute-start | bytes 417800 | tf_op jit(solution)/shard_map/ppermute | solution.py:369
  61.9 2.4 %collective-permute-done.9.refs_1_ = bf16[544,128]{1,0:T(8,128)(2,1)S(1)} collective-permute-done((bf16[544,128]{1,0:T(8,128)(2,1)S(1)}, bf16[544,128]{1,0:T(8,128)(2,1)S(1)}, u32[]{:S(2)}, u32[]{:S(2)}) %collective-permute-start.9) | collective-permute-done | bytes 139296 | tf_op jit(solution)/shard_map/ppermute | solution.py:369
  64.9 1.5 %shard_map.121.refs_3_ = f32[64,512]{1,0:T(8,128)} custom-call(s32[14]{0:T(128)S(1)} %stack.59.refs_0_, bf16[544,128]{1,0:T(8,128)(2,1)S(1)} %collective-permute-done.9.refs_1_, f32[544,128]{1,0:T(8,128)S(1)} %get-tuple-element.65.refs_2_, bf16[512,256]{1,0:T(8,128)(2,1)S(1)} %get-tuple-element.43.refs_6_.refs_5_.refs_3_, ...), custom_call_target="tpu_custom_call" | custom-call | bytes 679992 | tf_op jit(solution)/shard_map/pallas_call | solution.py:44
  68.6 1.2 %collective-permute-start.13 = (bf16[256,128]{1,0:T(8,128)(2,1)S(1)}, bf16[256,128]{1,0:T(8,128)(2,1)S(1)}, u32[]{:S(2)}, u32[]{:S(2)}) collective-permute-start(bf16[256,128]{1,0:T(8,128)(2,1)S(1)} %get-tuple-element.66.refs_4_.refs_2_), channel_id=1, source_target_pairs={{0,12},{4,8},{8,4},{12,0},{16,28},{20,24},{24,20},{28,16},{1,13},{... | collective-permute-start | bytes 196616 | tf_op jit(solution)/shard_map/ppermute | solution.py:369
  70.3 2.4 %collective-permute-done.13.refs_5_ = bf16[256,128]{1,0:T(8,128)(2,1)S(1)} collective-permute-done((bf16[256,128]{1,0:T(8,128)(2,1)S(1)}, bf16[256,128]{1,0:T(8,128)(2,1)S(1)}, u32[]{:S(2)}, u32[]{:S(2)}) %collective-permute-start.13) | collective-permute-done | bytes 65568 | tf_op jit(solution)/shard_map/ppermute | solution.py:369
  72.7 1.7 %collective-permute-done.12.refs_4_ = bf16[256,128]{1,0:T(8,128)(2,1)S(1)} collective-permute-done((bf16[256,128]{1,0:T(8,128)(2,1)S(1)}, bf16[256,128]{1,0:T(8,128)(2,1)S(1)}, u32[]{:S(2)}, u32[]{:S(2)}) %collective-permute-start.12) | collective-permute-done | bytes 65568 | tf_op jit(solution)/shard_map/ppermute | solution.py:369
  74.4 1.5 %shard_map.123 = (f32[512,256]{1,0:T(8,128)}, f32[1,512]{1,0:T(1,128)}) custom-call(s32[14]{0:T(128)S(1)} %stack.59.refs_0_, bf16[288,128]{1,0:T(8,128)(2,1)S(1)} %get-tuple-element.67.refs_1_, bf16[256,128]{1,0:T(8,128)(2,1)S(1)} %get-tuple-element.66.refs_4_.refs_2_, bf16[288,128]{1,0:T(8,128)(2,1)S(1)} %collective-permute-done.11.refs_3_, ...), custom_call_target="tpu_custom_call" | custom-call | bytes 344120 | tf_op jit(solution)/shard_map/pallas_call | solution.py:44
  75.9 1.0 %copy-done.1 = f32[512,256]{1,0:T(8,128)S(1)} copy-done((f32[512,256]{1,0:T(8,128)S(1)}, f32[512,256]{1,0:T(8,128)}, u32[]{:S(2)}) %copy-start.1) | copy-done | bytes 524312
  76.9 1.3 %shard_map.124 = (bf16[2,256,256]{2,1,0:T(8,128)(2,1)}, f32[2,256]{1,0:T(2,128)}) custom-call(s32[14]{0:T(128)S(1)} %stack.59.refs_0_, bf16[272,256]{1,0:T(8,128)(2,1)S(1)} %shard_map.122.refs_6_.refs_1_, bf16[272,256]{1,0:T(8,128)(2,1)S(1)} %collective-permute-done.15.refs_2_, f32[512,256]{1,0:T(8,128)S(1)} %copy-done.1), custom_call_target="tpu_custom_call" | custom-call | bytes 278584 | tf_op jit(solution)/shard_map/pallas_call | solution.py:44
  (36 shorter events, 9.8 us)
Async XLA Ops:
  1.3 14.5 %collective-permute-start = (bf16[2,512]{1,0:T(2,128)(2,1)S(1)}, bf16[2,512]{1,0:T(2,128)(2,1)S(1)}, u32[]{:S(2)}, u32[]{:S(2)}) collective-permute-start(bf16[2,512]{1,0:T(2,128)(2,1)S(1)} %slice.3), channel_id=1, source_target_pairs={{0,1},{1,2},{2,3},{4,5},{5,6},{6,7},{8,9},{9,10},{10,11},{12,13},{... | collective-permute-start | bytes 6152 | tf_op jit(solution)/shard_map/ppermute | solution.py:365
  6.4 0.7 copy-start.3
  7.1 1.1 %copy-start.4 = (bf16[768,512]{1,0:T(8,128)(2,1)S(1)}, bf16[768,512]{1,0:T(8,128)(2,1)}, u32[]{:S(2)}) copy-start(bf16[768,512]{1,0:T(8,128)(2,1)} %refs_1_.1) | copy-start | bytes 2359300
  8.2 1.6 %copy-start.5 = (bf16[2048,512]{1,0:T(8,128)(2,1)S(1)}, bf16[2048,512]{1,0:T(8,128)(2,1)}, u32[]{:S(2)}) copy-start(bf16[2048,512]{1,0:T(8,128)(2,1)} %refs_2_.1) | copy-start | bytes 6291460
  9.8 1.2 %copy-start.6 = (bf16[2,1024,256]{2,1,0:T(8,128)(2,1)S(1)}, bf16[2,1024,256]{2,1,0:T(8,128)(2,1)}, u32[]{:S(2)}) copy-start(bf16[2,1024,256]{2,1,0:T(8,128)(2,1)} %refs_5_.1) | copy-start | bytes 3145732
  11.0 0.9 %copy-start.7 = (bf16[512,256]{1,0:T(8,128)(2,1)S(1)}, bf16[512,256]{1,0:T(8,128)(2,1)}, u32[]{:S(2)}) copy-start(bf16[512,256]{1,0:T(8,128)(2,1)} %refs_6_.1) | copy-start | bytes 786436
  12.0 0.7 copy-start.8
  17.6 2.5 %collective-permute-start.1 = (bf16[3360,128]{1,0:T(8,128)(2,1)S(1)}, bf16[3360,128]{1,0:T(8,128)(2,1)S(1)}, u32[]{:S(2)}, u32[]{:S(2)}) collective-permute-start(bf16[3360,128]{1,0:T(8,128)(2,1)S(1)} %get-tuple-element.48.refs_6_), channel_id=1, source_target_pairs={{0,4},{4,0},{8,12},{12,8},{16,20},{20,16},{24,28},{28,24},{1,5},{5... | collective-permute-start | bytes 2580488 | tf_op jit(solution)/shard_map/ppermute | solution.py:369
  20.7 10.0 %collective-permute-start.3 = (bf16[1312,128]{1,0:T(8,128)(2,1)S(1)}, bf16[1312,128]{1,0:T(8,128)(2,1)S(1)}, u32[]{:S(2)}, u32[]{:S(2)}) collective-permute-start(bf16[1312,128]{1,0:T(8,128)(2,1)S(1)} %get-tuple-element.53.refs_4_), channel_id=1, source_target_pairs={{0,8},{4,12},{8,0},{12,4},{16,24},{20,28},{24,16},{28,20},{1,9},{5... | collective-permute-start | bytes 1007624 | tf_op jit(solution)/shard_map/ppermute | solution.py:369
  31.3 16.9 %collective-permute-start.4 = (bf16[800,128]{1,0:T(8,128)(2,1)S(1)}, bf16[800,128]{1,0:T(8,128)(2,1)S(1)}, u32[]{:S(2)}, u32[]{:S(2)}) collective-permute-start(bf16[800,128]{1,0:T(8,128)(2,1)S(1)} %get-tuple-element.57.refs_4_), channel_id=1, source_target_pairs={{0,16},{4,20},{8,24},{12,28},{16,0},{20,4},{24,8},{28,12},{1,17},{... | collective-permute-start | bytes 614408 | tf_op jit(solution)/shard_map/ppermute | solution.py:369
  32.9 19.6 %collective-permute-start.6 = (bf16[272,256]{1,0:T(8,128)(2,1)S(1)}, bf16[272,256]{1,0:T(8,128)(2,1)S(1)}, u32[]{:S(2)}, u32[]{:S(2)}) collective-permute-start(bf16[272,256]{1,0:T(8,128)(2,1)S(1)} %get-tuple-element.61), channel_id=1, source_target_pairs={{0,1},{1,2},{2,3},{3,0},{4,5},{5,6},{6,7},{7,4},{8,9},{9,10},{10,1... | collective-permute-start | bytes 417800 | tf_op jit(solution)/shard_map/ppermute | solution.py:474
  34.5 18.0 %collective-permute-start.7 = (bf16[272,256]{1,0:T(8,128)(2,1)S(1)}, bf16[272,256]{1,0:T(8,128)(2,1)S(1)}, u32[]{:S(2)}, u32[]{:S(2)}) collective-permute-start(bf16[272,256]{1,0:T(8,128)(2,1)S(1)} %get-tuple-element.62), channel_id=1, source_target_pairs={{0,2},{1,3},{2,0},{3,1},{4,6},{5,7},{6,4},{7,5},{8,10},{9,11},{10,... | collective-permute-start | bytes 417800 | tf_op jit(solution)/shard_map/ppermute | solution.py:474
  35.5 17.0 %collective-permute-start.8 = (bf16[272,256]{1,0:T(8,128)(2,1)S(1)}, bf16[272,256]{1,0:T(8,128)(2,1)S(1)}, u32[]{:S(2)}, u32[]{:S(2)}) collective-permute-start(bf16[272,256]{1,0:T(8,128)(2,1)S(1)} %get-tuple-element.63), channel_id=1, source_target_pairs={{0,3},{1,0},{2,1},{3,2},{4,7},{5,4},{6,5},{7,6},{8,11},{9,8},{10,9... | collective-permute-start | bytes 417800 | tf_op jit(solution)/shard_map/ppermute | solution.py:474
  38.4 7.2 %collective-permute-start.2 = (bf16[16,512]{1,0:T(8,128)(2,1)S(1)}, bf16[16,512]{1,0:T(8,128)(2,1)S(1)}, u32[]{:S(2)}, u32[]{:S(2)}) collective-permute-start(bf16[16,512]{1,0:T(8,128)(2,1)S(1)} %get-tuple-element.54), channel_id=1, source_target_pairs={{1,0},{2,1},{3,2},{5,4},{6,5},{7,6},{9,8},{10,9},{11,10},{13,12},{... | collective-permute-start | bytes 49160 | tf_op jit(solution)/shard_map/ppermute | solution.py:365
  48.2 1.1 %copy-start = (bf16[768,512]{1,0:T(8,128)(2,1)S(1)}, bf16[768,512]{1,0:T(8,128)(2,1)}, u32[]{:S(2)}) copy-start(bf16[768,512]{1,0:T(8,128)(2,1)} %shard_map.115.refs_3_) | copy-start | bytes 2359300
  49.9 6.4 %collective-permute-start.5 = (bf16[544,128]{1,0:T(8,128)(2,1)S(1)}, bf16[544,128]{1,0:T(8,128)(2,1)S(1)}, u32[]{:S(2)}, u32[]{:S(2)}) collective-permute-start(bf16[544,128]{1,0:T(8,128)(2,1)S(1)} %get-tuple-element.59.refs_5_), channel_id=1, source_target_pairs={{0,2},{1,3},{2,0},{3,1},{4,6},{5,7},{6,4},{7,5},{8,10},{9,11},{10,... | collective-permute-start | bytes 417800 | tf_op jit(solution)/shard_map/ppermute | solution.py:369
  53.2 7.5 %collective-permute-start.10 = (bf16[272,256]{1,0:T(8,128)(2,1)S(1)}, bf16[272,256]{1,0:T(8,128)(2,1)S(1)}, u32[]{:S(2)}, u32[]{:S(2)}) collective-permute-start(bf16[272,256]{1,0:T(8,128)(2,1)S(1)} %shard_map.117.refs_3_.refs_1_), channel_id=1, source_target_pairs={{0,8},{4,12},{8,0},{12,4},{16,24},{20,28},{24,16},{28,20},{1,9},{5... | collective-permute-start | bytes 417800 | tf_op jit(solution)/shard_map/ppermute | solution.py:369
  57.0 7.3 %collective-permute-start.9 = (bf16[544,128]{1,0:T(8,128)(2,1)S(1)}, bf16[544,128]{1,0:T(8,128)(2,1)S(1)}, u32[]{:S(2)}, u32[]{:S(2)}) collective-permute-start(bf16[544,128]{1,0:T(8,128)(2,1)S(1)} %get-tuple-element.64.refs_3_), channel_id=1, source_target_pairs={{0,1},{1,0},{2,3},{3,2},{4,5},{5,4},{6,7},{7,6},{8,9},{9,8},{10,11... | collective-permute-start | bytes 417800 | tf_op jit(solution)/shard_map/ppermute | solution.py:369
  61.3 5.1 %collective-permute-start.14 = (bf16[272,256]{1,0:T(8,128)(2,1)S(1)}, bf16[272,256]{1,0:T(8,128)(2,1)S(1)}, u32[]{:S(2)}, u32[]{:S(2)}) collective-permute-start(bf16[272,256]{1,0:T(8,128)(2,1)S(1)} %shard_map.119.refs_3_.refs_1_), channel_id=1, source_target_pairs={{0,16},{4,20},{8,24},{12,28},{16,0},{20,4},{24,8},{28,12},{1,17},{... | collective-permute-start | bytes 417800 | tf_op jit(solution)/shard_map/ppermute | solution.py:369
  66.4 0.9 %copy-start.2 = (f32[64,512]{1,0:T(8,128)S(1)}, f32[64,512]{1,0:T(8,128)}, u32[]{:S(2)}) copy-start(f32[64,512]{1,0:T(8,128)} %shard_map.121.refs_3_) | copy-start | bytes 393220
  68.0 7.9 %collective-permute-start.15 = (bf16[272,256]{1,0:T(8,128)(2,1)S(1)}, bf16[272,256]{1,0:T(8,128)(2,1)S(1)}, u32[]{:S(2)}, u32[]{:S(2)}) collective-permute-start(bf16[272,256]{1,0:T(8,128)(2,1)S(1)} %shard_map.122.refs_6_.refs_1_), channel_id=1, source_target_pairs={{0,4},{4,0},{8,12},{12,8},{16,20},{20,16},{24,28},{28,24},{1,5},{5... | collective-permute-start | bytes 417800 | tf_op jit(solution)/shard_map/ppermute | solution.py:369
  68.1 6.3 %collective-permute-start.11 = (bf16[288,128]{1,0:T(8,128)(2,1)S(1)}, bf16[288,128]{1,0:T(8,128)(2,1)S(1)}, u32[]{:S(2)}, u32[]{:S(2)}) collective-permute-start(bf16[288,128]{1,0:T(8,128)(2,1)S(1)} %get-tuple-element.67.refs_1_), channel_id=1, source_target_pairs={{0,4},{4,0},{8,12},{12,8},{16,20},{20,16},{24,28},{28,24},{1,5},{5... | collective-permute-start | bytes 221192 | tf_op jit(solution)/shard_map/ppermute | solution.py:369
  68.6 4.1 %collective-permute-start.13 = (bf16[256,128]{1,0:T(8,128)(2,1)S(1)}, bf16[256,128]{1,0:T(8,128)(2,1)S(1)}, u32[]{:S(2)}, u32[]{:S(2)}) collective-permute-start(bf16[256,128]{1,0:T(8,128)(2,1)S(1)} %get-tuple-element.66.refs_4_.refs_2_), channel_id=1, source_target_pairs={{0,12},{4,8},{8,4},{12,0},{16,28},{20,24},{24,20},{28,16},{1,13},{... | collective-permute-start | bytes 196616 | tf_op jit(solution)/shard_map/ppermute | solution.py:369
  69.7 4.6 %collective-permute-start.12 = (bf16[256,128]{1,0:T(8,128)(2,1)S(1)}, bf16[256,128]{1,0:T(8,128)(2,1)S(1)}, u32[]{:S(2)}, u32[]{:S(2)}) collective-permute-start(bf16[256,128]{1,0:T(8,128)(2,1)S(1)} %get-tuple-element.66.refs_4_.refs_2_), channel_id=1, source_target_pairs={{0,8},{4,12},{8,0},{12,4},{16,24},{20,28},{24,16},{28,20},{1,9},{5... | collective-permute-start | bytes 196616 | tf_op jit(solution)/shard_map/ppermute | solution.py:369
  75.9 1.0 %copy-start.1 = (f32[512,256]{1,0:T(8,128)S(1)}, f32[512,256]{1,0:T(8,128)}, u32[]{:S(2)}) copy-start(f32[512,256]{1,0:T(8,128)} %get-tuple-element.36.refs_3_) | copy-start | bytes 1572868

commit v3 on v2

--- a/solution.py
+++ b/solution.py
@@ -26,31 +26,36 @@
     return lax.dot_general(a, b, (((1,), (1,)), ((), ())), preferred_element_type=F32)
 
 
-ANY = pl.ANY
 VMEM = pltpu.VMEM
 
 
-def call(body, out_shape, args, after=(), anywhere=(), scratch=(), aliases=None, flops=0):
+def call(body, out_shape, args, after=(), scratch=(), aliases=None, token=False, flops=0):
     count = len(args)
+    many = isinstance(out_shape, (list, tuple))
+    shapes = list(out_shape) if many else [out_shape]
 
     def kernel(*refs):
-        body(*refs[:count], *refs[count + len(after):])
+        ends = count + len(after)
+        if token:
+            refs[ends + len(shapes)][...] = jnp.zeros((8, LANES), F32)
+            refs = refs[:ends + len(shapes)] + refs[ends + len(shapes) + 1:]
+        body(*refs[:count], *refs[ends:])
 
     specs = [pl.BlockSpec(memory_space=pltpu.SMEM)]
-    specs += [pl.BlockSpec(memory_space=ANY if k in anywhere else VMEM) for k in range(1, count)]
-    specs += [pl.BlockSpec(memory_space=ANY)] * len(after)
-    moved = sum(a.size * a.dtype.itemsize for a in args)
-    many = isinstance(out_shape, (list, tuple))
-    return pl.pallas_call(
+    specs += [pl.BlockSpec(memory_space=VMEM)] * (count - 1)
+    specs += [pl.BlockSpec(memory_space=pl.ANY)] * len(after)
+    shown = shapes + [shape((8, LANES), F32)] * token
+    outs = pl.pallas_call(
         kernel,
-        out_shape=out_shape,
+        out_shape=shown,
         in_specs=specs,
-        out_specs=[pl.BlockSpec(memory_space=VMEM)] * len(out_shape) if many else pl.BlockSpec(memory_space=VMEM),
+        out_specs=[pl.BlockSpec(memory_space=VMEM)] * len(shown),
         scratch_shapes=list(scratch),
         input_output_aliases=aliases or {},
         compiler_params=pltpu.CompilerParams(vmem_limit_bytes=VMEM_LIMIT),
-        cost_estimate=pl.CostEstimate(flops=flops, bytes_accessed=moved, transcendentals=0),
+        cost_estimate=pl.CostEstimate(flops=flops, bytes_accessed=0, transcendentals=0),
     )(*args, *after)
+    return outs if len(shown) > 1 else outs[0]
 
 
 def shape(dims, dtype):
@@ -72,31 +77,26 @@
     return jnp.where(codes == places, 1.0, 0.0).astype(BF16)
 
 
-def local_kernel(info, feats_in, weight_in, bias, codes, books_in, proj_in,
-                 unfold, conv, chosen, weight, proj, feats, books, wide, sems):
-    loads = [pltpu.make_async_copy(src, dst, sems.at[k]) for k, (src, dst) in enumerate(
-        [(feats_in, feats), (weight_in, weight), (books_in, books), (proj_in, proj)])]
-    for load in loads:
-        load.start()
+def halo_kernel(info, feats, out):
+    out[...] = feats[feats.shape[0] - out.shape[0]:, :]
+
+
+def local_kernel(info, feats, weight, bias, codes, books, unfold, conv, chosen, wide):
     rows, channels = feats.shape
     frames = rows // 2
-    loads[0].wait()
     for j in range(channels // LANES):
         wide[j, 0:8, :] = jnp.zeros((8, LANES), F32)
         wide[j, 8:, :] = feats[:, j * LANES:(j + 1) * LANES].astype(F32)
         for tap in range(4):
             start = tap * channels + j * LANES
             unfold[:, start:start + LANES] = wide[j, pl.ds(6 + tap, frames, stride=2), :].astype(BF16)
-    loads[1].wait()
     conv[...] = nn(unfold[...], weight[...]) + bias[...]
-    loads[2].wait()
     levels = books.shape[0]
     padded = jnp.concatenate([codes[...].astype(F32), jnp.zeros((8 - levels, frames), F32)], 0)
     tall = jnp.transpose(padded).astype(jnp.int32)
     for level in range(levels):
         matches = one_hot(tall[:, level:level + 1], 1, 0, books.shape[1])
         chosen[level] = nn(matches, books[level]).astype(BF16)
-    loads[3].wait()
 
 
 def walk(order, halved, count):
@@ -155,7 +155,8 @@
     half = width // 2
     dz = proj.shape[1]
     row = lax.broadcasted_iota(jnp.int32, (16, half), 0)
-    left = jnp.concatenate([halo[0:1, :], halo[1:2, :]], 1).astype(F32)
+    last = halo[...].astype(F32)
+    left = jnp.concatenate([last[14:15, :], last[15:16, :]], 1)
     head = jnp.where(row == 0, jnp.broadcast_to(left, (16, half)), 0.0)
     unfold[0:16, 0:half] = (unfold_in[0:16, 0:half].astype(F32) + head).astype(BF16)
     fix = nn(head.astype(BF16), weight[0:half, :])
@@ -179,10 +180,11 @@
         at += frames + code_rows
 
 
-def rest_kernel(plan, info, flipped, unfold, hidden, latent_grad, proj, keep, hidden_grad, extras):
+def rest_kernel(plan, info, flipped, unfold, hidden, latent_grad, proj, keep, hidden_grad, extras, row):
     correlate(flipped[...], (unfold, hidden), plan, info[0], keep)
     back = nt(latent_grad[...], proj[...]).astype(BF16)
     hidden_grad[...] = back
+    row[...] = back[0:16, :]
     stride = extras.shape[0] // 4
     extras[...] = jnp.zeros(extras.shape, F32)
     sums = jnp.sum(back.astype(F32), 0, keepdims=True)
@@ -228,13 +230,6 @@
     keep[at:, :] = extras[...]
 
 
-def step_kernel(halves, place, info, got, kept, send, keep):
-    at_in, at_out = split_sum(halves, info[place], got, kept, send, keep)
-    block = digit_block(add_digits(kept[at_in:, :], got[at_in:, :].astype(F32)))
-    send[at_out:, :] = block.astype(BF16)
-    keep[at_out:, :] = block
-
-
 def feat_kernel(info, grad, after, weight, out, wide, inter):
     frames, channels = grad.shape
     half = weight.shape[0] // 2
@@ -251,26 +246,25 @@
         out[:, j * LANES:(j + 1) * LANES] = inter[j].astype(BF16)
 
 
-def sums_kernel(first, place, info, got, own, hidden_grad, keep, *sends):
-    row, sends = sends[-1], sends[:-1]
-    row[...] = hidden_grad[0:16, :]
+def sums_kernel(first, frames, place, count, info, got, own, send, keep):
     rows, dz = own.shape
     theirs = jnp.concatenate([got[first + j * rows:first + (j + 1) * rows, :] for j in range(dz // LANES)], 1)
-    frames = hidden_grad.shape[0]
     ones = jnp.ones((8, frames), BF16)
     parts = []
     for block in (own[...], theirs):
         parts.append((block[0:frames, :], codes_of(block[frames:, :], frames)))
-    for shift, out in enumerate((keep,) + sends):
-        count = out.shape[0] - 16
-        total = jnp.zeros((count, dz), F32)
-        counts = jnp.zeros((8, count), F32)
-        for values, codes in parts:
-            matches = one_hot(codes, 0, info[place + shift], count)
-            total = total + nn(matches, values)
-            counts = counts + nt(ones, matches)
-        out[0:count, :] = total.astype(out.dtype)
-        out[count:, :] = count_rows(counts[0:1], dz).astype(out.dtype)
+    size = count + 16
+    for out in (send, keep):
+        for top in range(0, out.shape[0], size):
+            total = jnp.zeros((count, dz), F32)
+            counts = jnp.zeros((8, count), F32)
+            for values, codes in parts:
+                matches = one_hot(codes, 0, info[place], count)
+                total = total + nn(matches, values)
+                counts = counts + nt(ones, matches)
+            out[top:top + count, :] = total.astype(out.dtype)
+            out[top + count:top + size, :] = count_rows(counts[0:1], dz).astype(out.dtype)
+            place += 1
 
 
 def count_rows(count, width):
@@ -288,45 +282,55 @@
     return (block[0:1] * 65536.0 + block[1:2] * 256.0 + block[2:3])[:, :own]
 
 
-def sums_step_kernel(info, kept, *refs):
-    gots, out = refs[:-1], refs[-1]
-    own = out.shape[0] - 16
-    total = kept[0:own, :].astype(F32)
-    count = count_of(kept[own:, :].astype(F32), own)
-    for got in gots:
-        total = total + got[0:own, :].astype(F32)
-        count = count + count_of(got[own:, :].astype(F32), own)
-    out[0:own, :] = total.astype(BF16)
-    out[own:, :] = count_rows(count, out.shape[1]).astype(BF16)
-
-
-def means_kernel(info, kept, got, out):
-    own = out.shape[0] - 16
-    count = count_of(kept[own:, :].astype(F32), own) + count_of(got[own:, :].astype(F32), own)
-    square = (own, own)
-    same = lax.broadcasted_iota(jnp.int32, square, 0) == lax.broadcasted_iota(jnp.int32, square, 1)
-    tall = jnp.sum(jnp.where(same, jnp.broadcast_to(count, square), 0.0), 1, keepdims=True)
-    total = kept[0:own, :].astype(F32) + got[0:own, :].astype(F32)
-    out[0:own, :] = (total / jnp.maximum(tall, 1.0)).astype(BF16)
-    out[own:, :] = count_rows(count, out.shape[1]).astype(BF16)
-
-
-def means_out_kernel(scale, info, mine, theirs, means, usage):
-    own = mine.shape[0] - 16
-    bit = info[0]
-    means[bit] = mine[0:own, :]
-    means[1 - bit] = theirs[0:own, :]
-    first = count_of(mine[own:, :].astype(F32), own) * scale
-    second = count_of(theirs[own:, :].astype(F32), own) * scale
-    usage[0:1, :] = jnp.where(bit == 1, second, first)
-    usage[1:2, :] = jnp.where(bit == 1, first, second)
-
-
-def last_kernel(first, second, got, kept, pieces, extras):
+def sums_step(halved, count, bit, got, kept, send, keep):
+    size = count + 16
+    dz = got.shape[1]
+    half = kept.shape[0] // 2 if halved else 0
+    outs = [(send, (1 - bit) * half), (keep, bit * half)] if halved else [(send, 0)]
+    for out, start in outs:
+        for top in range(0, out.shape[0], size):
+            here = top + pl.multiple_of(start, 16) if halved else top
+            sums = pl.ds(here, count)
+            tail = pl.ds(here + count, 16)
+            value = kept[sums, :].astype(F32) + got[sums, :].astype(F32)
+            number = count_of(kept[tail, :].astype(F32), count) + count_of(got[tail, :].astype(F32), count)
+            out[top:top + count, :] = value.astype(out.dtype)
+            out[top + count:top + size, :] = count_rows(number, dz).astype(out.dtype)
+    if not halved:
+        keep[...] = send[...].astype(F32)
+
+
+def window_kernel(halves, place, sums_halved, sums_count, sums_place, pass_on, info, got, kept, sums_got, sums_kept,
+                  *refs):
+    if pass_on:
+        refs[-1][...] = refs[0][...]
+        refs = refs[1:-1]
+    send, keep, sums_send, sums_keep = refs
+    at_in, at_out = split_sum(halves, info[place], got, kept, send, keep)
+    block = digit_block(add_digits(kept[at_in:, :], got[at_in:, :].astype(F32)))
+    send[at_out:, :] = block.astype(BF16)
+    keep[at_out:, :] = block
+    sums_step(sums_halved, sums_count, info[sums_place], sums_got, sums_kept, sums_send, sums_keep)
+
+
+def last_kernel(first, second, count, info, got, kept, sums_got, sums_kept, pieces, mine):
     pieces[...] = (kept[first:second, :] + got[first:second, :].astype(F32)).astype(BF16)
     block = digit_block(add_digits(kept[second:, :], got[second:, :].astype(F32)))
-    extras[0:second - first, :] = pieces[...]
-    extras[second - first:, :] = block.astype(BF16)
+    at = second - first
+    mine[0:at, :] = pieces[...]
+    mine[at:at + block.shape[0], :] = block.astype(BF16)
+    at += block.shape[0]
+    number = count_of(sums_kept[count:, :].astype(F32), count) + count_of(sums_got[count:, :].astype(F32), count)
+    square = (count, count)
+    same = lax.broadcasted_iota(jnp.int32, square, 0) == lax.broadcasted_iota(jnp.int32, square, 1)
+    tall = jnp.sum(jnp.where(same, jnp.broadcast_to(number, square), 0.0), 1, keepdims=True)
+    total = sums_kept[0:count, :].astype(F32) + sums_got[0:count, :].astype(F32)
+    means = (total / jnp.maximum(tall, 1.0)).astype(BF16)
+    digits = count_rows(number, means.shape[1]).astype(BF16)
+    for j in range(means.shape[1] // LANES):
+        mine[at:at + count, :] = means[:, j * LANES:(j + 1) * LANES]
+        mine[at + count:at + count + 16, :] = digits[:, j * LANES:(j + 1) * LANES]
+        at += count + 16
 
 
 def conv_out_kernel(total_frames, place, info, got, kept, proj, out, wide):
@@ -346,17 +350,31 @@
         out[...] = taken
 
 
-def proj_out_kernel(total_frames, dz, place, inner, info, mine, *refs):
-    parts, out, bias = refs[:-2], refs[-2], refs[-1]
+def out_kernel(total_frames, use_scale, count, dz, place, inner, extra, info, mine, *refs):
+    parts, (out, bias, means, usage) = refs[:-4], refs[-4:]
     scale = 1.0 / total_frames
     for j, ref in enumerate(parts):
         for k in range(inner):
             start = pl.multiple_of((info[place + j] + k) * LANES, LANES)
             out[pl.ds(start, LANES), :] = jnp.transpose(ref[k * dz:(k + 1) * dz, :].astype(F32)) * scale
+    theirs = parts[1]
     top = inner * dz
-    value = add_digits(mine[top:, :].astype(F32), parts[1][top:, :].astype(F32)) * scale
+    value = add_digits(mine[top:top + extra, :].astype(F32), theirs[top:top + extra, :].astype(F32)) * scale
     for j in range(bias.shape[1] // LANES):
         bias[:, j * LANES:(j + 1) * LANES] = value[j:j + 1, :]
+    bit = info[0]
+    numbers = []
+    for ref, level in ((mine, bit), (theirs, 1 - bit)):
+        at = top + extra
+        blocks = []
+        for j in range(dz // LANES):
+            blocks.append(ref[at:at + count + 16, :])
+            at += count + 16
+        whole = jnp.concatenate(blocks, 1)
+        means[level] = whole[0:count, :]
+        numbers.append(count_of(whole[count:, :].astype(F32), count) * use_scale)
+    usage[0:1, :] = jnp.where(bit == 1, numbers[1], numbers[0])
+    usage[1:2, :] = jnp.where(bit == 1, numbers[0], numbers[1])
 
 
 def shifted(block, axis, distance):
@@ -398,30 +416,38 @@
     now_a = pieces_a // 2 if plan[0][2] else pieces_a
     now_c = pieces_c // 2 if plan[1][2] else pieces_c
 
+    sums_exchanges = [("tm", b) for b in range(tm_bits)] + [("dp", b) for b in range(1, dp_bits)]
+
     at_dp, at_tm = lax.axis_index("dp"), lax.axis_index("tm")
-    bits = [((at_dp if axis == "dp" else at_tm) >> b) & 1 for axis, b, _ in exchanges]
+
+    def bit_of(axis, b):
+        return ((at_dp if axis == "dp" else at_tm) >> b) & 1
+
+    bits = [bit_of(axis, b) for axis, b, _ in exchanges]
+    sums_bits = [bit_of(axis, b) for axis, b in sums_exchanges]
     masks = list(range(1 << c_bits))
     own_piece = sum((bits[k] << c_split[k]) for k in range(c_bits))
     flips = [sum(1 << c_split[k] for k in range(c_bits) if m >> k & 1) for m in masks]
+    quarters = [sum(((position >> (tm_bits - 1 - b)) & 1) << b for b in range(tm_bits)) for position in range(tm)]
+    lead = at_tm & 1
+    send_quarters = [(q | (1 - lead)) * per_shard for q in quarters[:tm // 2]]
+    keep_quarters = [(q | lead) * per_shard for q in quarters[:tm // 2]]
     at_start = len(bits)
     at_codes = at_start + 1
     at_pieces = at_codes + tm
+    at_sums = at_pieces + len(masks)
     info = jnp.stack(
-        bits + [((at_dp * tm + at_tm) * owner_rows) & (LANES - 1)]
-        + [((at_tm + shift) & (tm - 1)) * per_shard for shift in range(tm)]
-        + [own_piece ^ flip for flip in flips]).astype(jnp.int32)
-
-    halo = shifted(feats[-2:], "tm", 1)
-    codes = codes[0]
-    unfold, conv, chosen, weight, proj = call(
+        bits + [((at_dp * tm + at_tm) * owner_rows) & (LANES - 1)] + send_quarters + keep_quarters
+        + [own_piece ^ flip for flip in flips] + sums_bits).astype(jnp.int32)
+
+    halo = shifted(
+        call(halo_kernel, shape((16, channels), BF16), [info, feats], flops=10 ** 11), "tm", 1)
+    weight, proj, codes = conv_weight, proj_weight, codes[0]
+    unfold, conv, chosen = call(
         local_kernel,
-        [shape((frames, width), BF16), shape((frames, channels), F32), shape((levels, frames, dz), BF16),
-         shape(conv_weight.shape, BF16), shape(proj_weight.shape, BF16)],
-        [info, feats, conv_weight, conv_bias[None, :], codes, codebooks, proj_weight],
-        anywhere=(1, 2, 5, 6),
-        scratch=[VMEM((rows_in, channels), BF16), VMEM(codebooks.shape, BF16),
-                 VMEM((channels // LANES, rows_in + 8, LANES), F32), pltpu.SemaphoreType.DMA((4,))],
-        flops=2 * frames * (width * channels + levels * book_size * dz),
+        [shape((frames, width), BF16), shape((frames, channels), F32), shape((levels, frames, dz), BF16)],
+        [info, feats, weight, conv_bias[None, :], codes, codebooks],
+        scratch=[VMEM((channels // LANES, rows_in + 8, LANES), F32)],
     )
 
     extra = 4 * (-(-channels // LANES // 8) * 8)
@@ -435,103 +461,91 @@
          shape((corr_rows + rows_b * (dz // LANES), LANES), BF16)],
         [info, halo, unfold, conv, chosen, weight, proj, codes],
         aliases={2: 0},
-        flops=2 * frames * (width * dz + 3 * channels * dz),
     )
     got = swapped(send, "dp", 1)
-    keep, hidden_grad, extras = call(
+    keep, hidden_grad, extras, row = call(
         functools.partial(rest_kernel, plan),
-        [shape((corr_rows, LANES), F32), shape((frames, channels), BF16), shape((extra, LANES), F32)],
+        [shape((corr_rows, LANES), F32), shape((frames, channels), BF16), shape((extra, LANES), F32),
+         shape((16, channels), BF16)],
         [info, flipped, unfold, hidden, latent_grad, proj],
         after=[send],
-        flops=2 * frames * (width * dz // 2 + channels * dz),
     )
-
-    def step(k, body, args, after):
+    after = shifted(row, "tm", -1)
+
+    def halves_at(k):
         nonlocal now_a, now_c
         halves = [(now_a * dz, a_split[k] is not None), (now_c * dz, c_split[k] is not None)]
         now_a = now_a // 2 if halves[0][1] else now_a
         now_c = now_c // 2 if halves[1][1] else now_c
-        rows = (now_a + now_c) * dz + extra
-        return call(
-            functools.partial(body, halves, k),
-            [shape((rows, LANES), BF16), shape((rows, LANES), F32)],
-            [info] + args, after=after)
-
-    def exchange(k, block):
-        axis, b, _ = exchanges[k]
-        return swapped(block, axis, 1 << b)
-
-    send, keep = step(1, first_step_kernel, [got, keep, extras], [])
-    got_x = exchange(1, send)
-    sums = call(
-        functools.partial(sums_kernel, corr_rows, at_codes),
-        [shape((per_shard + 16, dz), F32)] + [shape((per_shard + 16, dz), BF16)] * (tm - 1)
-        + [shape((16, channels), BF16)],
-        [info, got, own, hidden_grad],
-        after=[send],
-        flops=4 * frames * book_size * dz,
-    )
-    ring = [lax.ppermute(sums[shift], "tm", [(i, (i + shift) % tm) for i in range(tm)]) for shift in range(1, tm)]
-    after = shifted(sums[-1], "tm", -1)
-    send, keep = step(2, step_kernel, [got_x, keep], [sums[0]])
-    got = exchange(2, send)
-    feat_grad = call(
-        feat_kernel,
-        shape((rows_in, channels), BF16),
-        [info, hidden_grad, after, weight],
-        after=[send],
-        scratch=[VMEM((frames + 8, channels), F32), VMEM((channels // LANES, rows_in, LANES), F32)],
-        flops=2 * frames * width * channels,
-    )
-    last = feat_grad
-    sums_bits = list(range(1, dp_bits))
-    sums_now = None
-    for k in range(3, len(exchanges)):
-        send, keep = step(k, step_kernel, [got, keep], [last])
-        got = exchange(k, send)
-        if sums_now is None:
-            sums_now = call(sums_step_kernel, shape((per_shard + 16, dz), BF16),
-                            [info, sums[0]] + ring, after=[send])
-            last = sums_now
-        elif len(sums_bits) > 1:
-            sums_got = swapped(sums_now, "dp", 1 << sums_bits.pop(0))
-            sums_now = call(sums_step_kernel, shape((per_shard + 16, dz), BF16),
-                            [info, sums_now, sums_got], after=[send])
-            last = sums_now
-    assert now_a == 1
+        return halves, (now_a + now_c) * dz + extra
+
+    halves, rows = halves_at(1)
+    core_got = got
+    send, keep = call(
+        functools.partial(first_step_kernel, halves, 1),
+        [shape((rows, LANES), BF16), shape((rows, LANES), F32)],
+        [info, got, keep, extras])
+    got = swapped(send, exchanges[1][0], 1 << exchanges[1][1])
+    size = per_shard + 16
+    sums_rows = size * (tm // 2)
+    sums_send, sums_keep = call(
+        functools.partial(sums_kernel, corr_rows, frames, at_codes, per_shard),
+        [shape((sums_rows, dz), BF16), shape((sums_rows, dz), F32)],
+        [info, core_got, own],
+        after=[send])
+    sums_got = swapped(sums_send, sums_exchanges[0][0], 1 << sums_exchanges[0][1])
+
+    ordered = []
+    for k in range(2, len(exchanges)):
+        halves, rows = halves_at(k)
+        halved = sums_exchanges[k - 1][0] == "tm"
+        sums_rows = sums_rows // 2 if halved else sums_rows
+        pass_on = k == 3
+        outs = [shape((rows, LANES), BF16), shape((rows, LANES), F32),
+                shape((sums_rows, dz), BF16), shape((sums_rows, dz), F32)]
+        outs = call(
+            functools.partial(window_kernel, halves, k, halved, per_shard, at_sums + k - 1, pass_on),
+            outs + [shape((16, channels), BF16)] * pass_on,
+            [info, got, keep, sums_got, sums_keep] + [after] * pass_on,
+            after=ordered)
+        send, keep, sums_send, sums_keep = outs[:4]
+        after = outs[4] if pass_on else after
+        got = swapped(send, exchanges[k][0], 1 << exchanges[k][1])
+        sums_got = swapped(sums_send, sums_exchanges[k - 1][0], 1 << sums_exchanges[k - 1][1])
+        if pass_on:
+            feat_grad, *ordered = call(
+                feat_kernel,
+                shape((rows_in, channels), BF16),
+                [info, hidden_grad, after, weight],
+                after=[send],
+                token=True,
+                scratch=[VMEM((frames + 8, channels), F32), VMEM((channels // LANES, rows_in, LANES), F32)],
+            )
+    assert now_a == 1 and sums_rows == size
+
     first = now_a * dz
     second = first + now_c * dz
-
     piece, mine = call(
-        lambda info, *refs: last_kernel(first, second, *refs),
-        [shape((second - first, LANES), BF16), shape((second - first + extra, LANES), BF16)],
-        [info, got, keep], after=[last])
+        functools.partial(last_kernel, first, second, per_shard),
+        [shape((second - first, LANES), BF16),
+         shape((second - first + extra + size * (dz // LANES), LANES), BF16)],
+        [info, got, keep, sums_got, sums_keep])
     parts = [piece] + [swapped(mine if m == 1 else piece, "dp", m) for m in masks[1:]]
-    conv_grad = call(
+    conv_grad, last = call(
         functools.partial(conv_out_kernel, total_frames, at_start),
         shape((owner_rows, channels), F32),
         [info, got, keep, proj],
         after=[piece],
+        token=True,
         scratch=[VMEM((LANES, channels), F32)],
     )
-    while len(sums_bits) > 1:
-        sums_got = swapped(sums_now, "dp", 1 << sums_bits.pop(0))
-        sums_now = call(sums_step_kernel, shape((per_shard + 16, dz), BF16),
-                        [info, sums_now, sums_got], after=[conv_grad])
-    sums_got = swapped(sums_now, "dp", 1 << sums_bits.pop(0))
-    means = call(means_kernel, shape((per_shard + 16, dz), BF16), [info, sums_now, sums_got], after=[conv_grad])
-    other = swapped(means, "dp", 1)
-    proj_grad, bias_grad = call(
-        functools.partial(proj_out_kernel, total_frames, dz, at_pieces, now_c),
-        [shape((channels, dz), F32), shape((1, channels), F32)],
+    proj_grad, bias_grad, code_means, code_usage = call(
+        functools.partial(
+            out_kernel, total_frames, book_size / total_frames, per_shard, dz, at_pieces, now_c, extra),
+        [shape((channels, dz), F32), shape((1, channels), F32), shape((levels, per_shard, dz), BF16),
+         shape((levels, per_shard), F32)],
         [info, mine] + parts,
-        after=[means],
-    )
-    code_means, code_usage = call(
-        functools.partial(means_out_kernel, book_size / total_frames),
-        [shape((levels, per_shard, dz), BF16), shape((levels, per_shard), F32)],
-        [info, means, other],
-        after=[proj_grad],
+        after=[last],
     )
     return feat_grad, conv_grad, bias_grad[0], proj_grad, code_means, code_usage
 

time: 78.7 us -> 59.9 us (0.76)
  local copies, waits for them, and re-layouts: 10.1 us -> 1.25 us
  starting transfers between devices: 25.6 us -> 17.7 us
  Pallas kernels: 19.5 us -> 16.1 us
  waiting for transfers between devices: 22.1 us -> 23.9 us
    unnamed x18 -> x12, local copies, waits for them, and re-layouts: 9.34 us -> 1.15 us
    ppermute x3 -> x0, starting transfers between devices: 5.51 us -> none  [shards(): lax.ppermute(sums[shift], 'tm', [(i, (i + shift) % tm) for i in range(tm)])]
    pallas_call x16 -> x13, Pallas kernels: 19.5 us -> 16.1 us  [call(): pl.pallas_call(kernel, out_shape=shown, in_specs=specs, out_specs=[pl.Blo...]
    ppermute x11 -> x12, waiting for transfers between devices: 16.2 us -> 19.2 us  [swapped(): lax.ppermute(block, axis, [(i, i ^ mask) for i in range(lax.axis_size(axi...]
    ppermute x11 -> x12, starting transfers between devices: 13.9 us -> 11.3 us  [swapped(): lax.ppermute(block, axis, [(i, i ^ mask) for i in range(lax.axis_size(axi...]
    ppermute x2, waiting for transfers between devices: 5.92 us -> 4.63 us  [shifted(): return lax.ppermute(block, axis, route)]
  transfers between devices with their start and end apart: 16 -> 14, of which waited for: 7 -> 9; matrix products, arithmetic and copies ran while one was open for 0% -> 0% of each run, Pallas kernels for 19% -> 15%
where the time goes in v3:
time: 59.9 us; the launch traced here: 59.7 us
  waiting for transfers between devices  23.9 us (40%)
  starting transfers between devices  17.7 us (30%)
  Pallas kernels  16.1 us (27%)
  local copies, waits for them, and re-layouts  1.25 us (2%)
  between operations  0.82 us (1%)
    ppermute x12, waiting for transfers between devices, swapped(): lax.ppermute(block, axis, [(i, i ^ mask) for i in range(lax.axis_size(axi...  19.2 us
    pallas_call x13, Pallas kernels, call(): pl.pallas_call(kernel, out_shape=shown, in_specs=specs, out_specs=[pl.Blo...  16.1 us
    ppermute x12, starting transfers between devices, swapped(): lax.ppermute(block, axis, [(i, i ^ mask) for i in range(lax.axis_size(axi...  11.3 us
    ppermute x2, starting transfers between devices, shifted(): return lax.ppermute(block, axis, route)  6.34 us
    ppermute x2, waiting for transfers between devices, shifted(): return lax.ppermute(block, axis, route)  4.63 us
  transfers between devices with their start and end apart: 14, of which 9 were waited for; matrix products, arithmetic and copies ran while one was open for 0% of the time, Pallas kernels for 15%

profile of v3, /device:TPU:0, one launch (start us, length us, event | category | flops | bytes accessed | tf_op | source)
XLA Modules:
  0.0 59.7 jit_solution(10895260699008943303)
XLA Ops:
  0.8 1.1 %copy-done.3 = bf16[768,512]{1,0:T(8,128)(2,1)S(1)} copy-done((bf16[768,512]{1,0:T(8,128)(2,1)S(1)}, bf16[768,512]{1,0:T(8,128)(2,1)}, u32[]{:S(2)}) %copy-start.3) | copy-done | bytes 786456
  1.9 0.5 shard_map.109
  2.4 5.1 %collective-permute-start = (bf16[16,512]{1,0:T(8,128)(2,1)S(1)}, bf16[16,512]{1,0:T(8,128)(2,1)S(1)}, u32[]{:S(2)}, u32[]{:S(2)}) collective-permute-start(bf16[16,512]{1,0:T(8,128)(2,1)S(1)} %shard_map.109), channel_id=1, source_target_pairs={{0,1},{1,2},{2,3},{4,5},{5,6},{6,7},{8,9},{9,10},{10,11},{12,13},{... | collective-permute-start | bytes 49160 | tf_op jit(solution)/shard_map/ppermute | solution.py:383
  7.6 2.1 %shard_map.110 = (bf16[384,2048]{1,0:T(8,128)(2,1)S(1)}, f32[384,512]{1,0:T(8,128)S(1)}, bf16[2,384,256]{2,1,0:T(8,128)(2,1)S(1)}) custom-call(s32[18]{0:T(128)S(1)} %stack.63.refs_0_, bf16[768,512]{1,0:T(8,128)(2,1)S(1)} %copy-done.3, bf16[2048,512]{1,0:T(8,128)(2,1)S(1)} %copy-done, f32[1,512]{1,0:T(1,128)S(1)} %bitcast.19, s32[2,384]{1,0:T(2,128)S(1)} %bitcast.17, ...), custom_call_target="tpu_custom_call" | custom-call | tf_op jit(solution)/shard_map/pallas_call | solution.py:48
  9.7 1.7 %shard_map.111 = (bf16[384,2048]{1,0:T(8,128)(2,1)S(1)}, bf16[384,512]{1,0:T(8,128)(2,1)S(1)}, bf16[384,256]{1,0:T(8,128)(2,1)S(1)}, bf16[256,384]{1,0:T(8,128)(...) custom-call(s32[18]{0:T(128)S(1)} %stack.63.refs_0_, ...), custom_call_target="tpu_custom_call", output_to_operand_aliasing={{0}: (2, {})} | custom-call | tf_op jit(solution)/shard_map/pallas_call | solution.py:48
  11.5 1.2 %shard_map.112 = (f32[2560,128]{1,0:T(8,128)S(1)}, bf16[384,512]{1,0:T(8,128)(2,1)S(1)}, f32[32,128]{1,0:T(8,128)S(1)}, bf16[16,512]{1,0:T(8,128)(2,1)S(1)}) custom-call(s32[18]{0:T(128)S(1)} %stack.63.refs_0_, bf16[256,384]{1,0:T(8,128)(2,1)S(1)} %get-tuple-element.49.refs_1_, bf16[384,2048]{1,0:T(8,128)(2,1)S(1)} %get-tuple-element.50.refs_2_, ...), custom_call_target="tpu_custom_call" | custom-call | tf_op jit(solution)/shard_map/pallas_call | solution.py:48
  12.7 1.2 %collective-permute-done.1.refs_1_ = bf16[3360,128]{1,0:T(8,128)(2,1)S(1)} collective-permute-done((bf16[3360,128]{1,0:T(8,128)(2,1)S(1)}, bf16[3360,128]{1,0:T(8,128)(2,1)S(1)}, u32[]{:S(2)}, u32[]{:S(2)}) %collective-permute-start.1) | collective-permute-done | bytes 860192 | tf_op jit(solution)/shard_map/ppermute | solution.py:387
  13.8 0.7 %shard_map.113 = (bf16[1312,128]{1,0:T(8,128)(2,1)S(1)}, f32[1312,128]{1,0:T(8,128)S(1)}) custom-call(s32[18]{0:T(128)S(1)} %stack.63.refs_0_, bf16[3360,128]{1,0:T(8,128)(2,1)S(1)} %collective-permute-done.1.refs_1_, f32[2560,128]{1,0:T(8,128)S(1)} %get-tuple-element.55.refs_2_, f32[32,128]{1,0:T(8,128)S(1)} %get-tuple-element.56.refs_3_), custom_call_target="tpu_custom_call" | custom-call | tf_op jit(solution)/shard_map/pallas_call | solution.py:48
  14.5 1.5 %collective-permute-start.2 = (bf16[1312,128]{1,0:T(8,128)(2,1)S(1)}, bf16[1312,128]{1,0:T(8,128)(2,1)S(1)}, u32[]{:S(2)}, u32[]{:S(2)}) collective-permute-start(bf16[1312,128]{1,0:T(8,128)(2,1)S(1)} %get-tuple-element.57.refs_3_), channel_id=1, source_target_pairs={{0,8},{4,12},{8,0},{12,4},{16,24},{20,28},{24,16},{28,20},{1,9},{5... | collective-permute-start | bytes 1007624 | tf_op jit(solution)/shard_map/ppermute | solution.py:387
  16.1 1.6 %shard_map.114 = (bf16[544,256]{1,0:T(8,128)(2,1)S(1)}, f32[544,256]{1,0:T(8,128)S(1)}) custom-call(s32[18]{0:T(128)S(1)} %stack.63.refs_0_, bf16[3360,128]{1,0:T(8,128)(2,1)S(1)} %collective-permute-done.1.refs_1_, bf16[400,256]{1,0:T(8,128)(2,1)S(1)} %get-tuple-element.59.refs_2_, bf16[1312,128]{1,0:T(8,128)(2,1)S(1)} %get-tuple-element.57.refs_3_), custom_call_target="tpu_custom_call" | custom-call | tf_op jit(solution)/shard_map/pallas_call | solution.py:48
  17.7 1.6 %collective-permute-start.3 = (bf16[544,256]{1,0:T(8,128)(2,1)S(1)}, bf16[544,256]{1,0:T(8,128)(2,1)S(1)}, u32[]{:S(2)}, u32[]{:S(2)}) collective-permute-start(bf16[544,256]{1,0:T(8,128)(2,1)S(1)} %get-tuple-element.60), channel_id=1, source_target_pairs={{0,1},{1,0},{2,3},{3,2},{4,5},{5,4},{6,7},{7,6},{8,9},{9,8},{10,11... | collective-permute-start | bytes 835592 | tf_op jit(solution)/shard_map/ppermute | solution.py:387
  19.4 6.8 %collective-permute-done.3.refs_3_ = bf16[544,256]{1,0:T(8,128)(2,1)S(1)} collective-permute-done((bf16[544,256]{1,0:T(8,128)(2,1)S(1)}, bf16[544,256]{1,0:T(8,128)(2,1)S(1)}, u32[]{:S(2)}, u32[]{:S(2)}) %collective-permute-start.3) | collective-permute-done | bytes 278560 | tf_op jit(solution)/shard_map/ppermute | solution.py:387
  26.2 0.7 %shard_map.115 = (bf16[800,128]{1,0:T(8,128)(2,1)S(1)}, f32[800,128]{1,0:T(8,128)S(1)}, bf16[272,256]{1,0:T(8,128)(2,1)S(1)}, f32[272,256]{1,0:T(8,128)S(1)}) custom-call(s32[18]{0:T(128)S(1)} %stack.63.refs_0_, bf16[1312,128]{1,0:T(8,128)(2,1)S(1)} %collective-permute-done.2.refs_1_, f32[1312,128]{1,0:T(8,128)S(1)} %get-tuple-element.58.refs_2_, ...), custom_call_target="tpu_custom_call" | custom-call | tf_op jit(solution)/shard_map/pallas_call | solution.py:48
  26.9 1.6 %collective-permute-start.4 = (bf16[800,128]{1,0:T(8,128)(2,1)S(1)}, bf16[800,128]{1,0:T(8,128)(2,1)S(1)}, u32[]{:S(2)}, u32[]{:S(2)}) collective-permute-start(bf16[800,128]{1,0:T(8,128)(2,1)S(1)} %get-tuple-element.62), channel_id=1, source_target_pairs={{0,16},{4,20},{8,24},{12,28},{16,0},{20,4},{24,8},{28,12},{1,17},{... | collective-permute-start | bytes 614408 | tf_op jit(solution)/shard_map/ppermute | solution.py:387
  28.5 2.6 %collective-permute-start.5 = (bf16[272,256]{1,0:T(8,128)(2,1)S(1)}, bf16[272,256]{1,0:T(8,128)(2,1)S(1)}, u32[]{:S(2)}, u32[]{:S(2)}) collective-permute-start(bf16[272,256]{1,0:T(8,128)(2,1)S(1)} %get-tuple-element.64), channel_id=1, source_target_pairs={{0,2},{1,3},{2,0},{3,1},{4,6},{5,7},{6,4},{7,5},{8,10},{9,11},{10,... | collective-permute-start | bytes 417800 | tf_op jit(solution)/shard_map/ppermute | solution.py:387
  31.1 1.3 %collective-permute-start.6 = (bf16[16,512]{1,0:T(8,128)(2,1)S(1)}, bf16[16,512]{1,0:T(8,128)(2,1)S(1)}, u32[]{:S(2)}, u32[]{:S(2)}) collective-permute-start(bf16[16,512]{1,0:T(8,128)(2,1)S(1)} %get-tuple-element.66), channel_id=1, source_target_pairs={{1,0},{2,1},{3,2},{5,4},{6,5},{7,6},{9,8},{10,9},{11,10},{13,12},{... | collective-permute-start | bytes 49160 | tf_op jit(solution)/shard_map/ppermute | solution.py:383
  32.4 4.6 %collective-permute-done.6.refs_5_ = bf16[16,512]{1,0:T(8,128)(2,1)S(1)} collective-permute-done((bf16[16,512]{1,0:T(8,128)(2,1)S(1)}, bf16[16,512]{1,0:T(8,128)(2,1)S(1)}, u32[]{:S(2)}, u32[]{:S(2)}) %collective-permute-start.6) | collective-permute-done | bytes 16416 | tf_op jit(solution)/shard_map/ppermute | solution.py:383
  37.0 0.6 %shard_map.116 = (bf16[544,128]{1,0:T(8,128)(2,1)S(1)}, f32[544,128]{1,0:T(8,128)S(1)}, bf16[272,256]{1,0:T(8,128)(2,1)S(1)}, f32[272,256]{1,0:T(8,128)S(1)}, bf16[16,512]{1,0:T(8,128)(2,1)S(1)}) custom-call(s32[18]{0:T(128)S(1)} %stack.63.refs_0_, bf16[800,128]{1,0:T(8,128)(2,1)S(1)} %collective-permute-done.4.refs_1_, ...), custom_call_target="tpu_custom_call" | custom-call | tf_op jit(solution)/shard_map/pallas_call | solution.py:48
  37.6 0.6 collective-permute-start.8
  38.2 0.4 collective-permute-start.7
  38.7 2.6 %shard_map.117 = (bf16[768,512]{1,0:T(8,128)(2,1)}, f32[8,128]{1,0:T(8,128)S(1)}) custom-call(s32[18]{0:T(128)S(1)} %stack.63.refs_0_, bf16[384,512]{1,0:T(8,128)(2,1)S(1)} %get-tuple-element.54.refs_1_, bf16[16,512]{1,0:T(8,128)(2,1)S(1)} %get-tuple-element.67.refs_2_, bf16[2048,512]{1,0:T(8,128)(2,1)S(1)} %copy-done, ...), custom_call_target="tpu_custom_call" | custom-call | tf_op jit(solution)/shard_map/pallas_call | solution.py:48
  41.2 1.5 %collective-permute-done.8.refs_3_ = bf16[272,256]{1,0:T(8,128)(2,1)S(1)} collective-permute-done((bf16[272,256]{1,0:T(8,128)(2,1)S(1)}, bf16[272,256]{1,0:T(8,128)(2,1)S(1)}, u32[]{:S(2)}, u32[]{:S(2)}) %collective-permute-start.8) | collective-permute-done | bytes 139296 | tf_op jit(solution)/shard_map/ppermute | solution.py:387
  42.8 2.9 %collective-permute-done.7.refs_1_ = bf16[544,128]{1,0:T(8,128)(2,1)S(1)} collective-permute-done((bf16[544,128]{1,0:T(8,128)(2,1)S(1)}, bf16[544,128]{1,0:T(8,128)(2,1)S(1)}, u32[]{:S(2)}, u32[]{:S(2)}) %collective-permute-start.7) | collective-permute-done | bytes 139296 | tf_op jit(solution)/shard_map/ppermute | solution.py:387
  45.7 0.6 %shard_map.118 = (bf16[544,128]{1,0:T(8,128)(2,1)S(1)}, f32[544,128]{1,0:T(8,128)S(1)}, bf16[272,256]{1,0:T(8,128)(2,1)S(1)}, f32[272,256]{1,0:T(8,128)S(1)}) custom-call(s32[18]{0:T(128)S(1)} %stack.63.refs_0_, bf16[544,128]{1,0:T(8,128)(2,1)S(1)} %collective-permute-done.7.refs_1_, f32[544,128]{1,0:T(8,128)S(1)} %get-tuple-element.70.refs_2_, ...), custom_call_target="tpu_custom_call" | custom-call | tf_op jit(solution)/shard_map/pallas_call | solution.py:48
  46.4 0.6 collective-permute-start.10
  47.0 4.5 %collective-permute-done.9.refs_1_ = bf16[544,128]{1,0:T(8,128)(2,1)S(1)} collective-permute-done((bf16[544,128]{1,0:T(8,128)(2,1)S(1)}, bf16[544,128]{1,0:T(8,128)(2,1)S(1)}, u32[]{:S(2)}, u32[]{:S(2)}) %collective-permute-start.9) | collective-permute-done | bytes 139296 | tf_op jit(solution)/shard_map/ppermute | solution.py:387
  51.5 0.7 %shard_map.119 = (bf16[256,128]{1,0:T(8,128)(2,1)S(1)}, bf16[832,128]{1,0:T(8,128)(2,1)S(1)}) custom-call(s32[18]{0:T(128)S(1)} %stack.63.refs_0_, bf16[544,128]{1,0:T(8,128)(2,1)S(1)} %collective-permute-done.9.refs_1_, f32[544,128]{1,0:T(8,128)S(1)} %get-tuple-element.75.refs_2_, bf16[272,256]{1,0:T(8,128)(2,1)S(1)} %collective-permute-done.10.refs_3_, ...), custom_call_target="tpu_custom_call" | custom-call | tf_op jit(solution)/shard_map/pallas_call | solution.py:48
  52.3 1.6 %collective-permute-start.13 = (bf16[256,128]{1,0:T(8,128)(2,1)S(1)}, bf16[256,128]{1,0:T(8,128)(2,1)S(1)}, u32[]{:S(2)}, u32[]{:S(2)}) collective-permute-start(bf16[256,128]{1,0:T(8,128)(2,1)S(1)} %get-tuple-element.78.refs_4_.refs_2_), channel_id=1, source_target_pairs={{0,12},{4,8},{8,4},{12,0},{16,28},{20,24},{24,20},{28,16},{1,13},{... | collective-permute-start | bytes 196616 | tf_op jit(solution)/shard_map/ppermute | solution.py:387
  53.9 0.5 collective-permute-start.12
  54.4 1.5 %shard_map.120 = (f32[64,512]{1,0:T(8,128)}, f32[8,128]{1,0:T(8,128)S(1)}) custom-call(s32[18]{0:T(128)S(1)} %stack.63.refs_0_, bf16[544,128]{1,0:T(8,128)(2,1)S(1)} %collective-permute-done.9.refs_1_, f32[544,128]{1,0:T(8,128)S(1)} %get-tuple-element.75.refs_2_, bf16[512,256]{1,0:T(8,128)(2,1)S(1)} %copy-done.1, ...), custom_call_target="tpu_custom_call" | custom-call | tf_op jit(solution)/shard_map/pallas_call | solution.py:48
  56.3 1.8 %collective-permute-done.12.refs_4_ = bf16[256,128]{1,0:T(8,128)(2,1)S(1)} collective-permute-done((bf16[256,128]{1,0:T(8,128)(2,1)S(1)}, bf16[256,128]{1,0:T(8,128)(2,1)S(1)}, u32[]{:S(2)}, u32[]{:S(2)}) %collective-permute-start.12) | collective-permute-done | bytes 65568 | tf_op jit(solution)/shard_map/ppermute | solution.py:387
  58.2 1.5 %shard_map.121 = (f32[512,256]{1,0:T(8,128)}, f32[1,512]{1,0:T(1,128)}, bf16[2,256,256]{2,1,0:T(8,128)(2,1)}, f32[2,256]{1,0:T(2,128)}) custom-call(s32[18]{0:T(128)S(1)} %stack.63.refs_0_, bf16[832,128]{1,0:T(8,128)(2,1)S(1)} %get-tuple-element.80.refs_1_, bf16[256,128]{1,0:T(8,128)(2,1)S(1)} %get-tuple-element.78.refs_4_.refs_2_, ...), custom_call_target="tpu_custom_call" | custom-call | tf_op jit(solution)/shard_map/pallas_call | solution.py:48
  (22 shorter events, 0.8 us)
Async XLA Ops:
  0.7 1.1 %copy-start.3 = (bf16[768,512]{1,0:T(8,128)(2,1)S(1)}, bf16[768,512]{1,0:T(8,128)(2,1)}, u32[]{:S(2)}) copy-start(bf16[768,512]{1,0:T(8,128)(2,1)} %refs_1_.3) | copy-start | bytes 2359300
  1.9 5.6 %copy-start = (bf16[2048,512]{1,0:T(8,128)(2,1)S(1)}, bf16[2048,512]{1,0:T(8,128)(2,1)}, u32[]{:S(2)}) copy-start(bf16[2048,512]{1,0:T(8,128)(2,1)} %refs_3_.2) | copy-start | bytes 6291460
  1.9 5.6 %copy-start.2 = (bf16[2,1024,256]{2,1,0:T(8,128)(2,1)S(1)}, bf16[2,1024,256]{2,1,0:T(8,128)(2,1)}, u32[]{:S(2)}) copy-start(bf16[2,1024,256]{2,1,0:T(8,128)(2,1)} %refs_5_.3) | copy-start | bytes 3145732
  1.9 5.6 %copy-start.4 = (s32[1,2,384]{2,1,0:T(2,128)S(1)}, s32[1,2,384]{2,1,0:T(2,128)}, u32[]{:S(2)}) copy-start(s32[1,2,384]{2,1,0:T(2,128)} %param.7) | copy-start | bytes 9220
  1.9 5.7 %copy-start.5 = (f32[512]{0:T(512)S(1)}, f32[512]{0:T(512)}, u32[]{:S(2)}) copy-start(f32[512]{0:T(512)} %param.9) | copy-start | bytes 6148
  2.4 7.2 %collective-permute-start = (bf16[16,512]{1,0:T(8,128)(2,1)S(1)}, bf16[16,512]{1,0:T(8,128)(2,1)S(1)}, u32[]{:S(2)}, u32[]{:S(2)}) collective-permute-start(bf16[16,512]{1,0:T(8,128)(2,1)S(1)} %shard_map.109), channel_id=1, source_target_pairs={{0,1},{1,2},{2,3},{4,5},{5,6},{6,7},{8,9},{9,10},{10,11},{12,13},{... | collective-permute-start | bytes 49160 | tf_op jit(solution)/shard_map/ppermute | solution.py:383
  7.6 2.1 %copy-start.1 = (bf16[512,256]{1,0:T(8,128)(2,1)S(1)}, bf16[512,256]{1,0:T(8,128)(2,1)}, u32[]{:S(2)}) copy-start(bf16[512,256]{1,0:T(8,128)(2,1)} %refs_3_.3) | copy-start | bytes 786436
  11.4 2.5 %collective-permute-start.1 = (bf16[3360,128]{1,0:T(8,128)(2,1)S(1)}, bf16[3360,128]{1,0:T(8,128)(2,1)S(1)}, u32[]{:S(2)}, u32[]{:S(2)}) collective-permute-start(bf16[3360,128]{1,0:T(8,128)(2,1)S(1)} %get-tuple-element.53.refs_6_), channel_id=1, source_target_pairs={{0,4},{4,0},{8,12},{12,8},{16,20},{20,16},{24,28},{28,24},{1,5},{5... | collective-permute-start | bytes 2580488 | tf_op jit(solution)/shard_map/ppermute | solution.py:387
  14.5 11.7 %collective-permute-start.2 = (bf16[1312,128]{1,0:T(8,128)(2,1)S(1)}, bf16[1312,128]{1,0:T(8,128)(2,1)S(1)}, u32[]{:S(2)}, u32[]{:S(2)}) collective-permute-start(bf16[1312,128]{1,0:T(8,128)(2,1)S(1)} %get-tuple-element.57.refs_3_), channel_id=1, source_target_pairs={{0,8},{4,12},{8,0},{12,4},{16,24},{20,28},{24,16},{28,20},{1,9},{5... | collective-permute-start | bytes 1007624 | tf_op jit(solution)/shard_map/ppermute | solution.py:387
  17.7 8.5 %collective-permute-start.3 = (bf16[544,256]{1,0:T(8,128)(2,1)S(1)}, bf16[544,256]{1,0:T(8,128)(2,1)S(1)}, u32[]{:S(2)}, u32[]{:S(2)}) collective-permute-start(bf16[544,256]{1,0:T(8,128)(2,1)S(1)} %get-tuple-element.60), channel_id=1, source_target_pairs={{0,1},{1,0},{2,3},{3,2},{4,5},{5,4},{6,7},{7,6},{8,9},{9,8},{10,11... | collective-permute-start | bytes 835592 | tf_op jit(solution)/shard_map/ppermute | solution.py:387
  26.9 10.1 %collective-permute-start.4 = (bf16[800,128]{1,0:T(8,128)(2,1)S(1)}, bf16[800,128]{1,0:T(8,128)(2,1)S(1)}, u32[]{:S(2)}, u32[]{:S(2)}) collective-permute-start(bf16[800,128]{1,0:T(8,128)(2,1)S(1)} %get-tuple-element.62), channel_id=1, source_target_pairs={{0,16},{4,20},{8,24},{12,28},{16,0},{20,4},{24,8},{28,12},{1,17},{... | collective-permute-start | bytes 614408 | tf_op jit(solution)/shard_map/ppermute | solution.py:387
  28.5 8.5 %collective-permute-start.5 = (bf16[272,256]{1,0:T(8,128)(2,1)S(1)}, bf16[272,256]{1,0:T(8,128)(2,1)S(1)}, u32[]{:S(2)}, u32[]{:S(2)}) collective-permute-start(bf16[272,256]{1,0:T(8,128)(2,1)S(1)} %get-tuple-element.64), channel_id=1, source_target_pairs={{0,2},{1,3},{2,0},{3,1},{4,6},{5,7},{6,4},{7,5},{8,10},{9,11},{10,... | collective-permute-start | bytes 417800 | tf_op jit(solution)/shard_map/ppermute | solution.py:387
  31.1 5.9 %collective-permute-start.6 = (bf16[16,512]{1,0:T(8,128)(2,1)S(1)}, bf16[16,512]{1,0:T(8,128)(2,1)S(1)}, u32[]{:S(2)}, u32[]{:S(2)}) collective-permute-start(bf16[16,512]{1,0:T(8,128)(2,1)S(1)} %get-tuple-element.66), channel_id=1, source_target_pairs={{1,0},{2,1},{3,2},{5,4},{6,5},{7,6},{9,8},{10,9},{11,10},{13,12},{... | collective-permute-start | bytes 49160 | tf_op jit(solution)/shard_map/ppermute | solution.py:383
  37.6 5.1 %collective-permute-start.8 = (bf16[272,256]{1,0:T(8,128)(2,1)S(1)}, bf16[272,256]{1,0:T(8,128)(2,1)S(1)}, u32[]{:S(2)}, u32[]{:S(2)}) collective-permute-start(bf16[272,256]{1,0:T(8,128)(2,1)S(1)} %get-tuple-element.71), channel_id=1, source_target_pairs={{0,8},{4,12},{8,0},{12,4},{16,24},{20,28},{24,16},{28,20},{1,9},{5... | collective-permute-start | bytes 417800 | tf_op jit(solution)/shard_map/ppermute | solution.py:387
  38.2 7.4 %collective-permute-start.7 = (bf16[544,128]{1,0:T(8,128)(2,1)S(1)}, bf16[544,128]{1,0:T(8,128)(2,1)S(1)}, u32[]{:S(2)}, u32[]{:S(2)}) collective-permute-start(bf16[544,128]{1,0:T(8,128)(2,1)S(1)} %get-tuple-element.68.refs_4_), channel_id=1, source_target_pairs={{0,2},{1,3},{2,0},{3,1},{4,6},{5,7},{6,4},{7,5},{8,10},{9,11},{10,... | collective-permute-start | bytes 417800 | tf_op jit(solution)/shard_map/ppermute | solution.py:387
  46.3 5.1 %collective-permute-start.9 = (bf16[544,128]{1,0:T(8,128)(2,1)S(1)}, bf16[544,128]{1,0:T(8,128)(2,1)S(1)}, u32[]{:S(2)}, u32[]{:S(2)}) collective-permute-start(bf16[544,128]{1,0:T(8,128)(2,1)S(1)} %get-tuple-element.74), channel_id=1, source_target_pairs={{0,1},{1,0},{2,3},{3,2},{4,5},{5,4},{6,7},{7,6},{8,9},{9,8},{10,11... | collective-permute-start | bytes 417800 | tf_op jit(solution)/shard_map/ppermute | solution.py:387
  46.4 5.1 %collective-permute-start.10 = (bf16[272,256]{1,0:T(8,128)(2,1)S(1)}, bf16[272,256]{1,0:T(8,128)(2,1)S(1)}, u32[]{:S(2)}, u32[]{:S(2)}) collective-permute-start(bf16[272,256]{1,0:T(8,128)(2,1)S(1)} %get-tuple-element.76), channel_id=1, source_target_pairs={{0,16},{4,20},{8,24},{12,28},{16,0},{20,4},{24,8},{28,12},{1,17},{... | collective-permute-start | bytes 417800 | tf_op jit(solution)/shard_map/ppermute | solution.py:387
  52.2 6.0 %collective-permute-start.11 = (bf16[832,128]{1,0:T(8,128)(2,1)S(1)}, bf16[832,128]{1,0:T(8,128)(2,1)S(1)}, u32[]{:S(2)}, u32[]{:S(2)}) collective-permute-start(bf16[832,128]{1,0:T(8,128)(2,1)S(1)} %get-tuple-element.80.refs_1_), channel_id=1, source_target_pairs={{0,4},{4,0},{8,12},{12,8},{16,20},{20,16},{24,28},{28,24},{1,5},{5... | collective-permute-start | bytes 638984 | tf_op jit(solution)/shard_map/ppermute | solution.py:387
  52.3 4.0 %collective-permute-start.13 = (bf16[256,128]{1,0:T(8,128)(2,1)S(1)}, bf16[256,128]{1,0:T(8,128)(2,1)S(1)}, u32[]{:S(2)}, u32[]{:S(2)}) collective-permute-start(bf16[256,128]{1,0:T(8,128)(2,1)S(1)} %get-tuple-element.78.refs_4_.refs_2_), channel_id=1, source_target_pairs={{0,12},{4,8},{8,4},{12,0},{16,28},{20,24},{24,20},{28,16},{1,13},{... | collective-permute-start | bytes 196616 | tf_op jit(solution)/shard_map/ppermute | solution.py:387
  53.9 4.3 %collective-permute-start.12 = (bf16[256,128]{1,0:T(8,128)(2,1)S(1)}, bf16[256,128]{1,0:T(8,128)(2,1)S(1)}, u32[]{:S(2)}, u32[]{:S(2)}) collective-permute-start(bf16[256,128]{1,0:T(8,128)(2,1)S(1)} %get-tuple-element.78.refs_4_.refs_2_), channel_id=1, source_target_pairs={{0,8},{4,12},{8,0},{12,4},{16,24},{20,28},{24,16},{28,20},{1,9},{5... | collective-permute-start | bytes 196616 | tf_op jit(solution)/shard_map/ppermute | solution.py:387

commit v4 on v3

--- a/solution.py
+++ b/solution.py
@@ -180,8 +180,10 @@
         at += frames + code_rows
 
 
-def rest_kernel(plan, info, flipped, unfold, hidden, latent_grad, proj, keep, hidden_grad, extras, row):
-    correlate(flipped[...], (unfold, hidden), plan, info[0], keep)
+def rest_kernel(plan, info, flipped, unfold, hidden, latent_grad, proj, keep_a, keep_c, hidden_grad, extras, row):
+    bit = info[0]
+    correlate(flipped[...], (unfold,), plan[:1], bit, keep_a)
+    correlate(flipped[...], (hidden,), plan[1:], bit, keep_c)
     back = nt(latent_grad[...], proj[...]).astype(BF16)
     hidden_grad[...] = back
     row[...] = back[0:16, :]
@@ -193,25 +195,18 @@
             extras[digit * stride + j:digit * stride + j + 1, :] = part[:, j * LANES:(j + 1) * LANES]
 
 
-def split_sum(halves, bit, got, kept, send, keep):
-    at_in = 0
-    at_out = 0
-    for rows, halved in halves:
-        if halved:
-            half = rows // 2
-            away = pl.multiple_of(at_in + (1 - bit) * half, 16)
-            home = pl.multiple_of(at_in + bit * half, 16)
-            send[at_out:at_out + half, :] = (
-                kept[pl.ds(away, half), :] + got[pl.ds(away, half), :].astype(F32)).astype(BF16)
-            keep[at_out:at_out + half, :] = kept[pl.ds(home, half), :] + got[pl.ds(home, half), :].astype(F32)
-            at_out += half
-        else:
-            total = (kept[at_in:at_in + rows, :] + got[at_in:at_in + rows, :].astype(F32)).astype(BF16)
-            send[at_out:at_out + rows, :] = total
-            keep[at_out:at_out + rows, :] = total.astype(F32)
-            at_out += rows
-        at_in += rows
-    return at_in, at_out
+def split_sum(halved, bit, got, at, kept, rows, send, to, keep):
+    if halved:
+        half = rows // 2
+        away = pl.multiple_of((1 - bit) * half, 16)
+        home = pl.multiple_of(bit * half, 16)
+        send[to:to + half, :] = (kept[pl.ds(away, half), :] + got[pl.ds(at + away, half), :].astype(F32)).astype(BF16)
+        keep[0:half, :] = kept[pl.ds(home, half), :] + got[pl.ds(at + home, half), :].astype(F32)
+        return half
+    total = (kept[0:rows, :] + got[at:at + rows, :].astype(F32)).astype(BF16)
+    send[to:to + rows, :] = total
+    keep[0:rows, :] = total.astype(F32)
+    return rows
 
 
 def add_digits(mine, theirs):
@@ -224,10 +219,12 @@
     return jnp.concatenate(list(digits_of(value)) + [jnp.zeros_like(value)], 0)
 
 
-def first_step_kernel(halves, place, info, got, kept, extras, send, keep):
-    _, at = split_sum(halves, info[place], got, kept, send, keep)
-    send[at:, :] = extras[...].astype(BF16)
-    keep[at:, :] = extras[...]
+def first_step_kernel(halves, place, info, got, kept_a, kept_c, extras, send, keep_a, keep_c):
+    (rows_a, halved_a), (rows_c, halved_c) = halves
+    to = split_sum(halved_a, info[place], got, 0, kept_a, rows_a, send, 0, keep_a)
+    gone = split_sum(halved_c, info[place], got, rows_a, kept_c, rows_c, send, to, keep_c)
+    send[to + gone:, :] = extras[...].astype(BF16)
+    keep_c[gone:, :] = extras[...]
 
 
 def feat_kernel(info, grad, after, weight, out, wide, inter):
@@ -246,7 +243,21 @@
         out[:, j * LANES:(j + 1) * LANES] = inter[j].astype(BF16)
 
 
-def sums_kernel(first, frames, place, count, info, got, own, send, keep):
+def put_row(out, row):
+    wide = out.shape[1]
+    parts = row.shape[1] // wide
+    for j in range(parts):
+        top = out.shape[0] - (parts - j) * row.shape[0]
+        out[top:top + row.shape[0], :] = row[:, j * wide:(j + 1) * wide]
+
+
+def get_row(block, parts):
+    tall = 16
+    tops = [block.shape[0] - (parts - j) * tall for j in range(parts)]
+    return jnp.concatenate([block[top:top + tall, :] for top in tops], 1)
+
+
+def sums_kernel(first, frames, place, count, info, got, own, row, send, keep):
     rows, dz = own.shape
     theirs = jnp.concatenate([got[first + j * rows:first + (j + 1) * rows, :] for j in range(dz // LANES)], 1)
     ones = jnp.ones((8, frames), BF16)
@@ -254,8 +265,9 @@
     for block in (own[...], theirs):
         parts.append((block[0:frames, :], codes_of(block[frames:, :], frames)))
     size = count + 16
+    put_row(send, row[...])
     for out in (send, keep):
-        for top in range(0, out.shape[0], size):
+        for top in range(0, keep.shape[0], size):
             total = jnp.zeros((count, dz), F32)
             counts = jnp.zeros((8, count), F32)
             for values, codes in parts:
@@ -288,7 +300,7 @@
     half = kept.shape[0] // 2 if halved else 0
     outs = [(send, (1 - bit) * half), (keep, bit * half)] if halved else [(send, 0)]
     for out, start in outs:
-        for top in range(0, out.shape[0], size):
+        for top in range(0, keep.shape[0], size):
             here = top + pl.multiple_of(start, 16) if halved else top
             sums = pl.ds(here, count)
             tail = pl.ds(here + count, 16)
@@ -297,26 +309,40 @@
             out[top:top + count, :] = value.astype(out.dtype)
             out[top + count:top + size, :] = count_rows(number, dz).astype(out.dtype)
     if not halved:
-        keep[...] = send[...].astype(F32)
-
-
-def window_kernel(halves, place, sums_halved, sums_count, sums_place, pass_on, info, got, kept, sums_got, sums_kept,
-                  *refs):
-    if pass_on:
-        refs[-1][...] = refs[0][...]
-        refs = refs[1:-1]
-    send, keep, sums_send, sums_keep = refs
-    at_in, at_out = split_sum(halves, info[place], got, kept, send, keep)
-    block = digit_block(add_digits(kept[at_in:, :], got[at_in:, :].astype(F32)))
-    send[at_out:, :] = block.astype(BF16)
-    keep[at_out:, :] = block
+        keep[...] = send[0:keep.shape[0], :].astype(F32)
+
+
+def window_kernel(halves, at_c, place, apart, sums_plan, row_plan, info, got_a, got_c, kept_a, kept_c, sums_got,
+                  sums_kept, *refs):
+    (rows_a, halved_a), (rows_c, halved_c) = halves
+    sums_halved, sums_count, sums_place = sums_plan
+    row_step, row_parts, row_place = row_plan
+    if row_step is not None:
+        row = get_row(sums_got, row_parts)
+        before = refs[0][...] if row_step else jnp.zeros_like(row)
+        refs[-1][...] = jnp.where(info[row_place] == row_step, row, before)
+        refs = refs[1 if row_step else 0:-1]
+    if apart:
+        send_a, send_c, keep_a, keep_c, sums_send, sums_keep = refs
+    else:
+        send_a, keep_a, keep_c, sums_send, sums_keep = refs
+        send_c = send_a
+    to = split_sum(halved_a, info[place], got_a, 0, kept_a, rows_a, send_a, 0, keep_a)
+    to = 0 if apart else to
+    gone = split_sum(halved_c, info[place], got_c, at_c, kept_c, rows_c, send_c, to, keep_c)
+    block = digit_block(add_digits(kept_c[rows_c:, :], got_c[at_c + rows_c:, :].astype(F32)))
+    send_c[to + gone:, :] = block.astype(BF16)
+    keep_c[gone:, :] = block
     sums_step(sums_halved, sums_count, info[sums_place], sums_got, sums_kept, sums_send, sums_keep)
-
-
-def last_kernel(first, second, count, info, got, kept, sums_got, sums_kept, pieces, mine):
-    pieces[...] = (kept[first:second, :] + got[first:second, :].astype(F32)).astype(BF16)
-    block = digit_block(add_digits(kept[second:, :], got[second:, :].astype(F32)))
-    at = second - first
+    if row_step is not None and sums_send.shape[0] > sums_keep.shape[0]:
+        put_row(sums_send, row)
+
+
+def last_kernel(rows, count, info, got_a, kept_a, got, kept, sums_got, sums_kept, corr, pieces, mine):
+    corr[...] = kept_a[...] + got_a[...].astype(F32)
+    pieces[...] = (kept[0:rows, :] + got[0:rows, :].astype(F32)).astype(BF16)
+    block = digit_block(add_digits(kept[rows:, :], got[rows:, :].astype(F32)))
+    at = rows
     mine[0:at, :] = pieces[...]
     mine[at:at + block.shape[0], :] = block.astype(BF16)
     at += block.shape[0]
@@ -333,10 +359,9 @@
         at += count + 16
 
 
-def conv_out_kernel(total_frames, place, info, got, kept, proj, out, wide):
+def conv_out_kernel(total_frames, place, info, corr, proj, out, wide):
     rows = out.shape[0]
-    corr = kept[0:proj.shape[1], :] + got[0:proj.shape[1], :].astype(F32)
-    flipped = jnp.transpose(corr)
+    flipped = jnp.transpose(corr[...])
     high = flipped.astype(BF16)
     low = (flipped - high.astype(F32)).astype(BF16)
     wide[...] = (nt(high, proj[...]) + nt(low, proj[...])) * (1.0 / total_frames)
@@ -436,9 +461,11 @@
     at_codes = at_start + 1
     at_pieces = at_codes + tm
     at_sums = at_pieces + len(masks)
+    at_row = at_sums + len(sums_bits)
+    ones_below = sum(((at_tm + 1) & ((1 << (b + 1)) - 1) == 0).astype(jnp.int32) for b in range(tm_bits))
     info = jnp.stack(
         bits + [((at_dp * tm + at_tm) * owner_rows) & (LANES - 1)] + send_quarters + keep_quarters
-        + [own_piece ^ flip for flip in flips] + sums_bits).astype(jnp.int32)
+        + [own_piece ^ flip for flip in flips] + sums_bits + [ones_below]).astype(jnp.int32)
 
     halo = shifted(
         call(halo_kernel, shape((16, channels), BF16), [info, feats], flops=10 ** 11), "tm", 1)
@@ -463,78 +490,83 @@
         aliases={2: 0},
     )
     got = swapped(send, "dp", 1)
-    keep, hidden_grad, extras, row = call(
+    keep_a, keep_c, hidden_grad, extras, row = call(
         functools.partial(rest_kernel, plan),
-        [shape((corr_rows, LANES), F32), shape((frames, channels), BF16), shape((extra, LANES), F32),
-         shape((16, channels), BF16)],
+        [shape((now_a * dz, LANES), F32), shape((now_c * dz, LANES), F32), shape((frames, channels), BF16),
+         shape((extra, LANES), F32), shape((16, channels), BF16)],
         [info, flipped, unfold, hidden, latent_grad, proj],
         after=[send],
     )
-    after = shifted(row, "tm", -1)
 
     def halves_at(k):
         nonlocal now_a, now_c
         halves = [(now_a * dz, a_split[k] is not None), (now_c * dz, c_split[k] is not None)]
         now_a = now_a // 2 if halves[0][1] else now_a
         now_c = now_c // 2 if halves[1][1] else now_c
-        return halves, (now_a + now_c) * dz + extra
-
-    halves, rows = halves_at(1)
+        return halves, now_a * dz, now_c * dz + extra
+
+    halves, rows_a, rows_c = halves_at(1)
     core_got = got
-    send, keep = call(
+    send, keep_a, keep_c = call(
         functools.partial(first_step_kernel, halves, 1),
-        [shape((rows, LANES), BF16), shape((rows, LANES), F32)],
-        [info, got, keep, extras])
-    got = swapped(send, exchanges[1][0], 1 << exchanges[1][1])
+        [shape((rows_a + rows_c, LANES), BF16), shape((rows_a, LANES), F32), shape((rows_c, LANES), F32)],
+        [info, got, keep_a, keep_c, extras])
+    got_a = got_c = swapped(send, exchanges[1][0], 1 << exchanges[1][1])
     size = per_shard + 16
+    row_parts = channels // dz
     sums_rows = size * (tm // 2)
     sums_send, sums_keep = call(
         functools.partial(sums_kernel, corr_rows, frames, at_codes, per_shard),
-        [shape((sums_rows, dz), BF16), shape((sums_rows, dz), F32)],
-        [info, core_got, own],
+        [shape((sums_rows + 16 * row_parts, dz), BF16), shape((sums_rows, dz), F32)],
+        [info, core_got, own, row],
         after=[send])
     sums_got = swapped(sums_send, sums_exchanges[0][0], 1 << sums_exchanges[0][1])
-
+    after = None
     ordered = []
     for k in range(2, len(exchanges)):
-        halves, rows = halves_at(k)
+        at_c = now_a * dz if got_a is got_c else 0
+        halves, rows_a, rows_c = halves_at(k)
+        apart = k >= dp_bits
         halved = sums_exchanges[k - 1][0] == "tm"
         sums_rows = sums_rows // 2 if halved else sums_rows
-        pass_on = k == 3
-        outs = [shape((rows, LANES), BF16), shape((rows, LANES), F32),
-                shape((sums_rows, dz), BF16), shape((sums_rows, dz), F32)]
+        row_step = k - 2 if k - 2 < tm_bits else None
+        row_sent = 16 * row_parts * halved
+        sends = [rows_a, rows_c] if apart else [rows_a + rows_c]
+        outs = [shape((rows, LANES), BF16) for rows in sends] + [shape((rows, LANES), F32) for rows in (rows_a, rows_c)]
+        outs += [shape((sums_rows + row_sent, dz), BF16), shape((sums_rows, dz), F32)]
         outs = call(
-            functools.partial(window_kernel, halves, k, halved, per_shard, at_sums + k - 1, pass_on),
-            outs + [shape((16, channels), BF16)] * pass_on,
-            [info, got, keep, sums_got, sums_keep] + [after] * pass_on,
+            functools.partial(window_kernel, halves, at_c, k, apart, (halved, per_shard, at_sums + k - 1),
+                              (row_step, row_parts, at_row)),
+            outs + [shape((16, channels), BF16)] * (row_step is not None),
+            [info, got_a, got_c, keep_a, keep_c, sums_got, sums_keep] + [after] * bool(row_step),
             after=ordered)
-        send, keep, sums_send, sums_keep = outs[:4]
-        after = outs[4] if pass_on else after
-        got = swapped(send, exchanges[k][0], 1 << exchanges[k][1])
+        after = outs[-1] if row_step is not None else after
+        got_a = got_c = swapped(outs[0], exchanges[k][0], 1 << exchanges[k][1])
+        if apart:
+            got_c = swapped(outs[1], "tm", 1 << (k - dp_bits))
+        keep_a, keep_c, sums_send, sums_keep = outs[len(sends):len(sends) + 4]
         sums_got = swapped(sums_send, sums_exchanges[k - 1][0], 1 << sums_exchanges[k - 1][1])
-        if pass_on:
+        if k == tm_bits + 1:
             feat_grad, *ordered = call(
                 feat_kernel,
                 shape((rows_in, channels), BF16),
                 [info, hidden_grad, after, weight],
-                after=[send],
+                after=[outs[0]],
                 token=True,
                 scratch=[VMEM((frames + 8, channels), F32), VMEM((channels // LANES, rows_in, LANES), F32)],
             )
     assert now_a == 1 and sums_rows == size
 
-    first = now_a * dz
-    second = first + now_c * dz
-    piece, mine = call(
-        functools.partial(last_kernel, first, second, per_shard),
-        [shape((second - first, LANES), BF16),
-         shape((second - first + extra + size * (dz // LANES), LANES), BF16)],
-        [info, got, keep, sums_got, sums_keep])
+    corr, piece, mine = call(
+        functools.partial(last_kernel, rows_c - extra, per_shard),
+        [shape((rows_a, LANES), F32), shape((rows_c - extra, LANES), BF16), shape((rows_c + size * (dz // LANES), LANES), BF16)],
+        [info, got_a, keep_a, got_c, keep_c, sums_got, sums_keep],
+        after=ordered)
     parts = [piece] + [swapped(mine if m == 1 else piece, "dp", m) for m in masks[1:]]
     conv_grad, last = call(
         functools.partial(conv_out_kernel, total_frames, at_start),
         shape((owner_rows, channels), F32),
-        [info, got, keep, proj],
+        [info, corr, proj],
         after=[piece],
         token=True,
         scratch=[VMEM((LANES, channels), F32)],

time: 59.9 us -> 62 us (1.035)
  starting transfers between devices: 17.7 us -> 22.2 us
  waiting for transfers between devices: 23.9 us -> 21.5 us
    ppermute x12 -> x14, starting transfers between devices: 11.3 us -> 17.1 us  [swapped(): lax.ppermute(block, axis, [(i, i ^ mask) for i in range(lax.axis_size(axi...]
    ppermute x2 -> x1, waiting for transfers between devices: 4.63 us -> 0.01 us  [shifted(): return lax.ppermute(block, axis, route)]
    ppermute x12 -> x14, waiting for transfers between devices: 19.2 us -> 21.5 us  [swapped(): lax.ppermute(block, axis, [(i, i ^ mask) for i in range(lax.axis_size(axi...]
    ppermute x2 -> x1, starting transfers between devices: 6.34 us -> 5.06 us  [shifted(): return lax.ppermute(block, axis, route)]
  transfers between devices with their start and end apart: 14 -> 15, of which waited for: 9 -> 7; matrix products, arithmetic and copies ran while one was open for 0% -> 0% of each run, Pallas kernels for 15% -> 15%
where the time goes in v4:
time: 62 us; the launch traced here: 61.8 us
  starting transfers between devices  22.2 us (36%)
  waiting for transfers between devices  21.5 us (35%)
  Pallas kernels  16.1 us (26%)
  local copies, waits for them, and re-layouts  1.25 us (2%)
  between operations  0.81 us (1%)
    ppermute x14, waiting for transfers between devices, swapped(): lax.ppermute(block, axis, [(i, i ^ mask) for i in range(lax.axis_size(axi...  21.5 us
    ppermute x14, starting transfers between devices, swapped(): lax.ppermute(block, axis, [(i, i ^ mask) for i in range(lax.axis_size(axi...  17.1 us
    pallas_call x13, Pallas kernels, call(): pl.pallas_call(kernel, out_shape=shown, in_specs=specs, out_specs=[pl.Blo...  16.1 us
    ppermute x1, starting transfers between devices, shifted(): return lax.ppermute(block, axis, route)  5.06 us
  transfers between devices with their start and end apart: 15, of which 7 were waited for; matrix products, arithmetic and copies ran while one was open for 0% of the time, Pallas kernels for 15%

profile of v4, /device:TPU:0, one launch (start us, length us, event | category | flops | bytes accessed | tf_op | source)
XLA Modules:
  0.0 61.8 jit_solution(7988127422168861519)
XLA Ops:
  0.8 1.1 %copy-done.3 = bf16[768,512]{1,0:T(8,128)(2,1)S(1)} copy-done((bf16[768,512]{1,0:T(8,128)(2,1)S(1)}, bf16[768,512]{1,0:T(8,128)(2,1)}, u32[]{:S(2)}) %copy-start.3) | copy-done | bytes 786456
  1.9 0.5 shard_map.109
  2.5 5.1 %collective-permute-start = (bf16[16,512]{1,0:T(8,128)(2,1)S(1)}, bf16[16,512]{1,0:T(8,128)(2,1)S(1)}, u32[]{:S(2)}, u32[]{:S(2)}) collective-permute-start(bf16[16,512]{1,0:T(8,128)(2,1)S(1)} %shard_map.109), channel_id=1, source_target_pairs={{0,1},{1,2},{2,3},{4,5},{5,6},{6,7},{8,9},{9,10},{10,11},{12,13},{... | collective-permute-start | bytes 49160 | tf_op jit(solution)/shard_map/ppermute | solution.py:408
  7.6 2.1 %shard_map.110 = (bf16[384,2048]{1,0:T(8,128)(2,1)S(1)}, f32[384,512]{1,0:T(8,128)S(1)}, bf16[2,384,256]{2,1,0:T(8,128)(2,1)S(1)}) custom-call(s32[19]{0:T(128)S(1)} %stack.67.refs_0_, bf16[768,512]{1,0:T(8,128)(2,1)S(1)} %copy-done.3, bf16[2048,512]{1,0:T(8,128)(2,1)S(1)} %copy-done, f32[1,512]{1,0:T(1,128)S(1)} %bitcast.20, s32[2,384]{1,0:T(2,128)S(1)} %bitcast.18, ...), custom_call_target="tpu_custom_call" | custom-call | tf_op jit(solution)/shard_map/pallas_call | solution.py:48
  9.7 1.7 %shard_map.111 = (bf16[384,2048]{1,0:T(8,128)(2,1)S(1)}, bf16[384,512]{1,0:T(8,128)(2,1)S(1)}, bf16[384,256]{1,0:T(8,128)(2,1)S(1)}, bf16[256,384]{1,0:T(8,128)(...) custom-call(s32[19]{0:T(128)S(1)} %stack.67.refs_0_, ...), custom_call_target="tpu_custom_call", output_to_operand_aliasing={{0}: (2, {})} | custom-call | tf_op jit(solution)/shard_map/pallas_call | solution.py:48
  11.5 1.2 %shard_map.112 = (f32[2048,128]{1,0:T(8,128)S(1)}, f32[512,128]{1,0:T(8,128)S(1)}, bf16[384,512]{1,0:T(8,128)(2,1)S(1)}, f32[32,128]{1,0:T(8,128)S(1)}, bf16[16,512]{1,0:T(8,128)(2,1)S(1)}) custom-call(s32[19]{0:T(128)S(1)} %stack.67.refs_0_, bf16[256,384]{1,0:T(8,128)(2,1)S(1)} %get-tuple-element.58.refs_1_, ...), custom_call_target="tpu_custom_call" | custom-call | tf_op jit(solution)/shard_map/pallas_call | solution.py:48
  12.7 1.2 %collective-permute-done.1.refs_1_ = bf16[3360,128]{1,0:T(8,128)(2,1)S(1)} collective-permute-done((bf16[3360,128]{1,0:T(8,128)(2,1)S(1)}, bf16[3360,128]{1,0:T(8,128)(2,1)S(1)}, u32[]{:S(2)}, u32[]{:S(2)}) %collective-permute-start.1) | collective-permute-done | bytes 860192 | tf_op jit(solution)/shard_map/ppermute | solution.py:412
  13.9 0.7 %shard_map.113 = (bf16[1312,128]{1,0:T(8,128)(2,1)S(1)}, f32[1024,128]{1,0:T(8,128)S(1)}, f32[288,128]{1,0:T(8,128)S(1)}) custom-call(s32[19]{0:T(128)S(1)} %stack.67.refs_0_, bf16[3360,128]{1,0:T(8,128)(2,1)S(1)} %collective-permute-done.1.refs_1_, f32[2048,128]{1,0:T(8,128)S(1)} %get-tuple-element.64.refs_2_, f32[512,128]{1,0:T(8,128)S(1)} %get-tuple-element.65.refs_3_, ...), custom_call_target="tpu_custom_call" | custom-call | tf_op jit(solution)/shard_map/pallas_call | solution.py:48
  14.5 1.6 %collective-permute-start.2 = (bf16[1312,128]{1,0:T(8,128)(2,1)S(1)}, bf16[1312,128]{1,0:T(8,128)(2,1)S(1)}, u32[]{:S(2)}, u32[]{:S(2)}) collective-permute-start(bf16[1312,128]{1,0:T(8,128)(2,1)S(1)} %get-tuple-element.67.refs_4_), channel_id=1, source_target_pairs={{0,8},{4,12},{8,0},{12,4},{16,24},{20,28},{24,16},{28,20},{1,9},{5... | collective-permute-start | bytes 1007624 | tf_op jit(solution)/shard_map/ppermute | solution.py:412
  16.1 1.6 %shard_map.114 = (bf16[576,256]{1,0:T(8,128)(2,1)S(1)}, f32[544,256]{1,0:T(8,128)S(1)}) custom-call(s32[19]{0:T(128)S(1)} %stack.67.refs_0_, bf16[3360,128]{1,0:T(8,128)(2,1)S(1)} %collective-permute-done.1.refs_1_, bf16[400,256]{1,0:T(8,128)(2,1)S(1)} %get-tuple-element.70.refs_2_, bf16[16,512]{1,0:T(8,128)(2,1)S(1)} %get-tuple-element.71.refs_3_, ...), custom_call_target="tpu_custom_call" | custom-call | tf_op jit(solution)/shard_map/pallas_call | solution.py:48
  17.7 1.6 %collective-permute-start.3 = (bf16[576,256]{1,0:T(8,128)(2,1)S(1)}, bf16[576,256]{1,0:T(8,128)(2,1)S(1)}, u32[]{:S(2)}, u32[]{:S(2)}) collective-permute-start(bf16[576,256]{1,0:T(8,128)(2,1)S(1)} %get-tuple-element.72), channel_id=1, source_target_pairs={{0,1},{1,0},{2,3},{3,2},{4,5},{5,4},{6,7},{7,6},{8,9},{9,8},{10,11... | collective-permute-start | bytes 884744 | tf_op jit(solution)/shard_map/ppermute | solution.py:412
  19.4 7.2 %collective-permute-done.3.refs_5_ = bf16[576,256]{1,0:T(8,128)(2,1)S(1)} collective-permute-done((bf16[576,256]{1,0:T(8,128)(2,1)S(1)}, bf16[576,256]{1,0:T(8,128)(2,1)S(1)}, u32[]{:S(2)}, u32[]{:S(2)}) %collective-permute-start.3) | collective-permute-done | bytes 294944 | tf_op jit(solution)/shard_map/ppermute | solution.py:412
  26.6 0.7 %shard_map.115 = (bf16[800,128]{1,0:T(8,128)(2,1)S(1)}, f32[512,128]{1,0:T(8,128)S(1)}, f32[288,128]{1,0:T(8,128)S(1)}, bf16[304,256]{1,0:T(8,128)(2,1)S(1)}, f3...) custom-call(s32[19]{0:T(128)S(1)} %stack.67.refs_0_, bf16[1312,128]{1,0:T(8,128)(2,1)S(1)} %collective-permute-done.2.refs_1_.refs_2_, ...), custom_call_target="tpu_custom_call" | custom-call | tf_op jit(solution)/shard_map/pallas_call | solution.py:48
  27.2 1.6 %collective-permute-start.4 = (bf16[800,128]{1,0:T(8,128)(2,1)S(1)}, bf16[800,128]{1,0:T(8,128)(2,1)S(1)}, u32[]{:S(2)}, u32[]{:S(2)}) collective-permute-start(bf16[800,128]{1,0:T(8,128)(2,1)S(1)} %get-tuple-element.74), channel_id=1, source_target_pairs={{0,16},{4,20},{8,24},{12,28},{16,0},{20,4},{24,8},{28,12},{1,17},{... | collective-permute-start | bytes 614408 | tf_op jit(solution)/shard_map/ppermute | solution.py:412
  28.8 2.6 %collective-permute-start.5 = (bf16[304,256]{1,0:T(8,128)(2,1)S(1)}, bf16[304,256]{1,0:T(8,128)(2,1)S(1)}, u32[]{:S(2)}, u32[]{:S(2)}) collective-permute-start(bf16[304,256]{1,0:T(8,128)(2,1)S(1)} %get-tuple-element.77), channel_id=1, source_target_pairs={{0,2},{1,3},{2,0},{3,1},{4,6},{5,7},{6,4},{7,5},{8,10},{9,11},{10,... | collective-permute-start | bytes 466952 | tf_op jit(solution)/shard_map/ppermute | solution.py:412
  31.4 6.3 %collective-permute-done.5.refs_5_ = bf16[304,256]{1,0:T(8,128)(2,1)S(1)} collective-permute-done((bf16[304,256]{1,0:T(8,128)(2,1)S(1)}, bf16[304,256]{1,0:T(8,128)(2,1)S(1)}, u32[]{:S(2)}, u32[]{:S(2)}) %collective-permute-start.5) | collective-permute-done | bytes 155680 | tf_op jit(solution)/shard_map/ppermute | solution.py:412
  37.7 0.6 %shard_map.116 = (bf16[256,128]{1,0:T(8,128)(2,1)S(1)}, bf16[288,128]{1,0:T(8,128)(2,1)S(1)}, f32[256,128]{1,0:T(8,128)S(1)}, f32[288,128]{1,0:T(8,128)S(1)}, bf...) custom-call(s32[19]{0:T(128)S(1)} %stack.67.refs_0_, ...), custom_call_target="tpu_custom_call" | custom-call | tf_op jit(solution)/shard_map/pallas_call | solution.py:48
  38.3 0.6 %collective-permute-start.8 = (bf16[272,256]{1,0:T(8,128)(2,1)S(1)}, bf16[272,256]{1,0:T(8,128)(2,1)S(1)}, u32[]{:S(2)}, u32[]{:S(2)}) collective-permute-start(bf16[272,256]{1,0:T(8,128)(2,1)S(1)} %get-tuple-element.86), channel_id=1, source_target_pairs={{0,8},{4,12},{8,0},{12,4},{16,24},{20,28},{24,16},{28,20},{1,9},{5... | collective-permute-start | bytes 417800 | tf_op jit(solution)/shard_map/ppermute | solution.py:412
  39.0 0.7 %collective-permute-start.7 = (bf16[288,128]{1,0:T(8,128)(2,1)S(1)}, bf16[288,128]{1,0:T(8,128)(2,1)S(1)}, u32[]{:S(2)}, u32[]{:S(2)}) collective-permute-start(bf16[288,128]{1,0:T(8,128)(2,1)S(1)} %get-tuple-element.83), channel_id=1, source_target_pairs={{0,1},{1,0},{2,3},{3,2},{4,5},{5,4},{6,7},{7,6},{8,9},{9,8},{10,11... | collective-permute-start | bytes 221192 | tf_op jit(solution)/shard_map/ppermute | solution.py:412
  39.6 3.4 %collective-permute-start.6 = (bf16[256,128]{1,0:T(8,128)(2,1)S(1)}, bf16[256,128]{1,0:T(8,128)(2,1)S(1)}, u32[]{:S(2)}, u32[]{:S(2)}) collective-permute-start(bf16[256,128]{1,0:T(8,128)(2,1)S(1)} %get-tuple-element.81.refs_4_), channel_id=1, source_target_pairs={{0,2},{1,3},{2,0},{3,1},{4,6},{5,7},{6,4},{7,5},{8,10},{9,11},{10,... | collective-permute-start | bytes 196616 | tf_op jit(solution)/shard_map/ppermute | solution.py:412
  43.0 2.6 %shard_map.117 = (bf16[768,512]{1,0:T(8,128)(2,1)}, f32[8,128]{1,0:T(8,128)S(1)}) custom-call(s32[19]{0:T(128)S(1)} %stack.67.refs_0_, bf16[384,512]{1,0:T(8,128)(2,1)S(1)} %get-tuple-element.63.refs_1_, bf16[16,512]{1,0:T(8,128)(2,1)S(1)} %get-tuple-element.80.refs_2_, bf16[2048,512]{1,0:T(8,128)(2,1)S(1)} %copy-done, ...), custom_call_target="tpu_custom_call" | custom-call | tf_op jit(solution)/shard_map/pallas_call | solution.py:48
  45.6 0.4 collective-permute-done.6.refs_1_
  46.0 0.6 %shard_map.118 = (bf16[256,128]{1,0:T(8,128)(2,1)S(1)}, bf16[288,128]{1,0:T(8,128)(2,1)S(1)}, f32[256,128]{1,0:T(8,128)S(1)}, f32[288,128]{1,0:T(8,128)S(1)}, bf...) custom-call(s32[19]{0:T(128)S(1)} %stack.67.refs_0_, bf16[256,128]{1,0:T(8,128)(2,1)S(1)} %collective-permute-done.6.refs_1_, ...), custom_call_target="tpu_custom_call" | custom-call | tf_op jit(solution)/shard_map/pallas_call | solution.py:48
  46.6 0.6 collective-permute-start.11
  47.2 2.2 %collective-permute-start.10 = (bf16[288,128]{1,0:T(8,128)(2,1)S(1)}, bf16[288,128]{1,0:T(8,128)(2,1)S(1)}, u32[]{:S(2)}, u32[]{:S(2)}) collective-permute-start(bf16[288,128]{1,0:T(8,128)(2,1)S(1)} %get-tuple-element.91), channel_id=1, source_target_pairs={{0,2},{1,3},{2,0},{3,1},{4,6},{5,7},{6,4},{7,5},{8,10},{9,11},{10,... | collective-permute-start | bytes 221192 | tf_op jit(solution)/shard_map/ppermute | solution.py:412
  49.4 4.2 %collective-permute-done.9.refs_1_ = bf16[256,128]{1,0:T(8,128)(2,1)S(1)} collective-permute-done((bf16[256,128]{1,0:T(8,128)(2,1)S(1)}, bf16[256,128]{1,0:T(8,128)(2,1)S(1)}, u32[]{:S(2)}, u32[]{:S(2)}) %collective-permute-start.9) | collective-permute-done | bytes 65568 | tf_op jit(solution)/shard_map/ppermute | solution.py:412
  53.7 0.7 %shard_map.119 = (f32[256,128]{1,0:T(8,128)S(1)}, bf16[256,128]{1,0:T(8,128)(2,1)S(1)}, bf16[832,128]{1,0:T(8,128)(2,1)S(1)}) custom-call(s32[19]{0:T(128)S(1)} %stack.67.refs_0_, bf16[256,128]{1,0:T(8,128)(2,1)S(1)} %collective-permute-done.9.refs_1_, f32[256,128]{1,0:T(8,128)S(1)} %get-tuple-element.90.refs_2_, ...), custom_call_target="tpu_custom_call" | custom-call | tf_op jit(solution)/shard_map/pallas_call | solution.py:48
  54.4 1.6 %collective-permute-start.14 = (bf16[256,128]{1,0:T(8,128)(2,1)S(1)}, bf16[256,128]{1,0:T(8,128)(2,1)S(1)}, u32[]{:S(2)}, u32[]{:S(2)}) collective-permute-start(bf16[256,128]{1,0:T(8,128)(2,1)S(1)} %get-tuple-element.96.refs_3_.refs_2_), channel_id=1, source_target_pairs={{0,12},{4,8},{8,4},{12,0},{16,28},{20,24},{24,20},{28,16},{1,13},{... | collective-permute-start | bytes 196616 | tf_op jit(solution)/shard_map/ppermute | solution.py:412
  56.0 0.5 collective-permute-start.13
  56.6 1.5 %shard_map.120 = (f32[64,512]{1,0:T(8,128)}, f32[8,128]{1,0:T(8,128)S(1)}) custom-call(s32[19]{0:T(128)S(1)} %stack.67.refs_0_, f32[256,128]{1,0:T(8,128)S(1)} %get-tuple-element.95.refs_1_, bf16[512,256]{1,0:T(8,128)(2,1)S(1)} %copy-done.1, bf16[256,128]{1,0:T(8,128)(2,1)S(1)} %get-tuple-element.96.refs_3_.refs_2_), custom_call_target="tpu_custom_call" | custom-call | tf_op jit(solution)/shard_map/pallas_call | solution.py:48
  58.4 1.8 %collective-permute-done.13.refs_4_ = bf16[256,128]{1,0:T(8,128)(2,1)S(1)} collective-permute-done((bf16[256,128]{1,0:T(8,128)(2,1)S(1)}, bf16[256,128]{1,0:T(8,128)(2,1)S(1)}, u32[]{:S(2)}, u32[]{:S(2)}) %collective-permute-start.13) | collective-permute-done | bytes 65568 | tf_op jit(solution)/shard_map/ppermute | solution.py:412
  60.3 1.5 %shard_map.121 = (f32[512,256]{1,0:T(8,128)}, f32[1,512]{1,0:T(1,128)}, bf16[2,256,256]{2,1,0:T(8,128)(2,1)}, f32[2,256]{1,0:T(2,128)}) custom-call(s32[19]{0:T(128)S(1)} %stack.67.refs_0_, bf16[832,128]{1,0:T(8,128)(2,1)S(1)} %get-tuple-element.98.refs_1_, bf16[256,128]{1,0:T(8,128)(2,1)S(1)} %get-tuple-element.96.refs_3_.refs_2_, ...), custom_call_target="tpu_custom_call" | custom-call | tf_op jit(solution)/shard_map/pallas_call | solution.py:48
  (24 shorter events, 0.7 us)
Async XLA Ops:
  0.8 1.1 %copy-start.3 = (bf16[768,512]{1,0:T(8,128)(2,1)S(1)}, bf16[768,512]{1,0:T(8,128)(2,1)}, u32[]{:S(2)}) copy-start(bf16[768,512]{1,0:T(8,128)(2,1)} %refs_1_.3) | copy-start | bytes 2359300
  1.9 5.6 %copy-start = (bf16[2048,512]{1,0:T(8,128)(2,1)S(1)}, bf16[2048,512]{1,0:T(8,128)(2,1)}, u32[]{:S(2)}) copy-start(bf16[2048,512]{1,0:T(8,128)(2,1)} %refs_3_.1) | copy-start | bytes 6291460
  1.9 5.6 %copy-start.2 = (bf16[2,1024,256]{2,1,0:T(8,128)(2,1)S(1)}, bf16[2,1024,256]{2,1,0:T(8,128)(2,1)}, u32[]{:S(2)}) copy-start(bf16[2,1024,256]{2,1,0:T(8,128)(2,1)} %refs_5_.3) | copy-start | bytes 3145732
  1.9 5.6 %copy-start.4 = (s32[1,2,384]{2,1,0:T(2,128)S(1)}, s32[1,2,384]{2,1,0:T(2,128)}, u32[]{:S(2)}) copy-start(s32[1,2,384]{2,1,0:T(2,128)} %param.7) | copy-start | bytes 9220
  1.9 5.7 %copy-start.5 = (f32[512]{0:T(512)S(1)}, f32[512]{0:T(512)}, u32[]{:S(2)}) copy-start(f32[512]{0:T(512)} %param.9) | copy-start | bytes 6148
  2.5 7.2 %collective-permute-start = (bf16[16,512]{1,0:T(8,128)(2,1)S(1)}, bf16[16,512]{1,0:T(8,128)(2,1)S(1)}, u32[]{:S(2)}, u32[]{:S(2)}) collective-permute-start(bf16[16,512]{1,0:T(8,128)(2,1)S(1)} %shard_map.109), channel_id=1, source_target_pairs={{0,1},{1,2},{2,3},{4,5},{5,6},{6,7},{8,9},{9,10},{10,11},{12,13},{... | collective-permute-start | bytes 49160 | tf_op jit(solution)/shard_map/ppermute | solution.py:408
  7.6 2.1 %copy-start.1 = (bf16[512,256]{1,0:T(8,128)(2,1)S(1)}, bf16[512,256]{1,0:T(8,128)(2,1)}, u32[]{:S(2)}) copy-start(bf16[512,256]{1,0:T(8,128)(2,1)} %refs_2_.3) | copy-start | bytes 786436
  11.4 2.5 %collective-permute-start.1 = (bf16[3360,128]{1,0:T(8,128)(2,1)S(1)}, bf16[3360,128]{1,0:T(8,128)(2,1)S(1)}, u32[]{:S(2)}, u32[]{:S(2)}) collective-permute-start(bf16[3360,128]{1,0:T(8,128)(2,1)S(1)} %get-tuple-element.62.refs_6_), channel_id=1, source_target_pairs={{0,4},{4,0},{8,12},{12,8},{16,20},{20,16},{24,28},{28,24},{1,5},{5... | collective-permute-start | bytes 2580488 | tf_op jit(solution)/shard_map/ppermute | solution.py:412
  14.5 12.0 %collective-permute-start.2 = (bf16[1312,128]{1,0:T(8,128)(2,1)S(1)}, bf16[1312,128]{1,0:T(8,128)(2,1)S(1)}, u32[]{:S(2)}, u32[]{:S(2)}) collective-permute-start(bf16[1312,128]{1,0:T(8,128)(2,1)S(1)} %get-tuple-element.67.refs_4_), channel_id=1, source_target_pairs={{0,8},{4,12},{8,0},{12,4},{16,24},{20,28},{24,16},{28,20},{1,9},{5... | collective-permute-start | bytes 1007624 | tf_op jit(solution)/shard_map/ppermute | solution.py:412
  17.7 8.8 %collective-permute-start.3 = (bf16[576,256]{1,0:T(8,128)(2,1)S(1)}, bf16[576,256]{1,0:T(8,128)(2,1)S(1)}, u32[]{:S(2)}, u32[]{:S(2)}) collective-permute-start(bf16[576,256]{1,0:T(8,128)(2,1)S(1)} %get-tuple-element.72), channel_id=1, source_target_pairs={{0,1},{1,0},{2,3},{3,2},{4,5},{5,4},{6,7},{7,6},{8,9},{9,8},{10,11... | collective-permute-start | bytes 884744 | tf_op jit(solution)/shard_map/ppermute | solution.py:412
  27.2 10.4 %collective-permute-start.4 = (bf16[800,128]{1,0:T(8,128)(2,1)S(1)}, bf16[800,128]{1,0:T(8,128)(2,1)S(1)}, u32[]{:S(2)}, u32[]{:S(2)}) collective-permute-start(bf16[800,128]{1,0:T(8,128)(2,1)S(1)} %get-tuple-element.74), channel_id=1, source_target_pairs={{0,16},{4,20},{8,24},{12,28},{16,0},{20,4},{24,8},{28,12},{1,17},{... | collective-permute-start | bytes 614408 | tf_op jit(solution)/shard_map/ppermute | solution.py:412
  28.8 8.9 %collective-permute-start.5 = (bf16[304,256]{1,0:T(8,128)(2,1)S(1)}, bf16[304,256]{1,0:T(8,128)(2,1)S(1)}, u32[]{:S(2)}, u32[]{:S(2)}) collective-permute-start(bf16[304,256]{1,0:T(8,128)(2,1)S(1)} %get-tuple-element.77), channel_id=1, source_target_pairs={{0,2},{1,3},{2,0},{3,1},{4,6},{5,7},{6,4},{7,5},{8,10},{9,11},{10,... | collective-permute-start | bytes 466952 | tf_op jit(solution)/shard_map/ppermute | solution.py:412
  38.3 7.6 %collective-permute-start.8 = (bf16[272,256]{1,0:T(8,128)(2,1)S(1)}, bf16[272,256]{1,0:T(8,128)(2,1)S(1)}, u32[]{:S(2)}, u32[]{:S(2)}) collective-permute-start(bf16[272,256]{1,0:T(8,128)(2,1)S(1)} %get-tuple-element.86), channel_id=1, source_target_pairs={{0,8},{4,12},{8,0},{12,4},{16,24},{20,28},{24,16},{28,20},{1,9},{5... | collective-permute-start | bytes 417800 | tf_op jit(solution)/shard_map/ppermute | solution.py:412
  39.0 7.0 %collective-permute-start.7 = (bf16[288,128]{1,0:T(8,128)(2,1)S(1)}, bf16[288,128]{1,0:T(8,128)(2,1)S(1)}, u32[]{:S(2)}, u32[]{:S(2)}) collective-permute-start(bf16[288,128]{1,0:T(8,128)(2,1)S(1)} %get-tuple-element.83), channel_id=1, source_target_pairs={{0,1},{1,0},{2,3},{3,2},{4,5},{5,4},{6,7},{7,6},{8,9},{9,8},{10,11... | collective-permute-start | bytes 221192 | tf_op jit(solution)/shard_map/ppermute | solution.py:412
  39.6 6.3 %collective-permute-start.6 = (bf16[256,128]{1,0:T(8,128)(2,1)S(1)}, bf16[256,128]{1,0:T(8,128)(2,1)S(1)}, u32[]{:S(2)}, u32[]{:S(2)}) collective-permute-start(bf16[256,128]{1,0:T(8,128)(2,1)S(1)} %get-tuple-element.81.refs_4_), channel_id=1, source_target_pairs={{0,2},{1,3},{2,0},{3,1},{4,6},{5,7},{6,4},{7,5},{8,10},{9,11},{10,... | collective-permute-start | bytes 196616 | tf_op jit(solution)/shard_map/ppermute | solution.py:412
  46.6 7.1 %collective-permute-start.11 = (bf16[272,256]{1,0:T(8,128)(2,1)S(1)}, bf16[272,256]{1,0:T(8,128)(2,1)S(1)}, u32[]{:S(2)}, u32[]{:S(2)}) collective-permute-start(bf16[272,256]{1,0:T(8,128)(2,1)S(1)} %get-tuple-element.93), channel_id=1, source_target_pairs={{0,16},{4,20},{8,24},{12,28},{16,0},{20,4},{24,8},{28,12},{1,17},{... | collective-permute-start | bytes 417800 | tf_op jit(solution)/shard_map/ppermute | solution.py:412
  47.2 6.5 %collective-permute-start.10 = (bf16[288,128]{1,0:T(8,128)(2,1)S(1)}, bf16[288,128]{1,0:T(8,128)(2,1)S(1)}, u32[]{:S(2)}, u32[]{:S(2)}) collective-permute-start(bf16[288,128]{1,0:T(8,128)(2,1)S(1)} %get-tuple-element.91), channel_id=1, source_target_pairs={{0,2},{1,3},{2,0},{3,1},{4,6},{5,7},{6,4},{7,5},{8,10},{9,11},{10,... | collective-permute-start | bytes 221192 | tf_op jit(solution)/shard_map/ppermute | solution.py:412
  49.4 4.3 %collective-permute-start.9 = (bf16[256,128]{1,0:T(8,128)(2,1)S(1)}, bf16[256,128]{1,0:T(8,128)(2,1)S(1)}, u32[]{:S(2)}, u32[]{:S(2)}) collective-permute-start(bf16[256,128]{1,0:T(8,128)(2,1)S(1)} %get-tuple-element.89), channel_id=1, source_target_pairs={{0,1},{1,0},{2,3},{3,2},{4,5},{5,4},{6,7},{7,6},{8,9},{9,8},{10,11... | collective-permute-start | bytes 196616 | tf_op jit(solution)/shard_map/ppermute | solution.py:412
  54.3 5.9 %collective-permute-start.12 = (bf16[832,128]{1,0:T(8,128)(2,1)S(1)}, bf16[832,128]{1,0:T(8,128)(2,1)S(1)}, u32[]{:S(2)}, u32[]{:S(2)}) collective-permute-start(bf16[832,128]{1,0:T(8,128)(2,1)S(1)} %get-tuple-element.98.refs_1_), channel_id=1, source_target_pairs={{0,4},{4,0},{8,12},{12,8},{16,20},{20,16},{24,28},{28,24},{1,5},{5... | collective-permute-start | bytes 638984 | tf_op jit(solution)/shard_map/ppermute | solution.py:412
  54.4 4.0 %collective-permute-start.14 = (bf16[256,128]{1,0:T(8,128)(2,1)S(1)}, bf16[256,128]{1,0:T(8,128)(2,1)S(1)}, u32[]{:S(2)}, u32[]{:S(2)}) collective-permute-start(bf16[256,128]{1,0:T(8,128)(2,1)S(1)} %get-tuple-element.96.refs_3_.refs_2_), channel_id=1, source_target_pairs={{0,12},{4,8},{8,4},{12,0},{16,28},{20,24},{24,20},{28,16},{1,13},{... | collective-permute-start | bytes 196616 | tf_op jit(solution)/shard_map/ppermute | solution.py:412
  56.0 4.3 %collective-permute-start.13 = (bf16[256,128]{1,0:T(8,128)(2,1)S(1)}, bf16[256,128]{1,0:T(8,128)(2,1)S(1)}, u32[]{:S(2)}, u32[]{:S(2)}) collective-permute-start(bf16[256,128]{1,0:T(8,128)(2,1)S(1)} %get-tuple-element.96.refs_3_.refs_2_), channel_id=1, source_target_pairs={{0,8},{4,12},{8,0},{12,4},{16,24},{20,28},{24,16},{28,20},{1,9},{5... | collective-permute-start | bytes 196616 | tf_op jit(solution)/shard_map/ppermute | solution.py:412

commit v5 on v4

--- a/solution.py
+++ b/solution.py
@@ -73,8 +73,8 @@
 def one_hot(codes, axis_codes, first, count):
     frames = codes.shape[1 - axis_codes]
     dims = (count, frames) if axis_codes == 0 else (frames, count)
-    places = lax.broadcasted_iota(jnp.int32, dims, axis_codes) + first
-    return jnp.where(codes == places, 1.0, 0.0).astype(BF16)
+    places = lax.broadcasted_iota(jnp.int16, dims, axis_codes)
+    return jnp.where((codes - first).astype(jnp.int16) == places, jnp.ones((), BF16), jnp.zeros((), BF16))
 
 
 def halo_kernel(info, feats, out):
@@ -187,7 +187,7 @@
     back = nt(latent_grad[...], proj[...]).astype(BF16)
     hidden_grad[...] = back
     row[...] = back[0:16, :]
-    stride = extras.shape[0] // 4
+    stride = extras.shape[0] // 6
     extras[...] = jnp.zeros(extras.shape, F32)
     sums = jnp.sum(back.astype(F32), 0, keepdims=True)
     for digit, part in enumerate(digits_of(sums)):
@@ -210,13 +210,13 @@
 
 
 def add_digits(mine, theirs):
-    stride = mine.shape[0] // 4
+    stride = mine.shape[0] // 6
     return ((mine[0:stride] + mine[stride:2 * stride]) + mine[2 * stride:3 * stride]) + (
         (theirs[0:stride] + theirs[stride:2 * stride]) + theirs[2 * stride:3 * stride])
 
 
 def digit_block(value):
-    return jnp.concatenate(list(digits_of(value)) + [jnp.zeros_like(value)], 0)
+    return jnp.concatenate(list(digits_of(value)) + [jnp.zeros_like(value)] * 3, 0)
 
 
 def first_step_kernel(halves, place, info, got, kept_a, kept_c, extras, send, keep_a, keep_c):
@@ -243,20 +243,6 @@
         out[:, j * LANES:(j + 1) * LANES] = inter[j].astype(BF16)
 
 
-def put_row(out, row):
-    wide = out.shape[1]
-    parts = row.shape[1] // wide
-    for j in range(parts):
-        top = out.shape[0] - (parts - j) * row.shape[0]
-        out[top:top + row.shape[0], :] = row[:, j * wide:(j + 1) * wide]
-
-
-def get_row(block, parts):
-    tall = 16
-    tops = [block.shape[0] - (parts - j) * tall for j in range(parts)]
-    return jnp.concatenate([block[top:top + tall, :] for top in tops], 1)
-
-
 def sums_kernel(first, frames, place, count, info, got, own, row, send, keep):
     rows, dz = own.shape
     theirs = jnp.concatenate([got[first + j * rows:first + (j + 1) * rows, :] for j in range(dz // LANES)], 1)
@@ -265,7 +251,7 @@
     for block in (own[...], theirs):
         parts.append((block[0:frames, :], codes_of(block[frames:, :], frames)))
     size = count + 16
-    put_row(send, row[...])
+    riding = row[...].astype(F32)[0:1, :]
     for out in (send, keep):
         for top in range(0, keep.shape[0], size):
             total = jnp.zeros((count, dz), F32)
@@ -275,26 +261,34 @@
                 total = total + nn(matches, values)
                 counts = counts + nt(ones, matches)
             out[top:top + count, :] = total.astype(out.dtype)
-            out[top + count:top + size, :] = count_rows(counts[0:1], dz).astype(out.dtype)
+            out[top + count:top + size, :] = count_rows(counts[0:1], dz, riding).astype(out.dtype)
             place += 1
 
 
-def count_rows(count, width):
+def count_rows(count, width, riding=None):
     high = jnp.floor(count * (1.0 / 65536.0))
     rest = count - high * 65536.0
     middle = jnp.floor(rest * (1.0 / 256.0))
     low = rest - middle * 256.0
-    block = jnp.concatenate([high, middle, low, jnp.zeros((13, count.shape[1]), F32)], 0)
+    block = jnp.concatenate([high, middle, low], 0)
     if count.shape[1] < width:
-        block = jnp.concatenate([block, jnp.zeros((16, width - count.shape[1]), F32)], 1)
-    return block
+        block = jnp.concatenate([block, jnp.zeros((3, width - count.shape[1]), F32)], 1)
+    parts = [block]
+    if riding is not None:
+        parts += [riding[:, at:at + width] for at in range(0, riding.shape[1], width)]
+    parts.append(jnp.zeros((16 - sum(part.shape[0] for part in parts), width), F32))
+    return jnp.concatenate(parts, 0)
+
+
+def riding_row(block, parts):
+    return jnp.concatenate([block[3 + j:4 + j, :] for j in range(parts)], 1)
 
 
 def count_of(block, own):
     return (block[0:1] * 65536.0 + block[1:2] * 256.0 + block[2:3])[:, :own]
 
 
-def sums_step(halved, count, bit, got, kept, send, keep):
+def sums_step(halved, count, bit, riding, got, kept, send, keep):
     size = count + 16
     dz = got.shape[1]
     half = kept.shape[0] // 2 if halved else 0
@@ -307,9 +301,9 @@
             value = kept[sums, :].astype(F32) + got[sums, :].astype(F32)
             number = count_of(kept[tail, :].astype(F32), count) + count_of(got[tail, :].astype(F32), count)
             out[top:top + count, :] = value.astype(out.dtype)
-            out[top + count:top + size, :] = count_rows(number, dz).astype(out.dtype)
+            out[top + count:top + size, :] = count_rows(number, dz, riding).astype(out.dtype)
     if not halved:
-        keep[...] = send[0:keep.shape[0], :].astype(F32)
+        keep[...] = send[...].astype(F32)
 
 
 def window_kernel(halves, at_c, place, apart, sums_plan, row_plan, info, got_a, got_c, kept_a, kept_c, sums_got,
@@ -317,10 +311,12 @@
     (rows_a, halved_a), (rows_c, halved_c) = halves
     sums_halved, sums_count, sums_place = sums_plan
     row_step, row_parts, row_place = row_plan
+    row = None
     if row_step is not None:
-        row = get_row(sums_got, row_parts)
-        before = refs[0][...] if row_step else jnp.zeros_like(row)
-        refs[-1][...] = jnp.where(info[row_place] == row_step, row, before)
+        row = riding_row(sums_got[sums_count:sums_count + 16, :].astype(F32), row_parts)
+        wide = jnp.broadcast_to(row, refs[-1].shape)
+        before = refs[0][...].astype(F32) if row_step else jnp.zeros_like(wide)
+        refs[-1][...] = jnp.where(info[row_place] == row_step, wide, before).astype(BF16)
         refs = refs[1 if row_step else 0:-1]
     if apart:
         send_a, send_c, keep_a, keep_c, sums_send, sums_keep = refs
@@ -333,15 +329,13 @@
     block = digit_block(add_digits(kept_c[rows_c:, :], got_c[at_c + rows_c:, :].astype(F32)))
     send_c[to + gone:, :] = block.astype(BF16)
     keep_c[gone:, :] = block
-    sums_step(sums_halved, sums_count, info[sums_place], sums_got, sums_kept, sums_send, sums_keep)
-    if row_step is not None and sums_send.shape[0] > sums_keep.shape[0]:
-        put_row(sums_send, row)
-
-
-def last_kernel(rows, count, info, got_a, kept_a, got, kept, sums_got, sums_kept, corr, pieces, mine):
-    corr[...] = kept_a[...] + got_a[...].astype(F32)
-    pieces[...] = (kept[0:rows, :] + got[0:rows, :].astype(F32)).astype(BF16)
-    block = digit_block(add_digits(kept[rows:, :], got[rows:, :].astype(F32)))
+    sums_step(sums_halved, sums_count, info[sums_place], row, sums_got, sums_kept, sums_send, sums_keep)
+
+
+def last_kernel(rows, at_c, count, info, got_a, kept_a, got, kept, sums_got, sums_kept, corr, pieces, mine):
+    corr[...] = kept_a[...] + got_a[0:corr.shape[0], :].astype(F32)
+    pieces[...] = (kept[0:rows, :] + got[at_c:at_c + rows, :].astype(F32)).astype(BF16)
+    block = digit_block(add_digits(kept[rows:, :], got[at_c + rows:, :].astype(F32)))
     at = rows
     mine[0:at, :] = pieces[...]
     mine[at:at + block.shape[0], :] = block.astype(BF16)
@@ -375,16 +369,9 @@
         out[...] = taken
 
 
-def out_kernel(total_frames, use_scale, count, dz, place, inner, extra, info, mine, *refs):
-    parts, (out, bias, means, usage) = refs[:-4], refs[-4:]
-    scale = 1.0 / total_frames
-    for j, ref in enumerate(parts):
-        for k in range(inner):
-            start = pl.multiple_of((info[place + j] + k) * LANES, LANES)
-            out[pl.ds(start, LANES), :] = jnp.transpose(ref[k * dz:(k + 1) * dz, :].astype(F32)) * scale
-    theirs = parts[1]
-    top = inner * dz
-    value = add_digits(mine[top:top + extra, :].astype(F32), theirs[top:top + extra, :].astype(F32)) * scale
+def means_out_kernel(total_frames, use_scale, count, dz, top, extra, info, mine, theirs, bias, means, usage):
+    value = add_digits(mine[top:top + extra, :].astype(F32), theirs[top:top + extra, :].astype(F32)) * (
+        1.0 / total_frames)
     for j in range(bias.shape[1] // LANES):
         bias[:, j * LANES:(j + 1) * LANES] = value[j:j + 1, :]
     bit = info[0]
@@ -400,6 +387,15 @@
         numbers.append(count_of(whole[count:, :].astype(F32), count) * use_scale)
     usage[0:1, :] = jnp.where(bit == 1, numbers[1], numbers[0])
     usage[1:2, :] = jnp.where(bit == 1, numbers[0], numbers[1])
+
+
+def proj_out_kernel(total_frames, dz, place, inner, info, *refs):
+    parts, out = refs[:-1], refs[-1]
+    for j, ref in enumerate(parts):
+        for k in range(inner):
+            start = pl.multiple_of((info[place + j] + k) * LANES, LANES)
+            turned = jnp.transpose(ref[k * dz:(k + 1) * dz, :])
+            out[pl.ds(start, LANES), :] = turned.astype(F32) * (1.0 / total_frames)
 
 
 def shifted(block, axis, distance):
@@ -477,7 +473,7 @@
         scratch=[VMEM((channels // LANES, rows_in + 8, LANES), F32)],
     )
 
-    extra = 4 * (-(-channels // LANES // 8) * 8)
+    extra = 6 * (-(-channels // LANES // 8) * 8)
     code_rows = -(-(2 * -(-frames // dz)) // 16) * 16
     corr_rows = (now_a + now_c) * dz
     rows_b = frames + code_rows
@@ -517,7 +513,7 @@
     sums_rows = size * (tm // 2)
     sums_send, sums_keep = call(
         functools.partial(sums_kernel, corr_rows, frames, at_codes, per_shard),
-        [shape((sums_rows + 16 * row_parts, dz), BF16), shape((sums_rows, dz), F32)],
+        [shape((sums_rows, dz), BF16), shape((sums_rows, dz), F32)],
         [info, core_got, own, row],
         after=[send])
     sums_got = swapped(sums_send, sums_exchanges[0][0], 1 << sums_exchanges[0][1])
@@ -526,14 +522,13 @@
     for k in range(2, len(exchanges)):
         at_c = now_a * dz if got_a is got_c else 0
         halves, rows_a, rows_c = halves_at(k)
-        apart = k >= dp_bits
+        apart = k <= tm_bits
         halved = sums_exchanges[k - 1][0] == "tm"
         sums_rows = sums_rows // 2 if halved else sums_rows
         row_step = k - 2 if k - 2 < tm_bits else None
-        row_sent = 16 * row_parts * halved
         sends = [rows_a, rows_c] if apart else [rows_a + rows_c]
         outs = [shape((rows, LANES), BF16) for rows in sends] + [shape((rows, LANES), F32) for rows in (rows_a, rows_c)]
-        outs += [shape((sums_rows + row_sent, dz), BF16), shape((sums_rows, dz), F32)]
+        outs += [shape((sums_rows, dz), BF16), shape((sums_rows, dz), F32)]
         outs = call(
             functools.partial(window_kernel, halves, at_c, k, apart, (halved, per_shard, at_sums + k - 1),
                               (row_step, row_parts, at_row)),
@@ -543,7 +538,7 @@
         after = outs[-1] if row_step is not None else after
         got_a = got_c = swapped(outs[0], exchanges[k][0], 1 << exchanges[k][1])
         if apart:
-            got_c = swapped(outs[1], "tm", 1 << (k - dp_bits))
+            got_c = swapped(outs[1], exchanges[k][0], 1 << exchanges[k][1])
         keep_a, keep_c, sums_send, sums_keep = outs[len(sends):len(sends) + 4]
         sums_got = swapped(sums_send, sums_exchanges[k - 1][0], 1 << sums_exchanges[k - 1][1])
         if k == tm_bits + 1:
@@ -558,8 +553,9 @@
     assert now_a == 1 and sums_rows == size
 
     corr, piece, mine = call(
-        functools.partial(last_kernel, rows_c - extra, per_shard),
-        [shape((rows_a, LANES), F32), shape((rows_c - extra, LANES), BF16), shape((rows_c + size * (dz // LANES), LANES), BF16)],
+        functools.partial(last_kernel, rows_c - extra, rows_a if got_a is got_c else 0, per_shard),
+        [shape((rows_a, LANES), F32), shape((rows_c - extra, LANES), BF16),
+         shape((rows_c + size * (dz // LANES), LANES), BF16)],
         [info, got_a, keep_a, got_c, keep_c, sums_got, sums_keep],
         after=ordered)
     parts = [piece] + [swapped(mine if m == 1 else piece, "dp", m) for m in masks[1:]]
@@ -571,12 +567,18 @@
         token=True,
         scratch=[VMEM((LANES, channels), F32)],
     )
-    proj_grad, bias_grad, code_means, code_usage = call(
+    bias_grad, code_means, code_usage, last = call(
         functools.partial(
-            out_kernel, total_frames, book_size / total_frames, per_shard, dz, at_pieces, now_c, extra),
-        [shape((channels, dz), F32), shape((1, channels), F32), shape((levels, per_shard, dz), BF16),
-         shape((levels, per_shard), F32)],
-        [info, mine] + parts,
+            means_out_kernel, total_frames, book_size / total_frames, per_shard, dz, rows_c - extra, extra),
+        [shape((1, channels), F32), shape((levels, per_shard, dz), BF16), shape((levels, per_shard), F32)],
+        [info, mine, parts[1]],
+        after=[last],
+        token=True,
+    )
+    proj_grad = call(
+        functools.partial(proj_out_kernel, total_frames, dz, at_pieces, now_c),
+        shape((channels, dz), F32),
+        [info] + parts,
         after=[last],
     )
     return feat_grad, conv_grad, bias_grad[0], proj_grad, code_means, code_usage

time: 62 us -> 59.3 us (0.956)
  starting transfers between devices: 22.2 us -> 18.3 us
  Pallas kernels: 16.1 us -> 17.3 us
    ppermute x14 -> x13, starting transfers between devices: 17.1 us -> 13.2 us  [swapped(): lax.ppermute(block, axis, [(i, i ^ mask) for i in range(lax.axis_size(axi...]
    pallas_call x13 -> x14, Pallas kernels: 16.1 us -> 17.3 us  [call(): pl.pallas_call(kernel, out_shape=shown, in_specs=specs, out_specs=[pl.Blo...]
    ppermute x14 -> x13, waiting for transfers between devices: 21.5 us -> 21.5 us  [swapped(): lax.ppermute(block, axis, [(i, i ^ mask) for i in range(lax.axis_size(axi...]
  transfers between devices with their start and end apart: 15 -> 14, of which waited for: 7 -> 7; matrix products, arithmetic and copies ran while one was open for 0% -> 0% of each run, Pallas kernels for 15% -> 18%
where the time goes in v5:
time: 59.3 us; the launch traced here: 59.1 us
  waiting for transfers between devices  21.5 us (36%)
  starting transfers between devices  18.3 us (31%)
  Pallas kernels  17.3 us (29%)
  local copies, waits for them, and re-layouts  1.25 us (2%)
  between operations  0.82 us (1%)
    ppermute x13, waiting for transfers between devices, swapped(): lax.ppermute(block, axis, [(i, i ^ mask) for i in range(lax.axis_size(axi...  21.5 us
    pallas_call x14, Pallas kernels, call(): pl.pallas_call(kernel, out_shape=shown, in_specs=specs, out_specs=[pl.Blo...  17.3 us
    ppermute x13, starting transfers between devices, swapped(): lax.ppermute(block, axis, [(i, i ^ mask) for i in range(lax.axis_size(axi...  13.2 us
    ppermute x1, starting transfers between devices, shifted(): return lax.ppermute(block, axis, route)  5.06 us
  transfers between devices with their start and end apart: 14, of which 7 were waited for; matrix products, arithmetic and copies ran while one was open for 0% of the time, Pallas kernels for 18%

profile of v5, /device:TPU:0, one launch (start us, length us, event | category | flops | bytes accessed | tf_op | source)
XLA Modules:
  0.0 59.1 jit_solution(6348514823281577445)
XLA Ops:
  0.8 1.1 %copy-done.3 = bf16[768,512]{1,0:T(8,128)(2,1)S(1)} copy-done((bf16[768,512]{1,0:T(8,128)(2,1)S(1)}, bf16[768,512]{1,0:T(8,128)(2,1)}, u32[]{:S(2)}) %copy-start.3) | copy-done | bytes 786456
  1.9 0.5 shard_map.109
  2.5 5.1 %collective-permute-start = (bf16[16,512]{1,0:T(8,128)(2,1)S(1)}, bf16[16,512]{1,0:T(8,128)(2,1)S(1)}, u32[]{:S(2)}, u32[]{:S(2)}) collective-permute-start(bf16[16,512]{1,0:T(8,128)(2,1)S(1)} %shard_map.109), channel_id=1, source_target_pairs={{0,1},{1,2},{2,3},{4,5},{5,6},{6,7},{8,9},{9,10},{10,11},{12,13},{... | collective-permute-start | bytes 49160 | tf_op jit(solution)/shard_map/ppermute | solution.py:404
  7.6 2.2 %shard_map.110 = (bf16[384,2048]{1,0:T(8,128)(2,1)S(1)}, f32[384,512]{1,0:T(8,128)S(1)}, bf16[2,384,256]{2,1,0:T(8,128)(2,1)S(1)}) custom-call(s32[19]{0:T(128)S(1)} %stack.67.refs_0_, bf16[768,512]{1,0:T(8,128)(2,1)S(1)} %copy-done.3, bf16[2048,512]{1,0:T(8,128)(2,1)S(1)} %copy-done, f32[1,512]{1,0:T(1,128)S(1)} %bitcast.20, s32[2,384]{1,0:T(2,128)S(1)} %bitcast.18, ...), custom_call_target="tpu_custom_call" | custom-call | tf_op jit(solution)/shard_map/pallas_call | solution.py:48
  9.8 1.7 %shard_map.111 = (bf16[384,2048]{1,0:T(8,128)(2,1)S(1)}, bf16[384,512]{1,0:T(8,128)(2,1)S(1)}, bf16[384,256]{1,0:T(8,128)(2,1)S(1)}, bf16[256,384]{1,0:T(8,128)(...) custom-call(s32[19]{0:T(128)S(1)} %stack.67.refs_0_, ...), custom_call_target="tpu_custom_call", output_to_operand_aliasing={{0}: (2, {})} | custom-call | tf_op jit(solution)/shard_map/pallas_call | solution.py:48
  11.6 1.2 %shard_map.112 = (f32[2048,128]{1,0:T(8,128)S(1)}, f32[512,128]{1,0:T(8,128)S(1)}, bf16[384,512]{1,0:T(8,128)(2,1)S(1)}, f32[48,128]{1,0:T(8,128)S(1)}, bf16[16,512]{1,0:T(8,128)(2,1)S(1)}) custom-call(s32[19]{0:T(128)S(1)} %stack.67.refs_0_, bf16[256,384]{1,0:T(8,128)(2,1)S(1)} %get-tuple-element.57.refs_1_, ...), custom_call_target="tpu_custom_call" | custom-call | tf_op jit(solution)/shard_map/pallas_call | solution.py:48
  12.8 1.2 %collective-permute-done.1.refs_1_ = bf16[3360,128]{1,0:T(8,128)(2,1)S(1)} collective-permute-done((bf16[3360,128]{1,0:T(8,128)(2,1)S(1)}, bf16[3360,128]{1,0:T(8,128)(2,1)S(1)}, u32[]{:S(2)}, u32[]{:S(2)}) %collective-permute-start.1) | collective-permute-done | bytes 860192 | tf_op jit(solution)/shard_map/ppermute | solution.py:408
  14.0 0.7 %shard_map.113 = (bf16[1328,128]{1,0:T(8,128)(2,1)S(1)}, f32[1024,128]{1,0:T(8,128)S(1)}, f32[304,128]{1,0:T(8,128)S(1)}) custom-call(s32[19]{0:T(128)S(1)} %stack.67.refs_0_, bf16[3360,128]{1,0:T(8,128)(2,1)S(1)} %collective-permute-done.1.refs_1_, f32[2048,128]{1,0:T(8,128)S(1)} %get-tuple-element.63.refs_2_, f32[512,128]{1,0:T(8,128)S(1)} %get-tuple-element.64.refs_3_, ...), custom_call_target="tpu_custom_call" | custom-call | tf_op jit(solution)/shard_map/pallas_call | solution.py:48
  14.6 1.6 %collective-permute-start.2 = (bf16[1328,128]{1,0:T(8,128)(2,1)S(1)}, bf16[1328,128]{1,0:T(8,128)(2,1)S(1)}, u32[]{:S(2)}, u32[]{:S(2)}) collective-permute-start(bf16[1328,128]{1,0:T(8,128)(2,1)S(1)} %get-tuple-element.66.refs_4_), channel_id=1, source_target_pairs={{0,8},{4,12},{8,0},{12,4},{16,24},{20,28},{24,16},{28,20},{1,9},{5... | collective-permute-start | bytes 1019912 | tf_op jit(solution)/shard_map/ppermute | solution.py:408
  16.2 1.6 %shard_map.114 = (bf16[544,256]{1,0:T(8,128)(2,1)S(1)}, f32[544,256]{1,0:T(8,128)S(1)}) custom-call(s32[19]{0:T(128)S(1)} %stack.67.refs_0_, bf16[3360,128]{1,0:T(8,128)(2,1)S(1)} %collective-permute-done.1.refs_1_, bf16[400,256]{1,0:T(8,128)(2,1)S(1)} %get-tuple-element.69.refs_2_, bf16[16,512]{1,0:T(8,128)(2,1)S(1)} %get-tuple-element.70.refs_3_, ...), custom_call_target="tpu_custom_call" | custom-call | tf_op jit(solution)/shard_map/pallas_call | solution.py:48
  17.8 1.6 %collective-permute-start.3 = (bf16[544,256]{1,0:T(8,128)(2,1)S(1)}, bf16[544,256]{1,0:T(8,128)(2,1)S(1)}, u32[]{:S(2)}, u32[]{:S(2)}) collective-permute-start(bf16[544,256]{1,0:T(8,128)(2,1)S(1)} %get-tuple-element.71), channel_id=1, source_target_pairs={{0,1},{1,0},{2,3},{3,2},{4,5},{5,4},{6,7},{7,6},{8,9},{9,8},{10,11... | collective-permute-start | bytes 835592 | tf_op jit(solution)/shard_map/ppermute | solution.py:408
  19.4 6.8 %collective-permute-done.3.refs_5_ = bf16[544,256]{1,0:T(8,128)(2,1)S(1)} collective-permute-done((bf16[544,256]{1,0:T(8,128)(2,1)S(1)}, bf16[544,256]{1,0:T(8,128)(2,1)S(1)}, u32[]{:S(2)}, u32[]{:S(2)}) %collective-permute-start.3) | collective-permute-done | bytes 278560 | tf_op jit(solution)/shard_map/ppermute | solution.py:408
  26.3 0.7 %shard_map.115 = (bf16[512,128]{1,0:T(8,128)(2,1)S(1)}, bf16[304,128]{1,0:T(8,128)(2,1)S(1)}, f32[512,128]{1,0:T(8,128)S(1)}, f32[304,128]{1,0:T(8,128)S(1)}, bf...) custom-call(s32[19]{0:T(128)S(1)} %stack.67.refs_0_, ...), custom_call_target="tpu_custom_call" | custom-call | tf_op jit(solution)/shard_map/pallas_call | solution.py:48
  27.0 2.7 %collective-permute-start.6 = (bf16[272,256]{1,0:T(8,128)(2,1)S(1)}, bf16[272,256]{1,0:T(8,128)(2,1)S(1)}, u32[]{:S(2)}, u32[]{:S(2)}) collective-permute-start(bf16[272,256]{1,0:T(8,128)(2,1)S(1)} %get-tuple-element.77), channel_id=1, source_target_pairs={{0,2},{1,3},{2,0},{3,1},{4,6},{5,7},{6,4},{7,5},{8,10},{9,11},{10,... | collective-permute-start | bytes 417800 | tf_op jit(solution)/shard_map/ppermute | solution.py:408
  29.6 1.5 %collective-permute-start.4 = (bf16[512,128]{1,0:T(8,128)(2,1)S(1)}, bf16[512,128]{1,0:T(8,128)(2,1)S(1)}, u32[]{:S(2)}, u32[]{:S(2)}) collective-permute-start(bf16[512,128]{1,0:T(8,128)(2,1)S(1)} %get-tuple-element.73), channel_id=1, source_target_pairs={{0,16},{4,20},{8,24},{12,28},{16,0},{20,4},{24,8},{28,12},{1,17},{... | collective-permute-start | bytes 393224 | tf_op jit(solution)/shard_map/ppermute | solution.py:408
  31.7 3.9 %collective-permute-done.5.refs_2_ = bf16[304,128]{1,0:T(8,128)(2,1)S(1)} collective-permute-done((bf16[304,128]{1,0:T(8,128)(2,1)S(1)}, bf16[304,128]{1,0:T(8,128)(2,1)S(1)}, u32[]{:S(2)}, u32[]{:S(2)}) %collective-permute-start.5) | collective-permute-done | bytes 77856 | tf_op jit(solution)/shard_map/ppermute | solution.py:408
  35.6 0.6 %shard_map.116 = (bf16[560,128]{1,0:T(8,128)(2,1)S(1)}, f32[256,128]{1,0:T(8,128)S(1)}, f32[304,128]{1,0:T(8,128)S(1)}, bf16[272,256]{1,0:T(8,128)(2,1)S(1)}, f3...) custom-call(s32[19]{0:T(128)S(1)} %stack.67.refs_0_, bf16[512,128]{1,0:T(8,128)(2,1)S(1)} %collective-permute-done.4.refs_1_, ...), custom_call_target="tpu_custom_call" | custom-call | tf_op jit(solution)/shard_map/pallas_call | solution.py:48
  36.6 0.5 collective-permute-start.8
  37.1 2.6 %shard_map.117 = (bf16[768,512]{1,0:T(8,128)(2,1)}, f32[8,128]{1,0:T(8,128)S(1)}) custom-call(s32[19]{0:T(128)S(1)} %stack.67.refs_0_, bf16[384,512]{1,0:T(8,128)(2,1)S(1)} %get-tuple-element.62.refs_1_, bf16[16,512]{1,0:T(8,128)(2,1)S(1)} %get-tuple-element.80.refs_2_, bf16[2048,512]{1,0:T(8,128)(2,1)S(1)} %copy-done, ...), custom_call_target="tpu_custom_call" | custom-call | tf_op jit(solution)/shard_map/pallas_call | solution.py:48
  39.7 2.0 %collective-permute-done.8.refs_5_ = bf16[272,256]{1,0:T(8,128)(2,1)S(1)} collective-permute-done((bf16[272,256]{1,0:T(8,128)(2,1)S(1)}, bf16[272,256]{1,0:T(8,128)(2,1)S(1)}, u32[]{:S(2)}, u32[]{:S(2)}) %collective-permute-start.8) | collective-permute-done | bytes 139296 | tf_op jit(solution)/shard_map/ppermute | solution.py:408
  41.7 3.1 %collective-permute-done.7.refs_1_.refs_2_ = bf16[560,128]{1,0:T(8,128)(2,1)S(1)} collective-permute-done((bf16[560,128]{1,0:T(8,128)(2,1)S(1)}, bf16[560,128]{1,0:T(8,128)(2,1)S(1)}, u32[]{:S(2)}, u32[]{:S(2)}) %collective-permute-start.7) | collective-permute-done | bytes 143392 | tf_op jit(solution)/shard_map/ppermute | solution.py:408
  44.8 0.6 %shard_map.118 = (bf16[560,128]{1,0:T(8,128)(2,1)S(1)}, f32[256,128]{1,0:T(8,128)S(1)}, f32[304,128]{1,0:T(8,128)S(1)}, bf16[272,256]{1,0:T(8,128)(2,1)S(1)}, f32[272,256]{1,0:T(8,128)S(1)}) custom-call(s32[19]{0:T(128)S(1)} %stack.67.refs_0_, bf16[560,128]{1,0:T(8,128)(2,1)S(1)} %collective-permute-done.7.refs_1_.refs_2_, ...), custom_call_target="tpu_custom_call" | custom-call | tf_op jit(solution)/shard_map/pallas_call | solution.py:48
  45.4 0.6 %collective-permute-start.9 = (bf16[560,128]{1,0:T(8,128)(2,1)S(1)}, bf16[560,128]{1,0:T(8,128)(2,1)S(1)}, u32[]{:S(2)}, u32[]{:S(2)}) collective-permute-start(bf16[560,128]{1,0:T(8,128)(2,1)S(1)} %get-tuple-element.88), channel_id=1, source_target_pairs={{0,1},{1,0},{2,3},{3,2},{4,5},{5,4},{6,7},{7,6},{8,9},{9,8},{10,11... | collective-permute-start | bytes 430088 | tf_op jit(solution)/shard_map/ppermute | solution.py:408
  46.0 1.5 %collective-permute-start.10 = (bf16[272,256]{1,0:T(8,128)(2,1)S(1)}, bf16[272,256]{1,0:T(8,128)(2,1)S(1)}, u32[]{:S(2)}, u32[]{:S(2)}) collective-permute-start(bf16[272,256]{1,0:T(8,128)(2,1)S(1)} %get-tuple-element.91), channel_id=1, source_target_pairs={{0,16},{4,20},{8,24},{12,28},{16,0},{20,4},{24,8},{28,12},{1,17},{... | collective-permute-start | bytes 417800 | tf_op jit(solution)/shard_map/ppermute | solution.py:408
  47.5 3.5 %collective-permute-done.10.refs_5_ = bf16[272,256]{1,0:T(8,128)(2,1)S(1)} collective-permute-done((bf16[272,256]{1,0:T(8,128)(2,1)S(1)}, bf16[272,256]{1,0:T(8,128)(2,1)S(1)}, u32[]{:S(2)}, u32[]{:S(2)}) %collective-permute-start.10) | collective-permute-done | bytes 139296 | tf_op jit(solution)/shard_map/ppermute | solution.py:408
  51.1 0.7 %shard_map.119 = (f32[256,128]{1,0:T(8,128)S(1)}, bf16[256,128]{1,0:T(8,128)(2,1)S(1)}, bf16[848,128]{1,0:T(8,128)(2,1)S(1)}) custom-call(s32[19]{0:T(128)S(1)} %stack.67.refs_0_, bf16[560,128]{1,0:T(8,128)(2,1)S(1)} %collective-permute-done.9.refs_1_.refs_3_, f32[256,128]{1,0:T(8,128)S(1)} %get-tuple-element.89.refs_2_, ...), custom_call_target="tpu_custom_call" | custom-call | tf_op jit(solution)/shard_map/pallas_call | solution.py:48
  51.8 0.7 %collective-permute-start.13 = (bf16[256,128]{1,0:T(8,128)(2,1)S(1)}, bf16[256,128]{1,0:T(8,128)(2,1)S(1)}, u32[]{:S(2)}, u32[]{:S(2)}) collective-permute-start(bf16[256,128]{1,0:T(8,128)(2,1)S(1)} %get-tuple-element.94.refs_3_.refs_1_), channel_id=1, source_target_pairs={{0,12},{4,8},{8,4},{12,0},{16,28},{20,24},{24,20},{28,16},{1,13},{... | collective-permute-start | bytes 196616 | tf_op jit(solution)/shard_map/ppermute | solution.py:408
  52.5 1.5 %collective-permute-start.12 = (bf16[256,128]{1,0:T(8,128)(2,1)S(1)}, bf16[256,128]{1,0:T(8,128)(2,1)S(1)}, u32[]{:S(2)}, u32[]{:S(2)}) collective-permute-start(bf16[256,128]{1,0:T(8,128)(2,1)S(1)} %get-tuple-element.94.refs_3_.refs_1_), channel_id=1, source_target_pairs={{0,8},{4,12},{8,0},{12,4},{16,24},{20,28},{24,16},{28,20},{1,9},{5... | collective-permute-start | bytes 196616 | tf_op jit(solution)/shard_map/ppermute | solution.py:408
  54.0 1.5 %shard_map.120 = (f32[64,512]{1,0:T(8,128)}, f32[8,128]{1,0:T(8,128)S(1)}) custom-call(s32[19]{0:T(128)S(1)} %stack.67.refs_0_, f32[256,128]{1,0:T(8,128)S(1)} %get-tuple-element.93.refs_1_, bf16[512,256]{1,0:T(8,128)(2,1)S(1)} %copy-done.1, bf16[256,128]{1,0:T(8,128)(2,1)S(1)} %get-tuple-element.94.refs_3_.refs_1_), custom_call_target="tpu_custom_call" | custom-call | tf_op jit(solution)/shard_map/pallas_call | solution.py:48
  55.5 1.3 %shard_map.121 = (f32[1,512]{1,0:T(1,128)}, bf16[2,256,256]{2,1,0:T(8,128)(2,1)}, f32[2,256]{1,0:T(2,128)}, f32[8,128]{1,0:T(8,128)S(1)}) custom-call(s32[19]{0:T(128)S(1)} %stack.67.refs_0_, bf16[848,128]{1,0:T(8,128)(2,1)S(1)} %get-tuple-element.96.refs_1_, bf16[848,128]{1,0:T(8,128)(2,1)S(1)} %collective-permute-done.11.refs_2_, ...), custom_call_target="tpu_custom_call" | custom-call | tf_op jit(solution)/shard_map/pallas_call | solution.py:48
  56.7 0.9 %collective-permute-done.12.refs_3_ = bf16[256,128]{1,0:T(8,128)(2,1)S(1)} collective-permute-done((bf16[256,128]{1,0:T(8,128)(2,1)S(1)}, bf16[256,128]{1,0:T(8,128)(2,1)S(1)}, u32[]{:S(2)}, u32[]{:S(2)}) %collective-permute-start.12) | collective-permute-done | bytes 65568 | tf_op jit(solution)/shard_map/ppermute | solution.py:408
  57.7 1.5 %shard_map.122 = f32[512,256]{1,0:T(8,128)} custom-call(s32[19]{0:T(128)S(1)} %stack.67.refs_0_, bf16[256,128]{1,0:T(8,128)(2,1)S(1)} %get-tuple-element.94.refs_3_.refs_1_, bf16[848,128]{1,0:T(8,128)(2,1)S(1)} %collective-permute-done.11.refs_2_, bf16[256,128]{1,0:T(8,128)(2,1)S(1)} %collective-permute-done.12.refs_3_, ...), custom_call_target="tpu_custom_call" | custom-call | tf_op jit(solution)/shard_map/pallas_call | solution.py:48
  (23 shorter events, 1.2 us)
Async XLA Ops:
  0.8 1.1 %copy-start.3 = (bf16[768,512]{1,0:T(8,128)(2,1)S(1)}, bf16[768,512]{1,0:T(8,128)(2,1)}, u32[]{:S(2)}) copy-start(bf16[768,512]{1,0:T(8,128)(2,1)} %refs_1_.3) | copy-start | bytes 2359300
  1.9 5.6 %copy-start = (bf16[2048,512]{1,0:T(8,128)(2,1)S(1)}, bf16[2048,512]{1,0:T(8,128)(2,1)}, u32[]{:S(2)}) copy-start(bf16[2048,512]{1,0:T(8,128)(2,1)} %refs_3_.1) | copy-start | bytes 6291460
  1.9 5.6 %copy-start.2 = (bf16[2,1024,256]{2,1,0:T(8,128)(2,1)S(1)}, bf16[2,1024,256]{2,1,0:T(8,128)(2,1)}, u32[]{:S(2)}) copy-start(bf16[2,1024,256]{2,1,0:T(8,128)(2,1)} %refs_5_.3) | copy-start | bytes 3145732
  1.9 5.6 %copy-start.4 = (s32[1,2,384]{2,1,0:T(2,128)S(1)}, s32[1,2,384]{2,1,0:T(2,128)}, u32[]{:S(2)}) copy-start(s32[1,2,384]{2,1,0:T(2,128)} %param.7) | copy-start | bytes 9220
  1.9 5.7 %copy-start.5 = (f32[512]{0:T(512)S(1)}, f32[512]{0:T(512)}, u32[]{:S(2)}) copy-start(f32[512]{0:T(512)} %param.9) | copy-start | bytes 6148
  2.5 7.3 %collective-permute-start = (bf16[16,512]{1,0:T(8,128)(2,1)S(1)}, bf16[16,512]{1,0:T(8,128)(2,1)S(1)}, u32[]{:S(2)}, u32[]{:S(2)}) collective-permute-start(bf16[16,512]{1,0:T(8,128)(2,1)S(1)} %shard_map.109), channel_id=1, source_target_pairs={{0,1},{1,2},{2,3},{4,5},{5,6},{6,7},{8,9},{9,10},{10,11},{12,13},{... | collective-permute-start | bytes 49160 | tf_op jit(solution)/shard_map/ppermute | solution.py:404
  7.6 2.2 %copy-start.1 = (bf16[512,256]{1,0:T(8,128)(2,1)S(1)}, bf16[512,256]{1,0:T(8,128)(2,1)}, u32[]{:S(2)}) copy-start(bf16[512,256]{1,0:T(8,128)(2,1)} %refs_2_.3) | copy-start | bytes 786436
  11.5 2.5 %collective-permute-start.1 = (bf16[3360,128]{1,0:T(8,128)(2,1)S(1)}, bf16[3360,128]{1,0:T(8,128)(2,1)S(1)}, u32[]{:S(2)}, u32[]{:S(2)}) collective-permute-start(bf16[3360,128]{1,0:T(8,128)(2,1)S(1)} %get-tuple-element.61.refs_6_), channel_id=1, source_target_pairs={{0,4},{4,0},{8,12},{12,8},{16,20},{20,16},{24,28},{28,24},{1,5},{5... | collective-permute-start | bytes 2580488 | tf_op jit(solution)/shard_map/ppermute | solution.py:408
  14.6 11.7 %collective-permute-start.2 = (bf16[1328,128]{1,0:T(8,128)(2,1)S(1)}, bf16[1328,128]{1,0:T(8,128)(2,1)S(1)}, u32[]{:S(2)}, u32[]{:S(2)}) collective-permute-start(bf16[1328,128]{1,0:T(8,128)(2,1)S(1)} %get-tuple-element.66.refs_4_), channel_id=1, source_target_pairs={{0,8},{4,12},{8,0},{12,4},{16,24},{20,28},{24,16},{28,20},{1,9},{5... | collective-permute-start | bytes 1019912 | tf_op jit(solution)/shard_map/ppermute | solution.py:408
  17.8 8.5 %collective-permute-start.3 = (bf16[544,256]{1,0:T(8,128)(2,1)S(1)}, bf16[544,256]{1,0:T(8,128)(2,1)S(1)}, u32[]{:S(2)}, u32[]{:S(2)}) collective-permute-start(bf16[544,256]{1,0:T(8,128)(2,1)S(1)} %get-tuple-element.71), channel_id=1, source_target_pairs={{0,1},{1,0},{2,3},{3,2},{4,5},{5,4},{6,7},{7,6},{8,9},{9,8},{10,11... | collective-permute-start | bytes 835592 | tf_op jit(solution)/shard_map/ppermute | solution.py:408
  27.0 8.6 %collective-permute-start.6 = (bf16[272,256]{1,0:T(8,128)(2,1)S(1)}, bf16[272,256]{1,0:T(8,128)(2,1)S(1)}, u32[]{:S(2)}, u32[]{:S(2)}) collective-permute-start(bf16[272,256]{1,0:T(8,128)(2,1)S(1)} %get-tuple-element.77), channel_id=1, source_target_pairs={{0,2},{1,3},{2,0},{3,1},{4,6},{5,7},{6,4},{7,5},{8,10},{9,11},{10,... | collective-permute-start | bytes 417800 | tf_op jit(solution)/shard_map/ppermute | solution.py:408
  29.6 5.9 %collective-permute-start.4 = (bf16[512,128]{1,0:T(8,128)(2,1)S(1)}, bf16[512,128]{1,0:T(8,128)(2,1)S(1)}, u32[]{:S(2)}, u32[]{:S(2)}) collective-permute-start(bf16[512,128]{1,0:T(8,128)(2,1)S(1)} %get-tuple-element.73), channel_id=1, source_target_pairs={{0,16},{4,20},{8,24},{12,28},{16,0},{20,4},{24,8},{28,12},{1,17},{... | collective-permute-start | bytes 393224 | tf_op jit(solution)/shard_map/ppermute | solution.py:408
  31.2 4.4 %collective-permute-start.5 = (bf16[304,128]{1,0:T(8,128)(2,1)S(1)}, bf16[304,128]{1,0:T(8,128)(2,1)S(1)}, u32[]{:S(2)}, u32[]{:S(2)}) collective-permute-start(bf16[304,128]{1,0:T(8,128)(2,1)S(1)} %get-tuple-element.74), channel_id=1, source_target_pairs={{0,16},{4,20},{8,24},{12,28},{16,0},{20,4},{24,8},{28,12},{1,17},{... | collective-permute-start | bytes 233480 | tf_op jit(solution)/shard_map/ppermute | solution.py:408
  36.2 8.6 %collective-permute-start.7 = (bf16[560,128]{1,0:T(8,128)(2,1)S(1)}, bf16[560,128]{1,0:T(8,128)(2,1)S(1)}, u32[]{:S(2)}, u32[]{:S(2)}) collective-permute-start(bf16[560,128]{1,0:T(8,128)(2,1)S(1)} %get-tuple-element.81.refs_4_), channel_id=1, source_target_pairs={{0,2},{1,3},{2,0},{3,1},{4,6},{5,7},{6,4},{7,5},{8,10},{9,11},{10,... | collective-permute-start | bytes 430088 | tf_op jit(solution)/shard_map/ppermute | solution.py:408
  36.6 5.1 %collective-permute-start.8 = (bf16[272,256]{1,0:T(8,128)(2,1)S(1)}, bf16[272,256]{1,0:T(8,128)(2,1)S(1)}, u32[]{:S(2)}, u32[]{:S(2)}) collective-permute-start(bf16[272,256]{1,0:T(8,128)(2,1)S(1)} %get-tuple-element.85), channel_id=1, source_target_pairs={{0,8},{4,12},{8,0},{12,4},{16,24},{20,28},{24,16},{28,20},{1,9},{5... | collective-permute-start | bytes 417800 | tf_op jit(solution)/shard_map/ppermute | solution.py:408
  45.4 5.7 %collective-permute-start.9 = (bf16[560,128]{1,0:T(8,128)(2,1)S(1)}, bf16[560,128]{1,0:T(8,128)(2,1)S(1)}, u32[]{:S(2)}, u32[]{:S(2)}) collective-permute-start(bf16[560,128]{1,0:T(8,128)(2,1)S(1)} %get-tuple-element.88), channel_id=1, source_target_pairs={{0,1},{1,0},{2,3},{3,2},{4,5},{5,4},{6,7},{7,6},{8,9},{9,8},{10,11... | collective-permute-start | bytes 430088 | tf_op jit(solution)/shard_map/ppermute | solution.py:408
  46.0 5.1 %collective-permute-start.10 = (bf16[272,256]{1,0:T(8,128)(2,1)S(1)}, bf16[272,256]{1,0:T(8,128)(2,1)S(1)}, u32[]{:S(2)}, u32[]{:S(2)}) collective-permute-start(bf16[272,256]{1,0:T(8,128)(2,1)S(1)} %get-tuple-element.91), channel_id=1, source_target_pairs={{0,16},{4,20},{8,24},{12,28},{16,0},{20,4},{24,8},{28,12},{1,17},{... | collective-permute-start | bytes 417800 | tf_op jit(solution)/shard_map/ppermute | solution.py:408
  51.7 3.7 %collective-permute-start.11 = (bf16[848,128]{1,0:T(8,128)(2,1)S(1)}, bf16[848,128]{1,0:T(8,128)(2,1)S(1)}, u32[]{:S(2)}, u32[]{:S(2)}) collective-permute-start(bf16[848,128]{1,0:T(8,128)(2,1)S(1)} %get-tuple-element.96.refs_1_), channel_id=1, source_target_pairs={{0,4},{4,0},{8,12},{12,8},{16,20},{20,16},{24,28},{28,24},{1,5},{5... | collective-permute-start | bytes 651272 | tf_op jit(solution)/shard_map/ppermute | solution.py:408
  51.8 4.9 %collective-permute-start.13 = (bf16[256,128]{1,0:T(8,128)(2,1)S(1)}, bf16[256,128]{1,0:T(8,128)(2,1)S(1)}, u32[]{:S(2)}, u32[]{:S(2)}) collective-permute-start(bf16[256,128]{1,0:T(8,128)(2,1)S(1)} %get-tuple-element.94.refs_3_.refs_1_), channel_id=1, source_target_pairs={{0,12},{4,8},{8,4},{12,0},{16,28},{20,24},{24,20},{28,16},{1,13},{... | collective-permute-start | bytes 196616 | tf_op jit(solution)/shard_map/ppermute | solution.py:408
  52.5 5.2 %collective-permute-start.12 = (bf16[256,128]{1,0:T(8,128)(2,1)S(1)}, bf16[256,128]{1,0:T(8,128)(2,1)S(1)}, u32[]{:S(2)}, u32[]{:S(2)}) collective-permute-start(bf16[256,128]{1,0:T(8,128)(2,1)S(1)} %get-tuple-element.94.refs_3_.refs_1_), channel_id=1, source_target_pairs={{0,8},{4,12},{8,0},{12,4},{16,24},{20,28},{24,16},{28,20},{1,9},{5... | collective-permute-start | bytes 196616 | tf_op jit(solution)/shard_map/ppermute | solution.py:408

commit v6 on v5

--- a/solution.py
+++ b/solution.py
@@ -73,8 +73,8 @@
 def one_hot(codes, axis_codes, first, count):
     frames = codes.shape[1 - axis_codes]
     dims = (count, frames) if axis_codes == 0 else (frames, count)
-    places = lax.broadcasted_iota(jnp.int16, dims, axis_codes)
-    return jnp.where((codes - first).astype(jnp.int16) == places, jnp.ones((), BF16), jnp.zeros((), BF16))
+    places = lax.broadcasted_iota(jnp.int32, dims, axis_codes) + first
+    return jnp.where(codes == places, 1.0, 0.0).astype(BF16)
 
 
 def halo_kernel(info, feats, out):
@@ -243,26 +243,24 @@
         out[:, j * LANES:(j + 1) * LANES] = inter[j].astype(BF16)
 
 
-def sums_kernel(first, frames, place, count, info, got, own, row, send, keep):
+def sums_kernel(first, frames, info, got, own, row, send):
     rows, dz = own.shape
     theirs = jnp.concatenate([got[first + j * rows:first + (j + 1) * rows, :] for j in range(dz // LANES)], 1)
     ones = jnp.ones((8, frames), BF16)
     parts = []
     for block in (own[...], theirs):
         parts.append((block[0:frames, :], codes_of(block[frames:, :], frames)))
-    size = count + 16
+    count = send.shape[1] - 16
     riding = row[...].astype(F32)[0:1, :]
-    for out in (send, keep):
-        for top in range(0, keep.shape[0], size):
-            total = jnp.zeros((count, dz), F32)
-            counts = jnp.zeros((8, count), F32)
-            for values, codes in parts:
-                matches = one_hot(codes, 0, info[place], count)
-                total = total + nn(matches, values)
-                counts = counts + nt(ones, matches)
-            out[top:top + count, :] = total.astype(out.dtype)
-            out[top + count:top + size, :] = count_rows(counts[0:1], dz, riding).astype(out.dtype)
-            place += 1
+    for place in range(send.shape[0]):
+        total = jnp.zeros((count, dz), F32)
+        counts = jnp.zeros((8, count), F32)
+        for values, codes in parts:
+            matches = one_hot(codes, 0, place * count, count)
+            total = total + nn(matches, values)
+            counts = counts + nt(ones, matches)
+        send[place, 0:count, :] = total.astype(BF16)
+        send[place, count:, :] = count_rows(counts[0:1], dz, riding).astype(BF16)
 
 
 def count_rows(count, width, riding=None):
@@ -288,48 +286,43 @@
     return (block[0:1] * 65536.0 + block[1:2] * 256.0 + block[2:3])[:, :own]
 
 
-def sums_step(halved, count, bit, riding, got, kept, send, keep):
-    size = count + 16
-    dz = got.shape[1]
-    half = kept.shape[0] // 2 if halved else 0
-    outs = [(send, (1 - bit) * half), (keep, bit * half)] if halved else [(send, 0)]
-    for out, start in outs:
-        for top in range(0, keep.shape[0], size):
-            here = top + pl.multiple_of(start, 16) if halved else top
-            sums = pl.ds(here, count)
-            tail = pl.ds(here + count, 16)
-            value = kept[sums, :].astype(F32) + got[sums, :].astype(F32)
-            number = count_of(kept[tail, :].astype(F32), count) + count_of(got[tail, :].astype(F32), count)
-            out[top:top + count, :] = value.astype(out.dtype)
-            out[top + count:top + size, :] = count_rows(number, dz, riding).astype(out.dtype)
-    if not halved:
-        keep[...] = send[...].astype(F32)
-
-
-def window_kernel(halves, at_c, place, apart, sums_plan, row_plan, info, got_a, got_c, kept_a, kept_c, sums_got,
-                  sums_kept, *refs):
+def sums_step(gots, kept, send, keep):
+    count = keep.shape[0] - 16
+    value = kept[0:count, :].astype(F32)
+    number = count_of(kept[count:, :].astype(F32), count)
+    for got in gots:
+        value = value + got[0:count, :].astype(F32)
+        number = number + count_of(got[count:, :].astype(F32), count)
+    send[0:count, :] = value.astype(BF16)
+    send[count:, :] = count_rows(number, send.shape[1]).astype(BF16)
+    keep[...] = send[...].astype(F32)
+
+
+def window_kernel(halves, place, at_tm, info, got, kept_a, kept_c, *refs):
     (rows_a, halved_a), (rows_c, halved_c) = halves
-    sums_halved, sums_count, sums_place = sums_plan
-    row_step, row_parts, row_place = row_plan
-    row = None
-    if row_step is not None:
-        row = riding_row(sums_got[sums_count:sums_count + 16, :].astype(F32), row_parts)
-        wide = jnp.broadcast_to(row, refs[-1].shape)
-        before = refs[0][...].astype(F32) if row_step else jnp.zeros_like(wide)
-        refs[-1][...] = jnp.where(info[row_place] == row_step, wide, before).astype(BF16)
-        refs = refs[1 if row_step else 0:-1]
-    if apart:
-        send_a, send_c, keep_a, keep_c, sums_send, sums_keep = refs
-    else:
-        send_a, keep_a, keep_c, sums_send, sums_keep = refs
-        send_c = send_a
-    to = split_sum(halved_a, info[place], got_a, 0, kept_a, rows_a, send_a, 0, keep_a)
-    to = 0 if apart else to
-    gone = split_sum(halved_c, info[place], got_c, at_c, kept_c, rows_c, send_c, to, keep_c)
-    block = digit_block(add_digits(kept_c[rows_c:, :], got_c[at_c + rows_c:, :].astype(F32)))
-    send_c[to + gone:, :] = block.astype(BF16)
+    if at_tm is not None:
+        blocks = refs[0]
+        after = refs[-1]
+        refs = refs[1:-1]
+        tm = blocks.shape[0]
+        count = blocks.shape[1] - 16
+        here = info[at_tm]
+        following = blocks[jnp.minimum(here + 1, tm - 1), count:, :].astype(F32)
+        row = riding_row(following, after.shape[1] // blocks.shape[2])
+        row = jnp.where(here + 1 < tm, row, jnp.zeros_like(row))
+        after[...] = jnp.broadcast_to(row, after.shape).astype(BF16)
+        gots, sums_kept = [blocks.at[j] for j in range(1, tm)], blocks.at[0]
+    elif len(refs) > 3:
+        gots, sums_kept = [refs[0]], refs[1]
+        refs = refs[2:]
+    send, keep_a, keep_c = refs[:3]
+    to = split_sum(halved_a, info[place], got, 0, kept_a, rows_a, send, 0, keep_a)
+    gone = split_sum(halved_c, info[place], got, rows_a, kept_c, rows_c, send, to, keep_c)
+    block = digit_block(add_digits(kept_c[rows_c:, :], got[rows_a + rows_c:, :].astype(F32)))
+    send[to + gone:, :] = block.astype(BF16)
     keep_c[gone:, :] = block
-    sums_step(sums_halved, sums_count, info[sums_place], row, sums_got, sums_kept, sums_send, sums_keep)
+    if len(refs) > 3:
+        sums_step(gots, sums_kept, refs[3], refs[4])
 
 
 def last_kernel(rows, at_c, count, info, got_a, kept_a, got, kept, sums_got, sums_kept, corr, pieces, mine):
@@ -437,31 +430,21 @@
     now_a = pieces_a // 2 if plan[0][2] else pieces_a
     now_c = pieces_c // 2 if plan[1][2] else pieces_c
 
-    sums_exchanges = [("tm", b) for b in range(tm_bits)] + [("dp", b) for b in range(1, dp_bits)]
-
     at_dp, at_tm = lax.axis_index("dp"), lax.axis_index("tm")
 
     def bit_of(axis, b):
         return ((at_dp if axis == "dp" else at_tm) >> b) & 1
 
     bits = [bit_of(axis, b) for axis, b, _ in exchanges]
-    sums_bits = [bit_of(axis, b) for axis, b in sums_exchanges]
     masks = list(range(1 << c_bits))
     own_piece = sum((bits[k] << c_split[k]) for k in range(c_bits))
     flips = [sum(1 << c_split[k] for k in range(c_bits) if m >> k & 1) for m in masks]
-    quarters = [sum(((position >> (tm_bits - 1 - b)) & 1) << b for b in range(tm_bits)) for position in range(tm)]
-    lead = at_tm & 1
-    send_quarters = [(q | (1 - lead)) * per_shard for q in quarters[:tm // 2]]
-    keep_quarters = [(q | lead) * per_shard for q in quarters[:tm // 2]]
     at_start = len(bits)
-    at_codes = at_start + 1
-    at_pieces = at_codes + tm
-    at_sums = at_pieces + len(masks)
-    at_row = at_sums + len(sums_bits)
-    ones_below = sum(((at_tm + 1) & ((1 << (b + 1)) - 1) == 0).astype(jnp.int32) for b in range(tm_bits))
+    at_pieces = at_start + 1
+    at_row = at_pieces + len(masks)
     info = jnp.stack(
-        bits + [((at_dp * tm + at_tm) * owner_rows) & (LANES - 1)] + send_quarters + keep_quarters
-        + [own_piece ^ flip for flip in flips] + sums_bits + [ones_below]).astype(jnp.int32)
+        bits + [((at_dp * tm + at_tm) * owner_rows) & (LANES - 1)] + [own_piece ^ flip for flip in flips]
+        + [at_tm]).astype(jnp.int32)
 
     halo = shifted(
         call(halo_kernel, shape((16, channels), BF16), [info, feats], flops=10 ** 11), "tm", 1)
@@ -507,56 +490,51 @@
         functools.partial(first_step_kernel, halves, 1),
         [shape((rows_a + rows_c, LANES), BF16), shape((rows_a, LANES), F32), shape((rows_c, LANES), F32)],
         [info, got, keep_a, keep_c, extras])
-    got_a = got_c = swapped(send, exchanges[1][0], 1 << exchanges[1][1])
+    got = swapped(send, exchanges[1][0], 1 << exchanges[1][1])
     size = per_shard + 16
-    row_parts = channels // dz
-    sums_rows = size * (tm // 2)
-    sums_send, sums_keep = call(
-        functools.partial(sums_kernel, corr_rows, frames, at_codes, per_shard),
-        [shape((sums_rows, dz), BF16), shape((sums_rows, dz), F32)],
+    sums_send = call(
+        functools.partial(sums_kernel, corr_rows, frames),
+        shape((tm, size, dz), BF16),
         [info, core_got, own, row],
         after=[send])
-    sums_got = swapped(sums_send, sums_exchanges[0][0], 1 << sums_exchanges[0][1])
-    after = None
+    blocks = lax.all_to_all(sums_send, "tm", 0, 0)
+    sums_bits = list(range(1, dp_bits))
     ordered = []
     for k in range(2, len(exchanges)):
-        at_c = now_a * dz if got_a is got_c else 0
         halves, rows_a, rows_c = halves_at(k)
-        apart = k <= tm_bits
-        halved = sums_exchanges[k - 1][0] == "tm"
-        sums_rows = sums_rows // 2 if halved else sums_rows
-        row_step = k - 2 if k - 2 < tm_bits else None
-        sends = [rows_a, rows_c] if apart else [rows_a + rows_c]
-        outs = [shape((rows, LANES), BF16) for rows in sends] + [shape((rows, LANES), F32) for rows in (rows_a, rows_c)]
-        outs += [shape((sums_rows, dz), BF16), shape((sums_rows, dz), F32)]
+        outs = [shape((rows_a + rows_c, LANES), BF16), shape((rows_a, LANES), F32), shape((rows_c, LANES), F32)]
+        args = [info, got, keep_a, keep_c]
+        summed = len(exchanges) - k <= len(sums_bits)
+        first_sum = summed and len(sums_bits) == dp_bits - 1
+        if summed:
+            outs += [shape((size, dz), BF16), shape((size, dz), F32)]
+            args += [blocks] if first_sum else [sums_got, sums_keep]
         outs = call(
-            functools.partial(window_kernel, halves, at_c, k, apart, (halved, per_shard, at_sums + k - 1),
-                              (row_step, row_parts, at_row)),
-            outs + [shape((16, channels), BF16)] * (row_step is not None),
-            [info, got_a, got_c, keep_a, keep_c, sums_got, sums_keep] + [after] * bool(row_step),
+            functools.partial(window_kernel, halves, k, at_row if first_sum else None),
+            outs + [shape((16, channels), BF16)] * first_sum,
+            args,
             after=ordered)
-        after = outs[-1] if row_step is not None else after
-        got_a = got_c = swapped(outs[0], exchanges[k][0], 1 << exchanges[k][1])
-        if apart:
-            got_c = swapped(outs[1], exchanges[k][0], 1 << exchanges[k][1])
-        keep_a, keep_c, sums_send, sums_keep = outs[len(sends):len(sends) + 4]
-        sums_got = swapped(sums_send, sums_exchanges[k - 1][0], 1 << sums_exchanges[k - 1][1])
-        if k == tm_bits + 1:
+        send, keep_a, keep_c = outs[:3]
+        got = swapped(send, exchanges[k][0], 1 << exchanges[k][1])
+        if summed:
+            sums_send, sums_keep = outs[3:5]
+            sums_got = swapped(sums_send, "dp", 1 << sums_bits.pop(0))
+        if first_sum:
             feat_grad, *ordered = call(
                 feat_kernel,
                 shape((rows_in, channels), BF16),
-                [info, hidden_grad, after, weight],
-                after=[outs[0]],
+                [info, hidden_grad, outs[5], weight],
+                after=[send],
                 token=True,
                 scratch=[VMEM((frames + 8, channels), F32), VMEM((channels // LANES, rows_in, LANES), F32)],
             )
-    assert now_a == 1 and sums_rows == size
+    assert now_a == 1 and not sums_bits
 
     corr, piece, mine = call(
-        functools.partial(last_kernel, rows_c - extra, rows_a if got_a is got_c else 0, per_shard),
+        functools.partial(last_kernel, rows_c - extra, rows_a, per_shard),
         [shape((rows_a, LANES), F32), shape((rows_c - extra, LANES), BF16),
          shape((rows_c + size * (dz // LANES), LANES), BF16)],
-        [info, got_a, keep_a, got_c, keep_c, sums_got, sums_keep],
+        [info, got, keep_a, got, keep_c, sums_got, sums_keep],
         after=ordered)
     parts = [piece] + [swapped(mine if m == 1 else piece, "dp", m) for m in masks[1:]]
     conv_grad, last = call(

time: 59.3 us -> 67.8 us (1.14)
  local copies, waits for them, and re-layouts: 1.25 us -> 7.76 us
  starting transfers between devices: 18.3 us -> 22 us
  waiting for transfers between devices: 21.5 us -> 18.9 us
  Pallas kernels: 17.3 us -> 18 us
    unnamed x12 -> x30, local copies, waits for them, and re-layouts: 1.15 us -> 7.67 us
    all_to_all x0 -> x1, starting transfers between devices: none -> 4.86 us  [shards(): blocks = lax.all_to_all(sums_send, 'tm', 0, 0)]
    ppermute x13 -> x10, waiting for transfers between devices: 21.5 us -> 18.9 us  [swapped(): lax.ppermute(block, axis, [(i, i ^ mask) for i in range(lax.axis_size(axi...]
    ppermute x13 -> x10, starting transfers between devices: 13.2 us -> 12 us  [swapped(): lax.ppermute(block, axis, [(i, i ^ mask) for i in range(lax.axis_size(axi...]
  transfers between devices with their start and end apart: 14 -> 12, of which waited for: 7 -> 6; matrix products, arithmetic and copies ran while one was open for 0% -> 0% of each run, Pallas kernels for 18% -> 14%
where the time goes in v6:
time: 67.8 us; the launch traced here: 67.4 us
  starting transfers between devices  22 us (32%)
  waiting for transfers between devices  18.9 us (28%)
  Pallas kernels  18 us (27%)
  local copies, waits for them, and re-layouts  7.76 us (11%)
  between operations  0.84 us (1%)
    ppermute x10, waiting for transfers between devices, swapped(): lax.ppermute(block, axis, [(i, i ^ mask) for i in range(lax.axis_size(axi...  18.9 us
    pallas_call x14, Pallas kernels, call(): pl.pallas_call(kernel, out_shape=shown, in_specs=specs, out_specs=[pl.Blo...  18 us
    ppermute x10, starting transfers between devices, swapped(): lax.ppermute(block, axis, [(i, i ^ mask) for i in range(lax.axis_size(axi...  12 us
    unnamed x30, local copies, waits for them, and re-layouts  7.67 us
    ppermute x1, starting transfers between devices, shifted(): return lax.ppermute(block, axis, route)  5.06 us
    all_to_all x1, starting transfers between devices, shards(): blocks = lax.all_to_all(sums_send, 'tm', 0, 0)  4.86 us
  transfers between devices with their start and end apart: 12, of which 6 were waited for; matrix products, arithmetic and copies ran while one was open for 0% of the time, Pallas kernels for 14%

profile of v6, /device:TPU:0, one launch (start us, length us, event | category | flops | bytes accessed | tf_op | source)
XLA Modules:
  0.0 67.4 jit_solution(15835246234911909012)
XLA Ops:
  0.7 1.1 %copy-done.3 = bf16[768,512]{1,0:T(8,128)(2,1)S(1)} copy-done((bf16[768,512]{1,0:T(8,128)(2,1)S(1)}, bf16[768,512]{1,0:T(8,128)(2,1)}, u32[]{:S(2)}) %copy-start.3) | copy-done | bytes 786456
  2.4 5.1 %collective-permute-start = (bf16[16,512]{1,0:T(8,128)(2,1)S(1)}, bf16[16,512]{1,0:T(8,128)(2,1)S(1)}, u32[]{:S(2)}, u32[]{:S(2)}) collective-permute-start(bf16[16,512]{1,0:T(8,128)(2,1)S(1)} %shard_map.109), channel_id=1, source_target_pairs={{0,1},{1,2},{2,3},{4,5},{5,6},{6,7},{8,9},{9,10},{10,11},{12,13},{... | collective-permute-start | bytes 49160 | tf_op jit(solution)/shard_map/ppermute | solution.py:397
  7.6 2.1 %shard_map.110 = (bf16[384,2048]{1,0:T(8,128)(2,1)S(1)}, f32[384,512]{1,0:T(8,128)S(1)}, bf16[2,384,256]{2,1,0:T(8,128)(2,1)S(1)}) custom-call(s32[11]{0:T(128)S(1)} %stack.47.refs_0_, bf16[768,512]{1,0:T(8,128)(2,1)S(1)} %copy-done.3, bf16[2048,512]{1,0:T(8,128)(2,1)S(1)} %copy-done, f32[1,512]{1,0:T(1,128)S(1)} %bitcast.16, s32[2,384]{1,0:T(2,128)S(1)} %bitcast.14, ...), custom_call_target="tpu_custom_call" | custom-call | tf_op jit(solution)/shard_map/pallas_call | solution.py:48
  9.7 1.7 %shard_map.111 = (bf16[384,2048]{1,0:T(8,128)(2,1)S(1)}, bf16[384,512]{1,0:T(8,128)(2,1)S(1)}, bf16[384,256]{1,0:T(8,128)(2,1)S(1)}, bf16[256,384]{1,0:T(8,128)(...) custom-call(s32[11]{0:T(128)S(1)} %stack.47.refs_0_, ...), custom_call_target="tpu_custom_call", output_to_operand_aliasing={{0}: (2, {})} | custom-call | tf_op jit(solution)/shard_map/pallas_call | solution.py:48
  11.4 1.2 %shard_map.112 = (f32[2048,128]{1,0:T(8,128)S(1)}, f32[512,128]{1,0:T(8,128)S(1)}, bf16[384,512]{1,0:T(8,128)(2,1)S(1)}, f32[48,128]{1,0:T(8,128)S(1)}, bf16[16,512]{1,0:T(8,128)(2,1)S(1)}) custom-call(s32[11]{0:T(128)S(1)} %stack.47.refs_0_, bf16[256,384]{1,0:T(8,128)(2,1)S(1)} %get-tuple-element.51.refs_1_, ...), custom_call_target="tpu_custom_call" | custom-call | tf_op jit(solution)/shard_map/pallas_call | solution.py:48
  12.6 1.2 %collective-permute-done.1.refs_1_ = bf16[3360,128]{1,0:T(8,128)(2,1)S(1)} collective-permute-done((bf16[3360,128]{1,0:T(8,128)(2,1)S(1)}, bf16[3360,128]{1,0:T(8,128)(2,1)S(1)}, u32[]{:S(2)}, u32[]{:S(2)}) %collective-permute-start.1) | collective-permute-done | bytes 860192 | tf_op jit(solution)/shard_map/ppermute | solution.py:401
  15.1 2.4 %shard_map.115 = bf16[4,272,256]{2,1,0:T(8,128)(2,1)} custom-call(s32[11]{0:T(128)S(1)} %stack.47.refs_0_, bf16[3360,128]{1,0:T(8,128)(2,1)S(1)} %collective-permute-done.1.refs_1_, bf16[400,256]{1,0:T(8,128)(2,1)S(1)} %get-tuple-element.66.refs_2_, bf16[16,512]{1,0:T(8,128)(2,1)S(1)} %get-tuple-element.67.refs_3_, ...), custom_call_target="tpu_custom_call" | custom-call | tf_op jit(solution)/shard_map/pallas_call | solution.py:48
  17.6 0.7 %copy-done.6 = bf16[1328,128]{1,0:T(8,128)(2,1)} copy-done((bf16[1328,128]{1,0:T(8,128)(2,1)}, bf16[1328,128]{1,0:T(8,128)(2,1)S(1)}, u32[]{:S(2)}) %copy-start.6) | copy-done | bytes 339992
  18.3 4.9 %all-to-all-start = ((bf16[4,272,256]{2,1,0:T(8,128)(2,1)}), bf16[4,272,256]{2,1,0:T(8,128)(2,1)S(1)}, u32[]{:S(2)}, u32[]{:S(2)}) async-start(bf16[4,272,256]{2,1,0:T(8,128)(2,1)} %shard_map.115), calls=%async_computation | async-start | bytes 1114112 | tf_op jit(solution)/shard_map/all_to_all | solution.py:500
  23.2 1.5 %collective-permute-start.2 = (bf16[1328,128]{1,0:T(8,128)(2,1)}, bf16[1328,128]{1,0:T(8,128)(2,1)S(1)}, u32[]{:S(2)}, u32[]{:S(2)}) collective-permute-start(bf16[1328,128]{1,0:T(8,128)(2,1)} %copy-done.6), channel_id=1, source_target_pairs={{0,8},{4,12},{8,0},{12,4},{16,24},{20,28},{24,16},{28,20},{1,9},{5... | collective-permute-start | bytes 1019912 | tf_op jit(solution)/shard_map/ppermute | solution.py:401
  24.6 8.5 %collective-permute-done.2.refs_1_ = bf16[1328,128]{1,0:T(8,128)(2,1)S(1)} collective-permute-done((bf16[1328,128]{1,0:T(8,128)(2,1)}, bf16[1328,128]{1,0:T(8,128)(2,1)S(1)}, u32[]{:S(2)}, u32[]{:S(2)}) %collective-permute-start.2) | collective-permute-done | bytes 340000 | tf_op jit(solution)/shard_map/ppermute | solution.py:401
  33.1 0.9 %copy-done.10 = f32[304,128]{1,0:T(8,128)S(1)} copy-done((f32[304,128]{1,0:T(8,128)S(1)}, f32[304,128]{1,0:T(8,128)}, u32[]{:S(2)}) %copy-start.10) | copy-done | bytes 155672
  34.6 0.7 %copy-done.7 = f32[512,128]{1,0:T(8,128)} copy-done((f32[512,128]{1,0:T(8,128)}, f32[512,128]{1,0:T(8,128)S(1)}, u32[]{:S(2)}) %copy-start.7) | copy-done | bytes 262168
  35.3 0.7 copy-done.11
  36.0 1.5 %collective-permute-start.3 = (bf16[816,128]{1,0:T(8,128)(2,1)S(1)}, bf16[816,128]{1,0:T(8,128)(2,1)S(1)}, u32[]{:S(2)}, u32[]{:S(2)}) collective-permute-start(bf16[816,128]{1,0:T(8,128)(2,1)S(1)} %get-tuple-element.63), channel_id=1, source_target_pairs={{0,16},{4,20},{8,24},{12,28},{16,0},{20,4},{24,8},{28,12},{1,17},{... | collective-permute-start | bytes 626696 | tf_op jit(solution)/shard_map/ppermute | solution.py:401
  37.5 4.5 %collective-permute-done.3.refs_1_ = bf16[816,128]{1,0:T(8,128)(2,1)S(1)} collective-permute-done((bf16[816,128]{1,0:T(8,128)(2,1)S(1)}, bf16[816,128]{1,0:T(8,128)(2,1)S(1)}, u32[]{:S(2)}, u32[]{:S(2)}) %collective-permute-start.3) | collective-permute-done | bytes 208928 | tf_op jit(solution)/shard_map/ppermute | solution.py:401
  42.1 0.9 %copy-done.8 = f32[512,128]{1,0:T(8,128)S(1)} copy-done((f32[512,128]{1,0:T(8,128)S(1)}, f32[512,128]{1,0:T(8,128)}, u32[]{:S(2)}) %copy-start.8) | copy-done | bytes 262168
  43.0 0.9 %copy-done.12 = f32[304,128]{1,0:T(8,128)S(1)} copy-done((f32[304,128]{1,0:T(8,128)S(1)}, f32[304,128]{1,0:T(8,128)}, u32[]{:S(2)}) %copy-start.12) | copy-done | bytes 155672
  43.9 0.7 %shard_map.116 = (bf16[560,128]{1,0:T(8,128)(2,1)S(1)}, f32[256,128]{1,0:T(8,128)S(1)}, f32[304,128]{1,0:T(8,128)S(1)}, bf16[272,256]{1,0:T(8,128)(2,1)S(1)}, f3...) custom-call(s32[11]{0:T(128)S(1)} %stack.47.refs_0_, bf16[816,128]{1,0:T(8,128)(2,1)S(1)} %collective-permute-done.3.refs_1_, ...), custom_call_target="tpu_custom_call" | custom-call | tf_op jit(solution)/shard_map/pallas_call | solution.py:48
  44.6 2.5 %collective-permute-start.4 = (bf16[560,128]{1,0:T(8,128)(2,1)S(1)}, bf16[560,128]{1,0:T(8,128)(2,1)S(1)}, u32[]{:S(2)}, u32[]{:S(2)}) collective-permute-start(bf16[560,128]{1,0:T(8,128)(2,1)S(1)} %get-tuple-element.69.refs_4_), channel_id=1, source_target_pairs={{0,2},{1,3},{2,0},{3,1},{4,6},{5,7},{6,4},{7,5},{8,10},{9,11},{10,... | collective-permute-start | bytes 430088 | tf_op jit(solution)/shard_map/ppermute | solution.py:401
  47.1 1.5 %collective-permute-start.5 = (bf16[272,256]{1,0:T(8,128)(2,1)S(1)}, bf16[272,256]{1,0:T(8,128)(2,1)S(1)}, u32[]{:S(2)}, u32[]{:S(2)}) collective-permute-start(bf16[272,256]{1,0:T(8,128)(2,1)S(1)} %get-tuple-element.73), channel_id=1, source_target_pairs={{0,8},{4,12},{8,0},{12,4},{16,24},{20,28},{24,16},{28,20},{1,9},{5... | collective-permute-start | bytes 417800 | tf_op jit(solution)/shard_map/ppermute | solution.py:401
  48.6 1.0 %copy-done.5 = bf16[384,512]{1,0:T(8,128)(2,1)S(1)} copy-done((bf16[384,512]{1,0:T(8,128)(2,1)S(1)}, bf16[384,512]{1,0:T(8,128)(2,1)}, u32[]{:S(2)}) %copy-start.5) | copy-done | bytes 393240
  49.6 2.6 %shard_map.117 = (bf16[768,512]{1,0:T(8,128)(2,1)}, f32[8,128]{1,0:T(8,128)S(1)}) custom-call(s32[11]{0:T(128)S(1)} %stack.47.refs_0_, bf16[384,512]{1,0:T(8,128)(2,1)S(1)} %copy-done.5, bf16[16,512]{1,0:T(8,128)(2,1)S(1)} %get-tuple-element.68.refs_2_, bf16[2048,512]{1,0:T(8,128)(2,1)S(1)} %copy-done, bf16[560,128]{1,0:T(8,128)(2,1)S(1)} %get-tuple-element.69.refs_4_), custom_call_target="tpu_custom_call" | custom-call | tf_op jit(solution)/shard_map/pallas_call | solution.py:48
  53.0 1.3 %collective-permute-start.6 = (bf16[560,128]{1,0:T(8,128)(2,1)S(1)}, bf16[560,128]{1,0:T(8,128)(2,1)S(1)}, u32[]{:S(2)}, u32[]{:S(2)}) collective-permute-start(bf16[560,128]{1,0:T(8,128)(2,1)S(1)} %get-tuple-element.76), channel_id=1, source_target_pairs={{0,1},{1,0},{2,3},{3,2},{4,5},{5,4},{6,7},{7,6},{8,9},{9,8},{10,11... | collective-permute-start | bytes 430088 | tf_op jit(solution)/shard_map/ppermute | solution.py:401
  54.3 1.5 %collective-permute-start.7 = (bf16[272,256]{1,0:T(8,128)(2,1)S(1)}, bf16[272,256]{1,0:T(8,128)(2,1)S(1)}, u32[]{:S(2)}, u32[]{:S(2)}) collective-permute-start(bf16[272,256]{1,0:T(8,128)(2,1)S(1)} %get-tuple-element.79), channel_id=1, source_target_pairs={{0,16},{4,20},{8,24},{12,28},{16,0},{20,4},{24,8},{28,12},{1,17},{... | collective-permute-start | bytes 417800 | tf_op jit(solution)/shard_map/ppermute | solution.py:401
  55.8 3.5 %collective-permute-done.7.refs_5_ = bf16[272,256]{1,0:T(8,128)(2,1)S(1)} collective-permute-done((bf16[272,256]{1,0:T(8,128)(2,1)S(1)}, bf16[272,256]{1,0:T(8,128)(2,1)S(1)}, u32[]{:S(2)}, u32[]{:S(2)}) %collective-permute-start.7) | collective-permute-done | bytes 139296 | tf_op jit(solution)/shard_map/ppermute | solution.py:401
  59.4 0.7 shard_map.119
  60.1 1.6 %collective-permute-start.10 = (bf16[256,128]{1,0:T(8,128)(2,1)S(1)}, bf16[256,128]{1,0:T(8,128)(2,1)S(1)}, u32[]{:S(2)}, u32[]{:S(2)}) collective-permute-start(bf16[256,128]{1,0:T(8,128)(2,1)S(1)} %get-tuple-element.82.refs_3_.refs_1_), channel_id=1, source_target_pairs={{0,12},{4,8},{8,4},{12,0},{16,28},{20,24},{24,20},{28,16},{1,13},{... | collective-permute-start | bytes 196616 | tf_op jit(solution)/shard_map/ppermute | solution.py:401
  62.3 1.5 %shard_map.120 = (f32[64,512]{1,0:T(8,128)}, f32[8,128]{1,0:T(8,128)S(1)}) custom-call(s32[11]{0:T(128)S(1)} %stack.47.refs_0_, f32[256,128]{1,0:T(8,128)S(1)} %get-tuple-element.81.refs_1_, bf16[512,256]{1,0:T(8,128)(2,1)S(1)} %copy-done.1, bf16[256,128]{1,0:T(8,128)(2,1)S(1)} %get-tuple-element.82.refs_3_.refs_1_), custom_call_target="tpu_custom_call" | custom-call | tf_op jit(solution)/shard_map/pallas_call | solution.py:48
  63.8 1.3 %shard_map.121 = (f32[1,512]{1,0:T(1,128)}, bf16[2,256,256]{2,1,0:T(8,128)(2,1)}, f32[2,256]{1,0:T(2,128)}, f32[8,128]{1,0:T(8,128)S(1)}) custom-call(s32[11]{0:T(128)S(1)} %stack.47.refs_0_, bf16[848,128]{1,0:T(8,128)(2,1)S(1)} %get-tuple-element.84.refs_1_, bf16[848,128]{1,0:T(8,128)(2,1)S(1)} %collective-permute-done.8.refs_2_, ...), custom_call_target="tpu_custom_call" | custom-call | tf_op jit(solution)/shard_map/pallas_call | solution.py:48
  65.0 0.9 %collective-permute-done.9.refs_3_ = bf16[256,128]{1,0:T(8,128)(2,1)S(1)} collective-permute-done((bf16[256,128]{1,0:T(8,128)(2,1)S(1)}, bf16[256,128]{1,0:T(8,128)(2,1)S(1)}, u32[]{:S(2)}, u32[]{:S(2)}) %collective-permute-start.9) | collective-permute-done | bytes 65568 | tf_op jit(solution)/shard_map/ppermute | solution.py:401
  66.0 1.5 %shard_map.122 = f32[512,256]{1,0:T(8,128)} custom-call(s32[11]{0:T(128)S(1)} %stack.47.refs_0_, bf16[256,128]{1,0:T(8,128)(2,1)S(1)} %get-tuple-element.82.refs_3_.refs_1_, bf16[848,128]{1,0:T(8,128)(2,1)S(1)} %collective-permute-done.8.refs_2_, bf16[256,128]{1,0:T(8,128)(2,1)S(1)} %collective-permute-done.9.refs_3_, ...), custom_call_target="tpu_custom_call" | custom-call | tf_op jit(solution)/shard_map/pallas_call | solution.py:48
  (37 shorter events, 4.2 us)
Async XLA Ops:
  0.7 1.1 %copy-start.3 = (bf16[768,512]{1,0:T(8,128)(2,1)S(1)}, bf16[768,512]{1,0:T(8,128)(2,1)}, u32[]{:S(2)}) copy-start(bf16[768,512]{1,0:T(8,128)(2,1)} %refs_1_.3) | copy-start | bytes 2359300
  1.9 5.6 %copy-start = (bf16[2048,512]{1,0:T(8,128)(2,1)S(1)}, bf16[2048,512]{1,0:T(8,128)(2,1)}, u32[]{:S(2)}) copy-start(bf16[2048,512]{1,0:T(8,128)(2,1)} %refs_3_.1) | copy-start | bytes 6291460
  1.9 5.6 %copy-start.2 = (bf16[2,1024,256]{2,1,0:T(8,128)(2,1)S(1)}, bf16[2,1024,256]{2,1,0:T(8,128)(2,1)}, u32[]{:S(2)}) copy-start(bf16[2,1024,256]{2,1,0:T(8,128)(2,1)} %refs_5_.3) | copy-start | bytes 3145732
  1.9 5.6 %copy-start.13 = (s32[1,2,384]{2,1,0:T(2,128)S(1)}, s32[1,2,384]{2,1,0:T(2,128)}, u32[]{:S(2)}) copy-start(s32[1,2,384]{2,1,0:T(2,128)} %param.7) | copy-start | bytes 9220
  1.9 5.7 %copy-start.14 = (f32[512]{0:T(512)S(1)}, f32[512]{0:T(512)}, u32[]{:S(2)}) copy-start(f32[512]{0:T(512)} %param.9) | copy-start | bytes 6148
  2.4 7.2 %collective-permute-start = (bf16[16,512]{1,0:T(8,128)(2,1)S(1)}, bf16[16,512]{1,0:T(8,128)(2,1)S(1)}, u32[]{:S(2)}, u32[]{:S(2)}) collective-permute-start(bf16[16,512]{1,0:T(8,128)(2,1)S(1)} %shard_map.109), channel_id=1, source_target_pairs={{0,1},{1,2},{2,3},{4,5},{5,6},{6,7},{8,9},{9,10},{10,11},{12,13},{... | collective-permute-start | bytes 49160 | tf_op jit(solution)/shard_map/ppermute | solution.py:397
  7.5 2.1 %copy-start.1 = (bf16[512,256]{1,0:T(8,128)(2,1)S(1)}, bf16[512,256]{1,0:T(8,128)(2,1)}, u32[]{:S(2)}) copy-start(bf16[512,256]{1,0:T(8,128)(2,1)} %refs_2_.3) | copy-start | bytes 786436
  11.4 2.5 %collective-permute-start.1 = (bf16[3360,128]{1,0:T(8,128)(2,1)S(1)}, bf16[3360,128]{1,0:T(8,128)(2,1)S(1)}, u32[]{:S(2)}, u32[]{:S(2)}) collective-permute-start(bf16[3360,128]{1,0:T(8,128)(2,1)S(1)} %get-tuple-element.55.refs_6_), channel_id=1, source_target_pairs={{0,4},{4,0},{8,12},{12,8},{16,20},{20,16},{24,28},{28,24},{1,5},{5... | collective-permute-start | bytes 2580488 | tf_op jit(solution)/shard_map/ppermute | solution.py:401
  12.6 1.8 %copy-start.4 = (bf16[384,512]{1,0:T(8,128)(2,1)}, bf16[384,512]{1,0:T(8,128)(2,1)S(1)}, u32[]{:S(2)}) copy-start(bf16[384,512]{1,0:T(8,128)(2,1)S(1)} %get-tuple-element.56.refs_1_) | copy-start | bytes 1179652
  14.5 0.7 copy-start.9
  17.6 0.7 %copy-start.6 = (bf16[1328,128]{1,0:T(8,128)(2,1)}, bf16[1328,128]{1,0:T(8,128)(2,1)S(1)}, u32[]{:S(2)}) copy-start(bf16[1328,128]{1,0:T(8,128)(2,1)S(1)} %get-tuple-element.60.refs_4_) | copy-start | bytes 1019908
  18.3 23.8 %all-to-all-start = ((bf16[4,272,256]{2,1,0:T(8,128)(2,1)}), bf16[4,272,256]{2,1,0:T(8,128)(2,1)S(1)}, u32[]{:S(2)}, u32[]{:S(2)}) async-start(bf16[4,272,256]{2,1,0:T(8,128)(2,1)} %shard_map.115), calls=%async_computation | async-start | bytes 1114112 | tf_op jit(solution)/shard_map/all_to_all | solution.py:500
  23.2 9.9 %collective-permute-start.2 = (bf16[1328,128]{1,0:T(8,128)(2,1)}, bf16[1328,128]{1,0:T(8,128)(2,1)S(1)}, u32[]{:S(2)}, u32[]{:S(2)}) collective-permute-start(bf16[1328,128]{1,0:T(8,128)(2,1)} %copy-done.6), channel_id=1, source_target_pairs={{0,8},{4,12},{8,0},{12,4},{16,24},{20,28},{24,16},{28,20},{1,9},{5... | collective-permute-start | bytes 1019912 | tf_op jit(solution)/shard_map/ppermute | solution.py:401
  33.1 0.9 %copy-start.10 = (f32[304,128]{1,0:T(8,128)S(1)}, f32[304,128]{1,0:T(8,128)}, u32[]{:S(2)}) copy-start(f32[304,128]{1,0:T(8,128)} %copy-done.9) | copy-start | bytes 466948
  34.6 0.7 %copy-start.7 = (f32[512,128]{1,0:T(8,128)}, f32[512,128]{1,0:T(8,128)S(1)}, u32[]{:S(2)}) copy-start(f32[512,128]{1,0:T(8,128)S(1)} %get-tuple-element.64.refs_2_) | copy-start | bytes 786436
  35.3 0.7 copy-start.11
  36.0 6.0 %collective-permute-start.3 = (bf16[816,128]{1,0:T(8,128)(2,1)S(1)}, bf16[816,128]{1,0:T(8,128)(2,1)S(1)}, u32[]{:S(2)}, u32[]{:S(2)}) collective-permute-start(bf16[816,128]{1,0:T(8,128)(2,1)S(1)} %get-tuple-element.63), channel_id=1, source_target_pairs={{0,16},{4,20},{8,24},{12,28},{16,0},{20,4},{24,8},{28,12},{1,17},{... | collective-permute-start | bytes 626696 | tf_op jit(solution)/shard_map/ppermute | solution.py:401
  42.1 1.0 %copy-start.8 = (f32[512,128]{1,0:T(8,128)S(1)}, f32[512,128]{1,0:T(8,128)}, u32[]{:S(2)}) copy-start(f32[512,128]{1,0:T(8,128)} %copy-done.7) | copy-start | bytes 786436
  43.0 0.9 %copy-start.12 = (f32[304,128]{1,0:T(8,128)S(1)}, f32[304,128]{1,0:T(8,128)}, u32[]{:S(2)}) copy-start(f32[304,128]{1,0:T(8,128)} %copy-done.11) | copy-start | bytes 466948
  44.6 7.8 %collective-permute-start.4 = (bf16[560,128]{1,0:T(8,128)(2,1)S(1)}, bf16[560,128]{1,0:T(8,128)(2,1)S(1)}, u32[]{:S(2)}, u32[]{:S(2)}) collective-permute-start(bf16[560,128]{1,0:T(8,128)(2,1)S(1)} %get-tuple-element.69.refs_4_), channel_id=1, source_target_pairs={{0,2},{1,3},{2,0},{3,1},{4,6},{5,7},{6,4},{7,5},{8,10},{9,11},{10,... | collective-permute-start | bytes 430088 | tf_op jit(solution)/shard_map/ppermute | solution.py:401
  47.1 5.1 %collective-permute-start.5 = (bf16[272,256]{1,0:T(8,128)(2,1)S(1)}, bf16[272,256]{1,0:T(8,128)(2,1)S(1)}, u32[]{:S(2)}, u32[]{:S(2)}) collective-permute-start(bf16[272,256]{1,0:T(8,128)(2,1)S(1)} %get-tuple-element.73), channel_id=1, source_target_pairs={{0,8},{4,12},{8,0},{12,4},{16,24},{20,28},{24,16},{28,20},{1,9},{5... | collective-permute-start | bytes 417800 | tf_op jit(solution)/shard_map/ppermute | solution.py:401
  48.6 1.0 %copy-start.5 = (bf16[384,512]{1,0:T(8,128)(2,1)S(1)}, bf16[384,512]{1,0:T(8,128)(2,1)}, u32[]{:S(2)}) copy-start(bf16[384,512]{1,0:T(8,128)(2,1)} %copy-done.4) | copy-start | bytes 1179652
  53.0 6.3 %collective-permute-start.6 = (bf16[560,128]{1,0:T(8,128)(2,1)S(1)}, bf16[560,128]{1,0:T(8,128)(2,1)S(1)}, u32[]{:S(2)}, u32[]{:S(2)}) collective-permute-start(bf16[560,128]{1,0:T(8,128)(2,1)S(1)} %get-tuple-element.76), channel_id=1, source_target_pairs={{0,1},{1,0},{2,3},{3,2},{4,5},{5,4},{6,7},{7,6},{8,9},{9,8},{10,11... | collective-permute-start | bytes 430088 | tf_op jit(solution)/shard_map/ppermute | solution.py:401
  54.3 5.1 %collective-permute-start.7 = (bf16[272,256]{1,0:T(8,128)(2,1)S(1)}, bf16[272,256]{1,0:T(8,128)(2,1)S(1)}, u32[]{:S(2)}, u32[]{:S(2)}) collective-permute-start(bf16[272,256]{1,0:T(8,128)(2,1)S(1)} %get-tuple-element.79), channel_id=1, source_target_pairs={{0,16},{4,20},{8,24},{12,28},{16,0},{20,4},{24,8},{28,12},{1,17},{... | collective-permute-start | bytes 417800 | tf_op jit(solution)/shard_map/ppermute | solution.py:401
  60.0 3.7 %collective-permute-start.8 = (bf16[848,128]{1,0:T(8,128)(2,1)S(1)}, bf16[848,128]{1,0:T(8,128)(2,1)S(1)}, u32[]{:S(2)}, u32[]{:S(2)}) collective-permute-start(bf16[848,128]{1,0:T(8,128)(2,1)S(1)} %get-tuple-element.84.refs_1_), channel_id=1, source_target_pairs={{0,4},{4,0},{8,12},{12,8},{16,20},{20,16},{24,28},{28,24},{1,5},{5... | collective-permute-start | bytes 651272 | tf_op jit(solution)/shard_map/ppermute | solution.py:401
  60.1 4.9 %collective-permute-start.10 = (bf16[256,128]{1,0:T(8,128)(2,1)S(1)}, bf16[256,128]{1,0:T(8,128)(2,1)S(1)}, u32[]{:S(2)}, u32[]{:S(2)}) collective-permute-start(bf16[256,128]{1,0:T(8,128)(2,1)S(1)} %get-tuple-element.82.refs_3_.refs_1_), channel_id=1, source_target_pairs={{0,12},{4,8},{8,4},{12,0},{16,28},{20,24},{24,20},{28,16},{1,13},{... | collective-permute-start | bytes 196616 | tf_op jit(solution)/shard_map/ppermute | solution.py:401
  61.7 4.3 %collective-permute-start.9 = (bf16[256,128]{1,0:T(8,128)(2,1)S(1)}, bf16[256,128]{1,0:T(8,128)(2,1)S(1)}, u32[]{:S(2)}, u32[]{:S(2)}) collective-permute-start(bf16[256,128]{1,0:T(8,128)(2,1)S(1)} %get-tuple-element.82.refs_3_.refs_1_), channel_id=1, source_target_pairs={{0,8},{4,12},{8,0},{12,4},{16,24},{20,28},{24,16},{28,20},{1,9},{5... | collective-permute-start | bytes 196616 | tf_op jit(solution)/shard_map/ppermute | solution.py:401

commit v7 on v5

--- a/solution.py
+++ b/solution.py
@@ -73,8 +73,8 @@
 def one_hot(codes, axis_codes, first, count):
     frames = codes.shape[1 - axis_codes]
     dims = (count, frames) if axis_codes == 0 else (frames, count)
-    places = lax.broadcasted_iota(jnp.int16, dims, axis_codes)
-    return jnp.where((codes - first).astype(jnp.int16) == places, jnp.ones((), BF16), jnp.zeros((), BF16))
+    places = lax.broadcasted_iota(jnp.int32, dims, axis_codes) + first
+    return jnp.where(codes == places, 1.0, 0.0).astype(BF16)
 
 
 def halo_kernel(info, feats, out):
@@ -99,32 +99,31 @@
         chosen[level] = nn(matches, books[level]).astype(BF16)
 
 
-def walk(order, halved, count):
-    others = order[1:] if halved else order
+def walk(orders, halved, count):
+    start = 1 if halved else 0
     shown = count // 2 if halved else count
-    step = 2 if shown > 1 and others[-1] == 0 else 1
+    bits = log2(shown)
+    step = 2 if shown > 1 and all(order[-1] == 0 for order in orders) else 1
     for position in range(0, shown, step):
-        piece = 0
-        for k, bit in enumerate(others):
-            piece += ((position >> (len(others) - 1 - k)) & 1) << bit
-        yield position, piece, step
-
-
-def correlate(flipped, sources, plan, bit, out):
+        yield position, [
+            sum(((position >> (bits - 1 - k)) & 1) << bit for k, bit in enumerate(order[start:])) for order in orders
+        ], step
+
+
+def correlate(flipped, sources, plan, core, bit, out):
     dz = flipped.shape[0]
     at = 0
-    for source, (count, order, halved) in zip(sources, plan):
-        shown = count // 2 if halved else count
-        for position, piece, step in walk(order, halved, count):
+    for source, (count, orders, halved) in zip(sources, plan):
+        for position, pieces, step in walk(orders, halved, count):
+            column = pieces[0] + core * (pieces[1] - pieces[0])
             if halved:
-                column = pl.multiple_of((piece + (bit << order[0])) * LANES, LANES)
-                product = nn(flipped, source[:, pl.ds(column, step * LANES)])
-            else:
-                product = nn(flipped, source[:, piece * LANES:(piece + step) * LANES])
+                column = column + (bit << orders[0][0])
+            column = pl.multiple_of(column * LANES, LANES)
+            product = nn(flipped, source[:, pl.ds(column, step * LANES)])
             for j in range(step):
                 top = (at + position + j) * dz
                 out[top:top + dz, :] = product[:, j * LANES:(j + 1) * LANES].astype(out.dtype)
-        at += shown
+        at += count // 2 if halved else count
     return at * dz
 
 
@@ -167,7 +166,7 @@
     latent_grad[...] = total.astype(BF16)
     flipped[...] = jnp.transpose(latent_grad[...].astype(F32)).astype(BF16)
     bit = info[0]
-    at = correlate(flipped[...], (unfold, hidden), plan, 1 - bit, send)
+    at = correlate(flipped[...], (unfold, hidden), plan, 1 - bit, 1 - bit, send)
     code_rows = own.shape[0] - frames
     digits = [code_digits(codes[level:level + 1], dz, code_rows) for level in range(2)]
     own[0:frames, :] = jnp.where(bit == 1, once, latent).astype(BF16)
@@ -182,8 +181,8 @@
 
 def rest_kernel(plan, info, flipped, unfold, hidden, latent_grad, proj, keep_a, keep_c, hidden_grad, extras, row):
     bit = info[0]
-    correlate(flipped[...], (unfold,), plan[:1], bit, keep_a)
-    correlate(flipped[...], (hidden,), plan[1:], bit, keep_c)
+    correlate(flipped[...], (unfold,), plan[:1], bit, bit, keep_a)
+    correlate(flipped[...], (hidden,), plan[1:], bit, bit, keep_c)
     back = nt(latent_grad[...], proj[...]).astype(BF16)
     hidden_grad[...] = back
     row[...] = back[0:16, :]
@@ -219,11 +218,11 @@
     return jnp.concatenate(list(digits_of(value)) + [jnp.zeros_like(value)] * 3, 0)
 
 
-def first_step_kernel(halves, place, info, got, kept_a, kept_c, extras, send, keep_a, keep_c):
+def first_step_kernel(halves, place, info, got, kept_a, kept_c, extras, send_a, send_c, keep_a, keep_c):
     (rows_a, halved_a), (rows_c, halved_c) = halves
-    to = split_sum(halved_a, info[place], got, 0, kept_a, rows_a, send, 0, keep_a)
-    gone = split_sum(halved_c, info[place], got, rows_a, kept_c, rows_c, send, to, keep_c)
-    send[to + gone:, :] = extras[...].astype(BF16)
+    split_sum(halved_a, info[place], got, 0, kept_a, rows_a, send_a, 0, keep_a)
+    gone = split_sum(halved_c, info[place], got, rows_a, kept_c, rows_c, send_c, 0, keep_c)
+    send_c[gone:, :] = extras[...].astype(BF16)
     keep_c[gone:, :] = extras[...]
 
 
@@ -243,7 +242,7 @@
         out[:, j * LANES:(j + 1) * LANES] = inter[j].astype(BF16)
 
 
-def sums_kernel(first, frames, place, count, info, got, own, row, send, keep):
+def sums_kernel(first, frames, place, count, info, got, own, row, out):
     rows, dz = own.shape
     theirs = jnp.concatenate([got[first + j * rows:first + (j + 1) * rows, :] for j in range(dz // LANES)], 1)
     ones = jnp.ones((8, frames), BF16)
@@ -251,21 +250,20 @@
     for block in (own[...], theirs):
         parts.append((block[0:frames, :], codes_of(block[frames:, :], frames)))
     size = count + 16
-    riding = row[...].astype(F32)[0:1, :]
-    for out in (send, keep):
-        for top in range(0, keep.shape[0], size):
-            total = jnp.zeros((count, dz), F32)
-            counts = jnp.zeros((8, count), F32)
-            for values, codes in parts:
-                matches = one_hot(codes, 0, info[place], count)
-                total = total + nn(matches, values)
-                counts = counts + nt(ones, matches)
-            out[top:top + count, :] = total.astype(out.dtype)
-            out[top + count:top + size, :] = count_rows(counts[0:1], dz, riding).astype(out.dtype)
-            place += 1
-
-
-def count_rows(count, width, riding=None):
+    riding = [row[...].astype(F32)[0:1, :]]
+    for top in range(0, out.shape[0], size):
+        total = jnp.zeros((count, dz), F32)
+        counts = jnp.zeros((8, count), F32)
+        for values, codes in parts:
+            matches = one_hot(codes, 0, info[place], count)
+            total = total + nn(matches, values)
+            counts = counts + nt(ones, matches)
+        out[top:top + count, :] = total.astype(out.dtype)
+        out[top + count:top + size, :] = count_rows(counts[0:1], dz, riding).astype(out.dtype)
+        place += 1
+
+
+def count_rows(count, width, riding=()):
     high = jnp.floor(count * (1.0 / 65536.0))
     rest = count - high * 65536.0
     middle = jnp.floor(rest * (1.0 / 256.0))
@@ -274,14 +272,14 @@
     if count.shape[1] < width:
         block = jnp.concatenate([block, jnp.zeros((3, width - count.shape[1]), F32)], 1)
     parts = [block]
-    if riding is not None:
-        parts += [riding[:, at:at + width] for at in range(0, riding.shape[1], width)]
-    parts.append(jnp.zeros((16 - sum(part.shape[0] for part in parts), width), F32))
-    return jnp.concatenate(parts, 0)
-
-
-def riding_row(block, parts):
-    return jnp.concatenate([block[3 + j:4 + j, :] for j in range(parts)], 1)
+    for row in riding:
+        parts += [row[:, at:at + width] for at in range(0, row.shape[1], width)]
+    left = 16 - sum(part.shape[0] for part in parts)
+    return jnp.concatenate(parts + [jnp.zeros((left, width), F32)] * (left > 0), 0)
+
+
+def riding_row(block, index, parts):
+    return jnp.concatenate([block[3 + index * parts + j:4 + index * parts + j, :] for j in range(parts)], 1)
 
 
 def count_of(block, own):
@@ -306,30 +304,58 @@
         keep[...] = send[...].astype(F32)
 
 
-def window_kernel(halves, at_c, place, apart, sums_plan, row_plan, info, got_a, got_c, kept_a, kept_c, sums_got,
+def swap_halves(first, second, core):
+    half = LANES // 2
+    left = lax.broadcasted_iota(jnp.int32, first.shape, 1) < half
+    turned_first, turned_second = pltpu.roll(first, half, 1), pltpu.roll(second, half, 1)
+    swapped_first = jnp.where(left, first, turned_second)
+    swapped_second = jnp.where(left, turned_first, second)
+    return jnp.where(core == 1, swapped_first, first), jnp.where(core == 1, swapped_second, second)
+
+
+def window_kernel(halves, at_c, place, apart, mixed, sums_plan, row_plan, info, got_a, got_c, kept_a, kept_c, sums_got,
                   sums_kept, *refs):
     (rows_a, halved_a), (rows_c, halved_c) = halves
     sums_halved, sums_count, sums_place = sums_plan
-    row_step, row_parts, row_place = row_plan
-    row = None
+    row_step, row_place = row_plan
+    riding = ()
     if row_step is not None:
-        row = riding_row(sums_got[sums_count:sums_count + 16, :].astype(F32), row_parts)
-        wide = jnp.broadcast_to(row, refs[-1].shape)
-        before = refs[0][...].astype(F32) if row_step else jnp.zeros_like(wide)
-        refs[-1][...] = jnp.where(info[row_place] == row_step, wide, before).astype(BF16)
-        refs = refs[1 if row_step else 0:-1]
+        known, refs = refs[0][...].astype(F32), refs[1:]
+        after, refs = refs[-1], refs[:-1]
+        parts = known.shape[1] // sums_got.shape[1]
+        block = sums_got[sums_count:sums_count + 16, :].astype(F32)
+        rows = [known[j:j + 1, :] for j in range(1 << row_step)]
+        rows += [riding_row(block, j, parts) for j in range(1 << row_step)]
+        riding = rows if sums_halved else ()
+        if sums_halved:
+            total = rows + [jnp.zeros((16 - len(rows), known.shape[1]), F32)]
+            after[...] = jnp.concatenate(total, 0).astype(BF16)
+        else:
+            wide = jnp.zeros(after.shape, F32)
+            for j in range(1, len(rows)):
+                wide = jnp.where(info[row_place] == j, jnp.broadcast_to(rows[j], after.shape), wide)
+            after[...] = wide.astype(BF16)
     if apart:
         send_a, send_c, keep_a, keep_c, sums_send, sums_keep = refs
     else:
         send_a, keep_a, keep_c, sums_send, sums_keep = refs
         send_c = send_a
-    to = split_sum(halved_a, info[place], got_a, 0, kept_a, rows_a, send_a, 0, keep_a)
+    if mixed:
+        half = rows_a // 2
+        total = kept_a[0:rows_a, :] + got_a[0:rows_a, :].astype(F32)
+        first, second = swap_halves(total[0:half, :], total[half:, :], info[0])
+        low = info[place] == 0
+        send_a[0:half, :] = jnp.where(low, second, first).astype(BF16)
+        keep_a[...] = jnp.where(low, first, second)
+        to = half
+    else:
+        to = split_sum(halved_a, info[place], got_a, 0, kept_a, rows_a, send_a, 0, keep_a)
     to = 0 if apart else to
     gone = split_sum(halved_c, info[place], got_c, at_c, kept_c, rows_c, send_c, to, keep_c)
     block = digit_block(add_digits(kept_c[rows_c:, :], got_c[at_c + rows_c:, :].astype(F32)))
     send_c[to + gone:, :] = block.astype(BF16)
     keep_c[gone:, :] = block
-    sums_step(sums_halved, sums_count, info[sums_place], row, sums_got, sums_kept, sums_send, sums_keep)
+    sums_step(sums_halved, sums_count, info[sums_place], riding, sums_got, sums_kept, sums_send, sums_keep)
 
 
 def last_kernel(rows, at_c, count, info, got_a, kept_a, got, kept, sums_got, sums_kept, corr, pieces, mine):
@@ -404,8 +430,26 @@
     return lax.ppermute(block, axis, route)
 
 
-def swapped(block, axis, mask):
-    return lax.ppermute(block, axis, [(i, i ^ mask) for i in range(lax.axis_size(axis))])
+def swapped(block, steps):
+    tm = lax.axis_size("tm")
+
+    def partner(device):
+        axis, bit = steps[(device // tm) & 1]
+        return device ^ ((1 << bit) * (tm if axis == "dp" else 1))
+
+    route = [(device, partner(device)) for device in range(lax.axis_size("dp") * tm)]
+    return lax.ppermute(block, ("dp", "tm"), route)
+
+
+def crossed(block, steps):
+    tm = lax.axis_size("tm")
+
+    def partner(device):
+        axis, bit = steps[(device // tm) & 1]
+        return device ^ tm ^ ((1 << bit) * (tm if axis == "dp" else 1))
+
+    route = [(device, partner(device)) for device in range(lax.axis_size("dp") * tm)]
+    return lax.ppermute(block, ("dp", "tm"), route)
 
 
 def shards(feats, codes, conv_weight, conv_bias, proj_weight, codebooks):
@@ -420,48 +464,80 @@
     dp_bits, tm_bits = log2(dp), log2(tm)
     owner_rows = width // (dp * tm)
 
-    exchanges = [("dp", b, b + tm_bits) for b in range(dp_bits)]
-    exchanges += [("tm", b, b) for b in reversed(range(tm_bits))]
+    assert dp_bits >= 3 and 1 <= tm_bits <= 2
     pieces_a, pieces_c = width // LANES, channels // LANES
     under = max(dp_bits + tm_bits - log2(pieces_a), 0)
-    c_bits = min(log2(pieces_c), 2, dp_bits)
-    a_split = [bit - under if bit >= under else None for _, _, bit in exchanges]
+    c_bits = 2
+    assert pieces_c >= 4
+    whole_bits = [b for b in range(1, dp_bits) if b + tm_bits < under]
+    piece_bits = [b for b in range(1, dp_bits) if b + tm_bits >= under]
+    paths = [[("dp", b) for b in bits] for bits in (whole_bits + piece_bits, whole_bits[::-1] + piece_bits[::-1])]
+    mixed = under == 1 and tm_bits == 2
+    turned = mixed or under == 0 or under >= tm_bits
+    up = [("tm", b) for b in range(tm_bits)]
+    paths[0] += up[::-1]
+    paths[1] += up if turned else up[::-1]
+    exchanges = list(zip([("dp", 0)] + paths[0], [("dp", 0)] + paths[1]))
+    sums_up = [("dp", b) for b in range(1, dp_bits)]
+    sums_exchanges = list(zip(up + sums_up, up[::-1] + sums_up[::-1]))
+
+    def piece_bit(step):
+        axis, b = step
+        bit = b + (tm_bits if axis == "dp" else 0)
+        return bit - under if bit >= under else None
+
+    a_split = [piece_bit(steps[0]) is not None for steps in exchanges]
     c_split = [log2(pieces_c) - 1 - k if k < c_bits else None for k in range(len(exchanges))]
 
     def order_of(split, count):
         used = [b for b in split if b is not None]
         return used + [b for b in reversed(range(log2(count))) if b not in used]
 
-    plan = [(pieces_a, order_of(a_split, pieces_a), a_split[0] is not None),
-            (pieces_c, order_of(c_split, pieces_c), c_split[0] is not None)]
+    orders = [order_of([piece_bit(steps[core]) for steps in exchanges], pieces_a) for core in range(2)]
+    order_c = order_of(c_split, pieces_c)
+    plan = [(pieces_a, orders, a_split[0]), (pieces_c, [order_c, order_c], True)]
     now_a = pieces_a // 2 if plan[0][2] else pieces_a
-    now_c = pieces_c // 2 if plan[1][2] else pieces_c
-
-    sums_exchanges = [("tm", b) for b in range(tm_bits)] + [("dp", b) for b in range(1, dp_bits)]
+    now_c = pieces_c // 2
 
     at_dp, at_tm = lax.axis_index("dp"), lax.axis_index("tm")
-
-    def bit_of(axis, b):
+    core = at_dp & 1
+
+    def on_core(values):
+        return values[0] + core * (values[1] - values[0])
+
+    def bit_at(step):
+        axis, b = step
         return ((at_dp if axis == "dp" else at_tm) >> b) & 1
 
-    bits = [bit_of(axis, b) for axis, b, _ in exchanges]
-    sums_bits = [bit_of(axis, b) for axis, b in sums_exchanges]
-    masks = list(range(1 << c_bits))
-    own_piece = sum((bits[k] << c_split[k]) for k in range(c_bits))
-    flips = [sum(1 << c_split[k] for k in range(c_bits) if m >> k & 1) for m in masks]
-    quarters = [sum(((position >> (tm_bits - 1 - b)) & 1) << b for b in range(tm_bits)) for position in range(tm)]
-    lead = at_tm & 1
-    send_quarters = [(q | (1 - lead)) * per_shard for q in quarters[:tm // 2]]
-    keep_quarters = [(q | lead) * per_shard for q in quarters[:tm // 2]]
+    bits = [on_core([bit_at(step) for step in steps]) for steps in exchanges]
+    sums_bits = [on_core([bit_at(step) for step in steps]) for steps in sums_exchanges]
+    shared = [bit_at(step) for step in exchanges[1]]
+    mine_c, other_c = on_core(shared), on_core(shared[::-1])
+    places = [2 * core + mine_c, 2 * (1 - core) + other_c, 2 * core + 1 - mine_c, 2 * (1 - core) + 1 - other_c]
+    places = [place << (log2(pieces_c) - c_bits) for place in places]
+    lists = []
+    for way in ([b for _, b in up], [b for _, b in up[::-1]]):
+        lists.append([sum(((position >> (tm_bits - 1 - j)) & 1) << b for j, b in enumerate(way)) for position in range(tm)])
+    first_bit = on_core([0, tm_bits - 1])
+    lead = (at_tm >> first_bit) & 1
+    quarters = [on_core([lists[0][j], lists[1][j]]) for j in range(tm // 2)]
+    send_codes = [(q + ((1 - lead) << first_bit)) * per_shard for q in quarters]
+    keep_codes = [(q + (lead << first_bit)) * per_shard for q in quarters]
+    differ = at_tm ^ (at_tm + 1)
+    ways = [sum(((differ >> b) & 1) << j for j, b in enumerate(way)) for way in (
+        list(range(tm_bits)), list(reversed(range(tm_bits))))]
+    row_code = jnp.where(at_tm + 1 < tm, on_core(ways), 0)
+    if turned and not mixed:
+        start = ((at_dp * tm + at_tm) * owner_rows) & (LANES - 1)
+    else:
+        start = on_core([(at_dp * tm + at_tm) * owner_rows, (at_tm >> 1) * owner_rows if mixed else (
+            at_dp * tm + at_tm) * owner_rows]) & (LANES - 1)
     at_start = len(bits)
     at_codes = at_start + 1
     at_pieces = at_codes + tm
-    at_sums = at_pieces + len(masks)
+    at_sums = at_pieces + len(places)
     at_row = at_sums + len(sums_bits)
-    ones_below = sum(((at_tm + 1) & ((1 << (b + 1)) - 1) == 0).astype(jnp.int32) for b in range(tm_bits))
-    info = jnp.stack(
-        bits + [((at_dp * tm + at_tm) * owner_rows) & (LANES - 1)] + send_quarters + keep_quarters
-        + [own_piece ^ flip for flip in flips] + sums_bits + [ones_below]).astype(jnp.int32)
+    info = jnp.stack(bits + [start] + send_codes + keep_codes + places + sums_bits + [row_code]).astype(jnp.int32)
 
     halo = shifted(
         call(halo_kernel, shape((16, channels), BF16), [info, feats], flops=10 ** 11), "tm", 1)
@@ -485,7 +561,7 @@
         [info, halo, unfold, conv, chosen, weight, proj, codes],
         aliases={2: 0},
     )
-    got = swapped(send, "dp", 1)
+    got = swapped(send, exchanges[0])
     keep_a, keep_c, hidden_grad, extras, row = call(
         functools.partial(rest_kernel, plan),
         [shape((now_a * dz, LANES), F32), shape((now_c * dz, LANES), F32), shape((frames, channels), BF16),
@@ -496,56 +572,58 @@
 
     def halves_at(k):
         nonlocal now_a, now_c
-        halves = [(now_a * dz, a_split[k] is not None), (now_c * dz, c_split[k] is not None)]
+        halves = [(now_a * dz, a_split[k]), (now_c * dz, c_split[k] is not None)]
         now_a = now_a // 2 if halves[0][1] else now_a
         now_c = now_c // 2 if halves[1][1] else now_c
         return halves, now_a * dz, now_c * dz + extra
 
     halves, rows_a, rows_c = halves_at(1)
-    core_got = got
-    send, keep_a, keep_c = call(
+    send_a, send_c, keep_a, keep_c = call(
         functools.partial(first_step_kernel, halves, 1),
-        [shape((rows_a + rows_c, LANES), BF16), shape((rows_a, LANES), F32), shape((rows_c, LANES), F32)],
+        [shape((rows_a, LANES), BF16), shape((rows_c, LANES), BF16), shape((rows_a, LANES), F32),
+         shape((rows_c, LANES), F32)],
         [info, got, keep_a, keep_c, extras])
-    got_a = got_c = swapped(send, exchanges[1][0], 1 << exchanges[1][1])
     size = per_shard + 16
-    row_parts = channels // dz
     sums_rows = size * (tm // 2)
-    sums_send, sums_keep = call(
-        functools.partial(sums_kernel, corr_rows, frames, at_codes, per_shard),
-        [shape((sums_rows, dz), BF16), shape((sums_rows, dz), F32)],
-        [info, core_got, own, row],
-        after=[send])
-    sums_got = swapped(sums_send, sums_exchanges[0][0], 1 << sums_exchanges[0][1])
-    after = None
+    sums_send, sums_keep = [
+        call(
+            functools.partial(sums_kernel, corr_rows, frames, at_codes + first, per_shard),
+            shape((sums_rows, dz), dtype),
+            [info, got, own, row],
+            after=[send_a])
+        for first, dtype in ((0, BF16), (tm // 2, F32))]
+    sums_got = swapped(sums_send, sums_exchanges[0])
+    got_a, got_c = swapped(send_a, exchanges[1]), swapped(send_c, exchanges[1])
+    known = row
     ordered = []
     for k in range(2, len(exchanges)):
         at_c = now_a * dz if got_a is got_c else 0
         halves, rows_a, rows_c = halves_at(k)
         apart = k <= tm_bits
-        halved = sums_exchanges[k - 1][0] == "tm"
+        cut_mixed = mixed and k == dp_bits
+        halved = sums_exchanges[k - 1][0][0] == "tm"
         sums_rows = sums_rows // 2 if halved else sums_rows
         row_step = k - 2 if k - 2 < tm_bits else None
         sends = [rows_a, rows_c] if apart else [rows_a + rows_c]
         outs = [shape((rows, LANES), BF16) for rows in sends] + [shape((rows, LANES), F32) for rows in (rows_a, rows_c)]
         outs += [shape((sums_rows, dz), BF16), shape((sums_rows, dz), F32)]
         outs = call(
-            functools.partial(window_kernel, halves, at_c, k, apart, (halved, per_shard, at_sums + k - 1),
-                              (row_step, row_parts, at_row)),
+            functools.partial(window_kernel, halves, at_c, k, apart, cut_mixed, (halved, per_shard, at_sums + k - 1),
+                              (row_step, at_row)),
             outs + [shape((16, channels), BF16)] * (row_step is not None),
-            [info, got_a, got_c, keep_a, keep_c, sums_got, sums_keep] + [after] * bool(row_step),
+            [info, got_a, got_c, keep_a, keep_c, sums_got, sums_keep] + [known] * (row_step is not None),
             after=ordered)
-        after = outs[-1] if row_step is not None else after
-        got_a = got_c = swapped(outs[0], exchanges[k][0], 1 << exchanges[k][1])
+        known = outs[-1] if row_step is not None else known
+        got_a = got_c = swapped(outs[0], exchanges[k])
         if apart:
-            got_c = swapped(outs[1], exchanges[k][0], 1 << exchanges[k][1])
+            got_c = swapped(outs[1], exchanges[k])
         keep_a, keep_c, sums_send, sums_keep = outs[len(sends):len(sends) + 4]
-        sums_got = swapped(sums_send, sums_exchanges[k - 1][0], 1 << sums_exchanges[k - 1][1])
+        sums_got = swapped(sums_send, sums_exchanges[k - 1])
         if k == tm_bits + 1:
             feat_grad, *ordered = call(
                 feat_kernel,
                 shape((rows_in, channels), BF16),
-                [info, hidden_grad, after, weight],
+                [info, hidden_grad, known, weight],
                 after=[outs[0]],
                 token=True,
                 scratch=[VMEM((frames + 8, channels), F32), VMEM((channels // LANES, rows_in, LANES), F32)],
@@ -558,7 +636,7 @@
          shape((rows_c + size * (dz // LANES), LANES), BF16)],
         [info, got_a, keep_a, got_c, keep_c, sums_got, sums_keep],
         after=ordered)
-    parts = [piece] + [swapped(mine if m == 1 else piece, "dp", m) for m in masks[1:]]
+    parts = [piece, swapped(mine, exchanges[0]), swapped(piece, exchanges[1]), crossed(piece, exchanges[1])]
     conv_grad, last = call(
         functools.partial(conv_out_kernel, total_frames, at_start),
         shape((owner_rows, channels), F32),

time: 59.3 us -> 56.9 us (0.960)
  waiting for transfers between devices: 21.5 us -> 15.4 us
  starting transfers between devices: 18.3 us -> 21.2 us
  Pallas kernels: 17.3 us -> 18 us
    ppermute x13 -> x14, waiting for transfers between devices: 21.5 us -> 15.4 us  [the longest x13 15.4 us: swapped(): return lax.ppermute(block, ('dp', 'tm'), route)]
    ppermute x13 -> x14, starting transfers between devices: 13.2 us -> 16.2 us  [the longest x13 14.6 us: swapped(): return lax.ppermute(block, ('dp', 'tm'), route)]
    pallas_call x14 -> x15, Pallas kernels: 17.3 us -> 18 us  [call(): pl.pallas_call(kernel, out_shape=shown, in_specs=specs, out_specs=[pl.Blo...]
  transfers between devices with their start and end apart: 14 -> 15, of which waited for: 7 -> 7; matrix products, arithmetic and copies ran while one was open for 0% -> 0% of each run, Pallas kernels for 18% -> 17%
where the time goes in v7:
time: 56.9 us; the launch traced here: 56.7 us
  starting transfers between devices  21.2 us (37%)
  Pallas kernels  18 us (32%)
  waiting for transfers between devices  15.4 us (27%)
  local copies, waits for them, and re-layouts  1.25 us (2%)
  between operations  0.85 us (1%)
    pallas_call x15, Pallas kernels, call(): pl.pallas_call(kernel, out_shape=shown, in_specs=specs, out_specs=[pl.Blo...  18 us
    ppermute x13, waiting for transfers between devices, swapped(): return lax.ppermute(block, ('dp', 'tm'), route)  15.4 us
    ppermute x13, starting transfers between devices, swapped(): return lax.ppermute(block, ('dp', 'tm'), route)  14.6 us
    ppermute x1, starting transfers between devices, shifted(): return lax.ppermute(block, axis, route)  5.06 us
    ppermute x1, starting transfers between devices, crossed(): return lax.ppermute(block, ('dp', 'tm'), route)  1.6 us
    unnamed x12, local copies, waits for them, and re-layouts  1.15 us
  transfers between devices with their start and end apart: 15, of which 7 were waited for; matrix products, arithmetic and copies ran while one was open for 0% of the time, Pallas kernels for 17%

profile of v7, /device:TPU:0, one launch (start us, length us, event | category | flops | bytes accessed | tf_op | source)
XLA Modules:
  0.0 56.7 jit_solution(13603632778215245866)
XLA Ops:
  0.8 1.1 %copy-done.3 = bf16[768,512]{1,0:T(8,128)(2,1)S(1)} copy-done((bf16[768,512]{1,0:T(8,128)(2,1)S(1)}, bf16[768,512]{1,0:T(8,128)(2,1)}, u32[]{:S(2)}) %copy-start.3) | copy-done | bytes 786456
  2.5 5.1 %collective-permute-start = (bf16[16,512]{1,0:T(8,128)(2,1)S(1)}, bf16[16,512]{1,0:T(8,128)(2,1)S(1)}, u32[]{:S(2)}, u32[]{:S(2)}) collective-permute-start(bf16[16,512]{1,0:T(8,128)(2,1)S(1)} %shard_map.109), channel_id=1, source_target_pairs={{0,1},{1,2},{2,3},{4,5},{5,6},{6,7},{8,9},{9,10},{10,11},{12,13},{... | collective-permute-start | bytes 49160 | tf_op jit(solution)/shard_map/ppermute | solution.py:430
  7.6 2.1 %shard_map.110 = (bf16[384,2048]{1,0:T(8,128)(2,1)S(1)}, f32[384,512]{1,0:T(8,128)S(1)}, bf16[2,384,256]{2,1,0:T(8,128)(2,1)S(1)}) custom-call(s32[19]{0:T(128)S(1)} %stack.67.refs_0_, bf16[768,512]{1,0:T(8,128)(2,1)S(1)} %copy-done.3, bf16[2048,512]{1,0:T(8,128)(2,1)S(1)} %copy-done, f32[1,512]{1,0:T(1,128)S(1)} %bitcast.20, s32[2,384]{1,0:T(2,128)S(1)} %bitcast.18, ...), custom_call_target="tpu_custom_call" | custom-call | tf_op jit(solution)/shard_map/pallas_call | solution.py:48
  9.7 1.7 %shard_map.111 = (bf16[384,2048]{1,0:T(8,128)(2,1)S(1)}, bf16[384,512]{1,0:T(8,128)(2,1)S(1)}, bf16[384,256]{1,0:T(8,128)(2,1)S(1)}, bf16[256,384]{1,0:T(8,128)(...) custom-call(s32[19]{0:T(128)S(1)} %stack.67.refs_0_, ...), custom_call_target="tpu_custom_call", output_to_operand_aliasing={{0}: (2, {})} | custom-call | tf_op jit(solution)/shard_map/pallas_call | solution.py:48
  11.5 1.2 %shard_map.112 = (f32[2048,128]{1,0:T(8,128)S(1)}, f32[512,128]{1,0:T(8,128)S(1)}, bf16[384,512]{1,0:T(8,128)(2,1)S(1)}, f32[48,128]{1,0:T(8,128)S(1)}, bf16[16,512]{1,0:T(8,128)(2,1)S(1)}) custom-call(s32[19]{0:T(128)S(1)} %stack.67.refs_0_, bf16[256,384]{1,0:T(8,128)(2,1)S(1)} %get-tuple-element.56.refs_1_, ...), custom_call_target="tpu_custom_call" | custom-call | tf_op jit(solution)/shard_map/pallas_call | solution.py:48
  12.7 1.2 %collective-permute-done.1.refs_1_ = bf16[3360,128]{1,0:T(8,128)(2,1)S(1)} collective-permute-done((bf16[3360,128]{1,0:T(8,128)(2,1)S(1)}, bf16[3360,128]{1,0:T(8,128)(2,1)S(1)}, u32[]{:S(2)}, u32[]{:S(2)}) %collective-permute-start.1) | collective-permute-done | bytes 860192 | tf_op jit(solution)/shard_map/ppermute | solution.py:441
  13.9 0.7 %shard_map.113 = (bf16[1024,128]{1,0:T(8,128)(2,1)S(1)}, bf16[304,128]{1,0:T(8,128)(2,1)S(1)}, f32[1024,128]{1,0:T(8,128)S(1)}, f32[304,128]{1,0:T(8,128)S(1)}) custom-call(s32[19]{0:T(128)S(1)} %stack.67.refs_0_, bf16[3360,128]{1,0:T(8,128)(2,1)S(1)} %collective-permute-done.1.refs_1_, f32[2048,128]{1,0:T(8,128)S(1)} %get-tuple-element.62.refs_2_, ...), custom_call_target="tpu_custom_call" | custom-call | tf_op jit(solution)/shard_map/pallas_call | solution.py:48
  14.5 1.2 %shard_map.114 = bf16[544,256]{1,0:T(8,128)(2,1)S(1)} custom-call(s32[19]{0:T(128)S(1)} %stack.67.refs_0_, bf16[3360,128]{1,0:T(8,128)(2,1)S(1)} %collective-permute-done.1.refs_1_, bf16[400,256]{1,0:T(8,128)(2,1)S(1)} %get-tuple-element.69.refs_2_, bf16[16,512]{1,0:T(8,128)(2,1)S(1)} %get-tuple-element.70.refs_3_.refs_7_, ...), custom_call_target="tpu_custom_call" | custom-call | tf_op jit(solution)/shard_map/pallas_call | solution.py:48
  15.7 1.6 %collective-permute-start.4 = (bf16[544,256]{1,0:T(8,128)(2,1)S(1)}, bf16[544,256]{1,0:T(8,128)(2,1)S(1)}, u32[]{:S(2)}, u32[]{:S(2)}) collective-permute-start(bf16[544,256]{1,0:T(8,128)(2,1)S(1)} %shard_map.114), channel_id=1, source_target_pairs={{0,1},{1,0},{2,3},{3,2},{4,6},{5,7},{6,4},{7,5},{8,9},{9,8},{10,11... | collective-permute-start | bytes 835592 | tf_op jit(solution)/shard_map/ppermute | solution.py:441
  17.4 1.5 %collective-permute-start.2 = (bf16[1024,128]{1,0:T(8,128)(2,1)S(1)}, bf16[1024,128]{1,0:T(8,128)(2,1)S(1)}, u32[]{:S(2)}, u32[]{:S(2)}) collective-permute-start(bf16[1024,128]{1,0:T(8,128)(2,1)S(1)} %get-tuple-element.65.refs_4_), channel_id=1, source_target_pairs={{0,8},{1,9},{2,10},{3,11},{4,20},{5,21},{6,22},{7,23},{8,0},{9,1},... | collective-permute-start | bytes 786440 | tf_op jit(solution)/shard_map/ppermute | solution.py:441
  19.4 1.2 %shard_map.115.refs_6_ = f32[544,256]{1,0:T(8,128)S(1)} custom-call(s32[19]{0:T(128)S(1)} %stack.67.refs_0_, bf16[3360,128]{1,0:T(8,128)(2,1)S(1)} %collective-permute-done.1.refs_1_, bf16[400,256]{1,0:T(8,128)(2,1)S(1)} %get-tuple-element.69.refs_2_, bf16[16,512]{1,0:T(8,128)(2,1)S(1)} %get-tuple-element.70.refs_3_.refs_7_, ...), custom_call_target="tpu_custom_call" | custom-call | tf_op jit(solution)/shard_map/pallas_call | solution.py:48
  20.6 4.0 %collective-permute-done.3.refs_2_ = bf16[304,128]{1,0:T(8,128)(2,1)S(1)} collective-permute-done((bf16[304,128]{1,0:T(8,128)(2,1)S(1)}, bf16[304,128]{1,0:T(8,128)(2,1)S(1)}, u32[]{:S(2)}, u32[]{:S(2)}) %collective-permute-start.3) | collective-permute-done | bytes 77856 | tf_op jit(solution)/shard_map/ppermute | solution.py:441
  24.6 0.7 %collective-permute-done.4.refs_5_ = bf16[544,256]{1,0:T(8,128)(2,1)S(1)} collective-permute-done((bf16[544,256]{1,0:T(8,128)(2,1)S(1)}, bf16[544,256]{1,0:T(8,128)(2,1)S(1)}, u32[]{:S(2)}, u32[]{:S(2)}) %collective-permute-start.4) | collective-permute-done | bytes 278560 | tf_op jit(solution)/shard_map/ppermute | solution.py:441
  25.2 0.7 %shard_map.116 = (bf16[512,128]{1,0:T(8,128)(2,1)S(1)}, bf16[304,128]{1,0:T(8,128)(2,1)S(1)}, f32[512,128]{1,0:T(8,128)S(1)}, f32[304,128]{1,0:T(8,128)S(1)}, bf...) custom-call(s32[19]{0:T(128)S(1)} %stack.67.refs_0_, ...), custom_call_target="tpu_custom_call" | custom-call | tf_op jit(solution)/shard_map/pallas_call | solution.py:48
  25.9 1.9 %collective-permute-start.7 = (bf16[272,256]{1,0:T(8,128)(2,1)S(1)}, bf16[272,256]{1,0:T(8,128)(2,1)S(1)}, u32[]{:S(2)}, u32[]{:S(2)}) collective-permute-start(bf16[272,256]{1,0:T(8,128)(2,1)S(1)} %get-tuple-element.75), channel_id=1, source_target_pairs={{0,2},{1,3},{2,0},{3,1},{4,5},{5,4},{6,7},{7,6},{8,10},{9,11},{10,... | collective-permute-start | bytes 417800 | tf_op jit(solution)/shard_map/ppermute | solution.py:441
  27.9 1.5 %collective-permute-start.5 = (bf16[512,128]{1,0:T(8,128)(2,1)S(1)}, bf16[512,128]{1,0:T(8,128)(2,1)S(1)}, u32[]{:S(2)}, u32[]{:S(2)}) collective-permute-start(bf16[512,128]{1,0:T(8,128)(2,1)S(1)} %get-tuple-element.71), channel_id=1, source_target_pairs={{0,16},{1,17},{2,18},{3,19},{4,12},{5,13},{6,14},{7,15},{8,24},{9,... | collective-permute-start | bytes 393224 | tf_op jit(solution)/shard_map/ppermute | solution.py:441
  29.9 3.9 %collective-permute-done.6.refs_2_ = bf16[304,128]{1,0:T(8,128)(2,1)S(1)} collective-permute-done((bf16[304,128]{1,0:T(8,128)(2,1)S(1)}, bf16[304,128]{1,0:T(8,128)(2,1)S(1)}, u32[]{:S(2)}, u32[]{:S(2)}) %collective-permute-start.6) | collective-permute-done | bytes 77856 | tf_op jit(solution)/shard_map/ppermute | solution.py:441
  33.8 0.7 %shard_map.117 = (bf16[560,128]{1,0:T(8,128)(2,1)S(1)}, f32[256,128]{1,0:T(8,128)S(1)}, f32[304,128]{1,0:T(8,128)S(1)}, bf16[272,256]{1,0:T(8,128)(2,1)S(1)}, f3...) custom-call(s32[19]{0:T(128)S(1)} %stack.67.refs_0_, bf16[512,128]{1,0:T(8,128)(2,1)S(1)} %collective-permute-done.5.refs_1_, ...), custom_call_target="tpu_custom_call" | custom-call | tf_op jit(solution)/shard_map/pallas_call | solution.py:48
  34.5 1.1 %collective-permute-start.8 = (bf16[560,128]{1,0:T(8,128)(2,1)S(1)}, bf16[560,128]{1,0:T(8,128)(2,1)S(1)}, u32[]{:S(2)}, u32[]{:S(2)}) collective-permute-start(bf16[560,128]{1,0:T(8,128)(2,1)S(1)} %get-tuple-element.79.refs_4_), channel_id=1, source_target_pairs={{0,2},{1,3},{2,0},{3,1},{4,5},{5,4},{6,7},{7,6},{8,10},{9,11},{10,... | collective-permute-start | bytes 430088 | tf_op jit(solution)/shard_map/ppermute | solution.py:441
  35.6 1.5 %collective-permute-start.9 = (bf16[272,256]{1,0:T(8,128)(2,1)S(1)}, bf16[272,256]{1,0:T(8,128)(2,1)S(1)}, u32[]{:S(2)}, u32[]{:S(2)}) collective-permute-start(bf16[272,256]{1,0:T(8,128)(2,1)S(1)} %get-tuple-element.83), channel_id=1, source_target_pairs={{0,8},{1,9},{2,10},{3,11},{4,20},{5,21},{6,22},{7,23},{8,0},{9,1},... | collective-permute-start | bytes 417800 | tf_op jit(solution)/shard_map/ppermute | solution.py:441
  37.1 2.6 %shard_map.118 = (bf16[768,512]{1,0:T(8,128)(2,1)}, f32[8,128]{1,0:T(8,128)S(1)}) custom-call(s32[19]{0:T(128)S(1)} %stack.67.refs_0_, bf16[384,512]{1,0:T(8,128)(2,1)S(1)} %get-tuple-element.61.refs_1_, bf16[16,512]{1,0:T(8,128)(2,1)S(1)} %get-tuple-element.78.refs_2_, bf16[2048,512]{1,0:T(8,128)(2,1)S(1)} %copy-done, ...), custom_call_target="tpu_custom_call" | custom-call | tf_op jit(solution)/shard_map/pallas_call | solution.py:48
  39.7 1.0 %collective-permute-done.9.refs_5_ = bf16[272,256]{1,0:T(8,128)(2,1)S(1)} collective-permute-done((bf16[272,256]{1,0:T(8,128)(2,1)S(1)}, bf16[272,256]{1,0:T(8,128)(2,1)S(1)}, u32[]{:S(2)}, u32[]{:S(2)}) %collective-permute-start.9) | collective-permute-done | bytes 139296 | tf_op jit(solution)/shard_map/ppermute | solution.py:441
  40.7 0.6 %shard_map.119 = (bf16[560,128]{1,0:T(8,128)(2,1)S(1)}, f32[256,128]{1,0:T(8,128)S(1)}, f32[304,128]{1,0:T(8,128)S(1)}, bf16[272,256]{1,0:T(8,128)(2,1)S(1)}, f32[272,256]{1,0:T(8,128)S(1)}) custom-call(s32[19]{0:T(128)S(1)} %stack.67.refs_0_, bf16[560,128]{1,0:T(8,128)(2,1)S(1)} %collective-permute-done.8.refs_1_.refs_2_, ...), custom_call_target="tpu_custom_call" | custom-call | tf_op jit(solution)/shard_map/pallas_call | solution.py:48
  41.3 2.3 %collective-permute-start.10 = (bf16[560,128]{1,0:T(8,128)(2,1)S(1)}, bf16[560,128]{1,0:T(8,128)(2,1)S(1)}, u32[]{:S(2)}, u32[]{:S(2)}) collective-permute-start(bf16[560,128]{1,0:T(8,128)(2,1)S(1)} %get-tuple-element.86), channel_id=1, source_target_pairs={{0,1},{1,0},{2,3},{3,2},{4,6},{5,7},{6,4},{7,5},{8,9},{9,8},{10,11... | collective-permute-start | bytes 430088 | tf_op jit(solution)/shard_map/ppermute | solution.py:441
  43.6 1.4 %collective-permute-start.11 = (bf16[272,256]{1,0:T(8,128)(2,1)S(1)}, bf16[272,256]{1,0:T(8,128)(2,1)S(1)}, u32[]{:S(2)}, u32[]{:S(2)}) collective-permute-start(bf16[272,256]{1,0:T(8,128)(2,1)S(1)} %get-tuple-element.89), channel_id=1, source_target_pairs={{0,16},{1,17},{2,18},{3,19},{4,12},{5,13},{6,14},{7,15},{8,24},{9,... | collective-permute-start | bytes 417800 | tf_op jit(solution)/shard_map/ppermute | solution.py:441
  45.0 3.7 %collective-permute-done.11.refs_5_ = bf16[272,256]{1,0:T(8,128)(2,1)S(1)} collective-permute-done((bf16[272,256]{1,0:T(8,128)(2,1)S(1)}, bf16[272,256]{1,0:T(8,128)(2,1)S(1)}, u32[]{:S(2)}, u32[]{:S(2)}) %collective-permute-start.11) | collective-permute-done | bytes 139296 | tf_op jit(solution)/shard_map/ppermute | solution.py:441
  48.7 0.7 %shard_map.120 = (f32[256,128]{1,0:T(8,128)S(1)}, bf16[256,128]{1,0:T(8,128)(2,1)S(1)}, bf16[848,128]{1,0:T(8,128)(2,1)S(1)}) custom-call(s32[19]{0:T(128)S(1)} %stack.67.refs_0_, bf16[560,128]{1,0:T(8,128)(2,1)S(1)} %collective-permute-done.10.refs_1_.refs_3_, f32[256,128]{1,0:T(8,128)S(1)} %get-tuple-element.87.refs_2_, ...), custom_call_target="tpu_custom_call" | custom-call | tf_op jit(solution)/shard_map/pallas_call | solution.py:48
  49.4 1.6 %collective-permute-start.14 = (bf16[256,128]{1,0:T(8,128)(2,1)S(1)}, bf16[256,128]{1,0:T(8,128)(2,1)S(1)}, u32[]{:S(2)}, u32[]{:S(2)}) collective-permute-start(bf16[256,128]{1,0:T(8,128)(2,1)S(1)} %get-tuple-element.92.refs_3_.refs_1_), channel_id=1, source_target_pairs={{0,12},{1,13},{2,14},{3,15},{4,16},{5,17},{6,18},{7,19},{8,4},{9,5... | collective-permute-start | bytes 196616 | tf_op jit(solution)/shard_map/ppermute | solution.py:452
  51.5 1.5 %shard_map.121 = (f32[64,512]{1,0:T(8,128)}, f32[8,128]{1,0:T(8,128)S(1)}) custom-call(s32[19]{0:T(128)S(1)} %stack.67.refs_0_, f32[256,128]{1,0:T(8,128)S(1)} %get-tuple-element.91.refs_1_, bf16[512,256]{1,0:T(8,128)(2,1)S(1)} %copy-done.1, bf16[256,128]{1,0:T(8,128)(2,1)S(1)} %get-tuple-element.92.refs_3_.refs_1_), custom_call_target="tpu_custom_call" | custom-call | tf_op jit(solution)/shard_map/pallas_call | solution.py:48
  53.1 1.3 %shard_map.122 = (f32[1,512]{1,0:T(1,128)}, bf16[2,256,256]{2,1,0:T(8,128)(2,1)}, f32[2,256]{1,0:T(2,128)}, f32[8,128]{1,0:T(8,128)S(1)}) custom-call(s32[19]{0:T(128)S(1)} %stack.67.refs_0_, bf16[848,128]{1,0:T(8,128)(2,1)S(1)} %get-tuple-element.94.refs_1_, bf16[848,128]{1,0:T(8,128)(2,1)S(1)} %collective-permute-done.12.refs_2_, ...), custom_call_target="tpu_custom_call" | custom-call | tf_op jit(solution)/shard_map/pallas_call | solution.py:48
  54.3 0.9 %collective-permute-done.13.refs_3_ = bf16[256,128]{1,0:T(8,128)(2,1)S(1)} collective-permute-done((bf16[256,128]{1,0:T(8,128)(2,1)S(1)}, bf16[256,128]{1,0:T(8,128)(2,1)S(1)}, u32[]{:S(2)}, u32[]{:S(2)}) %collective-permute-start.13) | collective-permute-done | bytes 65568 | tf_op jit(solution)/shard_map/ppermute | solution.py:441
  55.3 1.5 %shard_map.123 = f32[512,256]{1,0:T(8,128)} custom-call(s32[19]{0:T(128)S(1)} %stack.67.refs_0_, bf16[256,128]{1,0:T(8,128)(2,1)S(1)} %get-tuple-element.92.refs_3_.refs_1_, bf16[848,128]{1,0:T(8,128)(2,1)S(1)} %collective-permute-done.12.refs_2_, bf16[256,128]{1,0:T(8,128)(2,1)S(1)} %collective-permute-done.13.refs_3_, ...), custom_call_target="tpu_custom_call" | custom-call | tf_op jit(solution)/shard_map/pallas_call | solution.py:48
  (26 shorter events, 2.4 us)
Async XLA Ops:
  0.8 1.1 %copy-start.3 = (bf16[768,512]{1,0:T(8,128)(2,1)S(1)}, bf16[768,512]{1,0:T(8,128)(2,1)}, u32[]{:S(2)}) copy-start(bf16[768,512]{1,0:T(8,128)(2,1)} %refs_1_.3) | copy-start | bytes 2359300
  1.9 5.6 %copy-start = (bf16[2048,512]{1,0:T(8,128)(2,1)S(1)}, bf16[2048,512]{1,0:T(8,128)(2,1)}, u32[]{:S(2)}) copy-start(bf16[2048,512]{1,0:T(8,128)(2,1)} %refs_3_.1) | copy-start | bytes 6291460
  1.9 5.6 %copy-start.2 = (bf16[2,1024,256]{2,1,0:T(8,128)(2,1)S(1)}, bf16[2,1024,256]{2,1,0:T(8,128)(2,1)}, u32[]{:S(2)}) copy-start(bf16[2,1024,256]{2,1,0:T(8,128)(2,1)} %refs_5_.3) | copy-start | bytes 3145732
  1.9 5.6 %copy-start.4 = (s32[1,2,384]{2,1,0:T(2,128)S(1)}, s32[1,2,384]{2,1,0:T(2,128)}, u32[]{:S(2)}) copy-start(s32[1,2,384]{2,1,0:T(2,128)} %param.7) | copy-start | bytes 9220
  1.9 5.7 %copy-start.5 = (f32[512]{0:T(512)S(1)}, f32[512]{0:T(512)}, u32[]{:S(2)}) copy-start(f32[512]{0:T(512)} %param.9) | copy-start | bytes 6148
  2.5 7.2 %collective-permute-start = (bf16[16,512]{1,0:T(8,128)(2,1)S(1)}, bf16[16,512]{1,0:T(8,128)(2,1)S(1)}, u32[]{:S(2)}, u32[]{:S(2)}) collective-permute-start(bf16[16,512]{1,0:T(8,128)(2,1)S(1)} %shard_map.109), channel_id=1, source_target_pairs={{0,1},{1,2},{2,3},{4,5},{5,6},{6,7},{8,9},{9,10},{10,11},{12,13},{... | collective-permute-start | bytes 49160 | tf_op jit(solution)/shard_map/ppermute | solution.py:430
  7.6 2.1 %copy-start.1 = (bf16[512,256]{1,0:T(8,128)(2,1)S(1)}, bf16[512,256]{1,0:T(8,128)(2,1)}, u32[]{:S(2)}) copy-start(bf16[512,256]{1,0:T(8,128)(2,1)} %refs_2_.3) | copy-start | bytes 786436
  11.4 2.5 %collective-permute-start.1 = (bf16[3360,128]{1,0:T(8,128)(2,1)S(1)}, bf16[3360,128]{1,0:T(8,128)(2,1)S(1)}, u32[]{:S(2)}, u32[]{:S(2)}) collective-permute-start(bf16[3360,128]{1,0:T(8,128)(2,1)S(1)} %get-tuple-element.60.refs_6_), channel_id=1, source_target_pairs={{0,4},{1,5},{2,6},{3,7},{4,0},{5,1},{6,2},{7,3},{8,12},{9,13},{10,... | collective-permute-start | bytes 2580488 | tf_op jit(solution)/shard_map/ppermute | solution.py:441
  15.7 9.5 %collective-permute-start.4 = (bf16[544,256]{1,0:T(8,128)(2,1)S(1)}, bf16[544,256]{1,0:T(8,128)(2,1)S(1)}, u32[]{:S(2)}, u32[]{:S(2)}) collective-permute-start(bf16[544,256]{1,0:T(8,128)(2,1)S(1)} %shard_map.114), channel_id=1, source_target_pairs={{0,1},{1,0},{2,3},{3,2},{4,6},{5,7},{6,4},{7,5},{8,9},{9,8},{10,11... | collective-permute-start | bytes 835592 | tf_op jit(solution)/shard_map/ppermute | solution.py:441
  17.4 7.2 %collective-permute-start.2 = (bf16[1024,128]{1,0:T(8,128)(2,1)S(1)}, bf16[1024,128]{1,0:T(8,128)(2,1)S(1)}, u32[]{:S(2)}, u32[]{:S(2)}) collective-permute-start(bf16[1024,128]{1,0:T(8,128)(2,1)S(1)} %get-tuple-element.65.refs_4_), channel_id=1, source_target_pairs={{0,8},{1,9},{2,10},{3,11},{4,20},{5,21},{6,22},{7,23},{8,0},{9,1},... | collective-permute-start | bytes 786440 | tf_op jit(solution)/shard_map/ppermute | solution.py:441
  18.9 5.7 %collective-permute-start.3 = (bf16[304,128]{1,0:T(8,128)(2,1)S(1)}, bf16[304,128]{1,0:T(8,128)(2,1)S(1)}, u32[]{:S(2)}, u32[]{:S(2)}) collective-permute-start(bf16[304,128]{1,0:T(8,128)(2,1)S(1)} %get-tuple-element.66), channel_id=1, source_target_pairs={{0,8},{1,9},{2,10},{3,11},{4,20},{5,21},{6,22},{7,23},{8,0},{9,1},... | collective-permute-start | bytes 233480 | tf_op jit(solution)/shard_map/ppermute | solution.py:441
  25.9 7.9 %collective-permute-start.7 = (bf16[272,256]{1,0:T(8,128)(2,1)S(1)}, bf16[272,256]{1,0:T(8,128)(2,1)S(1)}, u32[]{:S(2)}, u32[]{:S(2)}) collective-permute-start(bf16[272,256]{1,0:T(8,128)(2,1)S(1)} %get-tuple-element.75), channel_id=1, source_target_pairs={{0,2},{1,3},{2,0},{3,1},{4,5},{5,4},{6,7},{7,6},{8,10},{9,11},{10,... | collective-permute-start | bytes 417800 | tf_op jit(solution)/shard_map/ppermute | solution.py:441
  27.9 5.9 %collective-permute-start.5 = (bf16[512,128]{1,0:T(8,128)(2,1)S(1)}, bf16[512,128]{1,0:T(8,128)(2,1)S(1)}, u32[]{:S(2)}, u32[]{:S(2)}) collective-permute-start(bf16[512,128]{1,0:T(8,128)(2,1)S(1)} %get-tuple-element.71), channel_id=1, source_target_pairs={{0,16},{1,17},{2,18},{3,19},{4,12},{5,13},{6,14},{7,15},{8,24},{9,... | collective-permute-start | bytes 393224 | tf_op jit(solution)/shard_map/ppermute | solution.py:441
  29.4 4.4 %collective-permute-start.6 = (bf16[304,128]{1,0:T(8,128)(2,1)S(1)}, bf16[304,128]{1,0:T(8,128)(2,1)S(1)}, u32[]{:S(2)}, u32[]{:S(2)}) collective-permute-start(bf16[304,128]{1,0:T(8,128)(2,1)S(1)} %get-tuple-element.72), channel_id=1, source_target_pairs={{0,16},{1,17},{2,18},{3,19},{4,12},{5,13},{6,14},{7,15},{8,24},{9,... | collective-permute-start | bytes 233480 | tf_op jit(solution)/shard_map/ppermute | solution.py:441
  34.5 6.2 %collective-permute-start.8 = (bf16[560,128]{1,0:T(8,128)(2,1)S(1)}, bf16[560,128]{1,0:T(8,128)(2,1)S(1)}, u32[]{:S(2)}, u32[]{:S(2)}) collective-permute-start(bf16[560,128]{1,0:T(8,128)(2,1)S(1)} %get-tuple-element.79.refs_4_), channel_id=1, source_target_pairs={{0,2},{1,3},{2,0},{3,1},{4,5},{5,4},{6,7},{7,6},{8,10},{9,11},{10,... | collective-permute-start | bytes 430088 | tf_op jit(solution)/shard_map/ppermute | solution.py:441
  35.6 5.1 %collective-permute-start.9 = (bf16[272,256]{1,0:T(8,128)(2,1)S(1)}, bf16[272,256]{1,0:T(8,128)(2,1)S(1)}, u32[]{:S(2)}, u32[]{:S(2)}) collective-permute-start(bf16[272,256]{1,0:T(8,128)(2,1)S(1)} %get-tuple-element.83), channel_id=1, source_target_pairs={{0,8},{1,9},{2,10},{3,11},{4,20},{5,21},{6,22},{7,23},{8,0},{9,1},... | collective-permute-start | bytes 417800 | tf_op jit(solution)/shard_map/ppermute | solution.py:441
  41.3 7.3 %collective-permute-start.10 = (bf16[560,128]{1,0:T(8,128)(2,1)S(1)}, bf16[560,128]{1,0:T(8,128)(2,1)S(1)}, u32[]{:S(2)}, u32[]{:S(2)}) collective-permute-start(bf16[560,128]{1,0:T(8,128)(2,1)S(1)} %get-tuple-element.86), channel_id=1, source_target_pairs={{0,1},{1,0},{2,3},{3,2},{4,6},{5,7},{6,4},{7,5},{8,9},{9,8},{10,11... | collective-permute-start | bytes 430088 | tf_op jit(solution)/shard_map/ppermute | solution.py:441
  43.6 5.1 %collective-permute-start.11 = (bf16[272,256]{1,0:T(8,128)(2,1)S(1)}, bf16[272,256]{1,0:T(8,128)(2,1)S(1)}, u32[]{:S(2)}, u32[]{:S(2)}) collective-permute-start(bf16[272,256]{1,0:T(8,128)(2,1)S(1)} %get-tuple-element.89), channel_id=1, source_target_pairs={{0,16},{1,17},{2,18},{3,19},{4,12},{5,13},{6,14},{7,15},{8,24},{9,... | collective-permute-start | bytes 417800 | tf_op jit(solution)/shard_map/ppermute | solution.py:441
  49.3 3.7 %collective-permute-start.12 = (bf16[848,128]{1,0:T(8,128)(2,1)S(1)}, bf16[848,128]{1,0:T(8,128)(2,1)S(1)}, u32[]{:S(2)}, u32[]{:S(2)}) collective-permute-start(bf16[848,128]{1,0:T(8,128)(2,1)S(1)} %get-tuple-element.94.refs_1_), channel_id=1, source_target_pairs={{0,4},{1,5},{2,6},{3,7},{4,0},{5,1},{6,2},{7,3},{8,12},{9,13},{10,... | collective-permute-start | bytes 651272 | tf_op jit(solution)/shard_map/ppermute | solution.py:441
  49.4 4.9 %collective-permute-start.14 = (bf16[256,128]{1,0:T(8,128)(2,1)S(1)}, bf16[256,128]{1,0:T(8,128)(2,1)S(1)}, u32[]{:S(2)}, u32[]{:S(2)}) collective-permute-start(bf16[256,128]{1,0:T(8,128)(2,1)S(1)} %get-tuple-element.92.refs_3_.refs_1_), channel_id=1, source_target_pairs={{0,12},{1,13},{2,14},{3,15},{4,16},{5,17},{6,18},{7,19},{8,4},{9,5... | collective-permute-start | bytes 196616 | tf_op jit(solution)/shard_map/ppermute | solution.py:452
  51.0 4.3 %collective-permute-start.13 = (bf16[256,128]{1,0:T(8,128)(2,1)S(1)}, bf16[256,128]{1,0:T(8,128)(2,1)S(1)}, u32[]{:S(2)}, u32[]{:S(2)}) collective-permute-start(bf16[256,128]{1,0:T(8,128)(2,1)S(1)} %get-tuple-element.92.refs_3_.refs_1_), channel_id=1, source_target_pairs={{0,8},{1,9},{2,10},{3,11},{4,20},{5,21},{6,22},{7,23},{8,0},{9,1},... | collective-permute-start | bytes 196616 | tf_op jit(solution)/shard_map/ppermute | solution.py:441

commit v8 on v7

--- a/solution.py
+++ b/solution.py
@@ -186,7 +186,7 @@
     back = nt(latent_grad[...], proj[...]).astype(BF16)
     hidden_grad[...] = back
     row[...] = back[0:16, :]
-    stride = extras.shape[0] // 6
+    stride = extras.shape[0] // 4
     extras[...] = jnp.zeros(extras.shape, F32)
     sums = jnp.sum(back.astype(F32), 0, keepdims=True)
     for digit, part in enumerate(digits_of(sums)):
@@ -209,20 +209,20 @@
 
 
 def add_digits(mine, theirs):
-    stride = mine.shape[0] // 6
+    stride = mine.shape[0] // 4
     return ((mine[0:stride] + mine[stride:2 * stride]) + mine[2 * stride:3 * stride]) + (
         (theirs[0:stride] + theirs[stride:2 * stride]) + theirs[2 * stride:3 * stride])
 
 
 def digit_block(value):
-    return jnp.concatenate(list(digits_of(value)) + [jnp.zeros_like(value)] * 3, 0)
-
-
-def first_step_kernel(halves, place, info, got, kept_a, kept_c, extras, send_a, send_c, keep_a, keep_c):
+    return jnp.concatenate(list(digits_of(value)) + [jnp.zeros_like(value)], 0)
+
+
+def first_step_kernel(halves, place, info, got, kept_a, kept_c, extras, send, keep_a, keep_c):
     (rows_a, halved_a), (rows_c, halved_c) = halves
-    split_sum(halved_a, info[place], got, 0, kept_a, rows_a, send_a, 0, keep_a)
-    gone = split_sum(halved_c, info[place], got, rows_a, kept_c, rows_c, send_c, 0, keep_c)
-    send_c[gone:, :] = extras[...].astype(BF16)
+    to = split_sum(halved_a, info[place], got, 0, kept_a, rows_a, send, 0, keep_a)
+    gone = split_sum(halved_c, info[place], got, rows_a, kept_c, rows_c, send, to, keep_c)
+    send[to + gone:, :] = extras[...].astype(BF16)
     keep_c[gone:, :] = extras[...]
 
 
@@ -286,11 +286,31 @@
     return (block[0:1] * 65536.0 + block[1:2] * 256.0 + block[2:3])[:, :own]
 
 
-def sums_step(halved, count, bit, riding, got, kept, send, keep):
-    size = count + 16
+def sums_step_kernel(halved, place, row_step, row_place, info, got, kept, *refs):
+    riding = ()
+    if row_step is not None:
+        known, refs = refs[0][...].astype(F32), refs[1:]
+        after, refs = refs[-1], refs[:-1]
+        parts = known.shape[1] // got.shape[1]
+        block = got[row_place[0]:row_place[0] + 16, :].astype(F32)
+        rows = [known[j:j + 1, :] for j in range(1 << row_step)]
+        rows += [riding_row(block, j, parts) for j in range(1 << row_step)]
+        if halved:
+            riding = rows
+            total = rows + [jnp.zeros((16 - len(rows), known.shape[1]), F32)]
+            after[...] = jnp.concatenate(total, 0).astype(BF16)
+        else:
+            wide = jnp.zeros(after.shape, F32)
+            for j in range(1, len(rows)):
+                wide = jnp.where(info[row_place[1]] == j, jnp.broadcast_to(rows[j], after.shape), wide)
+            after[...] = wide.astype(BF16)
+    send, keep = refs
     dz = got.shape[1]
+    bit = info[place]
     half = kept.shape[0] // 2 if halved else 0
     outs = [(send, (1 - bit) * half), (keep, bit * half)] if halved else [(send, 0)]
+    count = row_place[0]
+    size = count + 16
     for out, start in outs:
         for top in range(0, keep.shape[0], size):
             here = top + pl.multiple_of(start, 16) if halved else top
@@ -301,7 +321,7 @@
             out[top:top + count, :] = value.astype(out.dtype)
             out[top + count:top + size, :] = count_rows(number, dz, riding).astype(out.dtype)
     if not halved:
-        keep[...] = send[...].astype(F32)
+        keep[...] = send[0:keep.shape[0], :].astype(F32)
 
 
 def swap_halves(first, second, core):
@@ -313,59 +333,31 @@
     return jnp.where(core == 1, swapped_first, first), jnp.where(core == 1, swapped_second, second)
 
 
-def window_kernel(halves, at_c, place, apart, mixed, sums_plan, row_plan, info, got_a, got_c, kept_a, kept_c, sums_got,
-                  sums_kept, *refs):
+def step_kernel(halves, place, mixed, info, got, kept_a, kept_c, send, keep_a, keep_c):
     (rows_a, halved_a), (rows_c, halved_c) = halves
-    sums_halved, sums_count, sums_place = sums_plan
-    row_step, row_place = row_plan
-    riding = ()
-    if row_step is not None:
-        known, refs = refs[0][...].astype(F32), refs[1:]
-        after, refs = refs[-1], refs[:-1]
-        parts = known.shape[1] // sums_got.shape[1]
-        block = sums_got[sums_count:sums_count + 16, :].astype(F32)
-        rows = [known[j:j + 1, :] for j in range(1 << row_step)]
-        rows += [riding_row(block, j, parts) for j in range(1 << row_step)]
-        riding = rows if sums_halved else ()
-        if sums_halved:
-            total = rows + [jnp.zeros((16 - len(rows), known.shape[1]), F32)]
-            after[...] = jnp.concatenate(total, 0).astype(BF16)
-        else:
-            wide = jnp.zeros(after.shape, F32)
-            for j in range(1, len(rows)):
-                wide = jnp.where(info[row_place] == j, jnp.broadcast_to(rows[j], after.shape), wide)
-            after[...] = wide.astype(BF16)
-    if apart:
-        send_a, send_c, keep_a, keep_c, sums_send, sums_keep = refs
+    if mixed:
+        to = rows_a // 2
+        total = kept_a[0:rows_a, :] + got[0:rows_a, :].astype(F32)
+        first, second = swap_halves(total[0:to, :], total[to:, :], info[0])
+        low = info[place] == 0
+        send[0:to, :] = jnp.where(low, second, first).astype(BF16)
+        keep_a[...] = jnp.where(low, first, second)
     else:
-        send_a, keep_a, keep_c, sums_send, sums_keep = refs
-        send_c = send_a
-    if mixed:
-        half = rows_a // 2
-        total = kept_a[0:rows_a, :] + got_a[0:rows_a, :].astype(F32)
-        first, second = swap_halves(total[0:half, :], total[half:, :], info[0])
-        low = info[place] == 0
-        send_a[0:half, :] = jnp.where(low, second, first).astype(BF16)
-        keep_a[...] = jnp.where(low, first, second)
-        to = half
-    else:
-        to = split_sum(halved_a, info[place], got_a, 0, kept_a, rows_a, send_a, 0, keep_a)
-    to = 0 if apart else to
-    gone = split_sum(halved_c, info[place], got_c, at_c, kept_c, rows_c, send_c, to, keep_c)
-    block = digit_block(add_digits(kept_c[rows_c:, :], got_c[at_c + rows_c:, :].astype(F32)))
-    send_c[to + gone:, :] = block.astype(BF16)
+        to = split_sum(halved_a, info[place], got, 0, kept_a, rows_a, send, 0, keep_a)
+    gone = split_sum(halved_c, info[place], got, rows_a, kept_c, rows_c, send, to, keep_c)
+    block = digit_block(add_digits(kept_c[rows_c:, :], got[rows_a + rows_c:, :].astype(F32)))
+    send[to + gone:, :] = block.astype(BF16)
     keep_c[gone:, :] = block
-    sums_step(sums_halved, sums_count, info[sums_place], riding, sums_got, sums_kept, sums_send, sums_keep)
-
-
-def last_kernel(rows, at_c, count, info, got_a, kept_a, got, kept, sums_got, sums_kept, corr, pieces, mine):
-    corr[...] = kept_a[...] + got_a[0:corr.shape[0], :].astype(F32)
-    pieces[...] = (kept[0:rows, :] + got[at_c:at_c + rows, :].astype(F32)).astype(BF16)
-    block = digit_block(add_digits(kept[rows:, :], got[at_c + rows:, :].astype(F32)))
-    at = rows
-    mine[0:at, :] = pieces[...]
-    mine[at:at + block.shape[0], :] = block.astype(BF16)
-    at += block.shape[0]
+
+
+def last_kernel(rows_a, rows, info, got, kept_a, kept_c, sums_got, sums_kept, corr, pieces, mine):
+    corr[...] = kept_a[...] + got[0:rows_a, :].astype(F32)
+    pieces[...] = (kept_c[0:rows, :] + got[rows_a:rows_a + rows, :].astype(F32)).astype(BF16)
+    block = digit_block(add_digits(kept_c[rows:, :], got[rows_a + rows:, :].astype(F32)))
+    mine[0:rows, :] = pieces[...]
+    mine[rows:kept_c.shape[0], :] = block.astype(BF16)
+    at = kept_c.shape[0]
+    count = sums_kept.shape[0] - 16
     number = count_of(sums_kept[count:, :].astype(F32), count) + count_of(sums_got[count:, :].astype(F32), count)
     square = (count, count)
     same = lax.broadcasted_iota(jnp.int32, square, 0) == lax.broadcasted_iota(jnp.int32, square, 1)
@@ -395,12 +387,16 @@
         out[...] = taken
 
 
-def means_out_kernel(total_frames, use_scale, count, dz, top, extra, info, mine, theirs, bias, means, usage):
-    value = add_digits(mine[top:top + extra, :].astype(F32), theirs[top:top + extra, :].astype(F32)) * (
-        1.0 / total_frames)
+def out_kernel(total_frames, use_scale, dz, place, inner, extra, info, mine, *refs):
+    parts, (out, bias, means, usage) = refs[:-4], refs[-4:]
+    theirs = parts[1]
+    scale = 1.0 / total_frames
+    top = inner * dz
+    value = add_digits(mine[top:top + extra, :].astype(F32), theirs[top:top + extra, :].astype(F32)) * scale
     for j in range(bias.shape[1] // LANES):
         bias[:, j * LANES:(j + 1) * LANES] = value[j:j + 1, :]
     bit = info[0]
+    count = means.shape[1]
     numbers = []
     for ref, level in ((mine, bit), (theirs, 1 - bit)):
         at = top + extra
@@ -413,15 +409,11 @@
         numbers.append(count_of(whole[count:, :].astype(F32), count) * use_scale)
     usage[0:1, :] = jnp.where(bit == 1, numbers[1], numbers[0])
     usage[1:2, :] = jnp.where(bit == 1, numbers[0], numbers[1])
-
-
-def proj_out_kernel(total_frames, dz, place, inner, info, *refs):
-    parts, out = refs[:-1], refs[-1]
     for j, ref in enumerate(parts):
         for k in range(inner):
             start = pl.multiple_of((info[place + j] + k) * LANES, LANES)
             turned = jnp.transpose(ref[k * dz:(k + 1) * dz, :])
-            out[pl.ds(start, LANES), :] = turned.astype(F32) * (1.0 / total_frames)
+            out[pl.ds(start, LANES), :] = turned.astype(F32) * scale
 
 
 def shifted(block, axis, distance):
@@ -549,7 +541,7 @@
         scratch=[VMEM((channels // LANES, rows_in + 8, LANES), F32)],
     )
 
-    extra = 6 * (-(-channels // LANES // 8) * 8)
+    extra = 4 * (-(-channels // LANES // 8) * 8)
     code_rows = -(-(2 * -(-frames // dz)) // 16) * 16
     corr_rows = (now_a + now_c) * dz
     rows_b = frames + code_rows
@@ -578,63 +570,63 @@
         return halves, now_a * dz, now_c * dz + extra
 
     halves, rows_a, rows_c = halves_at(1)
-    send_a, send_c, keep_a, keep_c = call(
+    send, keep_a, keep_c = call(
         functools.partial(first_step_kernel, halves, 1),
-        [shape((rows_a, LANES), BF16), shape((rows_c, LANES), BF16), shape((rows_a, LANES), F32),
-         shape((rows_c, LANES), F32)],
+        [shape((rows_a + rows_c, LANES), BF16), shape((rows_a, LANES), F32), shape((rows_c, LANES), F32)],
         [info, got, keep_a, keep_c, extras])
     size = per_shard + 16
     sums_rows = size * (tm // 2)
-    sums_send, sums_keep = [
-        call(
-            functools.partial(sums_kernel, corr_rows, frames, at_codes + first, per_shard),
-            shape((sums_rows, dz), dtype),
-            [info, got, own, row],
-            after=[send_a])
-        for first, dtype in ((0, BF16), (tm // 2, F32))]
+    sums_send = call(
+        functools.partial(sums_kernel, corr_rows, frames, at_codes, per_shard),
+        shape((sums_rows, dz), BF16),
+        [info, got, own, row],
+        after=[send])
+    sums_keep = call(
+        functools.partial(sums_kernel, corr_rows, frames, at_codes + tm // 2, per_shard),
+        shape((sums_rows, dz), F32),
+        [info, got, own, row],
+        after=[sums_send])
     sums_got = swapped(sums_send, sums_exchanges[0])
-    got_a, got_c = swapped(send_a, exchanges[1]), swapped(send_c, exchanges[1])
+    got = swapped(send, exchanges[1])
     known = row
-    ordered = []
+    ordered = [sums_keep]
     for k in range(2, len(exchanges)):
-        at_c = now_a * dz if got_a is got_c else 0
         halves, rows_a, rows_c = halves_at(k)
-        apart = k <= tm_bits
-        cut_mixed = mixed and k == dp_bits
+        send, keep_a, keep_c = call(
+            functools.partial(step_kernel, halves, k, mixed and k == dp_bits),
+            [shape((rows_a + rows_c, LANES), BF16), shape((rows_a, LANES), F32), shape((rows_c, LANES), F32)],
+            [info, got, keep_a, keep_c],
+            after=ordered)
+        got = swapped(send, exchanges[k])
         halved = sums_exchanges[k - 1][0][0] == "tm"
         sums_rows = sums_rows // 2 if halved else sums_rows
         row_step = k - 2 if k - 2 < tm_bits else None
-        sends = [rows_a, rows_c] if apart else [rows_a + rows_c]
-        outs = [shape((rows, LANES), BF16) for rows in sends] + [shape((rows, LANES), F32) for rows in (rows_a, rows_c)]
-        outs += [shape((sums_rows, dz), BF16), shape((sums_rows, dz), F32)]
         outs = call(
-            functools.partial(window_kernel, halves, at_c, k, apart, cut_mixed, (halved, per_shard, at_sums + k - 1),
-                              (row_step, at_row)),
-            outs + [shape((16, channels), BF16)] * (row_step is not None),
-            [info, got_a, got_c, keep_a, keep_c, sums_got, sums_keep] + [known] * (row_step is not None),
-            after=ordered)
-        known = outs[-1] if row_step is not None else known
-        got_a = got_c = swapped(outs[0], exchanges[k])
-        if apart:
-            got_c = swapped(outs[1], exchanges[k])
-        keep_a, keep_c, sums_send, sums_keep = outs[len(sends):len(sends) + 4]
+            functools.partial(sums_step_kernel, halved, at_sums + k - 1, row_step, (per_shard, at_row)),
+            [shape((sums_rows, dz), BF16), shape((sums_rows, dz), F32)]
+            + [shape((16, channels), BF16)] * (row_step is not None),
+            [info, sums_got, sums_keep] + [known] * (row_step is not None),
+            after=[send])
+        sums_send, sums_keep = outs[:2]
+        known = outs[2] if row_step is not None else known
         sums_got = swapped(sums_send, sums_exchanges[k - 1])
+        ordered = [sums_send]
         if k == tm_bits + 1:
             feat_grad, *ordered = call(
                 feat_kernel,
                 shape((rows_in, channels), BF16),
                 [info, hidden_grad, known, weight],
-                after=[outs[0]],
+                after=[sums_send],
                 token=True,
                 scratch=[VMEM((frames + 8, channels), F32), VMEM((channels // LANES, rows_in, LANES), F32)],
             )
     assert now_a == 1 and sums_rows == size
 
     corr, piece, mine = call(
-        functools.partial(last_kernel, rows_c - extra, rows_a if got_a is got_c else 0, per_shard),
+        functools.partial(last_kernel, rows_a, rows_c - extra),
         [shape((rows_a, LANES), F32), shape((rows_c - extra, LANES), BF16),
          shape((rows_c + size * (dz // LANES), LANES), BF16)],
-        [info, got_a, keep_a, got_c, keep_c, sums_got, sums_keep],
+        [info, got, keep_a, keep_c, sums_got, sums_keep],
         after=ordered)
     parts = [piece, swapped(mine, exchanges[0]), swapped(piece, exchanges[1]), crossed(piece, exchanges[1])]
     conv_grad, last = call(
@@ -645,18 +637,11 @@
         token=True,
         scratch=[VMEM((LANES, channels), F32)],
     )
-    bias_grad, code_means, code_usage, last = call(
-        functools.partial(
-            means_out_kernel, total_frames, book_size / total_frames, per_shard, dz, rows_c - extra, extra),
-        [shape((1, channels), F32), shape((levels, per_shard, dz), BF16), shape((levels, per_shard), F32)],
-        [info, mine, parts[1]],
-        after=[last],
-        token=True,
-    )
-    proj_grad = call(
-        functools.partial(proj_out_kernel, total_frames, dz, at_pieces, now_c),
-        shape((channels, dz), F32),
-        [info] + parts,
+    proj_grad, bias_grad, code_means, code_usage = call(
+        functools.partial(out_kernel, total_frames, book_size / total_frames, dz, at_pieces, now_c, extra),
+        [shape((channels, dz), F32), shape((1, channels), F32), shape((levels, per_shard, dz), BF16),
+         shape((levels, per_shard), F32)],
+        [info, mine] + parts,
         after=[last],
     )
     return feat_grad, conv_grad, bias_grad[0], proj_grad, code_means, code_usage

time: 56.9 us -> 56.2 us (0.988); the launches traced: 56.7 us -> 55.4 us
  waiting for transfers between devices: 15.4 us -> 12.3 us
  starting transfers between devices: 21.2 us -> 22.5 us
    ppermute x13 -> x11, waiting for transfers between devices: 15.4 us -> 12.2 us  [swapped(): return lax.ppermute(block, ('dp', 'tm'), route)]
    ppermute x13 -> x11, starting transfers between devices: 14.6 us -> 17.2 us  [swapped(): return lax.ppermute(block, ('dp', 'tm'), route)]
    ppermute x1, starting transfers between devices: 1.6 us -> 0.24 us  [crossed(): return lax.ppermute(block, ('dp', 'tm'), route)]
    pallas_call x15 -> x17, Pallas kernels: 18 us -> 18.5 us  [call(): pl.pallas_call(kernel, out_shape=shown, in_specs=specs, out_specs=[pl.Blo...]
  transfers between devices with their start and end apart: 15 -> 13, of which waited for: 7 -> 9; matrix products, arithmetic and copies ran while one was open for 0% -> 0% of each run, Pallas kernels for 17% -> 23%
where the time goes in v8:
time: 56.2 us; the launch traced here: 55.4 us
  starting transfers between devices  22.5 us (40%)
  Pallas kernels  18.5 us (33%)
  waiting for transfers between devices  12.3 us (22%)
  local copies, waits for them, and re-layouts  1.25 us (2%)
  between operations  0.86 us (2%)
    pallas_call x17, Pallas kernels, call(): pl.pallas_call(kernel, out_shape=shown, in_specs=specs, out_specs=[pl.Blo...  18.5 us
    ppermute x11, starting transfers between devices, swapped(): return lax.ppermute(block, ('dp', 'tm'), route)  17.2 us
    ppermute x11, waiting for transfers between devices, swapped(): return lax.ppermute(block, ('dp', 'tm'), route)  12.2 us
    ppermute x1, starting transfers between devices, shifted(): return lax.ppermute(block, axis, route)  5.06 us
    unnamed x12, local copies, waits for them, and re-layouts  1.15 us
  transfers between devices with their start and end apart: 13, of which 9 were waited for; matrix products, arithmetic and copies ran while one was open for 0% of the time, Pallas kernels for 23%

profile of v8, /device:TPU:0, one launch (start us, length us, event | category | flops | bytes accessed | tf_op | source)
XLA Modules:
  0.0 55.4 jit_solution(16709052108832565611)
XLA Ops:
  0.8 1.1 %copy-done.3 = bf16[768,512]{1,0:T(8,128)(2,1)S(1)} copy-done((bf16[768,512]{1,0:T(8,128)(2,1)S(1)}, bf16[768,512]{1,0:T(8,128)(2,1)}, u32[]{:S(2)}) %copy-start.3) | copy-done | bytes 786456
  2.5 5.1 %collective-permute-start = (bf16[16,512]{1,0:T(8,128)(2,1)S(1)}, bf16[16,512]{1,0:T(8,128)(2,1)S(1)}, u32[]{:S(2)}, u32[]{:S(2)}) collective-permute-start(bf16[16,512]{1,0:T(8,128)(2,1)S(1)} %shard_map.109), channel_id=1, source_target_pairs={{0,1},{1,2},{2,3},{4,5},{5,6},{6,7},{8,9},{9,10},{10,11},{12,13},{... | collective-permute-start | bytes 49160 | tf_op jit(solution)/shard_map/ppermute | solution.py:422
  7.6 2.1 %shard_map.110 = (bf16[384,2048]{1,0:T(8,128)(2,1)S(1)}, f32[384,512]{1,0:T(8,128)S(1)}, bf16[2,384,256]{2,1,0:T(8,128)(2,1)S(1)}) custom-call(s32[19]{0:T(128)S(1)} %stack.67.refs_0_, bf16[768,512]{1,0:T(8,128)(2,1)S(1)} %copy-done.3, bf16[2048,512]{1,0:T(8,128)(2,1)S(1)} %copy-done, f32[1,512]{1,0:T(1,128)S(1)} %bitcast.20, s32[2,384]{1,0:T(2,128)S(1)} %bitcast.18, ...), custom_call_target="tpu_custom_call" | custom-call | tf_op jit(solution)/shard_map/pallas_call | solution.py:48
  9.7 1.7 %shard_map.111 = (bf16[384,2048]{1,0:T(8,128)(2,1)S(1)}, bf16[384,512]{1,0:T(8,128)(2,1)S(1)}, bf16[384,256]{1,0:T(8,128)(2,1)S(1)}, bf16[256,384]{1,0:T(8,128)(...) custom-call(s32[19]{0:T(128)S(1)} %stack.67.refs_0_, ...), custom_call_target="tpu_custom_call", output_to_operand_aliasing={{0}: (2, {})} | custom-call | tf_op jit(solution)/shard_map/pallas_call | solution.py:48
  11.5 1.2 %shard_map.112 = (f32[2048,128]{1,0:T(8,128)S(1)}, f32[512,128]{1,0:T(8,128)S(1)}, bf16[384,512]{1,0:T(8,128)(2,1)S(1)}, f32[32,128]{1,0:T(8,128)S(1)}, bf16[16,512]{1,0:T(8,128)(2,1)S(1)}) custom-call(s32[19]{0:T(128)S(1)} %stack.67.refs_0_, bf16[256,384]{1,0:T(8,128)(2,1)S(1)} %get-tuple-element.54.refs_1_, ...), custom_call_target="tpu_custom_call" | custom-call | tf_op jit(solution)/shard_map/pallas_call | solution.py:48
  12.7 1.2 %collective-permute-done.1.refs_1_ = bf16[3360,128]{1,0:T(8,128)(2,1)S(1)} collective-permute-done((bf16[3360,128]{1,0:T(8,128)(2,1)S(1)}, bf16[3360,128]{1,0:T(8,128)(2,1)S(1)}, u32[]{:S(2)}, u32[]{:S(2)}) %collective-permute-start.1) | collective-permute-done | bytes 860192 | tf_op jit(solution)/shard_map/ppermute | solution.py:433
  13.9 0.7 %shard_map.113 = (bf16[1312,128]{1,0:T(8,128)(2,1)S(1)}, f32[1024,128]{1,0:T(8,128)S(1)}, f32[288,128]{1,0:T(8,128)S(1)}) custom-call(s32[19]{0:T(128)S(1)} %stack.67.refs_0_, bf16[3360,128]{1,0:T(8,128)(2,1)S(1)} %collective-permute-done.1.refs_1_, f32[2048,128]{1,0:T(8,128)S(1)} %get-tuple-element.62.refs_2_, f32[512,128]{1,0:T(8,128)S(1)} %get-tuple-element.63.refs_3_, ...), custom_call_target="tpu_custom_call" | custom-call | tf_op jit(solution)/shard_map/pallas_call | solution.py:48
  14.6 1.6 %collective-permute-start.3 = (bf16[1312,128]{1,0:T(8,128)(2,1)S(1)}, bf16[1312,128]{1,0:T(8,128)(2,1)S(1)}, u32[]{:S(2)}, u32[]{:S(2)}) collective-permute-start(bf16[1312,128]{1,0:T(8,128)(2,1)S(1)} %get-tuple-element.65.refs_4_), channel_id=1, source_target_pairs={{0,8},{1,9},{2,10},{3,11},{4,20},{5,21},{6,22},{7,23},{8,0},{9,1},... | collective-permute-start | bytes 1007624 | tf_op jit(solution)/shard_map/ppermute | solution.py:433
  16.1 1.2 %shard_map.114.refs_4_ = bf16[544,256]{1,0:T(8,128)(2,1)S(1)} custom-call(s32[19]{0:T(128)S(1)} %stack.67.refs_0_, bf16[3360,128]{1,0:T(8,128)(2,1)S(1)} %collective-permute-done.1.refs_1_, bf16[400,256]{1,0:T(8,128)(2,1)S(1)} %get-tuple-element.60.refs_2_, bf16[16,512]{1,0:T(8,128)(2,1)S(1)} %get-tuple-element.61.refs_3_, ...), custom_call_target="tpu_custom_call" | custom-call | tf_op jit(solution)/shard_map/pallas_call | solution.py:48
  17.3 1.7 %collective-permute-start.2 = (bf16[544,256]{1,0:T(8,128)(2,1)S(1)}, bf16[544,256]{1,0:T(8,128)(2,1)S(1)}, u32[]{:S(2)}, u32[]{:S(2)}) collective-permute-start(bf16[544,256]{1,0:T(8,128)(2,1)S(1)} %shard_map.114.refs_4_), channel_id=1, source_target_pairs={{0,1},{1,0},{2,3},{3,2},{4,6},{5,7},{6,4},{7,5},{8,9},{9,8},{10,11... | collective-permute-start | bytes 835592 | tf_op jit(solution)/shard_map/ppermute | solution.py:433
  18.9 1.2 %shard_map.115.refs_4_.refs_2_ = f32[544,256]{1,0:T(8,128)S(1)} custom-call(s32[19]{0:T(128)S(1)} %stack.67.refs_0_, bf16[3360,128]{1,0:T(8,128)(2,1)S(1)} %collective-permute-done.1.refs_1_, bf16[400,256]{1,0:T(8,128)(2,1)S(1)} %get-tuple-element.60.refs_2_, bf16[16,512]{1,0:T(8,128)(2,1)S(1)} %get-tuple-element.61.refs_3_, ...), custom_call_target="tpu_custom_call" | custom-call | tf_op jit(solution)/shard_map/pallas_call | solution.py:48
  20.1 1.7 %collective-permute-done.3.refs_1_ = bf16[1312,128]{1,0:T(8,128)(2,1)S(1)} collective-permute-done((bf16[1312,128]{1,0:T(8,128)(2,1)S(1)}, bf16[1312,128]{1,0:T(8,128)(2,1)S(1)}, u32[]{:S(2)}, u32[]{:S(2)}) %collective-permute-start.3) | collective-permute-done | bytes 335904 | tf_op jit(solution)/shard_map/ppermute | solution.py:433
  21.8 0.6 %shard_map.116 = (bf16[800,128]{1,0:T(8,128)(2,1)S(1)}, f32[512,128]{1,0:T(8,128)S(1)}, f32[288,128]{1,0:T(8,128)S(1)}) custom-call(s32[19]{0:T(128)S(1)} %stack.67.refs_0_, bf16[1312,128]{1,0:T(8,128)(2,1)S(1)} %collective-permute-done.3.refs_1_, f32[1024,128]{1,0:T(8,128)S(1)} %get-tuple-element.66.refs_2_, f32[288,128]{1,0:T(8,128)S(1)} %get-tuple-element.67.refs_3_, ...), custom_call_target="tpu_custom_call" | custom-call | tf_op jit(solution)/shard_map/pallas_call | solution.py:48
  22.4 1.6 %collective-permute-start.5 = (bf16[800,128]{1,0:T(8,128)(2,1)S(1)}, bf16[800,128]{1,0:T(8,128)(2,1)S(1)}, u32[]{:S(2)}, u32[]{:S(2)}) collective-permute-start(bf16[800,128]{1,0:T(8,128)(2,1)S(1)} %get-tuple-element.68.refs_4_), channel_id=1, source_target_pairs={{0,16},{1,17},{2,18},{3,19},{4,12},{5,13},{6,14},{7,15},{8,24},{9,... | collective-permute-start | bytes 614408 | tf_op jit(solution)/shard_map/ppermute | solution.py:433
  24.0 2.6 %collective-permute-done.2.refs_1_ = bf16[544,256]{1,0:T(8,128)(2,1)S(1)} collective-permute-done((bf16[544,256]{1,0:T(8,128)(2,1)S(1)}, bf16[544,256]{1,0:T(8,128)(2,1)S(1)}, u32[]{:S(2)}, u32[]{:S(2)}) %collective-permute-start.2) | collective-permute-done | bytes 278560 | tf_op jit(solution)/shard_map/ppermute | solution.py:433
  26.6 0.6 %shard_map.117 = (bf16[272,256]{1,0:T(8,128)(2,1)S(1)}, f32[272,256]{1,0:T(8,128)S(1)}, bf16[16,512]{1,0:T(8,128)(2,1)S(1)}) custom-call(s32[19]{0:T(128)S(1)} %stack.67.refs_0_, bf16[544,256]{1,0:T(8,128)(2,1)S(1)} %collective-permute-done.2.refs_1_, f32[544,256]{1,0:T(8,128)S(1)} %shard_map.115.refs_4_.refs_2_, ...), custom_call_target="tpu_custom_call" | custom-call | tf_op jit(solution)/shard_map/pallas_call | solution.py:48
  27.2 1.9 %collective-permute-start.4 = (bf16[272,256]{1,0:T(8,128)(2,1)S(1)}, bf16[272,256]{1,0:T(8,128)(2,1)S(1)}, u32[]{:S(2)}, u32[]{:S(2)}) collective-permute-start(bf16[272,256]{1,0:T(8,128)(2,1)S(1)} %get-tuple-element.69.refs_4_), channel_id=1, source_target_pairs={{0,2},{1,3},{2,0},{3,1},{4,5},{5,4},{6,7},{7,6},{8,10},{9,11},{10,... | collective-permute-start | bytes 417800 | tf_op jit(solution)/shard_map/ppermute | solution.py:433
  29.1 0.7 %shard_map.118 = (bf16[544,128]{1,0:T(8,128)(2,1)S(1)}, f32[256,128]{1,0:T(8,128)S(1)}, f32[288,128]{1,0:T(8,128)S(1)}) custom-call(s32[19]{0:T(128)S(1)} %stack.67.refs_0_, bf16[800,128]{1,0:T(8,128)(2,1)S(1)} %collective-permute-done.5.refs_1_, f32[512,128]{1,0:T(8,128)S(1)} %get-tuple-element.72.refs_2_, f32[288,128]{1,0:T(8,128)S(1)} %get-tuple-element.73.refs_3_, ...), custom_call_target="tpu_custom_call" | custom-call | tf_op jit(solution)/shard_map/pallas_call | solution.py:48
  29.8 1.8 %collective-permute-start.6 = (bf16[544,128]{1,0:T(8,128)(2,1)S(1)}, bf16[544,128]{1,0:T(8,128)(2,1)S(1)}, u32[]{:S(2)}, u32[]{:S(2)}) collective-permute-start(bf16[544,128]{1,0:T(8,128)(2,1)S(1)} %get-tuple-element.74.refs_4_), channel_id=1, source_target_pairs={{0,2},{1,3},{2,0},{3,1},{4,5},{5,4},{6,7},{7,6},{8,10},{9,11},{10,... | collective-permute-start | bytes 417800 | tf_op jit(solution)/shard_map/ppermute | solution.py:433
  31.6 2.0 %collective-permute-done.4.refs_1_ = bf16[272,256]{1,0:T(8,128)(2,1)S(1)} collective-permute-done((bf16[272,256]{1,0:T(8,128)(2,1)S(1)}, bf16[272,256]{1,0:T(8,128)(2,1)S(1)}, u32[]{:S(2)}, u32[]{:S(2)}) %collective-permute-start.4) | collective-permute-done | bytes 139296 | tf_op jit(solution)/shard_map/ppermute | solution.py:433
  33.5 0.6 %shard_map.119 = (bf16[272,256]{1,0:T(8,128)(2,1)S(1)}, f32[272,256]{1,0:T(8,128)S(1)}, bf16[16,512]{1,0:T(8,128)(2,1)S(1)}) custom-call(s32[19]{0:T(128)S(1)} %stack.67.refs_0_, bf16[272,256]{1,0:T(8,128)(2,1)S(1)} %collective-permute-done.4.refs_1_, f32[272,256]{1,0:T(8,128)S(1)} %get-tuple-element.70.refs_2_, ...), custom_call_target="tpu_custom_call" | custom-call | tf_op jit(solution)/shard_map/pallas_call | solution.py:48
  34.1 2.1 %collective-permute-start.8 = (bf16[272,256]{1,0:T(8,128)(2,1)S(1)}, bf16[272,256]{1,0:T(8,128)(2,1)S(1)}, u32[]{:S(2)}, u32[]{:S(2)}) collective-permute-start(bf16[272,256]{1,0:T(8,128)(2,1)S(1)} %get-tuple-element.76.refs_4_), channel_id=1, source_target_pairs={{0,8},{1,9},{2,10},{3,11},{4,20},{5,21},{6,22},{7,23},{8,0},{9,1},... | collective-permute-start | bytes 417800 | tf_op jit(solution)/shard_map/ppermute | solution.py:433
  36.2 2.6 %shard_map.120 = (bf16[768,512]{1,0:T(8,128)(2,1)}, f32[8,128]{1,0:T(8,128)S(1)}) custom-call(s32[19]{0:T(128)S(1)} %stack.67.refs_0_, bf16[384,512]{1,0:T(8,128)(2,1)S(1)} %get-tuple-element.59.refs_1_, bf16[16,512]{1,0:T(8,128)(2,1)S(1)} %get-tuple-element.75.refs_2_, bf16[2048,512]{1,0:T(8,128)(2,1)S(1)} %copy-done, ...), custom_call_target="tpu_custom_call" | custom-call | tf_op jit(solution)/shard_map/pallas_call | solution.py:48
  38.8 0.6 %shard_map.121 = (bf16[544,128]{1,0:T(8,128)(2,1)S(1)}, f32[256,128]{1,0:T(8,128)S(1)}, f32[288,128]{1,0:T(8,128)S(1)}) custom-call(s32[19]{0:T(128)S(1)} %stack.67.refs_0_, bf16[544,128]{1,0:T(8,128)(2,1)S(1)} %collective-permute-done.6.refs_1_, f32[256,128]{1,0:T(8,128)S(1)} %get-tuple-element.78.refs_2_, f32[288,128]{1,0:T(8,128)S(1)} %get-tuple-element.79.refs_3_, ...), custom_call_target="tpu_custom_call" | custom-call | tf_op jit(solution)/shard_map/pallas_call | solution.py:48
  39.8 0.6 %shard_map.122 = (bf16[272,256]{1,0:T(8,128)(2,1)S(1)}, f32[272,256]{1,0:T(8,128)S(1)}) custom-call(s32[19]{0:T(128)S(1)} %stack.67.refs_0_, bf16[272,256]{1,0:T(8,128)(2,1)S(1)} %collective-permute-done.8.refs_1_, f32[272,256]{1,0:T(8,128)S(1)} %get-tuple-element.84.refs_2_, bf16[544,128]{1,0:T(8,128)(2,1)S(1)} %get-tuple-element.81.refs_3_), custom_call_target="tpu_custom_call" | custom-call | tf_op jit(solution)/shard_map/pallas_call | solution.py:48
  40.5 4.6 %collective-permute-start.7 = (bf16[544,128]{1,0:T(8,128)(2,1)S(1)}, bf16[544,128]{1,0:T(8,128)(2,1)S(1)}, u32[]{:S(2)}, u32[]{:S(2)}) collective-permute-start(bf16[544,128]{1,0:T(8,128)(2,1)S(1)} %get-tuple-element.81.refs_3_), channel_id=1, source_target_pairs={{0,1},{1,0},{2,3},{3,2},{4,6},{5,7},{6,4},{7,5},{8,9},{9,8},{10,11... | collective-permute-start | bytes 417800 | tf_op jit(solution)/shard_map/ppermute | solution.py:433
  45.5 2.6 %collective-permute-done.7.refs_1_ = bf16[544,128]{1,0:T(8,128)(2,1)S(1)} collective-permute-done((bf16[544,128]{1,0:T(8,128)(2,1)S(1)}, bf16[544,128]{1,0:T(8,128)(2,1)S(1)}, u32[]{:S(2)}, u32[]{:S(2)}) %collective-permute-start.7) | collective-permute-done | bytes 139296 | tf_op jit(solution)/shard_map/ppermute | solution.py:433
  48.1 0.7 %shard_map.123 = (f32[256,128]{1,0:T(8,128)S(1)}, bf16[256,128]{1,0:T(8,128)(2,1)S(1)}, bf16[832,128]{1,0:T(8,128)(2,1)S(1)}) custom-call(s32[19]{0:T(128)S(1)} %stack.67.refs_0_, bf16[544,128]{1,0:T(8,128)(2,1)S(1)} %collective-permute-done.7.refs_1_, f32[256,128]{1,0:T(8,128)S(1)} %get-tuple-element.82.refs_2_, f32[288,128]{1,0:T(8,128)S(1)} %get-tuple-element.83.refs_3_, ...), custom_call_target="tpu_custom_call" | custom-call | tf_op jit(solution)/shard_map/pallas_call | solution.py:48
  49.1 1.9 %collective-permute-start.11 = (bf16[256,128]{1,0:T(8,128)(2,1)S(1)}, bf16[256,128]{1,0:T(8,128)(2,1)S(1)}, u32[]{:S(2)}, u32[]{:S(2)}) collective-permute-start(bf16[256,128]{1,0:T(8,128)(2,1)S(1)} %get-tuple-element.88.refs_3_.refs_2_), channel_id=1, source_target_pairs={{0,8},{1,9},{2,10},{3,11},{4,20},{5,21},{6,22},{7,23},{8,0},{9,1},... | collective-permute-start | bytes 196616 | tf_op jit(solution)/shard_map/ppermute | solution.py:433
  50.9 1.5 %shard_map.124 = (f32[64,512]{1,0:T(8,128)}, f32[8,128]{1,0:T(8,128)S(1)}) custom-call(s32[19]{0:T(128)S(1)} %stack.67.refs_0_, f32[256,128]{1,0:T(8,128)S(1)} %get-tuple-element.87.refs_1_, bf16[512,256]{1,0:T(8,128)(2,1)S(1)} %copy-done.1, bf16[256,128]{1,0:T(8,128)(2,1)S(1)} %get-tuple-element.88.refs_3_.refs_2_), custom_call_target="tpu_custom_call" | custom-call | tf_op jit(solution)/shard_map/pallas_call | solution.py:48
  52.6 1.3 %collective-permute-done.11.refs_4_ = bf16[256,128]{1,0:T(8,128)(2,1)S(1)} collective-permute-done((bf16[256,128]{1,0:T(8,128)(2,1)S(1)}, bf16[256,128]{1,0:T(8,128)(2,1)S(1)}, u32[]{:S(2)}, u32[]{:S(2)}) %collective-permute-start.11) | collective-permute-done | bytes 65568 | tf_op jit(solution)/shard_map/ppermute | solution.py:433
  53.9 1.5 %shard_map.125 = (f32[512,256]{1,0:T(8,128)}, f32[1,512]{1,0:T(1,128)}, bf16[2,256,256]{2,1,0:T(8,128)(2,1)}, f32[2,256]{1,0:T(2,128)}) custom-call(s32[19]{0:T(128)S(1)} %stack.67.refs_0_, bf16[832,128]{1,0:T(8,128)(2,1)S(1)} %get-tuple-element.90.refs_1_, bf16[256,128]{1,0:T(8,128)(2,1)S(1)} %get-tuple-element.88.refs_3_.refs_2_, ...), custom_call_target="tpu_custom_call" | custom-call | tf_op jit(solution)/shard_map/pallas_call | solution.py:48
  (24 shorter events, 2.1 us)
Async XLA Ops:
  0.8 1.1 %copy-start.3 = (bf16[768,512]{1,0:T(8,128)(2,1)S(1)}, bf16[768,512]{1,0:T(8,128)(2,1)}, u32[]{:S(2)}) copy-start(bf16[768,512]{1,0:T(8,128)(2,1)} %refs_1_.3) | copy-start | bytes 2359300
  1.9 5.6 %copy-start = (bf16[2048,512]{1,0:T(8,128)(2,1)S(1)}, bf16[2048,512]{1,0:T(8,128)(2,1)}, u32[]{:S(2)}) copy-start(bf16[2048,512]{1,0:T(8,128)(2,1)} %refs_3_.1) | copy-start | bytes 6291460
  1.9 5.6 %copy-start.2 = (bf16[2,1024,256]{2,1,0:T(8,128)(2,1)S(1)}, bf16[2,1024,256]{2,1,0:T(8,128)(2,1)}, u32[]{:S(2)}) copy-start(bf16[2,1024,256]{2,1,0:T(8,128)(2,1)} %refs_5_.3) | copy-start | bytes 3145732
  1.9 5.6 %copy-start.4 = (s32[1,2,384]{2,1,0:T(2,128)S(1)}, s32[1,2,384]{2,1,0:T(2,128)}, u32[]{:S(2)}) copy-start(s32[1,2,384]{2,1,0:T(2,128)} %param.7) | copy-start | bytes 9220
  1.9 5.7 %copy-start.5 = (f32[512]{0:T(512)S(1)}, f32[512]{0:T(512)}, u32[]{:S(2)}) copy-start(f32[512]{0:T(512)} %param.9) | copy-start | bytes 6148
  2.5 7.2 %collective-permute-start = (bf16[16,512]{1,0:T(8,128)(2,1)S(1)}, bf16[16,512]{1,0:T(8,128)(2,1)S(1)}, u32[]{:S(2)}, u32[]{:S(2)}) collective-permute-start(bf16[16,512]{1,0:T(8,128)(2,1)S(1)} %shard_map.109), channel_id=1, source_target_pairs={{0,1},{1,2},{2,3},{4,5},{5,6},{6,7},{8,9},{9,10},{10,11},{12,13},{... | collective-permute-start | bytes 49160 | tf_op jit(solution)/shard_map/ppermute | solution.py:422
  7.6 2.1 %copy-start.1 = (bf16[512,256]{1,0:T(8,128)(2,1)S(1)}, bf16[512,256]{1,0:T(8,128)(2,1)}, u32[]{:S(2)}) copy-start(bf16[512,256]{1,0:T(8,128)(2,1)} %refs_2_.3) | copy-start | bytes 786436
  11.4 2.5 %collective-permute-start.1 = (bf16[3360,128]{1,0:T(8,128)(2,1)S(1)}, bf16[3360,128]{1,0:T(8,128)(2,1)S(1)}, u32[]{:S(2)}, u32[]{:S(2)}) collective-permute-start(bf16[3360,128]{1,0:T(8,128)(2,1)S(1)} %get-tuple-element.58.refs_6_), channel_id=1, source_target_pairs={{0,4},{1,5},{2,6},{3,7},{4,0},{5,1},{6,2},{7,3},{8,12},{9,13},{10,... | collective-permute-start | bytes 2580488 | tf_op jit(solution)/shard_map/ppermute | solution.py:433
  14.6 7.2 %collective-permute-start.3 = (bf16[1312,128]{1,0:T(8,128)(2,1)S(1)}, bf16[1312,128]{1,0:T(8,128)(2,1)S(1)}, u32[]{:S(2)}, u32[]{:S(2)}) collective-permute-start(bf16[1312,128]{1,0:T(8,128)(2,1)S(1)} %get-tuple-element.65.refs_4_), channel_id=1, source_target_pairs={{0,8},{1,9},{2,10},{3,11},{4,20},{5,21},{6,22},{7,23},{8,0},{9,1},... | collective-permute-start | bytes 1007624 | tf_op jit(solution)/shard_map/ppermute | solution.py:433
  17.3 9.3 %collective-permute-start.2 = (bf16[544,256]{1,0:T(8,128)(2,1)S(1)}, bf16[544,256]{1,0:T(8,128)(2,1)S(1)}, u32[]{:S(2)}, u32[]{:S(2)}) collective-permute-start(bf16[544,256]{1,0:T(8,128)(2,1)S(1)} %shard_map.114.refs_4_), channel_id=1, source_target_pairs={{0,1},{1,0},{2,3},{3,2},{4,6},{5,7},{6,4},{7,5},{8,9},{9,8},{10,11... | collective-permute-start | bytes 835592 | tf_op jit(solution)/shard_map/ppermute | solution.py:433
  22.4 6.7 %collective-permute-start.5 = (bf16[800,128]{1,0:T(8,128)(2,1)S(1)}, bf16[800,128]{1,0:T(8,128)(2,1)S(1)}, u32[]{:S(2)}, u32[]{:S(2)}) collective-permute-start(bf16[800,128]{1,0:T(8,128)(2,1)S(1)} %get-tuple-element.68.refs_4_), channel_id=1, source_target_pairs={{0,16},{1,17},{2,18},{3,19},{4,12},{5,13},{6,14},{7,15},{8,24},{9,... | collective-permute-start | bytes 614408 | tf_op jit(solution)/shard_map/ppermute | solution.py:433
  27.2 6.3 %collective-permute-start.4 = (bf16[272,256]{1,0:T(8,128)(2,1)S(1)}, bf16[272,256]{1,0:T(8,128)(2,1)S(1)}, u32[]{:S(2)}, u32[]{:S(2)}) collective-permute-start(bf16[272,256]{1,0:T(8,128)(2,1)S(1)} %get-tuple-element.69.refs_4_), channel_id=1, source_target_pairs={{0,2},{1,3},{2,0},{3,1},{4,5},{5,4},{6,7},{7,6},{8,10},{9,11},{10,... | collective-permute-start | bytes 417800 | tf_op jit(solution)/shard_map/ppermute | solution.py:433
  29.8 9.0 %collective-permute-start.6 = (bf16[544,128]{1,0:T(8,128)(2,1)S(1)}, bf16[544,128]{1,0:T(8,128)(2,1)S(1)}, u32[]{:S(2)}, u32[]{:S(2)}) collective-permute-start(bf16[544,128]{1,0:T(8,128)(2,1)S(1)} %get-tuple-element.74.refs_4_), channel_id=1, source_target_pairs={{0,2},{1,3},{2,0},{3,1},{4,5},{5,4},{6,7},{7,6},{8,10},{9,11},{10,... | collective-permute-start | bytes 417800 | tf_op jit(solution)/shard_map/ppermute | solution.py:433
  34.1 5.7 %collective-permute-start.8 = (bf16[272,256]{1,0:T(8,128)(2,1)S(1)}, bf16[272,256]{1,0:T(8,128)(2,1)S(1)}, u32[]{:S(2)}, u32[]{:S(2)}) collective-permute-start(bf16[272,256]{1,0:T(8,128)(2,1)S(1)} %get-tuple-element.76.refs_4_), channel_id=1, source_target_pairs={{0,8},{1,9},{2,10},{3,11},{4,20},{5,21},{6,22},{7,23},{8,0},{9,1},... | collective-permute-start | bytes 417800 | tf_op jit(solution)/shard_map/ppermute | solution.py:433
  40.4 5.1 %collective-permute-start.9 = (bf16[272,256]{1,0:T(8,128)(2,1)S(1)}, bf16[272,256]{1,0:T(8,128)(2,1)S(1)}, u32[]{:S(2)}, u32[]{:S(2)}) collective-permute-start(bf16[272,256]{1,0:T(8,128)(2,1)S(1)} %get-tuple-element.85.refs_6_), channel_id=1, source_target_pairs={{0,16},{1,17},{2,18},{3,19},{4,12},{5,13},{6,14},{7,15},{8,24},{9,... | collective-permute-start | bytes 417800 | tf_op jit(solution)/shard_map/ppermute | solution.py:433
  40.5 7.6 %collective-permute-start.7 = (bf16[544,128]{1,0:T(8,128)(2,1)S(1)}, bf16[544,128]{1,0:T(8,128)(2,1)S(1)}, u32[]{:S(2)}, u32[]{:S(2)}) collective-permute-start(bf16[544,128]{1,0:T(8,128)(2,1)S(1)} %get-tuple-element.81.refs_3_), channel_id=1, source_target_pairs={{0,1},{1,0},{2,3},{3,2},{4,6},{5,7},{6,4},{7,5},{8,9},{9,8},{10,11... | collective-permute-start | bytes 417800 | tf_op jit(solution)/shard_map/ppermute | solution.py:433
  48.7 5.2 %collective-permute-start.10 = (bf16[832,128]{1,0:T(8,128)(2,1)S(1)}, bf16[832,128]{1,0:T(8,128)(2,1)S(1)}, u32[]{:S(2)}, u32[]{:S(2)}) collective-permute-start(bf16[832,128]{1,0:T(8,128)(2,1)S(1)} %get-tuple-element.90.refs_1_), channel_id=1, source_target_pairs={{0,4},{1,5},{2,6},{3,7},{4,0},{5,1},{6,2},{7,3},{8,12},{9,13},{10,... | collective-permute-start | bytes 638984 | tf_op jit(solution)/shard_map/ppermute | solution.py:433
  48.8 3.7 %collective-permute-start.12 = (bf16[256,128]{1,0:T(8,128)(2,1)S(1)}, bf16[256,128]{1,0:T(8,128)(2,1)S(1)}, u32[]{:S(2)}, u32[]{:S(2)}) collective-permute-start(bf16[256,128]{1,0:T(8,128)(2,1)S(1)} %get-tuple-element.88.refs_3_.refs_2_), channel_id=1, source_target_pairs={{0,12},{1,13},{2,14},{3,15},{4,16},{5,17},{6,18},{7,19},{8,4},{9,5... | collective-permute-start | bytes 196616 | tf_op jit(solution)/shard_map/ppermute | solution.py:444
  49.1 4.8 %collective-permute-start.11 = (bf16[256,128]{1,0:T(8,128)(2,1)S(1)}, bf16[256,128]{1,0:T(8,128)(2,1)S(1)}, u32[]{:S(2)}, u32[]{:S(2)}) collective-permute-start(bf16[256,128]{1,0:T(8,128)(2,1)S(1)} %get-tuple-element.88.refs_3_.refs_2_), channel_id=1, source_target_pairs={{0,8},{1,9},{2,10},{3,11},{4,20},{5,21},{6,22},{7,23},{8,0},{9,1},... | collective-permute-start | bytes 196616 | tf_op jit(solution)/shard_map/ppermute | solution.py:433

commit v9 on v8

--- a/solution.py
+++ b/solution.py
@@ -346,14 +346,18 @@
         to = split_sum(halved_a, info[place], got, 0, kept_a, rows_a, send, 0, keep_a)
     gone = split_sum(halved_c, info[place], got, rows_a, kept_c, rows_c, send, to, keep_c)
     block = digit_block(add_digits(kept_c[rows_c:, :], got[rows_a + rows_c:, :].astype(F32)))
-    send[to + gone:, :] = block.astype(BF16)
     keep_c[gone:, :] = block
+    to += gone
+    send[to:to + block.shape[0], :] = block.astype(BF16)
+    to += block.shape[0]
+    if to < send.shape[0]:
+        send[to:, :] = jnp.zeros((send.shape[0] - to, LANES), BF16)
 
 
 def last_kernel(rows_a, rows, info, got, kept_a, kept_c, sums_got, sums_kept, corr, pieces, mine):
     corr[...] = kept_a[...] + got[0:rows_a, :].astype(F32)
     pieces[...] = (kept_c[0:rows, :] + got[rows_a:rows_a + rows, :].astype(F32)).astype(BF16)
-    block = digit_block(add_digits(kept_c[rows:, :], got[rows_a + rows:, :].astype(F32)))
+    block = digit_block(add_digits(kept_c[rows:, :], got[rows_a + rows:rows_a + kept_c.shape[0], :].astype(F32)))
     mine[0:rows, :] = pieces[...]
     mine[rows:kept_c.shape[0], :] = block.astype(BF16)
     at = kept_c.shape[0]
@@ -592,9 +596,10 @@
     ordered = [sums_keep]
     for k in range(2, len(exchanges)):
         halves, rows_a, rows_c = halves_at(k)
+        spare = 16 * (k == len(exchanges) - 1)
         send, keep_a, keep_c = call(
             functools.partial(step_kernel, halves, k, mixed and k == dp_bits),
-            [shape((rows_a + rows_c, LANES), BF16), shape((rows_a, LANES), F32), shape((rows_c, LANES), F32)],
+            [shape((rows_a + rows_c + spare, LANES), BF16), shape((rows_a, LANES), F32), shape((rows_c, LANES), F32)],
             [info, got, keep_a, keep_c],
             after=ordered)
         got = swapped(send, exchanges[k])
@@ -611,23 +616,22 @@
         known = outs[2] if row_step is not None else known
         sums_got = swapped(sums_send, sums_exchanges[k - 1])
         ordered = [sums_send]
-        if k == tm_bits + 1:
-            feat_grad, *ordered = call(
-                feat_kernel,
-                shape((rows_in, channels), BF16),
-                [info, hidden_grad, known, weight],
-                after=[sums_send],
-                token=True,
-                scratch=[VMEM((frames + 8, channels), F32), VMEM((channels // LANES, rows_in, LANES), F32)],
-            )
     assert now_a == 1 and sums_rows == size
+    feat_grad, last = call(
+        feat_kernel,
+        shape((rows_in, channels), BF16),
+        [info, hidden_grad, known, weight],
+        after=[sums_send],
+        token=True,
+        scratch=[VMEM((frames + 8, channels), F32), VMEM((channels // LANES, rows_in, LANES), F32)],
+    )
 
     corr, piece, mine = call(
         functools.partial(last_kernel, rows_a, rows_c - extra),
         [shape((rows_a, LANES), F32), shape((rows_c - extra, LANES), BF16),
          shape((rows_c + size * (dz // LANES), LANES), BF16)],
         [info, got, keep_a, keep_c, sums_got, sums_keep],
-        after=ordered)
+        after=[last])
     parts = [piece, swapped(mine, exchanges[0]), swapped(piece, exchanges[1]), crossed(piece, exchanges[1])]
     conv_grad, last = call(
         functools.partial(conv_out_kernel, total_frames, at_start),

time: 56.2 us -> 54.5 us (0.970)
  waiting for transfers between devices: 12.3 us -> 11.2 us
  starting transfers between devices: 22.5 us -> 21.8 us
    ppermute x11, waiting for transfers between devices: 12.2 us -> 10.8 us  [swapped(): return lax.ppermute(block, ('dp', 'tm'), route)]
    ppermute x11, starting transfers between devices: 17.2 us -> 15.9 us  [swapped(): return lax.ppermute(block, ('dp', 'tm'), route)]
    ppermute x1, starting transfers between devices: 0.24 us -> 0.82 us  [crossed(): return lax.ppermute(block, ('dp', 'tm'), route)]
  transfers between devices with their start and end apart: 13 -> 13, of which waited for: 9 -> 9; matrix products, arithmetic and copies ran while one was open for 0% -> 0% of each run, Pallas kernels for 23% -> 25%
where the time goes in v9:
time: 54.5 us; the launch traced here: 53.6 us
  starting transfers between devices  21.8 us (40%)
  Pallas kernels  18.5 us (34%)
  waiting for transfers between devices  11.2 us (21%)
  local copies, waits for them, and re-layouts  1.25 us (2%)
  between operations  0.86 us (2%)
    pallas_call x17, Pallas kernels, call(): pl.pallas_call(kernel, out_shape=shown, in_specs=specs, out_specs=[pl.Blo...  18.5 us
    ppermute x11, starting transfers between devices, swapped(): return lax.ppermute(block, ('dp', 'tm'), route)  15.9 us
    ppermute x11, waiting for transfers between devices, swapped(): return lax.ppermute(block, ('dp', 'tm'), route)  10.8 us
    ppermute x1, starting transfers between devices, shifted(): return lax.ppermute(block, axis, route)  5.06 us
    unnamed x12, local copies, waits for them, and re-layouts  1.15 us
  transfers between devices with their start and end apart: 13, of which 9 were waited for; matrix products, arithmetic and copies ran while one was open for 0% of the time, Pallas kernels for 25%

profile of v9, /device:TPU:0, one launch (start us, length us, event | category | flops | bytes accessed | tf_op | source)
XLA Modules:
  0.0 53.6 jit_solution(6586386352446081918)
XLA Ops:
  0.8 1.1 %copy-done.3 = bf16[768,512]{1,0:T(8,128)(2,1)S(1)} copy-done((bf16[768,512]{1,0:T(8,128)(2,1)S(1)}, bf16[768,512]{1,0:T(8,128)(2,1)}, u32[]{:S(2)}) %copy-start.3) | copy-done | bytes 786456
  2.5 5.1 %collective-permute-start = (bf16[16,512]{1,0:T(8,128)(2,1)S(1)}, bf16[16,512]{1,0:T(8,128)(2,1)S(1)}, u32[]{:S(2)}, u32[]{:S(2)}) collective-permute-start(bf16[16,512]{1,0:T(8,128)(2,1)S(1)} %shard_map.109), channel_id=1, source_target_pairs={{0,1},{1,2},{2,3},{4,5},{5,6},{6,7},{8,9},{9,10},{10,11},{12,13},{... | collective-permute-start | bytes 49160 | tf_op jit(solution)/shard_map/ppermute | solution.py:426
  7.6 2.1 %shard_map.110 = (bf16[384,2048]{1,0:T(8,128)(2,1)S(1)}, f32[384,512]{1,0:T(8,128)S(1)}, bf16[2,384,256]{2,1,0:T(8,128)(2,1)S(1)}) custom-call(s32[19]{0:T(128)S(1)} %stack.67.refs_0_, bf16[768,512]{1,0:T(8,128)(2,1)S(1)} %copy-done.3, bf16[2048,512]{1,0:T(8,128)(2,1)S(1)} %copy-done, f32[1,512]{1,0:T(1,128)S(1)} %bitcast.20, s32[2,384]{1,0:T(2,128)S(1)} %bitcast.18, ...), custom_call_target="tpu_custom_call" | custom-call | tf_op jit(solution)/shard_map/pallas_call | solution.py:48
  9.7 1.7 %shard_map.111 = (bf16[384,2048]{1,0:T(8,128)(2,1)S(1)}, bf16[384,512]{1,0:T(8,128)(2,1)S(1)}, bf16[384,256]{1,0:T(8,128)(2,1)S(1)}, bf16[256,384]{1,0:T(8,128)(...) custom-call(s32[19]{0:T(128)S(1)} %stack.67.refs_0_, ...), custom_call_target="tpu_custom_call", output_to_operand_aliasing={{0}: (2, {})} | custom-call | tf_op jit(solution)/shard_map/pallas_call | solution.py:48
  11.5 1.2 %shard_map.112 = (f32[2048,128]{1,0:T(8,128)S(1)}, f32[512,128]{1,0:T(8,128)S(1)}, bf16[384,512]{1,0:T(8,128)(2,1)S(1)}, f32[32,128]{1,0:T(8,128)S(1)}, bf16[16,512]{1,0:T(8,128)(2,1)S(1)}) custom-call(s32[19]{0:T(128)S(1)} %stack.67.refs_0_, bf16[256,384]{1,0:T(8,128)(2,1)S(1)} %get-tuple-element.54.refs_1_, ...), custom_call_target="tpu_custom_call" | custom-call | tf_op jit(solution)/shard_map/pallas_call | solution.py:48
  12.7 1.2 %collective-permute-done.1.refs_1_ = bf16[3360,128]{1,0:T(8,128)(2,1)S(1)} collective-permute-done((bf16[3360,128]{1,0:T(8,128)(2,1)S(1)}, bf16[3360,128]{1,0:T(8,128)(2,1)S(1)}, u32[]{:S(2)}, u32[]{:S(2)}) %collective-permute-start.1) | collective-permute-done | bytes 860192 | tf_op jit(solution)/shard_map/ppermute | solution.py:437
  13.9 0.7 %shard_map.113 = (bf16[1312,128]{1,0:T(8,128)(2,1)S(1)}, f32[1024,128]{1,0:T(8,128)S(1)}, f32[288,128]{1,0:T(8,128)S(1)}) custom-call(s32[19]{0:T(128)S(1)} %stack.67.refs_0_, bf16[3360,128]{1,0:T(8,128)(2,1)S(1)} %collective-permute-done.1.refs_1_, f32[2048,128]{1,0:T(8,128)S(1)} %get-tuple-element.62.refs_2_, f32[512,128]{1,0:T(8,128)S(1)} %get-tuple-element.63.refs_3_, ...), custom_call_target="tpu_custom_call" | custom-call | tf_op jit(solution)/shard_map/pallas_call | solution.py:48
  14.6 1.6 %collective-permute-start.3 = (bf16[1312,128]{1,0:T(8,128)(2,1)S(1)}, bf16[1312,128]{1,0:T(8,128)(2,1)S(1)}, u32[]{:S(2)}, u32[]{:S(2)}) collective-permute-start(bf16[1312,128]{1,0:T(8,128)(2,1)S(1)} %get-tuple-element.65.refs_4_), channel_id=1, source_target_pairs={{0,8},{1,9},{2,10},{3,11},{4,20},{5,21},{6,22},{7,23},{8,0},{9,1},... | collective-permute-start | bytes 1007624 | tf_op jit(solution)/shard_map/ppermute | solution.py:437
  16.1 1.2 %shard_map.114.refs_4_ = bf16[544,256]{1,0:T(8,128)(2,1)S(1)} custom-call(s32[19]{0:T(128)S(1)} %stack.67.refs_0_, bf16[3360,128]{1,0:T(8,128)(2,1)S(1)} %collective-permute-done.1.refs_1_, bf16[400,256]{1,0:T(8,128)(2,1)S(1)} %get-tuple-element.60.refs_2_, bf16[16,512]{1,0:T(8,128)(2,1)S(1)} %get-tuple-element.61.refs_3_, ...), custom_call_target="tpu_custom_call" | custom-call | tf_op jit(solution)/shard_map/pallas_call | solution.py:48
  17.3 1.7 %collective-permute-start.2 = (bf16[544,256]{1,0:T(8,128)(2,1)S(1)}, bf16[544,256]{1,0:T(8,128)(2,1)S(1)}, u32[]{:S(2)}, u32[]{:S(2)}) collective-permute-start(bf16[544,256]{1,0:T(8,128)(2,1)S(1)} %shard_map.114.refs_4_), channel_id=1, source_target_pairs={{0,1},{1,0},{2,3},{3,2},{4,6},{5,7},{6,4},{7,5},{8,9},{9,8},{10,11... | collective-permute-start | bytes 835592 | tf_op jit(solution)/shard_map/ppermute | solution.py:437
  18.9 1.2 %shard_map.115.refs_4_.refs_2_ = f32[544,256]{1,0:T(8,128)S(1)} custom-call(s32[19]{0:T(128)S(1)} %stack.67.refs_0_, bf16[3360,128]{1,0:T(8,128)(2,1)S(1)} %collective-permute-done.1.refs_1_, bf16[400,256]{1,0:T(8,128)(2,1)S(1)} %get-tuple-element.60.refs_2_, bf16[16,512]{1,0:T(8,128)(2,1)S(1)} %get-tuple-element.61.refs_3_, ...), custom_call_target="tpu_custom_call" | custom-call | tf_op jit(solution)/shard_map/pallas_call | solution.py:48
  20.1 1.7 %collective-permute-done.3.refs_1_ = bf16[1312,128]{1,0:T(8,128)(2,1)S(1)} collective-permute-done((bf16[1312,128]{1,0:T(8,128)(2,1)S(1)}, bf16[1312,128]{1,0:T(8,128)(2,1)S(1)}, u32[]{:S(2)}, u32[]{:S(2)}) %collective-permute-start.3) | collective-permute-done | bytes 335904 | tf_op jit(solution)/shard_map/ppermute | solution.py:437
  21.8 0.6 %shard_map.116 = (bf16[800,128]{1,0:T(8,128)(2,1)S(1)}, f32[512,128]{1,0:T(8,128)S(1)}, f32[288,128]{1,0:T(8,128)S(1)}) custom-call(s32[19]{0:T(128)S(1)} %stack.67.refs_0_, bf16[1312,128]{1,0:T(8,128)(2,1)S(1)} %collective-permute-done.3.refs_1_, f32[1024,128]{1,0:T(8,128)S(1)} %get-tuple-element.66.refs_2_, f32[288,128]{1,0:T(8,128)S(1)} %get-tuple-element.67.refs_3_, ...), custom_call_target="tpu_custom_call" | custom-call | tf_op jit(solution)/shard_map/pallas_call | solution.py:48
  22.4 1.6 %collective-permute-start.5 = (bf16[800,128]{1,0:T(8,128)(2,1)S(1)}, bf16[800,128]{1,0:T(8,128)(2,1)S(1)}, u32[]{:S(2)}, u32[]{:S(2)}) collective-permute-start(bf16[800,128]{1,0:T(8,128)(2,1)S(1)} %get-tuple-element.68.refs_4_), channel_id=1, source_target_pairs={{0,16},{1,17},{2,18},{3,19},{4,12},{5,13},{6,14},{7,15},{8,24},{9,... | collective-permute-start | bytes 614408 | tf_op jit(solution)/shard_map/ppermute | solution.py:437
  24.0 2.6 %collective-permute-done.2.refs_1_ = bf16[544,256]{1,0:T(8,128)(2,1)S(1)} collective-permute-done((bf16[544,256]{1,0:T(8,128)(2,1)S(1)}, bf16[544,256]{1,0:T(8,128)(2,1)S(1)}, u32[]{:S(2)}, u32[]{:S(2)}) %collective-permute-start.2) | collective-permute-done | bytes 278560 | tf_op jit(solution)/shard_map/ppermute | solution.py:437
  26.6 0.6 %shard_map.117 = (bf16[272,256]{1,0:T(8,128)(2,1)S(1)}, f32[272,256]{1,0:T(8,128)S(1)}, bf16[16,512]{1,0:T(8,128)(2,1)S(1)}) custom-call(s32[19]{0:T(128)S(1)} %stack.67.refs_0_, bf16[544,256]{1,0:T(8,128)(2,1)S(1)} %collective-permute-done.2.refs_1_, f32[544,256]{1,0:T(8,128)S(1)} %shard_map.115.refs_4_.refs_2_, ...), custom_call_target="tpu_custom_call" | custom-call | tf_op jit(solution)/shard_map/pallas_call | solution.py:48
  27.2 1.9 %collective-permute-start.4 = (bf16[272,256]{1,0:T(8,128)(2,1)S(1)}, bf16[272,256]{1,0:T(8,128)(2,1)S(1)}, u32[]{:S(2)}, u32[]{:S(2)}) collective-permute-start(bf16[272,256]{1,0:T(8,128)(2,1)S(1)} %get-tuple-element.69.refs_4_), channel_id=1, source_target_pairs={{0,2},{1,3},{2,0},{3,1},{4,5},{5,4},{6,7},{7,6},{8,10},{9,11},{10,... | collective-permute-start | bytes 417800 | tf_op jit(solution)/shard_map/ppermute | solution.py:437
  29.1 0.7 %shard_map.118 = (bf16[544,128]{1,0:T(8,128)(2,1)S(1)}, f32[256,128]{1,0:T(8,128)S(1)}, f32[288,128]{1,0:T(8,128)S(1)}) custom-call(s32[19]{0:T(128)S(1)} %stack.67.refs_0_, bf16[800,128]{1,0:T(8,128)(2,1)S(1)} %collective-permute-done.5.refs_1_, f32[512,128]{1,0:T(8,128)S(1)} %get-tuple-element.72.refs_2_, f32[288,128]{1,0:T(8,128)S(1)} %get-tuple-element.73.refs_3_, ...), custom_call_target="tpu_custom_call" | custom-call | tf_op jit(solution)/shard_map/pallas_call | solution.py:48
  29.8 1.8 %collective-permute-start.7 = (bf16[544,128]{1,0:T(8,128)(2,1)S(1)}, bf16[544,128]{1,0:T(8,128)(2,1)S(1)}, u32[]{:S(2)}, u32[]{:S(2)}) collective-permute-start(bf16[544,128]{1,0:T(8,128)(2,1)S(1)} %get-tuple-element.74.refs_4_), channel_id=1, source_target_pairs={{0,2},{1,3},{2,0},{3,1},{4,5},{5,4},{6,7},{7,6},{8,10},{9,11},{10,... | collective-permute-start | bytes 417800 | tf_op jit(solution)/shard_map/ppermute | solution.py:437
  31.6 2.0 %collective-permute-done.4.refs_1_ = bf16[272,256]{1,0:T(8,128)(2,1)S(1)} collective-permute-done((bf16[272,256]{1,0:T(8,128)(2,1)S(1)}, bf16[272,256]{1,0:T(8,128)(2,1)S(1)}, u32[]{:S(2)}, u32[]{:S(2)}) %collective-permute-start.4) | collective-permute-done | bytes 139296 | tf_op jit(solution)/shard_map/ppermute | solution.py:437
  33.5 0.6 %shard_map.119 = (bf16[272,256]{1,0:T(8,128)(2,1)S(1)}, f32[272,256]{1,0:T(8,128)S(1)}, bf16[16,512]{1,0:T(8,128)(2,1)S(1)}) custom-call(s32[19]{0:T(128)S(1)} %stack.67.refs_0_, bf16[272,256]{1,0:T(8,128)(2,1)S(1)} %collective-permute-done.4.refs_1_, f32[272,256]{1,0:T(8,128)S(1)} %get-tuple-element.70.refs_2_, ...), custom_call_target="tpu_custom_call" | custom-call | tf_op jit(solution)/shard_map/pallas_call | solution.py:48
  34.1 2.1 %collective-permute-start.6 = (bf16[272,256]{1,0:T(8,128)(2,1)S(1)}, bf16[272,256]{1,0:T(8,128)(2,1)S(1)}, u32[]{:S(2)}, u32[]{:S(2)}) collective-permute-start(bf16[272,256]{1,0:T(8,128)(2,1)S(1)} %get-tuple-element.76.refs_4_), channel_id=1, source_target_pairs={{0,8},{1,9},{2,10},{3,11},{4,20},{5,21},{6,22},{7,23},{8,0},{9,1},... | collective-permute-start | bytes 417800 | tf_op jit(solution)/shard_map/ppermute | solution.py:437
  36.2 1.7 %collective-permute-done.7.refs_1_ = bf16[544,128]{1,0:T(8,128)(2,1)S(1)} collective-permute-done((bf16[544,128]{1,0:T(8,128)(2,1)S(1)}, bf16[544,128]{1,0:T(8,128)(2,1)S(1)}, u32[]{:S(2)}, u32[]{:S(2)}) %collective-permute-start.7) | collective-permute-done | bytes 139296 | tf_op jit(solution)/shard_map/ppermute | solution.py:437
  39.3 0.6 %shard_map.121 = (bf16[272,256]{1,0:T(8,128)(2,1)S(1)}, f32[272,256]{1,0:T(8,128)S(1)}) custom-call(s32[19]{0:T(128)S(1)} %stack.67.refs_0_, bf16[272,256]{1,0:T(8,128)(2,1)S(1)} %collective-permute-done.6.refs_1_, f32[272,256]{1,0:T(8,128)S(1)} %get-tuple-element.77.refs_2_, bf16[560,128]{1,0:T(8,128)(2,1)S(1)} %get-tuple-element.80.refs_3_), custom_call_target="tpu_custom_call" | custom-call | tf_op jit(solution)/shard_map/pallas_call | solution.py:48
  39.9 3.4 %collective-permute-start.9 = (bf16[272,256]{1,0:T(8,128)(2,1)S(1)}, bf16[272,256]{1,0:T(8,128)(2,1)S(1)}, u32[]{:S(2)}, u32[]{:S(2)}) collective-permute-start(bf16[272,256]{1,0:T(8,128)(2,1)S(1)} %get-tuple-element.81.refs_4_), channel_id=1, source_target_pairs={{0,16},{1,17},{2,18},{3,19},{4,12},{5,13},{6,14},{7,15},{8,24},{9,... | collective-permute-start | bytes 417800 | tf_op jit(solution)/shard_map/ppermute | solution.py:437
  43.2 2.6 %shard_map.122 = (bf16[768,512]{1,0:T(8,128)(2,1)}, f32[8,128]{1,0:T(8,128)S(1)}) custom-call(s32[19]{0:T(128)S(1)} %stack.67.refs_0_, bf16[384,512]{1,0:T(8,128)(2,1)S(1)} %get-tuple-element.59.refs_1_, bf16[16,512]{1,0:T(8,128)(2,1)S(1)} %get-tuple-element.75.refs_2_, bf16[2048,512]{1,0:T(8,128)(2,1)S(1)} %copy-done, ...), custom_call_target="tpu_custom_call" | custom-call | tf_op jit(solution)/shard_map/pallas_call | solution.py:48
  46.3 0.7 %shard_map.123 = (f32[256,128]{1,0:T(8,128)S(1)}, bf16[256,128]{1,0:T(8,128)(2,1)S(1)}, bf16[832,128]{1,0:T(8,128)(2,1)S(1)}) custom-call(s32[19]{0:T(128)S(1)} %stack.67.refs_0_, bf16[560,128]{1,0:T(8,128)(2,1)S(1)} %collective-permute-done.8.refs_1_, f32[256,128]{1,0:T(8,128)S(1)} %get-tuple-element.83.refs_2_, f32[288,128]{1,0:T(8,128)S(1)} %get-tuple-element.84.refs_3_, ...), custom_call_target="tpu_custom_call" | custom-call | tf_op jit(solution)/shard_map/pallas_call | solution.py:48
  47.0 0.8 %collective-permute-start.12 = (bf16[256,128]{1,0:T(8,128)(2,1)S(1)}, bf16[256,128]{1,0:T(8,128)(2,1)S(1)}, u32[]{:S(2)}, u32[]{:S(2)}) collective-permute-start(bf16[256,128]{1,0:T(8,128)(2,1)S(1)} %get-tuple-element.88.refs_3_.refs_2_), channel_id=1, source_target_pairs={{0,12},{1,13},{2,14},{3,15},{4,16},{5,17},{6,18},{7,19},{8,4},{9,5... | collective-permute-start | bytes 196616 | tf_op jit(solution)/shard_map/ppermute | solution.py:448
  47.9 1.3 %collective-permute-start.11 = (bf16[256,128]{1,0:T(8,128)(2,1)S(1)}, bf16[256,128]{1,0:T(8,128)(2,1)S(1)}, u32[]{:S(2)}, u32[]{:S(2)}) collective-permute-start(bf16[256,128]{1,0:T(8,128)(2,1)S(1)} %get-tuple-element.88.refs_3_.refs_2_), channel_id=1, source_target_pairs={{0,8},{1,9},{2,10},{3,11},{4,20},{5,21},{6,22},{7,23},{8,0},{9,1},... | collective-permute-start | bytes 196616 | tf_op jit(solution)/shard_map/ppermute | solution.py:437
  49.2 1.5 %shard_map.124 = (f32[64,512]{1,0:T(8,128)}, f32[8,128]{1,0:T(8,128)S(1)}) custom-call(s32[19]{0:T(128)S(1)} %stack.67.refs_0_, f32[256,128]{1,0:T(8,128)S(1)} %get-tuple-element.87.refs_1_, bf16[512,256]{1,0:T(8,128)(2,1)S(1)} %copy-done.1, bf16[256,128]{1,0:T(8,128)(2,1)S(1)} %get-tuple-element.88.refs_3_.refs_2_), custom_call_target="tpu_custom_call" | custom-call | tf_op jit(solution)/shard_map/pallas_call | solution.py:48
  51.1 1.0 %collective-permute-done.11.refs_4_ = bf16[256,128]{1,0:T(8,128)(2,1)S(1)} collective-permute-done((bf16[256,128]{1,0:T(8,128)(2,1)S(1)}, bf16[256,128]{1,0:T(8,128)(2,1)S(1)}, u32[]{:S(2)}, u32[]{:S(2)}) %collective-permute-start.11) | collective-permute-done | bytes 65568 | tf_op jit(solution)/shard_map/ppermute | solution.py:437
  52.1 1.5 %shard_map.125 = (f32[512,256]{1,0:T(8,128)}, f32[1,512]{1,0:T(1,128)}, bf16[2,256,256]{2,1,0:T(8,128)(2,1)}, f32[2,256]{1,0:T(2,128)}) custom-call(s32[19]{0:T(128)S(1)} %stack.67.refs_0_, bf16[832,128]{1,0:T(8,128)(2,1)S(1)} %get-tuple-element.90.refs_1_, bf16[256,128]{1,0:T(8,128)(2,1)S(1)} %get-tuple-element.88.refs_3_.refs_2_, ...), custom_call_target="tpu_custom_call" | custom-call | tf_op jit(solution)/shard_map/pallas_call | solution.py:48
  (24 shorter events, 3.0 us)
Async XLA Ops:
  0.8 1.1 %copy-start.3 = (bf16[768,512]{1,0:T(8,128)(2,1)S(1)}, bf16[768,512]{1,0:T(8,128)(2,1)}, u32[]{:S(2)}) copy-start(bf16[768,512]{1,0:T(8,128)(2,1)} %refs_1_.3) | copy-start | bytes 2359300
  1.9 5.6 %copy-start = (bf16[2048,512]{1,0:T(8,128)(2,1)S(1)}, bf16[2048,512]{1,0:T(8,128)(2,1)}, u32[]{:S(2)}) copy-start(bf16[2048,512]{1,0:T(8,128)(2,1)} %refs_3_.1) | copy-start | bytes 6291460
  1.9 5.6 %copy-start.2 = (bf16[2,1024,256]{2,1,0:T(8,128)(2,1)S(1)}, bf16[2,1024,256]{2,1,0:T(8,128)(2,1)}, u32[]{:S(2)}) copy-start(bf16[2,1024,256]{2,1,0:T(8,128)(2,1)} %refs_5_.3) | copy-start | bytes 3145732
  1.9 5.6 %copy-start.4 = (s32[1,2,384]{2,1,0:T(2,128)S(1)}, s32[1,2,384]{2,1,0:T(2,128)}, u32[]{:S(2)}) copy-start(s32[1,2,384]{2,1,0:T(2,128)} %param.7) | copy-start | bytes 9220
  1.9 5.7 %copy-start.5 = (f32[512]{0:T(512)S(1)}, f32[512]{0:T(512)}, u32[]{:S(2)}) copy-start(f32[512]{0:T(512)} %param.9) | copy-start | bytes 6148
  2.5 7.2 %collective-permute-start = (bf16[16,512]{1,0:T(8,128)(2,1)S(1)}, bf16[16,512]{1,0:T(8,128)(2,1)S(1)}, u32[]{:S(2)}, u32[]{:S(2)}) collective-permute-start(bf16[16,512]{1,0:T(8,128)(2,1)S(1)} %shard_map.109), channel_id=1, source_target_pairs={{0,1},{1,2},{2,3},{4,5},{5,6},{6,7},{8,9},{9,10},{10,11},{12,13},{... | collective-permute-start | bytes 49160 | tf_op jit(solution)/shard_map/ppermute | solution.py:426
  7.6 2.1 %copy-start.1 = (bf16[512,256]{1,0:T(8,128)(2,1)S(1)}, bf16[512,256]{1,0:T(8,128)(2,1)}, u32[]{:S(2)}) copy-start(bf16[512,256]{1,0:T(8,128)(2,1)} %refs_2_.3) | copy-start | bytes 786436
  11.4 2.5 %collective-permute-start.1 = (bf16[3360,128]{1,0:T(8,128)(2,1)S(1)}, bf16[3360,128]{1,0:T(8,128)(2,1)S(1)}, u32[]{:S(2)}, u32[]{:S(2)}) collective-permute-start(bf16[3360,128]{1,0:T(8,128)(2,1)S(1)} %get-tuple-element.58.refs_6_), channel_id=1, source_target_pairs={{0,4},{1,5},{2,6},{3,7},{4,0},{5,1},{6,2},{7,3},{8,12},{9,13},{10,... | collective-permute-start | bytes 2580488 | tf_op jit(solution)/shard_map/ppermute | solution.py:437
  14.6 7.2 %collective-permute-start.3 = (bf16[1312,128]{1,0:T(8,128)(2,1)S(1)}, bf16[1312,128]{1,0:T(8,128)(2,1)S(1)}, u32[]{:S(2)}, u32[]{:S(2)}) collective-permute-start(bf16[1312,128]{1,0:T(8,128)(2,1)S(1)} %get-tuple-element.65.refs_4_), channel_id=1, source_target_pairs={{0,8},{1,9},{2,10},{3,11},{4,20},{5,21},{6,22},{7,23},{8,0},{9,1},... | collective-permute-start | bytes 1007624 | tf_op jit(solution)/shard_map/ppermute | solution.py:437
  17.3 9.3 %collective-permute-start.2 = (bf16[544,256]{1,0:T(8,128)(2,1)S(1)}, bf16[544,256]{1,0:T(8,128)(2,1)S(1)}, u32[]{:S(2)}, u32[]{:S(2)}) collective-permute-start(bf16[544,256]{1,0:T(8,128)(2,1)S(1)} %shard_map.114.refs_4_), channel_id=1, source_target_pairs={{0,1},{1,0},{2,3},{3,2},{4,6},{5,7},{6,4},{7,5},{8,9},{9,8},{10,11... | collective-permute-start | bytes 835592 | tf_op jit(solution)/shard_map/ppermute | solution.py:437
  22.4 6.7 %collective-permute-start.5 = (bf16[800,128]{1,0:T(8,128)(2,1)S(1)}, bf16[800,128]{1,0:T(8,128)(2,1)S(1)}, u32[]{:S(2)}, u32[]{:S(2)}) collective-permute-start(bf16[800,128]{1,0:T(8,128)(2,1)S(1)} %get-tuple-element.68.refs_4_), channel_id=1, source_target_pairs={{0,16},{1,17},{2,18},{3,19},{4,12},{5,13},{6,14},{7,15},{8,24},{9,... | collective-permute-start | bytes 614408 | tf_op jit(solution)/shard_map/ppermute | solution.py:437
  27.2 6.3 %collective-permute-start.4 = (bf16[272,256]{1,0:T(8,128)(2,1)S(1)}, bf16[272,256]{1,0:T(8,128)(2,1)S(1)}, u32[]{:S(2)}, u32[]{:S(2)}) collective-permute-start(bf16[272,256]{1,0:T(8,128)(2,1)S(1)} %get-tuple-element.69.refs_4_), channel_id=1, source_target_pairs={{0,2},{1,3},{2,0},{3,1},{4,5},{5,4},{6,7},{7,6},{8,10},{9,11},{10,... | collective-permute-start | bytes 417800 | tf_op jit(solution)/shard_map/ppermute | solution.py:437
  29.8 8.2 %collective-permute-start.7 = (bf16[544,128]{1,0:T(8,128)(2,1)S(1)}, bf16[544,128]{1,0:T(8,128)(2,1)S(1)}, u32[]{:S(2)}, u32[]{:S(2)}) collective-permute-start(bf16[544,128]{1,0:T(8,128)(2,1)S(1)} %get-tuple-element.74.refs_4_), channel_id=1, source_target_pairs={{0,2},{1,3},{2,0},{3,1},{4,5},{5,4},{6,7},{7,6},{8,10},{9,11},{10,... | collective-permute-start | bytes 417800 | tf_op jit(solution)/shard_map/ppermute | solution.py:437
  34.1 5.1 %collective-permute-start.6 = (bf16[272,256]{1,0:T(8,128)(2,1)S(1)}, bf16[272,256]{1,0:T(8,128)(2,1)S(1)}, u32[]{:S(2)}, u32[]{:S(2)}) collective-permute-start(bf16[272,256]{1,0:T(8,128)(2,1)S(1)} %get-tuple-element.76.refs_4_), channel_id=1, source_target_pairs={{0,8},{1,9},{2,10},{3,11},{4,20},{5,21},{6,22},{7,23},{8,0},{9,1},... | collective-permute-start | bytes 417800 | tf_op jit(solution)/shard_map/ppermute | solution.py:437
  38.5 7.7 %collective-permute-start.8 = (bf16[560,128]{1,0:T(8,128)(2,1)S(1)}, bf16[560,128]{1,0:T(8,128)(2,1)S(1)}, u32[]{:S(2)}, u32[]{:S(2)}) collective-permute-start(bf16[560,128]{1,0:T(8,128)(2,1)S(1)} %get-tuple-element.80.refs_3_), channel_id=1, source_target_pairs={{0,1},{1,0},{2,3},{3,2},{4,6},{5,7},{6,4},{7,5},{8,9},{9,8},{10,11... | collective-permute-start | bytes 430088 | tf_op jit(solution)/shard_map/ppermute | solution.py:437
  39.9 6.4 %collective-permute-start.9 = (bf16[272,256]{1,0:T(8,128)(2,1)S(1)}, bf16[272,256]{1,0:T(8,128)(2,1)S(1)}, u32[]{:S(2)}, u32[]{:S(2)}) collective-permute-start(bf16[272,256]{1,0:T(8,128)(2,1)S(1)} %get-tuple-element.81.refs_4_), channel_id=1, source_target_pairs={{0,16},{1,17},{2,18},{3,19},{4,12},{5,13},{6,14},{7,15},{8,24},{9,... | collective-permute-start | bytes 417800 | tf_op jit(solution)/shard_map/ppermute | solution.py:437
  47.0 5.2 %collective-permute-start.10 = (bf16[832,128]{1,0:T(8,128)(2,1)S(1)}, bf16[832,128]{1,0:T(8,128)(2,1)S(1)}, u32[]{:S(2)}, u32[]{:S(2)}) collective-permute-start(bf16[832,128]{1,0:T(8,128)(2,1)S(1)} %get-tuple-element.90.refs_1_), channel_id=1, source_target_pairs={{0,4},{1,5},{2,6},{3,7},{4,0},{5,1},{6,2},{7,3},{8,12},{9,13},{10,... | collective-permute-start | bytes 638984 | tf_op jit(solution)/shard_map/ppermute | solution.py:437
  47.0 4.1 %collective-permute-start.12 = (bf16[256,128]{1,0:T(8,128)(2,1)S(1)}, bf16[256,128]{1,0:T(8,128)(2,1)S(1)}, u32[]{:S(2)}, u32[]{:S(2)}) collective-permute-start(bf16[256,128]{1,0:T(8,128)(2,1)S(1)} %get-tuple-element.88.refs_3_.refs_2_), channel_id=1, source_target_pairs={{0,12},{1,13},{2,14},{3,15},{4,16},{5,17},{6,18},{7,19},{8,4},{9,5... | collective-permute-start | bytes 196616 | tf_op jit(solution)/shard_map/ppermute | solution.py:448
  47.9 4.3 %collective-permute-start.11 = (bf16[256,128]{1,0:T(8,128)(2,1)S(1)}, bf16[256,128]{1,0:T(8,128)(2,1)S(1)}, u32[]{:S(2)}, u32[]{:S(2)}) collective-permute-start(bf16[256,128]{1,0:T(8,128)(2,1)S(1)} %get-tuple-element.88.refs_3_.refs_2_), channel_id=1, source_target_pairs={{0,8},{1,9},{2,10},{3,11},{4,20},{5,21},{6,22},{7,23},{8,0},{9,1},... | collective-permute-start | bytes 196616 | tf_op jit(solution)/shard_map/ppermute | solution.py:437

commit v10 on v9

--- a/solution.py
+++ b/solution.py
@@ -475,7 +475,7 @@
     paths[1] += up if turned else up[::-1]
     exchanges = list(zip([("dp", 0)] + paths[0], [("dp", 0)] + paths[1]))
     sums_up = [("dp", b) for b in range(1, dp_bits)]
-    sums_exchanges = list(zip(up + sums_up, up[::-1] + sums_up[::-1]))
+    sums_exchanges = list(zip(up[::-1] + sums_up, up + sums_up[::-1]))
 
     def piece_bit(step):
         axis, b = step
@@ -512,16 +512,16 @@
     places = [2 * core + mine_c, 2 * (1 - core) + other_c, 2 * core + 1 - mine_c, 2 * (1 - core) + 1 - other_c]
     places = [place << (log2(pieces_c) - c_bits) for place in places]
     lists = []
-    for way in ([b for _, b in up], [b for _, b in up[::-1]]):
+    for way in ([b for _, b in up[::-1]], [b for _, b in up]):
         lists.append([sum(((position >> (tm_bits - 1 - j)) & 1) << b for j, b in enumerate(way)) for position in range(tm)])
-    first_bit = on_core([0, tm_bits - 1])
+    first_bit = on_core([tm_bits - 1, 0])
     lead = (at_tm >> first_bit) & 1
     quarters = [on_core([lists[0][j], lists[1][j]]) for j in range(tm // 2)]
     send_codes = [(q + ((1 - lead) << first_bit)) * per_shard for q in quarters]
     keep_codes = [(q + (lead << first_bit)) * per_shard for q in quarters]
     differ = at_tm ^ (at_tm + 1)
     ways = [sum(((differ >> b) & 1) << j for j, b in enumerate(way)) for way in (
-        list(range(tm_bits)), list(reversed(range(tm_bits))))]
+        list(reversed(range(tm_bits))), list(range(tm_bits)))]
     row_code = jnp.where(at_tm + 1 < tm, on_core(ways), 0)
     if turned and not mixed:
         start = ((at_dp * tm + at_tm) * owner_rows) & (LANES - 1)

time: 54.5 us -> 56.2 us (1.031); the launches traced: 53.6 us -> 56 us
  starting transfers between devices: 21.8 us -> 23.2 us
  waiting for transfers between devices: 11.2 us -> 12.2 us
    ppermute x11, starting transfers between devices: 15.9 us -> 18.1 us  [swapped(): return lax.ppermute(block, ('dp', 'tm'), route)]
    ppermute x11, waiting for transfers between devices: 10.8 us -> 11.8 us  [swapped(): return lax.ppermute(block, ('dp', 'tm'), route)]
    ppermute x1, starting transfers between devices: 0.82 us -> 0.06 us  [crossed(): return lax.ppermute(block, ('dp', 'tm'), route)]
  transfers between devices with their start and end apart: 13 -> 13, of which waited for: 9 -> 9; matrix products, arithmetic and copies ran while one was open for 0% -> 0% of each run, Pallas kernels for 25% -> 24%
where the time goes in v10:
time: 56.2 us; the launch traced here: 56 us
  starting transfers between devices  23.2 us (41%)
  Pallas kernels  18.5 us (33%)
  waiting for transfers between devices  12.2 us (22%)
  local copies, waits for them, and re-layouts  1.25 us (2%)
  between operations  0.87 us (2%)
    pallas_call x17, Pallas kernels, call(): pl.pallas_call(kernel, out_shape=shown, in_specs=specs, out_specs=[pl.Blo...  18.5 us
    ppermute x11, starting transfers between devices, swapped(): return lax.ppermute(block, ('dp', 'tm'), route)  18.1 us
    ppermute x11, waiting for transfers between devices, swapped(): return lax.ppermute(block, ('dp', 'tm'), route)  11.8 us
    ppermute x1, starting transfers between devices, shifted(): return lax.ppermute(block, axis, route)  5.06 us
    unnamed x12, local copies, waits for them, and re-layouts  1.15 us
  transfers between devices with their start and end apart: 13, of which 9 were waited for; matrix products, arithmetic and copies ran while one was open for 0% of the time, Pallas kernels for 24%

profile of v10, /device:TPU:0, one launch (start us, length us, event | category | flops | bytes accessed | tf_op | source)
XLA Modules:
  0.0 56.0 jit_solution(10171435527319395326)
XLA Ops:
  0.8 1.1 %copy-done.3 = bf16[768,512]{1,0:T(8,128)(2,1)S(1)} copy-done((bf16[768,512]{1,0:T(8,128)(2,1)S(1)}, bf16[768,512]{1,0:T(8,128)(2,1)}, u32[]{:S(2)}) %copy-start.3) | copy-done | bytes 786456
  2.5 5.1 %collective-permute-start = (bf16[16,512]{1,0:T(8,128)(2,1)S(1)}, bf16[16,512]{1,0:T(8,128)(2,1)S(1)}, u32[]{:S(2)}, u32[]{:S(2)}) collective-permute-start(bf16[16,512]{1,0:T(8,128)(2,1)S(1)} %shard_map.109), channel_id=1, source_target_pairs={{0,1},{1,2},{2,3},{4,5},{5,6},{6,7},{8,9},{9,10},{10,11},{12,13},{... | collective-permute-start | bytes 49160 | tf_op jit(solution)/shard_map/ppermute | solution.py:426
  7.6 2.1 %shard_map.110 = (bf16[384,2048]{1,0:T(8,128)(2,1)S(1)}, f32[384,512]{1,0:T(8,128)S(1)}, bf16[2,384,256]{2,1,0:T(8,128)(2,1)S(1)}) custom-call(s32[19]{0:T(128)S(1)} %stack.67.refs_0_, bf16[768,512]{1,0:T(8,128)(2,1)S(1)} %copy-done.3, bf16[2048,512]{1,0:T(8,128)(2,1)S(1)} %copy-done, f32[1,512]{1,0:T(1,128)S(1)} %bitcast.20, s32[2,384]{1,0:T(2,128)S(1)} %bitcast.18, ...), custom_call_target="tpu_custom_call" | custom-call | tf_op jit(solution)/shard_map/pallas_call | solution.py:48
  9.7 1.7 %shard_map.111 = (bf16[384,2048]{1,0:T(8,128)(2,1)S(1)}, bf16[384,512]{1,0:T(8,128)(2,1)S(1)}, bf16[384,256]{1,0:T(8,128)(2,1)S(1)}, bf16[256,384]{1,0:T(8,128)(...) custom-call(s32[19]{0:T(128)S(1)} %stack.67.refs_0_, ...), custom_call_target="tpu_custom_call", output_to_operand_aliasing={{0}: (2, {})} | custom-call | tf_op jit(solution)/shard_map/pallas_call | solution.py:48
  11.5 1.2 %shard_map.112 = (f32[2048,128]{1,0:T(8,128)S(1)}, f32[512,128]{1,0:T(8,128)S(1)}, bf16[384,512]{1,0:T(8,128)(2,1)S(1)}, f32[32,128]{1,0:T(8,128)S(1)}, bf16[16,512]{1,0:T(8,128)(2,1)S(1)}) custom-call(s32[19]{0:T(128)S(1)} %stack.67.refs_0_, bf16[256,384]{1,0:T(8,128)(2,1)S(1)} %get-tuple-element.54.refs_1_, ...), custom_call_target="tpu_custom_call" | custom-call | tf_op jit(solution)/shard_map/pallas_call | solution.py:48
  12.7 1.2 %collective-permute-done.1.refs_1_ = bf16[3360,128]{1,0:T(8,128)(2,1)S(1)} collective-permute-done((bf16[3360,128]{1,0:T(8,128)(2,1)S(1)}, bf16[3360,128]{1,0:T(8,128)(2,1)S(1)}, u32[]{:S(2)}, u32[]{:S(2)}) %collective-permute-start.1) | collective-permute-done | bytes 860192 | tf_op jit(solution)/shard_map/ppermute | solution.py:437
  13.9 0.7 %shard_map.113 = (bf16[1312,128]{1,0:T(8,128)(2,1)S(1)}, f32[1024,128]{1,0:T(8,128)S(1)}, f32[288,128]{1,0:T(8,128)S(1)}) custom-call(s32[19]{0:T(128)S(1)} %stack.67.refs_0_, bf16[3360,128]{1,0:T(8,128)(2,1)S(1)} %collective-permute-done.1.refs_1_, f32[2048,128]{1,0:T(8,128)S(1)} %get-tuple-element.62.refs_2_, f32[512,128]{1,0:T(8,128)S(1)} %get-tuple-element.63.refs_3_, ...), custom_call_target="tpu_custom_call" | custom-call | tf_op jit(solution)/shard_map/pallas_call | solution.py:48
  14.6 1.6 %collective-permute-start.3 = (bf16[1312,128]{1,0:T(8,128)(2,1)S(1)}, bf16[1312,128]{1,0:T(8,128)(2,1)S(1)}, u32[]{:S(2)}, u32[]{:S(2)}) collective-permute-start(bf16[1312,128]{1,0:T(8,128)(2,1)S(1)} %get-tuple-element.65.refs_4_), channel_id=1, source_target_pairs={{0,8},{1,9},{2,10},{3,11},{4,20},{5,21},{6,22},{7,23},{8,0},{9,1},... | collective-permute-start | bytes 1007624 | tf_op jit(solution)/shard_map/ppermute | solution.py:437
  16.1 1.2 %shard_map.114.refs_4_ = bf16[544,256]{1,0:T(8,128)(2,1)S(1)} custom-call(s32[19]{0:T(128)S(1)} %stack.67.refs_0_, bf16[3360,128]{1,0:T(8,128)(2,1)S(1)} %collective-permute-done.1.refs_1_, bf16[400,256]{1,0:T(8,128)(2,1)S(1)} %get-tuple-element.60.refs_2_, bf16[16,512]{1,0:T(8,128)(2,1)S(1)} %get-tuple-element.61.refs_3_, ...), custom_call_target="tpu_custom_call" | custom-call | tf_op jit(solution)/shard_map/pallas_call | solution.py:48
  17.3 2.7 %collective-permute-start.2 = (bf16[544,256]{1,0:T(8,128)(2,1)S(1)}, bf16[544,256]{1,0:T(8,128)(2,1)S(1)}, u32[]{:S(2)}, u32[]{:S(2)}) collective-permute-start(bf16[544,256]{1,0:T(8,128)(2,1)S(1)} %shard_map.114.refs_4_), channel_id=1, source_target_pairs={{0,2},{1,3},{2,0},{3,1},{4,5},{5,4},{6,7},{7,6},{8,10},{9,11},{10,... | collective-permute-start | bytes 835592 | tf_op jit(solution)/shard_map/ppermute | solution.py:437
  20.0 1.2 %shard_map.115.refs_4_.refs_2_ = f32[544,256]{1,0:T(8,128)S(1)} custom-call(s32[19]{0:T(128)S(1)} %stack.67.refs_0_, bf16[3360,128]{1,0:T(8,128)(2,1)S(1)} %collective-permute-done.1.refs_1_, bf16[400,256]{1,0:T(8,128)(2,1)S(1)} %get-tuple-element.60.refs_2_, bf16[16,512]{1,0:T(8,128)(2,1)S(1)} %get-tuple-element.61.refs_3_, ...), custom_call_target="tpu_custom_call" | custom-call | tf_op jit(solution)/shard_map/pallas_call | solution.py:48
  21.1 0.7 %collective-permute-done.3.refs_1_ = bf16[1312,128]{1,0:T(8,128)(2,1)S(1)} collective-permute-done((bf16[1312,128]{1,0:T(8,128)(2,1)S(1)}, bf16[1312,128]{1,0:T(8,128)(2,1)S(1)}, u32[]{:S(2)}, u32[]{:S(2)}) %collective-permute-start.3) | collective-permute-done | bytes 335904 | tf_op jit(solution)/shard_map/ppermute | solution.py:437
  21.8 0.6 %shard_map.116 = (bf16[800,128]{1,0:T(8,128)(2,1)S(1)}, f32[512,128]{1,0:T(8,128)S(1)}, f32[288,128]{1,0:T(8,128)S(1)}) custom-call(s32[19]{0:T(128)S(1)} %stack.67.refs_0_, bf16[1312,128]{1,0:T(8,128)(2,1)S(1)} %collective-permute-done.3.refs_1_, f32[1024,128]{1,0:T(8,128)S(1)} %get-tuple-element.66.refs_2_, f32[288,128]{1,0:T(8,128)S(1)} %get-tuple-element.67.refs_3_, ...), custom_call_target="tpu_custom_call" | custom-call | tf_op jit(solution)/shard_map/pallas_call | solution.py:48
  22.4 1.6 %collective-permute-start.5 = (bf16[800,128]{1,0:T(8,128)(2,1)S(1)}, bf16[800,128]{1,0:T(8,128)(2,1)S(1)}, u32[]{:S(2)}, u32[]{:S(2)}) collective-permute-start(bf16[800,128]{1,0:T(8,128)(2,1)S(1)} %get-tuple-element.68.refs_4_), channel_id=1, source_target_pairs={{0,16},{1,17},{2,18},{3,19},{4,12},{5,13},{6,14},{7,15},{8,24},{9,... | collective-permute-start | bytes 614408 | tf_op jit(solution)/shard_map/ppermute | solution.py:437
  24.0 2.9 %collective-permute-done.2.refs_1_ = bf16[544,256]{1,0:T(8,128)(2,1)S(1)} collective-permute-done((bf16[544,256]{1,0:T(8,128)(2,1)S(1)}, bf16[544,256]{1,0:T(8,128)(2,1)S(1)}, u32[]{:S(2)}, u32[]{:S(2)}) %collective-permute-start.2) | collective-permute-done | bytes 278560 | tf_op jit(solution)/shard_map/ppermute | solution.py:437
  26.9 0.6 %shard_map.117 = (bf16[272,256]{1,0:T(8,128)(2,1)S(1)}, f32[272,256]{1,0:T(8,128)S(1)}, bf16[16,512]{1,0:T(8,128)(2,1)S(1)}) custom-call(s32[19]{0:T(128)S(1)} %stack.67.refs_0_, bf16[544,256]{1,0:T(8,128)(2,1)S(1)} %collective-permute-done.2.refs_1_, f32[544,256]{1,0:T(8,128)S(1)} %shard_map.115.refs_4_.refs_2_, ...), custom_call_target="tpu_custom_call" | custom-call | tf_op jit(solution)/shard_map/pallas_call | solution.py:48
  27.5 1.7 %collective-permute-start.4 = (bf16[272,256]{1,0:T(8,128)(2,1)S(1)}, bf16[272,256]{1,0:T(8,128)(2,1)S(1)}, u32[]{:S(2)}, u32[]{:S(2)}) collective-permute-start(bf16[272,256]{1,0:T(8,128)(2,1)S(1)} %get-tuple-element.69.refs_4_), channel_id=1, source_target_pairs={{0,1},{1,0},{2,3},{3,2},{4,6},{5,7},{6,4},{7,5},{8,9},{9,8},{10,11... | collective-permute-start | bytes 417800 | tf_op jit(solution)/shard_map/ppermute | solution.py:437
  29.2 0.7 %shard_map.118 = (bf16[544,128]{1,0:T(8,128)(2,1)S(1)}, f32[256,128]{1,0:T(8,128)S(1)}, f32[288,128]{1,0:T(8,128)S(1)}) custom-call(s32[19]{0:T(128)S(1)} %stack.67.refs_0_, bf16[800,128]{1,0:T(8,128)(2,1)S(1)} %collective-permute-done.5.refs_1_, f32[512,128]{1,0:T(8,128)S(1)} %get-tuple-element.72.refs_2_, f32[288,128]{1,0:T(8,128)S(1)} %get-tuple-element.73.refs_3_, ...), custom_call_target="tpu_custom_call" | custom-call | tf_op jit(solution)/shard_map/pallas_call | solution.py:48
  29.9 3.4 %collective-permute-start.7 = (bf16[544,128]{1,0:T(8,128)(2,1)S(1)}, bf16[544,128]{1,0:T(8,128)(2,1)S(1)}, u32[]{:S(2)}, u32[]{:S(2)}) collective-permute-start(bf16[544,128]{1,0:T(8,128)(2,1)S(1)} %get-tuple-element.74.refs_4_), channel_id=1, source_target_pairs={{0,2},{1,3},{2,0},{3,1},{4,5},{5,4},{6,7},{7,6},{8,10},{9,11},{10,... | collective-permute-start | bytes 417800 | tf_op jit(solution)/shard_map/ppermute | solution.py:437
  33.4 1.6 %collective-permute-done.4.refs_1_ = bf16[272,256]{1,0:T(8,128)(2,1)S(1)} collective-permute-done((bf16[272,256]{1,0:T(8,128)(2,1)S(1)}, bf16[272,256]{1,0:T(8,128)(2,1)S(1)}, u32[]{:S(2)}, u32[]{:S(2)}) %collective-permute-start.4) | collective-permute-done | bytes 139296 | tf_op jit(solution)/shard_map/ppermute | solution.py:437
  34.9 0.6 %shard_map.119 = (bf16[272,256]{1,0:T(8,128)(2,1)S(1)}, f32[272,256]{1,0:T(8,128)S(1)}, bf16[16,512]{1,0:T(8,128)(2,1)S(1)}) custom-call(s32[19]{0:T(128)S(1)} %stack.67.refs_0_, bf16[272,256]{1,0:T(8,128)(2,1)S(1)} %collective-permute-done.4.refs_1_, f32[272,256]{1,0:T(8,128)S(1)} %get-tuple-element.70.refs_2_, ...), custom_call_target="tpu_custom_call" | custom-call | tf_op jit(solution)/shard_map/pallas_call | solution.py:48
  35.5 0.6 %collective-permute-start.6 = (bf16[272,256]{1,0:T(8,128)(2,1)S(1)}, bf16[272,256]{1,0:T(8,128)(2,1)S(1)}, u32[]{:S(2)}, u32[]{:S(2)}) collective-permute-start(bf16[272,256]{1,0:T(8,128)(2,1)S(1)} %get-tuple-element.76.refs_4_), channel_id=1, source_target_pairs={{0,8},{1,9},{2,10},{3,11},{4,20},{5,21},{6,22},{7,23},{8,0},{9,1},... | collective-permute-start | bytes 417800 | tf_op jit(solution)/shard_map/ppermute | solution.py:437
  36.2 1.7 %collective-permute-done.7.refs_1_ = bf16[544,128]{1,0:T(8,128)(2,1)S(1)} collective-permute-done((bf16[544,128]{1,0:T(8,128)(2,1)S(1)}, bf16[544,128]{1,0:T(8,128)(2,1)S(1)}, u32[]{:S(2)}, u32[]{:S(2)}) %collective-permute-start.7) | collective-permute-done | bytes 139296 | tf_op jit(solution)/shard_map/ppermute | solution.py:437
  38.6 2.3 %collective-permute-done.6.refs_1_ = bf16[272,256]{1,0:T(8,128)(2,1)S(1)} collective-permute-done((bf16[272,256]{1,0:T(8,128)(2,1)S(1)}, bf16[272,256]{1,0:T(8,128)(2,1)S(1)}, u32[]{:S(2)}, u32[]{:S(2)}) %collective-permute-start.6) | collective-permute-done | bytes 139296 | tf_op jit(solution)/shard_map/ppermute | solution.py:437
  40.8 0.6 %shard_map.121 = (bf16[272,256]{1,0:T(8,128)(2,1)S(1)}, f32[272,256]{1,0:T(8,128)S(1)}) custom-call(s32[19]{0:T(128)S(1)} %stack.67.refs_0_, bf16[272,256]{1,0:T(8,128)(2,1)S(1)} %collective-permute-done.6.refs_1_, f32[272,256]{1,0:T(8,128)S(1)} %get-tuple-element.77.refs_2_, bf16[560,128]{1,0:T(8,128)(2,1)S(1)} %get-tuple-element.80.refs_3_), custom_call_target="tpu_custom_call" | custom-call | tf_op jit(solution)/shard_map/pallas_call | solution.py:48
  41.4 4.2 %collective-permute-start.9 = (bf16[272,256]{1,0:T(8,128)(2,1)S(1)}, bf16[272,256]{1,0:T(8,128)(2,1)S(1)}, u32[]{:S(2)}, u32[]{:S(2)}) collective-permute-start(bf16[272,256]{1,0:T(8,128)(2,1)S(1)} %get-tuple-element.81.refs_4_), channel_id=1, source_target_pairs={{0,16},{1,17},{2,18},{3,19},{4,12},{5,13},{6,14},{7,15},{8,24},{9,... | collective-permute-start | bytes 417800 | tf_op jit(solution)/shard_map/ppermute | solution.py:437
  45.6 2.6 %shard_map.122 = (bf16[768,512]{1,0:T(8,128)(2,1)}, f32[8,128]{1,0:T(8,128)S(1)}) custom-call(s32[19]{0:T(128)S(1)} %stack.67.refs_0_, bf16[384,512]{1,0:T(8,128)(2,1)S(1)} %get-tuple-element.59.refs_1_, bf16[16,512]{1,0:T(8,128)(2,1)S(1)} %get-tuple-element.75.refs_2_, bf16[2048,512]{1,0:T(8,128)(2,1)S(1)} %copy-done, ...), custom_call_target="tpu_custom_call" | custom-call | tf_op jit(solution)/shard_map/pallas_call | solution.py:48
  48.6 0.7 %shard_map.123 = (f32[256,128]{1,0:T(8,128)S(1)}, bf16[256,128]{1,0:T(8,128)(2,1)S(1)}, bf16[832,128]{1,0:T(8,128)(2,1)S(1)}) custom-call(s32[19]{0:T(128)S(1)} %stack.67.refs_0_, bf16[560,128]{1,0:T(8,128)(2,1)S(1)} %collective-permute-done.8.refs_1_, f32[256,128]{1,0:T(8,128)S(1)} %get-tuple-element.83.refs_2_, f32[288,128]{1,0:T(8,128)S(1)} %get-tuple-element.84.refs_3_, ...), custom_call_target="tpu_custom_call" | custom-call | tf_op jit(solution)/shard_map/pallas_call | solution.py:48
  49.5 2.1 %collective-permute-start.11 = (bf16[256,128]{1,0:T(8,128)(2,1)S(1)}, bf16[256,128]{1,0:T(8,128)(2,1)S(1)}, u32[]{:S(2)}, u32[]{:S(2)}) collective-permute-start(bf16[256,128]{1,0:T(8,128)(2,1)S(1)} %get-tuple-element.88.refs_3_.refs_2_), channel_id=1, source_target_pairs={{0,8},{1,9},{2,10},{3,11},{4,20},{5,21},{6,22},{7,23},{8,0},{9,1},... | collective-permute-start | bytes 196616 | tf_op jit(solution)/shard_map/ppermute | solution.py:437
  51.5 1.5 %shard_map.124 = (f32[64,512]{1,0:T(8,128)}, f32[8,128]{1,0:T(8,128)S(1)}) custom-call(s32[19]{0:T(128)S(1)} %stack.67.refs_0_, f32[256,128]{1,0:T(8,128)S(1)} %get-tuple-element.87.refs_1_, bf16[512,256]{1,0:T(8,128)(2,1)S(1)} %copy-done.1, bf16[256,128]{1,0:T(8,128)(2,1)S(1)} %get-tuple-element.88.refs_3_.refs_2_), custom_call_target="tpu_custom_call" | custom-call | tf_op jit(solution)/shard_map/pallas_call | solution.py:48
  53.5 1.0 %collective-permute-done.11.refs_4_ = bf16[256,128]{1,0:T(8,128)(2,1)S(1)} collective-permute-done((bf16[256,128]{1,0:T(8,128)(2,1)S(1)}, bf16[256,128]{1,0:T(8,128)(2,1)S(1)}, u32[]{:S(2)}, u32[]{:S(2)}) %collective-permute-start.11) | collective-permute-done | bytes 65568 | tf_op jit(solution)/shard_map/ppermute | solution.py:437
  54.5 1.5 %shard_map.125 = (f32[512,256]{1,0:T(8,128)}, f32[1,512]{1,0:T(1,128)}, bf16[2,256,256]{2,1,0:T(8,128)(2,1)}, f32[2,256]{1,0:T(2,128)}) custom-call(s32[19]{0:T(128)S(1)} %stack.67.refs_0_, bf16[832,128]{1,0:T(8,128)(2,1)S(1)} %get-tuple-element.90.refs_1_, bf16[256,128]{1,0:T(8,128)(2,1)S(1)} %get-tuple-element.88.refs_3_.refs_2_, ...), custom_call_target="tpu_custom_call" | custom-call | tf_op jit(solution)/shard_map/pallas_call | solution.py:48
  (24 shorter events, 2.4 us)
Async XLA Ops:
  0.8 1.1 %copy-start.3 = (bf16[768,512]{1,0:T(8,128)(2,1)S(1)}, bf16[768,512]{1,0:T(8,128)(2,1)}, u32[]{:S(2)}) copy-start(bf16[768,512]{1,0:T(8,128)(2,1)} %refs_1_.3) | copy-start | bytes 2359300
  1.9 5.6 %copy-start = (bf16[2048,512]{1,0:T(8,128)(2,1)S(1)}, bf16[2048,512]{1,0:T(8,128)(2,1)}, u32[]{:S(2)}) copy-start(bf16[2048,512]{1,0:T(8,128)(2,1)} %refs_3_.1) | copy-start | bytes 6291460
  1.9 5.6 %copy-start.2 = (bf16[2,1024,256]{2,1,0:T(8,128)(2,1)S(1)}, bf16[2,1024,256]{2,1,0:T(8,128)(2,1)}, u32[]{:S(2)}) copy-start(bf16[2,1024,256]{2,1,0:T(8,128)(2,1)} %refs_5_.3) | copy-start | bytes 3145732
  1.9 5.6 %copy-start.4 = (s32[1,2,384]{2,1,0:T(2,128)S(1)}, s32[1,2,384]{2,1,0:T(2,128)}, u32[]{:S(2)}) copy-start(s32[1,2,384]{2,1,0:T(2,128)} %param.7) | copy-start | bytes 9220
  1.9 5.7 %copy-start.5 = (f32[512]{0:T(512)S(1)}, f32[512]{0:T(512)}, u32[]{:S(2)}) copy-start(f32[512]{0:T(512)} %param.9) | copy-start | bytes 6148
  2.5 7.2 %collective-permute-start = (bf16[16,512]{1,0:T(8,128)(2,1)S(1)}, bf16[16,512]{1,0:T(8,128)(2,1)S(1)}, u32[]{:S(2)}, u32[]{:S(2)}) collective-permute-start(bf16[16,512]{1,0:T(8,128)(2,1)S(1)} %shard_map.109), channel_id=1, source_target_pairs={{0,1},{1,2},{2,3},{4,5},{5,6},{6,7},{8,9},{9,10},{10,11},{12,13},{... | collective-permute-start | bytes 49160 | tf_op jit(solution)/shard_map/ppermute | solution.py:426
  7.6 2.1 %copy-start.1 = (bf16[512,256]{1,0:T(8,128)(2,1)S(1)}, bf16[512,256]{1,0:T(8,128)(2,1)}, u32[]{:S(2)}) copy-start(bf16[512,256]{1,0:T(8,128)(2,1)} %refs_2_.3) | copy-start | bytes 786436
  11.4 2.5 %collective-permute-start.1 = (bf16[3360,128]{1,0:T(8,128)(2,1)S(1)}, bf16[3360,128]{1,0:T(8,128)(2,1)S(1)}, u32[]{:S(2)}, u32[]{:S(2)}) collective-permute-start(bf16[3360,128]{1,0:T(8,128)(2,1)S(1)} %get-tuple-element.58.refs_6_), channel_id=1, source_target_pairs={{0,4},{1,5},{2,6},{3,7},{4,0},{5,1},{6,2},{7,3},{8,12},{9,13},{10,... | collective-permute-start | bytes 2580488 | tf_op jit(solution)/shard_map/ppermute | solution.py:437
  14.6 7.2 %collective-permute-start.3 = (bf16[1312,128]{1,0:T(8,128)(2,1)S(1)}, bf16[1312,128]{1,0:T(8,128)(2,1)S(1)}, u32[]{:S(2)}, u32[]{:S(2)}) collective-permute-start(bf16[1312,128]{1,0:T(8,128)(2,1)S(1)} %get-tuple-element.65.refs_4_), channel_id=1, source_target_pairs={{0,8},{1,9},{2,10},{3,11},{4,20},{5,21},{6,22},{7,23},{8,0},{9,1},... | collective-permute-start | bytes 1007624 | tf_op jit(solution)/shard_map/ppermute | solution.py:437
  17.3 9.6 %collective-permute-start.2 = (bf16[544,256]{1,0:T(8,128)(2,1)S(1)}, bf16[544,256]{1,0:T(8,128)(2,1)S(1)}, u32[]{:S(2)}, u32[]{:S(2)}) collective-permute-start(bf16[544,256]{1,0:T(8,128)(2,1)S(1)} %shard_map.114.refs_4_), channel_id=1, source_target_pairs={{0,2},{1,3},{2,0},{3,1},{4,5},{5,4},{6,7},{7,6},{8,10},{9,11},{10,... | collective-permute-start | bytes 835592 | tf_op jit(solution)/shard_map/ppermute | solution.py:437
  22.4 6.8 %collective-permute-start.5 = (bf16[800,128]{1,0:T(8,128)(2,1)S(1)}, bf16[800,128]{1,0:T(8,128)(2,1)S(1)}, u32[]{:S(2)}, u32[]{:S(2)}) collective-permute-start(bf16[800,128]{1,0:T(8,128)(2,1)S(1)} %get-tuple-element.68.refs_4_), channel_id=1, source_target_pairs={{0,16},{1,17},{2,18},{3,19},{4,12},{5,13},{6,14},{7,15},{8,24},{9,... | collective-permute-start | bytes 614408 | tf_op jit(solution)/shard_map/ppermute | solution.py:437
  27.5 7.4 %collective-permute-start.4 = (bf16[272,256]{1,0:T(8,128)(2,1)S(1)}, bf16[272,256]{1,0:T(8,128)(2,1)S(1)}, u32[]{:S(2)}, u32[]{:S(2)}) collective-permute-start(bf16[272,256]{1,0:T(8,128)(2,1)S(1)} %get-tuple-element.69.refs_4_), channel_id=1, source_target_pairs={{0,1},{1,0},{2,3},{3,2},{4,6},{5,7},{6,4},{7,5},{8,9},{9,8},{10,11... | collective-permute-start | bytes 417800 | tf_op jit(solution)/shard_map/ppermute | solution.py:437
  29.9 8.0 %collective-permute-start.7 = (bf16[544,128]{1,0:T(8,128)(2,1)S(1)}, bf16[544,128]{1,0:T(8,128)(2,1)S(1)}, u32[]{:S(2)}, u32[]{:S(2)}) collective-permute-start(bf16[544,128]{1,0:T(8,128)(2,1)S(1)} %get-tuple-element.74.refs_4_), channel_id=1, source_target_pairs={{0,2},{1,3},{2,0},{3,1},{4,5},{5,4},{6,7},{7,6},{8,10},{9,11},{10,... | collective-permute-start | bytes 417800 | tf_op jit(solution)/shard_map/ppermute | solution.py:437
  35.5 5.3 %collective-permute-start.6 = (bf16[272,256]{1,0:T(8,128)(2,1)S(1)}, bf16[272,256]{1,0:T(8,128)(2,1)S(1)}, u32[]{:S(2)}, u32[]{:S(2)}) collective-permute-start(bf16[272,256]{1,0:T(8,128)(2,1)S(1)} %get-tuple-element.76.refs_4_), channel_id=1, source_target_pairs={{0,8},{1,9},{2,10},{3,11},{4,20},{5,21},{6,22},{7,23},{8,0},{9,1},... | collective-permute-start | bytes 417800 | tf_op jit(solution)/shard_map/ppermute | solution.py:437
  38.5 10.1 %collective-permute-start.8 = (bf16[560,128]{1,0:T(8,128)(2,1)S(1)}, bf16[560,128]{1,0:T(8,128)(2,1)S(1)}, u32[]{:S(2)}, u32[]{:S(2)}) collective-permute-start(bf16[560,128]{1,0:T(8,128)(2,1)S(1)} %get-tuple-element.80.refs_3_), channel_id=1, source_target_pairs={{0,1},{1,0},{2,3},{3,2},{4,6},{5,7},{6,4},{7,5},{8,9},{9,8},{10,11... | collective-permute-start | bytes 430088 | tf_op jit(solution)/shard_map/ppermute | solution.py:437
  41.4 7.2 %collective-permute-start.9 = (bf16[272,256]{1,0:T(8,128)(2,1)S(1)}, bf16[272,256]{1,0:T(8,128)(2,1)S(1)}, u32[]{:S(2)}, u32[]{:S(2)}) collective-permute-start(bf16[272,256]{1,0:T(8,128)(2,1)S(1)} %get-tuple-element.81.refs_4_), channel_id=1, source_target_pairs={{0,16},{1,17},{2,18},{3,19},{4,12},{5,13},{6,14},{7,15},{8,24},{9,... | collective-permute-start | bytes 417800 | tf_op jit(solution)/shard_map/ppermute | solution.py:437
  49.3 5.2 %collective-permute-start.10 = (bf16[832,128]{1,0:T(8,128)(2,1)S(1)}, bf16[832,128]{1,0:T(8,128)(2,1)S(1)}, u32[]{:S(2)}, u32[]{:S(2)}) collective-permute-start(bf16[832,128]{1,0:T(8,128)(2,1)S(1)} %get-tuple-element.90.refs_1_), channel_id=1, source_target_pairs={{0,4},{1,5},{2,6},{3,7},{4,0},{5,1},{6,2},{7,3},{8,12},{9,13},{10,... | collective-permute-start | bytes 638984 | tf_op jit(solution)/shard_map/ppermute | solution.py:437
  49.4 4.1 %collective-permute-start.12 = (bf16[256,128]{1,0:T(8,128)(2,1)S(1)}, bf16[256,128]{1,0:T(8,128)(2,1)S(1)}, u32[]{:S(2)}, u32[]{:S(2)}) collective-permute-start(bf16[256,128]{1,0:T(8,128)(2,1)S(1)} %get-tuple-element.88.refs_3_.refs_2_), channel_id=1, source_target_pairs={{0,12},{1,13},{2,14},{3,15},{4,16},{5,17},{6,18},{7,19},{8,4},{9,5... | collective-permute-start | bytes 196616 | tf_op jit(solution)/shard_map/ppermute | solution.py:448
  49.5 5.0 %collective-permute-start.11 = (bf16[256,128]{1,0:T(8,128)(2,1)S(1)}, bf16[256,128]{1,0:T(8,128)(2,1)S(1)}, u32[]{:S(2)}, u32[]{:S(2)}) collective-permute-start(bf16[256,128]{1,0:T(8,128)(2,1)S(1)} %get-tuple-element.88.refs_3_.refs_2_), channel_id=1, source_target_pairs={{0,8},{1,9},{2,10},{3,11},{4,20},{5,21},{6,22},{7,23},{8,0},{9,1},... | collective-permute-start | bytes 196616 | tf_op jit(solution)/shard_map/ppermute | solution.py:437

commit v11 on v9

--- a/solution.py
+++ b/solution.py
@@ -77,8 +77,8 @@
     return jnp.where(codes == places, 1.0, 0.0).astype(BF16)
 
 
-def halo_kernel(info, feats, out):
-    out[...] = feats[feats.shape[0] - out.shape[0]:, :]
+def idle_kernel(info, out):
+    out[...] = jnp.zeros(out.shape, F32)
 
 
 def local_kernel(info, feats, weight, bias, codes, books, unfold, conv, chosen, wide):
@@ -154,8 +154,7 @@
     half = width // 2
     dz = proj.shape[1]
     row = lax.broadcasted_iota(jnp.int32, (16, half), 0)
-    last = halo[...].astype(F32)
-    left = jnp.concatenate([last[14:15, :], last[15:16, :]], 1)
+    left = jnp.concatenate([halo[0:1, :], halo[1:2, :]], 1).astype(F32)
     head = jnp.where(row == 0, jnp.broadcast_to(left, (16, half)), 0.0)
     unfold[0:16, 0:half] = (unfold_in[0:16, 0:half].astype(F32) + head).astype(BF16)
     fix = nn(head.astype(BF16), weight[0:half, :])
@@ -535,13 +534,14 @@
     at_row = at_sums + len(sums_bits)
     info = jnp.stack(bits + [start] + send_codes + keep_codes + places + sums_bits + [row_code]).astype(jnp.int32)
 
-    halo = shifted(
-        call(halo_kernel, shape((16, channels), BF16), [info, feats], flops=10 ** 11), "tm", 1)
+    halo = shifted(feats[-2:], "tm", 1)
+    idle = call(idle_kernel, shape((8, LANES), F32), [info], flops=10 ** 11)
     weight, proj, codes = conv_weight, proj_weight, codes[0]
     unfold, conv, chosen = call(
         local_kernel,
         [shape((frames, width), BF16), shape((frames, channels), F32), shape((levels, frames, dz), BF16)],
         [info, feats, weight, conv_bias[None, :], codes, codebooks],
+        after=[idle],
         scratch=[VMEM((channels // LANES, rows_in + 8, LANES), F32)],
     )
 

time: 54.5 us -> 54.6 us (level)
  starting transfers between devices: 21.8 us -> 18.5 us
  waiting for transfers between devices: 11.2 us -> 14.1 us
  local copies, waits for them, and re-layouts: 1.25 us -> 2.3 us
    ppermute x11, starting transfers between devices: 15.9 us -> 11.7 us  [swapped(): return lax.ppermute(block, ('dp', 'tm'), route)]
    ppermute x11, waiting for transfers between devices: 10.8 us -> 14 us  [swapped(): return lax.ppermute(block, ('dp', 'tm'), route)]
    ppermute x1, starting transfers between devices: 0.82 us -> 1.79 us  [crossed(): return lax.ppermute(block, ('dp', 'tm'), route)]
    slice x0 -> x1, local copies, waits for them, and re-layouts: none -> 0.71 us  [shards(): halo = shifted(feats[-2:], 'tm', 1)]
  transfers between devices with their start and end apart: 13 -> 13, of which waited for: 9 -> 9; matrix products, arithmetic and copies ran while one was open for 0% -> 0% of each run, Pallas kernels for 25% -> 26%
where the time goes in v11:
time: 54.6 us; the launch traced here: 54.2 us
  starting transfers between devices  18.5 us (34%)
  Pallas kernels  18.5 us (34%)
  waiting for transfers between devices  14.1 us (26%)
  local copies, waits for them, and re-layouts  2.3 us (4%)
  between operations  0.85 us (2%)
    pallas_call x17, Pallas kernels, call(): pl.pallas_call(kernel, out_shape=shown, in_specs=specs, out_specs=[pl.Blo...  18.5 us
    ppermute x11, waiting for transfers between devices, swapped(): return lax.ppermute(block, ('dp', 'tm'), route)  14 us
    ppermute x11, starting transfers between devices, swapped(): return lax.ppermute(block, ('dp', 'tm'), route)  11.7 us
    ppermute x1, starting transfers between devices, shifted(): return lax.ppermute(block, axis, route)  4.92 us
    ppermute x1, starting transfers between devices, crossed(): return lax.ppermute(block, ('dp', 'tm'), route)  1.79 us
    unnamed x12, local copies, waits for them, and re-layouts  1.5 us
  transfers between devices with their start and end apart: 13, of which 9 were waited for; matrix products, arithmetic and copies ran while one was open for 0% of the time, Pallas kernels for 26%

profile of v11, /device:TPU:0, one launch (start us, length us, event | category | flops | bytes accessed | tf_op | source)
XLA Modules:
  0.0 54.2 jit_solution(3003125015484611725)
XLA Ops:
  0.6 0.7 %slice.3 = bf16[2,512]{1,0:T(2,128)(2,1)S(1)} slice(bf16[768,512]{1,0:T(8,128)(2,1)} %refs_1_.1), slice={[766:768], [0:512]} | slice | bytes 4096 | tf_op jit(solution)/shard_map/slice | solution.py:537
  1.3 4.9 %collective-permute-start = (bf16[2,512]{1,0:T(2,128)(2,1)S(1)}, bf16[2,512]{1,0:T(2,128)(2,1)S(1)}, u32[]{:S(2)}, u32[]{:S(2)}) collective-permute-start(bf16[2,512]{1,0:T(2,128)(2,1)S(1)} %slice.3), channel_id=1, source_target_pairs={{0,1},{1,2},{2,3},{4,5},{5,6},{6,7},{8,9},{9,10},{10,11},{12,13},{... | collective-permute-start | bytes 6152 | tf_op jit(solution)/shard_map/ppermute | solution.py:425
  7.0 1.0 %copy-done = bf16[2048,512]{1,0:T(8,128)(2,1)S(1)} copy-done((bf16[2048,512]{1,0:T(8,128)(2,1)S(1)}, bf16[2048,512]{1,0:T(8,128)(2,1)}, u32[]{:S(2)}) %copy-start) | copy-done | bytes 2097176
  8.5 2.1 %shard_map.110 = (bf16[384,2048]{1,0:T(8,128)(2,1)S(1)}, f32[384,512]{1,0:T(8,128)S(1)}, bf16[2,384,256]{2,1,0:T(8,128)(2,1)S(1)}) custom-call(s32[19]{0:T(128)S(1)} %stack.67.refs_0_, bf16[768,512]{1,0:T(8,128)(2,1)S(1)} %copy-done.3, bf16[2048,512]{1,0:T(8,128)(2,1)S(1)} %copy-done, f32[1,512]{1,0:T(1,128)S(1)} %bitcast.20, s32[2,384]{1,0:T(2,128)S(1)} %bitcast.18, ...), custom_call_target="tpu_custom_call" | custom-call | tf_op jit(solution)/shard_map/pallas_call | solution.py:48
  10.6 1.7 %shard_map.111 = (bf16[384,2048]{1,0:T(8,128)(2,1)S(1)}, bf16[384,512]{1,0:T(8,128)(2,1)S(1)}, bf16[384,256]{1,0:T(8,128)(2,1)S(1)}, bf16[256,384]{1,0:T(8,128)(...) custom-call(s32[19]{0:T(128)S(1)} %stack.67.refs_0_, ...), custom_call_target="tpu_custom_call", output_to_operand_aliasing={{0}: (2, {})} | custom-call | tf_op jit(solution)/shard_map/pallas_call | solution.py:48
  12.4 1.2 %shard_map.112 = (f32[2048,128]{1,0:T(8,128)S(1)}, f32[512,128]{1,0:T(8,128)S(1)}, bf16[384,512]{1,0:T(8,128)(2,1)S(1)}, f32[32,128]{1,0:T(8,128)S(1)}, bf16[16,512]{1,0:T(8,128)(2,1)S(1)}) custom-call(s32[19]{0:T(128)S(1)} %stack.67.refs_0_, bf16[256,384]{1,0:T(8,128)(2,1)S(1)} %get-tuple-element.54.refs_1_, ...), custom_call_target="tpu_custom_call" | custom-call | tf_op jit(solution)/shard_map/pallas_call | solution.py:48
  13.6 1.2 %collective-permute-done.1.refs_1_ = bf16[3360,128]{1,0:T(8,128)(2,1)S(1)} collective-permute-done((bf16[3360,128]{1,0:T(8,128)(2,1)S(1)}, bf16[3360,128]{1,0:T(8,128)(2,1)S(1)}, u32[]{:S(2)}, u32[]{:S(2)}) %collective-permute-start.1) | collective-permute-done | bytes 860192 | tf_op jit(solution)/shard_map/ppermute | solution.py:436
  14.7 0.7 %shard_map.113 = (bf16[1312,128]{1,0:T(8,128)(2,1)S(1)}, f32[1024,128]{1,0:T(8,128)S(1)}, f32[288,128]{1,0:T(8,128)S(1)}) custom-call(s32[19]{0:T(128)S(1)} %stack.67.refs_0_, bf16[3360,128]{1,0:T(8,128)(2,1)S(1)} %collective-permute-done.1.refs_1_, f32[2048,128]{1,0:T(8,128)S(1)} %get-tuple-element.62.refs_2_, f32[512,128]{1,0:T(8,128)S(1)} %get-tuple-element.63.refs_3_, ...), custom_call_target="tpu_custom_call" | custom-call | tf_op jit(solution)/shard_map/pallas_call | solution.py:48
  15.4 1.6 %collective-permute-start.3 = (bf16[1312,128]{1,0:T(8,128)(2,1)S(1)}, bf16[1312,128]{1,0:T(8,128)(2,1)S(1)}, u32[]{:S(2)}, u32[]{:S(2)}) collective-permute-start(bf16[1312,128]{1,0:T(8,128)(2,1)S(1)} %get-tuple-element.65.refs_4_), channel_id=1, source_target_pairs={{0,8},{1,9},{2,10},{3,11},{4,20},{5,21},{6,22},{7,23},{8,0},{9,1},... | collective-permute-start | bytes 1007624 | tf_op jit(solution)/shard_map/ppermute | solution.py:436
  17.0 1.2 %shard_map.114.refs_4_ = bf16[544,256]{1,0:T(8,128)(2,1)S(1)} custom-call(s32[19]{0:T(128)S(1)} %stack.67.refs_0_, bf16[3360,128]{1,0:T(8,128)(2,1)S(1)} %collective-permute-done.1.refs_1_, bf16[400,256]{1,0:T(8,128)(2,1)S(1)} %get-tuple-element.60.refs_2_, bf16[16,512]{1,0:T(8,128)(2,1)S(1)} %get-tuple-element.61.refs_3_, ...), custom_call_target="tpu_custom_call" | custom-call | tf_op jit(solution)/shard_map/pallas_call | solution.py:48
  18.2 1.6 %collective-permute-start.2 = (bf16[544,256]{1,0:T(8,128)(2,1)S(1)}, bf16[544,256]{1,0:T(8,128)(2,1)S(1)}, u32[]{:S(2)}, u32[]{:S(2)}) collective-permute-start(bf16[544,256]{1,0:T(8,128)(2,1)S(1)} %shard_map.114.refs_4_), channel_id=1, source_target_pairs={{0,1},{1,0},{2,3},{3,2},{4,6},{5,7},{6,4},{7,5},{8,9},{9,8},{10,11... | collective-permute-start | bytes 835592 | tf_op jit(solution)/shard_map/ppermute | solution.py:436
  19.8 1.2 %shard_map.115.refs_4_.refs_2_ = f32[544,256]{1,0:T(8,128)S(1)} custom-call(s32[19]{0:T(128)S(1)} %stack.67.refs_0_, bf16[3360,128]{1,0:T(8,128)(2,1)S(1)} %collective-permute-done.1.refs_1_, bf16[400,256]{1,0:T(8,128)(2,1)S(1)} %get-tuple-element.60.refs_2_, bf16[16,512]{1,0:T(8,128)(2,1)S(1)} %get-tuple-element.61.refs_3_, ...), custom_call_target="tpu_custom_call" | custom-call | tf_op jit(solution)/shard_map/pallas_call | solution.py:48
  21.0 1.7 %collective-permute-done.3.refs_1_ = bf16[1312,128]{1,0:T(8,128)(2,1)S(1)} collective-permute-done((bf16[1312,128]{1,0:T(8,128)(2,1)S(1)}, bf16[1312,128]{1,0:T(8,128)(2,1)S(1)}, u32[]{:S(2)}, u32[]{:S(2)}) %collective-permute-start.3) | collective-permute-done | bytes 335904 | tf_op jit(solution)/shard_map/ppermute | solution.py:436
  22.7 0.6 %shard_map.116 = (bf16[800,128]{1,0:T(8,128)(2,1)S(1)}, f32[512,128]{1,0:T(8,128)S(1)}, f32[288,128]{1,0:T(8,128)S(1)}) custom-call(s32[19]{0:T(128)S(1)} %stack.67.refs_0_, bf16[1312,128]{1,0:T(8,128)(2,1)S(1)} %collective-permute-done.3.refs_1_, f32[1024,128]{1,0:T(8,128)S(1)} %get-tuple-element.66.refs_2_, f32[288,128]{1,0:T(8,128)S(1)} %get-tuple-element.67.refs_3_, ...), custom_call_target="tpu_custom_call" | custom-call | tf_op jit(solution)/shard_map/pallas_call | solution.py:48
  23.3 1.6 %collective-permute-start.5 = (bf16[800,128]{1,0:T(8,128)(2,1)S(1)}, bf16[800,128]{1,0:T(8,128)(2,1)S(1)}, u32[]{:S(2)}, u32[]{:S(2)}) collective-permute-start(bf16[800,128]{1,0:T(8,128)(2,1)S(1)} %get-tuple-element.68.refs_4_), channel_id=1, source_target_pairs={{0,16},{1,17},{2,18},{3,19},{4,12},{5,13},{6,14},{7,15},{8,24},{9,... | collective-permute-start | bytes 614408 | tf_op jit(solution)/shard_map/ppermute | solution.py:436
  24.9 2.6 %collective-permute-done.2.refs_1_ = bf16[544,256]{1,0:T(8,128)(2,1)S(1)} collective-permute-done((bf16[544,256]{1,0:T(8,128)(2,1)S(1)}, bf16[544,256]{1,0:T(8,128)(2,1)S(1)}, u32[]{:S(2)}, u32[]{:S(2)}) %collective-permute-start.2) | collective-permute-done | bytes 278560 | tf_op jit(solution)/shard_map/ppermute | solution.py:436
  27.5 0.6 %shard_map.117 = (bf16[272,256]{1,0:T(8,128)(2,1)S(1)}, f32[272,256]{1,0:T(8,128)S(1)}, bf16[16,512]{1,0:T(8,128)(2,1)S(1)}) custom-call(s32[19]{0:T(128)S(1)} %stack.67.refs_0_, bf16[544,256]{1,0:T(8,128)(2,1)S(1)} %collective-permute-done.2.refs_1_, f32[544,256]{1,0:T(8,128)S(1)} %shard_map.115.refs_4_.refs_2_, ...), custom_call_target="tpu_custom_call" | custom-call | tf_op jit(solution)/shard_map/pallas_call | solution.py:48
  28.1 1.8 %collective-permute-start.4 = (bf16[272,256]{1,0:T(8,128)(2,1)S(1)}, bf16[272,256]{1,0:T(8,128)(2,1)S(1)}, u32[]{:S(2)}, u32[]{:S(2)}) collective-permute-start(bf16[272,256]{1,0:T(8,128)(2,1)S(1)} %get-tuple-element.69.refs_4_), channel_id=1, source_target_pairs={{0,2},{1,3},{2,0},{3,1},{4,5},{5,4},{6,7},{7,6},{8,10},{9,11},{10,... | collective-permute-start | bytes 417800 | tf_op jit(solution)/shard_map/ppermute | solution.py:436
  29.9 0.7 %shard_map.118 = (bf16[544,128]{1,0:T(8,128)(2,1)S(1)}, f32[256,128]{1,0:T(8,128)S(1)}, f32[288,128]{1,0:T(8,128)S(1)}) custom-call(s32[19]{0:T(128)S(1)} %stack.67.refs_0_, bf16[800,128]{1,0:T(8,128)(2,1)S(1)} %collective-permute-done.5.refs_1_, f32[512,128]{1,0:T(8,128)S(1)} %get-tuple-element.72.refs_2_, f32[288,128]{1,0:T(8,128)S(1)} %get-tuple-element.73.refs_3_, ...), custom_call_target="tpu_custom_call" | custom-call | tf_op jit(solution)/shard_map/pallas_call | solution.py:48
  30.6 1.9 %collective-permute-start.7 = (bf16[544,128]{1,0:T(8,128)(2,1)S(1)}, bf16[544,128]{1,0:T(8,128)(2,1)S(1)}, u32[]{:S(2)}, u32[]{:S(2)}) collective-permute-start(bf16[544,128]{1,0:T(8,128)(2,1)S(1)} %get-tuple-element.74.refs_4_), channel_id=1, source_target_pairs={{0,2},{1,3},{2,0},{3,1},{4,5},{5,4},{6,7},{7,6},{8,10},{9,11},{10,... | collective-permute-start | bytes 417800 | tf_op jit(solution)/shard_map/ppermute | solution.py:436
  32.4 2.0 %collective-permute-done.4.refs_1_ = bf16[272,256]{1,0:T(8,128)(2,1)S(1)} collective-permute-done((bf16[272,256]{1,0:T(8,128)(2,1)S(1)}, bf16[272,256]{1,0:T(8,128)(2,1)S(1)}, u32[]{:S(2)}, u32[]{:S(2)}) %collective-permute-start.4) | collective-permute-done | bytes 139296 | tf_op jit(solution)/shard_map/ppermute | solution.py:436
  34.4 0.6 %shard_map.119 = (bf16[272,256]{1,0:T(8,128)(2,1)S(1)}, f32[272,256]{1,0:T(8,128)S(1)}, bf16[16,512]{1,0:T(8,128)(2,1)S(1)}) custom-call(s32[19]{0:T(128)S(1)} %stack.67.refs_0_, bf16[272,256]{1,0:T(8,128)(2,1)S(1)} %collective-permute-done.4.refs_1_, f32[272,256]{1,0:T(8,128)S(1)} %get-tuple-element.70.refs_2_, ...), custom_call_target="tpu_custom_call" | custom-call | tf_op jit(solution)/shard_map/pallas_call | solution.py:48
  35.0 1.8 %collective-permute-start.6 = (bf16[272,256]{1,0:T(8,128)(2,1)S(1)}, bf16[272,256]{1,0:T(8,128)(2,1)S(1)}, u32[]{:S(2)}, u32[]{:S(2)}) collective-permute-start(bf16[272,256]{1,0:T(8,128)(2,1)S(1)} %get-tuple-element.76.refs_4_), channel_id=1, source_target_pairs={{0,8},{1,9},{2,10},{3,11},{4,20},{5,21},{6,22},{7,23},{8,0},{9,1},... | collective-permute-start | bytes 417800 | tf_op jit(solution)/shard_map/ppermute | solution.py:436
  36.8 2.2 %collective-permute-done.7.refs_1_ = bf16[544,128]{1,0:T(8,128)(2,1)S(1)} collective-permute-done((bf16[544,128]{1,0:T(8,128)(2,1)S(1)}, bf16[544,128]{1,0:T(8,128)(2,1)S(1)}, u32[]{:S(2)}, u32[]{:S(2)}) %collective-permute-start.7) | collective-permute-done | bytes 139296 | tf_op jit(solution)/shard_map/ppermute | solution.py:436
  40.7 0.7 %collective-permute-start.9 = (bf16[272,256]{1,0:T(8,128)(2,1)S(1)}, bf16[272,256]{1,0:T(8,128)(2,1)S(1)}, u32[]{:S(2)}, u32[]{:S(2)}) collective-permute-start(bf16[272,256]{1,0:T(8,128)(2,1)S(1)} %get-tuple-element.81.refs_4_), channel_id=1, source_target_pairs={{0,16},{1,17},{2,18},{3,19},{4,12},{5,13},{6,14},{7,15},{8,24},{9,... | collective-permute-start | bytes 417800 | tf_op jit(solution)/shard_map/ppermute | solution.py:436
  41.4 2.6 %shard_map.122 = (bf16[768,512]{1,0:T(8,128)(2,1)}, f32[8,128]{1,0:T(8,128)S(1)}) custom-call(s32[19]{0:T(128)S(1)} %stack.67.refs_0_, bf16[384,512]{1,0:T(8,128)(2,1)S(1)} %get-tuple-element.59.refs_1_, bf16[16,512]{1,0:T(8,128)(2,1)S(1)} %get-tuple-element.75.refs_2_, bf16[2048,512]{1,0:T(8,128)(2,1)S(1)} %copy-done, ...), custom_call_target="tpu_custom_call" | custom-call | tf_op jit(solution)/shard_map/pallas_call | solution.py:48
  44.0 1.9 %collective-permute-done.9.refs_4_ = bf16[272,256]{1,0:T(8,128)(2,1)S(1)} collective-permute-done((bf16[272,256]{1,0:T(8,128)(2,1)S(1)}, bf16[272,256]{1,0:T(8,128)(2,1)S(1)}, u32[]{:S(2)}, u32[]{:S(2)}) %collective-permute-start.9) | collective-permute-done | bytes 139296 | tf_op jit(solution)/shard_map/ppermute | solution.py:436
  45.9 0.7 %shard_map.123 = (f32[256,128]{1,0:T(8,128)S(1)}, bf16[256,128]{1,0:T(8,128)(2,1)S(1)}, bf16[832,128]{1,0:T(8,128)(2,1)S(1)}) custom-call(s32[19]{0:T(128)S(1)} %stack.67.refs_0_, bf16[560,128]{1,0:T(8,128)(2,1)S(1)} %collective-permute-done.8.refs_1_, f32[256,128]{1,0:T(8,128)S(1)} %get-tuple-element.83.refs_2_, f32[288,128]{1,0:T(8,128)S(1)} %get-tuple-element.84.refs_3_, ...), custom_call_target="tpu_custom_call" | custom-call | tf_op jit(solution)/shard_map/pallas_call | solution.py:48
  46.6 1.8 %collective-permute-start.12 = (bf16[256,128]{1,0:T(8,128)(2,1)S(1)}, bf16[256,128]{1,0:T(8,128)(2,1)S(1)}, u32[]{:S(2)}, u32[]{:S(2)}) collective-permute-start(bf16[256,128]{1,0:T(8,128)(2,1)S(1)} %get-tuple-element.88.refs_3_.refs_2_), channel_id=1, source_target_pairs={{0,12},{1,13},{2,14},{3,15},{4,16},{5,17},{6,18},{7,19},{8,4},{9,5... | collective-permute-start | bytes 196616 | tf_op jit(solution)/shard_map/ppermute | solution.py:447
  48.7 1.5 %shard_map.124 = (f32[64,512]{1,0:T(8,128)}, f32[8,128]{1,0:T(8,128)S(1)}) custom-call(s32[19]{0:T(128)S(1)} %stack.67.refs_0_, f32[256,128]{1,0:T(8,128)S(1)} %get-tuple-element.87.refs_1_, bf16[512,256]{1,0:T(8,128)(2,1)S(1)} %copy-done.1, bf16[256,128]{1,0:T(8,128)(2,1)S(1)} %get-tuple-element.88.refs_3_.refs_2_), custom_call_target="tpu_custom_call" | custom-call | tf_op jit(solution)/shard_map/pallas_call | solution.py:48
  50.4 2.3 %collective-permute-done.11.refs_4_ = bf16[256,128]{1,0:T(8,128)(2,1)S(1)} collective-permute-done((bf16[256,128]{1,0:T(8,128)(2,1)S(1)}, bf16[256,128]{1,0:T(8,128)(2,1)S(1)}, u32[]{:S(2)}, u32[]{:S(2)}) %collective-permute-start.11) | collective-permute-done | bytes 65568 | tf_op jit(solution)/shard_map/ppermute | solution.py:436
  52.7 1.5 %shard_map.125 = (f32[512,256]{1,0:T(8,128)}, f32[1,512]{1,0:T(1,128)}, bf16[2,256,256]{2,1,0:T(8,128)(2,1)}, f32[2,256]{1,0:T(2,128)}) custom-call(s32[19]{0:T(128)S(1)} %stack.67.refs_0_, bf16[832,128]{1,0:T(8,128)(2,1)S(1)} %get-tuple-element.90.refs_1_, bf16[256,128]{1,0:T(8,128)(2,1)S(1)} %get-tuple-element.88.refs_3_.refs_2_, ...), custom_call_target="tpu_custom_call" | custom-call | tf_op jit(solution)/shard_map/pallas_call | solution.py:48
  (25 shorter events, 3.5 us)
Async XLA Ops:
  1.3 9.2 %collective-permute-start = (bf16[2,512]{1,0:T(2,128)(2,1)S(1)}, bf16[2,512]{1,0:T(2,128)(2,1)S(1)}, u32[]{:S(2)}, u32[]{:S(2)}) collective-permute-start(bf16[2,512]{1,0:T(2,128)(2,1)S(1)} %slice.3), channel_id=1, source_target_pairs={{0,1},{1,2},{2,3},{4,5},{5,6},{6,7},{8,9},{9,10},{10,11},{12,13},{... | collective-permute-start | bytes 6152 | tf_op jit(solution)/shard_map/ppermute | solution.py:425
  6.4 1.6 %copy-start = (bf16[2048,512]{1,0:T(8,128)(2,1)S(1)}, bf16[2048,512]{1,0:T(8,128)(2,1)}, u32[]{:S(2)}) copy-start(bf16[2048,512]{1,0:T(8,128)(2,1)} %refs_3_.1) | copy-start | bytes 6291460
  6.4 1.8 %copy-start.2 = (bf16[2,1024,256]{2,1,0:T(8,128)(2,1)S(1)}, bf16[2,1024,256]{2,1,0:T(8,128)(2,1)}, u32[]{:S(2)}) copy-start(bf16[2,1024,256]{2,1,0:T(8,128)(2,1)} %refs_5_.3) | copy-start | bytes 3145732
  6.4 2.1 %copy-start.3 = (bf16[768,512]{1,0:T(8,128)(2,1)S(1)}, bf16[768,512]{1,0:T(8,128)(2,1)}, u32[]{:S(2)}) copy-start(bf16[768,512]{1,0:T(8,128)(2,1)} %refs_1_.1) | copy-start | bytes 2359300
  6.4 2.0 %copy-start.4 = (s32[1,2,384]{2,1,0:T(2,128)S(1)}, s32[1,2,384]{2,1,0:T(2,128)}, u32[]{:S(2)}) copy-start(s32[1,2,384]{2,1,0:T(2,128)} %param.7) | copy-start | bytes 9220
  6.5 2.0 %copy-start.5 = (f32[512]{0:T(512)S(1)}, f32[512]{0:T(512)}, u32[]{:S(2)}) copy-start(f32[512]{0:T(512)} %param.9) | copy-start | bytes 6148
  8.5 2.1 %copy-start.1 = (bf16[512,256]{1,0:T(8,128)(2,1)S(1)}, bf16[512,256]{1,0:T(8,128)(2,1)}, u32[]{:S(2)}) copy-start(bf16[512,256]{1,0:T(8,128)(2,1)} %refs_2_.3) | copy-start | bytes 786436
  12.3 2.5 %collective-permute-start.1 = (bf16[3360,128]{1,0:T(8,128)(2,1)S(1)}, bf16[3360,128]{1,0:T(8,128)(2,1)S(1)}, u32[]{:S(2)}, u32[]{:S(2)}) collective-permute-start(bf16[3360,128]{1,0:T(8,128)(2,1)S(1)} %get-tuple-element.58.refs_6_), channel_id=1, source_target_pairs={{0,4},{1,5},{2,6},{3,7},{4,0},{5,1},{6,2},{7,3},{8,12},{9,13},{10,... | collective-permute-start | bytes 2580488 | tf_op jit(solution)/shard_map/ppermute | solution.py:436
  15.4 7.2 %collective-permute-start.3 = (bf16[1312,128]{1,0:T(8,128)(2,1)S(1)}, bf16[1312,128]{1,0:T(8,128)(2,1)S(1)}, u32[]{:S(2)}, u32[]{:S(2)}) collective-permute-start(bf16[1312,128]{1,0:T(8,128)(2,1)S(1)} %get-tuple-element.65.refs_4_), channel_id=1, source_target_pairs={{0,8},{1,9},{2,10},{3,11},{4,20},{5,21},{6,22},{7,23},{8,0},{9,1},... | collective-permute-start | bytes 1007624 | tf_op jit(solution)/shard_map/ppermute | solution.py:436
  18.2 9.3 %collective-permute-start.2 = (bf16[544,256]{1,0:T(8,128)(2,1)S(1)}, bf16[544,256]{1,0:T(8,128)(2,1)S(1)}, u32[]{:S(2)}, u32[]{:S(2)}) collective-permute-start(bf16[544,256]{1,0:T(8,128)(2,1)S(1)} %shard_map.114.refs_4_), channel_id=1, source_target_pairs={{0,1},{1,0},{2,3},{3,2},{4,6},{5,7},{6,4},{7,5},{8,9},{9,8},{10,11... | collective-permute-start | bytes 835592 | tf_op jit(solution)/shard_map/ppermute | solution.py:436
  23.3 6.6 %collective-permute-start.5 = (bf16[800,128]{1,0:T(8,128)(2,1)S(1)}, bf16[800,128]{1,0:T(8,128)(2,1)S(1)}, u32[]{:S(2)}, u32[]{:S(2)}) collective-permute-start(bf16[800,128]{1,0:T(8,128)(2,1)S(1)} %get-tuple-element.68.refs_4_), channel_id=1, source_target_pairs={{0,16},{1,17},{2,18},{3,19},{4,12},{5,13},{6,14},{7,15},{8,24},{9,... | collective-permute-start | bytes 614408 | tf_op jit(solution)/shard_map/ppermute | solution.py:436
  28.1 6.3 %collective-permute-start.4 = (bf16[272,256]{1,0:T(8,128)(2,1)S(1)}, bf16[272,256]{1,0:T(8,128)(2,1)S(1)}, u32[]{:S(2)}, u32[]{:S(2)}) collective-permute-start(bf16[272,256]{1,0:T(8,128)(2,1)S(1)} %get-tuple-element.69.refs_4_), channel_id=1, source_target_pairs={{0,2},{1,3},{2,0},{3,1},{4,5},{5,4},{6,7},{7,6},{8,10},{9,11},{10,... | collective-permute-start | bytes 417800 | tf_op jit(solution)/shard_map/ppermute | solution.py:436
  30.6 8.4 %collective-permute-start.7 = (bf16[544,128]{1,0:T(8,128)(2,1)S(1)}, bf16[544,128]{1,0:T(8,128)(2,1)S(1)}, u32[]{:S(2)}, u32[]{:S(2)}) collective-permute-start(bf16[544,128]{1,0:T(8,128)(2,1)S(1)} %get-tuple-element.74.refs_4_), channel_id=1, source_target_pairs={{0,2},{1,3},{2,0},{3,1},{4,5},{5,4},{6,7},{7,6},{8,10},{9,11},{10,... | collective-permute-start | bytes 417800 | tf_op jit(solution)/shard_map/ppermute | solution.py:436
  35.0 5.1 %collective-permute-start.6 = (bf16[272,256]{1,0:T(8,128)(2,1)S(1)}, bf16[272,256]{1,0:T(8,128)(2,1)S(1)}, u32[]{:S(2)}, u32[]{:S(2)}) collective-permute-start(bf16[272,256]{1,0:T(8,128)(2,1)S(1)} %get-tuple-element.76.refs_4_), channel_id=1, source_target_pairs={{0,8},{1,9},{2,10},{3,11},{4,20},{5,21},{6,22},{7,23},{8,0},{9,1},... | collective-permute-start | bytes 417800 | tf_op jit(solution)/shard_map/ppermute | solution.py:436
  39.6 6.3 %collective-permute-start.8 = (bf16[560,128]{1,0:T(8,128)(2,1)S(1)}, bf16[560,128]{1,0:T(8,128)(2,1)S(1)}, u32[]{:S(2)}, u32[]{:S(2)}) collective-permute-start(bf16[560,128]{1,0:T(8,128)(2,1)S(1)} %get-tuple-element.80.refs_3_), channel_id=1, source_target_pairs={{0,1},{1,0},{2,3},{3,2},{4,6},{5,7},{6,4},{7,5},{8,9},{9,8},{10,11... | collective-permute-start | bytes 430088 | tf_op jit(solution)/shard_map/ppermute | solution.py:436
  40.7 5.1 %collective-permute-start.9 = (bf16[272,256]{1,0:T(8,128)(2,1)S(1)}, bf16[272,256]{1,0:T(8,128)(2,1)S(1)}, u32[]{:S(2)}, u32[]{:S(2)}) collective-permute-start(bf16[272,256]{1,0:T(8,128)(2,1)S(1)} %get-tuple-element.81.refs_4_), channel_id=1, source_target_pairs={{0,16},{1,17},{2,18},{3,19},{4,12},{5,13},{6,14},{7,15},{8,24},{9,... | collective-permute-start | bytes 417800 | tf_op jit(solution)/shard_map/ppermute | solution.py:436
  46.5 6.1 %collective-permute-start.10 = (bf16[832,128]{1,0:T(8,128)(2,1)S(1)}, bf16[832,128]{1,0:T(8,128)(2,1)S(1)}, u32[]{:S(2)}, u32[]{:S(2)}) collective-permute-start(bf16[832,128]{1,0:T(8,128)(2,1)S(1)} %get-tuple-element.90.refs_1_), channel_id=1, source_target_pairs={{0,4},{1,5},{2,6},{3,7},{4,0},{5,1},{6,2},{7,3},{8,12},{9,13},{10,... | collective-permute-start | bytes 638984 | tf_op jit(solution)/shard_map/ppermute | solution.py:436
  46.6 3.7 %collective-permute-start.12 = (bf16[256,128]{1,0:T(8,128)(2,1)S(1)}, bf16[256,128]{1,0:T(8,128)(2,1)S(1)}, u32[]{:S(2)}, u32[]{:S(2)}) collective-permute-start(bf16[256,128]{1,0:T(8,128)(2,1)S(1)} %get-tuple-element.88.refs_3_.refs_2_), channel_id=1, source_target_pairs={{0,12},{1,13},{2,14},{3,15},{4,16},{5,17},{6,18},{7,19},{8,4},{9,5... | collective-permute-start | bytes 196616 | tf_op jit(solution)/shard_map/ppermute | solution.py:447
  48.4 4.3 %collective-permute-start.11 = (bf16[256,128]{1,0:T(8,128)(2,1)S(1)}, bf16[256,128]{1,0:T(8,128)(2,1)S(1)}, u32[]{:S(2)}, u32[]{:S(2)}) collective-permute-start(bf16[256,128]{1,0:T(8,128)(2,1)S(1)} %get-tuple-element.88.refs_3_.refs_2_), channel_id=1, source_target_pairs={{0,8},{1,9},{2,10},{3,11},{4,20},{5,21},{6,22},{7,23},{8,0},{9,1},... | collective-permute-start | bytes 196616 | tf_op jit(solution)/shard_map/ppermute | solution.py:436

commit v12 on v11

--- a/solution.py
+++ b/solution.py
@@ -77,8 +77,8 @@
     return jnp.where(codes == places, 1.0, 0.0).astype(BF16)
 
 
-def idle_kernel(info, out):
-    out[...] = jnp.zeros(out.shape, F32)
+def halo_kernel(info, rows, out):
+    out[...] = rows[...]
 
 
 def local_kernel(info, feats, weight, bias, codes, books, unfold, conv, chosen, wide):
@@ -534,14 +534,12 @@
     at_row = at_sums + len(sums_bits)
     info = jnp.stack(bits + [start] + send_codes + keep_codes + places + sums_bits + [row_code]).astype(jnp.int32)
 
-    halo = shifted(feats[-2:], "tm", 1)
-    idle = call(idle_kernel, shape((8, LANES), F32), [info], flops=10 ** 11)
+    halo = shifted(call(halo_kernel, shape((2, channels), BF16), [info, feats[-2:]], flops=10 ** 11), "tm", 1)
     weight, proj, codes = conv_weight, proj_weight, codes[0]
     unfold, conv, chosen = call(
         local_kernel,
         [shape((frames, width), BF16), shape((frames, channels), F32), shape((levels, frames, dz), BF16)],
         [info, feats, weight, conv_bias[None, :], codes, codebooks],
-        after=[idle],
         scratch=[VMEM((channels // LANES, rows_in + 8, LANES), F32)],
     )
 

time: 54.6 us -> 54.3 us (level)
  starting transfers between devices: 18.5 us -> 21.8 us
  waiting for transfers between devices: 14.1 us -> 11.4 us
  local copies, waits for them, and re-layouts: 2.3 us -> 0.84 us
    ppermute x11, starting transfers between devices: 11.7 us -> 16.3 us  [swapped(): return lax.ppermute(block, ('dp', 'tm'), route)]
    ppermute x11, waiting for transfers between devices: 14 us -> 10.9 us  [swapped(): return lax.ppermute(block, ('dp', 'tm'), route)]
    unnamed x12, local copies, waits for them, and re-layouts: 1.5 us -> 0.04 us
    ppermute x1, starting transfers between devices: 1.79 us -> 0.52 us  [crossed(): return lax.ppermute(block, ('dp', 'tm'), route)]
  transfers between devices with their start and end apart: 13 -> 13, of which waited for: 9 -> 9; matrix products, arithmetic and copies ran while one was open for 0% -> 0% of each run, Pallas kernels for 26% -> 25%
where the time goes in v12:
time: 54.3 us; the launch traced here: 53.4 us
  starting transfers between devices  21.8 us (40%)
  Pallas kernels  18.5 us (34%)
  waiting for transfers between devices  11.4 us (21%)
  between operations  0.9 us (2%)
  local copies, waits for them, and re-layouts  0.84 us (2%)
    pallas_call x17, Pallas kernels, call(): pl.pallas_call(kernel, out_shape=shown, in_specs=specs, out_specs=[pl.Blo...  18.5 us
    ppermute x11, starting transfers between devices, swapped(): return lax.ppermute(block, ('dp', 'tm'), route)  16.3 us
    ppermute x11, waiting for transfers between devices, swapped(): return lax.ppermute(block, ('dp', 'tm'), route)  10.9 us
    ppermute x1, starting transfers between devices, shifted(): return lax.ppermute(block, axis, route)  5.06 us
  transfers between devices with their start and end apart: 13, of which 9 were waited for; matrix products, arithmetic and copies ran while one was open for 0% of the time, Pallas kernels for 25%

profile of v12, /device:TPU:0, one launch (start us, length us, event | category | flops | bytes accessed | tf_op | source)
XLA Modules:
  0.0 53.4 jit_solution(293688206672338248)
XLA Ops:
  0.7 0.7 %slice.3.refs_1_ = bf16[2,512]{1,0:T(2,128)(2,1)S(1)} slice(bf16[768,512]{1,0:T(8,128)(2,1)} %refs_1_.1), slice={[766:768], [0:512]} | slice | bytes 4096 | tf_op jit(solution)/shard_map/slice | solution.py:537
  2.1 5.1 %collective-permute-start = (bf16[2,512]{1,0:T(2,128)(2,1)S(1)}, bf16[2,512]{1,0:T(2,128)(2,1)S(1)}, u32[]{:S(2)}, u32[]{:S(2)}) collective-permute-start(bf16[2,512]{1,0:T(2,128)(2,1)S(1)} %shard_map.109), channel_id=1, source_target_pairs={{0,1},{1,2},{2,3},{4,5},{5,6},{6,7},{8,9},{9,10},{10,11},{12,13},{... | collective-permute-start | bytes 6152 | tf_op jit(solution)/shard_map/ppermute | solution.py:425
  7.2 2.1 %shard_map.110 = (bf16[384,2048]{1,0:T(8,128)(2,1)S(1)}, f32[384,512]{1,0:T(8,128)S(1)}, bf16[2,384,256]{2,1,0:T(8,128)(2,1)S(1)}) custom-call(s32[19]{0:T(128)S(1)} %stack.67.refs_0_, bf16[768,512]{1,0:T(8,128)(2,1)S(1)} %copy-done.3, bf16[2048,512]{1,0:T(8,128)(2,1)S(1)} %copy-done, f32[1,512]{1,0:T(1,128)S(1)} %bitcast.20, s32[2,384]{1,0:T(2,128)S(1)} %bitcast.18, ...), custom_call_target="tpu_custom_call" | custom-call | tf_op jit(solution)/shard_map/pallas_call | solution.py:48
  9.3 1.7 %shard_map.111 = (bf16[384,2048]{1,0:T(8,128)(2,1)S(1)}, bf16[384,512]{1,0:T(8,128)(2,1)S(1)}, bf16[384,256]{1,0:T(8,128)(2,1)S(1)}, bf16[256,384]{1,0:T(8,128)(...) custom-call(s32[19]{0:T(128)S(1)} %stack.67.refs_0_, ...), custom_call_target="tpu_custom_call", output_to_operand_aliasing={{0}: (2, {})} | custom-call | tf_op jit(solution)/shard_map/pallas_call | solution.py:48
  11.1 1.2 %shard_map.112 = (f32[2048,128]{1,0:T(8,128)S(1)}, f32[512,128]{1,0:T(8,128)S(1)}, bf16[384,512]{1,0:T(8,128)(2,1)S(1)}, f32[32,128]{1,0:T(8,128)S(1)}, bf16[16,512]{1,0:T(8,128)(2,1)S(1)}) custom-call(s32[19]{0:T(128)S(1)} %stack.67.refs_0_, bf16[256,384]{1,0:T(8,128)(2,1)S(1)} %get-tuple-element.54.refs_1_, ...), custom_call_target="tpu_custom_call" | custom-call | tf_op jit(solution)/shard_map/pallas_call | solution.py:48
  12.3 1.2 %collective-permute-done.1.refs_1_ = bf16[3360,128]{1,0:T(8,128)(2,1)S(1)} collective-permute-done((bf16[3360,128]{1,0:T(8,128)(2,1)S(1)}, bf16[3360,128]{1,0:T(8,128)(2,1)S(1)}, u32[]{:S(2)}, u32[]{:S(2)}) %collective-permute-start.1) | collective-permute-done | bytes 860192 | tf_op jit(solution)/shard_map/ppermute | solution.py:436
  13.5 0.7 %shard_map.113 = (bf16[1312,128]{1,0:T(8,128)(2,1)S(1)}, f32[1024,128]{1,0:T(8,128)S(1)}, f32[288,128]{1,0:T(8,128)S(1)}) custom-call(s32[19]{0:T(128)S(1)} %stack.67.refs_0_, bf16[3360,128]{1,0:T(8,128)(2,1)S(1)} %collective-permute-done.1.refs_1_, f32[2048,128]{1,0:T(8,128)S(1)} %get-tuple-element.62.refs_2_, f32[512,128]{1,0:T(8,128)S(1)} %get-tuple-element.63.refs_3_, ...), custom_call_target="tpu_custom_call" | custom-call | tf_op jit(solution)/shard_map/pallas_call | solution.py:48
  14.2 1.6 %collective-permute-start.3 = (bf16[1312,128]{1,0:T(8,128)(2,1)S(1)}, bf16[1312,128]{1,0:T(8,128)(2,1)S(1)}, u32[]{:S(2)}, u32[]{:S(2)}) collective-permute-start(bf16[1312,128]{1,0:T(8,128)(2,1)S(1)} %get-tuple-element.65.refs_4_), channel_id=1, source_target_pairs={{0,8},{1,9},{2,10},{3,11},{4,20},{5,21},{6,22},{7,23},{8,0},{9,1},... | collective-permute-start | bytes 1007624 | tf_op jit(solution)/shard_map/ppermute | solution.py:436
  15.7 1.2 %shard_map.114.refs_4_ = bf16[544,256]{1,0:T(8,128)(2,1)S(1)} custom-call(s32[19]{0:T(128)S(1)} %stack.67.refs_0_, bf16[3360,128]{1,0:T(8,128)(2,1)S(1)} %collective-permute-done.1.refs_1_, bf16[400,256]{1,0:T(8,128)(2,1)S(1)} %get-tuple-element.60.refs_2_, bf16[16,512]{1,0:T(8,128)(2,1)S(1)} %get-tuple-element.61.refs_3_, ...), custom_call_target="tpu_custom_call" | custom-call | tf_op jit(solution)/shard_map/pallas_call | solution.py:48
  16.9 1.6 %collective-permute-start.2 = (bf16[544,256]{1,0:T(8,128)(2,1)S(1)}, bf16[544,256]{1,0:T(8,128)(2,1)S(1)}, u32[]{:S(2)}, u32[]{:S(2)}) collective-permute-start(bf16[544,256]{1,0:T(8,128)(2,1)S(1)} %shard_map.114.refs_4_), channel_id=1, source_target_pairs={{0,1},{1,0},{2,3},{3,2},{4,6},{5,7},{6,4},{7,5},{8,9},{9,8},{10,11... | collective-permute-start | bytes 835592 | tf_op jit(solution)/shard_map/ppermute | solution.py:436
  18.5 1.2 %shard_map.115.refs_4_.refs_2_ = f32[544,256]{1,0:T(8,128)S(1)} custom-call(s32[19]{0:T(128)S(1)} %stack.67.refs_0_, bf16[3360,128]{1,0:T(8,128)(2,1)S(1)} %collective-permute-done.1.refs_1_, bf16[400,256]{1,0:T(8,128)(2,1)S(1)} %get-tuple-element.60.refs_2_, bf16[16,512]{1,0:T(8,128)(2,1)S(1)} %get-tuple-element.61.refs_3_, ...), custom_call_target="tpu_custom_call" | custom-call | tf_op jit(solution)/shard_map/pallas_call | solution.py:48
  19.7 1.7 %collective-permute-done.3.refs_1_ = bf16[1312,128]{1,0:T(8,128)(2,1)S(1)} collective-permute-done((bf16[1312,128]{1,0:T(8,128)(2,1)S(1)}, bf16[1312,128]{1,0:T(8,128)(2,1)S(1)}, u32[]{:S(2)}, u32[]{:S(2)}) %collective-permute-start.3) | collective-permute-done | bytes 335904 | tf_op jit(solution)/shard_map/ppermute | solution.py:436
  21.4 0.6 %shard_map.116 = (bf16[800,128]{1,0:T(8,128)(2,1)S(1)}, f32[512,128]{1,0:T(8,128)S(1)}, f32[288,128]{1,0:T(8,128)S(1)}) custom-call(s32[19]{0:T(128)S(1)} %stack.67.refs_0_, bf16[1312,128]{1,0:T(8,128)(2,1)S(1)} %collective-permute-done.3.refs_1_, f32[1024,128]{1,0:T(8,128)S(1)} %get-tuple-element.66.refs_2_, f32[288,128]{1,0:T(8,128)S(1)} %get-tuple-element.67.refs_3_, ...), custom_call_target="tpu_custom_call" | custom-call | tf_op jit(solution)/shard_map/pallas_call | solution.py:48
  22.0 1.6 %collective-permute-start.5 = (bf16[800,128]{1,0:T(8,128)(2,1)S(1)}, bf16[800,128]{1,0:T(8,128)(2,1)S(1)}, u32[]{:S(2)}, u32[]{:S(2)}) collective-permute-start(bf16[800,128]{1,0:T(8,128)(2,1)S(1)} %get-tuple-element.68.refs_4_), channel_id=1, source_target_pairs={{0,16},{1,17},{2,18},{3,19},{4,12},{5,13},{6,14},{7,15},{8,24},{9,... | collective-permute-start | bytes 614408 | tf_op jit(solution)/shard_map/ppermute | solution.py:436
  23.6 2.6 %collective-permute-done.2.refs_1_ = bf16[544,256]{1,0:T(8,128)(2,1)S(1)} collective-permute-done((bf16[544,256]{1,0:T(8,128)(2,1)S(1)}, bf16[544,256]{1,0:T(8,128)(2,1)S(1)}, u32[]{:S(2)}, u32[]{:S(2)}) %collective-permute-start.2) | collective-permute-done | bytes 278560 | tf_op jit(solution)/shard_map/ppermute | solution.py:436
  26.2 0.6 %shard_map.117 = (bf16[272,256]{1,0:T(8,128)(2,1)S(1)}, f32[272,256]{1,0:T(8,128)S(1)}, bf16[16,512]{1,0:T(8,128)(2,1)S(1)}) custom-call(s32[19]{0:T(128)S(1)} %stack.67.refs_0_, bf16[544,256]{1,0:T(8,128)(2,1)S(1)} %collective-permute-done.2.refs_1_, f32[544,256]{1,0:T(8,128)S(1)} %shard_map.115.refs_4_.refs_2_, ...), custom_call_target="tpu_custom_call" | custom-call | tf_op jit(solution)/shard_map/pallas_call | solution.py:48
  26.8 1.8 %collective-permute-start.4 = (bf16[272,256]{1,0:T(8,128)(2,1)S(1)}, bf16[272,256]{1,0:T(8,128)(2,1)S(1)}, u32[]{:S(2)}, u32[]{:S(2)}) collective-permute-start(bf16[272,256]{1,0:T(8,128)(2,1)S(1)} %get-tuple-element.69.refs_4_), channel_id=1, source_target_pairs={{0,2},{1,3},{2,0},{3,1},{4,5},{5,4},{6,7},{7,6},{8,10},{9,11},{10,... | collective-permute-start | bytes 417800 | tf_op jit(solution)/shard_map/ppermute | solution.py:436
  28.6 0.7 %shard_map.118 = (bf16[544,128]{1,0:T(8,128)(2,1)S(1)}, f32[256,128]{1,0:T(8,128)S(1)}, f32[288,128]{1,0:T(8,128)S(1)}) custom-call(s32[19]{0:T(128)S(1)} %stack.67.refs_0_, bf16[800,128]{1,0:T(8,128)(2,1)S(1)} %collective-permute-done.5.refs_1_, f32[512,128]{1,0:T(8,128)S(1)} %get-tuple-element.72.refs_2_, f32[288,128]{1,0:T(8,128)S(1)} %get-tuple-element.73.refs_3_, ...), custom_call_target="tpu_custom_call" | custom-call | tf_op jit(solution)/shard_map/pallas_call | solution.py:48
  29.3 1.9 %collective-permute-start.7 = (bf16[544,128]{1,0:T(8,128)(2,1)S(1)}, bf16[544,128]{1,0:T(8,128)(2,1)S(1)}, u32[]{:S(2)}, u32[]{:S(2)}) collective-permute-start(bf16[544,128]{1,0:T(8,128)(2,1)S(1)} %get-tuple-element.74.refs_4_), channel_id=1, source_target_pairs={{0,2},{1,3},{2,0},{3,1},{4,5},{5,4},{6,7},{7,6},{8,10},{9,11},{10,... | collective-permute-start | bytes 417800 | tf_op jit(solution)/shard_map/ppermute | solution.py:436
  31.2 2.0 %collective-permute-done.4.refs_1_ = bf16[272,256]{1,0:T(8,128)(2,1)S(1)} collective-permute-done((bf16[272,256]{1,0:T(8,128)(2,1)S(1)}, bf16[272,256]{1,0:T(8,128)(2,1)S(1)}, u32[]{:S(2)}, u32[]{:S(2)}) %collective-permute-start.4) | collective-permute-done | bytes 139296 | tf_op jit(solution)/shard_map/ppermute | solution.py:436
  33.1 0.6 %shard_map.119 = (bf16[272,256]{1,0:T(8,128)(2,1)S(1)}, f32[272,256]{1,0:T(8,128)S(1)}, bf16[16,512]{1,0:T(8,128)(2,1)S(1)}) custom-call(s32[19]{0:T(128)S(1)} %stack.67.refs_0_, bf16[272,256]{1,0:T(8,128)(2,1)S(1)} %collective-permute-done.4.refs_1_, f32[272,256]{1,0:T(8,128)S(1)} %get-tuple-element.70.refs_2_, ...), custom_call_target="tpu_custom_call" | custom-call | tf_op jit(solution)/shard_map/pallas_call | solution.py:48
  33.7 2.0 %collective-permute-start.6 = (bf16[272,256]{1,0:T(8,128)(2,1)S(1)}, bf16[272,256]{1,0:T(8,128)(2,1)S(1)}, u32[]{:S(2)}, u32[]{:S(2)}) collective-permute-start(bf16[272,256]{1,0:T(8,128)(2,1)S(1)} %get-tuple-element.76.refs_4_), channel_id=1, source_target_pairs={{0,8},{1,9},{2,10},{3,11},{4,20},{5,21},{6,22},{7,23},{8,0},{9,1},... | collective-permute-start | bytes 417800 | tf_op jit(solution)/shard_map/ppermute | solution.py:436
  35.7 1.9 %collective-permute-done.7.refs_1_ = bf16[544,128]{1,0:T(8,128)(2,1)S(1)} collective-permute-done((bf16[544,128]{1,0:T(8,128)(2,1)S(1)}, bf16[544,128]{1,0:T(8,128)(2,1)S(1)}, u32[]{:S(2)}, u32[]{:S(2)}) %collective-permute-start.7) | collective-permute-done | bytes 139296 | tf_op jit(solution)/shard_map/ppermute | solution.py:436
  37.6 0.6 %shard_map.120 = (bf16[560,128]{1,0:T(8,128)(2,1)S(1)}, f32[256,128]{1,0:T(8,128)S(1)}, f32[288,128]{1,0:T(8,128)S(1)}) custom-call(s32[19]{0:T(128)S(1)} %stack.67.refs_0_, bf16[544,128]{1,0:T(8,128)(2,1)S(1)} %collective-permute-done.7.refs_1_, f32[256,128]{1,0:T(8,128)S(1)} %get-tuple-element.78.refs_2_, f32[288,128]{1,0:T(8,128)S(1)} %get-tuple-element.79.refs_3_, ...), custom_call_target="tpu_custom_call" | custom-call | tf_op jit(solution)/shard_map/pallas_call | solution.py:48
  38.8 0.6 %shard_map.121 = (bf16[272,256]{1,0:T(8,128)(2,1)S(1)}, f32[272,256]{1,0:T(8,128)S(1)}) custom-call(s32[19]{0:T(128)S(1)} %stack.67.refs_0_, bf16[272,256]{1,0:T(8,128)(2,1)S(1)} %collective-permute-done.6.refs_1_, f32[272,256]{1,0:T(8,128)S(1)} %get-tuple-element.77.refs_2_, bf16[560,128]{1,0:T(8,128)(2,1)S(1)} %get-tuple-element.80.refs_3_), custom_call_target="tpu_custom_call" | custom-call | tf_op jit(solution)/shard_map/pallas_call | solution.py:48
  39.4 3.6 %collective-permute-start.9 = (bf16[272,256]{1,0:T(8,128)(2,1)S(1)}, bf16[272,256]{1,0:T(8,128)(2,1)S(1)}, u32[]{:S(2)}, u32[]{:S(2)}) collective-permute-start(bf16[272,256]{1,0:T(8,128)(2,1)S(1)} %get-tuple-element.81.refs_4_), channel_id=1, source_target_pairs={{0,16},{1,17},{2,18},{3,19},{4,12},{5,13},{6,14},{7,15},{8,24},{9,... | collective-permute-start | bytes 417800 | tf_op jit(solution)/shard_map/ppermute | solution.py:436
  43.0 2.6 %shard_map.122 = (bf16[768,512]{1,0:T(8,128)(2,1)}, f32[8,128]{1,0:T(8,128)S(1)}) custom-call(s32[19]{0:T(128)S(1)} %stack.67.refs_0_, bf16[384,512]{1,0:T(8,128)(2,1)S(1)} %get-tuple-element.59.refs_1_, bf16[16,512]{1,0:T(8,128)(2,1)S(1)} %get-tuple-element.75.refs_2_, bf16[2048,512]{1,0:T(8,128)(2,1)S(1)} %copy-done, ...), custom_call_target="tpu_custom_call" | custom-call | tf_op jit(solution)/shard_map/pallas_call | solution.py:48
  46.1 0.7 %shard_map.123 = (f32[256,128]{1,0:T(8,128)S(1)}, bf16[256,128]{1,0:T(8,128)(2,1)S(1)}, bf16[832,128]{1,0:T(8,128)(2,1)S(1)}) custom-call(s32[19]{0:T(128)S(1)} %stack.67.refs_0_, bf16[560,128]{1,0:T(8,128)(2,1)S(1)} %collective-permute-done.8.refs_1_, f32[256,128]{1,0:T(8,128)S(1)} %get-tuple-element.83.refs_2_, f32[288,128]{1,0:T(8,128)S(1)} %get-tuple-element.84.refs_3_, ...), custom_call_target="tpu_custom_call" | custom-call | tf_op jit(solution)/shard_map/pallas_call | solution.py:48
  47.3 1.6 %collective-permute-start.11 = (bf16[256,128]{1,0:T(8,128)(2,1)S(1)}, bf16[256,128]{1,0:T(8,128)(2,1)S(1)}, u32[]{:S(2)}, u32[]{:S(2)}) collective-permute-start(bf16[256,128]{1,0:T(8,128)(2,1)S(1)} %get-tuple-element.88.refs_3_.refs_2_), channel_id=1, source_target_pairs={{0,8},{1,9},{2,10},{3,11},{4,20},{5,21},{6,22},{7,23},{8,0},{9,1},... | collective-permute-start | bytes 196616 | tf_op jit(solution)/shard_map/ppermute | solution.py:436
  48.9 1.5 %shard_map.124 = (f32[64,512]{1,0:T(8,128)}, f32[8,128]{1,0:T(8,128)S(1)}) custom-call(s32[19]{0:T(128)S(1)} %stack.67.refs_0_, f32[256,128]{1,0:T(8,128)S(1)} %get-tuple-element.87.refs_1_, bf16[512,256]{1,0:T(8,128)(2,1)S(1)} %copy-done.1, bf16[256,128]{1,0:T(8,128)(2,1)S(1)} %get-tuple-element.88.refs_3_.refs_2_), custom_call_target="tpu_custom_call" | custom-call | tf_op jit(solution)/shard_map/pallas_call | solution.py:48
  50.9 1.0 %collective-permute-done.11.refs_4_ = bf16[256,128]{1,0:T(8,128)(2,1)S(1)} collective-permute-done((bf16[256,128]{1,0:T(8,128)(2,1)S(1)}, bf16[256,128]{1,0:T(8,128)(2,1)S(1)}, u32[]{:S(2)}, u32[]{:S(2)}) %collective-permute-start.11) | collective-permute-done | bytes 65568 | tf_op jit(solution)/shard_map/ppermute | solution.py:436
  51.9 1.5 %shard_map.125 = (f32[512,256]{1,0:T(8,128)}, f32[1,512]{1,0:T(1,128)}, bf16[2,256,256]{2,1,0:T(8,128)(2,1)}, f32[2,256]{1,0:T(2,128)}) custom-call(s32[19]{0:T(128)S(1)} %stack.67.refs_0_, bf16[832,128]{1,0:T(8,128)(2,1)S(1)} %get-tuple-element.90.refs_1_, bf16[256,128]{1,0:T(8,128)(2,1)S(1)} %get-tuple-element.88.refs_3_.refs_2_, ...), custom_call_target="tpu_custom_call" | custom-call | tf_op jit(solution)/shard_map/pallas_call | solution.py:48
  (25 shorter events, 2.9 us)
Async XLA Ops:
  1.5 5.7 %copy-start = (bf16[2048,512]{1,0:T(8,128)(2,1)S(1)}, bf16[2048,512]{1,0:T(8,128)(2,1)}, u32[]{:S(2)}) copy-start(bf16[2048,512]{1,0:T(8,128)(2,1)} %refs_3_.1) | copy-start | bytes 6291460
  1.5 5.7 %copy-start.2 = (bf16[2,1024,256]{2,1,0:T(8,128)(2,1)S(1)}, bf16[2,1024,256]{2,1,0:T(8,128)(2,1)}, u32[]{:S(2)}) copy-start(bf16[2,1024,256]{2,1,0:T(8,128)(2,1)} %refs_5_.3) | copy-start | bytes 3145732
  1.5 5.7 %copy-start.3 = (bf16[768,512]{1,0:T(8,128)(2,1)S(1)}, bf16[768,512]{1,0:T(8,128)(2,1)}, u32[]{:S(2)}) copy-start(bf16[768,512]{1,0:T(8,128)(2,1)} %refs_1_.1) | copy-start | bytes 2359300
  1.5 5.7 %copy-start.4 = (s32[1,2,384]{2,1,0:T(2,128)S(1)}, s32[1,2,384]{2,1,0:T(2,128)}, u32[]{:S(2)}) copy-start(s32[1,2,384]{2,1,0:T(2,128)} %param.7) | copy-start | bytes 9220
  1.5 5.7 %copy-start.5 = (f32[512]{0:T(512)S(1)}, f32[512]{0:T(512)}, u32[]{:S(2)}) copy-start(f32[512]{0:T(512)} %param.9) | copy-start | bytes 6148
  2.1 7.2 %collective-permute-start = (bf16[2,512]{1,0:T(2,128)(2,1)S(1)}, bf16[2,512]{1,0:T(2,128)(2,1)S(1)}, u32[]{:S(2)}, u32[]{:S(2)}) collective-permute-start(bf16[2,512]{1,0:T(2,128)(2,1)S(1)} %shard_map.109), channel_id=1, source_target_pairs={{0,1},{1,2},{2,3},{4,5},{5,6},{6,7},{8,9},{9,10},{10,11},{12,13},{... | collective-permute-start | bytes 6152 | tf_op jit(solution)/shard_map/ppermute | solution.py:425
  7.2 2.1 %copy-start.1 = (bf16[512,256]{1,0:T(8,128)(2,1)S(1)}, bf16[512,256]{1,0:T(8,128)(2,1)}, u32[]{:S(2)}) copy-start(bf16[512,256]{1,0:T(8,128)(2,1)} %refs_2_.3) | copy-start | bytes 786436
  11.0 2.5 %collective-permute-start.1 = (bf16[3360,128]{1,0:T(8,128)(2,1)S(1)}, bf16[3360,128]{1,0:T(8,128)(2,1)S(1)}, u32[]{:S(2)}, u32[]{:S(2)}) collective-permute-start(bf16[3360,128]{1,0:T(8,128)(2,1)S(1)} %get-tuple-element.58.refs_6_), channel_id=1, source_target_pairs={{0,4},{1,5},{2,6},{3,7},{4,0},{5,1},{6,2},{7,3},{8,12},{9,13},{10,... | collective-permute-start | bytes 2580488 | tf_op jit(solution)/shard_map/ppermute | solution.py:436
  14.2 7.2 %collective-permute-start.3 = (bf16[1312,128]{1,0:T(8,128)(2,1)S(1)}, bf16[1312,128]{1,0:T(8,128)(2,1)S(1)}, u32[]{:S(2)}, u32[]{:S(2)}) collective-permute-start(bf16[1312,128]{1,0:T(8,128)(2,1)S(1)} %get-tuple-element.65.refs_4_), channel_id=1, source_target_pairs={{0,8},{1,9},{2,10},{3,11},{4,20},{5,21},{6,22},{7,23},{8,0},{9,1},... | collective-permute-start | bytes 1007624 | tf_op jit(solution)/shard_map/ppermute | solution.py:436
  16.9 9.3 %collective-permute-start.2 = (bf16[544,256]{1,0:T(8,128)(2,1)S(1)}, bf16[544,256]{1,0:T(8,128)(2,1)S(1)}, u32[]{:S(2)}, u32[]{:S(2)}) collective-permute-start(bf16[544,256]{1,0:T(8,128)(2,1)S(1)} %shard_map.114.refs_4_), channel_id=1, source_target_pairs={{0,1},{1,0},{2,3},{3,2},{4,6},{5,7},{6,4},{7,5},{8,9},{9,8},{10,11... | collective-permute-start | bytes 835592 | tf_op jit(solution)/shard_map/ppermute | solution.py:436
  22.0 6.6 %collective-permute-start.5 = (bf16[800,128]{1,0:T(8,128)(2,1)S(1)}, bf16[800,128]{1,0:T(8,128)(2,1)S(1)}, u32[]{:S(2)}, u32[]{:S(2)}) collective-permute-start(bf16[800,128]{1,0:T(8,128)(2,1)S(1)} %get-tuple-element.68.refs_4_), channel_id=1, source_target_pairs={{0,16},{1,17},{2,18},{3,19},{4,12},{5,13},{6,14},{7,15},{8,24},{9,... | collective-permute-start | bytes 614408 | tf_op jit(solution)/shard_map/ppermute | solution.py:436
  26.8 6.3 %collective-permute-start.4 = (bf16[272,256]{1,0:T(8,128)(2,1)S(1)}, bf16[272,256]{1,0:T(8,128)(2,1)S(1)}, u32[]{:S(2)}, u32[]{:S(2)}) collective-permute-start(bf16[272,256]{1,0:T(8,128)(2,1)S(1)} %get-tuple-element.69.refs_4_), channel_id=1, source_target_pairs={{0,2},{1,3},{2,0},{3,1},{4,5},{5,4},{6,7},{7,6},{8,10},{9,11},{10,... | collective-permute-start | bytes 417800 | tf_op jit(solution)/shard_map/ppermute | solution.py:436
  29.3 8.3 %collective-permute-start.7 = (bf16[544,128]{1,0:T(8,128)(2,1)S(1)}, bf16[544,128]{1,0:T(8,128)(2,1)S(1)}, u32[]{:S(2)}, u32[]{:S(2)}) collective-permute-start(bf16[544,128]{1,0:T(8,128)(2,1)S(1)} %get-tuple-element.74.refs_4_), channel_id=1, source_target_pairs={{0,2},{1,3},{2,0},{3,1},{4,5},{5,4},{6,7},{7,6},{8,10},{9,11},{10,... | collective-permute-start | bytes 417800 | tf_op jit(solution)/shard_map/ppermute | solution.py:436
  33.7 5.1 %collective-permute-start.6 = (bf16[272,256]{1,0:T(8,128)(2,1)S(1)}, bf16[272,256]{1,0:T(8,128)(2,1)S(1)}, u32[]{:S(2)}, u32[]{:S(2)}) collective-permute-start(bf16[272,256]{1,0:T(8,128)(2,1)S(1)} %get-tuple-element.76.refs_4_), channel_id=1, source_target_pairs={{0,8},{1,9},{2,10},{3,11},{4,20},{5,21},{6,22},{7,23},{8,0},{9,1},... | collective-permute-start | bytes 417800 | tf_op jit(solution)/shard_map/ppermute | solution.py:436
  38.2 7.9 %collective-permute-start.8 = (bf16[560,128]{1,0:T(8,128)(2,1)S(1)}, bf16[560,128]{1,0:T(8,128)(2,1)S(1)}, u32[]{:S(2)}, u32[]{:S(2)}) collective-permute-start(bf16[560,128]{1,0:T(8,128)(2,1)S(1)} %get-tuple-element.80.refs_3_), channel_id=1, source_target_pairs={{0,1},{1,0},{2,3},{3,2},{4,6},{5,7},{6,4},{7,5},{8,9},{9,8},{10,11... | collective-permute-start | bytes 430088 | tf_op jit(solution)/shard_map/ppermute | solution.py:436
  39.4 6.6 %collective-permute-start.9 = (bf16[272,256]{1,0:T(8,128)(2,1)S(1)}, bf16[272,256]{1,0:T(8,128)(2,1)S(1)}, u32[]{:S(2)}, u32[]{:S(2)}) collective-permute-start(bf16[272,256]{1,0:T(8,128)(2,1)S(1)} %get-tuple-element.81.refs_4_), channel_id=1, source_target_pairs={{0,16},{1,17},{2,18},{3,19},{4,12},{5,13},{6,14},{7,15},{8,24},{9,... | collective-permute-start | bytes 417800 | tf_op jit(solution)/shard_map/ppermute | solution.py:436
  46.7 5.2 %collective-permute-start.10 = (bf16[832,128]{1,0:T(8,128)(2,1)S(1)}, bf16[832,128]{1,0:T(8,128)(2,1)S(1)}, u32[]{:S(2)}, u32[]{:S(2)}) collective-permute-start(bf16[832,128]{1,0:T(8,128)(2,1)S(1)} %get-tuple-element.90.refs_1_), channel_id=1, source_target_pairs={{0,4},{1,5},{2,6},{3,7},{4,0},{5,1},{6,2},{7,3},{8,12},{9,13},{10,... | collective-permute-start | bytes 638984 | tf_op jit(solution)/shard_map/ppermute | solution.py:436
  46.8 4.1 %collective-permute-start.12 = (bf16[256,128]{1,0:T(8,128)(2,1)S(1)}, bf16[256,128]{1,0:T(8,128)(2,1)S(1)}, u32[]{:S(2)}, u32[]{:S(2)}) collective-permute-start(bf16[256,128]{1,0:T(8,128)(2,1)S(1)} %get-tuple-element.88.refs_3_.refs_2_), channel_id=1, source_target_pairs={{0,12},{1,13},{2,14},{3,15},{4,16},{5,17},{6,18},{7,19},{8,4},{9,5... | collective-permute-start | bytes 196616 | tf_op jit(solution)/shard_map/ppermute | solution.py:447
  47.3 4.6 %collective-permute-start.11 = (bf16[256,128]{1,0:T(8,128)(2,1)S(1)}, bf16[256,128]{1,0:T(8,128)(2,1)S(1)}, u32[]{:S(2)}, u32[]{:S(2)}) collective-permute-start(bf16[256,128]{1,0:T(8,128)(2,1)S(1)} %get-tuple-element.88.refs_3_.refs_2_), channel_id=1, source_target_pairs={{0,8},{1,9},{2,10},{3,11},{4,20},{5,21},{6,22},{7,23},{8,0},{9,1},... | collective-permute-start | bytes 196616 | tf_op jit(solution)/shard_map/ppermute | solution.py:436

commit v13 on v12

--- a/solution.py
+++ b/solution.py
@@ -329,7 +329,7 @@
     turned_first, turned_second = pltpu.roll(first, half, 1), pltpu.roll(second, half, 1)
     swapped_first = jnp.where(left, first, turned_second)
     swapped_second = jnp.where(left, turned_first, second)
-    return jnp.where(core == 1, swapped_first, first), jnp.where(core == 1, swapped_second, second)
+    return jnp.where(core == 0, swapped_first, first), jnp.where(core == 0, swapped_second, second)
 
 
 def step_kernel(halves, place, mixed, info, got, kept_a, kept_c, send, keep_a, keep_c):
@@ -470,8 +470,8 @@
     mixed = under == 1 and tm_bits == 2
     turned = mixed or under == 0 or under >= tm_bits
     up = [("tm", b) for b in range(tm_bits)]
-    paths[0] += up[::-1]
-    paths[1] += up if turned else up[::-1]
+    paths[0] += up if turned else up[::-1]
+    paths[1] += up[::-1]
     exchanges = list(zip([("dp", 0)] + paths[0], [("dp", 0)] + paths[1]))
     sums_up = [("dp", b) for b in range(1, dp_bits)]
     sums_exchanges = list(zip(up + sums_up, up[::-1] + sums_up[::-1]))
@@ -481,7 +481,7 @@
         bit = b + (tm_bits if axis == "dp" else 0)
         return bit - under if bit >= under else None
 
-    a_split = [piece_bit(steps[0]) is not None for steps in exchanges]
+    a_split = [piece_bit(steps[1]) is not None for steps in exchanges]
     c_split = [log2(pieces_c) - 1 - k if k < c_bits else None for k in range(len(exchanges))]
 
     def order_of(split, count):
@@ -525,8 +525,8 @@
     if turned and not mixed:
         start = ((at_dp * tm + at_tm) * owner_rows) & (LANES - 1)
     else:
-        start = on_core([(at_dp * tm + at_tm) * owner_rows, (at_tm >> 1) * owner_rows if mixed else (
-            at_dp * tm + at_tm) * owner_rows]) & (LANES - 1)
+        start = on_core([(at_tm >> 1) * owner_rows if mixed else (at_dp * tm + at_tm) * owner_rows,
+                         (at_dp * tm + at_tm) * owner_rows]) & (LANES - 1)
     at_start = len(bits)
     at_codes = at_start + 1
     at_pieces = at_codes + tm

time: 54.3 us -> 56.7 us (1.044); the launches traced: 53.4 us -> 56.4 us
  waiting for transfers between devices: 11.4 us -> 18.8 us
  starting transfers between devices: 21.8 us -> 17.4 us
    ppermute x11, waiting for transfers between devices: 10.9 us -> 18.7 us  [swapped(): return lax.ppermute(block, ('dp', 'tm'), route)]
    ppermute x11, starting transfers between devices: 16.3 us -> 12.3 us  [swapped(): return lax.ppermute(block, ('dp', 'tm'), route)]
  transfers between devices with their start and end apart: 13 -> 13, of which waited for: 9 -> 8; matrix products, arithmetic and copies ran while one was open for 0% -> 0% of each run, Pallas kernels for 25% -> 24%
where the time goes in v13:
time: 56.7 us; the launch traced here: 56.4 us
  waiting for transfers between devices  18.8 us (33%)
  Pallas kernels  18.5 us (33%)
  starting transfers between devices  17.4 us (31%)
  between operations  0.93 us (2%)
  local copies, waits for them, and re-layouts  0.84 us (1%)
    ppermute x11, waiting for transfers between devices, swapped(): return lax.ppermute(block, ('dp', 'tm'), route)  18.7 us
    pallas_call x17, Pallas kernels, call(): pl.pallas_call(kernel, out_shape=shown, in_specs=specs, out_specs=[pl.Blo...  18.5 us
    ppermute x11, starting transfers between devices, swapped(): return lax.ppermute(block, ('dp', 'tm'), route)  12.3 us
    ppermute x1, starting transfers between devices, shifted(): return lax.ppermute(block, axis, route)  5.06 us
  transfers between devices with their start and end apart: 13, of which 8 were waited for; matrix products, arithmetic and copies ran while one was open for 0% of the time, Pallas kernels for 24%

profile of v13, /device:TPU:0, one launch (start us, length us, event | category | flops | bytes accessed | tf_op | source)
XLA Modules:
  0.0 56.4 jit_solution(14021898077438028714)
XLA Ops:
  0.7 0.7 %slice.3.refs_1_ = bf16[2,512]{1,0:T(2,128)(2,1)S(1)} slice(bf16[768,512]{1,0:T(8,128)(2,1)} %refs_1_.1), slice={[766:768], [0:512]} | slice | bytes 4096 | tf_op jit(solution)/shard_map/slice | solution.py:537
  2.1 5.1 %collective-permute-start = (bf16[2,512]{1,0:T(2,128)(2,1)S(1)}, bf16[2,512]{1,0:T(2,128)(2,1)S(1)}, u32[]{:S(2)}, u32[]{:S(2)}) collective-permute-start(bf16[2,512]{1,0:T(2,128)(2,1)S(1)} %shard_map.109), channel_id=1, source_target_pairs={{0,1},{1,2},{2,3},{4,5},{5,6},{6,7},{8,9},{9,10},{10,11},{12,13},{... | collective-permute-start | bytes 6152 | tf_op jit(solution)/shard_map/ppermute | solution.py:425
  7.2 2.1 %shard_map.110 = (bf16[384,2048]{1,0:T(8,128)(2,1)S(1)}, f32[384,512]{1,0:T(8,128)S(1)}, bf16[2,384,256]{2,1,0:T(8,128)(2,1)S(1)}) custom-call(s32[19]{0:T(128)S(1)} %stack.67.refs_0_, bf16[768,512]{1,0:T(8,128)(2,1)S(1)} %copy-done.3, bf16[2048,512]{1,0:T(8,128)(2,1)S(1)} %copy-done, f32[1,512]{1,0:T(1,128)S(1)} %bitcast.20, s32[2,384]{1,0:T(2,128)S(1)} %bitcast.18, ...), custom_call_target="tpu_custom_call" | custom-call | tf_op jit(solution)/shard_map/pallas_call | solution.py:48
  9.3 1.7 %shard_map.111 = (bf16[384,2048]{1,0:T(8,128)(2,1)S(1)}, bf16[384,512]{1,0:T(8,128)(2,1)S(1)}, bf16[384,256]{1,0:T(8,128)(2,1)S(1)}, bf16[256,384]{1,0:T(8,128)(...) custom-call(s32[19]{0:T(128)S(1)} %stack.67.refs_0_, ...), custom_call_target="tpu_custom_call", output_to_operand_aliasing={{0}: (2, {})} | custom-call | tf_op jit(solution)/shard_map/pallas_call | solution.py:48
  11.1 1.2 %shard_map.112 = (f32[2048,128]{1,0:T(8,128)S(1)}, f32[512,128]{1,0:T(8,128)S(1)}, bf16[384,512]{1,0:T(8,128)(2,1)S(1)}, f32[32,128]{1,0:T(8,128)S(1)}, bf16[16,512]{1,0:T(8,128)(2,1)S(1)}) custom-call(s32[19]{0:T(128)S(1)} %stack.67.refs_0_, bf16[256,384]{1,0:T(8,128)(2,1)S(1)} %get-tuple-element.54.refs_1_, ...), custom_call_target="tpu_custom_call" | custom-call | tf_op jit(solution)/shard_map/pallas_call | solution.py:48
  12.3 1.2 %collective-permute-done.1.refs_1_ = bf16[3360,128]{1,0:T(8,128)(2,1)S(1)} collective-permute-done((bf16[3360,128]{1,0:T(8,128)(2,1)S(1)}, bf16[3360,128]{1,0:T(8,128)(2,1)S(1)}, u32[]{:S(2)}, u32[]{:S(2)}) %collective-permute-start.1) | collective-permute-done | bytes 860192 | tf_op jit(solution)/shard_map/ppermute | solution.py:436
  13.5 0.7 %shard_map.113 = (bf16[1312,128]{1,0:T(8,128)(2,1)S(1)}, f32[1024,128]{1,0:T(8,128)S(1)}, f32[288,128]{1,0:T(8,128)S(1)}) custom-call(s32[19]{0:T(128)S(1)} %stack.67.refs_0_, bf16[3360,128]{1,0:T(8,128)(2,1)S(1)} %collective-permute-done.1.refs_1_, f32[2048,128]{1,0:T(8,128)S(1)} %get-tuple-element.62.refs_2_, f32[512,128]{1,0:T(8,128)S(1)} %get-tuple-element.63.refs_3_, ...), custom_call_target="tpu_custom_call" | custom-call | tf_op jit(solution)/shard_map/pallas_call | solution.py:48
  14.2 1.6 %collective-permute-start.3 = (bf16[1312,128]{1,0:T(8,128)(2,1)S(1)}, bf16[1312,128]{1,0:T(8,128)(2,1)S(1)}, u32[]{:S(2)}, u32[]{:S(2)}) collective-permute-start(bf16[1312,128]{1,0:T(8,128)(2,1)S(1)} %get-tuple-element.65.refs_4_), channel_id=1, source_target_pairs={{0,8},{1,9},{2,10},{3,11},{4,20},{5,21},{6,22},{7,23},{8,0},{9,1},... | collective-permute-start | bytes 1007624 | tf_op jit(solution)/shard_map/ppermute | solution.py:436
  15.7 1.2 %shard_map.114.refs_4_ = bf16[544,256]{1,0:T(8,128)(2,1)S(1)} custom-call(s32[19]{0:T(128)S(1)} %stack.67.refs_0_, bf16[3360,128]{1,0:T(8,128)(2,1)S(1)} %collective-permute-done.1.refs_1_, bf16[400,256]{1,0:T(8,128)(2,1)S(1)} %get-tuple-element.60.refs_2_, bf16[16,512]{1,0:T(8,128)(2,1)S(1)} %get-tuple-element.61.refs_3_, ...), custom_call_target="tpu_custom_call" | custom-call | tf_op jit(solution)/shard_map/pallas_call | solution.py:48
  16.9 1.6 %collective-permute-start.2 = (bf16[544,256]{1,0:T(8,128)(2,1)S(1)}, bf16[544,256]{1,0:T(8,128)(2,1)S(1)}, u32[]{:S(2)}, u32[]{:S(2)}) collective-permute-start(bf16[544,256]{1,0:T(8,128)(2,1)S(1)} %shard_map.114.refs_4_), channel_id=1, source_target_pairs={{0,1},{1,0},{2,3},{3,2},{4,6},{5,7},{6,4},{7,5},{8,9},{9,8},{10,11... | collective-permute-start | bytes 835592 | tf_op jit(solution)/shard_map/ppermute | solution.py:436
  18.5 1.2 %shard_map.115.refs_4_.refs_2_ = f32[544,256]{1,0:T(8,128)S(1)} custom-call(s32[19]{0:T(128)S(1)} %stack.67.refs_0_, bf16[3360,128]{1,0:T(8,128)(2,1)S(1)} %collective-permute-done.1.refs_1_, bf16[400,256]{1,0:T(8,128)(2,1)S(1)} %get-tuple-element.60.refs_2_, bf16[16,512]{1,0:T(8,128)(2,1)S(1)} %get-tuple-element.61.refs_3_, ...), custom_call_target="tpu_custom_call" | custom-call | tf_op jit(solution)/shard_map/pallas_call | solution.py:48
  19.7 1.7 %collective-permute-done.3.refs_1_ = bf16[1312,128]{1,0:T(8,128)(2,1)S(1)} collective-permute-done((bf16[1312,128]{1,0:T(8,128)(2,1)S(1)}, bf16[1312,128]{1,0:T(8,128)(2,1)S(1)}, u32[]{:S(2)}, u32[]{:S(2)}) %collective-permute-start.3) | collective-permute-done | bytes 335904 | tf_op jit(solution)/shard_map/ppermute | solution.py:436
  21.4 0.6 %shard_map.116 = (bf16[800,128]{1,0:T(8,128)(2,1)S(1)}, f32[512,128]{1,0:T(8,128)S(1)}, f32[288,128]{1,0:T(8,128)S(1)}) custom-call(s32[19]{0:T(128)S(1)} %stack.67.refs_0_, bf16[1312,128]{1,0:T(8,128)(2,1)S(1)} %collective-permute-done.3.refs_1_, f32[1024,128]{1,0:T(8,128)S(1)} %get-tuple-element.66.refs_2_, f32[288,128]{1,0:T(8,128)S(1)} %get-tuple-element.67.refs_3_, ...), custom_call_target="tpu_custom_call" | custom-call | tf_op jit(solution)/shard_map/pallas_call | solution.py:48
  22.0 1.6 %collective-permute-start.5 = (bf16[800,128]{1,0:T(8,128)(2,1)S(1)}, bf16[800,128]{1,0:T(8,128)(2,1)S(1)}, u32[]{:S(2)}, u32[]{:S(2)}) collective-permute-start(bf16[800,128]{1,0:T(8,128)(2,1)S(1)} %get-tuple-element.68.refs_4_), channel_id=1, source_target_pairs={{0,16},{1,17},{2,18},{3,19},{4,12},{5,13},{6,14},{7,15},{8,24},{9,... | collective-permute-start | bytes 614408 | tf_op jit(solution)/shard_map/ppermute | solution.py:436
  23.6 2.6 %collective-permute-done.2.refs_1_ = bf16[544,256]{1,0:T(8,128)(2,1)S(1)} collective-permute-done((bf16[544,256]{1,0:T(8,128)(2,1)S(1)}, bf16[544,256]{1,0:T(8,128)(2,1)S(1)}, u32[]{:S(2)}, u32[]{:S(2)}) %collective-permute-start.2) | collective-permute-done | bytes 278560 | tf_op jit(solution)/shard_map/ppermute | solution.py:436
  26.2 0.6 %shard_map.117 = (bf16[272,256]{1,0:T(8,128)(2,1)S(1)}, f32[272,256]{1,0:T(8,128)S(1)}, bf16[16,512]{1,0:T(8,128)(2,1)S(1)}) custom-call(s32[19]{0:T(128)S(1)} %stack.67.refs_0_, bf16[544,256]{1,0:T(8,128)(2,1)S(1)} %collective-permute-done.2.refs_1_, f32[544,256]{1,0:T(8,128)S(1)} %shard_map.115.refs_4_.refs_2_, ...), custom_call_target="tpu_custom_call" | custom-call | tf_op jit(solution)/shard_map/pallas_call | solution.py:48
  26.8 1.8 %collective-permute-start.4 = (bf16[272,256]{1,0:T(8,128)(2,1)S(1)}, bf16[272,256]{1,0:T(8,128)(2,1)S(1)}, u32[]{:S(2)}, u32[]{:S(2)}) collective-permute-start(bf16[272,256]{1,0:T(8,128)(2,1)S(1)} %get-tuple-element.69.refs_4_), channel_id=1, source_target_pairs={{0,2},{1,3},{2,0},{3,1},{4,5},{5,4},{6,7},{7,6},{8,10},{9,11},{10,... | collective-permute-start | bytes 417800 | tf_op jit(solution)/shard_map/ppermute | solution.py:436
  28.6 0.7 %shard_map.118 = (bf16[544,128]{1,0:T(8,128)(2,1)S(1)}, f32[256,128]{1,0:T(8,128)S(1)}, f32[288,128]{1,0:T(8,128)S(1)}) custom-call(s32[19]{0:T(128)S(1)} %stack.67.refs_0_, bf16[800,128]{1,0:T(8,128)(2,1)S(1)} %collective-permute-done.5.refs_1_, f32[512,128]{1,0:T(8,128)S(1)} %get-tuple-element.72.refs_2_, f32[288,128]{1,0:T(8,128)S(1)} %get-tuple-element.73.refs_3_, ...), custom_call_target="tpu_custom_call" | custom-call | tf_op jit(solution)/shard_map/pallas_call | solution.py:48
  29.3 2.5 %collective-permute-start.7 = (bf16[544,128]{1,0:T(8,128)(2,1)S(1)}, bf16[544,128]{1,0:T(8,128)(2,1)S(1)}, u32[]{:S(2)}, u32[]{:S(2)}) collective-permute-start(bf16[544,128]{1,0:T(8,128)(2,1)S(1)} %get-tuple-element.74.refs_4_), channel_id=1, source_target_pairs={{0,1},{1,0},{2,3},{3,2},{4,6},{5,7},{6,4},{7,5},{8,9},{9,8},{10,11... | collective-permute-start | bytes 417800 | tf_op jit(solution)/shard_map/ppermute | solution.py:436
  31.8 4.7 %collective-permute-done.4.refs_1_ = bf16[272,256]{1,0:T(8,128)(2,1)S(1)} collective-permute-done((bf16[272,256]{1,0:T(8,128)(2,1)S(1)}, bf16[272,256]{1,0:T(8,128)(2,1)S(1)}, u32[]{:S(2)}, u32[]{:S(2)}) %collective-permute-start.4) | collective-permute-done | bytes 139296 | tf_op jit(solution)/shard_map/ppermute | solution.py:436
  36.5 0.6 %shard_map.119 = (bf16[272,256]{1,0:T(8,128)(2,1)S(1)}, f32[272,256]{1,0:T(8,128)S(1)}, bf16[16,512]{1,0:T(8,128)(2,1)S(1)}) custom-call(s32[19]{0:T(128)S(1)} %stack.67.refs_0_, bf16[272,256]{1,0:T(8,128)(2,1)S(1)} %collective-permute-done.4.refs_1_, f32[272,256]{1,0:T(8,128)S(1)} %get-tuple-element.70.refs_2_, ...), custom_call_target="tpu_custom_call" | custom-call | tf_op jit(solution)/shard_map/pallas_call | solution.py:48
  37.1 0.6 %shard_map.120 = (bf16[560,128]{1,0:T(8,128)(2,1)S(1)}, f32[256,128]{1,0:T(8,128)S(1)}, f32[288,128]{1,0:T(8,128)S(1)}) custom-call(s32[19]{0:T(128)S(1)} %stack.67.refs_0_, bf16[544,128]{1,0:T(8,128)(2,1)S(1)} %collective-permute-done.7.refs_1_, f32[256,128]{1,0:T(8,128)S(1)} %get-tuple-element.78.refs_2_, f32[288,128]{1,0:T(8,128)S(1)} %get-tuple-element.79.refs_3_, ...), custom_call_target="tpu_custom_call" | custom-call | tf_op jit(solution)/shard_map/pallas_call | solution.py:48
  37.7 0.9 %collective-permute-start.8 = (bf16[560,128]{1,0:T(8,128)(2,1)S(1)}, bf16[560,128]{1,0:T(8,128)(2,1)S(1)}, u32[]{:S(2)}, u32[]{:S(2)}) collective-permute-start(bf16[560,128]{1,0:T(8,128)(2,1)S(1)} %get-tuple-element.80.refs_3_), channel_id=1, source_target_pairs={{0,2},{1,3},{2,0},{3,1},{4,5},{5,4},{6,7},{7,6},{8,10},{9,11},{10,... | collective-permute-start | bytes 430088 | tf_op jit(solution)/shard_map/ppermute | solution.py:436
  38.6 4.8 %collective-permute-done.6.refs_1_ = bf16[272,256]{1,0:T(8,128)(2,1)S(1)} collective-permute-done((bf16[272,256]{1,0:T(8,128)(2,1)S(1)}, bf16[272,256]{1,0:T(8,128)(2,1)S(1)}, u32[]{:S(2)}, u32[]{:S(2)}) %collective-permute-start.6) | collective-permute-done | bytes 139296 | tf_op jit(solution)/shard_map/ppermute | solution.py:436
  43.4 0.6 %shard_map.121 = (bf16[272,256]{1,0:T(8,128)(2,1)S(1)}, f32[272,256]{1,0:T(8,128)S(1)}) custom-call(s32[19]{0:T(128)S(1)} %stack.67.refs_0_, bf16[272,256]{1,0:T(8,128)(2,1)S(1)} %collective-permute-done.6.refs_1_, f32[272,256]{1,0:T(8,128)S(1)} %get-tuple-element.77.refs_2_, bf16[560,128]{1,0:T(8,128)(2,1)S(1)} %get-tuple-element.80.refs_3_), custom_call_target="tpu_custom_call" | custom-call | tf_op jit(solution)/shard_map/pallas_call | solution.py:48
  44.1 2.6 %shard_map.122 = (bf16[768,512]{1,0:T(8,128)(2,1)}, f32[8,128]{1,0:T(8,128)S(1)}) custom-call(s32[19]{0:T(128)S(1)} %stack.67.refs_0_, bf16[384,512]{1,0:T(8,128)(2,1)S(1)} %get-tuple-element.59.refs_1_, bf16[16,512]{1,0:T(8,128)(2,1)S(1)} %get-tuple-element.75.refs_2_, bf16[2048,512]{1,0:T(8,128)(2,1)S(1)} %copy-done, ...), custom_call_target="tpu_custom_call" | custom-call | tf_op jit(solution)/shard_map/pallas_call | solution.py:48
  46.6 2.5 %collective-permute-done.9.refs_4_ = bf16[272,256]{1,0:T(8,128)(2,1)S(1)} collective-permute-done((bf16[272,256]{1,0:T(8,128)(2,1)S(1)}, bf16[272,256]{1,0:T(8,128)(2,1)S(1)}, u32[]{:S(2)}, u32[]{:S(2)}) %collective-permute-start.9) | collective-permute-done | bytes 139296 | tf_op jit(solution)/shard_map/ppermute | solution.py:436
  49.1 0.7 %shard_map.123 = (f32[256,128]{1,0:T(8,128)S(1)}, bf16[256,128]{1,0:T(8,128)(2,1)S(1)}, bf16[832,128]{1,0:T(8,128)(2,1)S(1)}) custom-call(s32[19]{0:T(128)S(1)} %stack.67.refs_0_, bf16[560,128]{1,0:T(8,128)(2,1)S(1)} %collective-permute-done.8.refs_1_, f32[256,128]{1,0:T(8,128)S(1)} %get-tuple-element.83.refs_2_, f32[288,128]{1,0:T(8,128)S(1)} %get-tuple-element.84.refs_3_, ...), custom_call_target="tpu_custom_call" | custom-call | tf_op jit(solution)/shard_map/pallas_call | solution.py:48
  49.9 2.1 %collective-permute-start.11 = (bf16[256,128]{1,0:T(8,128)(2,1)S(1)}, bf16[256,128]{1,0:T(8,128)(2,1)S(1)}, u32[]{:S(2)}, u32[]{:S(2)}) collective-permute-start(bf16[256,128]{1,0:T(8,128)(2,1)S(1)} %get-tuple-element.88.refs_3_.refs_2_), channel_id=1, source_target_pairs={{0,8},{1,9},{2,10},{3,11},{4,20},{5,21},{6,22},{7,23},{8,0},{9,1},... | collective-permute-start | bytes 196616 | tf_op jit(solution)/shard_map/ppermute | solution.py:436
  52.0 1.5 %shard_map.124 = (f32[64,512]{1,0:T(8,128)}, f32[8,128]{1,0:T(8,128)S(1)}) custom-call(s32[19]{0:T(128)S(1)} %stack.67.refs_0_, f32[256,128]{1,0:T(8,128)S(1)} %get-tuple-element.87.refs_1_, bf16[512,256]{1,0:T(8,128)(2,1)S(1)} %copy-done.1, bf16[256,128]{1,0:T(8,128)(2,1)S(1)} %get-tuple-element.88.refs_3_.refs_2_), custom_call_target="tpu_custom_call" | custom-call | tf_op jit(solution)/shard_map/pallas_call | solution.py:48
  53.6 1.3 %collective-permute-done.11.refs_4_ = bf16[256,128]{1,0:T(8,128)(2,1)S(1)} collective-permute-done((bf16[256,128]{1,0:T(8,128)(2,1)S(1)}, bf16[256,128]{1,0:T(8,128)(2,1)S(1)}, u32[]{:S(2)}, u32[]{:S(2)}) %collective-permute-start.11) | collective-permute-done | bytes 65568 | tf_op jit(solution)/shard_map/ppermute | solution.py:436
  54.9 1.5 %shard_map.125 = (f32[512,256]{1,0:T(8,128)}, f32[1,512]{1,0:T(1,128)}, bf16[2,256,256]{2,1,0:T(8,128)(2,1)}, f32[2,256]{1,0:T(2,128)}) custom-call(s32[19]{0:T(128)S(1)} %stack.67.refs_0_, bf16[832,128]{1,0:T(8,128)(2,1)S(1)} %get-tuple-element.90.refs_1_, bf16[256,128]{1,0:T(8,128)(2,1)S(1)} %get-tuple-element.88.refs_3_.refs_2_, ...), custom_call_target="tpu_custom_call" | custom-call | tf_op jit(solution)/shard_map/pallas_call | solution.py:48
  (25 shorter events, 1.1 us)
Async XLA Ops:
  1.5 5.7 %copy-start = (bf16[2048,512]{1,0:T(8,128)(2,1)S(1)}, bf16[2048,512]{1,0:T(8,128)(2,1)}, u32[]{:S(2)}) copy-start(bf16[2048,512]{1,0:T(8,128)(2,1)} %refs_3_.1) | copy-start | bytes 6291460
  1.5 5.7 %copy-start.2 = (bf16[2,1024,256]{2,1,0:T(8,128)(2,1)S(1)}, bf16[2,1024,256]{2,1,0:T(8,128)(2,1)}, u32[]{:S(2)}) copy-start(bf16[2,1024,256]{2,1,0:T(8,128)(2,1)} %refs_5_.3) | copy-start | bytes 3145732
  1.5 5.7 %copy-start.3 = (bf16[768,512]{1,0:T(8,128)(2,1)S(1)}, bf16[768,512]{1,0:T(8,128)(2,1)}, u32[]{:S(2)}) copy-start(bf16[768,512]{1,0:T(8,128)(2,1)} %refs_1_.1) | copy-start | bytes 2359300
  1.5 5.7 %copy-start.4 = (s32[1,2,384]{2,1,0:T(2,128)S(1)}, s32[1,2,384]{2,1,0:T(2,128)}, u32[]{:S(2)}) copy-start(s32[1,2,384]{2,1,0:T(2,128)} %param.7) | copy-start | bytes 9220
  1.5 5.7 %copy-start.5 = (f32[512]{0:T(512)S(1)}, f32[512]{0:T(512)}, u32[]{:S(2)}) copy-start(f32[512]{0:T(512)} %param.9) | copy-start | bytes 6148
  2.1 7.2 %collective-permute-start = (bf16[2,512]{1,0:T(2,128)(2,1)S(1)}, bf16[2,512]{1,0:T(2,128)(2,1)S(1)}, u32[]{:S(2)}, u32[]{:S(2)}) collective-permute-start(bf16[2,512]{1,0:T(2,128)(2,1)S(1)} %shard_map.109), channel_id=1, source_target_pairs={{0,1},{1,2},{2,3},{4,5},{5,6},{6,7},{8,9},{9,10},{10,11},{12,13},{... | collective-permute-start | bytes 6152 | tf_op jit(solution)/shard_map/ppermute | solution.py:425
  7.2 2.1 %copy-start.1 = (bf16[512,256]{1,0:T(8,128)(2,1)S(1)}, bf16[512,256]{1,0:T(8,128)(2,1)}, u32[]{:S(2)}) copy-start(bf16[512,256]{1,0:T(8,128)(2,1)} %refs_2_.3) | copy-start | bytes 786436
  11.0 2.5 %collective-permute-start.1 = (bf16[3360,128]{1,0:T(8,128)(2,1)S(1)}, bf16[3360,128]{1,0:T(8,128)(2,1)S(1)}, u32[]{:S(2)}, u32[]{:S(2)}) collective-permute-start(bf16[3360,128]{1,0:T(8,128)(2,1)S(1)} %get-tuple-element.58.refs_6_), channel_id=1, source_target_pairs={{0,4},{1,5},{2,6},{3,7},{4,0},{5,1},{6,2},{7,3},{8,12},{9,13},{10,... | collective-permute-start | bytes 2580488 | tf_op jit(solution)/shard_map/ppermute | solution.py:436
  14.2 7.2 %collective-permute-start.3 = (bf16[1312,128]{1,0:T(8,128)(2,1)S(1)}, bf16[1312,128]{1,0:T(8,128)(2,1)S(1)}, u32[]{:S(2)}, u32[]{:S(2)}) collective-permute-start(bf16[1312,128]{1,0:T(8,128)(2,1)S(1)} %get-tuple-element.65.refs_4_), channel_id=1, source_target_pairs={{0,8},{1,9},{2,10},{3,11},{4,20},{5,21},{6,22},{7,23},{8,0},{9,1},... | collective-permute-start | bytes 1007624 | tf_op jit(solution)/shard_map/ppermute | solution.py:436
  16.9 9.3 %collective-permute-start.2 = (bf16[544,256]{1,0:T(8,128)(2,1)S(1)}, bf16[544,256]{1,0:T(8,128)(2,1)S(1)}, u32[]{:S(2)}, u32[]{:S(2)}) collective-permute-start(bf16[544,256]{1,0:T(8,128)(2,1)S(1)} %shard_map.114.refs_4_), channel_id=1, source_target_pairs={{0,1},{1,0},{2,3},{3,2},{4,6},{5,7},{6,4},{7,5},{8,9},{9,8},{10,11... | collective-permute-start | bytes 835592 | tf_op jit(solution)/shard_map/ppermute | solution.py:436
  22.0 6.6 %collective-permute-start.5 = (bf16[800,128]{1,0:T(8,128)(2,1)S(1)}, bf16[800,128]{1,0:T(8,128)(2,1)S(1)}, u32[]{:S(2)}, u32[]{:S(2)}) collective-permute-start(bf16[800,128]{1,0:T(8,128)(2,1)S(1)} %get-tuple-element.68.refs_4_), channel_id=1, source_target_pairs={{0,16},{1,17},{2,18},{3,19},{4,12},{5,13},{6,14},{7,15},{8,24},{9,... | collective-permute-start | bytes 614408 | tf_op jit(solution)/shard_map/ppermute | solution.py:436
  26.8 9.7 %collective-permute-start.4 = (bf16[272,256]{1,0:T(8,128)(2,1)S(1)}, bf16[272,256]{1,0:T(8,128)(2,1)S(1)}, u32[]{:S(2)}, u32[]{:S(2)}) collective-permute-start(bf16[272,256]{1,0:T(8,128)(2,1)S(1)} %get-tuple-element.69.refs_4_), channel_id=1, source_target_pairs={{0,2},{1,3},{2,0},{3,1},{4,5},{5,4},{6,7},{7,6},{8,10},{9,11},{10,... | collective-permute-start | bytes 417800 | tf_op jit(solution)/shard_map/ppermute | solution.py:436
  29.3 7.8 %collective-permute-start.7 = (bf16[544,128]{1,0:T(8,128)(2,1)S(1)}, bf16[544,128]{1,0:T(8,128)(2,1)S(1)}, u32[]{:S(2)}, u32[]{:S(2)}) collective-permute-start(bf16[544,128]{1,0:T(8,128)(2,1)S(1)} %get-tuple-element.74.refs_4_), channel_id=1, source_target_pairs={{0,1},{1,0},{2,3},{3,2},{4,6},{5,7},{6,4},{7,5},{8,9},{9,8},{10,11... | collective-permute-start | bytes 417800 | tf_op jit(solution)/shard_map/ppermute | solution.py:436
  37.1 6.3 %collective-permute-start.6 = (bf16[272,256]{1,0:T(8,128)(2,1)S(1)}, bf16[272,256]{1,0:T(8,128)(2,1)S(1)}, u32[]{:S(2)}, u32[]{:S(2)}) collective-permute-start(bf16[272,256]{1,0:T(8,128)(2,1)S(1)} %get-tuple-element.76.refs_4_), channel_id=1, source_target_pairs={{0,8},{1,9},{2,10},{3,11},{4,20},{5,21},{6,22},{7,23},{8,0},{9,1},... | collective-permute-start | bytes 417800 | tf_op jit(solution)/shard_map/ppermute | solution.py:436
  37.7 11.4 %collective-permute-start.8 = (bf16[560,128]{1,0:T(8,128)(2,1)S(1)}, bf16[560,128]{1,0:T(8,128)(2,1)S(1)}, u32[]{:S(2)}, u32[]{:S(2)}) collective-permute-start(bf16[560,128]{1,0:T(8,128)(2,1)S(1)} %get-tuple-element.80.refs_3_), channel_id=1, source_target_pairs={{0,2},{1,3},{2,0},{3,1},{4,5},{5,4},{6,7},{7,6},{8,10},{9,11},{10,... | collective-permute-start | bytes 430088 | tf_op jit(solution)/shard_map/ppermute | solution.py:436
  44.0 5.1 %collective-permute-start.9 = (bf16[272,256]{1,0:T(8,128)(2,1)S(1)}, bf16[272,256]{1,0:T(8,128)(2,1)S(1)}, u32[]{:S(2)}, u32[]{:S(2)}) collective-permute-start(bf16[272,256]{1,0:T(8,128)(2,1)S(1)} %get-tuple-element.81.refs_4_), channel_id=1, source_target_pairs={{0,16},{1,17},{2,18},{3,19},{4,12},{5,13},{6,14},{7,15},{8,24},{9,... | collective-permute-start | bytes 417800 | tf_op jit(solution)/shard_map/ppermute | solution.py:436
  49.8 5.2 %collective-permute-start.10 = (bf16[832,128]{1,0:T(8,128)(2,1)S(1)}, bf16[832,128]{1,0:T(8,128)(2,1)S(1)}, u32[]{:S(2)}, u32[]{:S(2)}) collective-permute-start(bf16[832,128]{1,0:T(8,128)(2,1)S(1)} %get-tuple-element.90.refs_1_), channel_id=1, source_target_pairs={{0,4},{1,5},{2,6},{3,7},{4,0},{5,1},{6,2},{7,3},{8,12},{9,13},{10,... | collective-permute-start | bytes 638984 | tf_op jit(solution)/shard_map/ppermute | solution.py:436
  49.9 3.7 %collective-permute-start.12 = (bf16[256,128]{1,0:T(8,128)(2,1)S(1)}, bf16[256,128]{1,0:T(8,128)(2,1)S(1)}, u32[]{:S(2)}, u32[]{:S(2)}) collective-permute-start(bf16[256,128]{1,0:T(8,128)(2,1)S(1)} %get-tuple-element.88.refs_3_.refs_2_), channel_id=1, source_target_pairs={{0,12},{1,13},{2,14},{3,15},{4,16},{5,17},{6,18},{7,19},{8,4},{9,5... | collective-permute-start | bytes 196616 | tf_op jit(solution)/shard_map/ppermute | solution.py:447
  49.9 5.0 %collective-permute-start.11 = (bf16[256,128]{1,0:T(8,128)(2,1)S(1)}, bf16[256,128]{1,0:T(8,128)(2,1)S(1)}, u32[]{:S(2)}, u32[]{:S(2)}) collective-permute-start(bf16[256,128]{1,0:T(8,128)(2,1)S(1)} %get-tuple-element.88.refs_3_.refs_2_), channel_id=1, source_target_pairs={{0,8},{1,9},{2,10},{3,11},{4,20},{5,21},{6,22},{7,23},{8,0},{9,1},... | collective-permute-start | bytes 196616 | tf_op jit(solution)/shard_map/ppermute | solution.py:436

commit v14 on v12

--- a/solution.py
+++ b/solution.py
@@ -81,24 +81,6 @@
     out[...] = rows[...]
 
 
-def local_kernel(info, feats, weight, bias, codes, books, unfold, conv, chosen, wide):
-    rows, channels = feats.shape
-    frames = rows // 2
-    for j in range(channels // LANES):
-        wide[j, 0:8, :] = jnp.zeros((8, LANES), F32)
-        wide[j, 8:, :] = feats[:, j * LANES:(j + 1) * LANES].astype(F32)
-        for tap in range(4):
-            start = tap * channels + j * LANES
-            unfold[:, start:start + LANES] = wide[j, pl.ds(6 + tap, frames, stride=2), :].astype(BF16)
-    conv[...] = nn(unfold[...], weight[...]) + bias[...]
-    levels = books.shape[0]
-    padded = jnp.concatenate([codes[...].astype(F32), jnp.zeros((8 - levels, frames), F32)], 0)
-    tall = jnp.transpose(padded).astype(jnp.int32)
-    for level in range(levels):
-        matches = one_hot(tall[:, level:level + 1], 1, 0, books.shape[1])
-        chosen[level] = nn(matches, books[level]).astype(BF16)
-
-
 def walk(orders, halved, count):
     start = 1 if halved else 0
     shown = count // 2 if halved else count
@@ -148,9 +130,59 @@
     return (parts[0] * 256.0 + parts[1]).astype(jnp.int32)
 
 
-def forward_kernel(plan, info, halo, unfold_in, conv, chosen, weight, proj, codes,
-                   unfold, hidden, latent_grad, flipped, own, send):
-    frames, width = unfold.shape
+def residuals(hidden, proj, chosen):
+    latent = nn(hidden, proj)
+    once = latent - chosen[0].astype(F32)
+    total = once + (once - chosen[1].astype(F32))
+    return latent, once, total.astype(BF16)
+
+
+def put_columns(out, at, rows, block):
+    for j in range(block.shape[1] // LANES):
+        out[at + j * rows:at + j * rows + block.shape[0], :] = block[:, j * LANES:(j + 1) * LANES]
+
+
+def local_kernel(plan, info, feats, weight, bias, codes, books, proj,
+                 unfold, hidden, latent_grad, flipped, own, send, first, part, wide, chosen):
+    rows, channels = feats.shape
+    frames = rows // 2
+    dz = proj.shape[1]
+    for j in range(channels // LANES):
+        wide[j, 0:8, :] = jnp.zeros((8, LANES), F32)
+        wide[j, 8:, :] = feats[:, j * LANES:(j + 1) * LANES].astype(F32)
+        for tap in range(4):
+            start = tap * channels + j * LANES
+            unfold[:, start:start + LANES] = wide[j, pl.ds(6 + tap, frames, stride=2), :].astype(BF16)
+    conv = nn(unfold[...], weight[...]) + bias[...]
+    first[...] = conv[0:16, :]
+    hidden[...] = conv.astype(BF16)
+    levels = books.shape[0]
+    padded = jnp.concatenate([codes[...].astype(F32), jnp.zeros((8 - levels, frames), F32)], 0)
+    tall = jnp.transpose(padded).astype(jnp.int32)
+    for level in range(levels):
+        matches = one_hot(tall[:, level:level + 1], 1, 0, books.shape[1])
+        chosen[level] = nn(matches, books[level]).astype(BF16)
+    latent, once, grad = residuals(hidden[...], proj[...], chosen)
+    latent_grad[...] = grad
+    row = lax.broadcasted_iota(jnp.int32, grad.shape, 0)
+    flipped[...] = jnp.transpose(jnp.where(row == 0, 0.0, grad.astype(F32))).astype(BF16)
+    bit = info[0]
+    at = correlate(flipped[...], (unfold, hidden), plan, 1 - bit, 1 - bit, part)
+    rows_b = own.shape[0]
+    code_rows = rows_b - frames
+    digits = [code_digits(codes[level:level + 1, :], dz, code_rows) for level in range(2)]
+    own[0:frames, :] = jnp.where(bit == 1, once, latent).astype(BF16)
+    own[frames:, :] = jnp.where(bit == 1, digits[1], digits[0])
+    put_columns(send, at, rows_b, jnp.where(bit == 1, latent, once).astype(BF16))
+    put_columns(send, at + frames, rows_b, jnp.where(bit == 1, digits[0], digits[1]))
+    for level in range(levels):
+        part[at + level * 16 * (dz // LANES):at + (level + 1) * 16 * (dz // LANES), :] = jnp.concatenate(
+            [chosen[level, 0:16, j * LANES:(j + 1) * LANES].astype(F32) for j in range(dz // LANES)], 0)
+
+
+def frame_kernel(plan, info, halo, first, part, weight, proj, unfold_in, hidden_in, grad_in, flipped_in, own_in, send_in,
+                 unfold, hidden, latent_grad, flipped, own, send):
+    width = unfold.shape[1]
     half = width // 2
     dz = proj.shape[1]
     row = lax.broadcasted_iota(jnp.int32, (16, half), 0)
@@ -158,24 +190,34 @@
     head = jnp.where(row == 0, jnp.broadcast_to(left, (16, half)), 0.0)
     unfold[0:16, 0:half] = (unfold_in[0:16, 0:half].astype(F32) + head).astype(BF16)
     fix = nn(head.astype(BF16), weight[0:half, :])
-    hidden[...] = jnp.concatenate([conv[0:16, :] + fix, conv[16:, :]], 0).astype(BF16)
-    latent = nn(hidden[...], proj[...])
-    once = latent - chosen[0].astype(F32)
-    total = once + (once - chosen[1].astype(F32))
-    latent_grad[...] = total.astype(BF16)
-    flipped[...] = jnp.transpose(latent_grad[...].astype(F32)).astype(BF16)
+    hidden[0:16, :] = (first[...] + fix).astype(BF16)
+    top = hidden[0:16, :]
+    pieces = part.shape[0] - 32 * (dz // LANES)
+    chosen = []
+    for level in range(2):
+        at = pieces + level * 16 * (dz // LANES)
+        chosen.append(jnp.concatenate([part[at + j * 16:at + (j + 1) * 16, :] for j in range(dz // LANES)], 1))
+    latent, once, grad = residuals(top, proj[...], chosen)
+    latent_grad[0:16, :] = grad
+    flipped[:, 0:LANES] = jnp.transpose(latent_grad[0:LANES, :].astype(F32)).astype(BF16)
+    column = flipped[:, 0:LANES].astype(F32)[:, 0:1]
     bit = info[0]
-    at = correlate(flipped[...], (unfold, hidden), plan, 1 - bit, 1 - bit, send)
-    code_rows = own.shape[0] - frames
-    digits = [code_digits(codes[level:level + 1], dz, code_rows) for level in range(2)]
-    own[0:frames, :] = jnp.where(bit == 1, once, latent).astype(BF16)
-    own[frames:, :] = jnp.where(bit == 1, digits[1], digits[0])
-    other = jnp.where(bit == 1, latent, once).astype(BF16)
-    other_digits = jnp.where(bit == 1, digits[0], digits[1])
-    for j in range(dz // LANES):
-        send[at:at + frames, :] = other[:, j * LANES:(j + 1) * LANES]
-        send[at + frames:at + frames + code_rows, :] = other_digits[:, j * LANES:(j + 1) * LANES]
-        at += frames + code_rows
+    at = 0
+    for source, (count, orders, halved) in zip((unfold, hidden), plan):
+        rows = source[0:16, :].astype(F32)[0:1, :]
+        for position, places, step in walk(orders, halved, count):
+            for j in range(step):
+                offsets = [places[0] + j, places[1] + j]
+                low = [offset for offset in offsets]
+                high = [offset + (1 << orders[0][0] if halved else 0) for offset in offsets]
+                picked = [rows[:, k * LANES:(k + 1) * LANES] for k in low + high]
+                piece = jnp.where(bit == 1, picked[0], picked[3]) if halved else jnp.where(bit == 1, picked[0], picked[1])
+                begin = (at + position + j) * dz
+                send[begin:begin + dz, :] = (part[begin:begin + dz, :] + column * piece).astype(BF16)
+        at += count // 2 if halved else count
+    rows_b = own.shape[0]
+    own[0:16, :] = jnp.where(bit == 1, once, latent).astype(BF16)
+    put_columns(send, at * dz, rows_b, jnp.where(bit == 1, latent, once).astype(BF16))
 
 
 def rest_kernel(plan, info, flipped, unfold, hidden, latent_grad, proj, keep_a, keep_c, hidden_grad, extras, row):
@@ -536,24 +578,24 @@
 
     halo = shifted(call(halo_kernel, shape((2, channels), BF16), [info, feats[-2:]], flops=10 ** 11), "tm", 1)
     weight, proj, codes = conv_weight, proj_weight, codes[0]
-    unfold, conv, chosen = call(
-        local_kernel,
-        [shape((frames, width), BF16), shape((frames, channels), F32), shape((levels, frames, dz), BF16)],
-        [info, feats, weight, conv_bias[None, :], codes, codebooks],
-        scratch=[VMEM((channels // LANES, rows_in + 8, LANES), F32)],
-    )
-
     extra = 4 * (-(-channels // LANES // 8) * 8)
     code_rows = -(-(2 * -(-frames // dz)) // 16) * 16
     corr_rows = (now_a + now_c) * dz
     rows_b = frames + code_rows
+    shared = [shape((frames, width), BF16), shape((frames, channels), BF16), shape((frames, dz), BF16),
+              shape((dz, frames), BF16), shape((rows_b, dz), BF16),
+              shape((corr_rows + rows_b * (dz // LANES), LANES), BF16)]
+    *arrays, first, part = call(
+        functools.partial(local_kernel, plan),
+        shared + [shape((16, channels), F32), shape((corr_rows + 32 * (dz // LANES), LANES), F32)],
+        [info, feats, weight, conv_bias[None, :], codes, codebooks, proj],
+        scratch=[VMEM((channels // LANES, rows_in + 8, LANES), F32), VMEM((levels, frames, dz), BF16)],
+    )
     unfold, hidden, latent_grad, flipped, own, send = call(
-        functools.partial(forward_kernel, plan),
-        [shape((frames, width), BF16), shape((frames, channels), BF16), shape((frames, dz), BF16),
-         shape((dz, frames), BF16), shape((rows_b, dz), BF16),
-         shape((corr_rows + rows_b * (dz // LANES), LANES), BF16)],
-        [info, halo, unfold, conv, chosen, weight, proj, codes],
-        aliases={2: 0},
+        functools.partial(frame_kernel, plan),
+        shared,
+        [info, halo, first, part, weight, proj] + arrays,
+        aliases={6 + k: k for k in range(len(shared))},
     )
     got = swapped(send, exchanges[0])
     keep_a, keep_c, hidden_grad, extras, row = call(

time: 54.3 us -> 54 us (level)
  starting transfers between devices: 21.8 us -> 18.6 us
  waiting for transfers between devices: 11.4 us -> 14.1 us
    ppermute x11, starting transfers between devices: 16.3 us -> 11.8 us  [swapped(): return lax.ppermute(block, ('dp', 'tm'), route)]
    ppermute x11, waiting for transfers between devices: 10.9 us -> 14 us  [swapped(): return lax.ppermute(block, ('dp', 'tm'), route)]
    ppermute x1, starting transfers between devices: 0.52 us -> 1.8 us  [crossed(): return lax.ppermute(block, ('dp', 'tm'), route)]
  transfers between devices with their start and end apart: 13 -> 13, of which waited for: 9 -> 9; matrix products, arithmetic and copies ran while one was open for 0% -> 0% of each run, Pallas kernels for 25% -> 27%
where the time goes in v14:
time: 54 us; the launch traced here: 53.2 us
  Pallas kernels  18.8 us (35%)
  starting transfers between devices  18.6 us (34%)
  waiting for transfers between devices  14.1 us (26%)
  between operations  0.9 us (2%)
  local copies, waits for them, and re-layouts  0.84 us (2%)
    pallas_call x17, Pallas kernels, call(): pl.pallas_call(kernel, out_shape=shown, in_specs=specs, out_specs=[pl.Blo...  18.8 us
    ppermute x11, waiting for transfers between devices, swapped(): return lax.ppermute(block, ('dp', 'tm'), route)  14 us
    ppermute x11, starting transfers between devices, swapped(): return lax.ppermute(block, ('dp', 'tm'), route)  11.8 us
    ppermute x1, starting transfers between devices, shifted(): return lax.ppermute(block, axis, route)  5.06 us
    ppermute x1, starting transfers between devices, crossed(): return lax.ppermute(block, ('dp', 'tm'), route)  1.8 us
  transfers between devices with their start and end apart: 13, of which 9 were waited for; matrix products, arithmetic and copies ran while one was open for 0% of the time, Pallas kernels for 27%

profile of v14, /device:TPU:0, one launch (start us, length us, event | category | flops | bytes accessed | tf_op | source)
XLA Modules:
  0.0 53.2 jit_solution(9547372515571714779)
XLA Ops:
  0.7 0.7 %slice.3.refs_1_ = bf16[2,512]{1,0:T(2,128)(2,1)S(1)} slice(bf16[768,512]{1,0:T(8,128)(2,1)} %refs_1_.1), slice={[766:768], [0:512]} | slice | bytes 4096 | tf_op jit(solution)/shard_map/slice | solution.py:579
  2.1 5.1 %collective-permute-start = (bf16[2,512]{1,0:T(2,128)(2,1)S(1)}, bf16[2,512]{1,0:T(2,128)(2,1)S(1)}, u32[]{:S(2)}, u32[]{:S(2)}) collective-permute-start(bf16[2,512]{1,0:T(2,128)(2,1)S(1)} %shard_map.109), channel_id=1, source_target_pairs={{0,1},{1,2},{2,3},{4,5},{5,6},{6,7},{8,9},{9,10},{10,11},{12,13},{... | collective-permute-start | bytes 6152 | tf_op jit(solution)/shard_map/ppermute | solution.py:467
  7.2 2.8 %shard_map.110 = (bf16[384,2048]{1,0:T(8,128)(2,1)S(1)}, bf16[384,512]{1,0:T(8,128)(2,1)S(1)}, bf16[384,256]{1,0:T(8,128)(2,1)S(1)}, bf16[256,384]{1,0:T(8,128)(...) custom-call(s32[19]{0:T(128)S(1)} %stack.67.refs_0_, ...), custom_call_target="tpu_custom_call" | custom-call | tf_op jit(solution)/shard_map/pallas_call | solution.py:48
  10.1 1.2 %shard_map.111 = (bf16[384,2048]{1,0:T(8,128)(2,1)S(1)}, bf16[384,512]{1,0:T(8,128)(2,1)S(1)}, bf16[384,256]{1,0:T(8,128)(2,1)S(1)}, bf16[256,384]{1,0:T(8,128)(...) custom-call(s32[19]{0:T(128)S(1)} %stack.67.refs_0_, ...), custom_call_target="tpu_custom_call", output_to_operand_aliasing={{0}: (6, {}), {1}: (7, {}), {2}: (8, {}), {3}: (9, {}), {4}... | custom-call | tf_op jit(solution)/shard_map/pallas_call | solution.py:48
  11.4 1.2 %shard_map.112 = (f32[2048,128]{1,0:T(8,128)S(1)}, f32[512,128]{1,0:T(8,128)S(1)}, bf16[384,512]{1,0:T(8,128)(2,1)S(1)}, f32[32,128]{1,0:T(8,128)S(1)}, bf16[16,512]{1,0:T(8,128)(2,1)S(1)}) custom-call(s32[19]{0:T(128)S(1)} %stack.67.refs_0_, bf16[256,384]{1,0:T(8,128)(2,1)S(1)} %get-tuple-element.64.refs_1_, ...), custom_call_target="tpu_custom_call" | custom-call | tf_op jit(solution)/shard_map/pallas_call | solution.py:48
  12.6 1.2 %collective-permute-done.1.refs_1_ = bf16[3360,128]{1,0:T(8,128)(2,1)S(1)} collective-permute-done((bf16[3360,128]{1,0:T(8,128)(2,1)S(1)}, bf16[3360,128]{1,0:T(8,128)(2,1)S(1)}, u32[]{:S(2)}, u32[]{:S(2)}) %collective-permute-start.1) | collective-permute-done | bytes 860192 | tf_op jit(solution)/shard_map/ppermute | solution.py:478
  13.8 0.7 %shard_map.113 = (bf16[1312,128]{1,0:T(8,128)(2,1)S(1)}, f32[1024,128]{1,0:T(8,128)S(1)}, f32[288,128]{1,0:T(8,128)S(1)}) custom-call(s32[19]{0:T(128)S(1)} %stack.67.refs_0_, bf16[3360,128]{1,0:T(8,128)(2,1)S(1)} %collective-permute-done.1.refs_1_, f32[2048,128]{1,0:T(8,128)S(1)} %get-tuple-element.72.refs_2_, f32[512,128]{1,0:T(8,128)S(1)} %get-tuple-element.73.refs_3_, ...), custom_call_target="tpu_custom_call" | custom-call | tf_op jit(solution)/shard_map/pallas_call | solution.py:48
  14.5 1.6 %collective-permute-start.3 = (bf16[1312,128]{1,0:T(8,128)(2,1)S(1)}, bf16[1312,128]{1,0:T(8,128)(2,1)S(1)}, u32[]{:S(2)}, u32[]{:S(2)}) collective-permute-start(bf16[1312,128]{1,0:T(8,128)(2,1)S(1)} %get-tuple-element.75.refs_4_), channel_id=1, source_target_pairs={{0,8},{1,9},{2,10},{3,11},{4,20},{5,21},{6,22},{7,23},{8,0},{9,1},... | collective-permute-start | bytes 1007624 | tf_op jit(solution)/shard_map/ppermute | solution.py:478
  16.0 1.2 %shard_map.114.refs_4_ = bf16[544,256]{1,0:T(8,128)(2,1)S(1)} custom-call(s32[19]{0:T(128)S(1)} %stack.67.refs_0_, bf16[3360,128]{1,0:T(8,128)(2,1)S(1)} %collective-permute-done.1.refs_1_, bf16[400,256]{1,0:T(8,128)(2,1)S(1)} %get-tuple-element.70.refs_2_, bf16[16,512]{1,0:T(8,128)(2,1)S(1)} %get-tuple-element.71.refs_3_, ...), custom_call_target="tpu_custom_call" | custom-call | tf_op jit(solution)/shard_map/pallas_call | solution.py:48
  17.2 1.6 %collective-permute-start.2 = (bf16[544,256]{1,0:T(8,128)(2,1)S(1)}, bf16[544,256]{1,0:T(8,128)(2,1)S(1)}, u32[]{:S(2)}, u32[]{:S(2)}) collective-permute-start(bf16[544,256]{1,0:T(8,128)(2,1)S(1)} %shard_map.114.refs_4_), channel_id=1, source_target_pairs={{0,1},{1,0},{2,3},{3,2},{4,6},{5,7},{6,4},{7,5},{8,9},{9,8},{10,11... | collective-permute-start | bytes 835592 | tf_op jit(solution)/shard_map/ppermute | solution.py:478
  18.8 1.2 %shard_map.115.refs_4_.refs_2_ = f32[544,256]{1,0:T(8,128)S(1)} custom-call(s32[19]{0:T(128)S(1)} %stack.67.refs_0_, bf16[3360,128]{1,0:T(8,128)(2,1)S(1)} %collective-permute-done.1.refs_1_, bf16[400,256]{1,0:T(8,128)(2,1)S(1)} %get-tuple-element.70.refs_2_, bf16[16,512]{1,0:T(8,128)(2,1)S(1)} %get-tuple-element.71.refs_3_, ...), custom_call_target="tpu_custom_call" | custom-call | tf_op jit(solution)/shard_map/pallas_call | solution.py:48
  20.0 1.7 %collective-permute-done.3.refs_1_ = bf16[1312,128]{1,0:T(8,128)(2,1)S(1)} collective-permute-done((bf16[1312,128]{1,0:T(8,128)(2,1)S(1)}, bf16[1312,128]{1,0:T(8,128)(2,1)S(1)}, u32[]{:S(2)}, u32[]{:S(2)}) %collective-permute-start.3) | collective-permute-done | bytes 335904 | tf_op jit(solution)/shard_map/ppermute | solution.py:478
  21.7 0.6 %shard_map.116 = (bf16[800,128]{1,0:T(8,128)(2,1)S(1)}, f32[512,128]{1,0:T(8,128)S(1)}, f32[288,128]{1,0:T(8,128)S(1)}) custom-call(s32[19]{0:T(128)S(1)} %stack.67.refs_0_, bf16[1312,128]{1,0:T(8,128)(2,1)S(1)} %collective-permute-done.3.refs_1_, f32[1024,128]{1,0:T(8,128)S(1)} %get-tuple-element.76.refs_2_, f32[288,128]{1,0:T(8,128)S(1)} %get-tuple-element.77.refs_3_, ...), custom_call_target="tpu_custom_call" | custom-call | tf_op jit(solution)/shard_map/pallas_call | solution.py:48
  22.3 1.6 %collective-permute-start.5 = (bf16[800,128]{1,0:T(8,128)(2,1)S(1)}, bf16[800,128]{1,0:T(8,128)(2,1)S(1)}, u32[]{:S(2)}, u32[]{:S(2)}) collective-permute-start(bf16[800,128]{1,0:T(8,128)(2,1)S(1)} %get-tuple-element.78.refs_4_), channel_id=1, source_target_pairs={{0,16},{1,17},{2,18},{3,19},{4,12},{5,13},{6,14},{7,15},{8,24},{9,... | collective-permute-start | bytes 614408 | tf_op jit(solution)/shard_map/ppermute | solution.py:478
  23.9 2.6 %collective-permute-done.2.refs_1_ = bf16[544,256]{1,0:T(8,128)(2,1)S(1)} collective-permute-done((bf16[544,256]{1,0:T(8,128)(2,1)S(1)}, bf16[544,256]{1,0:T(8,128)(2,1)S(1)}, u32[]{:S(2)}, u32[]{:S(2)}) %collective-permute-start.2) | collective-permute-done | bytes 278560 | tf_op jit(solution)/shard_map/ppermute | solution.py:478
  26.5 0.6 %shard_map.117 = (bf16[272,256]{1,0:T(8,128)(2,1)S(1)}, f32[272,256]{1,0:T(8,128)S(1)}, bf16[16,512]{1,0:T(8,128)(2,1)S(1)}) custom-call(s32[19]{0:T(128)S(1)} %stack.67.refs_0_, bf16[544,256]{1,0:T(8,128)(2,1)S(1)} %collective-permute-done.2.refs_1_, f32[544,256]{1,0:T(8,128)S(1)} %shard_map.115.refs_4_.refs_2_, ...), custom_call_target="tpu_custom_call" | custom-call | tf_op jit(solution)/shard_map/pallas_call | solution.py:48
  27.1 1.8 %collective-permute-start.4 = (bf16[272,256]{1,0:T(8,128)(2,1)S(1)}, bf16[272,256]{1,0:T(8,128)(2,1)S(1)}, u32[]{:S(2)}, u32[]{:S(2)}) collective-permute-start(bf16[272,256]{1,0:T(8,128)(2,1)S(1)} %get-tuple-element.79.refs_4_), channel_id=1, source_target_pairs={{0,2},{1,3},{2,0},{3,1},{4,5},{5,4},{6,7},{7,6},{8,10},{9,11},{10,... | collective-permute-start | bytes 417800 | tf_op jit(solution)/shard_map/ppermute | solution.py:478
  28.9 0.7 %shard_map.118 = (bf16[544,128]{1,0:T(8,128)(2,1)S(1)}, f32[256,128]{1,0:T(8,128)S(1)}, f32[288,128]{1,0:T(8,128)S(1)}) custom-call(s32[19]{0:T(128)S(1)} %stack.67.refs_0_, bf16[800,128]{1,0:T(8,128)(2,1)S(1)} %collective-permute-done.5.refs_1_, f32[512,128]{1,0:T(8,128)S(1)} %get-tuple-element.82.refs_2_, f32[288,128]{1,0:T(8,128)S(1)} %get-tuple-element.83.refs_3_, ...), custom_call_target="tpu_custom_call" | custom-call | tf_op jit(solution)/shard_map/pallas_call | solution.py:48
  29.6 1.9 %collective-permute-start.7 = (bf16[544,128]{1,0:T(8,128)(2,1)S(1)}, bf16[544,128]{1,0:T(8,128)(2,1)S(1)}, u32[]{:S(2)}, u32[]{:S(2)}) collective-permute-start(bf16[544,128]{1,0:T(8,128)(2,1)S(1)} %get-tuple-element.84.refs_4_), channel_id=1, source_target_pairs={{0,2},{1,3},{2,0},{3,1},{4,5},{5,4},{6,7},{7,6},{8,10},{9,11},{10,... | collective-permute-start | bytes 417800 | tf_op jit(solution)/shard_map/ppermute | solution.py:478
  31.5 2.0 %collective-permute-done.4.refs_1_ = bf16[272,256]{1,0:T(8,128)(2,1)S(1)} collective-permute-done((bf16[272,256]{1,0:T(8,128)(2,1)S(1)}, bf16[272,256]{1,0:T(8,128)(2,1)S(1)}, u32[]{:S(2)}, u32[]{:S(2)}) %collective-permute-start.4) | collective-permute-done | bytes 139296 | tf_op jit(solution)/shard_map/ppermute | solution.py:478
  33.4 0.6 %shard_map.119 = (bf16[272,256]{1,0:T(8,128)(2,1)S(1)}, f32[272,256]{1,0:T(8,128)S(1)}, bf16[16,512]{1,0:T(8,128)(2,1)S(1)}) custom-call(s32[19]{0:T(128)S(1)} %stack.67.refs_0_, bf16[272,256]{1,0:T(8,128)(2,1)S(1)} %collective-permute-done.4.refs_1_, f32[272,256]{1,0:T(8,128)S(1)} %get-tuple-element.80.refs_2_, ...), custom_call_target="tpu_custom_call" | custom-call | tf_op jit(solution)/shard_map/pallas_call | solution.py:48
  34.0 1.8 %collective-permute-start.6 = (bf16[272,256]{1,0:T(8,128)(2,1)S(1)}, bf16[272,256]{1,0:T(8,128)(2,1)S(1)}, u32[]{:S(2)}, u32[]{:S(2)}) collective-permute-start(bf16[272,256]{1,0:T(8,128)(2,1)S(1)} %get-tuple-element.86.refs_4_), channel_id=1, source_target_pairs={{0,8},{1,9},{2,10},{3,11},{4,20},{5,21},{6,22},{7,23},{8,0},{9,1},... | collective-permute-start | bytes 417800 | tf_op jit(solution)/shard_map/ppermute | solution.py:478
  35.8 2.2 %collective-permute-done.7.refs_1_ = bf16[544,128]{1,0:T(8,128)(2,1)S(1)} collective-permute-done((bf16[544,128]{1,0:T(8,128)(2,1)S(1)}, bf16[544,128]{1,0:T(8,128)(2,1)S(1)}, u32[]{:S(2)}, u32[]{:S(2)}) %collective-permute-start.7) | collective-permute-done | bytes 139296 | tf_op jit(solution)/shard_map/ppermute | solution.py:478
  39.2 0.6 %shard_map.121 = (bf16[272,256]{1,0:T(8,128)(2,1)S(1)}, f32[272,256]{1,0:T(8,128)S(1)}) custom-call(s32[19]{0:T(128)S(1)} %stack.67.refs_0_, bf16[272,256]{1,0:T(8,128)(2,1)S(1)} %collective-permute-done.6.refs_1_, f32[272,256]{1,0:T(8,128)S(1)} %get-tuple-element.87.refs_2_, bf16[560,128]{1,0:T(8,128)(2,1)S(1)} %get-tuple-element.90.refs_3_), custom_call_target="tpu_custom_call" | custom-call | tf_op jit(solution)/shard_map/pallas_call | solution.py:48
  39.8 0.7 %collective-permute-start.9 = (bf16[272,256]{1,0:T(8,128)(2,1)S(1)}, bf16[272,256]{1,0:T(8,128)(2,1)S(1)}, u32[]{:S(2)}, u32[]{:S(2)}) collective-permute-start(bf16[272,256]{1,0:T(8,128)(2,1)S(1)} %get-tuple-element.91.refs_4_), channel_id=1, source_target_pairs={{0,16},{1,17},{2,18},{3,19},{4,12},{5,13},{6,14},{7,15},{8,24},{9,... | collective-permute-start | bytes 417800 | tf_op jit(solution)/shard_map/ppermute | solution.py:478
  40.5 2.6 %shard_map.122 = (bf16[768,512]{1,0:T(8,128)(2,1)}, f32[8,128]{1,0:T(8,128)S(1)}) custom-call(s32[19]{0:T(128)S(1)} %stack.67.refs_0_, bf16[384,512]{1,0:T(8,128)(2,1)S(1)} %get-tuple-element.69.refs_1_, bf16[16,512]{1,0:T(8,128)(2,1)S(1)} %get-tuple-element.85.refs_2_, bf16[2048,512]{1,0:T(8,128)(2,1)S(1)} %copy-done, ...), custom_call_target="tpu_custom_call" | custom-call | tf_op jit(solution)/shard_map/pallas_call | solution.py:48
  43.0 1.8 %collective-permute-done.9.refs_4_ = bf16[272,256]{1,0:T(8,128)(2,1)S(1)} collective-permute-done((bf16[272,256]{1,0:T(8,128)(2,1)S(1)}, bf16[272,256]{1,0:T(8,128)(2,1)S(1)}, u32[]{:S(2)}, u32[]{:S(2)}) %collective-permute-start.9) | collective-permute-done | bytes 139296 | tf_op jit(solution)/shard_map/ppermute | solution.py:478
  44.9 0.7 %shard_map.123 = (f32[256,128]{1,0:T(8,128)S(1)}, bf16[256,128]{1,0:T(8,128)(2,1)S(1)}, bf16[832,128]{1,0:T(8,128)(2,1)S(1)}) custom-call(s32[19]{0:T(128)S(1)} %stack.67.refs_0_, bf16[560,128]{1,0:T(8,128)(2,1)S(1)} %collective-permute-done.8.refs_1_, f32[256,128]{1,0:T(8,128)S(1)} %get-tuple-element.93.refs_2_, f32[288,128]{1,0:T(8,128)S(1)} %get-tuple-element.94.refs_3_, ...), custom_call_target="tpu_custom_call" | custom-call | tf_op jit(solution)/shard_map/pallas_call | solution.py:48
  45.6 1.8 %collective-permute-start.12 = (bf16[256,128]{1,0:T(8,128)(2,1)S(1)}, bf16[256,128]{1,0:T(8,128)(2,1)S(1)}, u32[]{:S(2)}, u32[]{:S(2)}) collective-permute-start(bf16[256,128]{1,0:T(8,128)(2,1)S(1)} %get-tuple-element.98.refs_3_.refs_2_), channel_id=1, source_target_pairs={{0,12},{1,13},{2,14},{3,15},{4,16},{5,17},{6,18},{7,19},{8,4},{9,5... | collective-permute-start | bytes 196616 | tf_op jit(solution)/shard_map/ppermute | solution.py:489
  47.8 1.5 %shard_map.124 = (f32[64,512]{1,0:T(8,128)}, f32[8,128]{1,0:T(8,128)S(1)}) custom-call(s32[19]{0:T(128)S(1)} %stack.67.refs_0_, f32[256,128]{1,0:T(8,128)S(1)} %get-tuple-element.97.refs_1_, bf16[512,256]{1,0:T(8,128)(2,1)S(1)} %copy-done.1, bf16[256,128]{1,0:T(8,128)(2,1)S(1)} %get-tuple-element.98.refs_3_.refs_2_), custom_call_target="tpu_custom_call" | custom-call | tf_op jit(solution)/shard_map/pallas_call | solution.py:48
  49.4 2.3 %collective-permute-done.11.refs_4_ = bf16[256,128]{1,0:T(8,128)(2,1)S(1)} collective-permute-done((bf16[256,128]{1,0:T(8,128)(2,1)S(1)}, bf16[256,128]{1,0:T(8,128)(2,1)S(1)}, u32[]{:S(2)}, u32[]{:S(2)}) %collective-permute-start.11) | collective-permute-done | bytes 65568 | tf_op jit(solution)/shard_map/ppermute | solution.py:478
  51.7 1.5 %shard_map.125 = (f32[512,256]{1,0:T(8,128)}, f32[1,512]{1,0:T(1,128)}, bf16[2,256,256]{2,1,0:T(8,128)(2,1)}, f32[2,256]{1,0:T(2,128)}) custom-call(s32[19]{0:T(128)S(1)} %stack.67.refs_0_, bf16[832,128]{1,0:T(8,128)(2,1)S(1)} %get-tuple-element.100.refs_1_, bf16[256,128]{1,0:T(8,128)(2,1)S(1)} %get-tuple-element.98.refs_3_.refs_2_, ...), custom_call_target="tpu_custom_call" | custom-call | tf_op jit(solution)/shard_map/pallas_call | solution.py:48
  (25 shorter events, 2.4 us)
Async XLA Ops:
  1.5 5.7 %copy-start = (bf16[2048,512]{1,0:T(8,128)(2,1)S(1)}, bf16[2048,512]{1,0:T(8,128)(2,1)}, u32[]{:S(2)}) copy-start(bf16[2048,512]{1,0:T(8,128)(2,1)} %refs_3_.1) | copy-start | bytes 6291460
  1.5 5.7 %copy-start.1 = (bf16[512,256]{1,0:T(8,128)(2,1)S(1)}, bf16[512,256]{1,0:T(8,128)(2,1)}, u32[]{:S(2)}) copy-start(bf16[512,256]{1,0:T(8,128)(2,1)} %refs_2_.3) | copy-start | bytes 786436
  1.5 5.7 %copy-start.2 = (bf16[2,1024,256]{2,1,0:T(8,128)(2,1)S(1)}, bf16[2,1024,256]{2,1,0:T(8,128)(2,1)}, u32[]{:S(2)}) copy-start(bf16[2,1024,256]{2,1,0:T(8,128)(2,1)} %refs_5_.3) | copy-start | bytes 3145732
  1.5 5.7 %copy-start.3 = (bf16[768,512]{1,0:T(8,128)(2,1)S(1)}, bf16[768,512]{1,0:T(8,128)(2,1)}, u32[]{:S(2)}) copy-start(bf16[768,512]{1,0:T(8,128)(2,1)} %refs_1_.1) | copy-start | bytes 2359300
  1.5 5.7 %copy-start.4 = (s32[1,2,384]{2,1,0:T(2,128)S(1)}, s32[1,2,384]{2,1,0:T(2,128)}, u32[]{:S(2)}) copy-start(s32[1,2,384]{2,1,0:T(2,128)} %param.7) | copy-start | bytes 9220
  1.5 5.7 %copy-start.5 = (f32[512]{0:T(512)S(1)}, f32[512]{0:T(512)}, u32[]{:S(2)}) copy-start(f32[512]{0:T(512)} %param.9) | copy-start | bytes 6148
  2.1 8.0 %collective-permute-start = (bf16[2,512]{1,0:T(2,128)(2,1)S(1)}, bf16[2,512]{1,0:T(2,128)(2,1)S(1)}, u32[]{:S(2)}, u32[]{:S(2)}) collective-permute-start(bf16[2,512]{1,0:T(2,128)(2,1)S(1)} %shard_map.109), channel_id=1, source_target_pairs={{0,1},{1,2},{2,3},{4,5},{5,6},{6,7},{8,9},{9,10},{10,11},{12,13},{... | collective-permute-start | bytes 6152 | tf_op jit(solution)/shard_map/ppermute | solution.py:467
  11.3 2.5 %collective-permute-start.1 = (bf16[3360,128]{1,0:T(8,128)(2,1)S(1)}, bf16[3360,128]{1,0:T(8,128)(2,1)S(1)}, u32[]{:S(2)}, u32[]{:S(2)}) collective-permute-start(bf16[3360,128]{1,0:T(8,128)(2,1)S(1)} %get-tuple-element.68.refs_6_), channel_id=1, source_target_pairs={{0,4},{1,5},{2,6},{3,7},{4,0},{5,1},{6,2},{7,3},{8,12},{9,13},{10,... | collective-permute-start | bytes 2580488 | tf_op jit(solution)/shard_map/ppermute | solution.py:478
  14.5 7.2 %collective-permute-start.3 = (bf16[1312,128]{1,0:T(8,128)(2,1)S(1)}, bf16[1312,128]{1,0:T(8,128)(2,1)S(1)}, u32[]{:S(2)}, u32[]{:S(2)}) collective-permute-start(bf16[1312,128]{1,0:T(8,128)(2,1)S(1)} %get-tuple-element.75.refs_4_), channel_id=1, source_target_pairs={{0,8},{1,9},{2,10},{3,11},{4,20},{5,21},{6,22},{7,23},{8,0},{9,1},... | collective-permute-start | bytes 1007624 | tf_op jit(solution)/shard_map/ppermute | solution.py:478
  17.2 9.3 %collective-permute-start.2 = (bf16[544,256]{1,0:T(8,128)(2,1)S(1)}, bf16[544,256]{1,0:T(8,128)(2,1)S(1)}, u32[]{:S(2)}, u32[]{:S(2)}) collective-permute-start(bf16[544,256]{1,0:T(8,128)(2,1)S(1)} %shard_map.114.refs_4_), channel_id=1, source_target_pairs={{0,1},{1,0},{2,3},{3,2},{4,6},{5,7},{6,4},{7,5},{8,9},{9,8},{10,11... | collective-permute-start | bytes 835592 | tf_op jit(solution)/shard_map/ppermute | solution.py:478
  22.3 6.6 %collective-permute-start.5 = (bf16[800,128]{1,0:T(8,128)(2,1)S(1)}, bf16[800,128]{1,0:T(8,128)(2,1)S(1)}, u32[]{:S(2)}, u32[]{:S(2)}) collective-permute-start(bf16[800,128]{1,0:T(8,128)(2,1)S(1)} %get-tuple-element.78.refs_4_), channel_id=1, source_target_pairs={{0,16},{1,17},{2,18},{3,19},{4,12},{5,13},{6,14},{7,15},{8,24},{9,... | collective-permute-start | bytes 614408 | tf_op jit(solution)/shard_map/ppermute | solution.py:478
  27.1 6.3 %collective-permute-start.4 = (bf16[272,256]{1,0:T(8,128)(2,1)S(1)}, bf16[272,256]{1,0:T(8,128)(2,1)S(1)}, u32[]{:S(2)}, u32[]{:S(2)}) collective-permute-start(bf16[272,256]{1,0:T(8,128)(2,1)S(1)} %get-tuple-element.79.refs_4_), channel_id=1, source_target_pairs={{0,2},{1,3},{2,0},{3,1},{4,5},{5,4},{6,7},{7,6},{8,10},{9,11},{10,... | collective-permute-start | bytes 417800 | tf_op jit(solution)/shard_map/ppermute | solution.py:478
  29.6 8.4 %collective-permute-start.7 = (bf16[544,128]{1,0:T(8,128)(2,1)S(1)}, bf16[544,128]{1,0:T(8,128)(2,1)S(1)}, u32[]{:S(2)}, u32[]{:S(2)}) collective-permute-start(bf16[544,128]{1,0:T(8,128)(2,1)S(1)} %get-tuple-element.84.refs_4_), channel_id=1, source_target_pairs={{0,2},{1,3},{2,0},{3,1},{4,5},{5,4},{6,7},{7,6},{8,10},{9,11},{10,... | collective-permute-start | bytes 417800 | tf_op jit(solution)/shard_map/ppermute | solution.py:478
  34.0 5.1 %collective-permute-start.6 = (bf16[272,256]{1,0:T(8,128)(2,1)S(1)}, bf16[272,256]{1,0:T(8,128)(2,1)S(1)}, u32[]{:S(2)}, u32[]{:S(2)}) collective-permute-start(bf16[272,256]{1,0:T(8,128)(2,1)S(1)} %get-tuple-element.86.refs_4_), channel_id=1, source_target_pairs={{0,8},{1,9},{2,10},{3,11},{4,20},{5,21},{6,22},{7,23},{8,0},{9,1},... | collective-permute-start | bytes 417800 | tf_op jit(solution)/shard_map/ppermute | solution.py:478
  38.6 6.3 %collective-permute-start.8 = (bf16[560,128]{1,0:T(8,128)(2,1)S(1)}, bf16[560,128]{1,0:T(8,128)(2,1)S(1)}, u32[]{:S(2)}, u32[]{:S(2)}) collective-permute-start(bf16[560,128]{1,0:T(8,128)(2,1)S(1)} %get-tuple-element.90.refs_3_), channel_id=1, source_target_pairs={{0,1},{1,0},{2,3},{3,2},{4,6},{5,7},{6,4},{7,5},{8,9},{9,8},{10,11... | collective-permute-start | bytes 430088 | tf_op jit(solution)/shard_map/ppermute | solution.py:478
  39.8 5.1 %collective-permute-start.9 = (bf16[272,256]{1,0:T(8,128)(2,1)S(1)}, bf16[272,256]{1,0:T(8,128)(2,1)S(1)}, u32[]{:S(2)}, u32[]{:S(2)}) collective-permute-start(bf16[272,256]{1,0:T(8,128)(2,1)S(1)} %get-tuple-element.91.refs_4_), channel_id=1, source_target_pairs={{0,16},{1,17},{2,18},{3,19},{4,12},{5,13},{6,14},{7,15},{8,24},{9,... | collective-permute-start | bytes 417800 | tf_op jit(solution)/shard_map/ppermute | solution.py:478
  45.6 6.2 %collective-permute-start.10 = (bf16[832,128]{1,0:T(8,128)(2,1)S(1)}, bf16[832,128]{1,0:T(8,128)(2,1)S(1)}, u32[]{:S(2)}, u32[]{:S(2)}) collective-permute-start(bf16[832,128]{1,0:T(8,128)(2,1)S(1)} %get-tuple-element.100.refs_1_), channel_id=1, source_target_pairs={{0,4},{1,5},{2,6},{3,7},{4,0},{5,1},{6,2},{7,3},{8,12},{9,13},{10,... | collective-permute-start | bytes 638984 | tf_op jit(solution)/shard_map/ppermute | solution.py:478
  45.6 3.7 %collective-permute-start.12 = (bf16[256,128]{1,0:T(8,128)(2,1)S(1)}, bf16[256,128]{1,0:T(8,128)(2,1)S(1)}, u32[]{:S(2)}, u32[]{:S(2)}) collective-permute-start(bf16[256,128]{1,0:T(8,128)(2,1)S(1)} %get-tuple-element.98.refs_3_.refs_2_), channel_id=1, source_target_pairs={{0,12},{1,13},{2,14},{3,15},{4,16},{5,17},{6,18},{7,19},{8,4},{9,5... | collective-permute-start | bytes 196616 | tf_op jit(solution)/shard_map/ppermute | solution.py:489
  47.4 4.3 %collective-permute-start.11 = (bf16[256,128]{1,0:T(8,128)(2,1)S(1)}, bf16[256,128]{1,0:T(8,128)(2,1)S(1)}, u32[]{:S(2)}, u32[]{:S(2)}) collective-permute-start(bf16[256,128]{1,0:T(8,128)(2,1)S(1)} %get-tuple-element.98.refs_3_.refs_2_), channel_id=1, source_target_pairs={{0,8},{1,9},{2,10},{3,11},{4,20},{5,21},{6,22},{7,23},{8,0},{9,1},... | collective-permute-start | bytes 196616 | tf_op jit(solution)/shard_map/ppermute | solution.py:478

commit v15 on v14

--- a/solution.py
+++ b/solution.py
@@ -259,11 +259,11 @@
     return jnp.concatenate(list(digits_of(value)) + [jnp.zeros_like(value)], 0)
 
 
-def first_step_kernel(halves, place, info, got, kept_a, kept_c, extras, send, keep_a, keep_c):
+def first_step_kernel(halves, place, info, got, kept_a, kept_c, extras, send_a, send_c, keep_a, keep_c):
     (rows_a, halved_a), (rows_c, halved_c) = halves
-    to = split_sum(halved_a, info[place], got, 0, kept_a, rows_a, send, 0, keep_a)
-    gone = split_sum(halved_c, info[place], got, rows_a, kept_c, rows_c, send, to, keep_c)
-    send[to + gone:, :] = extras[...].astype(BF16)
+    split_sum(halved_a, info[place], got, 0, kept_a, rows_a, send_a, 0, keep_a)
+    gone = split_sum(halved_c, info[place], got, rows_a, kept_c, rows_c, send_c, 0, keep_c)
+    send_c[gone:, :] = extras[...].astype(BF16)
     keep_c[gone:, :] = extras[...]
 
 
@@ -374,7 +374,7 @@
     return jnp.where(core == 1, swapped_first, first), jnp.where(core == 1, swapped_second, second)
 
 
-def step_kernel(halves, place, mixed, info, got, kept_a, kept_c, send, keep_a, keep_c):
+def step_kernel(halves, at_c, place, mixed, info, got, got_c, kept_a, kept_c, send, keep_a, keep_c):
     (rows_a, halved_a), (rows_c, halved_c) = halves
     if mixed:
         to = rows_a // 2
@@ -385,8 +385,8 @@
         keep_a[...] = jnp.where(low, first, second)
     else:
         to = split_sum(halved_a, info[place], got, 0, kept_a, rows_a, send, 0, keep_a)
-    gone = split_sum(halved_c, info[place], got, rows_a, kept_c, rows_c, send, to, keep_c)
-    block = digit_block(add_digits(kept_c[rows_c:, :], got[rows_a + rows_c:, :].astype(F32)))
+    gone = split_sum(halved_c, info[place], got_c, at_c, kept_c, rows_c, send, to, keep_c)
+    block = digit_block(add_digits(kept_c[rows_c:, :], got_c[at_c + rows_c:, :].astype(F32)))
     keep_c[gone:, :] = block
     to += gone
     send[to:to + block.shape[0], :] = block.astype(BF16)
@@ -613,36 +613,38 @@
         now_c = now_c // 2 if halves[1][1] else now_c
         return halves, now_a * dz, now_c * dz + extra
 
-    halves, rows_a, rows_c = halves_at(1)
-    send, keep_a, keep_c = call(
-        functools.partial(first_step_kernel, halves, 1),
-        [shape((rows_a + rows_c, LANES), BF16), shape((rows_a, LANES), F32), shape((rows_c, LANES), F32)],
-        [info, got, keep_a, keep_c, extras])
     size = per_shard + 16
     sums_rows = size * (tm // 2)
     sums_send = call(
         functools.partial(sums_kernel, corr_rows, frames, at_codes, per_shard),
         shape((sums_rows, dz), BF16),
-        [info, got, own, row],
-        after=[send])
+        [info, got, own, row])
+    sums_got = swapped(sums_send, sums_exchanges[0])
+    halves, rows_a, rows_c = halves_at(1)
+    send, send_c, keep_a, keep_c = call(
+        functools.partial(first_step_kernel, halves, 1),
+        [shape((rows_a, LANES), BF16), shape((rows_c, LANES), BF16), shape((rows_a, LANES), F32),
+         shape((rows_c, LANES), F32)],
+        [info, got, keep_a, keep_c, extras],
+        after=[sums_send])
     sums_keep = call(
         functools.partial(sums_kernel, corr_rows, frames, at_codes + tm // 2, per_shard),
         shape((sums_rows, dz), F32),
         [info, got, own, row],
-        after=[sums_send])
-    sums_got = swapped(sums_send, sums_exchanges[0])
-    got = swapped(send, exchanges[1])
+        after=[send])
+    got, got_c = swapped(send, exchanges[1]), swapped(send_c, exchanges[1])
     known = row
-    ordered = [sums_keep]
+    ordered = [sums_keep, sums_got]
     for k in range(2, len(exchanges)):
+        at_c = 0 if k == 2 else rows_a
         halves, rows_a, rows_c = halves_at(k)
         spare = 16 * (k == len(exchanges) - 1)
         send, keep_a, keep_c = call(
-            functools.partial(step_kernel, halves, k, mixed and k == dp_bits),
+            functools.partial(step_kernel, halves, at_c, k, mixed and k == dp_bits),
             [shape((rows_a + rows_c + spare, LANES), BF16), shape((rows_a, LANES), F32), shape((rows_c, LANES), F32)],
-            [info, got, keep_a, keep_c],
+            [info, got, got_c, keep_a, keep_c],
             after=ordered)
-        got = swapped(send, exchanges[k])
+        got = got_c = swapped(send, exchanges[k])
         halved = sums_exchanges[k - 1][0][0] == "tm"
         sums_rows = sums_rows // 2 if halved else sums_rows
         row_step = k - 2 if k - 2 < tm_bits else None

time: 54 us -> 54.8 us (1.015)
  waiting for transfers between devices: 14.1 us -> 15.3 us
    ppermute x11 -> x12, waiting for transfers between devices: 14 us -> 15.3 us  [swapped(): return lax.ppermute(block, ('dp', 'tm'), route)]
    ppermute x11 -> x12, starting transfers between devices: 11.8 us -> 12 us  [swapped(): return lax.ppermute(block, ('dp', 'tm'), route)]
  transfers between devices with their start and end apart: 13 -> 14, of which waited for: 9 -> 9; matrix products, arithmetic and copies ran while one was open for 0% -> 0% of each run, Pallas kernels for 27% -> 24%
where the time goes in v15:
time: 54.8 us; the launch traced here: 54.6 us
  Pallas kernels  18.8 us (34%)
  starting transfers between devices  18.7 us (34%)
  waiting for transfers between devices  15.3 us (28%)
  between operations  0.9 us (2%)
  local copies, waits for them, and re-layouts  0.84 us (2%)
    pallas_call x17, Pallas kernels, call(): pl.pallas_call(kernel, out_shape=shown, in_specs=specs, out_specs=[pl.Blo...  18.8 us
    ppermute x12, waiting for transfers between devices, swapped(): return lax.ppermute(block, ('dp', 'tm'), route)  15.3 us
    ppermute x12, starting transfers between devices, swapped(): return lax.ppermute(block, ('dp', 'tm'), route)  12 us
    ppermute x1, starting transfers between devices, shifted(): return lax.ppermute(block, axis, route)  5.06 us
    ppermute x1, starting transfers between devices, crossed(): return lax.ppermute(block, ('dp', 'tm'), route)  1.59 us
  transfers between devices with their start and end apart: 14, of which 9 were waited for; matrix products, arithmetic and copies ran while one was open for 0% of the time, Pallas kernels for 24%

profile of v15, /device:TPU:0, one launch (start us, length us, event | category | flops | bytes accessed | tf_op | source)
XLA Modules:
  0.0 54.6 jit_solution(6929403767978935744)
XLA Ops:
  0.7 0.7 %slice.3.refs_1_ = bf16[2,512]{1,0:T(2,128)(2,1)S(1)} slice(bf16[768,512]{1,0:T(8,128)(2,1)} %refs_1_.1), slice={[766:768], [0:512]} | slice | bytes 4096 | tf_op jit(solution)/shard_map/slice | solution.py:579
  2.1 5.1 %collective-permute-start = (bf16[2,512]{1,0:T(2,128)(2,1)S(1)}, bf16[2,512]{1,0:T(2,128)(2,1)S(1)}, u32[]{:S(2)}, u32[]{:S(2)}) collective-permute-start(bf16[2,512]{1,0:T(2,128)(2,1)S(1)} %shard_map.109), channel_id=1, source_target_pairs={{0,1},{1,2},{2,3},{4,5},{5,6},{6,7},{8,9},{9,10},{10,11},{12,13},{... | collective-permute-start | bytes 6152 | tf_op jit(solution)/shard_map/ppermute | solution.py:467
  7.2 2.8 %shard_map.110 = (bf16[384,2048]{1,0:T(8,128)(2,1)S(1)}, bf16[384,512]{1,0:T(8,128)(2,1)S(1)}, bf16[384,256]{1,0:T(8,128)(2,1)S(1)}, bf16[256,384]{1,0:T(8,128)(...) custom-call(s32[19]{0:T(128)S(1)} %stack.67.refs_0_, ...), custom_call_target="tpu_custom_call" | custom-call | tf_op jit(solution)/shard_map/pallas_call | solution.py:48
  10.1 1.2 %shard_map.111 = (bf16[384,2048]{1,0:T(8,128)(2,1)S(1)}, bf16[384,512]{1,0:T(8,128)(2,1)S(1)}, bf16[384,256]{1,0:T(8,128)(2,1)S(1)}, bf16[256,384]{1,0:T(8,128)(...) custom-call(s32[19]{0:T(128)S(1)} %stack.67.refs_0_, ...), custom_call_target="tpu_custom_call", output_to_operand_aliasing={{0}: (6, {}), {1}: (7, {}), {2}: (8, {}), {3}: (9, {}), {4}... | custom-call | tf_op jit(solution)/shard_map/pallas_call | solution.py:48
  11.4 1.2 %shard_map.112 = (f32[2048,128]{1,0:T(8,128)S(1)}, f32[512,128]{1,0:T(8,128)S(1)}, bf16[384,512]{1,0:T(8,128)(2,1)S(1)}, f32[32,128]{1,0:T(8,128)S(1)}, bf16[16,512]{1,0:T(8,128)(2,1)S(1)}) custom-call(s32[19]{0:T(128)S(1)} %stack.67.refs_0_, bf16[256,384]{1,0:T(8,128)(2,1)S(1)} %get-tuple-element.65.refs_1_, ...), custom_call_target="tpu_custom_call" | custom-call | tf_op jit(solution)/shard_map/pallas_call | solution.py:48
  12.6 1.2 %collective-permute-done.1.refs_1_ = bf16[3360,128]{1,0:T(8,128)(2,1)S(1)} collective-permute-done((bf16[3360,128]{1,0:T(8,128)(2,1)S(1)}, bf16[3360,128]{1,0:T(8,128)(2,1)S(1)}, u32[]{:S(2)}, u32[]{:S(2)}) %collective-permute-start.1) | collective-permute-done | bytes 860192 | tf_op jit(solution)/shard_map/ppermute | solution.py:478
  13.8 1.2 %shard_map.113.refs_5_ = bf16[544,256]{1,0:T(8,128)(2,1)S(1)} custom-call(s32[19]{0:T(128)S(1)} %stack.67.refs_0_, bf16[3360,128]{1,0:T(8,128)(2,1)S(1)} %collective-permute-done.1.refs_1_, bf16[400,256]{1,0:T(8,128)(2,1)S(1)} %get-tuple-element.71.refs_2_, bf16[16,512]{1,0:T(8,128)(2,1)S(1)} %get-tuple-element.72.refs_3_), custom_call_target="tpu_custom_call" | custom-call | tf_op jit(solution)/shard_map/pallas_call | solution.py:48
  15.0 1.6 %collective-permute-start.2 = (bf16[544,256]{1,0:T(8,128)(2,1)S(1)}, bf16[544,256]{1,0:T(8,128)(2,1)S(1)}, u32[]{:S(2)}, u32[]{:S(2)}) collective-permute-start(bf16[544,256]{1,0:T(8,128)(2,1)S(1)} %shard_map.113.refs_5_), channel_id=1, source_target_pairs={{0,1},{1,0},{2,3},{3,2},{4,6},{5,7},{6,4},{7,5},{8,9},{9,8},{10,11... | collective-permute-start | bytes 835592 | tf_op jit(solution)/shard_map/ppermute | solution.py:478
  16.6 0.7 %shard_map.114 = (bf16[1024,128]{1,0:T(8,128)(2,1)S(1)}, bf16[288,128]{1,0:T(8,128)(2,1)S(1)}, f32[1024,128]{1,0:T(8,128)S(1)}, f32[288,128]{1,0:T(8,128)S(1)}) custom-call(s32[19]{0:T(128)S(1)} %stack.67.refs_0_, bf16[3360,128]{1,0:T(8,128)(2,1)S(1)} %collective-permute-done.1.refs_1_, f32[2048,128]{1,0:T(8,128)S(1)} %get-tuple-element.73.refs_2_, ...), custom_call_target="tpu_custom_call" | custom-call | tf_op jit(solution)/shard_map/pallas_call | solution.py:48
  17.3 1.6 %collective-permute-start.3 = (bf16[1024,128]{1,0:T(8,128)(2,1)S(1)}, bf16[1024,128]{1,0:T(8,128)(2,1)S(1)}, u32[]{:S(2)}, u32[]{:S(2)}) collective-permute-start(bf16[1024,128]{1,0:T(8,128)(2,1)S(1)} %get-tuple-element.76.refs_4_), channel_id=1, source_target_pairs={{0,8},{1,9},{2,10},{3,11},{4,20},{5,21},{6,22},{7,23},{8,0},{9,1},... | collective-permute-start | bytes 786440 | tf_op jit(solution)/shard_map/ppermute | solution.py:478
  19.4 1.2 %shard_map.115.refs_5_.refs_2_ = f32[544,256]{1,0:T(8,128)S(1)} custom-call(s32[19]{0:T(128)S(1)} %stack.67.refs_0_, bf16[3360,128]{1,0:T(8,128)(2,1)S(1)} %collective-permute-done.1.refs_1_, bf16[400,256]{1,0:T(8,128)(2,1)S(1)} %get-tuple-element.71.refs_2_, bf16[16,512]{1,0:T(8,128)(2,1)S(1)} %get-tuple-element.72.refs_3_, ...), custom_call_target="tpu_custom_call" | custom-call | tf_op jit(solution)/shard_map/pallas_call | solution.py:48
  20.6 4.0 %collective-permute-done.4.refs_2_ = bf16[288,128]{1,0:T(8,128)(2,1)S(1)} collective-permute-done((bf16[288,128]{1,0:T(8,128)(2,1)S(1)}, bf16[288,128]{1,0:T(8,128)(2,1)S(1)}, u32[]{:S(2)}, u32[]{:S(2)}) %collective-permute-start.4) | collective-permute-done | bytes 73760 | tf_op jit(solution)/shard_map/ppermute | solution.py:478
  24.5 0.6 %shard_map.116 = (bf16[800,128]{1,0:T(8,128)(2,1)S(1)}, f32[512,128]{1,0:T(8,128)S(1)}, f32[288,128]{1,0:T(8,128)S(1)}) custom-call(s32[19]{0:T(128)S(1)} %stack.67.refs_0_, bf16[1024,128]{1,0:T(8,128)(2,1)S(1)} %collective-permute-done.3.refs_1_, bf16[288,128]{1,0:T(8,128)(2,1)S(1)} %collective-permute-done.4.refs_2_, ...), custom_call_target="tpu_custom_call" | custom-call | tf_op jit(solution)/shard_map/pallas_call | solution.py:48
  25.2 1.6 %collective-permute-start.6 = (bf16[800,128]{1,0:T(8,128)(2,1)S(1)}, bf16[800,128]{1,0:T(8,128)(2,1)S(1)}, u32[]{:S(2)}, u32[]{:S(2)}) collective-permute-start(bf16[800,128]{1,0:T(8,128)(2,1)S(1)} %get-tuple-element.80.refs_4_), channel_id=1, source_target_pairs={{0,16},{1,17},{2,18},{3,19},{4,12},{5,13},{6,14},{7,15},{8,24},{9,... | collective-permute-start | bytes 614408 | tf_op jit(solution)/shard_map/ppermute | solution.py:478
  26.7 0.6 %shard_map.117 = (bf16[272,256]{1,0:T(8,128)(2,1)S(1)}, f32[272,256]{1,0:T(8,128)S(1)}, bf16[16,512]{1,0:T(8,128)(2,1)S(1)}) custom-call(s32[19]{0:T(128)S(1)} %stack.67.refs_0_, bf16[544,256]{1,0:T(8,128)(2,1)S(1)} %collective-permute-done.2.refs_6_.refs_1_, f32[544,256]{1,0:T(8,128)S(1)} %shard_map.115.refs_5_.refs_2_, ...), custom_call_target="tpu_custom_call" | custom-call | tf_op jit(solution)/shard_map/pallas_call | solution.py:48
  27.4 1.7 %collective-permute-start.5 = (bf16[272,256]{1,0:T(8,128)(2,1)S(1)}, bf16[272,256]{1,0:T(8,128)(2,1)S(1)}, u32[]{:S(2)}, u32[]{:S(2)}) collective-permute-start(bf16[272,256]{1,0:T(8,128)(2,1)S(1)} %get-tuple-element.81.refs_5_), channel_id=1, source_target_pairs={{0,2},{1,3},{2,0},{3,1},{4,5},{5,4},{6,7},{7,6},{8,10},{9,11},{10,... | collective-permute-start | bytes 417800 | tf_op jit(solution)/shard_map/ppermute | solution.py:478
  29.1 1.9 %collective-permute-done.6.refs_1_.refs_2_ = bf16[800,128]{1,0:T(8,128)(2,1)S(1)} collective-permute-done((bf16[800,128]{1,0:T(8,128)(2,1)S(1)}, bf16[800,128]{1,0:T(8,128)(2,1)S(1)}, u32[]{:S(2)}, u32[]{:S(2)}) %collective-permute-start.6) | collective-permute-done | bytes 204832 | tf_op jit(solution)/shard_map/ppermute | solution.py:478
  31.0 0.7 %shard_map.118 = (bf16[544,128]{1,0:T(8,128)(2,1)S(1)}, f32[256,128]{1,0:T(8,128)S(1)}, f32[288,128]{1,0:T(8,128)S(1)}) custom-call(s32[19]{0:T(128)S(1)} %stack.67.refs_0_, bf16[800,128]{1,0:T(8,128)(2,1)S(1)} %collective-permute-done.6.refs_1_.refs_2_, bf16[800,128]{1,0:T(8,128)(2,1)S(1)} %collective-permute-done.6.refs_1_.refs_2_, ...), custom_call_target="tpu_custom_call" | custom-call | tf_op jit(solution)/shard_map/pallas_call | solution.py:48
  31.7 1.8 %collective-permute-start.8 = (bf16[544,128]{1,0:T(8,128)(2,1)S(1)}, bf16[544,128]{1,0:T(8,128)(2,1)S(1)}, u32[]{:S(2)}, u32[]{:S(2)}) collective-permute-start(bf16[544,128]{1,0:T(8,128)(2,1)S(1)} %get-tuple-element.86.refs_4_), channel_id=1, source_target_pairs={{0,2},{1,3},{2,0},{3,1},{4,5},{5,4},{6,7},{7,6},{8,10},{9,11},{10,... | collective-permute-start | bytes 417800 | tf_op jit(solution)/shard_map/ppermute | solution.py:478
  33.4 1.6 %collective-permute-done.5.refs_1_ = bf16[272,256]{1,0:T(8,128)(2,1)S(1)} collective-permute-done((bf16[272,256]{1,0:T(8,128)(2,1)S(1)}, bf16[272,256]{1,0:T(8,128)(2,1)S(1)}, u32[]{:S(2)}, u32[]{:S(2)}) %collective-permute-start.5) | collective-permute-done | bytes 139296 | tf_op jit(solution)/shard_map/ppermute | solution.py:478
  35.0 0.6 %shard_map.119 = (bf16[272,256]{1,0:T(8,128)(2,1)S(1)}, f32[272,256]{1,0:T(8,128)S(1)}, bf16[16,512]{1,0:T(8,128)(2,1)S(1)}) custom-call(s32[19]{0:T(128)S(1)} %stack.67.refs_0_, bf16[272,256]{1,0:T(8,128)(2,1)S(1)} %collective-permute-done.5.refs_1_, f32[272,256]{1,0:T(8,128)S(1)} %get-tuple-element.82.refs_2_, ...), custom_call_target="tpu_custom_call" | custom-call | tf_op jit(solution)/shard_map/pallas_call | solution.py:48
  35.6 1.6 %collective-permute-start.7 = (bf16[272,256]{1,0:T(8,128)(2,1)S(1)}, bf16[272,256]{1,0:T(8,128)(2,1)S(1)}, u32[]{:S(2)}, u32[]{:S(2)}) collective-permute-start(bf16[272,256]{1,0:T(8,128)(2,1)S(1)} %get-tuple-element.88.refs_5_), channel_id=1, source_target_pairs={{0,8},{1,9},{2,10},{3,11},{4,20},{5,21},{6,22},{7,23},{8,0},{9,1},... | collective-permute-start | bytes 417800 | tf_op jit(solution)/shard_map/ppermute | solution.py:478
  37.1 2.0 %collective-permute-done.8.refs_1_.refs_2_ = bf16[544,128]{1,0:T(8,128)(2,1)S(1)} collective-permute-done((bf16[544,128]{1,0:T(8,128)(2,1)S(1)}, bf16[544,128]{1,0:T(8,128)(2,1)S(1)}, u32[]{:S(2)}, u32[]{:S(2)}) %collective-permute-start.8) | collective-permute-done | bytes 139296 | tf_op jit(solution)/shard_map/ppermute | solution.py:478
  39.9 0.8 %collective-permute-done.7.refs_1_ = bf16[272,256]{1,0:T(8,128)(2,1)S(1)} collective-permute-done((bf16[272,256]{1,0:T(8,128)(2,1)S(1)}, bf16[272,256]{1,0:T(8,128)(2,1)S(1)}, u32[]{:S(2)}, u32[]{:S(2)}) %collective-permute-start.7) | collective-permute-done | bytes 139296 | tf_op jit(solution)/shard_map/ppermute | solution.py:478
  41.3 0.9 %collective-permute-start.10 = (bf16[272,256]{1,0:T(8,128)(2,1)S(1)}, bf16[272,256]{1,0:T(8,128)(2,1)S(1)}, u32[]{:S(2)}, u32[]{:S(2)}) collective-permute-start(bf16[272,256]{1,0:T(8,128)(2,1)S(1)} %get-tuple-element.93.refs_4_), channel_id=1, source_target_pairs={{0,16},{1,17},{2,18},{3,19},{4,12},{5,13},{6,14},{7,15},{8,24},{9,... | collective-permute-start | bytes 417800 | tf_op jit(solution)/shard_map/ppermute | solution.py:478
  42.2 2.6 %shard_map.122 = (bf16[768,512]{1,0:T(8,128)(2,1)}, f32[8,128]{1,0:T(8,128)S(1)}) custom-call(s32[19]{0:T(128)S(1)} %stack.67.refs_0_, bf16[384,512]{1,0:T(8,128)(2,1)S(1)} %get-tuple-element.70.refs_1_, bf16[16,512]{1,0:T(8,128)(2,1)S(1)} %get-tuple-element.87.refs_2_, bf16[2048,512]{1,0:T(8,128)(2,1)S(1)} %copy-done, ...), custom_call_target="tpu_custom_call" | custom-call | tf_op jit(solution)/shard_map/pallas_call | solution.py:48
  44.8 1.7 %collective-permute-done.10.refs_4_ = bf16[272,256]{1,0:T(8,128)(2,1)S(1)} collective-permute-done((bf16[272,256]{1,0:T(8,128)(2,1)S(1)}, bf16[272,256]{1,0:T(8,128)(2,1)S(1)}, u32[]{:S(2)}, u32[]{:S(2)}) %collective-permute-start.10) | collective-permute-done | bytes 139296 | tf_op jit(solution)/shard_map/ppermute | solution.py:478
  46.4 0.7 %shard_map.123 = (f32[256,128]{1,0:T(8,128)S(1)}, bf16[256,128]{1,0:T(8,128)(2,1)S(1)}, bf16[832,128]{1,0:T(8,128)(2,1)S(1)}) custom-call(s32[19]{0:T(128)S(1)} %stack.67.refs_0_, bf16[560,128]{1,0:T(8,128)(2,1)S(1)} %collective-permute-done.9.refs_1_, f32[256,128]{1,0:T(8,128)S(1)} %get-tuple-element.95.refs_2_, f32[288,128]{1,0:T(8,128)S(1)} %get-tuple-element.96.refs_3_, ...), custom_call_target="tpu_custom_call" | custom-call | tf_op jit(solution)/shard_map/pallas_call | solution.py:48
  47.2 1.6 %collective-permute-start.13 = (bf16[256,128]{1,0:T(8,128)(2,1)S(1)}, bf16[256,128]{1,0:T(8,128)(2,1)S(1)}, u32[]{:S(2)}, u32[]{:S(2)}) collective-permute-start(bf16[256,128]{1,0:T(8,128)(2,1)S(1)} %get-tuple-element.100.refs_3_.refs_2_), channel_id=1, source_target_pairs={{0,12},{1,13},{2,14},{3,15},{4,16},{5,17},{6,18},{7,19},{8,4},{9,5... | collective-permute-start | bytes 196616 | tf_op jit(solution)/shard_map/ppermute | solution.py:489
  49.3 1.5 %shard_map.124 = (f32[64,512]{1,0:T(8,128)}, f32[8,128]{1,0:T(8,128)S(1)}) custom-call(s32[19]{0:T(128)S(1)} %stack.67.refs_0_, f32[256,128]{1,0:T(8,128)S(1)} %get-tuple-element.99.refs_1_, bf16[512,256]{1,0:T(8,128)(2,1)S(1)} %copy-done.1, bf16[256,128]{1,0:T(8,128)(2,1)S(1)} %get-tuple-element.100.refs_3_.refs_2_), custom_call_target="tpu_custom_call" | custom-call | tf_op jit(solution)/shard_map/pallas_call | solution.py:48
  50.9 2.1 %collective-permute-done.12.refs_4_ = bf16[256,128]{1,0:T(8,128)(2,1)S(1)} collective-permute-done((bf16[256,128]{1,0:T(8,128)(2,1)S(1)}, bf16[256,128]{1,0:T(8,128)(2,1)S(1)}, u32[]{:S(2)}, u32[]{:S(2)}) %collective-permute-start.12) | collective-permute-done | bytes 65568 | tf_op jit(solution)/shard_map/ppermute | solution.py:478
  53.0 1.5 %shard_map.125 = (f32[512,256]{1,0:T(8,128)}, f32[1,512]{1,0:T(1,128)}, bf16[2,256,256]{2,1,0:T(8,128)(2,1)}, f32[2,256]{1,0:T(2,128)}) custom-call(s32[19]{0:T(128)S(1)} %stack.67.refs_0_, bf16[832,128]{1,0:T(8,128)(2,1)S(1)} %get-tuple-element.102.refs_1_, bf16[256,128]{1,0:T(8,128)(2,1)S(1)} %get-tuple-element.100.refs_3_.refs_2_, ...), custom_call_target="tpu_custom_call" | custom-call | tf_op jit(solution)/shard_map/pallas_call | solution.py:48
  (27 shorter events, 3.3 us)
Async XLA Ops:
  1.5 5.7 %copy-start = (bf16[2048,512]{1,0:T(8,128)(2,1)S(1)}, bf16[2048,512]{1,0:T(8,128)(2,1)}, u32[]{:S(2)}) copy-start(bf16[2048,512]{1,0:T(8,128)(2,1)} %refs_3_.1) | copy-start | bytes 6291460
  1.5 5.7 %copy-start.1 = (bf16[512,256]{1,0:T(8,128)(2,1)S(1)}, bf16[512,256]{1,0:T(8,128)(2,1)}, u32[]{:S(2)}) copy-start(bf16[512,256]{1,0:T(8,128)(2,1)} %refs_2_.3) | copy-start | bytes 786436
  1.5 5.7 %copy-start.2 = (bf16[2,1024,256]{2,1,0:T(8,128)(2,1)S(1)}, bf16[2,1024,256]{2,1,0:T(8,128)(2,1)}, u32[]{:S(2)}) copy-start(bf16[2,1024,256]{2,1,0:T(8,128)(2,1)} %refs_5_.3) | copy-start | bytes 3145732
  1.5 5.7 %copy-start.3 = (bf16[768,512]{1,0:T(8,128)(2,1)S(1)}, bf16[768,512]{1,0:T(8,128)(2,1)}, u32[]{:S(2)}) copy-start(bf16[768,512]{1,0:T(8,128)(2,1)} %refs_1_.1) | copy-start | bytes 2359300
  1.5 5.7 %copy-start.4 = (s32[1,2,384]{2,1,0:T(2,128)S(1)}, s32[1,2,384]{2,1,0:T(2,128)}, u32[]{:S(2)}) copy-start(s32[1,2,384]{2,1,0:T(2,128)} %param.7) | copy-start | bytes 9220
  1.5 5.7 %copy-start.5 = (f32[512]{0:T(512)S(1)}, f32[512]{0:T(512)}, u32[]{:S(2)}) copy-start(f32[512]{0:T(512)} %param.9) | copy-start | bytes 6148
  2.1 8.0 %collective-permute-start = (bf16[2,512]{1,0:T(2,128)(2,1)S(1)}, bf16[2,512]{1,0:T(2,128)(2,1)S(1)}, u32[]{:S(2)}, u32[]{:S(2)}) collective-permute-start(bf16[2,512]{1,0:T(2,128)(2,1)S(1)} %shard_map.109), channel_id=1, source_target_pairs={{0,1},{1,2},{2,3},{4,5},{5,6},{6,7},{8,9},{9,10},{10,11},{12,13},{... | collective-permute-start | bytes 6152 | tf_op jit(solution)/shard_map/ppermute | solution.py:467
  11.3 2.5 %collective-permute-start.1 = (bf16[3360,128]{1,0:T(8,128)(2,1)S(1)}, bf16[3360,128]{1,0:T(8,128)(2,1)S(1)}, u32[]{:S(2)}, u32[]{:S(2)}) collective-permute-start(bf16[3360,128]{1,0:T(8,128)(2,1)S(1)} %get-tuple-element.69.refs_6_), channel_id=1, source_target_pairs={{0,4},{1,5},{2,6},{3,7},{4,0},{5,1},{6,2},{7,3},{8,12},{9,13},{10,... | collective-permute-start | bytes 2580488 | tf_op jit(solution)/shard_map/ppermute | solution.py:478
  15.0 9.6 %collective-permute-start.2 = (bf16[544,256]{1,0:T(8,128)(2,1)S(1)}, bf16[544,256]{1,0:T(8,128)(2,1)S(1)}, u32[]{:S(2)}, u32[]{:S(2)}) collective-permute-start(bf16[544,256]{1,0:T(8,128)(2,1)S(1)} %shard_map.113.refs_5_), channel_id=1, source_target_pairs={{0,1},{1,0},{2,3},{3,2},{4,6},{5,7},{6,4},{7,5},{8,9},{9,8},{10,11... | collective-permute-start | bytes 835592 | tf_op jit(solution)/shard_map/ppermute | solution.py:478
  17.3 7.2 %collective-permute-start.3 = (bf16[1024,128]{1,0:T(8,128)(2,1)S(1)}, bf16[1024,128]{1,0:T(8,128)(2,1)S(1)}, u32[]{:S(2)}, u32[]{:S(2)}) collective-permute-start(bf16[1024,128]{1,0:T(8,128)(2,1)S(1)} %get-tuple-element.76.refs_4_), channel_id=1, source_target_pairs={{0,8},{1,9},{2,10},{3,11},{4,20},{5,21},{6,22},{7,23},{8,0},{9,1},... | collective-permute-start | bytes 786440 | tf_op jit(solution)/shard_map/ppermute | solution.py:478
  18.8 5.7 %collective-permute-start.4 = (bf16[288,128]{1,0:T(8,128)(2,1)S(1)}, bf16[288,128]{1,0:T(8,128)(2,1)S(1)}, u32[]{:S(2)}, u32[]{:S(2)}) collective-permute-start(bf16[288,128]{1,0:T(8,128)(2,1)S(1)} %get-tuple-element.77), channel_id=1, source_target_pairs={{0,8},{1,9},{2,10},{3,11},{4,20},{5,21},{6,22},{7,23},{8,0},{9,1},... | collective-permute-start | bytes 221192 | tf_op jit(solution)/shard_map/ppermute | solution.py:478
  25.2 5.8 %collective-permute-start.6 = (bf16[800,128]{1,0:T(8,128)(2,1)S(1)}, bf16[800,128]{1,0:T(8,128)(2,1)S(1)}, u32[]{:S(2)}, u32[]{:S(2)}) collective-permute-start(bf16[800,128]{1,0:T(8,128)(2,1)S(1)} %get-tuple-element.80.refs_4_), channel_id=1, source_target_pairs={{0,16},{1,17},{2,18},{3,19},{4,12},{5,13},{6,14},{7,15},{8,24},{9,... | collective-permute-start | bytes 614408 | tf_op jit(solution)/shard_map/ppermute | solution.py:478
  27.4 7.6 %collective-permute-start.5 = (bf16[272,256]{1,0:T(8,128)(2,1)S(1)}, bf16[272,256]{1,0:T(8,128)(2,1)S(1)}, u32[]{:S(2)}, u32[]{:S(2)}) collective-permute-start(bf16[272,256]{1,0:T(8,128)(2,1)S(1)} %get-tuple-element.81.refs_5_), channel_id=1, source_target_pairs={{0,2},{1,3},{2,0},{3,1},{4,5},{5,4},{6,7},{7,6},{8,10},{9,11},{10,... | collective-permute-start | bytes 417800 | tf_op jit(solution)/shard_map/ppermute | solution.py:478
  31.7 7.5 %collective-permute-start.8 = (bf16[544,128]{1,0:T(8,128)(2,1)S(1)}, bf16[544,128]{1,0:T(8,128)(2,1)S(1)}, u32[]{:S(2)}, u32[]{:S(2)}) collective-permute-start(bf16[544,128]{1,0:T(8,128)(2,1)S(1)} %get-tuple-element.86.refs_4_), channel_id=1, source_target_pairs={{0,2},{1,3},{2,0},{3,1},{4,5},{5,4},{6,7},{7,6},{8,10},{9,11},{10,... | collective-permute-start | bytes 417800 | tf_op jit(solution)/shard_map/ppermute | solution.py:478
  35.6 5.1 %collective-permute-start.7 = (bf16[272,256]{1,0:T(8,128)(2,1)S(1)}, bf16[272,256]{1,0:T(8,128)(2,1)S(1)}, u32[]{:S(2)}, u32[]{:S(2)}) collective-permute-start(bf16[272,256]{1,0:T(8,128)(2,1)S(1)} %get-tuple-element.88.refs_5_), channel_id=1, source_target_pairs={{0,8},{1,9},{2,10},{3,11},{4,20},{5,21},{6,22},{7,23},{8,0},{9,1},... | collective-permute-start | bytes 417800 | tf_op jit(solution)/shard_map/ppermute | solution.py:478
  39.8 6.7 %collective-permute-start.9 = (bf16[560,128]{1,0:T(8,128)(2,1)S(1)}, bf16[560,128]{1,0:T(8,128)(2,1)S(1)}, u32[]{:S(2)}, u32[]{:S(2)}) collective-permute-start(bf16[560,128]{1,0:T(8,128)(2,1)S(1)} %get-tuple-element.92.refs_3_), channel_id=1, source_target_pairs={{0,1},{1,0},{2,3},{3,2},{4,6},{5,7},{6,4},{7,5},{8,9},{9,8},{10,11... | collective-permute-start | bytes 430088 | tf_op jit(solution)/shard_map/ppermute | solution.py:478
  41.3 5.1 %collective-permute-start.10 = (bf16[272,256]{1,0:T(8,128)(2,1)S(1)}, bf16[272,256]{1,0:T(8,128)(2,1)S(1)}, u32[]{:S(2)}, u32[]{:S(2)}) collective-permute-start(bf16[272,256]{1,0:T(8,128)(2,1)S(1)} %get-tuple-element.93.refs_4_), channel_id=1, source_target_pairs={{0,16},{1,17},{2,18},{3,19},{4,12},{5,13},{6,14},{7,15},{8,24},{9,... | collective-permute-start | bytes 417800 | tf_op jit(solution)/shard_map/ppermute | solution.py:478
  47.1 5.9 %collective-permute-start.11 = (bf16[832,128]{1,0:T(8,128)(2,1)S(1)}, bf16[832,128]{1,0:T(8,128)(2,1)S(1)}, u32[]{:S(2)}, u32[]{:S(2)}) collective-permute-start(bf16[832,128]{1,0:T(8,128)(2,1)S(1)} %get-tuple-element.102.refs_1_), channel_id=1, source_target_pairs={{0,4},{1,5},{2,6},{3,7},{4,0},{5,1},{6,2},{7,3},{8,12},{9,13},{10,... | collective-permute-start | bytes 638984 | tf_op jit(solution)/shard_map/ppermute | solution.py:478
  47.2 3.7 %collective-permute-start.13 = (bf16[256,128]{1,0:T(8,128)(2,1)S(1)}, bf16[256,128]{1,0:T(8,128)(2,1)S(1)}, u32[]{:S(2)}, u32[]{:S(2)}) collective-permute-start(bf16[256,128]{1,0:T(8,128)(2,1)S(1)} %get-tuple-element.100.refs_3_.refs_2_), channel_id=1, source_target_pairs={{0,12},{1,13},{2,14},{3,15},{4,16},{5,17},{6,18},{7,19},{8,4},{9,5... | collective-permute-start | bytes 196616 | tf_op jit(solution)/shard_map/ppermute | solution.py:489
  48.8 4.3 %collective-permute-start.12 = (bf16[256,128]{1,0:T(8,128)(2,1)S(1)}, bf16[256,128]{1,0:T(8,128)(2,1)S(1)}, u32[]{:S(2)}, u32[]{:S(2)}) collective-permute-start(bf16[256,128]{1,0:T(8,128)(2,1)S(1)} %get-tuple-element.100.refs_3_.refs_2_), channel_id=1, source_target_pairs={{0,8},{1,9},{2,10},{3,11},{4,20},{5,21},{6,22},{7,23},{8,0},{9,1},... | collective-permute-start | bytes 196616 | tf_op jit(solution)/shard_map/ppermute | solution.py:478

commit v16 on v15

--- a/solution.py
+++ b/solution.py
@@ -516,7 +516,7 @@
     paths[1] += up if turned else up[::-1]
     exchanges = list(zip([("dp", 0)] + paths[0], [("dp", 0)] + paths[1]))
     sums_up = [("dp", b) for b in range(1, dp_bits)]
-    sums_exchanges = list(zip(up + sums_up, up[::-1] + sums_up[::-1]))
+    sums_exchanges = list(zip(up[::-1] + sums_up, up + sums_up[::-1]))
 
     def piece_bit(step):
         axis, b = step
@@ -553,16 +553,16 @@
     places = [2 * core + mine_c, 2 * (1 - core) + other_c, 2 * core + 1 - mine_c, 2 * (1 - core) + 1 - other_c]
     places = [place << (log2(pieces_c) - c_bits) for place in places]
     lists = []
-    for way in ([b for _, b in up], [b for _, b in up[::-1]]):
+    for way in ([b for _, b in up[::-1]], [b for _, b in up]):
         lists.append([sum(((position >> (tm_bits - 1 - j)) & 1) << b for j, b in enumerate(way)) for position in range(tm)])
-    first_bit = on_core([0, tm_bits - 1])
+    first_bit = on_core([tm_bits - 1, 0])
     lead = (at_tm >> first_bit) & 1
     quarters = [on_core([lists[0][j], lists[1][j]]) for j in range(tm // 2)]
     send_codes = [(q + ((1 - lead) << first_bit)) * per_shard for q in quarters]
     keep_codes = [(q + (lead << first_bit)) * per_shard for q in quarters]
     differ = at_tm ^ (at_tm + 1)
     ways = [sum(((differ >> b) & 1) << j for j, b in enumerate(way)) for way in (
-        list(range(tm_bits)), list(reversed(range(tm_bits))))]
+        list(reversed(range(tm_bits))), list(range(tm_bits)))]
     row_code = jnp.where(at_tm + 1 < tm, on_core(ways), 0)
     if turned and not mixed:
         start = ((at_dp * tm + at_tm) * owner_rows) & (LANES - 1)

time: 54.8 us -> 57.5 us (1.049)
  waiting for transfers between devices: 15.3 us -> 18.1 us
    ppermute x12, waiting for transfers between devices: 15.3 us -> 17.6 us  [swapped(): return lax.ppermute(block, ('dp', 'tm'), route)]
  transfers between devices with their start and end apart: 14 -> 14, of which waited for: 9 -> 8; matrix products, arithmetic and copies ran while one was open for 0% -> 0% of each run, Pallas kernels for 24% -> 23%
where the time goes in v16:
time: 57.5 us; the launch traced here: 57.3 us
  Pallas kernels  18.8 us (33%)
  starting transfers between devices  18.7 us (33%)
  waiting for transfers between devices  18.1 us (31%)
  between operations  0.91 us (2%)
  local copies, waits for them, and re-layouts  0.84 us (1%)
    pallas_call x17, Pallas kernels, call(): pl.pallas_call(kernel, out_shape=shown, in_specs=specs, out_specs=[pl.Blo...  18.8 us
    ppermute x12, waiting for transfers between devices, swapped(): return lax.ppermute(block, ('dp', 'tm'), route)  17.6 us
    ppermute x12, starting transfers between devices, swapped(): return lax.ppermute(block, ('dp', 'tm'), route)  11.7 us
    ppermute x1, starting transfers between devices, shifted(): return lax.ppermute(block, axis, route)  5.06 us
    ppermute x1, starting transfers between devices, crossed(): return lax.ppermute(block, ('dp', 'tm'), route)  1.94 us
  transfers between devices with their start and end apart: 14, of which 8 were waited for; matrix products, arithmetic and copies ran while one was open for 0% of the time, Pallas kernels for 23%

profile of v16, /device:TPU:0, one launch (start us, length us, event | category | flops | bytes accessed | tf_op | source)
XLA Modules:
  0.0 57.3 jit_solution(14702141141527826623)
XLA Ops:
  0.7 0.7 %slice.3.refs_1_ = bf16[2,512]{1,0:T(2,128)(2,1)S(1)} slice(bf16[768,512]{1,0:T(8,128)(2,1)} %refs_1_.1), slice={[766:768], [0:512]} | slice | bytes 4096 | tf_op jit(solution)/shard_map/slice | solution.py:579
  2.1 5.1 %collective-permute-start = (bf16[2,512]{1,0:T(2,128)(2,1)S(1)}, bf16[2,512]{1,0:T(2,128)(2,1)S(1)}, u32[]{:S(2)}, u32[]{:S(2)}) collective-permute-start(bf16[2,512]{1,0:T(2,128)(2,1)S(1)} %shard_map.109), channel_id=1, source_target_pairs={{0,1},{1,2},{2,3},{4,5},{5,6},{6,7},{8,9},{9,10},{10,11},{12,13},{... | collective-permute-start | bytes 6152 | tf_op jit(solution)/shard_map/ppermute | solution.py:467
  7.2 2.8 %shard_map.110 = (bf16[384,2048]{1,0:T(8,128)(2,1)S(1)}, bf16[384,512]{1,0:T(8,128)(2,1)S(1)}, bf16[384,256]{1,0:T(8,128)(2,1)S(1)}, bf16[256,384]{1,0:T(8,128)(...) custom-call(s32[19]{0:T(128)S(1)} %stack.67.refs_0_, ...), custom_call_target="tpu_custom_call" | custom-call | tf_op jit(solution)/shard_map/pallas_call | solution.py:48
  10.1 1.2 %shard_map.111 = (bf16[384,2048]{1,0:T(8,128)(2,1)S(1)}, bf16[384,512]{1,0:T(8,128)(2,1)S(1)}, bf16[384,256]{1,0:T(8,128)(2,1)S(1)}, bf16[256,384]{1,0:T(8,128)(...) custom-call(s32[19]{0:T(128)S(1)} %stack.67.refs_0_, ...), custom_call_target="tpu_custom_call", output_to_operand_aliasing={{0}: (6, {}), {1}: (7, {}), {2}: (8, {}), {3}: (9, {}), {4}... | custom-call | tf_op jit(solution)/shard_map/pallas_call | solution.py:48
  11.4 1.2 %shard_map.112 = (f32[2048,128]{1,0:T(8,128)S(1)}, f32[512,128]{1,0:T(8,128)S(1)}, bf16[384,512]{1,0:T(8,128)(2,1)S(1)}, f32[32,128]{1,0:T(8,128)S(1)}, bf16[16,512]{1,0:T(8,128)(2,1)S(1)}) custom-call(s32[19]{0:T(128)S(1)} %stack.67.refs_0_, bf16[256,384]{1,0:T(8,128)(2,1)S(1)} %get-tuple-element.65.refs_1_, ...), custom_call_target="tpu_custom_call" | custom-call | tf_op jit(solution)/shard_map/pallas_call | solution.py:48
  12.6 1.2 %collective-permute-done.1.refs_1_ = bf16[3360,128]{1,0:T(8,128)(2,1)S(1)} collective-permute-done((bf16[3360,128]{1,0:T(8,128)(2,1)S(1)}, bf16[3360,128]{1,0:T(8,128)(2,1)S(1)}, u32[]{:S(2)}, u32[]{:S(2)}) %collective-permute-start.1) | collective-permute-done | bytes 860192 | tf_op jit(solution)/shard_map/ppermute | solution.py:478
  13.8 1.2 %shard_map.113.refs_5_ = bf16[544,256]{1,0:T(8,128)(2,1)S(1)} custom-call(s32[19]{0:T(128)S(1)} %stack.67.refs_0_, bf16[3360,128]{1,0:T(8,128)(2,1)S(1)} %collective-permute-done.1.refs_1_, bf16[400,256]{1,0:T(8,128)(2,1)S(1)} %get-tuple-element.71.refs_2_, bf16[16,512]{1,0:T(8,128)(2,1)S(1)} %get-tuple-element.72.refs_3_), custom_call_target="tpu_custom_call" | custom-call | tf_op jit(solution)/shard_map/pallas_call | solution.py:48
  15.0 2.7 %collective-permute-start.2 = (bf16[544,256]{1,0:T(8,128)(2,1)S(1)}, bf16[544,256]{1,0:T(8,128)(2,1)S(1)}, u32[]{:S(2)}, u32[]{:S(2)}) collective-permute-start(bf16[544,256]{1,0:T(8,128)(2,1)S(1)} %shard_map.113.refs_5_), channel_id=1, source_target_pairs={{0,2},{1,3},{2,0},{3,1},{4,5},{5,4},{6,7},{7,6},{8,10},{9,11},{10,... | collective-permute-start | bytes 835592 | tf_op jit(solution)/shard_map/ppermute | solution.py:478
  17.6 0.7 %shard_map.114 = (bf16[1024,128]{1,0:T(8,128)(2,1)S(1)}, bf16[288,128]{1,0:T(8,128)(2,1)S(1)}, f32[1024,128]{1,0:T(8,128)S(1)}, f32[288,128]{1,0:T(8,128)S(1)}) custom-call(s32[19]{0:T(128)S(1)} %stack.67.refs_0_, bf16[3360,128]{1,0:T(8,128)(2,1)S(1)} %collective-permute-done.1.refs_1_, f32[2048,128]{1,0:T(8,128)S(1)} %get-tuple-element.73.refs_2_, ...), custom_call_target="tpu_custom_call" | custom-call | tf_op jit(solution)/shard_map/pallas_call | solution.py:48
  18.3 1.6 %collective-permute-start.3 = (bf16[1024,128]{1,0:T(8,128)(2,1)S(1)}, bf16[1024,128]{1,0:T(8,128)(2,1)S(1)}, u32[]{:S(2)}, u32[]{:S(2)}) collective-permute-start(bf16[1024,128]{1,0:T(8,128)(2,1)S(1)} %get-tuple-element.76.refs_4_), channel_id=1, source_target_pairs={{0,8},{1,9},{2,10},{3,11},{4,20},{5,21},{6,22},{7,23},{8,0},{9,1},... | collective-permute-start | bytes 786440 | tf_op jit(solution)/shard_map/ppermute | solution.py:478
  20.4 1.2 %shard_map.115.refs_5_.refs_2_ = f32[544,256]{1,0:T(8,128)S(1)} custom-call(s32[19]{0:T(128)S(1)} %stack.67.refs_0_, bf16[3360,128]{1,0:T(8,128)(2,1)S(1)} %collective-permute-done.1.refs_1_, bf16[400,256]{1,0:T(8,128)(2,1)S(1)} %get-tuple-element.71.refs_2_, bf16[16,512]{1,0:T(8,128)(2,1)S(1)} %get-tuple-element.72.refs_3_, ...), custom_call_target="tpu_custom_call" | custom-call | tf_op jit(solution)/shard_map/pallas_call | solution.py:48
  21.6 4.0 %collective-permute-done.4.refs_2_ = bf16[288,128]{1,0:T(8,128)(2,1)S(1)} collective-permute-done((bf16[288,128]{1,0:T(8,128)(2,1)S(1)}, bf16[288,128]{1,0:T(8,128)(2,1)S(1)}, u32[]{:S(2)}, u32[]{:S(2)}) %collective-permute-start.4) | collective-permute-done | bytes 73760 | tf_op jit(solution)/shard_map/ppermute | solution.py:478
  25.5 0.6 %shard_map.116 = (bf16[800,128]{1,0:T(8,128)(2,1)S(1)}, f32[512,128]{1,0:T(8,128)S(1)}, f32[288,128]{1,0:T(8,128)S(1)}) custom-call(s32[19]{0:T(128)S(1)} %stack.67.refs_0_, bf16[1024,128]{1,0:T(8,128)(2,1)S(1)} %collective-permute-done.3.refs_1_, bf16[288,128]{1,0:T(8,128)(2,1)S(1)} %collective-permute-done.4.refs_2_, ...), custom_call_target="tpu_custom_call" | custom-call | tf_op jit(solution)/shard_map/pallas_call | solution.py:48
  26.2 1.6 %collective-permute-start.6 = (bf16[800,128]{1,0:T(8,128)(2,1)S(1)}, bf16[800,128]{1,0:T(8,128)(2,1)S(1)}, u32[]{:S(2)}, u32[]{:S(2)}) collective-permute-start(bf16[800,128]{1,0:T(8,128)(2,1)S(1)} %get-tuple-element.80.refs_4_), channel_id=1, source_target_pairs={{0,16},{1,17},{2,18},{3,19},{4,12},{5,13},{6,14},{7,15},{8,24},{9,... | collective-permute-start | bytes 614408 | tf_op jit(solution)/shard_map/ppermute | solution.py:478
  27.8 0.6 %shard_map.117 = (bf16[272,256]{1,0:T(8,128)(2,1)S(1)}, f32[272,256]{1,0:T(8,128)S(1)}, bf16[16,512]{1,0:T(8,128)(2,1)S(1)}) custom-call(s32[19]{0:T(128)S(1)} %stack.67.refs_0_, bf16[544,256]{1,0:T(8,128)(2,1)S(1)} %collective-permute-done.2.refs_6_.refs_1_, f32[544,256]{1,0:T(8,128)S(1)} %shard_map.115.refs_5_.refs_2_, ...), custom_call_target="tpu_custom_call" | custom-call | tf_op jit(solution)/shard_map/pallas_call | solution.py:48
  28.4 0.8 %collective-permute-start.5 = (bf16[272,256]{1,0:T(8,128)(2,1)S(1)}, bf16[272,256]{1,0:T(8,128)(2,1)S(1)}, u32[]{:S(2)}, u32[]{:S(2)}) collective-permute-start(bf16[272,256]{1,0:T(8,128)(2,1)S(1)} %get-tuple-element.81.refs_5_), channel_id=1, source_target_pairs={{0,1},{1,0},{2,3},{3,2},{4,6},{5,7},{6,4},{7,5},{8,9},{9,8},{10,11... | collective-permute-start | bytes 417800 | tf_op jit(solution)/shard_map/ppermute | solution.py:478
  29.2 2.8 %collective-permute-done.6.refs_1_.refs_2_ = bf16[800,128]{1,0:T(8,128)(2,1)S(1)} collective-permute-done((bf16[800,128]{1,0:T(8,128)(2,1)S(1)}, bf16[800,128]{1,0:T(8,128)(2,1)S(1)}, u32[]{:S(2)}, u32[]{:S(2)}) %collective-permute-start.6) | collective-permute-done | bytes 204832 | tf_op jit(solution)/shard_map/ppermute | solution.py:478
  32.0 0.7 %shard_map.118 = (bf16[544,128]{1,0:T(8,128)(2,1)S(1)}, f32[256,128]{1,0:T(8,128)S(1)}, f32[288,128]{1,0:T(8,128)S(1)}) custom-call(s32[19]{0:T(128)S(1)} %stack.67.refs_0_, bf16[800,128]{1,0:T(8,128)(2,1)S(1)} %collective-permute-done.6.refs_1_.refs_2_, bf16[800,128]{1,0:T(8,128)(2,1)S(1)} %collective-permute-done.6.refs_1_.refs_2_, ...), custom_call_target="tpu_custom_call" | custom-call | tf_op jit(solution)/shard_map/pallas_call | solution.py:48
  32.7 0.8 %collective-permute-start.8 = (bf16[544,128]{1,0:T(8,128)(2,1)S(1)}, bf16[544,128]{1,0:T(8,128)(2,1)S(1)}, u32[]{:S(2)}, u32[]{:S(2)}) collective-permute-start(bf16[544,128]{1,0:T(8,128)(2,1)S(1)} %get-tuple-element.86.refs_4_), channel_id=1, source_target_pairs={{0,2},{1,3},{2,0},{3,1},{4,5},{5,4},{6,7},{7,6},{8,10},{9,11},{10,... | collective-permute-start | bytes 417800 | tf_op jit(solution)/shard_map/ppermute | solution.py:478
  33.5 2.0 %collective-permute-done.5.refs_1_ = bf16[272,256]{1,0:T(8,128)(2,1)S(1)} collective-permute-done((bf16[272,256]{1,0:T(8,128)(2,1)S(1)}, bf16[272,256]{1,0:T(8,128)(2,1)S(1)}, u32[]{:S(2)}, u32[]{:S(2)}) %collective-permute-start.5) | collective-permute-done | bytes 139296 | tf_op jit(solution)/shard_map/ppermute | solution.py:478
  35.5 0.6 %shard_map.119 = (bf16[272,256]{1,0:T(8,128)(2,1)S(1)}, f32[272,256]{1,0:T(8,128)S(1)}, bf16[16,512]{1,0:T(8,128)(2,1)S(1)}) custom-call(s32[19]{0:T(128)S(1)} %stack.67.refs_0_, bf16[272,256]{1,0:T(8,128)(2,1)S(1)} %collective-permute-done.5.refs_1_, f32[272,256]{1,0:T(8,128)S(1)} %get-tuple-element.82.refs_2_, ...), custom_call_target="tpu_custom_call" | custom-call | tf_op jit(solution)/shard_map/pallas_call | solution.py:48
  36.1 0.9 %collective-permute-start.7 = (bf16[272,256]{1,0:T(8,128)(2,1)S(1)}, bf16[272,256]{1,0:T(8,128)(2,1)S(1)}, u32[]{:S(2)}, u32[]{:S(2)}) collective-permute-start(bf16[272,256]{1,0:T(8,128)(2,1)S(1)} %get-tuple-element.88.refs_5_), channel_id=1, source_target_pairs={{0,8},{1,9},{2,10},{3,11},{4,20},{5,21},{6,22},{7,23},{8,0},{9,1},... | collective-permute-start | bytes 417800 | tf_op jit(solution)/shard_map/ppermute | solution.py:478
  37.0 5.1 %collective-permute-done.8.refs_1_.refs_2_ = bf16[544,128]{1,0:T(8,128)(2,1)S(1)} collective-permute-done((bf16[544,128]{1,0:T(8,128)(2,1)S(1)}, bf16[544,128]{1,0:T(8,128)(2,1)S(1)}, u32[]{:S(2)}, u32[]{:S(2)}) %collective-permute-start.8) | collective-permute-done | bytes 139296 | tf_op jit(solution)/shard_map/ppermute | solution.py:478
  42.1 0.6 %shard_map.120 = (bf16[560,128]{1,0:T(8,128)(2,1)S(1)}, f32[256,128]{1,0:T(8,128)S(1)}, f32[288,128]{1,0:T(8,128)S(1)}) custom-call(s32[19]{0:T(128)S(1)} %stack.67.refs_0_, bf16[544,128]{1,0:T(8,128)(2,1)S(1)} %collective-permute-done.8.refs_1_.refs_2_, bf16[544,128]{1,0:T(8,128)(2,1)S(1)} %collective-permute-done.8.refs_1_.refs_2_, ...), custom_call_target="tpu_custom_call" | custom-call | tf_op jit(solution)/shard_map/pallas_call | solution.py:48
  42.8 0.6 %shard_map.121 = (bf16[272,256]{1,0:T(8,128)(2,1)S(1)}, f32[272,256]{1,0:T(8,128)S(1)}) custom-call(s32[19]{0:T(128)S(1)} %stack.67.refs_0_, bf16[272,256]{1,0:T(8,128)(2,1)S(1)} %collective-permute-done.7.refs_1_, f32[272,256]{1,0:T(8,128)S(1)} %get-tuple-element.89.refs_2_, bf16[560,128]{1,0:T(8,128)(2,1)S(1)} %get-tuple-element.92.refs_3_), custom_call_target="tpu_custom_call" | custom-call | tf_op jit(solution)/shard_map/pallas_call | solution.py:48
  43.4 2.4 %collective-permute-start.10 = (bf16[272,256]{1,0:T(8,128)(2,1)S(1)}, bf16[272,256]{1,0:T(8,128)(2,1)S(1)}, u32[]{:S(2)}, u32[]{:S(2)}) collective-permute-start(bf16[272,256]{1,0:T(8,128)(2,1)S(1)} %get-tuple-element.93.refs_4_), channel_id=1, source_target_pairs={{0,16},{1,17},{2,18},{3,19},{4,12},{5,13},{6,14},{7,15},{8,24},{9,... | collective-permute-start | bytes 417800 | tf_op jit(solution)/shard_map/ppermute | solution.py:478
  45.8 2.6 %shard_map.122 = (bf16[768,512]{1,0:T(8,128)(2,1)}, f32[8,128]{1,0:T(8,128)S(1)}) custom-call(s32[19]{0:T(128)S(1)} %stack.67.refs_0_, bf16[384,512]{1,0:T(8,128)(2,1)S(1)} %get-tuple-element.70.refs_1_, bf16[16,512]{1,0:T(8,128)(2,1)S(1)} %get-tuple-element.87.refs_2_, bf16[2048,512]{1,0:T(8,128)(2,1)S(1)} %copy-done, ...), custom_call_target="tpu_custom_call" | custom-call | tf_op jit(solution)/shard_map/pallas_call | solution.py:48
  48.8 0.7 %shard_map.123 = (f32[256,128]{1,0:T(8,128)S(1)}, bf16[256,128]{1,0:T(8,128)(2,1)S(1)}, bf16[832,128]{1,0:T(8,128)(2,1)S(1)}) custom-call(s32[19]{0:T(128)S(1)} %stack.67.refs_0_, bf16[560,128]{1,0:T(8,128)(2,1)S(1)} %collective-permute-done.9.refs_1_, f32[256,128]{1,0:T(8,128)S(1)} %get-tuple-element.95.refs_2_, f32[288,128]{1,0:T(8,128)S(1)} %get-tuple-element.96.refs_3_, ...), custom_call_target="tpu_custom_call" | custom-call | tf_op jit(solution)/shard_map/pallas_call | solution.py:48
  49.6 1.9 %collective-permute-start.13 = (bf16[256,128]{1,0:T(8,128)(2,1)S(1)}, bf16[256,128]{1,0:T(8,128)(2,1)S(1)}, u32[]{:S(2)}, u32[]{:S(2)}) collective-permute-start(bf16[256,128]{1,0:T(8,128)(2,1)S(1)} %get-tuple-element.100.refs_3_.refs_2_), channel_id=1, source_target_pairs={{0,12},{1,13},{2,14},{3,15},{4,16},{5,17},{6,18},{7,19},{8,4},{9,5... | collective-permute-start | bytes 196616 | tf_op jit(solution)/shard_map/ppermute | solution.py:489
  51.7 1.5 %shard_map.124 = (f32[64,512]{1,0:T(8,128)}, f32[8,128]{1,0:T(8,128)S(1)}) custom-call(s32[19]{0:T(128)S(1)} %stack.67.refs_0_, f32[256,128]{1,0:T(8,128)S(1)} %get-tuple-element.99.refs_1_, bf16[512,256]{1,0:T(8,128)(2,1)S(1)} %copy-done.1, bf16[256,128]{1,0:T(8,128)(2,1)S(1)} %get-tuple-element.100.refs_3_.refs_2_), custom_call_target="tpu_custom_call" | custom-call | tf_op jit(solution)/shard_map/pallas_call | solution.py:48
  53.6 2.1 %collective-permute-done.12.refs_4_ = bf16[256,128]{1,0:T(8,128)(2,1)S(1)} collective-permute-done((bf16[256,128]{1,0:T(8,128)(2,1)S(1)}, bf16[256,128]{1,0:T(8,128)(2,1)S(1)}, u32[]{:S(2)}, u32[]{:S(2)}) %collective-permute-start.12) | collective-permute-done | bytes 65568 | tf_op jit(solution)/shard_map/ppermute | solution.py:478
  55.8 1.5 %shard_map.125 = (f32[512,256]{1,0:T(8,128)}, f32[1,512]{1,0:T(1,128)}, bf16[2,256,256]{2,1,0:T(8,128)(2,1)}, f32[2,256]{1,0:T(2,128)}) custom-call(s32[19]{0:T(128)S(1)} %stack.67.refs_0_, bf16[832,128]{1,0:T(8,128)(2,1)S(1)} %get-tuple-element.102.refs_1_, bf16[256,128]{1,0:T(8,128)(2,1)S(1)} %get-tuple-element.100.refs_3_.refs_2_, ...), custom_call_target="tpu_custom_call" | custom-call | tf_op jit(solution)/shard_map/pallas_call | solution.py:48
  (27 shorter events, 2.5 us)
Async XLA Ops:
  1.5 5.7 %copy-start = (bf16[2048,512]{1,0:T(8,128)(2,1)S(1)}, bf16[2048,512]{1,0:T(8,128)(2,1)}, u32[]{:S(2)}) copy-start(bf16[2048,512]{1,0:T(8,128)(2,1)} %refs_3_.1) | copy-start | bytes 6291460
  1.5 5.7 %copy-start.1 = (bf16[512,256]{1,0:T(8,128)(2,1)S(1)}, bf16[512,256]{1,0:T(8,128)(2,1)}, u32[]{:S(2)}) copy-start(bf16[512,256]{1,0:T(8,128)(2,1)} %refs_2_.3) | copy-start | bytes 786436
  1.5 5.7 %copy-start.2 = (bf16[2,1024,256]{2,1,0:T(8,128)(2,1)S(1)}, bf16[2,1024,256]{2,1,0:T(8,128)(2,1)}, u32[]{:S(2)}) copy-start(bf16[2,1024,256]{2,1,0:T(8,128)(2,1)} %refs_5_.3) | copy-start | bytes 3145732
  1.5 5.7 %copy-start.3 = (bf16[768,512]{1,0:T(8,128)(2,1)S(1)}, bf16[768,512]{1,0:T(8,128)(2,1)}, u32[]{:S(2)}) copy-start(bf16[768,512]{1,0:T(8,128)(2,1)} %refs_1_.1) | copy-start | bytes 2359300
  1.5 5.7 %copy-start.4 = (s32[1,2,384]{2,1,0:T(2,128)S(1)}, s32[1,2,384]{2,1,0:T(2,128)}, u32[]{:S(2)}) copy-start(s32[1,2,384]{2,1,0:T(2,128)} %param.7) | copy-start | bytes 9220
  1.5 5.7 %copy-start.5 = (f32[512]{0:T(512)S(1)}, f32[512]{0:T(512)}, u32[]{:S(2)}) copy-start(f32[512]{0:T(512)} %param.9) | copy-start | bytes 6148
  2.1 8.0 %collective-permute-start = (bf16[2,512]{1,0:T(2,128)(2,1)S(1)}, bf16[2,512]{1,0:T(2,128)(2,1)S(1)}, u32[]{:S(2)}, u32[]{:S(2)}) collective-permute-start(bf16[2,512]{1,0:T(2,128)(2,1)S(1)} %shard_map.109), channel_id=1, source_target_pairs={{0,1},{1,2},{2,3},{4,5},{5,6},{6,7},{8,9},{9,10},{10,11},{12,13},{... | collective-permute-start | bytes 6152 | tf_op jit(solution)/shard_map/ppermute | solution.py:467
  11.3 2.5 %collective-permute-start.1 = (bf16[3360,128]{1,0:T(8,128)(2,1)S(1)}, bf16[3360,128]{1,0:T(8,128)(2,1)S(1)}, u32[]{:S(2)}, u32[]{:S(2)}) collective-permute-start(bf16[3360,128]{1,0:T(8,128)(2,1)S(1)} %get-tuple-element.69.refs_6_), channel_id=1, source_target_pairs={{0,4},{1,5},{2,6},{3,7},{4,0},{5,1},{6,2},{7,3},{8,12},{9,13},{10,... | collective-permute-start | bytes 2580488 | tf_op jit(solution)/shard_map/ppermute | solution.py:478
  15.0 10.6 %collective-permute-start.2 = (bf16[544,256]{1,0:T(8,128)(2,1)S(1)}, bf16[544,256]{1,0:T(8,128)(2,1)S(1)}, u32[]{:S(2)}, u32[]{:S(2)}) collective-permute-start(bf16[544,256]{1,0:T(8,128)(2,1)S(1)} %shard_map.113.refs_5_), channel_id=1, source_target_pairs={{0,2},{1,3},{2,0},{3,1},{4,5},{5,4},{6,7},{7,6},{8,10},{9,11},{10,... | collective-permute-start | bytes 835592 | tf_op jit(solution)/shard_map/ppermute | solution.py:478
  18.3 7.2 %collective-permute-start.3 = (bf16[1024,128]{1,0:T(8,128)(2,1)S(1)}, bf16[1024,128]{1,0:T(8,128)(2,1)S(1)}, u32[]{:S(2)}, u32[]{:S(2)}) collective-permute-start(bf16[1024,128]{1,0:T(8,128)(2,1)S(1)} %get-tuple-element.76.refs_4_), channel_id=1, source_target_pairs={{0,8},{1,9},{2,10},{3,11},{4,20},{5,21},{6,22},{7,23},{8,0},{9,1},... | collective-permute-start | bytes 786440 | tf_op jit(solution)/shard_map/ppermute | solution.py:478
  19.9 5.7 %collective-permute-start.4 = (bf16[288,128]{1,0:T(8,128)(2,1)S(1)}, bf16[288,128]{1,0:T(8,128)(2,1)S(1)}, u32[]{:S(2)}, u32[]{:S(2)}) collective-permute-start(bf16[288,128]{1,0:T(8,128)(2,1)S(1)} %get-tuple-element.77), channel_id=1, source_target_pairs={{0,8},{1,9},{2,10},{3,11},{4,20},{5,21},{6,22},{7,23},{8,0},{9,1},... | collective-permute-start | bytes 221192 | tf_op jit(solution)/shard_map/ppermute | solution.py:478
  26.2 5.8 %collective-permute-start.6 = (bf16[800,128]{1,0:T(8,128)(2,1)S(1)}, bf16[800,128]{1,0:T(8,128)(2,1)S(1)}, u32[]{:S(2)}, u32[]{:S(2)}) collective-permute-start(bf16[800,128]{1,0:T(8,128)(2,1)S(1)} %get-tuple-element.80.refs_4_), channel_id=1, source_target_pairs={{0,16},{1,17},{2,18},{3,19},{4,12},{5,13},{6,14},{7,15},{8,24},{9,... | collective-permute-start | bytes 614408 | tf_op jit(solution)/shard_map/ppermute | solution.py:478
  28.4 7.1 %collective-permute-start.5 = (bf16[272,256]{1,0:T(8,128)(2,1)S(1)}, bf16[272,256]{1,0:T(8,128)(2,1)S(1)}, u32[]{:S(2)}, u32[]{:S(2)}) collective-permute-start(bf16[272,256]{1,0:T(8,128)(2,1)S(1)} %get-tuple-element.81.refs_5_), channel_id=1, source_target_pairs={{0,1},{1,0},{2,3},{3,2},{4,6},{5,7},{6,4},{7,5},{8,9},{9,8},{10,11... | collective-permute-start | bytes 417800 | tf_op jit(solution)/shard_map/ppermute | solution.py:478
  32.7 9.5 %collective-permute-start.8 = (bf16[544,128]{1,0:T(8,128)(2,1)S(1)}, bf16[544,128]{1,0:T(8,128)(2,1)S(1)}, u32[]{:S(2)}, u32[]{:S(2)}) collective-permute-start(bf16[544,128]{1,0:T(8,128)(2,1)S(1)} %get-tuple-element.86.refs_4_), channel_id=1, source_target_pairs={{0,2},{1,3},{2,0},{3,1},{4,5},{5,4},{6,7},{7,6},{8,10},{9,11},{10,... | collective-permute-start | bytes 417800 | tf_op jit(solution)/shard_map/ppermute | solution.py:478
  36.1 6.7 %collective-permute-start.7 = (bf16[272,256]{1,0:T(8,128)(2,1)S(1)}, bf16[272,256]{1,0:T(8,128)(2,1)S(1)}, u32[]{:S(2)}, u32[]{:S(2)}) collective-permute-start(bf16[272,256]{1,0:T(8,128)(2,1)S(1)} %get-tuple-element.88.refs_5_), channel_id=1, source_target_pairs={{0,8},{1,9},{2,10},{3,11},{4,20},{5,21},{6,22},{7,23},{8,0},{9,1},... | collective-permute-start | bytes 417800 | tf_op jit(solution)/shard_map/ppermute | solution.py:478
  42.7 6.1 %collective-permute-start.9 = (bf16[560,128]{1,0:T(8,128)(2,1)S(1)}, bf16[560,128]{1,0:T(8,128)(2,1)S(1)}, u32[]{:S(2)}, u32[]{:S(2)}) collective-permute-start(bf16[560,128]{1,0:T(8,128)(2,1)S(1)} %get-tuple-element.92.refs_3_), channel_id=1, source_target_pairs={{0,1},{1,0},{2,3},{3,2},{4,6},{5,7},{6,4},{7,5},{8,9},{9,8},{10,11... | collective-permute-start | bytes 430088 | tf_op jit(solution)/shard_map/ppermute | solution.py:478
  43.4 5.4 %collective-permute-start.10 = (bf16[272,256]{1,0:T(8,128)(2,1)S(1)}, bf16[272,256]{1,0:T(8,128)(2,1)S(1)}, u32[]{:S(2)}, u32[]{:S(2)}) collective-permute-start(bf16[272,256]{1,0:T(8,128)(2,1)S(1)} %get-tuple-element.93.refs_4_), channel_id=1, source_target_pairs={{0,16},{1,17},{2,18},{3,19},{4,12},{5,13},{6,14},{7,15},{8,24},{9,... | collective-permute-start | bytes 417800 | tf_op jit(solution)/shard_map/ppermute | solution.py:478
  49.5 6.3 %collective-permute-start.11 = (bf16[832,128]{1,0:T(8,128)(2,1)S(1)}, bf16[832,128]{1,0:T(8,128)(2,1)S(1)}, u32[]{:S(2)}, u32[]{:S(2)}) collective-permute-start(bf16[832,128]{1,0:T(8,128)(2,1)S(1)} %get-tuple-element.102.refs_1_), channel_id=1, source_target_pairs={{0,4},{1,5},{2,6},{3,7},{4,0},{5,1},{6,2},{7,3},{8,12},{9,13},{10,... | collective-permute-start | bytes 638984 | tf_op jit(solution)/shard_map/ppermute | solution.py:478
  49.6 4.1 %collective-permute-start.13 = (bf16[256,128]{1,0:T(8,128)(2,1)S(1)}, bf16[256,128]{1,0:T(8,128)(2,1)S(1)}, u32[]{:S(2)}, u32[]{:S(2)}) collective-permute-start(bf16[256,128]{1,0:T(8,128)(2,1)S(1)} %get-tuple-element.100.refs_3_.refs_2_), channel_id=1, source_target_pairs={{0,12},{1,13},{2,14},{3,15},{4,16},{5,17},{6,18},{7,19},{8,4},{9,5... | collective-permute-start | bytes 196616 | tf_op jit(solution)/shard_map/ppermute | solution.py:489
  51.5 4.3 %collective-permute-start.12 = (bf16[256,128]{1,0:T(8,128)(2,1)S(1)}, bf16[256,128]{1,0:T(8,128)(2,1)S(1)}, u32[]{:S(2)}, u32[]{:S(2)}) collective-permute-start(bf16[256,128]{1,0:T(8,128)(2,1)S(1)} %get-tuple-element.100.refs_3_.refs_2_), channel_id=1, source_target_pairs={{0,8},{1,9},{2,10},{3,11},{4,20},{5,21},{6,22},{7,23},{8,0},{9,1},... | collective-permute-start | bytes 196616 | tf_op jit(solution)/shard_map/ppermute | solution.py:478

commit v17 on v14

--- a/solution.py
+++ b/solution.py
@@ -30,6 +30,7 @@
 
 
 def call(body, out_shape, args, after=(), scratch=(), aliases=None, token=False, flops=0):
+    info, args = args[0], args[1:]
     count = len(args)
     many = isinstance(out_shape, (list, tuple))
     shapes = list(out_shape) if many else [out_shape]
@@ -39,11 +40,9 @@
         if token:
             refs[ends + len(shapes)][...] = jnp.zeros((8, LANES), F32)
             refs = refs[:ends + len(shapes)] + refs[ends + len(shapes) + 1:]
-        body(*refs[:count], *refs[ends:])
-
-    specs = [pl.BlockSpec(memory_space=pltpu.SMEM)]
-    specs += [pl.BlockSpec(memory_space=VMEM)] * (count - 1)
-    specs += [pl.BlockSpec(memory_space=pl.ANY)] * len(after)
+        body(info(), *refs[:count], *refs[ends:])
+
+    specs = [pl.BlockSpec(memory_space=VMEM)] * count + [pl.BlockSpec(memory_space=pl.ANY)] * len(after)
     shown = shapes + [shape((8, LANES), F32)] * token
     outs = pl.pallas_call(
         kernel,
@@ -51,7 +50,7 @@
         in_specs=specs,
         out_specs=[pl.BlockSpec(memory_space=VMEM)] * len(shown),
         scratch_shapes=list(scratch),
-        input_output_aliases=aliases or {},
+        input_output_aliases={at - 1: out for at, out in (aliases or {}).items()},
         compiler_params=pltpu.CompilerParams(vmem_limit_bytes=VMEM_LIMIT),
         cost_estimate=pl.CostEstimate(flops=flops, bytes_accessed=0, transcendentals=0),
     )(*args, *after)
@@ -536,45 +535,48 @@
     now_a = pieces_a // 2 if plan[0][2] else pieces_a
     now_c = pieces_c // 2
 
-    at_dp, at_tm = lax.axis_index("dp"), lax.axis_index("tm")
-    core = at_dp & 1
-
-    def on_core(values):
-        return values[0] + core * (values[1] - values[0])
-
-    def bit_at(step):
-        axis, b = step
-        return ((at_dp if axis == "dp" else at_tm) >> b) & 1
-
-    bits = [on_core([bit_at(step) for step in steps]) for steps in exchanges]
-    sums_bits = [on_core([bit_at(step) for step in steps]) for steps in sums_exchanges]
-    shared = [bit_at(step) for step in exchanges[1]]
-    mine_c, other_c = on_core(shared), on_core(shared[::-1])
-    places = [2 * core + mine_c, 2 * (1 - core) + other_c, 2 * core + 1 - mine_c, 2 * (1 - core) + 1 - other_c]
-    places = [place << (log2(pieces_c) - c_bits) for place in places]
-    lists = []
-    for way in ([b for _, b in up], [b for _, b in up[::-1]]):
-        lists.append([sum(((position >> (tm_bits - 1 - j)) & 1) << b for j, b in enumerate(way)) for position in range(tm)])
-    first_bit = on_core([0, tm_bits - 1])
-    lead = (at_tm >> first_bit) & 1
-    quarters = [on_core([lists[0][j], lists[1][j]]) for j in range(tm // 2)]
-    send_codes = [(q + ((1 - lead) << first_bit)) * per_shard for q in quarters]
-    keep_codes = [(q + (lead << first_bit)) * per_shard for q in quarters]
-    differ = at_tm ^ (at_tm + 1)
-    ways = [sum(((differ >> b) & 1) << j for j, b in enumerate(way)) for way in (
-        list(range(tm_bits)), list(reversed(range(tm_bits))))]
-    row_code = jnp.where(at_tm + 1 < tm, on_core(ways), 0)
-    if turned and not mixed:
-        start = ((at_dp * tm + at_tm) * owner_rows) & (LANES - 1)
-    else:
-        start = on_core([(at_dp * tm + at_tm) * owner_rows, (at_tm >> 1) * owner_rows if mixed else (
-            at_dp * tm + at_tm) * owner_rows]) & (LANES - 1)
-    at_start = len(bits)
+    count_bits, count_places = len(exchanges), 4
+    at_start = count_bits
     at_codes = at_start + 1
     at_pieces = at_codes + tm
-    at_sums = at_pieces + len(places)
-    at_row = at_sums + len(sums_bits)
-    info = jnp.stack(bits + [start] + send_codes + keep_codes + places + sums_bits + [row_code]).astype(jnp.int32)
+    at_sums = at_pieces + count_places
+    at_row = at_sums + len(sums_exchanges)
+
+    def info():
+        at_dp, at_tm = lax.axis_index("dp"), lax.axis_index("tm")
+        core = at_dp & 1
+
+        def on_core(values):
+            return values[0] + core * (values[1] - values[0])
+
+        def bit_at(step):
+            axis, b = step
+            return ((at_dp if axis == "dp" else at_tm) >> b) & 1
+
+        bits = [on_core([bit_at(step) for step in steps]) for steps in exchanges]
+        sums_bits = [on_core([bit_at(step) for step in steps]) for steps in sums_exchanges]
+        shared = [bit_at(step) for step in exchanges[1]]
+        mine_c, other_c = on_core(shared), on_core(shared[::-1])
+        places = [2 * core + mine_c, 2 * (1 - core) + other_c, 2 * core + 1 - mine_c, 2 * (1 - core) + 1 - other_c]
+        places = [place << (log2(pieces_c) - c_bits) for place in places]
+        lists = []
+        for way in ([b for _, b in up], [b for _, b in up[::-1]]):
+            lists.append([sum(((position >> (tm_bits - 1 - j)) & 1) << b for j, b in enumerate(way)) for position in range(tm)])
+        first_bit = on_core([0, tm_bits - 1])
+        lead = (at_tm >> first_bit) & 1
+        quarters = [on_core([lists[0][j], lists[1][j]]) for j in range(tm // 2)]
+        send_codes = [(q + ((1 - lead) << first_bit)) * per_shard for q in quarters]
+        keep_codes = [(q + (lead << first_bit)) * per_shard for q in quarters]
+        differ = at_tm ^ (at_tm + 1)
+        ways = [sum(((differ >> b) & 1) << j for j, b in enumerate(way)) for way in (
+            list(range(tm_bits)), list(reversed(range(tm_bits))))]
+        row_code = jnp.where(at_tm + 1 < tm, on_core(ways), 0)
+        if turned and not mixed:
+            start = ((at_dp * tm + at_tm) * owner_rows) & (LANES - 1)
+        else:
+            start = on_core([(at_dp * tm + at_tm) * owner_rows, (at_tm >> 1) * owner_rows if mixed else (
+                at_dp * tm + at_tm) * owner_rows]) & (LANES - 1)
+        return bits + [start] + send_codes + keep_codes + places + sums_bits + [row_code]
 
     halo = shifted(call(halo_kernel, shape((2, channels), BF16), [info, feats[-2:]], flops=10 ** 11), "tm", 1)
     weight, proj, codes = conv_weight, proj_weight, codes[0]

time: 54 us -> 48.9 us (0.906)
  the two profiles are of different devices: /device:TPU:0 before, /device:TPU:24 now
where the time goes in v17:
time: 48.9 us; the launch traced here: 48.6 us
  waiting for transfers between devices  25.7 us (53%)
  starting transfers between devices  11.2 us (23%)
  Pallas kernels  9.64 us (20%)
  local copies, waits for them, and re-layouts  1.25 us (3%)
  between operations  0.81 us (2%)
    ppermute x11, waiting for transfers between devices, swapped(): return lax.ppermute(block, ('dp', 'tm'), route)  23.8 us
    pallas_call x17, Pallas kernels, call(): pl.pallas_call(kernel, out_shape=shown, in_specs=specs, out_specs=[pl.Blo...  9.64 us
    ppermute x11, starting transfers between devices, swapped(): return lax.ppermute(block, ('dp', 'tm'), route)  9.61 us
    ppermute x1, starting transfers between devices, shifted(): return lax.ppermute(block, axis, route)  1.56 us
    ppermute x1, waiting for transfers between devices, shifted(): return lax.ppermute(block, axis, route)  1.32 us
  transfers between devices with their start and end apart: 13, of which 11 were waited for; matrix products, arithmetic and copies ran while one was open for 0% of the time, Pallas kernels for 16%

profile of v17, /device:TPU:24, one launch (start us, length us, event | category | flops | bytes accessed | tf_op | source)
XLA Modules:
  0.0 48.6 jit_solution(12399218082304072929)
XLA Ops:
  0.6 0.7 %slice.3.refs_0_ = bf16[2,512]{1,0:T(2,128)(2,1)S(1)} slice(bf16[768,512]{1,0:T(8,128)(2,1)} %refs_0_.1), slice={[766:768], [0:512]} | slice | bytes 4096 | tf_op jit(solution)/shard_map/slice | solution.py:581
  1.4 1.6 %collective-permute-start = (bf16[2,512]{1,0:T(2,128)(2,1)S(1)}, bf16[2,512]{1,0:T(2,128)(2,1)S(1)}, u32[]{:S(2)}, u32[]{:S(2)}) collective-permute-start(bf16[2,512]{1,0:T(2,128)(2,1)S(1)} %shard_map.109), channel_id=1, source_target_pairs={{0,1},{1,2},{2,3},{4,5},{5,6},{6,7},{8,9},{9,10},{10,11},{12,13},{... | collective-permute-start | bytes 6152 | tf_op jit(solution)/shard_map/ppermute | solution.py:466
  3.0 0.3 copy-done.2
  3.3 0.2 copy-done.3
  3.5 2.3 %shard_map.110 = (bf16[384,2048]{1,0:T(8,128)(2,1)S(1)}, bf16[384,512]{1,0:T(8,128)(2,1)S(1)}, bf16[384,256]{1,0:T(8,128)(2,1)S(1)}, bf16[256,384]{1,0:T(8,128)(...) custom-call(bf16[768,512]{1,0:T(8,128)(2,1)S(1)} %copy-done.3, ...), custom_call_target="tpu_custom_call" | custom-call | tf_op jit(solution)/shard_map/pallas_call | solution.py:47
  5.8 1.3 %collective-permute-done.refs_0_ = bf16[2,512]{1,0:T(2,128)(2,1)S(1)} collective-permute-done((bf16[2,512]{1,0:T(2,128)(2,1)S(1)}, bf16[2,512]{1,0:T(2,128)(2,1)S(1)}, u32[]{:S(2)}, u32[]{:S(2)}) %collective-permute-start) | collective-permute-done | bytes 2080 | tf_op jit(solution)/shard_map/ppermute | solution.py:466
  7.1 0.7 %shard_map.111 = (bf16[384,2048]{1,0:T(8,128)(2,1)S(1)}, bf16[384,512]{1,0:T(8,128)(2,1)S(1)}, bf16[384,256]{1,0:T(8,128)(2,1)S(1)}, bf16[256,384]{1,0:T(8,128)(...) custom-call(bf16[2,512]{1,0:T(2,128)(2,1)S(1)} %collective-permute-d, ...), custom_call_target="tpu_custom_call", output_to_operand_aliasing={{0}: (5, {}), {1}: (6, {}), {2}: (7, {}), {3}: (8, {}), {4}... | custom-call | tf_op jit(solution)/shard_map/pallas_call | solution.py:47
  7.9 0.7 %shard_map.112 = (f32[2048,128]{1,0:T(8,128)S(1)}, f32[512,128]{1,0:T(8,128)S(1)}, bf16[384,512]{1,0:T(8,128)(2,1)S(1)}, f32[32,128]{1,0:T(8,128)S(1)}, bf16[16,512]{1,0:T(8,128)(2,1)S(1)}) custom-call(bf16[256,384]{1,0:T(8,128)(2,1)S(1)} %get-tuple-element.64.refs_0_, bf16[384,2048]{1,0:T(8,128)(2,1)S(1)} %get-tuple-element.65.refs_1_, ...), custom_call_target="tpu_custom_call" | custom-call | tf_op jit(solution)/shard_map/pallas_call | solution.py:47
  8.6 1.7 %collective-permute-done.1.refs_0_ = bf16[3360,128]{1,0:T(8,128)(2,1)S(1)} collective-permute-done((bf16[3360,128]{1,0:T(8,128)(2,1)S(1)}, bf16[3360,128]{1,0:T(8,128)(2,1)S(1)}, u32[]{:S(2)}, u32[]{:S(2)}) %collective-permute-start.1) | collective-permute-done | bytes 860192 | tf_op jit(solution)/shard_map/ppermute | solution.py:477
  10.3 0.1 shard_map.113
  10.4 1.6 %collective-permute-start.3 = (bf16[1312,128]{1,0:T(8,128)(2,1)S(1)}, bf16[1312,128]{1,0:T(8,128)(2,1)S(1)}, u32[]{:S(2)}, u32[]{:S(2)}) collective-permute-start(bf16[1312,128]{1,0:T(8,128)(2,1)S(1)} %get-tuple-element.75.refs_3_), channel_id=1, source_target_pairs={{0,8},{1,9},{2,10},{3,11},{4,20},{5,21},{6,22},{7,23},{8,0},{9,1},... | collective-permute-start | bytes 1007624 | tf_op jit(solution)/shard_map/ppermute | solution.py:477
  12.0 0.6 %shard_map.114.refs_3_ = bf16[544,256]{1,0:T(8,128)(2,1)S(1)} custom-call(bf16[3360,128]{1,0:T(8,128)(2,1)S(1)} %collective-permute-done.1.refs_0_, bf16[400,256]{1,0:T(8,128)(2,1)S(1)} %get-tuple-element.70.refs_1_, bf16[16,512]{1,0:T(8,128)(2,1)S(1)} %get-tuple-element.71.refs_2_, bf16[1312,128]{1,0:T(8,128)(2,1)S(1)} %get-tuple-element.75.refs_3_), custom_call_target="tpu_custom_call" | custom-call | tf_op jit(solution)/shard_map/pallas_call | solution.py:47
  12.6 0.9 %collective-permute-start.2 = (bf16[544,256]{1,0:T(8,128)(2,1)S(1)}, bf16[544,256]{1,0:T(8,128)(2,1)S(1)}, u32[]{:S(2)}, u32[]{:S(2)}) collective-permute-start(bf16[544,256]{1,0:T(8,128)(2,1)S(1)} %shard_map.114.refs_3_), channel_id=1, source_target_pairs={{0,1},{1,0},{2,3},{3,2},{4,6},{5,7},{6,4},{7,5},{8,9},{9,8},{10,11... | collective-permute-start | bytes 835592 | tf_op jit(solution)/shard_map/ppermute | solution.py:477
  13.5 0.6 %shard_map.115.refs_3_.refs_1_ = f32[544,256]{1,0:T(8,128)S(1)} custom-call(bf16[3360,128]{1,0:T(8,128)(2,1)S(1)} %collective-permute-done.1.refs_0_, bf16[400,256]{1,0:T(8,128)(2,1)S(1)} %get-tuple-element.70.refs_1_, bf16[16,512]{1,0:T(8,128)(2,1)S(1)} %get-tuple-element.71.refs_2_, bf16[544,256]{1,0:T(8,128)(2,1)S(1)} %shard_map.114.refs_3_), custom_call_target="tpu_custom_call" | custom-call | tf_op jit(solution)/shard_map/pallas_call | solution.py:47
  14.2 3.5 %collective-permute-done.3.refs_0_ = bf16[1312,128]{1,0:T(8,128)(2,1)S(1)} collective-permute-done((bf16[1312,128]{1,0:T(8,128)(2,1)S(1)}, bf16[1312,128]{1,0:T(8,128)(2,1)S(1)}, u32[]{:S(2)}, u32[]{:S(2)}) %collective-permute-start.3) | collective-permute-done | bytes 335904 | tf_op jit(solution)/shard_map/ppermute | solution.py:477
  17.7 1.6 %collective-permute-start.5 = (bf16[800,128]{1,0:T(8,128)(2,1)S(1)}, bf16[800,128]{1,0:T(8,128)(2,1)S(1)}, u32[]{:S(2)}, u32[]{:S(2)}) collective-permute-start(bf16[800,128]{1,0:T(8,128)(2,1)S(1)} %get-tuple-element.78.refs_3_), channel_id=1, source_target_pairs={{0,16},{1,17},{2,18},{3,19},{4,12},{5,13},{6,14},{7,15},{8,24},{9,... | collective-permute-start | bytes 614408 | tf_op jit(solution)/shard_map/ppermute | solution.py:477
  19.3 2.7 %collective-permute-done.2.refs_0_ = bf16[544,256]{1,0:T(8,128)(2,1)S(1)} collective-permute-done((bf16[544,256]{1,0:T(8,128)(2,1)S(1)}, bf16[544,256]{1,0:T(8,128)(2,1)S(1)}, u32[]{:S(2)}, u32[]{:S(2)}) %collective-permute-start.2) | collective-permute-done | bytes 278560 | tf_op jit(solution)/shard_map/ppermute | solution.py:477
  22.1 0.9 %collective-permute-start.4 = (bf16[272,256]{1,0:T(8,128)(2,1)S(1)}, bf16[272,256]{1,0:T(8,128)(2,1)S(1)}, u32[]{:S(2)}, u32[]{:S(2)}) collective-permute-start(bf16[272,256]{1,0:T(8,128)(2,1)S(1)} %get-tuple-element.79.refs_3_), channel_id=1, source_target_pairs={{0,2},{1,3},{2,0},{3,1},{4,5},{5,4},{6,7},{7,6},{8,10},{9,11},{10,... | collective-permute-start | bytes 417800 | tf_op jit(solution)/shard_map/ppermute | solution.py:477
  23.0 0.5 %collective-permute-done.5.refs_0_ = bf16[800,128]{1,0:T(8,128)(2,1)S(1)} collective-permute-done((bf16[800,128]{1,0:T(8,128)(2,1)S(1)}, bf16[800,128]{1,0:T(8,128)(2,1)S(1)}, u32[]{:S(2)}, u32[]{:S(2)}) %collective-permute-start.5) | collective-permute-done | bytes 204832 | tf_op jit(solution)/shard_map/ppermute | solution.py:477
  23.7 1.6 %collective-permute-start.7 = (bf16[544,128]{1,0:T(8,128)(2,1)S(1)}, bf16[544,128]{1,0:T(8,128)(2,1)S(1)}, u32[]{:S(2)}, u32[]{:S(2)}) collective-permute-start(bf16[544,128]{1,0:T(8,128)(2,1)S(1)} %get-tuple-element.84.refs_3_), channel_id=1, source_target_pairs={{0,2},{1,3},{2,0},{3,1},{4,5},{5,4},{6,7},{7,6},{8,10},{9,11},{10,... | collective-permute-start | bytes 417800 | tf_op jit(solution)/shard_map/ppermute | solution.py:477
  25.3 5.5 %collective-permute-done.4.refs_0_ = bf16[272,256]{1,0:T(8,128)(2,1)S(1)} collective-permute-done((bf16[272,256]{1,0:T(8,128)(2,1)S(1)}, bf16[272,256]{1,0:T(8,128)(2,1)S(1)}, u32[]{:S(2)}, u32[]{:S(2)}) %collective-permute-start.4) | collective-permute-done | bytes 139296 | tf_op jit(solution)/shard_map/ppermute | solution.py:477
  30.9 2.0 %collective-permute-done.7.refs_0_ = bf16[544,128]{1,0:T(8,128)(2,1)S(1)} collective-permute-done((bf16[544,128]{1,0:T(8,128)(2,1)S(1)}, bf16[544,128]{1,0:T(8,128)(2,1)S(1)}, u32[]{:S(2)}, u32[]{:S(2)}) %collective-permute-start.7) | collective-permute-done | bytes 139296 | tf_op jit(solution)/shard_map/ppermute | solution.py:477
  33.1 4.1 %collective-permute-done.6.refs_0_ = bf16[272,256]{1,0:T(8,128)(2,1)S(1)} collective-permute-done((bf16[272,256]{1,0:T(8,128)(2,1)S(1)}, bf16[272,256]{1,0:T(8,128)(2,1)S(1)}, u32[]{:S(2)}, u32[]{:S(2)}) %collective-permute-start.6) | collective-permute-done | bytes 139296 | tf_op jit(solution)/shard_map/ppermute | solution.py:477
  37.2 0.6 %collective-permute-start.9 = (bf16[272,256]{1,0:T(8,128)(2,1)S(1)}, bf16[272,256]{1,0:T(8,128)(2,1)S(1)}, u32[]{:S(2)}, u32[]{:S(2)}) collective-permute-start(bf16[272,256]{1,0:T(8,128)(2,1)S(1)} %get-tuple-element.91.refs_3_), channel_id=1, source_target_pairs={{0,16},{1,17},{2,18},{3,19},{4,12},{5,13},{6,14},{7,15},{8,24},{9,... | collective-permute-start | bytes 417800 | tf_op jit(solution)/shard_map/ppermute | solution.py:477
  37.9 2.0 %shard_map.122 = (bf16[768,512]{1,0:T(8,128)(2,1)}, f32[8,128]{1,0:T(8,128)S(1)}) custom-call(bf16[384,512]{1,0:T(8,128)(2,1)S(1)} %get-tuple-element.69.refs_0_, bf16[16,512]{1,0:T(8,128)(2,1)S(1)} %get-tuple-element.85.refs_1_, bf16[2048,512]{1,0:T(8,128)(2,1)S(1)} %copy-done, bf16[272,256]{1,0:T(8,128)(2,1)S(1)} %get-tuple-element.91.refs_3_), custom_call_target="tpu_custom_call" | custom-call | tf_op jit(solution)/shard_map/pallas_call | solution.py:47
  39.9 2.5 %collective-permute-done.9.refs_3_ = bf16[272,256]{1,0:T(8,128)(2,1)S(1)} collective-permute-done((bf16[272,256]{1,0:T(8,128)(2,1)S(1)}, bf16[272,256]{1,0:T(8,128)(2,1)S(1)}, u32[]{:S(2)}, u32[]{:S(2)}) %collective-permute-start.9) | collective-permute-done | bytes 139296 | tf_op jit(solution)/shard_map/ppermute | solution.py:477
  42.4 0.2 shard_map.123
  42.7 2.1 %collective-permute-start.11 = (bf16[256,128]{1,0:T(8,128)(2,1)S(1)}, bf16[256,128]{1,0:T(8,128)(2,1)S(1)}, u32[]{:S(2)}, u32[]{:S(2)}) collective-permute-start(bf16[256,128]{1,0:T(8,128)(2,1)S(1)} %get-tuple-element.98.refs_2_.refs_1_), channel_id=1, source_target_pairs={{0,8},{1,9},{2,10},{3,11},{4,20},{5,21},{6,22},{7,23},{8,0},{9,1},... | collective-permute-start | bytes 196616 | tf_op jit(solution)/shard_map/ppermute | solution.py:477
  44.7 1.0 %shard_map.124 = (f32[64,512]{1,0:T(8,128)}, f32[8,128]{1,0:T(8,128)S(1)}) custom-call(f32[256,128]{1,0:T(8,128)S(1)} %get-tuple-element.97.refs_0_, bf16[512,256]{1,0:T(8,128)(2,1)S(1)} %copy-done.1, bf16[256,128]{1,0:T(8,128)(2,1)S(1)} %get-tuple-element.98.refs_2_.refs_1_), custom_call_target="tpu_custom_call" | custom-call | tf_op jit(solution)/shard_map/pallas_call | solution.py:47
  45.7 0.6 %collective-permute-done.12.refs_4_ = bf16[256,128]{1,0:T(8,128)(2,1)S(1)} collective-permute-done((bf16[256,128]{1,0:T(8,128)(2,1)S(1)}, bf16[256,128]{1,0:T(8,128)(2,1)S(1)}, u32[]{:S(2)}, u32[]{:S(2)}) %collective-permute-start.12) | collective-permute-done | bytes 65568 | tf_op jit(solution)/shard_map/ppermute | solution.py:488
  46.3 1.3 %collective-permute-done.11.refs_3_ = bf16[256,128]{1,0:T(8,128)(2,1)S(1)} collective-permute-done((bf16[256,128]{1,0:T(8,128)(2,1)S(1)}, bf16[256,128]{1,0:T(8,128)(2,1)S(1)}, u32[]{:S(2)}, u32[]{:S(2)}) %collective-permute-start.11) | collective-permute-done | bytes 65568 | tf_op jit(solution)/shard_map/ppermute | solution.py:477
  47.7 1.0 %shard_map.125 = (f32[512,256]{1,0:T(8,128)}, f32[1,512]{1,0:T(1,128)}, bf16[2,256,256]{2,1,0:T(8,128)(2,1)}, f32[2,256]{1,0:T(2,128)}) custom-call(bf16[832,128]{1,0:T(8,128)(2,1)S(1)} %get-tuple-element.100.refs_0_, bf16[256,128]{1,0:T(8,128)(2,1)S(1)} %get-tuple-element.98.refs_2_.refs_1_, bf16[832,128]{1,0:T(8,128)(2,1)S(1)} %collective-permute-done.10.refs_2_, ...), custom_call_target="tpu_custom_call" | custom-call | tf_op jit(solution)/shard_map/pallas_call | solution.py:47
  (24 shorter events, 0.8 us)
Async XLA Ops:
  1.3 1.6 %copy-start = (bf16[2048,512]{1,0:T(8,128)(2,1)S(1)}, bf16[2048,512]{1,0:T(8,128)(2,1)}, u32[]{:S(2)}) copy-start(bf16[2048,512]{1,0:T(8,128)(2,1)} %refs_2_.1) | copy-start | bytes 6291460
  1.3 1.6 %copy-start.1 = (bf16[512,256]{1,0:T(8,128)(2,1)S(1)}, bf16[512,256]{1,0:T(8,128)(2,1)}, u32[]{:S(2)}) copy-start(bf16[512,256]{1,0:T(8,128)(2,1)} %refs_1_.3) | copy-start | bytes 786436
  1.3 1.9 %copy-start.2 = (bf16[2,1024,256]{2,1,0:T(8,128)(2,1)S(1)}, bf16[2,1024,256]{2,1,0:T(8,128)(2,1)}, u32[]{:S(2)}) copy-start(bf16[2,1024,256]{2,1,0:T(8,128)(2,1)} %refs_4_.3) | copy-start | bytes 3145732
  1.3 2.1 %copy-start.3 = (bf16[768,512]{1,0:T(8,128)(2,1)S(1)}, bf16[768,512]{1,0:T(8,128)(2,1)}, u32[]{:S(2)}) copy-start(bf16[768,512]{1,0:T(8,128)(2,1)} %refs_0_.1) | copy-start | bytes 2359300
  1.4 2.1 %copy-start.4 = (s32[1,2,384]{2,1,0:T(2,128)S(1)}, s32[1,2,384]{2,1,0:T(2,128)}, u32[]{:S(2)}) copy-start(s32[1,2,384]{2,1,0:T(2,128)} %param.7) | copy-start | bytes 9220
  1.4 2.1 %copy-start.5 = (f32[512]{0:T(512)S(1)}, f32[512]{0:T(512)}, u32[]{:S(2)}) copy-start(f32[512]{0:T(512)} %param.9) | copy-start | bytes 6148
  1.4 5.7 %collective-permute-start = (bf16[2,512]{1,0:T(2,128)(2,1)S(1)}, bf16[2,512]{1,0:T(2,128)(2,1)S(1)}, u32[]{:S(2)}, u32[]{:S(2)}) collective-permute-start(bf16[2,512]{1,0:T(2,128)(2,1)S(1)} %shard_map.109), channel_id=1, source_target_pairs={{0,1},{1,2},{2,3},{4,5},{5,6},{6,7},{8,9},{9,10},{10,11},{12,13},{... | collective-permute-start | bytes 6152 | tf_op jit(solution)/shard_map/ppermute | solution.py:466
  7.8 2.5 %collective-permute-start.1 = (bf16[3360,128]{1,0:T(8,128)(2,1)S(1)}, bf16[3360,128]{1,0:T(8,128)(2,1)S(1)}, u32[]{:S(2)}, u32[]{:S(2)}) collective-permute-start(bf16[3360,128]{1,0:T(8,128)(2,1)S(1)} %get-tuple-element.68.refs_5_), channel_id=1, source_target_pairs={{0,4},{1,5},{2,6},{3,7},{4,0},{5,1},{6,2},{7,3},{8,12},{9,13},{10,... | collective-permute-start | bytes 2580488 | tf_op jit(solution)/shard_map/ppermute | solution.py:477
  10.4 7.2 %collective-permute-start.3 = (bf16[1312,128]{1,0:T(8,128)(2,1)S(1)}, bf16[1312,128]{1,0:T(8,128)(2,1)S(1)}, u32[]{:S(2)}, u32[]{:S(2)}) collective-permute-start(bf16[1312,128]{1,0:T(8,128)(2,1)S(1)} %get-tuple-element.75.refs_3_), channel_id=1, source_target_pairs={{0,8},{1,9},{2,10},{3,11},{4,20},{5,21},{6,22},{7,23},{8,0},{9,1},... | collective-permute-start | bytes 1007624 | tf_op jit(solution)/shard_map/ppermute | solution.py:477
  12.6 9.4 %collective-permute-start.2 = (bf16[544,256]{1,0:T(8,128)(2,1)S(1)}, bf16[544,256]{1,0:T(8,128)(2,1)S(1)}, u32[]{:S(2)}, u32[]{:S(2)}) collective-permute-start(bf16[544,256]{1,0:T(8,128)(2,1)S(1)} %shard_map.114.refs_3_), channel_id=1, source_target_pairs={{0,1},{1,0},{2,3},{3,2},{4,6},{5,7},{6,4},{7,5},{8,9},{9,8},{10,11... | collective-permute-start | bytes 835592 | tf_op jit(solution)/shard_map/ppermute | solution.py:477
  17.7 5.8 %collective-permute-start.5 = (bf16[800,128]{1,0:T(8,128)(2,1)S(1)}, bf16[800,128]{1,0:T(8,128)(2,1)S(1)}, u32[]{:S(2)}, u32[]{:S(2)}) collective-permute-start(bf16[800,128]{1,0:T(8,128)(2,1)S(1)} %get-tuple-element.78.refs_3_), channel_id=1, source_target_pairs={{0,16},{1,17},{2,18},{3,19},{4,12},{5,13},{6,14},{7,15},{8,24},{9,... | collective-permute-start | bytes 614408 | tf_op jit(solution)/shard_map/ppermute | solution.py:477
  22.1 8.7 %collective-permute-start.4 = (bf16[272,256]{1,0:T(8,128)(2,1)S(1)}, bf16[272,256]{1,0:T(8,128)(2,1)S(1)}, u32[]{:S(2)}, u32[]{:S(2)}) collective-permute-start(bf16[272,256]{1,0:T(8,128)(2,1)S(1)} %get-tuple-element.79.refs_3_), channel_id=1, source_target_pairs={{0,2},{1,3},{2,0},{3,1},{4,5},{5,4},{6,7},{7,6},{8,10},{9,11},{10,... | collective-permute-start | bytes 417800 | tf_op jit(solution)/shard_map/ppermute | solution.py:477
  23.7 9.2 %collective-permute-start.7 = (bf16[544,128]{1,0:T(8,128)(2,1)S(1)}, bf16[544,128]{1,0:T(8,128)(2,1)S(1)}, u32[]{:S(2)}, u32[]{:S(2)}) collective-permute-start(bf16[544,128]{1,0:T(8,128)(2,1)S(1)} %get-tuple-element.84.refs_3_), channel_id=1, source_target_pairs={{0,2},{1,3},{2,0},{3,1},{4,5},{5,4},{6,7},{7,6},{8,10},{9,11},{10,... | collective-permute-start | bytes 417800 | tf_op jit(solution)/shard_map/ppermute | solution.py:477
  30.8 6.3 %collective-permute-start.6 = (bf16[272,256]{1,0:T(8,128)(2,1)S(1)}, bf16[272,256]{1,0:T(8,128)(2,1)S(1)}, u32[]{:S(2)}, u32[]{:S(2)}) collective-permute-start(bf16[272,256]{1,0:T(8,128)(2,1)S(1)} %get-tuple-element.86.refs_3_), channel_id=1, source_target_pairs={{0,8},{1,9},{2,10},{3,11},{4,20},{5,21},{6,22},{7,23},{8,0},{9,1},... | collective-permute-start | bytes 417800 | tf_op jit(solution)/shard_map/ppermute | solution.py:477
  33.0 9.4 %collective-permute-start.8 = (bf16[560,128]{1,0:T(8,128)(2,1)S(1)}, bf16[560,128]{1,0:T(8,128)(2,1)S(1)}, u32[]{:S(2)}, u32[]{:S(2)}) collective-permute-start(bf16[560,128]{1,0:T(8,128)(2,1)S(1)} %get-tuple-element.90.refs_2_), channel_id=1, source_target_pairs={{0,1},{1,0},{2,3},{3,2},{4,6},{5,7},{6,4},{7,5},{8,9},{9,8},{10,11... | collective-permute-start | bytes 430088 | tf_op jit(solution)/shard_map/ppermute | solution.py:477
  37.2 5.1 %collective-permute-start.9 = (bf16[272,256]{1,0:T(8,128)(2,1)S(1)}, bf16[272,256]{1,0:T(8,128)(2,1)S(1)}, u32[]{:S(2)}, u32[]{:S(2)}) collective-permute-start(bf16[272,256]{1,0:T(8,128)(2,1)S(1)} %get-tuple-element.91.refs_3_), channel_id=1, source_target_pairs={{0,16},{1,17},{2,18},{3,19},{4,12},{5,13},{6,14},{7,15},{8,24},{9,... | collective-permute-start | bytes 417800 | tf_op jit(solution)/shard_map/ppermute | solution.py:477
  42.5 5.2 %collective-permute-start.10 = (bf16[832,128]{1,0:T(8,128)(2,1)S(1)}, bf16[832,128]{1,0:T(8,128)(2,1)S(1)}, u32[]{:S(2)}, u32[]{:S(2)}) collective-permute-start(bf16[832,128]{1,0:T(8,128)(2,1)S(1)} %get-tuple-element.100.refs_0_), channel_id=1, source_target_pairs={{0,4},{1,5},{2,6},{3,7},{4,0},{5,1},{6,2},{7,3},{8,12},{9,13},{10,... | collective-permute-start | bytes 638984 | tf_op jit(solution)/shard_map/ppermute | solution.py:477
  42.6 3.7 %collective-permute-start.12 = (bf16[256,128]{1,0:T(8,128)(2,1)S(1)}, bf16[256,128]{1,0:T(8,128)(2,1)S(1)}, u32[]{:S(2)}, u32[]{:S(2)}) collective-permute-start(bf16[256,128]{1,0:T(8,128)(2,1)S(1)} %get-tuple-element.98.refs_2_.refs_1_), channel_id=1, source_target_pairs={{0,12},{1,13},{2,14},{3,15},{4,16},{5,17},{6,18},{7,19},{8,4},{9,5... | collective-permute-start | bytes 196616 | tf_op jit(solution)/shard_map/ppermute | solution.py:488
  42.7 5.0 %collective-permute-start.11 = (bf16[256,128]{1,0:T(8,128)(2,1)S(1)}, bf16[256,128]{1,0:T(8,128)(2,1)S(1)}, u32[]{:S(2)}, u32[]{:S(2)}) collective-permute-start(bf16[256,128]{1,0:T(8,128)(2,1)S(1)} %get-tuple-element.98.refs_2_.refs_1_), channel_id=1, source_target_pairs={{0,8},{1,9},{2,10},{3,11},{4,20},{5,21},{6,22},{7,23},{8,0},{9,1},... | collective-permute-start | bytes 196616 | tf_op jit(solution)/shard_map/ppermute | solution.py:477

commit v18 on v17

--- a/solution.py
+++ b/solution.py
@@ -258,11 +258,11 @@
     return jnp.concatenate(list(digits_of(value)) + [jnp.zeros_like(value)], 0)
 
 
-def first_step_kernel(halves, place, info, got, kept_a, kept_c, extras, send, keep_a, keep_c):
+def first_step_kernel(halves, place, info, got, kept_a, kept_c, extras, send_a, send_c, keep_a, keep_c):
     (rows_a, halved_a), (rows_c, halved_c) = halves
-    to = split_sum(halved_a, info[place], got, 0, kept_a, rows_a, send, 0, keep_a)
-    gone = split_sum(halved_c, info[place], got, rows_a, kept_c, rows_c, send, to, keep_c)
-    send[to + gone:, :] = extras[...].astype(BF16)
+    split_sum(halved_a, info[place], got, 0, kept_a, rows_a, send_a, 0, keep_a)
+    gone = split_sum(halved_c, info[place], got, rows_a, kept_c, rows_c, send_c, 0, keep_c)
+    send_c[gone:, :] = extras[...].astype(BF16)
     keep_c[gone:, :] = extras[...]
 
 
@@ -282,22 +282,29 @@
         out[:, j * LANES:(j + 1) * LANES] = inter[j].astype(BF16)
 
 
-def sums_kernel(first, frames, place, count, info, got, own, row, out):
-    rows, dz = own.shape
+def own_sums_kernel(frames, place, count, info, own, out):
+    codes = codes_of(own[frames:, :], frames)
+    ones = jnp.ones((8, frames), BF16)
+    size = count + 16
+    for top in range(0, out.shape[0], size):
+        matches = one_hot(codes, 0, info[place], count)
+        out[top:top + count, :] = nn(matches, own[0:frames, :])
+        out[top + count:top + count + 8, 0:count] = nt(ones, matches)
+        place += 1
+
+
+def sums_kernel(first, frames, place, count, info, got, base, row, out):
+    dz = base.shape[1]
+    rows = (got.shape[0] - first) // (dz // LANES)
     theirs = jnp.concatenate([got[first + j * rows:first + (j + 1) * rows, :] for j in range(dz // LANES)], 1)
+    codes = codes_of(theirs[frames:, :], frames)
     ones = jnp.ones((8, frames), BF16)
-    parts = []
-    for block in (own[...], theirs):
-        parts.append((block[0:frames, :], codes_of(block[frames:, :], frames)))
     size = count + 16
     riding = [row[...].astype(F32)[0:1, :]]
     for top in range(0, out.shape[0], size):
-        total = jnp.zeros((count, dz), F32)
-        counts = jnp.zeros((8, count), F32)
-        for values, codes in parts:
-            matches = one_hot(codes, 0, info[place], count)
-            total = total + nn(matches, values)
-            counts = counts + nt(ones, matches)
+        matches = one_hot(codes, 0, info[place], count)
+        total = base[top:top + count, :] + nn(matches, theirs[0:frames, :])
+        counts = base[top + count:top + count + 8, 0:count] + nt(ones, matches)
         out[top:top + count, :] = total.astype(out.dtype)
         out[top + count:top + size, :] = count_rows(counts[0:1], dz, riding).astype(out.dtype)
         place += 1
@@ -373,7 +380,7 @@
     return jnp.where(core == 1, swapped_first, first), jnp.where(core == 1, swapped_second, second)
 
 
-def step_kernel(halves, place, mixed, info, got, kept_a, kept_c, send, keep_a, keep_c):
+def step_kernel(halves, at_c, place, mixed, info, got, got_c, kept_a, kept_c, send, keep_a, keep_c):
     (rows_a, halved_a), (rows_c, halved_c) = halves
     if mixed:
         to = rows_a // 2
@@ -384,8 +391,8 @@
         keep_a[...] = jnp.where(low, first, second)
     else:
         to = split_sum(halved_a, info[place], got, 0, kept_a, rows_a, send, 0, keep_a)
-    gone = split_sum(halved_c, info[place], got, rows_a, kept_c, rows_c, send, to, keep_c)
-    block = digit_block(add_digits(kept_c[rows_c:, :], got[rows_a + rows_c:, :].astype(F32)))
+    gone = split_sum(halved_c, info[place], got_c, at_c, kept_c, rows_c, send, to, keep_c)
+    block = digit_block(add_digits(kept_c[rows_c:, :], got_c[at_c + rows_c:, :].astype(F32)))
     keep_c[gone:, :] = block
     to += gone
     send[to:to + block.shape[0], :] = block.astype(BF16)
@@ -615,36 +622,46 @@
         now_c = now_c // 2 if halves[1][1] else now_c
         return halves, now_a * dz, now_c * dz + extra
 
-    halves, rows_a, rows_c = halves_at(1)
-    send, keep_a, keep_c = call(
-        functools.partial(first_step_kernel, halves, 1),
-        [shape((rows_a + rows_c, LANES), BF16), shape((rows_a, LANES), F32), shape((rows_c, LANES), F32)],
-        [info, got, keep_a, keep_c, extras])
     size = per_shard + 16
     sums_rows = size * (tm // 2)
-    sums_send = call(
-        functools.partial(sums_kernel, corr_rows, frames, at_codes, per_shard),
-        shape((sums_rows, dz), BF16),
-        [info, got, own, row],
-        after=[send])
-    sums_keep = call(
-        functools.partial(sums_kernel, corr_rows, frames, at_codes + tm // 2, per_shard),
-        shape((sums_rows, dz), F32),
-        [info, got, own, row],
+
+    def own_sums(first, after):
+        return call(
+            functools.partial(own_sums_kernel, frames, at_codes + first, per_shard),
+            shape((sums_rows, dz), F32),
+            [info, own],
+            after=after)
+
+    def both_sums(first, base, dtype, after):
+        return call(
+            functools.partial(sums_kernel, corr_rows, frames, at_codes + first, per_shard),
+            shape((sums_rows, dz), dtype),
+            [info, got, base, row],
+            after=after)
+
+    sums_send = both_sums(0, own_sums(0, [extras]), BF16, [])
+    sums_got = swapped(sums_send, sums_exchanges[0])
+    halves, rows_a, rows_c = halves_at(1)
+    send, send_c, keep_a, keep_c = call(
+        functools.partial(first_step_kernel, halves, 1),
+        [shape((rows_a, LANES), BF16), shape((rows_c, LANES), BF16), shape((rows_a, LANES), F32),
+         shape((rows_c, LANES), F32)],
+        [info, got, keep_a, keep_c, extras],
         after=[sums_send])
-    sums_got = swapped(sums_send, sums_exchanges[0])
-    got = swapped(send, exchanges[1])
+    sums_keep = both_sums(tm // 2, own_sums(tm // 2, [send]), F32, [])
+    got, got_c = swapped(send, exchanges[1]), swapped(send_c, exchanges[1])
     known = row
-    ordered = [sums_keep]
+    ordered = [sums_keep, sums_got]
     for k in range(2, len(exchanges)):
+        at_c = 0 if k == 2 else rows_a
         halves, rows_a, rows_c = halves_at(k)
         spare = 16 * (k == len(exchanges) - 1)
         send, keep_a, keep_c = call(
-            functools.partial(step_kernel, halves, k, mixed and k == dp_bits),
+            functools.partial(step_kernel, halves, at_c, k, mixed and k == dp_bits),
             [shape((rows_a + rows_c + spare, LANES), BF16), shape((rows_a, LANES), F32), shape((rows_c, LANES), F32)],
-            [info, got, keep_a, keep_c],
+            [info, got, got_c, keep_a, keep_c],
             after=ordered)
-        got = swapped(send, exchanges[k])
+        got = got_c = swapped(send, exchanges[k])
         halved = sums_exchanges[k - 1][0][0] == "tm"
         sums_rows = sums_rows // 2 if halved else sums_rows
         row_step = k - 2 if k - 2 < tm_bits else None

time: 48.9 us -> 49.7 us (1.016)
  the two profiles are of different devices: /device:TPU:24 before, /device:TPU:0 now
where the time goes in v18:
time: 49.7 us; the launch traced here: 49.5 us
  starting transfers between devices  20.3 us (41%)
  waiting for transfers between devices  17.6 us (35%)
  Pallas kernels  9.99 us (20%)
  between operations  0.84 us (2%)
  local copies, waits for them, and re-layouts  0.74 us (1%)
    ppermute x12, waiting for transfers between devices, swapped(): return lax.ppermute(block, ('dp', 'tm'), route)  16.7 us
    ppermute x12, starting transfers between devices, swapped(): return lax.ppermute(block, ('dp', 'tm'), route)  13.5 us
    pallas_call x19, Pallas kernels, call(): pl.pallas_call(kernel, out_shape=shown, in_specs=specs, out_specs=[pl.Blo...  9.99 us
    ppermute x1, starting transfers between devices, shifted(): return lax.ppermute(block, axis, route)  5.19 us
    ppermute x1, starting transfers between devices, crossed(): return lax.ppermute(block, ('dp', 'tm'), route)  1.62 us
  transfers between devices with their start and end apart: 14, of which 10 were waited for; matrix products, arithmetic and copies ran while one was open for 0% of the time, Pallas kernels for 16%

profile of v18, /device:TPU:0, one launch (start us, length us, event | category | flops | bytes accessed | tf_op | source)
XLA Modules:
  0.0 49.5 jit_solution(2144179261352580231)
XLA Ops:
  0.6 0.7 %slice.3.refs_0_ = bf16[2,512]{1,0:T(2,128)(2,1)S(1)} slice(bf16[768,512]{1,0:T(8,128)(2,1)} %refs_0_.1), slice={[766:768], [0:512]} | slice | bytes 4096 | tf_op jit(solution)/shard_map/slice | solution.py:588
  1.4 5.2 %collective-permute-start = (bf16[2,512]{1,0:T(2,128)(2,1)S(1)}, bf16[2,512]{1,0:T(2,128)(2,1)S(1)}, u32[]{:S(2)}, u32[]{:S(2)}) collective-permute-start(bf16[2,512]{1,0:T(2,128)(2,1)S(1)} %shard_map.109), channel_id=1, source_target_pairs={{0,1},{1,2},{2,3},{4,5},{5,6},{6,7},{8,9},{9,10},{10,11},{12,13},{... | collective-permute-start | bytes 6152 | tf_op jit(solution)/shard_map/ppermute | solution.py:473
  6.7 2.3 %shard_map.110 = (bf16[384,2048]{1,0:T(8,128)(2,1)S(1)}, bf16[384,512]{1,0:T(8,128)(2,1)S(1)}, bf16[384,256]{1,0:T(8,128)(2,1)S(1)}, bf16[256,384]{1,0:T(8,128)(...) custom-call(bf16[768,512]{1,0:T(8,128)(2,1)S(1)} %copy-done.3, ...), custom_call_target="tpu_custom_call" | custom-call | tf_op jit(solution)/shard_map/pallas_call | solution.py:47
  9.0 0.7 %shard_map.111 = (bf16[384,2048]{1,0:T(8,128)(2,1)S(1)}, bf16[384,512]{1,0:T(8,128)(2,1)S(1)}, bf16[384,256]{1,0:T(8,128)(2,1)S(1)}, bf16[256,384]{1,0:T(8,128)(...) custom-call(bf16[2,512]{1,0:T(2,128)(2,1)S(1)} %collective-permute-d, ...), custom_call_target="tpu_custom_call", output_to_operand_aliasing={{0}: (5, {}), {1}: (6, {}), {2}: (7, {}), {3}: (8, {}), {4}... | custom-call | tf_op jit(solution)/shard_map/pallas_call | solution.py:47
  9.8 0.7 %shard_map.112 = (f32[2048,128]{1,0:T(8,128)S(1)}, f32[512,128]{1,0:T(8,128)S(1)}, bf16[384,512]{1,0:T(8,128)(2,1)S(1)}, f32[32,128]{1,0:T(8,128)S(1)}, bf16[16,512]{1,0:T(8,128)(2,1)S(1)}) custom-call(bf16[256,384]{1,0:T(8,128)(2,1)S(1)} %get-tuple-element.65.refs_0_, bf16[384,2048]{1,0:T(8,128)(2,1)S(1)} %get-tuple-element.66.refs_1_, ...), custom_call_target="tpu_custom_call" | custom-call | tf_op jit(solution)/shard_map/pallas_call | solution.py:47
  10.4 0.4 shard_map.113.refs_1_
  10.8 1.3 %collective-permute-done.1.refs_0_ = bf16[3360,128]{1,0:T(8,128)(2,1)S(1)} collective-permute-done((bf16[3360,128]{1,0:T(8,128)(2,1)S(1)}, bf16[3360,128]{1,0:T(8,128)(2,1)S(1)}, u32[]{:S(2)}, u32[]{:S(2)}) %collective-permute-start.1) | collective-permute-done | bytes 860192 | tf_op jit(solution)/shard_map/ppermute | solution.py:484
  12.1 0.4 shard_map.114.refs_4_
  12.5 1.6 %collective-permute-start.2 = (bf16[544,256]{1,0:T(8,128)(2,1)S(1)}, bf16[544,256]{1,0:T(8,128)(2,1)S(1)}, u32[]{:S(2)}, u32[]{:S(2)}) collective-permute-start(bf16[544,256]{1,0:T(8,128)(2,1)S(1)} %shard_map.114.refs_4_), channel_id=1, source_target_pairs={{0,1},{1,0},{2,3},{3,2},{4,6},{5,7},{6,4},{7,5},{8,9},{9,8},{10,11... | collective-permute-start | bytes 835592 | tf_op jit(solution)/shard_map/ppermute | solution.py:484
  14.3 1.6 %collective-permute-start.3 = (bf16[1024,128]{1,0:T(8,128)(2,1)S(1)}, bf16[1024,128]{1,0:T(8,128)(2,1)S(1)}, u32[]{:S(2)}, u32[]{:S(2)}) collective-permute-start(bf16[1024,128]{1,0:T(8,128)(2,1)S(1)} %get-tuple-element.76.refs_1_), channel_id=1, source_target_pairs={{0,8},{1,9},{2,10},{3,11},{4,20},{5,21},{6,22},{7,23},{8,0},{9,1},... | collective-permute-start | bytes 786440 | tf_op jit(solution)/shard_map/ppermute | solution.py:484
  15.9 0.5 %collective-permute-start.4 = (bf16[288,128]{1,0:T(8,128)(2,1)S(1)}, bf16[288,128]{1,0:T(8,128)(2,1)S(1)}, u32[]{:S(2)}, u32[]{:S(2)}) collective-permute-start(bf16[288,128]{1,0:T(8,128)(2,1)S(1)} %get-tuple-element.77), channel_id=1, source_target_pairs={{0,8},{1,9},{2,10},{3,11},{4,20},{5,21},{6,22},{7,23},{8,0},{9,1},... | collective-permute-start | bytes 221192 | tf_op jit(solution)/shard_map/ppermute | solution.py:484
  16.4 0.4 shard_map.116.refs_1_
  16.8 0.4 shard_map.117.refs_4_.refs_1_
  17.2 4.3 %collective-permute-done.4.refs_1_ = bf16[288,128]{1,0:T(8,128)(2,1)S(1)} collective-permute-done((bf16[288,128]{1,0:T(8,128)(2,1)S(1)}, bf16[288,128]{1,0:T(8,128)(2,1)S(1)}, u32[]{:S(2)}, u32[]{:S(2)}) %collective-permute-start.4) | collective-permute-done | bytes 73760 | tf_op jit(solution)/shard_map/ppermute | solution.py:484
  21.6 0.5 %collective-permute-done.2.refs_5_.refs_0_ = bf16[544,256]{1,0:T(8,128)(2,1)S(1)} collective-permute-done((bf16[544,256]{1,0:T(8,128)(2,1)S(1)}, bf16[544,256]{1,0:T(8,128)(2,1)S(1)}, u32[]{:S(2)}, u32[]{:S(2)}) %collective-permute-start.2) | collective-permute-done | bytes 278560 | tf_op jit(solution)/shard_map/ppermute | solution.py:484
  22.2 1.6 %collective-permute-start.6 = (bf16[800,128]{1,0:T(8,128)(2,1)S(1)}, bf16[800,128]{1,0:T(8,128)(2,1)S(1)}, u32[]{:S(2)}, u32[]{:S(2)}) collective-permute-start(bf16[800,128]{1,0:T(8,128)(2,1)S(1)} %get-tuple-element.80.refs_3_), channel_id=1, source_target_pairs={{0,16},{1,17},{2,18},{3,19},{4,12},{5,13},{6,14},{7,15},{8,24},{9,... | collective-permute-start | bytes 614408 | tf_op jit(solution)/shard_map/ppermute | solution.py:484
  23.8 1.8 %collective-permute-start.5 = (bf16[272,256]{1,0:T(8,128)(2,1)S(1)}, bf16[272,256]{1,0:T(8,128)(2,1)S(1)}, u32[]{:S(2)}, u32[]{:S(2)}) collective-permute-start(bf16[272,256]{1,0:T(8,128)(2,1)S(1)} %get-tuple-element.81.refs_4_), channel_id=1, source_target_pairs={{0,2},{1,3},{2,0},{3,1},{4,5},{5,4},{6,7},{7,6},{8,10},{9,11},{10,... | collective-permute-start | bytes 417800 | tf_op jit(solution)/shard_map/ppermute | solution.py:484
  25.6 2.4 %collective-permute-done.6.refs_0_.refs_1_ = bf16[800,128]{1,0:T(8,128)(2,1)S(1)} collective-permute-done((bf16[800,128]{1,0:T(8,128)(2,1)S(1)}, bf16[800,128]{1,0:T(8,128)(2,1)S(1)}, u32[]{:S(2)}, u32[]{:S(2)}) %collective-permute-start.6) | collective-permute-done | bytes 204832 | tf_op jit(solution)/shard_map/ppermute | solution.py:484
  28.1 1.8 %collective-permute-start.8 = (bf16[544,128]{1,0:T(8,128)(2,1)S(1)}, bf16[544,128]{1,0:T(8,128)(2,1)S(1)}, u32[]{:S(2)}, u32[]{:S(2)}) collective-permute-start(bf16[544,128]{1,0:T(8,128)(2,1)S(1)} %get-tuple-element.86.refs_3_), channel_id=1, source_target_pairs={{0,2},{1,3},{2,0},{3,1},{4,5},{5,4},{6,7},{7,6},{8,10},{9,11},{10,... | collective-permute-start | bytes 417800 | tf_op jit(solution)/shard_map/ppermute | solution.py:484
  29.9 1.5 %collective-permute-done.5.refs_0_ = bf16[272,256]{1,0:T(8,128)(2,1)S(1)} collective-permute-done((bf16[272,256]{1,0:T(8,128)(2,1)S(1)}, bf16[272,256]{1,0:T(8,128)(2,1)S(1)}, u32[]{:S(2)}, u32[]{:S(2)}) %collective-permute-start.5) | collective-permute-done | bytes 139296 | tf_op jit(solution)/shard_map/ppermute | solution.py:484
  31.5 1.6 %collective-permute-start.7 = (bf16[272,256]{1,0:T(8,128)(2,1)S(1)}, bf16[272,256]{1,0:T(8,128)(2,1)S(1)}, u32[]{:S(2)}, u32[]{:S(2)}) collective-permute-start(bf16[272,256]{1,0:T(8,128)(2,1)S(1)} %get-tuple-element.88.refs_4_), channel_id=1, source_target_pairs={{0,8},{1,9},{2,10},{3,11},{4,20},{5,21},{6,22},{7,23},{8,0},{9,1},... | collective-permute-start | bytes 417800 | tf_op jit(solution)/shard_map/ppermute | solution.py:484
  33.1 3.0 %collective-permute-done.8.refs_0_.refs_1_ = bf16[544,128]{1,0:T(8,128)(2,1)S(1)} collective-permute-done((bf16[544,128]{1,0:T(8,128)(2,1)S(1)}, bf16[544,128]{1,0:T(8,128)(2,1)S(1)}, u32[]{:S(2)}, u32[]{:S(2)}) %collective-permute-start.8) | collective-permute-done | bytes 139296 | tf_op jit(solution)/shard_map/ppermute | solution.py:484
  36.2 0.8 %collective-permute-done.7.refs_0_ = bf16[272,256]{1,0:T(8,128)(2,1)S(1)} collective-permute-done((bf16[272,256]{1,0:T(8,128)(2,1)S(1)}, bf16[272,256]{1,0:T(8,128)(2,1)S(1)}, u32[]{:S(2)}, u32[]{:S(2)}) %collective-permute-start.7) | collective-permute-done | bytes 139296 | tf_op jit(solution)/shard_map/ppermute | solution.py:484
  37.1 2.3 %collective-permute-start.10 = (bf16[272,256]{1,0:T(8,128)(2,1)S(1)}, bf16[272,256]{1,0:T(8,128)(2,1)S(1)}, u32[]{:S(2)}, u32[]{:S(2)}) collective-permute-start(bf16[272,256]{1,0:T(8,128)(2,1)S(1)} %get-tuple-element.93.refs_3_), channel_id=1, source_target_pairs={{0,16},{1,17},{2,18},{3,19},{4,12},{5,13},{6,14},{7,15},{8,24},{9,... | collective-permute-start | bytes 417800 | tf_op jit(solution)/shard_map/ppermute | solution.py:484
  39.4 2.0 %shard_map.124 = (bf16[768,512]{1,0:T(8,128)(2,1)}, f32[8,128]{1,0:T(8,128)S(1)}) custom-call(bf16[384,512]{1,0:T(8,128)(2,1)S(1)} %get-tuple-element.70.refs_0_, bf16[16,512]{1,0:T(8,128)(2,1)S(1)} %get-tuple-element.87.refs_1_, bf16[2048,512]{1,0:T(8,128)(2,1)S(1)} %copy-done, bf16[272,256]{1,0:T(8,128)(2,1)S(1)} %get-tuple-element.93.refs_3_), custom_call_target="tpu_custom_call" | custom-call | tf_op jit(solution)/shard_map/pallas_call | solution.py:47
  41.4 1.0 %collective-permute-done.10.refs_3_ = bf16[272,256]{1,0:T(8,128)(2,1)S(1)} collective-permute-done((bf16[272,256]{1,0:T(8,128)(2,1)S(1)}, bf16[272,256]{1,0:T(8,128)(2,1)S(1)}, u32[]{:S(2)}, u32[]{:S(2)}) %collective-permute-start.10) | collective-permute-done | bytes 139296 | tf_op jit(solution)/shard_map/ppermute | solution.py:484
  42.7 1.6 %collective-permute-start.13 = (bf16[256,128]{1,0:T(8,128)(2,1)S(1)}, bf16[256,128]{1,0:T(8,128)(2,1)S(1)}, u32[]{:S(2)}, u32[]{:S(2)}) collective-permute-start(bf16[256,128]{1,0:T(8,128)(2,1)S(1)} %get-tuple-element.100.refs_2_.refs_1_), channel_id=1, source_target_pairs={{0,12},{1,13},{2,14},{3,15},{4,16},{5,17},{6,18},{7,19},{8,4},{9,5... | collective-permute-start | bytes 196616 | tf_op jit(solution)/shard_map/ppermute | solution.py:495
  44.3 0.5 %collective-permute-start.12 = (bf16[256,128]{1,0:T(8,128)(2,1)S(1)}, bf16[256,128]{1,0:T(8,128)(2,1)S(1)}, u32[]{:S(2)}, u32[]{:S(2)}) collective-permute-start(bf16[256,128]{1,0:T(8,128)(2,1)S(1)} %get-tuple-element.100.refs_2_.refs_1_), channel_id=1, source_target_pairs={{0,8},{1,9},{2,10},{3,11},{4,20},{5,21},{6,22},{7,23},{8,0},{9,1},... | collective-permute-start | bytes 196616 | tf_op jit(solution)/shard_map/ppermute | solution.py:484
  44.8 1.0 %shard_map.126 = (f32[64,512]{1,0:T(8,128)}, f32[8,128]{1,0:T(8,128)S(1)}) custom-call(f32[256,128]{1,0:T(8,128)S(1)} %get-tuple-element.99.refs_0_, bf16[512,256]{1,0:T(8,128)(2,1)S(1)} %copy-done.1, bf16[256,128]{1,0:T(8,128)(2,1)S(1)} %get-tuple-element.100.refs_2_.refs_1_), custom_call_target="tpu_custom_call" | custom-call | tf_op jit(solution)/shard_map/pallas_call | solution.py:47
  45.8 1.0 %collective-permute-done.13.refs_4_ = bf16[256,128]{1,0:T(8,128)(2,1)S(1)} collective-permute-done((bf16[256,128]{1,0:T(8,128)(2,1)S(1)}, bf16[256,128]{1,0:T(8,128)(2,1)S(1)}, u32[]{:S(2)}, u32[]{:S(2)}) %collective-permute-start.13) | collective-permute-done | bytes 65568 | tf_op jit(solution)/shard_map/ppermute | solution.py:495
  46.7 1.8 %collective-permute-done.12.refs_3_ = bf16[256,128]{1,0:T(8,128)(2,1)S(1)} collective-permute-done((bf16[256,128]{1,0:T(8,128)(2,1)S(1)}, bf16[256,128]{1,0:T(8,128)(2,1)S(1)}, u32[]{:S(2)}, u32[]{:S(2)}) %collective-permute-start.12) | collective-permute-done | bytes 65568 | tf_op jit(solution)/shard_map/ppermute | solution.py:484
  48.5 1.0 %shard_map.127 = (f32[512,256]{1,0:T(8,128)}, f32[1,512]{1,0:T(1,128)}, bf16[2,256,256]{2,1,0:T(8,128)(2,1)}, f32[2,256]{1,0:T(2,128)}) custom-call(bf16[832,128]{1,0:T(8,128)(2,1)S(1)} %get-tuple-element.102.refs_0_, bf16[256,128]{1,0:T(8,128)(2,1)S(1)} %get-tuple-element.100.refs_2_.refs_1_, bf16[832,128]{1,0:T(8,128)(2,1)S(1)} %collective-permute-done.11.refs_2_, ...), custom_call_target="tpu_custom_call" | custom-call | tf_op jit(solution)/shard_map/pallas_call | solution.py:47
  (28 shorter events, 1.0 us)
Async XLA Ops:
  1.3 5.3 %copy-start = (bf16[2048,512]{1,0:T(8,128)(2,1)S(1)}, bf16[2048,512]{1,0:T(8,128)(2,1)}, u32[]{:S(2)}) copy-start(bf16[2048,512]{1,0:T(8,128)(2,1)} %refs_2_.1) | copy-start | bytes 6291460
  1.3 5.3 %copy-start.1 = (bf16[512,256]{1,0:T(8,128)(2,1)S(1)}, bf16[512,256]{1,0:T(8,128)(2,1)}, u32[]{:S(2)}) copy-start(bf16[512,256]{1,0:T(8,128)(2,1)} %refs_1_.3) | copy-start | bytes 786436
  1.3 5.3 %copy-start.2 = (bf16[2,1024,256]{2,1,0:T(8,128)(2,1)S(1)}, bf16[2,1024,256]{2,1,0:T(8,128)(2,1)}, u32[]{:S(2)}) copy-start(bf16[2,1024,256]{2,1,0:T(8,128)(2,1)} %refs_4_.3) | copy-start | bytes 3145732
  1.3 5.3 %copy-start.3 = (bf16[768,512]{1,0:T(8,128)(2,1)S(1)}, bf16[768,512]{1,0:T(8,128)(2,1)}, u32[]{:S(2)}) copy-start(bf16[768,512]{1,0:T(8,128)(2,1)} %refs_0_.1) | copy-start | bytes 2359300
  1.4 5.3 %copy-start.4 = (s32[1,2,384]{2,1,0:T(2,128)S(1)}, s32[1,2,384]{2,1,0:T(2,128)}, u32[]{:S(2)}) copy-start(s32[1,2,384]{2,1,0:T(2,128)} %param.7) | copy-start | bytes 9220
  1.4 5.3 %copy-start.5 = (f32[512]{0:T(512)S(1)}, f32[512]{0:T(512)}, u32[]{:S(2)}) copy-start(f32[512]{0:T(512)} %param.9) | copy-start | bytes 6148
  1.4 7.6 %collective-permute-start = (bf16[2,512]{1,0:T(2,128)(2,1)S(1)}, bf16[2,512]{1,0:T(2,128)(2,1)S(1)}, u32[]{:S(2)}, u32[]{:S(2)}) collective-permute-start(bf16[2,512]{1,0:T(2,128)(2,1)S(1)} %shard_map.109), channel_id=1, source_target_pairs={{0,1},{1,2},{2,3},{4,5},{5,6},{6,7},{8,9},{9,10},{10,11},{12,13},{... | collective-permute-start | bytes 6152 | tf_op jit(solution)/shard_map/ppermute | solution.py:473
  9.7 2.5 %collective-permute-start.1 = (bf16[3360,128]{1,0:T(8,128)(2,1)S(1)}, bf16[3360,128]{1,0:T(8,128)(2,1)S(1)}, u32[]{:S(2)}, u32[]{:S(2)}) collective-permute-start(bf16[3360,128]{1,0:T(8,128)(2,1)S(1)} %get-tuple-element.69.refs_5_), channel_id=1, source_target_pairs={{0,4},{1,5},{2,6},{3,7},{4,0},{5,1},{6,2},{7,3},{8,12},{9,13},{10,... | collective-permute-start | bytes 2580488 | tf_op jit(solution)/shard_map/ppermute | solution.py:484
  12.5 9.5 %collective-permute-start.2 = (bf16[544,256]{1,0:T(8,128)(2,1)S(1)}, bf16[544,256]{1,0:T(8,128)(2,1)S(1)}, u32[]{:S(2)}, u32[]{:S(2)}) collective-permute-start(bf16[544,256]{1,0:T(8,128)(2,1)S(1)} %shard_map.114.refs_4_), channel_id=1, source_target_pairs={{0,1},{1,0},{2,3},{3,2},{4,6},{5,7},{6,4},{7,5},{8,9},{9,8},{10,11... | collective-permute-start | bytes 835592 | tf_op jit(solution)/shard_map/ppermute | solution.py:484
  14.3 7.2 %collective-permute-start.3 = (bf16[1024,128]{1,0:T(8,128)(2,1)S(1)}, bf16[1024,128]{1,0:T(8,128)(2,1)S(1)}, u32[]{:S(2)}, u32[]{:S(2)}) collective-permute-start(bf16[1024,128]{1,0:T(8,128)(2,1)S(1)} %get-tuple-element.76.refs_1_), channel_id=1, source_target_pairs={{0,8},{1,9},{2,10},{3,11},{4,20},{5,21},{6,22},{7,23},{8,0},{9,1},... | collective-permute-start | bytes 786440 | tf_op jit(solution)/shard_map/ppermute | solution.py:484
  15.9 5.7 %collective-permute-start.4 = (bf16[288,128]{1,0:T(8,128)(2,1)S(1)}, bf16[288,128]{1,0:T(8,128)(2,1)S(1)}, u32[]{:S(2)}, u32[]{:S(2)}) collective-permute-start(bf16[288,128]{1,0:T(8,128)(2,1)S(1)} %get-tuple-element.77), channel_id=1, source_target_pairs={{0,8},{1,9},{2,10},{3,11},{4,20},{5,21},{6,22},{7,23},{8,0},{9,1},... | collective-permute-start | bytes 221192 | tf_op jit(solution)/shard_map/ppermute | solution.py:484
  22.2 5.8 %collective-permute-start.6 = (bf16[800,128]{1,0:T(8,128)(2,1)S(1)}, bf16[800,128]{1,0:T(8,128)(2,1)S(1)}, u32[]{:S(2)}, u32[]{:S(2)}) collective-permute-start(bf16[800,128]{1,0:T(8,128)(2,1)S(1)} %get-tuple-element.80.refs_3_), channel_id=1, source_target_pairs={{0,16},{1,17},{2,18},{3,19},{4,12},{5,13},{6,14},{7,15},{8,24},{9,... | collective-permute-start | bytes 614408 | tf_op jit(solution)/shard_map/ppermute | solution.py:484
  23.8 7.6 %collective-permute-start.5 = (bf16[272,256]{1,0:T(8,128)(2,1)S(1)}, bf16[272,256]{1,0:T(8,128)(2,1)S(1)}, u32[]{:S(2)}, u32[]{:S(2)}) collective-permute-start(bf16[272,256]{1,0:T(8,128)(2,1)S(1)} %get-tuple-element.81.refs_4_), channel_id=1, source_target_pairs={{0,2},{1,3},{2,0},{3,1},{4,5},{5,4},{6,7},{7,6},{8,10},{9,11},{10,... | collective-permute-start | bytes 417800 | tf_op jit(solution)/shard_map/ppermute | solution.py:484
  28.1 7.9 %collective-permute-start.8 = (bf16[544,128]{1,0:T(8,128)(2,1)S(1)}, bf16[544,128]{1,0:T(8,128)(2,1)S(1)}, u32[]{:S(2)}, u32[]{:S(2)}) collective-permute-start(bf16[544,128]{1,0:T(8,128)(2,1)S(1)} %get-tuple-element.86.refs_3_), channel_id=1, source_target_pairs={{0,2},{1,3},{2,0},{3,1},{4,5},{5,4},{6,7},{7,6},{8,10},{9,11},{10,... | collective-permute-start | bytes 417800 | tf_op jit(solution)/shard_map/ppermute | solution.py:484
  31.5 5.5 %collective-permute-start.7 = (bf16[272,256]{1,0:T(8,128)(2,1)S(1)}, bf16[272,256]{1,0:T(8,128)(2,1)S(1)}, u32[]{:S(2)}, u32[]{:S(2)}) collective-permute-start(bf16[272,256]{1,0:T(8,128)(2,1)S(1)} %get-tuple-element.88.refs_4_), channel_id=1, source_target_pairs={{0,8},{1,9},{2,10},{3,11},{4,20},{5,21},{6,22},{7,23},{8,0},{9,1},... | collective-permute-start | bytes 417800 | tf_op jit(solution)/shard_map/ppermute | solution.py:484
  36.1 6.3 %collective-permute-start.9 = (bf16[560,128]{1,0:T(8,128)(2,1)S(1)}, bf16[560,128]{1,0:T(8,128)(2,1)S(1)}, u32[]{:S(2)}, u32[]{:S(2)}) collective-permute-start(bf16[560,128]{1,0:T(8,128)(2,1)S(1)} %get-tuple-element.92.refs_2_), channel_id=1, source_target_pairs={{0,1},{1,0},{2,3},{3,2},{4,6},{5,7},{6,4},{7,5},{8,9},{9,8},{10,11... | collective-permute-start | bytes 430088 | tf_op jit(solution)/shard_map/ppermute | solution.py:484
  37.1 5.3 %collective-permute-start.10 = (bf16[272,256]{1,0:T(8,128)(2,1)S(1)}, bf16[272,256]{1,0:T(8,128)(2,1)S(1)}, u32[]{:S(2)}, u32[]{:S(2)}) collective-permute-start(bf16[272,256]{1,0:T(8,128)(2,1)S(1)} %get-tuple-element.93.refs_3_), channel_id=1, source_target_pairs={{0,16},{1,17},{2,18},{3,19},{4,12},{5,13},{6,14},{7,15},{8,24},{9,... | collective-permute-start | bytes 417800 | tf_op jit(solution)/shard_map/ppermute | solution.py:484
  42.6 6.0 %collective-permute-start.11 = (bf16[832,128]{1,0:T(8,128)(2,1)S(1)}, bf16[832,128]{1,0:T(8,128)(2,1)S(1)}, u32[]{:S(2)}, u32[]{:S(2)}) collective-permute-start(bf16[832,128]{1,0:T(8,128)(2,1)S(1)} %get-tuple-element.102.refs_0_), channel_id=1, source_target_pairs={{0,4},{1,5},{2,6},{3,7},{4,0},{5,1},{6,2},{7,3},{8,12},{9,13},{10,... | collective-permute-start | bytes 638984 | tf_op jit(solution)/shard_map/ppermute | solution.py:484
  42.7 4.1 %collective-permute-start.13 = (bf16[256,128]{1,0:T(8,128)(2,1)S(1)}, bf16[256,128]{1,0:T(8,128)(2,1)S(1)}, u32[]{:S(2)}, u32[]{:S(2)}) collective-permute-start(bf16[256,128]{1,0:T(8,128)(2,1)S(1)} %get-tuple-element.100.refs_2_.refs_1_), channel_id=1, source_target_pairs={{0,12},{1,13},{2,14},{3,15},{4,16},{5,17},{6,18},{7,19},{8,4},{9,5... | collective-permute-start | bytes 196616 | tf_op jit(solution)/shard_map/ppermute | solution.py:495
  44.3 4.3 %collective-permute-start.12 = (bf16[256,128]{1,0:T(8,128)(2,1)S(1)}, bf16[256,128]{1,0:T(8,128)(2,1)S(1)}, u32[]{:S(2)}, u32[]{:S(2)}) collective-permute-start(bf16[256,128]{1,0:T(8,128)(2,1)S(1)} %get-tuple-element.100.refs_2_.refs_1_), channel_id=1, source_target_pairs={{0,8},{1,9},{2,10},{3,11},{4,20},{5,21},{6,22},{7,23},{8,0},{9,1},... | collective-permute-start | bytes 196616 | tf_op jit(solution)/shard_map/ppermute | solution.py:484

commit v19 on v18

--- a/solution.py
+++ b/solution.py
@@ -258,11 +258,11 @@
     return jnp.concatenate(list(digits_of(value)) + [jnp.zeros_like(value)], 0)
 
 
-def first_step_kernel(halves, place, info, got, kept_a, kept_c, extras, send_a, send_c, keep_a, keep_c):
+def first_step_kernel(halves, place, info, got, kept_a, kept_c, extras, send, keep_a, keep_c):
     (rows_a, halved_a), (rows_c, halved_c) = halves
-    split_sum(halved_a, info[place], got, 0, kept_a, rows_a, send_a, 0, keep_a)
-    gone = split_sum(halved_c, info[place], got, rows_a, kept_c, rows_c, send_c, 0, keep_c)
-    send_c[gone:, :] = extras[...].astype(BF16)
+    to = split_sum(halved_a, info[place], got, 0, kept_a, rows_a, send, 0, keep_a)
+    gone = split_sum(halved_c, info[place], got, rows_a, kept_c, rows_c, send, to, keep_c)
+    send[to + gone:, :] = extras[...].astype(BF16)
     keep_c[gone:, :] = extras[...]
 
 
@@ -293,7 +293,7 @@
         place += 1
 
 
-def sums_kernel(first, frames, place, count, info, got, base, row, out):
+def sums_kernel(first, frames, place, count, info, got, base, row, *outs):
     dz = base.shape[1]
     rows = (got.shape[0] - first) // (dz // LANES)
     theirs = jnp.concatenate([got[first + j * rows:first + (j + 1) * rows, :] for j in range(dz // LANES)], 1)
@@ -301,13 +301,13 @@
     ones = jnp.ones((8, frames), BF16)
     size = count + 16
     riding = [row[...].astype(F32)[0:1, :]]
-    for top in range(0, out.shape[0], size):
-        matches = one_hot(codes, 0, info[place], count)
+    for j, out in enumerate(outs):
+        top = j * size
+        matches = one_hot(codes, 0, info[place + j], count)
         total = base[top:top + count, :] + nn(matches, theirs[0:frames, :])
         counts = base[top + count:top + count + 8, 0:count] + nt(ones, matches)
-        out[top:top + count, :] = total.astype(out.dtype)
-        out[top + count:top + size, :] = count_rows(counts[0:1], dz, riding).astype(out.dtype)
-        place += 1
+        out[0:count, :] = total.astype(out.dtype)
+        out[count:, :] = count_rows(counts[0:1], dz, riding).astype(out.dtype)
 
 
 def count_rows(count, width, riding=()):
@@ -333,42 +333,38 @@
     return (block[0:1] * 65536.0 + block[1:2] * 256.0 + block[2:3])[:, :own]
 
 
-def sums_step_kernel(halved, place, row_step, row_place, info, got, kept, *refs):
-    riding = ()
-    if row_step is not None:
-        known, refs = refs[0][...].astype(F32), refs[1:]
-        after, refs = refs[-1], refs[:-1]
-        parts = known.shape[1] // got.shape[1]
-        block = got[row_place[0]:row_place[0] + 16, :].astype(F32)
-        rows = [known[j:j + 1, :] for j in range(1 << row_step)]
-        rows += [riding_row(block, j, parts) for j in range(1 << row_step)]
-        if halved:
-            riding = rows
-            total = rows + [jnp.zeros((16 - len(rows), known.shape[1]), F32)]
-            after[...] = jnp.concatenate(total, 0).astype(BF16)
-        else:
-            wide = jnp.zeros(after.shape, F32)
-            for j in range(1, len(rows)):
-                wide = jnp.where(info[row_place[1]] == j, jnp.broadcast_to(rows[j], after.shape), wide)
-            after[...] = wide.astype(BF16)
-    send, keep = refs
-    dz = got.shape[1]
-    bit = info[place]
-    half = kept.shape[0] // 2 if halved else 0
-    outs = [(send, (1 - bit) * half), (keep, bit * half)] if halved else [(send, 0)]
-    count = row_place[0]
-    size = count + 16
-    for out, start in outs:
-        for top in range(0, keep.shape[0], size):
-            here = top + pl.multiple_of(start, 16) if halved else top
-            sums = pl.ds(here, count)
-            tail = pl.ds(here + count, 16)
-            value = kept[sums, :].astype(F32) + got[sums, :].astype(F32)
-            number = count_of(kept[tail, :].astype(F32), count) + count_of(got[tail, :].astype(F32), count)
-            out[top:top + count, :] = value.astype(out.dtype)
-            out[top + count:top + size, :] = count_rows(number, dz, riding).astype(out.dtype)
-    if not halved:
-        keep[...] = send[0:keep.shape[0], :].astype(F32)
+def add_sums(kept, gots, out, riding=()):
+    count = out.shape[0] - 16
+    value = kept[0:count, :].astype(F32)
+    number = count_of(kept[count:, :].astype(F32), count)
+    for got in gots:
+        value = value + got[0:count, :].astype(F32)
+        number = number + count_of(got[count:, :].astype(F32), count)
+    out[0:count, :] = value.astype(out.dtype)
+    out[count:, :] = count_rows(number, out.shape[1], riding).astype(out.dtype)
+
+
+def forward_sums_kernel(info, got, kept, row, out, known):
+    parts = row.shape[1] // got.shape[1]
+    mine = row[...].astype(F32)[0:1, :]
+    other = riding_row(got[got.shape[0] - 16:, :].astype(F32), 0, parts)
+    add_sums(kept, [got], out, [mine, other])
+    known[...] = jnp.concatenate([mine, other, jnp.zeros((14, row.shape[1]), F32)], 0).astype(BF16)
+
+
+def own_block_kernel(row_place, info, first, second, kept, known, out, after):
+    parts = known.shape[1] // second.shape[1]
+    block = second[second.shape[0] - 16:, :].astype(F32)
+    rows = [known[...].astype(F32)[1:2, :], riding_row(block, 0, parts), riding_row(block, 1, parts)]
+    wide = jnp.zeros(after.shape, F32)
+    for j, row in enumerate(rows):
+        wide = jnp.where(info[row_place] == j + 1, jnp.broadcast_to(row, after.shape), wide)
+    after[...] = wide.astype(BF16)
+    add_sums(kept, [first, second], out)
+
+
+def sums_step_kernel(info, got, kept, out):
+    add_sums(kept, [got], out)
 
 
 def swap_halves(first, second, core):
@@ -380,8 +376,10 @@
     return jnp.where(core == 1, swapped_first, first), jnp.where(core == 1, swapped_second, second)
 
 
-def step_kernel(halves, at_c, place, mixed, info, got, got_c, kept_a, kept_c, send, keep_a, keep_c):
+def step_kernel(halves, at_c, place, mixed, apart, info, got, got_c, kept_a, kept_c, *refs):
     (rows_a, halved_a), (rows_c, halved_c) = halves
+    send, keep_a, keep_c = refs[0], refs[-2], refs[-1]
+    send_c = refs[1] if apart else send
     if mixed:
         to = rows_a // 2
         total = kept_a[0:rows_a, :] + got[0:rows_a, :].astype(F32)
@@ -391,14 +389,15 @@
         keep_a[...] = jnp.where(low, first, second)
     else:
         to = split_sum(halved_a, info[place], got, 0, kept_a, rows_a, send, 0, keep_a)
-    gone = split_sum(halved_c, info[place], got_c, at_c, kept_c, rows_c, send, to, keep_c)
+    to = 0 if apart else to
+    gone = split_sum(halved_c, info[place], got_c, at_c, kept_c, rows_c, send_c, to, keep_c)
     block = digit_block(add_digits(kept_c[rows_c:, :], got_c[at_c + rows_c:, :].astype(F32)))
     keep_c[gone:, :] = block
     to += gone
-    send[to:to + block.shape[0], :] = block.astype(BF16)
+    send_c[to:to + block.shape[0], :] = block.astype(BF16)
     to += block.shape[0]
-    if to < send.shape[0]:
-        send[to:, :] = jnp.zeros((send.shape[0] - to, LANES), BF16)
+    if to < send_c.shape[0]:
+        send_c[to:, :] = jnp.zeros((send_c.shape[0] - to, LANES), BF16)
 
 
 def last_kernel(rows_a, rows, info, got, kept_a, kept_c, sums_got, sums_kept, corr, pieces, mine):
@@ -507,7 +506,7 @@
     dp_bits, tm_bits = log2(dp), log2(tm)
     owner_rows = width // (dp * tm)
 
-    assert dp_bits >= 3 and 1 <= tm_bits <= 2
+    assert dp_bits >= 3 and tm_bits == 2
     pieces_a, pieces_c = width // LANES, channels // LANES
     under = max(dp_bits + tm_bits - log2(pieces_a), 0)
     c_bits = 2
@@ -546,8 +545,7 @@
     at_start = count_bits
     at_codes = at_start + 1
     at_pieces = at_codes + tm
-    at_sums = at_pieces + count_places
-    at_row = at_sums + len(sums_exchanges)
+    at_row = at_pieces + count_places
 
     def info():
         at_dp, at_tm = lax.axis_index("dp"), lax.axis_index("tm")
@@ -561,29 +559,23 @@
             return ((at_dp if axis == "dp" else at_tm) >> b) & 1
 
         bits = [on_core([bit_at(step) for step in steps]) for steps in exchanges]
-        sums_bits = [on_core([bit_at(step) for step in steps]) for steps in sums_exchanges]
         shared = [bit_at(step) for step in exchanges[1]]
         mine_c, other_c = on_core(shared), on_core(shared[::-1])
         places = [2 * core + mine_c, 2 * (1 - core) + other_c, 2 * core + 1 - mine_c, 2 * (1 - core) + 1 - other_c]
         places = [place << (log2(pieces_c) - c_bits) for place in places]
-        lists = []
-        for way in ([b for _, b in up], [b for _, b in up[::-1]]):
-            lists.append([sum(((position >> (tm_bits - 1 - j)) & 1) << b for j, b in enumerate(way)) for position in range(tm)])
-        first_bit = on_core([0, tm_bits - 1])
-        lead = (at_tm >> first_bit) & 1
-        quarters = [on_core([lists[0][j], lists[1][j]]) for j in range(tm // 2)]
-        send_codes = [(q + ((1 - lead) << first_bit)) * per_shard for q in quarters]
-        keep_codes = [(q + (lead << first_bit)) * per_shard for q in quarters]
+        ways = [[b for _, b in up], [b for _, b in up[::-1]]]
+        first_bit, second_bit = on_core([way[0] for way in ways]), on_core([way[1] for way in ways])
+        lead, other = (at_tm >> first_bit) & 1, (at_tm >> second_bit) & 1
+        blocks = [((a << first_bit) + (b << second_bit)) * per_shard for a in (1 - lead, lead) for b in (1 - other, other)]
         differ = at_tm ^ (at_tm + 1)
-        ways = [sum(((differ >> b) & 1) << j for j, b in enumerate(way)) for way in (
-            list(range(tm_bits)), list(reversed(range(tm_bits))))]
-        row_code = jnp.where(at_tm + 1 < tm, on_core(ways), 0)
+        coded = [sum(((differ >> b) & 1) << j for j, b in enumerate(way)) for way in ways]
+        row_code = jnp.where(at_tm + 1 < tm, on_core(coded), 0)
         if turned and not mixed:
             start = ((at_dp * tm + at_tm) * owner_rows) & (LANES - 1)
         else:
             start = on_core([(at_dp * tm + at_tm) * owner_rows, (at_tm >> 1) * owner_rows if mixed else (
                 at_dp * tm + at_tm) * owner_rows]) & (LANES - 1)
-        return bits + [start] + send_codes + keep_codes + places + sums_bits + [row_code]
+        return bits + [start] + blocks + places + [row_code]
 
     halo = shifted(call(halo_kernel, shape((2, channels), BF16), [info, feats[-2:]], flops=10 ** 11), "tm", 1)
     weight, proj, codes = conv_weight, proj_weight, codes[0]
@@ -623,64 +615,74 @@
         return halves, now_a * dz, now_c * dz + extra
 
     size = per_shard + 16
-    sums_rows = size * (tm // 2)
 
     def own_sums(first, after):
         return call(
             functools.partial(own_sums_kernel, frames, at_codes + first, per_shard),
-            shape((sums_rows, dz), F32),
+            shape((2 * size, dz), F32),
             [info, own],
             after=after)
+
+    base = own_sums(0, [extras])
+    halves, rows_a, rows_c = halves_at(1)
+    send, keep_a, keep_c = call(
+        functools.partial(first_step_kernel, halves, 1),
+        [shape((rows_a + rows_c, LANES), BF16), shape((rows_a, LANES), F32), shape((rows_c, LANES), F32)],
+        [info, got, keep_a, keep_c, extras],
+        after=[base])
+    got_core = got
+    got = swapped(send, exchanges[1])
 
     def both_sums(first, base, dtype, after):
         return call(
             functools.partial(sums_kernel, corr_rows, frames, at_codes + first, per_shard),
-            shape((sums_rows, dz), dtype),
-            [info, got, base, row],
+            [shape((size, dz), dtype)] * 2,
+            [info, got_core, base, row],
             after=after)
 
-    sums_send = both_sums(0, own_sums(0, [extras]), BF16, [])
-    sums_got = swapped(sums_send, sums_exchanges[0])
-    halves, rows_a, rows_c = halves_at(1)
-    send, send_c, keep_a, keep_c = call(
-        functools.partial(first_step_kernel, halves, 1),
-        [shape((rows_a, LANES), BF16), shape((rows_c, LANES), BF16), shape((rows_a, LANES), F32),
-         shape((rows_c, LANES), F32)],
-        [info, got, keep_a, keep_c, extras],
-        after=[sums_send])
-    sums_keep = both_sums(tm // 2, own_sums(tm // 2, [send]), F32, [])
-    got, got_c = swapped(send, exchanges[1]), swapped(send_c, exchanges[1])
-    known = row
-    ordered = [sums_keep, sums_got]
+    leaving = both_sums(0, base, BF16, [send])
+    sums_got = [swapped(block, sums_exchanges[0]) for block in leaving]
+    staying = both_sums(2, own_sums(2, [leaving[0]]), F32, [])
+    sums_kept, known = call(
+        forward_sums_kernel,
+        [shape((size, dz), BF16), shape((16, channels), BF16)],
+        [info, sums_got[0], staying[0], row],
+        after=[staying[1]])
+    sums_new = swapped(sums_kept, sums_exchanges[1])
+    got_c = got
+    ordered = [sums_kept]
     for k in range(2, len(exchanges)):
-        at_c = 0 if k == 2 else rows_a
+        at_c = rows_a if got_c is got else 0
         halves, rows_a, rows_c = halves_at(k)
+        apart = k == 2
         spare = 16 * (k == len(exchanges) - 1)
-        send, keep_a, keep_c = call(
-            functools.partial(step_kernel, halves, at_c, k, mixed and k == dp_bits),
-            [shape((rows_a + rows_c + spare, LANES), BF16), shape((rows_a, LANES), F32), shape((rows_c, LANES), F32)],
+        sends = [rows_a, rows_c] if apart else [rows_a + rows_c + spare]
+        *outs, keep_a, keep_c = call(
+            functools.partial(step_kernel, halves, at_c, k, mixed and k == dp_bits, apart),
+            [shape((rows, LANES), BF16) for rows in sends] + [shape((rows_a, LANES), F32), shape((rows_c, LANES), F32)],
             [info, got, got_c, keep_a, keep_c],
             after=ordered)
-        got = got_c = swapped(send, exchanges[k])
-        halved = sums_exchanges[k - 1][0][0] == "tm"
-        sums_rows = sums_rows // 2 if halved else sums_rows
-        row_step = k - 2 if k - 2 < tm_bits else None
-        outs = call(
-            functools.partial(sums_step_kernel, halved, at_sums + k - 1, row_step, (per_shard, at_row)),
-            [shape((sums_rows, dz), BF16), shape((sums_rows, dz), F32)]
-            + [shape((16, channels), BF16)] * (row_step is not None),
-            [info, sums_got, sums_keep] + [known] * (row_step is not None),
-            after=[send])
-        sums_send, sums_keep = outs[:2]
-        known = outs[2] if row_step is not None else known
-        sums_got = swapped(sums_send, sums_exchanges[k - 1])
-        ordered = [sums_send]
-    assert now_a == 1 and sums_rows == size
+        got = got_c = swapped(outs[0], exchanges[k])
+        if apart:
+            got_c = swapped(outs[1], exchanges[k])
+        ordered = [outs[0]]
+        if k == 3:
+            sums_kept, known = call(
+                functools.partial(own_block_kernel, at_row),
+                [shape((size, dz), BF16), shape((16, channels), BF16)],
+                [info, sums_got[1], sums_new, staying[1], known],
+                after=ordered)
+        elif k > 3:
+            sums_kept = call(sums_step_kernel, shape((size, dz), BF16), [info, sums_new, sums_kept], after=ordered)
+        if k > 2:
+            sums_new = swapped(sums_kept, sums_exchanges[k - 1])
+            ordered = [sums_kept]
+    assert now_a == 1
     feat_grad, last = call(
         feat_kernel,
         shape((rows_in, channels), BF16),
         [info, hidden_grad, known, weight],
-        after=[sums_send],
+        after=[sums_kept],
         token=True,
         scratch=[VMEM((frames + 8, channels), F32), VMEM((channels // LANES, rows_in, LANES), F32)],
     )
@@ -689,7 +691,7 @@
         functools.partial(last_kernel, rows_a, rows_c - extra),
         [shape((rows_a, LANES), F32), shape((rows_c - extra, LANES), BF16),
          shape((rows_c + size * (dz // LANES), LANES), BF16)],
-        [info, got, keep_a, keep_c, sums_got, sums_keep],
+        [info, got, keep_a, keep_c, sums_new, sums_kept],
         after=[last])
     parts = [piece, swapped(mine, exchanges[0]), swapped(piece, exchanges[1]), crossed(piece, exchanges[1])]
     conv_grad, last = call(

time: 49.7 us -> 51.8 us (1.042)
  waiting for transfers between devices: 17.6 us -> 21.9 us
  starting transfers between devices: 20.3 us -> 18.1 us
    ppermute x12 -> x13, waiting for transfers between devices: 16.7 us -> 21.3 us  [swapped(): return lax.ppermute(block, ('dp', 'tm'), route)]
    ppermute x1, starting transfers between devices: 1.62 us -> 0.06 us  [crossed(): return lax.ppermute(block, ('dp', 'tm'), route)]
    ppermute x12 -> x13, starting transfers between devices: 13.5 us -> 12.8 us  [swapped(): return lax.ppermute(block, ('dp', 'tm'), route)]
  transfers between devices with their start and end apart: 14 -> 15, of which waited for: 10 -> 7; matrix products, arithmetic and copies ran while one was open for 0% -> 0% of each run, Pallas kernels for 16% -> 16%
where the time goes in v19:
time: 51.8 us; the launch traced here: 51.5 us
  waiting for transfers between devices  21.9 us (42%)
  starting transfers between devices  18.1 us (35%)
  Pallas kernels  9.95 us (19%)
  between operations  0.85 us (2%)
  local copies, waits for them, and re-layouts  0.74 us (1%)
    ppermute x13, waiting for transfers between devices, swapped(): return lax.ppermute(block, ('dp', 'tm'), route)  21.3 us
    ppermute x13, starting transfers between devices, swapped(): return lax.ppermute(block, ('dp', 'tm'), route)  12.8 us
    pallas_call x19, Pallas kernels, call(): pl.pallas_call(kernel, out_shape=shown, in_specs=specs, out_specs=[pl.Blo...  9.95 us
    ppermute x1, starting transfers between devices, shifted(): return lax.ppermute(block, axis, route)  5.19 us
  transfers between devices with their start and end apart: 15, of which 7 were waited for; matrix products, arithmetic and copies ran while one was open for 0% of the time, Pallas kernels for 16%

profile of v19, /device:TPU:0, one launch (start us, length us, event | category | flops | bytes accessed | tf_op | source)
XLA Modules:
  0.0 51.5 jit_solution(13540587560846053077)
XLA Ops:
  0.6 0.7 %slice.3.refs_0_ = bf16[2,512]{1,0:T(2,128)(2,1)S(1)} slice(bf16[768,512]{1,0:T(8,128)(2,1)} %refs_0_.1), slice={[766:768], [0:512]} | slice | bytes 4096 | tf_op jit(solution)/shard_map/slice | solution.py:580
  1.4 5.2 %collective-permute-start = (bf16[2,512]{1,0:T(2,128)(2,1)S(1)}, bf16[2,512]{1,0:T(2,128)(2,1)S(1)}, u32[]{:S(2)}, u32[]{:S(2)}) collective-permute-start(bf16[2,512]{1,0:T(2,128)(2,1)S(1)} %shard_map.109), channel_id=1, source_target_pairs={{0,1},{1,2},{2,3},{4,5},{5,6},{6,7},{8,9},{9,10},{10,11},{12,13},{... | collective-permute-start | bytes 6152 | tf_op jit(solution)/shard_map/ppermute | solution.py:472
  6.7 2.3 %shard_map.110 = (bf16[384,2048]{1,0:T(8,128)(2,1)S(1)}, bf16[384,512]{1,0:T(8,128)(2,1)S(1)}, bf16[384,256]{1,0:T(8,128)(2,1)S(1)}, bf16[256,384]{1,0:T(8,128)(...) custom-call(bf16[768,512]{1,0:T(8,128)(2,1)S(1)} %copy-done.3, ...), custom_call_target="tpu_custom_call" | custom-call | tf_op jit(solution)/shard_map/pallas_call | solution.py:47
  9.0 0.7 %shard_map.111 = (bf16[384,2048]{1,0:T(8,128)(2,1)S(1)}, bf16[384,512]{1,0:T(8,128)(2,1)S(1)}, bf16[384,256]{1,0:T(8,128)(2,1)S(1)}, bf16[256,384]{1,0:T(8,128)(...) custom-call(bf16[2,512]{1,0:T(2,128)(2,1)S(1)} %collective-permute-d, ...), custom_call_target="tpu_custom_call", output_to_operand_aliasing={{0}: (5, {}), {1}: (6, {}), {2}: (7, {}), {3}: (8, {}), {4}... | custom-call | tf_op jit(solution)/shard_map/pallas_call | solution.py:47
  9.8 0.7 %shard_map.112 = (f32[2048,128]{1,0:T(8,128)S(1)}, f32[512,128]{1,0:T(8,128)S(1)}, bf16[384,512]{1,0:T(8,128)(2,1)S(1)}, f32[32,128]{1,0:T(8,128)S(1)}, bf16[16,512]{1,0:T(8,128)(2,1)S(1)}) custom-call(bf16[256,384]{1,0:T(8,128)(2,1)S(1)} %get-tuple-element.65.refs_0_, bf16[384,2048]{1,0:T(8,128)(2,1)S(1)} %get-tuple-element.66.refs_1_, ...), custom_call_target="tpu_custom_call" | custom-call | tf_op jit(solution)/shard_map/pallas_call | solution.py:47
  10.4 0.4 shard_map.113.refs_4_.refs_1_
  10.8 1.3 %collective-permute-done.1.refs_0_ = bf16[3360,128]{1,0:T(8,128)(2,1)S(1)} collective-permute-done((bf16[3360,128]{1,0:T(8,128)(2,1)S(1)}, bf16[3360,128]{1,0:T(8,128)(2,1)S(1)}, u32[]{:S(2)}, u32[]{:S(2)}) %collective-permute-start.1) | collective-permute-done | bytes 860192 | tf_op jit(solution)/shard_map/ppermute | solution.py:483
  12.1 0.1 shard_map.114
  12.3 1.6 %collective-permute-start.5 = (bf16[1312,128]{1,0:T(8,128)(2,1)S(1)}, bf16[1312,128]{1,0:T(8,128)(2,1)S(1)}, u32[]{:S(2)}, u32[]{:S(2)}) collective-permute-start(bf16[1312,128]{1,0:T(8,128)(2,1)S(1)} %get-tuple-element.76.refs_3_), channel_id=1, source_target_pairs={{0,8},{1,9},{2,10},{3,11},{4,20},{5,21},{6,22},{7,23},{8,0},{9,1},... | collective-permute-start | bytes 1007624 | tf_op jit(solution)/shard_map/ppermute | solution.py:483
  13.8 0.4 shard_map.115
  14.2 1.6 %collective-permute-start.3 = (bf16[272,256]{1,0:T(8,128)(2,1)S(1)}, bf16[272,256]{1,0:T(8,128)(2,1)S(1)}, u32[]{:S(2)}, u32[]{:S(2)}) collective-permute-start(bf16[272,256]{1,0:T(8,128)(2,1)S(1)} %get-tuple-element.78.refs_1_), channel_id=1, source_target_pairs={{0,1},{1,0},{2,3},{3,2},{4,6},{5,7},{6,4},{7,5},{8,9},{9,8},{10,11... | collective-permute-start | bytes 417800 | tf_op jit(solution)/shard_map/ppermute | solution.py:483
  15.9 0.4 shard_map.116.refs_1_
  16.3 0.5 collective-permute-start.2
  16.8 0.4 shard_map.117
  17.2 3.3 %collective-permute-done.3.refs_0_ = bf16[272,256]{1,0:T(8,128)(2,1)S(1)} collective-permute-done((bf16[272,256]{1,0:T(8,128)(2,1)S(1)}, bf16[272,256]{1,0:T(8,128)(2,1)S(1)}, u32[]{:S(2)}, u32[]{:S(2)}) %collective-permute-start.3) | collective-permute-done | bytes 139296 | tf_op jit(solution)/shard_map/ppermute | solution.py:483
  20.6 2.4 %collective-permute-start.4 = (bf16[272,256]{1,0:T(8,128)(2,1)S(1)}, bf16[272,256]{1,0:T(8,128)(2,1)S(1)}, u32[]{:S(2)}, u32[]{:S(2)}) collective-permute-start(bf16[272,256]{1,0:T(8,128)(2,1)S(1)} %get-tuple-element.81.refs_4_), channel_id=1, source_target_pairs={{0,2},{1,3},{2,0},{3,1},{4,5},{5,4},{6,7},{7,6},{8,10},{9,11},{10,... | collective-permute-start | bytes 417800 | tf_op jit(solution)/shard_map/ppermute | solution.py:483
  23.1 1.9 %collective-permute-start.6 = (bf16[512,128]{1,0:T(8,128)(2,1)S(1)}, bf16[512,128]{1,0:T(8,128)(2,1)S(1)}, u32[]{:S(2)}, u32[]{:S(2)}) collective-permute-start(bf16[512,128]{1,0:T(8,128)(2,1)S(1)} %get-tuple-element.85.refs_4_), channel_id=1, source_target_pairs={{0,16},{1,17},{2,18},{3,19},{4,12},{5,13},{6,14},{7,15},{8,24},{9,... | collective-permute-start | bytes 393224 | tf_op jit(solution)/shard_map/ppermute | solution.py:483
  25.1 0.2 collective-permute-start.7
  25.2 4.2 %collective-permute-done.7.refs_1_ = bf16[288,128]{1,0:T(8,128)(2,1)S(1)} collective-permute-done((bf16[288,128]{1,0:T(8,128)(2,1)S(1)}, bf16[288,128]{1,0:T(8,128)(2,1)S(1)}, u32[]{:S(2)}, u32[]{:S(2)}) %collective-permute-start.7) | collective-permute-done | bytes 73760 | tf_op jit(solution)/shard_map/ppermute | solution.py:483
  29.4 0.1 shard_map.120
  29.6 0.1 collective-permute-start.9
  29.8 0.8 %collective-permute-start.8 = (bf16[272,256]{1,0:T(8,128)(2,1)S(1)}, bf16[272,256]{1,0:T(8,128)(2,1)S(1)}, u32[]{:S(2)}, u32[]{:S(2)}) collective-permute-start(bf16[272,256]{1,0:T(8,128)(2,1)S(1)} %get-tuple-element.91.refs_4_.refs_1_), channel_id=1, source_target_pairs={{0,8},{1,9},{2,10},{3,11},{4,20},{5,21},{6,22},{7,23},{8,0},{9,1},... | collective-permute-start | bytes 417800 | tf_op jit(solution)/shard_map/ppermute | solution.py:483
  30.6 9.3 %collective-permute-done.9.refs_0_.refs_1_ = bf16[544,128]{1,0:T(8,128)(2,1)S(1)} collective-permute-done((bf16[544,128]{1,0:T(8,128)(2,1)S(1)}, bf16[544,128]{1,0:T(8,128)(2,1)S(1)}, u32[]{:S(2)}, u32[]{:S(2)}) %collective-permute-start.9) | collective-permute-done | bytes 139296 | tf_op jit(solution)/shard_map/ppermute | solution.py:483
  40.1 1.3 %collective-permute-start.11 = (bf16[272,256]{1,0:T(8,128)(2,1)S(1)}, bf16[272,256]{1,0:T(8,128)(2,1)S(1)}, u32[]{:S(2)}, u32[]{:S(2)}) collective-permute-start(bf16[272,256]{1,0:T(8,128)(2,1)S(1)} %shard_map.123.refs_3_.refs_4_), channel_id=1, source_target_pairs={{0,16},{1,17},{2,18},{3,19},{4,12},{5,13},{6,14},{7,15},{8,24},{9,... | collective-permute-start | bytes 417800 | tf_op jit(solution)/shard_map/ppermute | solution.py:483
  41.5 2.0 %shard_map.124 = (bf16[768,512]{1,0:T(8,128)(2,1)}, f32[8,128]{1,0:T(8,128)S(1)}) custom-call(bf16[384,512]{1,0:T(8,128)(2,1)S(1)} %get-tuple-element.70.refs_0_, bf16[16,512]{1,0:T(8,128)(2,1)S(1)} %get-tuple-element.90.refs_1_, bf16[2048,512]{1,0:T(8,128)(2,1)S(1)} %copy-done, bf16[272,256]{1,0:T(8,128)(2,1)S(1)} %shard_map.123.refs_3_.refs_4_), custom_call_target="tpu_custom_call" | custom-call | tf_op jit(solution)/shard_map/pallas_call | solution.py:47
  43.5 1.8 %collective-permute-done.11.refs_3_ = bf16[272,256]{1,0:T(8,128)(2,1)S(1)} collective-permute-done((bf16[272,256]{1,0:T(8,128)(2,1)S(1)}, bf16[272,256]{1,0:T(8,128)(2,1)S(1)}, u32[]{:S(2)}, u32[]{:S(2)}) %collective-permute-start.11) | collective-permute-done | bytes 139296 | tf_op jit(solution)/shard_map/ppermute | solution.py:483
  45.3 0.1 shard_map.125
  45.6 2.1 %collective-permute-start.13 = (bf16[256,128]{1,0:T(8,128)(2,1)S(1)}, bf16[256,128]{1,0:T(8,128)(2,1)S(1)}, u32[]{:S(2)}, u32[]{:S(2)}) collective-permute-start(bf16[256,128]{1,0:T(8,128)(2,1)S(1)} %get-tuple-element.100.refs_2_.refs_1_), channel_id=1, source_target_pairs={{0,8},{1,9},{2,10},{3,11},{4,20},{5,21},{6,22},{7,23},{8,0},{9,1},... | collective-permute-start | bytes 196616 | tf_op jit(solution)/shard_map/ppermute | solution.py:483
  47.6 1.0 %shard_map.126 = (f32[64,512]{1,0:T(8,128)}, f32[8,128]{1,0:T(8,128)S(1)}) custom-call(f32[256,128]{1,0:T(8,128)S(1)} %get-tuple-element.99.refs_0_, bf16[512,256]{1,0:T(8,128)(2,1)S(1)} %copy-done.1, bf16[256,128]{1,0:T(8,128)(2,1)S(1)} %get-tuple-element.100.refs_2_.refs_1_), custom_call_target="tpu_custom_call" | custom-call | tf_op jit(solution)/shard_map/pallas_call | solution.py:47
  48.6 0.6 %collective-permute-done.14.refs_4_ = bf16[256,128]{1,0:T(8,128)(2,1)S(1)} collective-permute-done((bf16[256,128]{1,0:T(8,128)(2,1)S(1)}, bf16[256,128]{1,0:T(8,128)(2,1)S(1)}, u32[]{:S(2)}, u32[]{:S(2)}) %collective-permute-start.14) | collective-permute-done | bytes 65568 | tf_op jit(solution)/shard_map/ppermute | solution.py:494
  49.2 1.3 %collective-permute-done.13.refs_3_ = bf16[256,128]{1,0:T(8,128)(2,1)S(1)} collective-permute-done((bf16[256,128]{1,0:T(8,128)(2,1)S(1)}, bf16[256,128]{1,0:T(8,128)(2,1)S(1)}, u32[]{:S(2)}, u32[]{:S(2)}) %collective-permute-start.13) | collective-permute-done | bytes 65568 | tf_op jit(solution)/shard_map/ppermute | solution.py:483
  50.6 1.0 %shard_map.127 = (f32[512,256]{1,0:T(8,128)}, f32[1,512]{1,0:T(1,128)}, bf16[2,256,256]{2,1,0:T(8,128)(2,1)}, f32[2,256]{1,0:T(2,128)}) custom-call(bf16[832,128]{1,0:T(8,128)(2,1)S(1)} %get-tuple-element.102.refs_0_, bf16[256,128]{1,0:T(8,128)(2,1)S(1)} %get-tuple-element.100.refs_2_.refs_1_, bf16[832,128]{1,0:T(8,128)(2,1)S(1)} %collective-permute-done.12.refs_2_, ...), custom_call_target="tpu_custom_call" | custom-call | tf_op jit(solution)/shard_map/pallas_call | solution.py:47
  (30 shorter events, 0.6 us)
Async XLA Ops:
  1.3 5.3 %copy-start = (bf16[2048,512]{1,0:T(8,128)(2,1)S(1)}, bf16[2048,512]{1,0:T(8,128)(2,1)}, u32[]{:S(2)}) copy-start(bf16[2048,512]{1,0:T(8,128)(2,1)} %refs_2_.1) | copy-start | bytes 6291460
  1.3 5.3 %copy-start.1 = (bf16[512,256]{1,0:T(8,128)(2,1)S(1)}, bf16[512,256]{1,0:T(8,128)(2,1)}, u32[]{:S(2)}) copy-start(bf16[512,256]{1,0:T(8,128)(2,1)} %refs_1_.3) | copy-start | bytes 786436
  1.3 5.3 %copy-start.2 = (bf16[2,1024,256]{2,1,0:T(8,128)(2,1)S(1)}, bf16[2,1024,256]{2,1,0:T(8,128)(2,1)}, u32[]{:S(2)}) copy-start(bf16[2,1024,256]{2,1,0:T(8,128)(2,1)} %refs_4_.3) | copy-start | bytes 3145732
  1.3 5.3 %copy-start.3 = (bf16[768,512]{1,0:T(8,128)(2,1)S(1)}, bf16[768,512]{1,0:T(8,128)(2,1)}, u32[]{:S(2)}) copy-start(bf16[768,512]{1,0:T(8,128)(2,1)} %refs_0_.1) | copy-start | bytes 2359300
  1.4 5.3 %copy-start.4 = (s32[1,2,384]{2,1,0:T(2,128)S(1)}, s32[1,2,384]{2,1,0:T(2,128)}, u32[]{:S(2)}) copy-start(s32[1,2,384]{2,1,0:T(2,128)} %param.7) | copy-start | bytes 9220
  1.4 5.3 %copy-start.5 = (f32[512]{0:T(512)S(1)}, f32[512]{0:T(512)}, u32[]{:S(2)}) copy-start(f32[512]{0:T(512)} %param.9) | copy-start | bytes 6148
  1.4 7.6 %collective-permute-start = (bf16[2,512]{1,0:T(2,128)(2,1)S(1)}, bf16[2,512]{1,0:T(2,128)(2,1)S(1)}, u32[]{:S(2)}, u32[]{:S(2)}) collective-permute-start(bf16[2,512]{1,0:T(2,128)(2,1)S(1)} %shard_map.109), channel_id=1, source_target_pairs={{0,1},{1,2},{2,3},{4,5},{5,6},{6,7},{8,9},{9,10},{10,11},{12,13},{... | collective-permute-start | bytes 6152 | tf_op jit(solution)/shard_map/ppermute | solution.py:472
  9.7 2.5 %collective-permute-start.1 = (bf16[3360,128]{1,0:T(8,128)(2,1)S(1)}, bf16[3360,128]{1,0:T(8,128)(2,1)S(1)}, u32[]{:S(2)}, u32[]{:S(2)}) collective-permute-start(bf16[3360,128]{1,0:T(8,128)(2,1)S(1)} %get-tuple-element.69.refs_5_), channel_id=1, source_target_pairs={{0,4},{1,5},{2,6},{3,7},{4,0},{5,1},{6,2},{7,3},{8,12},{9,13},{10,... | collective-permute-start | bytes 2580488 | tf_op jit(solution)/shard_map/ppermute | solution.py:483
  12.3 10.8 %collective-permute-start.5 = (bf16[1312,128]{1,0:T(8,128)(2,1)S(1)}, bf16[1312,128]{1,0:T(8,128)(2,1)S(1)}, u32[]{:S(2)}, u32[]{:S(2)}) collective-permute-start(bf16[1312,128]{1,0:T(8,128)(2,1)S(1)} %get-tuple-element.76.refs_3_), channel_id=1, source_target_pairs={{0,8},{1,9},{2,10},{3,11},{4,20},{5,21},{6,22},{7,23},{8,0},{9,1},... | collective-permute-start | bytes 1007624 | tf_op jit(solution)/shard_map/ppermute | solution.py:483
  14.2 6.3 %collective-permute-start.3 = (bf16[272,256]{1,0:T(8,128)(2,1)S(1)}, bf16[272,256]{1,0:T(8,128)(2,1)S(1)}, u32[]{:S(2)}, u32[]{:S(2)}) collective-permute-start(bf16[272,256]{1,0:T(8,128)(2,1)S(1)} %get-tuple-element.78.refs_1_), channel_id=1, source_target_pairs={{0,1},{1,0},{2,3},{3,2},{4,6},{5,7},{6,4},{7,5},{8,9},{9,8},{10,11... | collective-permute-start | bytes 417800 | tf_op jit(solution)/shard_map/ppermute | solution.py:483
  16.3 13.4 %collective-permute-start.2 = (bf16[272,256]{1,0:T(8,128)(2,1)S(1)}, bf16[272,256]{1,0:T(8,128)(2,1)S(1)}, u32[]{:S(2)}, u32[]{:S(2)}) collective-permute-start(bf16[272,256]{1,0:T(8,128)(2,1)S(1)} %get-tuple-element.77), channel_id=1, source_target_pairs={{0,1},{1,0},{2,3},{3,2},{4,6},{5,7},{6,4},{7,5},{8,9},{9,8},{10,11... | collective-permute-start | bytes 417800 | tf_op jit(solution)/shard_map/ppermute | solution.py:483
  20.6 9.1 %collective-permute-start.4 = (bf16[272,256]{1,0:T(8,128)(2,1)S(1)}, bf16[272,256]{1,0:T(8,128)(2,1)S(1)}, u32[]{:S(2)}, u32[]{:S(2)}) collective-permute-start(bf16[272,256]{1,0:T(8,128)(2,1)S(1)} %get-tuple-element.81.refs_4_), channel_id=1, source_target_pairs={{0,2},{1,3},{2,0},{3,1},{4,5},{5,4},{6,7},{7,6},{8,10},{9,11},{10,... | collective-permute-start | bytes 417800 | tf_op jit(solution)/shard_map/ppermute | solution.py:483
  23.1 6.3 %collective-permute-start.6 = (bf16[512,128]{1,0:T(8,128)(2,1)S(1)}, bf16[512,128]{1,0:T(8,128)(2,1)S(1)}, u32[]{:S(2)}, u32[]{:S(2)}) collective-permute-start(bf16[512,128]{1,0:T(8,128)(2,1)S(1)} %get-tuple-element.85.refs_4_), channel_id=1, source_target_pairs={{0,16},{1,17},{2,18},{3,19},{4,12},{5,13},{6,14},{7,15},{8,24},{9,... | collective-permute-start | bytes 393224 | tf_op jit(solution)/shard_map/ppermute | solution.py:483
  25.1 4.4 %collective-permute-start.7 = (bf16[288,128]{1,0:T(8,128)(2,1)S(1)}, bf16[288,128]{1,0:T(8,128)(2,1)S(1)}, u32[]{:S(2)}, u32[]{:S(2)}) collective-permute-start(bf16[288,128]{1,0:T(8,128)(2,1)S(1)} %get-tuple-element.86), channel_id=1, source_target_pairs={{0,16},{1,17},{2,18},{3,19},{4,12},{5,13},{6,14},{7,15},{8,24},{9,... | collective-permute-start | bytes 221192 | tf_op jit(solution)/shard_map/ppermute | solution.py:483
  29.6 10.4 %collective-permute-start.9 = (bf16[544,128]{1,0:T(8,128)(2,1)S(1)}, bf16[544,128]{1,0:T(8,128)(2,1)S(1)}, u32[]{:S(2)}, u32[]{:S(2)}) collective-permute-start(bf16[544,128]{1,0:T(8,128)(2,1)S(1)} %get-tuple-element.89.refs_4_), channel_id=1, source_target_pairs={{0,2},{1,3},{2,0},{3,1},{4,5},{5,4},{6,7},{7,6},{8,10},{9,11},{10,... | collective-permute-start | bytes 417800 | tf_op jit(solution)/shard_map/ppermute | solution.py:483
  29.8 10.3 %collective-permute-start.8 = (bf16[272,256]{1,0:T(8,128)(2,1)S(1)}, bf16[272,256]{1,0:T(8,128)(2,1)S(1)}, u32[]{:S(2)}, u32[]{:S(2)}) collective-permute-start(bf16[272,256]{1,0:T(8,128)(2,1)S(1)} %get-tuple-element.91.refs_4_.refs_1_), channel_id=1, source_target_pairs={{0,8},{1,9},{2,10},{3,11},{4,20},{5,21},{6,22},{7,23},{8,0},{9,1},... | collective-permute-start | bytes 417800 | tf_op jit(solution)/shard_map/ppermute | solution.py:483
  40.0 5.3 %collective-permute-start.10 = (bf16[560,128]{1,0:T(8,128)(2,1)S(1)}, bf16[560,128]{1,0:T(8,128)(2,1)S(1)}, u32[]{:S(2)}, u32[]{:S(2)}) collective-permute-start(bf16[560,128]{1,0:T(8,128)(2,1)S(1)} %get-tuple-element.94.refs_2_), channel_id=1, source_target_pairs={{0,1},{1,0},{2,3},{3,2},{4,6},{5,7},{6,4},{7,5},{8,9},{9,8},{10,11... | collective-permute-start | bytes 430088 | tf_op jit(solution)/shard_map/ppermute | solution.py:483
  40.1 5.1 %collective-permute-start.11 = (bf16[272,256]{1,0:T(8,128)(2,1)S(1)}, bf16[272,256]{1,0:T(8,128)(2,1)S(1)}, u32[]{:S(2)}, u32[]{:S(2)}) collective-permute-start(bf16[272,256]{1,0:T(8,128)(2,1)S(1)} %shard_map.123.refs_3_.refs_4_), channel_id=1, source_target_pairs={{0,16},{1,17},{2,18},{3,19},{4,12},{5,13},{6,14},{7,15},{8,24},{9,... | collective-permute-start | bytes 417800 | tf_op jit(solution)/shard_map/ppermute | solution.py:483
  45.4 5.2 %collective-permute-start.12 = (bf16[832,128]{1,0:T(8,128)(2,1)S(1)}, bf16[832,128]{1,0:T(8,128)(2,1)S(1)}, u32[]{:S(2)}, u32[]{:S(2)}) collective-permute-start(bf16[832,128]{1,0:T(8,128)(2,1)S(1)} %get-tuple-element.102.refs_0_), channel_id=1, source_target_pairs={{0,4},{1,5},{2,6},{3,7},{4,0},{5,1},{6,2},{7,3},{8,12},{9,13},{10,... | collective-permute-start | bytes 638984 | tf_op jit(solution)/shard_map/ppermute | solution.py:483
  45.5 3.7 %collective-permute-start.14 = (bf16[256,128]{1,0:T(8,128)(2,1)S(1)}, bf16[256,128]{1,0:T(8,128)(2,1)S(1)}, u32[]{:S(2)}, u32[]{:S(2)}) collective-permute-start(bf16[256,128]{1,0:T(8,128)(2,1)S(1)} %get-tuple-element.100.refs_2_.refs_1_), channel_id=1, source_target_pairs={{0,12},{1,13},{2,14},{3,15},{4,16},{5,17},{6,18},{7,19},{8,4},{9,5... | collective-permute-start | bytes 196616 | tf_op jit(solution)/shard_map/ppermute | solution.py:494
  45.6 5.0 %collective-permute-start.13 = (bf16[256,128]{1,0:T(8,128)(2,1)S(1)}, bf16[256,128]{1,0:T(8,128)(2,1)S(1)}, u32[]{:S(2)}, u32[]{:S(2)}) collective-permute-start(bf16[256,128]{1,0:T(8,128)(2,1)S(1)} %get-tuple-element.100.refs_2_.refs_1_), channel_id=1, source_target_pairs={{0,8},{1,9},{2,10},{3,11},{4,20},{5,21},{6,22},{7,23},{8,0},{9,1},... | collective-permute-start | bytes 196616 | tf_op jit(solution)/shard_map/ppermute | solution.py:483

commit v20 on v18

--- a/solution.py
+++ b/solution.py
@@ -258,11 +258,11 @@
     return jnp.concatenate(list(digits_of(value)) + [jnp.zeros_like(value)], 0)
 
 
-def first_step_kernel(halves, place, info, got, kept_a, kept_c, extras, send_a, send_c, keep_a, keep_c):
+def first_step_kernel(halves, place, info, got, kept_a, kept_c, extras, send, keep_a, keep_c):
     (rows_a, halved_a), (rows_c, halved_c) = halves
-    split_sum(halved_a, info[place], got, 0, kept_a, rows_a, send_a, 0, keep_a)
-    gone = split_sum(halved_c, info[place], got, rows_a, kept_c, rows_c, send_c, 0, keep_c)
-    send_c[gone:, :] = extras[...].astype(BF16)
+    to = split_sum(halved_a, info[place], got, 0, kept_a, rows_a, send, 0, keep_a)
+    gone = split_sum(halved_c, info[place], got, rows_a, kept_c, rows_c, send, to, keep_c)
+    send[to + gone:, :] = extras[...].astype(BF16)
     keep_c[gone:, :] = extras[...]
 
 
@@ -380,7 +380,7 @@
     return jnp.where(core == 1, swapped_first, first), jnp.where(core == 1, swapped_second, second)
 
 
-def step_kernel(halves, at_c, place, mixed, info, got, got_c, kept_a, kept_c, send, keep_a, keep_c):
+def step_kernel(halves, place, mixed, info, got, kept_a, kept_c, send, keep_a, keep_c):
     (rows_a, halved_a), (rows_c, halved_c) = halves
     if mixed:
         to = rows_a // 2
@@ -391,8 +391,8 @@
         keep_a[...] = jnp.where(low, first, second)
     else:
         to = split_sum(halved_a, info[place], got, 0, kept_a, rows_a, send, 0, keep_a)
-    gone = split_sum(halved_c, info[place], got_c, at_c, kept_c, rows_c, send, to, keep_c)
-    block = digit_block(add_digits(kept_c[rows_c:, :], got_c[at_c + rows_c:, :].astype(F32)))
+    gone = split_sum(halved_c, info[place], got, rows_a, kept_c, rows_c, send, to, keep_c)
+    block = digit_block(add_digits(kept_c[rows_c:, :], got[rows_a + rows_c:, :].astype(F32)))
     keep_c[gone:, :] = block
     to += gone
     send[to:to + block.shape[0], :] = block.astype(BF16)
@@ -624,6 +624,7 @@
 
     size = per_shard + 16
     sums_rows = size * (tm // 2)
+    got_core = got
 
     def own_sums(first, after):
         return call(
@@ -636,32 +637,31 @@
         return call(
             functools.partial(sums_kernel, corr_rows, frames, at_codes + first, per_shard),
             shape((sums_rows, dz), dtype),
-            [info, got, base, row],
+            [info, got_core, base, row],
             after=after)
 
-    sums_send = both_sums(0, own_sums(0, [extras]), BF16, [])
+    base = own_sums(0, [extras])
+    halves, rows_a, rows_c = halves_at(1)
+    send, keep_a, keep_c = call(
+        functools.partial(first_step_kernel, halves, 1),
+        [shape((rows_a + rows_c, LANES), BF16), shape((rows_a, LANES), F32), shape((rows_c, LANES), F32)],
+        [info, got, keep_a, keep_c, extras],
+        after=[base])
+    sums_send = both_sums(0, base, BF16, [send])
+    sums_keep = both_sums(tm // 2, own_sums(tm // 2, [sums_send]), F32, [])
     sums_got = swapped(sums_send, sums_exchanges[0])
-    halves, rows_a, rows_c = halves_at(1)
-    send, send_c, keep_a, keep_c = call(
-        functools.partial(first_step_kernel, halves, 1),
-        [shape((rows_a, LANES), BF16), shape((rows_c, LANES), BF16), shape((rows_a, LANES), F32),
-         shape((rows_c, LANES), F32)],
-        [info, got, keep_a, keep_c, extras],
-        after=[sums_send])
-    sums_keep = both_sums(tm // 2, own_sums(tm // 2, [send]), F32, [])
-    got, got_c = swapped(send, exchanges[1]), swapped(send_c, exchanges[1])
+    got = swapped(send, exchanges[1])
     known = row
-    ordered = [sums_keep, sums_got]
+    ordered = [sums_keep]
     for k in range(2, len(exchanges)):
-        at_c = 0 if k == 2 else rows_a
         halves, rows_a, rows_c = halves_at(k)
         spare = 16 * (k == len(exchanges) - 1)
         send, keep_a, keep_c = call(
-            functools.partial(step_kernel, halves, at_c, k, mixed and k == dp_bits),
+            functools.partial(step_kernel, halves, k, mixed and k == dp_bits),
             [shape((rows_a + rows_c + spare, LANES), BF16), shape((rows_a, LANES), F32), shape((rows_c, LANES), F32)],
-            [info, got, got_c, keep_a, keep_c],
+            [info, got, keep_a, keep_c],
             after=ordered)
-        got = got_c = swapped(send, exchanges[k])
+        got = swapped(send, exchanges[k])
         halved = sums_exchanges[k - 1][0][0] == "tm"
         sums_rows = sums_rows // 2 if halved else sums_rows
         row_step = k - 2 if k - 2 < tm_bits else None

time: 49.7 us -> 48.7 us (0.980)
  the two profiles are of different devices: /device:TPU:0 before, /device:TPU:24 now
where the time goes in v20:
time: 48.7 us; the launch traced here: 48.5 us
  waiting for transfers between devices  25.6 us (53%)
  starting transfers between devices  10.9 us (22%)
  Pallas kernels  9.97 us (20%)
  local copies, waits for them, and re-layouts  1.25 us (3%)
  between operations  0.82 us (2%)
    ppermute x11, waiting for transfers between devices, swapped(): return lax.ppermute(block, ('dp', 'tm'), route)  23.6 us
    pallas_call x19, Pallas kernels, call(): pl.pallas_call(kernel, out_shape=shown, in_specs=specs, out_specs=[pl.Blo...  9.97 us
    ppermute x11, starting transfers between devices, swapped(): return lax.ppermute(block, ('dp', 'tm'), route)  9.29 us
    ppermute x1, starting transfers between devices, shifted(): return lax.ppermute(block, axis, route)  1.56 us
    ppermute x1, waiting for transfers between devices, shifted(): return lax.ppermute(block, axis, route)  1.32 us
  transfers between devices with their start and end apart: 13, of which 11 were waited for; matrix products, arithmetic and copies ran while one was open for 0% of the time, Pallas kernels for 17%

profile of v20, /device:TPU:24, one launch (start us, length us, event | category | flops | bytes accessed | tf_op | source)
XLA Modules:
  0.0 48.5 jit_solution(13143945986089180025)
XLA Ops:
  0.6 0.7 %slice.3.refs_0_ = bf16[2,512]{1,0:T(2,128)(2,1)S(1)} slice(bf16[768,512]{1,0:T(8,128)(2,1)} %refs_0_.1), slice={[766:768], [0:512]} | slice | bytes 4096 | tf_op jit(solution)/shard_map/slice | solution.py:588
  1.4 1.6 %collective-permute-start = (bf16[2,512]{1,0:T(2,128)(2,1)S(1)}, bf16[2,512]{1,0:T(2,128)(2,1)S(1)}, u32[]{:S(2)}, u32[]{:S(2)}) collective-permute-start(bf16[2,512]{1,0:T(2,128)(2,1)S(1)} %shard_map.109), channel_id=1, source_target_pairs={{0,1},{1,2},{2,3},{4,5},{5,6},{6,7},{8,9},{9,10},{10,11},{12,13},{... | collective-permute-start | bytes 6152 | tf_op jit(solution)/shard_map/ppermute | solution.py:473
  3.0 0.3 copy-done.2
  3.3 0.2 copy-done.3
  3.5 2.3 %shard_map.110 = (bf16[384,2048]{1,0:T(8,128)(2,1)S(1)}, bf16[384,512]{1,0:T(8,128)(2,1)S(1)}, bf16[384,256]{1,0:T(8,128)(2,1)S(1)}, bf16[256,384]{1,0:T(8,128)(...) custom-call(bf16[768,512]{1,0:T(8,128)(2,1)S(1)} %copy-done.3, ...), custom_call_target="tpu_custom_call" | custom-call | tf_op jit(solution)/shard_map/pallas_call | solution.py:47
  5.8 1.3 %collective-permute-done.refs_0_ = bf16[2,512]{1,0:T(2,128)(2,1)S(1)} collective-permute-done((bf16[2,512]{1,0:T(2,128)(2,1)S(1)}, bf16[2,512]{1,0:T(2,128)(2,1)S(1)}, u32[]{:S(2)}, u32[]{:S(2)}) %collective-permute-start) | collective-permute-done | bytes 2080 | tf_op jit(solution)/shard_map/ppermute | solution.py:473
  7.1 0.7 %shard_map.111 = (bf16[384,2048]{1,0:T(8,128)(2,1)S(1)}, bf16[384,512]{1,0:T(8,128)(2,1)S(1)}, bf16[384,256]{1,0:T(8,128)(2,1)S(1)}, bf16[256,384]{1,0:T(8,128)(...) custom-call(bf16[2,512]{1,0:T(2,128)(2,1)S(1)} %collective-permute-d, ...), custom_call_target="tpu_custom_call", output_to_operand_aliasing={{0}: (5, {}), {1}: (6, {}), {2}: (7, {}), {3}: (8, {}), {4}... | custom-call | tf_op jit(solution)/shard_map/pallas_call | solution.py:47
  7.9 0.7 %shard_map.112 = (f32[2048,128]{1,0:T(8,128)S(1)}, f32[512,128]{1,0:T(8,128)S(1)}, bf16[384,512]{1,0:T(8,128)(2,1)S(1)}, f32[32,128]{1,0:T(8,128)S(1)}, bf16[16,512]{1,0:T(8,128)(2,1)S(1)}) custom-call(bf16[256,384]{1,0:T(8,128)(2,1)S(1)} %get-tuple-element.64.refs_0_, bf16[384,2048]{1,0:T(8,128)(2,1)S(1)} %get-tuple-element.65.refs_1_, ...), custom_call_target="tpu_custom_call" | custom-call | tf_op jit(solution)/shard_map/pallas_call | solution.py:47
  8.6 0.4 shard_map.113.refs_4_.refs_1_
  9.0 1.3 %collective-permute-done.1.refs_0_ = bf16[3360,128]{1,0:T(8,128)(2,1)S(1)} collective-permute-done((bf16[3360,128]{1,0:T(8,128)(2,1)S(1)}, bf16[3360,128]{1,0:T(8,128)(2,1)S(1)}, u32[]{:S(2)}, u32[]{:S(2)}) %collective-permute-start.1) | collective-permute-done | bytes 860192 | tf_op jit(solution)/shard_map/ppermute | solution.py:484
  10.4 1.6 %collective-permute-start.3 = (bf16[1312,128]{1,0:T(8,128)(2,1)S(1)}, bf16[1312,128]{1,0:T(8,128)(2,1)S(1)}, u32[]{:S(2)}, u32[]{:S(2)}) collective-permute-start(bf16[1312,128]{1,0:T(8,128)(2,1)S(1)} %get-tuple-element.75.refs_3_), channel_id=1, source_target_pairs={{0,8},{1,9},{2,10},{3,11},{4,20},{5,21},{6,22},{7,23},{8,0},{9,1},... | collective-permute-start | bytes 1007624 | tf_op jit(solution)/shard_map/ppermute | solution.py:484
  12.0 0.4 shard_map.115.refs_1_
  12.4 0.9 %collective-permute-start.2 = (bf16[544,256]{1,0:T(8,128)(2,1)S(1)}, bf16[544,256]{1,0:T(8,128)(2,1)S(1)}, u32[]{:S(2)}, u32[]{:S(2)}) collective-permute-start(bf16[544,256]{1,0:T(8,128)(2,1)S(1)} %shard_map.115.refs_1_), channel_id=1, source_target_pairs={{0,1},{1,0},{2,3},{3,2},{4,6},{5,7},{6,4},{7,5},{8,9},{9,8},{10,11... | collective-permute-start | bytes 835592 | tf_op jit(solution)/shard_map/ppermute | solution.py:484
  13.3 0.4 shard_map.116.refs_1_
  13.7 0.4 shard_map.117.refs_3_.refs_1_
  14.1 3.5 %collective-permute-done.3.refs_0_ = bf16[1312,128]{1,0:T(8,128)(2,1)S(1)} collective-permute-done((bf16[1312,128]{1,0:T(8,128)(2,1)S(1)}, bf16[1312,128]{1,0:T(8,128)(2,1)S(1)}, u32[]{:S(2)}, u32[]{:S(2)}) %collective-permute-start.3) | collective-permute-done | bytes 335904 | tf_op jit(solution)/shard_map/ppermute | solution.py:484
  17.7 1.6 %collective-permute-start.5 = (bf16[800,128]{1,0:T(8,128)(2,1)S(1)}, bf16[800,128]{1,0:T(8,128)(2,1)S(1)}, u32[]{:S(2)}, u32[]{:S(2)}) collective-permute-start(bf16[800,128]{1,0:T(8,128)(2,1)S(1)} %get-tuple-element.78.refs_3_), channel_id=1, source_target_pairs={{0,16},{1,17},{2,18},{3,19},{4,12},{5,13},{6,14},{7,15},{8,24},{9,... | collective-permute-start | bytes 614408 | tf_op jit(solution)/shard_map/ppermute | solution.py:484
  19.3 2.5 %collective-permute-done.2.refs_0_ = bf16[544,256]{1,0:T(8,128)(2,1)S(1)} collective-permute-done((bf16[544,256]{1,0:T(8,128)(2,1)S(1)}, bf16[544,256]{1,0:T(8,128)(2,1)S(1)}, u32[]{:S(2)}, u32[]{:S(2)}) %collective-permute-start.2) | collective-permute-done | bytes 278560 | tf_op jit(solution)/shard_map/ppermute | solution.py:484
  21.9 0.9 %collective-permute-start.4 = (bf16[272,256]{1,0:T(8,128)(2,1)S(1)}, bf16[272,256]{1,0:T(8,128)(2,1)S(1)}, u32[]{:S(2)}, u32[]{:S(2)}) collective-permute-start(bf16[272,256]{1,0:T(8,128)(2,1)S(1)} %get-tuple-element.79.refs_3_), channel_id=1, source_target_pairs={{0,2},{1,3},{2,0},{3,1},{4,5},{5,4},{6,7},{7,6},{8,10},{9,11},{10,... | collective-permute-start | bytes 417800 | tf_op jit(solution)/shard_map/ppermute | solution.py:484
  22.8 0.7 %collective-permute-done.5.refs_0_ = bf16[800,128]{1,0:T(8,128)(2,1)S(1)} collective-permute-done((bf16[800,128]{1,0:T(8,128)(2,1)S(1)}, bf16[800,128]{1,0:T(8,128)(2,1)S(1)}, u32[]{:S(2)}, u32[]{:S(2)}) %collective-permute-start.5) | collective-permute-done | bytes 204832 | tf_op jit(solution)/shard_map/ppermute | solution.py:484
  23.7 1.4 %collective-permute-start.7 = (bf16[544,128]{1,0:T(8,128)(2,1)S(1)}, bf16[544,128]{1,0:T(8,128)(2,1)S(1)}, u32[]{:S(2)}, u32[]{:S(2)}) collective-permute-start(bf16[544,128]{1,0:T(8,128)(2,1)S(1)} %get-tuple-element.84.refs_3_), channel_id=1, source_target_pairs={{0,2},{1,3},{2,0},{3,1},{4,5},{5,4},{6,7},{7,6},{8,10},{9,11},{10,... | collective-permute-start | bytes 417800 | tf_op jit(solution)/shard_map/ppermute | solution.py:484
  25.1 5.4 %collective-permute-done.4.refs_0_ = bf16[272,256]{1,0:T(8,128)(2,1)S(1)} collective-permute-done((bf16[272,256]{1,0:T(8,128)(2,1)S(1)}, bf16[272,256]{1,0:T(8,128)(2,1)S(1)}, u32[]{:S(2)}, u32[]{:S(2)}) %collective-permute-start.4) | collective-permute-done | bytes 139296 | tf_op jit(solution)/shard_map/ppermute | solution.py:484
  30.7 2.0 %collective-permute-done.7.refs_0_ = bf16[544,128]{1,0:T(8,128)(2,1)S(1)} collective-permute-done((bf16[544,128]{1,0:T(8,128)(2,1)S(1)}, bf16[544,128]{1,0:T(8,128)(2,1)S(1)}, u32[]{:S(2)}, u32[]{:S(2)}) %collective-permute-start.7) | collective-permute-done | bytes 139296 | tf_op jit(solution)/shard_map/ppermute | solution.py:484
  32.8 4.3 %collective-permute-done.6.refs_0_ = bf16[272,256]{1,0:T(8,128)(2,1)S(1)} collective-permute-done((bf16[272,256]{1,0:T(8,128)(2,1)S(1)}, bf16[272,256]{1,0:T(8,128)(2,1)S(1)}, u32[]{:S(2)}, u32[]{:S(2)}) %collective-permute-start.6) | collective-permute-done | bytes 139296 | tf_op jit(solution)/shard_map/ppermute | solution.py:484
  37.1 0.6 %collective-permute-start.9 = (bf16[272,256]{1,0:T(8,128)(2,1)S(1)}, bf16[272,256]{1,0:T(8,128)(2,1)S(1)}, u32[]{:S(2)}, u32[]{:S(2)}) collective-permute-start(bf16[272,256]{1,0:T(8,128)(2,1)S(1)} %get-tuple-element.91.refs_3_), channel_id=1, source_target_pairs={{0,16},{1,17},{2,18},{3,19},{4,12},{5,13},{6,14},{7,15},{8,24},{9,... | collective-permute-start | bytes 417800 | tf_op jit(solution)/shard_map/ppermute | solution.py:484
  37.6 2.0 %shard_map.124 = (bf16[768,512]{1,0:T(8,128)(2,1)}, f32[8,128]{1,0:T(8,128)S(1)}) custom-call(bf16[384,512]{1,0:T(8,128)(2,1)S(1)} %get-tuple-element.69.refs_0_, bf16[16,512]{1,0:T(8,128)(2,1)S(1)} %get-tuple-element.85.refs_1_, bf16[2048,512]{1,0:T(8,128)(2,1)S(1)} %copy-done, bf16[272,256]{1,0:T(8,128)(2,1)S(1)} %get-tuple-element.91.refs_3_), custom_call_target="tpu_custom_call" | custom-call | tf_op jit(solution)/shard_map/pallas_call | solution.py:47
  39.7 2.5 %collective-permute-done.9.refs_3_ = bf16[272,256]{1,0:T(8,128)(2,1)S(1)} collective-permute-done((bf16[272,256]{1,0:T(8,128)(2,1)S(1)}, bf16[272,256]{1,0:T(8,128)(2,1)S(1)}, u32[]{:S(2)}, u32[]{:S(2)}) %collective-permute-start.9) | collective-permute-done | bytes 139296 | tf_op jit(solution)/shard_map/ppermute | solution.py:484
  42.5 2.1 %collective-permute-start.11 = (bf16[256,128]{1,0:T(8,128)(2,1)S(1)}, bf16[256,128]{1,0:T(8,128)(2,1)S(1)}, u32[]{:S(2)}, u32[]{:S(2)}) collective-permute-start(bf16[256,128]{1,0:T(8,128)(2,1)S(1)} %get-tuple-element.98.refs_2_.refs_1_), channel_id=1, source_target_pairs={{0,8},{1,9},{2,10},{3,11},{4,20},{5,21},{6,22},{7,23},{8,0},{9,1},... | collective-permute-start | bytes 196616 | tf_op jit(solution)/shard_map/ppermute | solution.py:484
  44.6 1.0 %shard_map.126 = (f32[64,512]{1,0:T(8,128)}, f32[8,128]{1,0:T(8,128)S(1)}) custom-call(f32[256,128]{1,0:T(8,128)S(1)} %get-tuple-element.97.refs_0_, bf16[512,256]{1,0:T(8,128)(2,1)S(1)} %copy-done.1, bf16[256,128]{1,0:T(8,128)(2,1)S(1)} %get-tuple-element.98.refs_2_.refs_1_), custom_call_target="tpu_custom_call" | custom-call | tf_op jit(solution)/shard_map/pallas_call | solution.py:47
  45.6 0.6 %collective-permute-done.12.refs_4_ = bf16[256,128]{1,0:T(8,128)(2,1)S(1)} collective-permute-done((bf16[256,128]{1,0:T(8,128)(2,1)S(1)}, bf16[256,128]{1,0:T(8,128)(2,1)S(1)}, u32[]{:S(2)}, u32[]{:S(2)}) %collective-permute-start.12) | collective-permute-done | bytes 65568 | tf_op jit(solution)/shard_map/ppermute | solution.py:495
  46.2 1.3 %collective-permute-done.11.refs_3_ = bf16[256,128]{1,0:T(8,128)(2,1)S(1)} collective-permute-done((bf16[256,128]{1,0:T(8,128)(2,1)S(1)}, bf16[256,128]{1,0:T(8,128)(2,1)S(1)}, u32[]{:S(2)}, u32[]{:S(2)}) %collective-permute-start.11) | collective-permute-done | bytes 65568 | tf_op jit(solution)/shard_map/ppermute | solution.py:484
  47.5 1.0 %shard_map.127 = (f32[512,256]{1,0:T(8,128)}, f32[1,512]{1,0:T(1,128)}, bf16[2,256,256]{2,1,0:T(8,128)(2,1)}, f32[2,256]{1,0:T(2,128)}) custom-call(bf16[832,128]{1,0:T(8,128)(2,1)S(1)} %get-tuple-element.100.refs_0_, bf16[256,128]{1,0:T(8,128)(2,1)S(1)} %get-tuple-element.98.refs_2_.refs_1_, bf16[832,128]{1,0:T(8,128)(2,1)S(1)} %collective-permute-done.10.refs_2_, ...), custom_call_target="tpu_custom_call" | custom-call | tf_op jit(solution)/shard_map/pallas_call | solution.py:47
  (26 shorter events, 1.1 us)
Async XLA Ops:
  1.3 1.6 %copy-start = (bf16[2048,512]{1,0:T(8,128)(2,1)S(1)}, bf16[2048,512]{1,0:T(8,128)(2,1)}, u32[]{:S(2)}) copy-start(bf16[2048,512]{1,0:T(8,128)(2,1)} %refs_2_.1) | copy-start | bytes 6291460
  1.3 1.6 %copy-start.1 = (bf16[512,256]{1,0:T(8,128)(2,1)S(1)}, bf16[512,256]{1,0:T(8,128)(2,1)}, u32[]{:S(2)}) copy-start(bf16[512,256]{1,0:T(8,128)(2,1)} %refs_1_.3) | copy-start | bytes 786436
  1.3 1.9 %copy-start.2 = (bf16[2,1024,256]{2,1,0:T(8,128)(2,1)S(1)}, bf16[2,1024,256]{2,1,0:T(8,128)(2,1)}, u32[]{:S(2)}) copy-start(bf16[2,1024,256]{2,1,0:T(8,128)(2,1)} %refs_4_.3) | copy-start | bytes 3145732
  1.3 2.1 %copy-start.3 = (bf16[768,512]{1,0:T(8,128)(2,1)S(1)}, bf16[768,512]{1,0:T(8,128)(2,1)}, u32[]{:S(2)}) copy-start(bf16[768,512]{1,0:T(8,128)(2,1)} %refs_0_.1) | copy-start | bytes 2359300
  1.4 2.1 %copy-start.4 = (s32[1,2,384]{2,1,0:T(2,128)S(1)}, s32[1,2,384]{2,1,0:T(2,128)}, u32[]{:S(2)}) copy-start(s32[1,2,384]{2,1,0:T(2,128)} %param.7) | copy-start | bytes 9220
  1.4 2.1 %copy-start.5 = (f32[512]{0:T(512)S(1)}, f32[512]{0:T(512)}, u32[]{:S(2)}) copy-start(f32[512]{0:T(512)} %param.9) | copy-start | bytes 6148
  1.4 5.7 %collective-permute-start = (bf16[2,512]{1,0:T(2,128)(2,1)S(1)}, bf16[2,512]{1,0:T(2,128)(2,1)S(1)}, u32[]{:S(2)}, u32[]{:S(2)}) collective-permute-start(bf16[2,512]{1,0:T(2,128)(2,1)S(1)} %shard_map.109), channel_id=1, source_target_pairs={{0,1},{1,2},{2,3},{4,5},{5,6},{6,7},{8,9},{9,10},{10,11},{12,13},{... | collective-permute-start | bytes 6152 | tf_op jit(solution)/shard_map/ppermute | solution.py:473
  7.8 2.5 %collective-permute-start.1 = (bf16[3360,128]{1,0:T(8,128)(2,1)S(1)}, bf16[3360,128]{1,0:T(8,128)(2,1)S(1)}, u32[]{:S(2)}, u32[]{:S(2)}) collective-permute-start(bf16[3360,128]{1,0:T(8,128)(2,1)S(1)} %get-tuple-element.68.refs_5_), channel_id=1, source_target_pairs={{0,4},{1,5},{2,6},{3,7},{4,0},{5,1},{6,2},{7,3},{8,12},{9,13},{10,... | collective-permute-start | bytes 2580488 | tf_op jit(solution)/shard_map/ppermute | solution.py:484
  10.4 7.2 %collective-permute-start.3 = (bf16[1312,128]{1,0:T(8,128)(2,1)S(1)}, bf16[1312,128]{1,0:T(8,128)(2,1)S(1)}, u32[]{:S(2)}, u32[]{:S(2)}) collective-permute-start(bf16[1312,128]{1,0:T(8,128)(2,1)S(1)} %get-tuple-element.75.refs_3_), channel_id=1, source_target_pairs={{0,8},{1,9},{2,10},{3,11},{4,20},{5,21},{6,22},{7,23},{8,0},{9,1},... | collective-permute-start | bytes 1007624 | tf_op jit(solution)/shard_map/ppermute | solution.py:484
  12.4 9.4 %collective-permute-start.2 = (bf16[544,256]{1,0:T(8,128)(2,1)S(1)}, bf16[544,256]{1,0:T(8,128)(2,1)S(1)}, u32[]{:S(2)}, u32[]{:S(2)}) collective-permute-start(bf16[544,256]{1,0:T(8,128)(2,1)S(1)} %shard_map.115.refs_1_), channel_id=1, source_target_pairs={{0,1},{1,0},{2,3},{3,2},{4,6},{5,7},{6,4},{7,5},{8,9},{9,8},{10,11... | collective-permute-start | bytes 835592 | tf_op jit(solution)/shard_map/ppermute | solution.py:484
  17.7 5.8 %collective-permute-start.5 = (bf16[800,128]{1,0:T(8,128)(2,1)S(1)}, bf16[800,128]{1,0:T(8,128)(2,1)S(1)}, u32[]{:S(2)}, u32[]{:S(2)}) collective-permute-start(bf16[800,128]{1,0:T(8,128)(2,1)S(1)} %get-tuple-element.78.refs_3_), channel_id=1, source_target_pairs={{0,16},{1,17},{2,18},{3,19},{4,12},{5,13},{6,14},{7,15},{8,24},{9,... | collective-permute-start | bytes 614408 | tf_op jit(solution)/shard_map/ppermute | solution.py:484
  21.9 8.6 %collective-permute-start.4 = (bf16[272,256]{1,0:T(8,128)(2,1)S(1)}, bf16[272,256]{1,0:T(8,128)(2,1)S(1)}, u32[]{:S(2)}, u32[]{:S(2)}) collective-permute-start(bf16[272,256]{1,0:T(8,128)(2,1)S(1)} %get-tuple-element.79.refs_3_), channel_id=1, source_target_pairs={{0,2},{1,3},{2,0},{3,1},{4,5},{5,4},{6,7},{7,6},{8,10},{9,11},{10,... | collective-permute-start | bytes 417800 | tf_op jit(solution)/shard_map/ppermute | solution.py:484
  23.7 8.9 %collective-permute-start.7 = (bf16[544,128]{1,0:T(8,128)(2,1)S(1)}, bf16[544,128]{1,0:T(8,128)(2,1)S(1)}, u32[]{:S(2)}, u32[]{:S(2)}) collective-permute-start(bf16[544,128]{1,0:T(8,128)(2,1)S(1)} %get-tuple-element.84.refs_3_), channel_id=1, source_target_pairs={{0,2},{1,3},{2,0},{3,1},{4,5},{5,4},{6,7},{7,6},{8,10},{9,11},{10,... | collective-permute-start | bytes 417800 | tf_op jit(solution)/shard_map/ppermute | solution.py:484
  30.6 6.4 %collective-permute-start.6 = (bf16[272,256]{1,0:T(8,128)(2,1)S(1)}, bf16[272,256]{1,0:T(8,128)(2,1)S(1)}, u32[]{:S(2)}, u32[]{:S(2)}) collective-permute-start(bf16[272,256]{1,0:T(8,128)(2,1)S(1)} %get-tuple-element.86.refs_3_), channel_id=1, source_target_pairs={{0,8},{1,9},{2,10},{3,11},{4,20},{5,21},{6,22},{7,23},{8,0},{9,1},... | collective-permute-start | bytes 417800 | tf_op jit(solution)/shard_map/ppermute | solution.py:484
  32.7 9.5 %collective-permute-start.8 = (bf16[560,128]{1,0:T(8,128)(2,1)S(1)}, bf16[560,128]{1,0:T(8,128)(2,1)S(1)}, u32[]{:S(2)}, u32[]{:S(2)}) collective-permute-start(bf16[560,128]{1,0:T(8,128)(2,1)S(1)} %get-tuple-element.90.refs_2_), channel_id=1, source_target_pairs={{0,1},{1,0},{2,3},{3,2},{4,6},{5,7},{6,4},{7,5},{8,9},{9,8},{10,11... | collective-permute-start | bytes 430088 | tf_op jit(solution)/shard_map/ppermute | solution.py:484
  37.1 5.1 %collective-permute-start.9 = (bf16[272,256]{1,0:T(8,128)(2,1)S(1)}, bf16[272,256]{1,0:T(8,128)(2,1)S(1)}, u32[]{:S(2)}, u32[]{:S(2)}) collective-permute-start(bf16[272,256]{1,0:T(8,128)(2,1)S(1)} %get-tuple-element.91.refs_3_), channel_id=1, source_target_pairs={{0,16},{1,17},{2,18},{3,19},{4,12},{5,13},{6,14},{7,15},{8,24},{9,... | collective-permute-start | bytes 417800 | tf_op jit(solution)/shard_map/ppermute | solution.py:484
  42.4 5.2 %collective-permute-start.10 = (bf16[832,128]{1,0:T(8,128)(2,1)S(1)}, bf16[832,128]{1,0:T(8,128)(2,1)S(1)}, u32[]{:S(2)}, u32[]{:S(2)}) collective-permute-start(bf16[832,128]{1,0:T(8,128)(2,1)S(1)} %get-tuple-element.100.refs_0_), channel_id=1, source_target_pairs={{0,4},{1,5},{2,6},{3,7},{4,0},{5,1},{6,2},{7,3},{8,12},{9,13},{10,... | collective-permute-start | bytes 638984 | tf_op jit(solution)/shard_map/ppermute | solution.py:484
  42.5 3.7 %collective-permute-start.12 = (bf16[256,128]{1,0:T(8,128)(2,1)S(1)}, bf16[256,128]{1,0:T(8,128)(2,1)S(1)}, u32[]{:S(2)}, u32[]{:S(2)}) collective-permute-start(bf16[256,128]{1,0:T(8,128)(2,1)S(1)} %get-tuple-element.98.refs_2_.refs_1_), channel_id=1, source_target_pairs={{0,12},{1,13},{2,14},{3,15},{4,16},{5,17},{6,18},{7,19},{8,4},{9,5... | collective-permute-start | bytes 196616 | tf_op jit(solution)/shard_map/ppermute | solution.py:495
  42.5 5.0 %collective-permute-start.11 = (bf16[256,128]{1,0:T(8,128)(2,1)S(1)}, bf16[256,128]{1,0:T(8,128)(2,1)S(1)}, u32[]{:S(2)}, u32[]{:S(2)}) collective-permute-start(bf16[256,128]{1,0:T(8,128)(2,1)S(1)} %get-tuple-element.98.refs_2_.refs_1_), channel_id=1, source_target_pairs={{0,8},{1,9},{2,10},{3,11},{4,20},{5,21},{6,22},{7,23},{8,0},{9,1},... | collective-permute-start | bytes 196616 | tf_op jit(solution)/shard_map/ppermute | solution.py:484

commit v21 on v20

--- a/solution.py
+++ b/solution.py
@@ -29,7 +29,7 @@
 VMEM = pltpu.VMEM
 
 
-def call(body, out_shape, args, after=(), scratch=(), aliases=None, token=False, flops=0):
+def call(body, out_shape, args, after=(), scratch=(), aliases=None, token=False, flops=0, fuse=None):
     info, args = args[0], args[1:]
     count = len(args)
     many = isinstance(out_shape, (list, tuple))
@@ -51,7 +51,7 @@
         out_specs=[pl.BlockSpec(memory_space=VMEM)] * len(shown),
         scratch_shapes=list(scratch),
         input_output_aliases={at - 1: out for at, out in (aliases or {}).items()},
-        compiler_params=pltpu.CompilerParams(vmem_limit_bytes=VMEM_LIMIT),
+        compiler_params=pltpu.CompilerParams(vmem_limit_bytes=VMEM_LIMIT, allow_input_fusion=fuse),
         cost_estimate=pl.CostEstimate(flops=flops, bytes_accessed=0, transcendentals=0),
     )(*args, *after)
     return outs if len(shown) > 1 else outs[0]
@@ -585,7 +585,7 @@
                 at_dp * tm + at_tm) * owner_rows]) & (LANES - 1)
         return bits + [start] + send_codes + keep_codes + places + sums_bits + [row_code]
 
-    halo = shifted(call(halo_kernel, shape((2, channels), BF16), [info, feats[-2:]], flops=10 ** 11), "tm", 1)
+    halo = shifted(call(halo_kernel, shape((2, channels), BF16), [info, feats[-2:]], flops=10 ** 11, fuse=[True]), "tm", 1)
     weight, proj, codes = conv_weight, proj_weight, codes[0]
     extra = 4 * (-(-channels // LANES // 8) * 8)
     code_rows = -(-(2 * -(-frames // dz)) // 16) * 16

time: 48.7 us -> 48.7 us (level)
  no operation moved by 1% of the time
where the time goes in v21:
time: 48.7 us; the launch traced here: 48.5 us
  waiting for transfers between devices  25.6 us (53%)
  starting transfers between devices  10.9 us (22%)
  Pallas kernels  9.97 us (20%)
  local copies, waits for them, and re-layouts  1.25 us (3%)
  between operations  0.82 us (2%)
    ppermute x11, waiting for transfers between devices, swapped(): return lax.ppermute(block, ('dp', 'tm'), route)  23.6 us
    pallas_call x19, Pallas kernels, call(): pl.pallas_call(kernel, out_shape=shown, in_specs=specs, out_specs=[pl.Blo...  9.97 us
    ppermute x11, starting transfers between devices, swapped(): return lax.ppermute(block, ('dp', 'tm'), route)  9.29 us
    ppermute x1, starting transfers between devices, shifted(): return lax.ppermute(block, axis, route)  1.56 us
    ppermute x1, waiting for transfers between devices, shifted(): return lax.ppermute(block, axis, route)  1.32 us
  transfers between devices with their start and end apart: 13, of which 11 were waited for; matrix products, arithmetic and copies ran while one was open for 0% of the time, Pallas kernels for 17%

profile of v21, /device:TPU:24, one launch (start us, length us, event | category | flops | bytes accessed | tf_op | source)
XLA Modules:
  0.0 48.5 jit_solution(13143945986089180025)
XLA Ops:
  0.6 0.7 %slice.3.refs_0_ = bf16[2,512]{1,0:T(2,128)(2,1)S(1)} slice(bf16[768,512]{1,0:T(8,128)(2,1)} %refs_0_.1), slice={[766:768], [0:512]} | slice | bytes 4096 | tf_op jit(solution)/shard_map/slice | solution.py:588
  1.4 1.6 %collective-permute-start = (bf16[2,512]{1,0:T(2,128)(2,1)S(1)}, bf16[2,512]{1,0:T(2,128)(2,1)S(1)}, u32[]{:S(2)}, u32[]{:S(2)}) collective-permute-start(bf16[2,512]{1,0:T(2,128)(2,1)S(1)} %shard_map.109), channel_id=1, source_target_pairs={{0,1},{1,2},{2,3},{4,5},{5,6},{6,7},{8,9},{9,10},{10,11},{12,13},{... | collective-permute-start | bytes 6152 | tf_op jit(solution)/shard_map/ppermute | solution.py:473
  3.0 0.3 copy-done.2
  3.3 0.2 copy-done.3
  3.5 2.3 %shard_map.110 = (bf16[384,2048]{1,0:T(8,128)(2,1)S(1)}, bf16[384,512]{1,0:T(8,128)(2,1)S(1)}, bf16[384,256]{1,0:T(8,128)(2,1)S(1)}, bf16[256,384]{1,0:T(8,128)(...) custom-call(bf16[768,512]{1,0:T(8,128)(2,1)S(1)} %copy-done.3, ...), custom_call_target="tpu_custom_call" | custom-call | tf_op jit(solution)/shard_map/pallas_call | solution.py:47
  5.8 1.3 %collective-permute-done.refs_0_ = bf16[2,512]{1,0:T(2,128)(2,1)S(1)} collective-permute-done((bf16[2,512]{1,0:T(2,128)(2,1)S(1)}, bf16[2,512]{1,0:T(2,128)(2,1)S(1)}, u32[]{:S(2)}, u32[]{:S(2)}) %collective-permute-start) | collective-permute-done | bytes 2080 | tf_op jit(solution)/shard_map/ppermute | solution.py:473
  7.1 0.7 %shard_map.111 = (bf16[384,2048]{1,0:T(8,128)(2,1)S(1)}, bf16[384,512]{1,0:T(8,128)(2,1)S(1)}, bf16[384,256]{1,0:T(8,128)(2,1)S(1)}, bf16[256,384]{1,0:T(8,128)(...) custom-call(bf16[2,512]{1,0:T(2,128)(2,1)S(1)} %collective-permute-d, ...), custom_call_target="tpu_custom_call", output_to_operand_aliasing={{0}: (5, {}), {1}: (6, {}), {2}: (7, {}), {3}: (8, {}), {4}... | custom-call | tf_op jit(solution)/shard_map/pallas_call | solution.py:47
  7.9 0.7 %shard_map.112 = (f32[2048,128]{1,0:T(8,128)S(1)}, f32[512,128]{1,0:T(8,128)S(1)}, bf16[384,512]{1,0:T(8,128)(2,1)S(1)}, f32[32,128]{1,0:T(8,128)S(1)}, bf16[16,512]{1,0:T(8,128)(2,1)S(1)}) custom-call(bf16[256,384]{1,0:T(8,128)(2,1)S(1)} %get-tuple-element.64.refs_0_, bf16[384,2048]{1,0:T(8,128)(2,1)S(1)} %get-tuple-element.65.refs_1_, ...), custom_call_target="tpu_custom_call" | custom-call | tf_op jit(solution)/shard_map/pallas_call | solution.py:47
  8.6 0.4 shard_map.113.refs_4_.refs_1_
  9.0 1.3 %collective-permute-done.1.refs_0_ = bf16[3360,128]{1,0:T(8,128)(2,1)S(1)} collective-permute-done((bf16[3360,128]{1,0:T(8,128)(2,1)S(1)}, bf16[3360,128]{1,0:T(8,128)(2,1)S(1)}, u32[]{:S(2)}, u32[]{:S(2)}) %collective-permute-start.1) | collective-permute-done | bytes 860192 | tf_op jit(solution)/shard_map/ppermute | solution.py:484
  10.4 1.6 %collective-permute-start.3 = (bf16[1312,128]{1,0:T(8,128)(2,1)S(1)}, bf16[1312,128]{1,0:T(8,128)(2,1)S(1)}, u32[]{:S(2)}, u32[]{:S(2)}) collective-permute-start(bf16[1312,128]{1,0:T(8,128)(2,1)S(1)} %get-tuple-element.75.refs_3_), channel_id=1, source_target_pairs={{0,8},{1,9},{2,10},{3,11},{4,20},{5,21},{6,22},{7,23},{8,0},{9,1},... | collective-permute-start | bytes 1007624 | tf_op jit(solution)/shard_map/ppermute | solution.py:484
  12.0 0.4 shard_map.115.refs_1_
  12.4 0.9 %collective-permute-start.2 = (bf16[544,256]{1,0:T(8,128)(2,1)S(1)}, bf16[544,256]{1,0:T(8,128)(2,1)S(1)}, u32[]{:S(2)}, u32[]{:S(2)}) collective-permute-start(bf16[544,256]{1,0:T(8,128)(2,1)S(1)} %shard_map.115.refs_1_), channel_id=1, source_target_pairs={{0,1},{1,0},{2,3},{3,2},{4,6},{5,7},{6,4},{7,5},{8,9},{9,8},{10,11... | collective-permute-start | bytes 835592 | tf_op jit(solution)/shard_map/ppermute | solution.py:484
  13.3 0.4 shard_map.116.refs_1_
  13.7 0.4 shard_map.117.refs_3_.refs_1_
  14.1 3.5 %collective-permute-done.3.refs_0_ = bf16[1312,128]{1,0:T(8,128)(2,1)S(1)} collective-permute-done((bf16[1312,128]{1,0:T(8,128)(2,1)S(1)}, bf16[1312,128]{1,0:T(8,128)(2,1)S(1)}, u32[]{:S(2)}, u32[]{:S(2)}) %collective-permute-start.3) | collective-permute-done | bytes 335904 | tf_op jit(solution)/shard_map/ppermute | solution.py:484
  17.7 1.6 %collective-permute-start.5 = (bf16[800,128]{1,0:T(8,128)(2,1)S(1)}, bf16[800,128]{1,0:T(8,128)(2,1)S(1)}, u32[]{:S(2)}, u32[]{:S(2)}) collective-permute-start(bf16[800,128]{1,0:T(8,128)(2,1)S(1)} %get-tuple-element.78.refs_3_), channel_id=1, source_target_pairs={{0,16},{1,17},{2,18},{3,19},{4,12},{5,13},{6,14},{7,15},{8,24},{9,... | collective-permute-start | bytes 614408 | tf_op jit(solution)/shard_map/ppermute | solution.py:484
  19.3 2.5 %collective-permute-done.2.refs_0_ = bf16[544,256]{1,0:T(8,128)(2,1)S(1)} collective-permute-done((bf16[544,256]{1,0:T(8,128)(2,1)S(1)}, bf16[544,256]{1,0:T(8,128)(2,1)S(1)}, u32[]{:S(2)}, u32[]{:S(2)}) %collective-permute-start.2) | collective-permute-done | bytes 278560 | tf_op jit(solution)/shard_map/ppermute | solution.py:484
  21.9 0.9 %collective-permute-start.4 = (bf16[272,256]{1,0:T(8,128)(2,1)S(1)}, bf16[272,256]{1,0:T(8,128)(2,1)S(1)}, u32[]{:S(2)}, u32[]{:S(2)}) collective-permute-start(bf16[272,256]{1,0:T(8,128)(2,1)S(1)} %get-tuple-element.79.refs_3_), channel_id=1, source_target_pairs={{0,2},{1,3},{2,0},{3,1},{4,5},{5,4},{6,7},{7,6},{8,10},{9,11},{10,... | collective-permute-start | bytes 417800 | tf_op jit(solution)/shard_map/ppermute | solution.py:484
  22.8 0.7 %collective-permute-done.5.refs_0_ = bf16[800,128]{1,0:T(8,128)(2,1)S(1)} collective-permute-done((bf16[800,128]{1,0:T(8,128)(2,1)S(1)}, bf16[800,128]{1,0:T(8,128)(2,1)S(1)}, u32[]{:S(2)}, u32[]{:S(2)}) %collective-permute-start.5) | collective-permute-done | bytes 204832 | tf_op jit(solution)/shard_map/ppermute | solution.py:484
  23.7 1.4 %collective-permute-start.7 = (bf16[544,128]{1,0:T(8,128)(2,1)S(1)}, bf16[544,128]{1,0:T(8,128)(2,1)S(1)}, u32[]{:S(2)}, u32[]{:S(2)}) collective-permute-start(bf16[544,128]{1,0:T(8,128)(2,1)S(1)} %get-tuple-element.84.refs_3_), channel_id=1, source_target_pairs={{0,2},{1,3},{2,0},{3,1},{4,5},{5,4},{6,7},{7,6},{8,10},{9,11},{10,... | collective-permute-start | bytes 417800 | tf_op jit(solution)/shard_map/ppermute | solution.py:484
  25.1 5.4 %collective-permute-done.4.refs_0_ = bf16[272,256]{1,0:T(8,128)(2,1)S(1)} collective-permute-done((bf16[272,256]{1,0:T(8,128)(2,1)S(1)}, bf16[272,256]{1,0:T(8,128)(2,1)S(1)}, u32[]{:S(2)}, u32[]{:S(2)}) %collective-permute-start.4) | collective-permute-done | bytes 139296 | tf_op jit(solution)/shard_map/ppermute | solution.py:484
  30.7 2.0 %collective-permute-done.7.refs_0_ = bf16[544,128]{1,0:T(8,128)(2,1)S(1)} collective-permute-done((bf16[544,128]{1,0:T(8,128)(2,1)S(1)}, bf16[544,128]{1,0:T(8,128)(2,1)S(1)}, u32[]{:S(2)}, u32[]{:S(2)}) %collective-permute-start.7) | collective-permute-done | bytes 139296 | tf_op jit(solution)/shard_map/ppermute | solution.py:484
  32.8 4.3 %collective-permute-done.6.refs_0_ = bf16[272,256]{1,0:T(8,128)(2,1)S(1)} collective-permute-done((bf16[272,256]{1,0:T(8,128)(2,1)S(1)}, bf16[272,256]{1,0:T(8,128)(2,1)S(1)}, u32[]{:S(2)}, u32[]{:S(2)}) %collective-permute-start.6) | collective-permute-done | bytes 139296 | tf_op jit(solution)/shard_map/ppermute | solution.py:484
  37.1 0.6 %collective-permute-start.9 = (bf16[272,256]{1,0:T(8,128)(2,1)S(1)}, bf16[272,256]{1,0:T(8,128)(2,1)S(1)}, u32[]{:S(2)}, u32[]{:S(2)}) collective-permute-start(bf16[272,256]{1,0:T(8,128)(2,1)S(1)} %get-tuple-element.91.refs_3_), channel_id=1, source_target_pairs={{0,16},{1,17},{2,18},{3,19},{4,12},{5,13},{6,14},{7,15},{8,24},{9,... | collective-permute-start | bytes 417800 | tf_op jit(solution)/shard_map/ppermute | solution.py:484
  37.6 2.0 %shard_map.124 = (bf16[768,512]{1,0:T(8,128)(2,1)}, f32[8,128]{1,0:T(8,128)S(1)}) custom-call(bf16[384,512]{1,0:T(8,128)(2,1)S(1)} %get-tuple-element.69.refs_0_, bf16[16,512]{1,0:T(8,128)(2,1)S(1)} %get-tuple-element.85.refs_1_, bf16[2048,512]{1,0:T(8,128)(2,1)S(1)} %copy-done, bf16[272,256]{1,0:T(8,128)(2,1)S(1)} %get-tuple-element.91.refs_3_), custom_call_target="tpu_custom_call" | custom-call | tf_op jit(solution)/shard_map/pallas_call | solution.py:47
  39.7 2.5 %collective-permute-done.9.refs_3_ = bf16[272,256]{1,0:T(8,128)(2,1)S(1)} collective-permute-done((bf16[272,256]{1,0:T(8,128)(2,1)S(1)}, bf16[272,256]{1,0:T(8,128)(2,1)S(1)}, u32[]{:S(2)}, u32[]{:S(2)}) %collective-permute-start.9) | collective-permute-done | bytes 139296 | tf_op jit(solution)/shard_map/ppermute | solution.py:484
  42.5 2.1 %collective-permute-start.11 = (bf16[256,128]{1,0:T(8,128)(2,1)S(1)}, bf16[256,128]{1,0:T(8,128)(2,1)S(1)}, u32[]{:S(2)}, u32[]{:S(2)}) collective-permute-start(bf16[256,128]{1,0:T(8,128)(2,1)S(1)} %get-tuple-element.98.refs_2_.refs_1_), channel_id=1, source_target_pairs={{0,8},{1,9},{2,10},{3,11},{4,20},{5,21},{6,22},{7,23},{8,0},{9,1},... | collective-permute-start | bytes 196616 | tf_op jit(solution)/shard_map/ppermute | solution.py:484
  44.6 1.0 %shard_map.126 = (f32[64,512]{1,0:T(8,128)}, f32[8,128]{1,0:T(8,128)S(1)}) custom-call(f32[256,128]{1,0:T(8,128)S(1)} %get-tuple-element.97.refs_0_, bf16[512,256]{1,0:T(8,128)(2,1)S(1)} %copy-done.1, bf16[256,128]{1,0:T(8,128)(2,1)S(1)} %get-tuple-element.98.refs_2_.refs_1_), custom_call_target="tpu_custom_call" | custom-call | tf_op jit(solution)/shard_map/pallas_call | solution.py:47
  45.6 0.6 %collective-permute-done.12.refs_4_ = bf16[256,128]{1,0:T(8,128)(2,1)S(1)} collective-permute-done((bf16[256,128]{1,0:T(8,128)(2,1)S(1)}, bf16[256,128]{1,0:T(8,128)(2,1)S(1)}, u32[]{:S(2)}, u32[]{:S(2)}) %collective-permute-start.12) | collective-permute-done | bytes 65568 | tf_op jit(solution)/shard_map/ppermute | solution.py:495
  46.2 1.3 %collective-permute-done.11.refs_3_ = bf16[256,128]{1,0:T(8,128)(2,1)S(1)} collective-permute-done((bf16[256,128]{1,0:T(8,128)(2,1)S(1)}, bf16[256,128]{1,0:T(8,128)(2,1)S(1)}, u32[]{:S(2)}, u32[]{:S(2)}) %collective-permute-start.11) | collective-permute-done | bytes 65568 | tf_op jit(solution)/shard_map/ppermute | solution.py:484
  47.5 1.0 %shard_map.127 = (f32[512,256]{1,0:T(8,128)}, f32[1,512]{1,0:T(1,128)}, bf16[2,256,256]{2,1,0:T(8,128)(2,1)}, f32[2,256]{1,0:T(2,128)}) custom-call(bf16[832,128]{1,0:T(8,128)(2,1)S(1)} %get-tuple-element.100.refs_0_, bf16[256,128]{1,0:T(8,128)(2,1)S(1)} %get-tuple-element.98.refs_2_.refs_1_, bf16[832,128]{1,0:T(8,128)(2,1)S(1)} %collective-permute-done.10.refs_2_, ...), custom_call_target="tpu_custom_call" | custom-call | tf_op jit(solution)/shard_map/pallas_call | solution.py:47
  (26 shorter events, 1.1 us)
Async XLA Ops:
  1.3 1.6 %copy-start = (bf16[2048,512]{1,0:T(8,128)(2,1)S(1)}, bf16[2048,512]{1,0:T(8,128)(2,1)}, u32[]{:S(2)}) copy-start(bf16[2048,512]{1,0:T(8,128)(2,1)} %refs_2_.1) | copy-start | bytes 6291460
  1.3 1.6 %copy-start.1 = (bf16[512,256]{1,0:T(8,128)(2,1)S(1)}, bf16[512,256]{1,0:T(8,128)(2,1)}, u32[]{:S(2)}) copy-start(bf16[512,256]{1,0:T(8,128)(2,1)} %refs_1_.3) | copy-start | bytes 786436
  1.3 1.9 %copy-start.2 = (bf16[2,1024,256]{2,1,0:T(8,128)(2,1)S(1)}, bf16[2,1024,256]{2,1,0:T(8,128)(2,1)}, u32[]{:S(2)}) copy-start(bf16[2,1024,256]{2,1,0:T(8,128)(2,1)} %refs_4_.3) | copy-start | bytes 3145732
  1.3 2.1 %copy-start.3 = (bf16[768,512]{1,0:T(8,128)(2,1)S(1)}, bf16[768,512]{1,0:T(8,128)(2,1)}, u32[]{:S(2)}) copy-start(bf16[768,512]{1,0:T(8,128)(2,1)} %refs_0_.1) | copy-start | bytes 2359300
  1.4 2.1 %copy-start.4 = (s32[1,2,384]{2,1,0:T(2,128)S(1)}, s32[1,2,384]{2,1,0:T(2,128)}, u32[]{:S(2)}) copy-start(s32[1,2,384]{2,1,0:T(2,128)} %param.7) | copy-start | bytes 9220
  1.4 2.1 %copy-start.5 = (f32[512]{0:T(512)S(1)}, f32[512]{0:T(512)}, u32[]{:S(2)}) copy-start(f32[512]{0:T(512)} %param.9) | copy-start | bytes 6148
  1.4 5.7 %collective-permute-start = (bf16[2,512]{1,0:T(2,128)(2,1)S(1)}, bf16[2,512]{1,0:T(2,128)(2,1)S(1)}, u32[]{:S(2)}, u32[]{:S(2)}) collective-permute-start(bf16[2,512]{1,0:T(2,128)(2,1)S(1)} %shard_map.109), channel_id=1, source_target_pairs={{0,1},{1,2},{2,3},{4,5},{5,6},{6,7},{8,9},{9,10},{10,11},{12,13},{... | collective-permute-start | bytes 6152 | tf_op jit(solution)/shard_map/ppermute | solution.py:473
  7.8 2.5 %collective-permute-start.1 = (bf16[3360,128]{1,0:T(8,128)(2,1)S(1)}, bf16[3360,128]{1,0:T(8,128)(2,1)S(1)}, u32[]{:S(2)}, u32[]{:S(2)}) collective-permute-start(bf16[3360,128]{1,0:T(8,128)(2,1)S(1)} %get-tuple-element.68.refs_5_), channel_id=1, source_target_pairs={{0,4},{1,5},{2,6},{3,7},{4,0},{5,1},{6,2},{7,3},{8,12},{9,13},{10,... | collective-permute-start | bytes 2580488 | tf_op jit(solution)/shard_map/ppermute | solution.py:484
  10.4 7.2 %collective-permute-start.3 = (bf16[1312,128]{1,0:T(8,128)(2,1)S(1)}, bf16[1312,128]{1,0:T(8,128)(2,1)S(1)}, u32[]{:S(2)}, u32[]{:S(2)}) collective-permute-start(bf16[1312,128]{1,0:T(8,128)(2,1)S(1)} %get-tuple-element.75.refs_3_), channel_id=1, source_target_pairs={{0,8},{1,9},{2,10},{3,11},{4,20},{5,21},{6,22},{7,23},{8,0},{9,1},... | collective-permute-start | bytes 1007624 | tf_op jit(solution)/shard_map/ppermute | solution.py:484
  12.4 9.4 %collective-permute-start.2 = (bf16[544,256]{1,0:T(8,128)(2,1)S(1)}, bf16[544,256]{1,0:T(8,128)(2,1)S(1)}, u32[]{:S(2)}, u32[]{:S(2)}) collective-permute-start(bf16[544,256]{1,0:T(8,128)(2,1)S(1)} %shard_map.115.refs_1_), channel_id=1, source_target_pairs={{0,1},{1,0},{2,3},{3,2},{4,6},{5,7},{6,4},{7,5},{8,9},{9,8},{10,11... | collective-permute-start | bytes 835592 | tf_op jit(solution)/shard_map/ppermute | solution.py:484
  17.7 5.8 %collective-permute-start.5 = (bf16[800,128]{1,0:T(8,128)(2,1)S(1)}, bf16[800,128]{1,0:T(8,128)(2,1)S(1)}, u32[]{:S(2)}, u32[]{:S(2)}) collective-permute-start(bf16[800,128]{1,0:T(8,128)(2,1)S(1)} %get-tuple-element.78.refs_3_), channel_id=1, source_target_pairs={{0,16},{1,17},{2,18},{3,19},{4,12},{5,13},{6,14},{7,15},{8,24},{9,... | collective-permute-start | bytes 614408 | tf_op jit(solution)/shard_map/ppermute | solution.py:484
  21.9 8.6 %collective-permute-start.4 = (bf16[272,256]{1,0:T(8,128)(2,1)S(1)}, bf16[272,256]{1,0:T(8,128)(2,1)S(1)}, u32[]{:S(2)}, u32[]{:S(2)}) collective-permute-start(bf16[272,256]{1,0:T(8,128)(2,1)S(1)} %get-tuple-element.79.refs_3_), channel_id=1, source_target_pairs={{0,2},{1,3},{2,0},{3,1},{4,5},{5,4},{6,7},{7,6},{8,10},{9,11},{10,... | collective-permute-start | bytes 417800 | tf_op jit(solution)/shard_map/ppermute | solution.py:484
  23.7 8.9 %collective-permute-start.7 = (bf16[544,128]{1,0:T(8,128)(2,1)S(1)}, bf16[544,128]{1,0:T(8,128)(2,1)S(1)}, u32[]{:S(2)}, u32[]{:S(2)}) collective-permute-start(bf16[544,128]{1,0:T(8,128)(2,1)S(1)} %get-tuple-element.84.refs_3_), channel_id=1, source_target_pairs={{0,2},{1,3},{2,0},{3,1},{4,5},{5,4},{6,7},{7,6},{8,10},{9,11},{10,... | collective-permute-start | bytes 417800 | tf_op jit(solution)/shard_map/ppermute | solution.py:484
  30.6 6.4 %collective-permute-start.6 = (bf16[272,256]{1,0:T(8,128)(2,1)S(1)}, bf16[272,256]{1,0:T(8,128)(2,1)S(1)}, u32[]{:S(2)}, u32[]{:S(2)}) collective-permute-start(bf16[272,256]{1,0:T(8,128)(2,1)S(1)} %get-tuple-element.86.refs_3_), channel_id=1, source_target_pairs={{0,8},{1,9},{2,10},{3,11},{4,20},{5,21},{6,22},{7,23},{8,0},{9,1},... | collective-permute-start | bytes 417800 | tf_op jit(solution)/shard_map/ppermute | solution.py:484
  32.7 9.5 %collective-permute-start.8 = (bf16[560,128]{1,0:T(8,128)(2,1)S(1)}, bf16[560,128]{1,0:T(8,128)(2,1)S(1)}, u32[]{:S(2)}, u32[]{:S(2)}) collective-permute-start(bf16[560,128]{1,0:T(8,128)(2,1)S(1)} %get-tuple-element.90.refs_2_), channel_id=1, source_target_pairs={{0,1},{1,0},{2,3},{3,2},{4,6},{5,7},{6,4},{7,5},{8,9},{9,8},{10,11... | collective-permute-start | bytes 430088 | tf_op jit(solution)/shard_map/ppermute | solution.py:484
  37.1 5.1 %collective-permute-start.9 = (bf16[272,256]{1,0:T(8,128)(2,1)S(1)}, bf16[272,256]{1,0:T(8,128)(2,1)S(1)}, u32[]{:S(2)}, u32[]{:S(2)}) collective-permute-start(bf16[272,256]{1,0:T(8,128)(2,1)S(1)} %get-tuple-element.91.refs_3_), channel_id=1, source_target_pairs={{0,16},{1,17},{2,18},{3,19},{4,12},{5,13},{6,14},{7,15},{8,24},{9,... | collective-permute-start | bytes 417800 | tf_op jit(solution)/shard_map/ppermute | solution.py:484
  42.4 5.2 %collective-permute-start.10 = (bf16[832,128]{1,0:T(8,128)(2,1)S(1)}, bf16[832,128]{1,0:T(8,128)(2,1)S(1)}, u32[]{:S(2)}, u32[]{:S(2)}) collective-permute-start(bf16[832,128]{1,0:T(8,128)(2,1)S(1)} %get-tuple-element.100.refs_0_), channel_id=1, source_target_pairs={{0,4},{1,5},{2,6},{3,7},{4,0},{5,1},{6,2},{7,3},{8,12},{9,13},{10,... | collective-permute-start | bytes 638984 | tf_op jit(solution)/shard_map/ppermute | solution.py:484
  42.5 3.7 %collective-permute-start.12 = (bf16[256,128]{1,0:T(8,128)(2,1)S(1)}, bf16[256,128]{1,0:T(8,128)(2,1)S(1)}, u32[]{:S(2)}, u32[]{:S(2)}) collective-permute-start(bf16[256,128]{1,0:T(8,128)(2,1)S(1)} %get-tuple-element.98.refs_2_.refs_1_), channel_id=1, source_target_pairs={{0,12},{1,13},{2,14},{3,15},{4,16},{5,17},{6,18},{7,19},{8,4},{9,5... | collective-permute-start | bytes 196616 | tf_op jit(solution)/shard_map/ppermute | solution.py:495
  42.5 5.0 %collective-permute-start.11 = (bf16[256,128]{1,0:T(8,128)(2,1)S(1)}, bf16[256,128]{1,0:T(8,128)(2,1)S(1)}, u32[]{:S(2)}, u32[]{:S(2)}) collective-permute-start(bf16[256,128]{1,0:T(8,128)(2,1)S(1)} %get-tuple-element.98.refs_2_.refs_1_), channel_id=1, source_target_pairs={{0,8},{1,9},{2,10},{3,11},{4,20},{5,21},{6,22},{7,23},{8,0},{9,1},... | collective-permute-start | bytes 196616 | tf_op jit(solution)/shard_map/ppermute | solution.py:484

commit v22 on v20

--- a/solution.py
+++ b/solution.py
@@ -514,7 +514,7 @@
     assert pieces_c >= 4
     whole_bits = [b for b in range(1, dp_bits) if b + tm_bits < under]
     piece_bits = [b for b in range(1, dp_bits) if b + tm_bits >= under]
-    paths = [[("dp", b) for b in bits] for bits in (whole_bits + piece_bits, whole_bits[::-1] + piece_bits[::-1])]
+    paths = [[("dp", b) for b in bits] for bits in (whole_bits[::-1] + piece_bits[::-1], whole_bits + piece_bits)]
     mixed = under == 1 and tm_bits == 2
     turned = mixed or under == 0 or under >= tm_bits
     up = [("tm", b) for b in range(tm_bits)]
@@ -522,7 +522,7 @@
     paths[1] += up if turned else up[::-1]
     exchanges = list(zip([("dp", 0)] + paths[0], [("dp", 0)] + paths[1]))
     sums_up = [("dp", b) for b in range(1, dp_bits)]
-    sums_exchanges = list(zip(up + sums_up, up[::-1] + sums_up[::-1]))
+    sums_exchanges = list(zip(up + sums_up[::-1], up[::-1] + sums_up))
 
     def piece_bit(step):
         axis, b = step

time: 48.7 us -> 48.7 us (level)
  no operation moved by 1% of the time
where the time goes in v22:
time: 48.7 us; the launch traced here: 48.5 us
  waiting for transfers between devices  25.6 us (53%)
  starting transfers between devices  10.9 us (22%)
  Pallas kernels  9.97 us (20%)
  local copies, waits for them, and re-layouts  1.25 us (3%)
  between operations  0.82 us (2%)
    ppermute x11, waiting for transfers between devices, swapped(): return lax.ppermute(block, ('dp', 'tm'), route)  23.7 us
    pallas_call x19, Pallas kernels, call(): pl.pallas_call(kernel, out_shape=shown, in_specs=specs, out_specs=[pl.Blo...  9.97 us
    ppermute x11, starting transfers between devices, swapped(): return lax.ppermute(block, ('dp', 'tm'), route)  9.25 us
    ppermute x1, starting transfers between devices, shifted(): return lax.ppermute(block, axis, route)  1.56 us
    ppermute x1, waiting for transfers between devices, shifted(): return lax.ppermute(block, axis, route)  1.32 us
  transfers between devices with their start and end apart: 13, of which 11 were waited for; matrix products, arithmetic and copies ran while one was open for 0% of the time, Pallas kernels for 17%

profile of v22, /device:TPU:24, one launch (start us, length us, event | category | flops | bytes accessed | tf_op | source)
XLA Modules:
  0.0 48.5 jit_solution(8709303016551393790)
XLA Ops:
  0.6 0.7 %slice.3.refs_0_ = bf16[2,512]{1,0:T(2,128)(2,1)S(1)} slice(bf16[768,512]{1,0:T(8,128)(2,1)} %refs_0_.1), slice={[766:768], [0:512]} | slice | bytes 4096 | tf_op jit(solution)/shard_map/slice | solution.py:588
  1.4 1.6 %collective-permute-start = (bf16[2,512]{1,0:T(2,128)(2,1)S(1)}, bf16[2,512]{1,0:T(2,128)(2,1)S(1)}, u32[]{:S(2)}, u32[]{:S(2)}) collective-permute-start(bf16[2,512]{1,0:T(2,128)(2,1)S(1)} %shard_map.109), channel_id=1, source_target_pairs={{0,1},{1,2},{2,3},{4,5},{5,6},{6,7},{8,9},{9,10},{10,11},{12,13},{... | collective-permute-start | bytes 6152 | tf_op jit(solution)/shard_map/ppermute | solution.py:473
  3.0 0.3 copy-done.2
  3.3 0.2 copy-done.3
  3.5 2.3 %shard_map.110 = (bf16[384,2048]{1,0:T(8,128)(2,1)S(1)}, bf16[384,512]{1,0:T(8,128)(2,1)S(1)}, bf16[384,256]{1,0:T(8,128)(2,1)S(1)}, bf16[256,384]{1,0:T(8,128)(...) custom-call(bf16[768,512]{1,0:T(8,128)(2,1)S(1)} %copy-done.3, ...), custom_call_target="tpu_custom_call" | custom-call | tf_op jit(solution)/shard_map/pallas_call | solution.py:47
  5.8 1.3 %collective-permute-done.refs_0_ = bf16[2,512]{1,0:T(2,128)(2,1)S(1)} collective-permute-done((bf16[2,512]{1,0:T(2,128)(2,1)S(1)}, bf16[2,512]{1,0:T(2,128)(2,1)S(1)}, u32[]{:S(2)}, u32[]{:S(2)}) %collective-permute-start) | collective-permute-done | bytes 2080 | tf_op jit(solution)/shard_map/ppermute | solution.py:473
  7.1 0.7 %shard_map.111 = (bf16[384,2048]{1,0:T(8,128)(2,1)S(1)}, bf16[384,512]{1,0:T(8,128)(2,1)S(1)}, bf16[384,256]{1,0:T(8,128)(2,1)S(1)}, bf16[256,384]{1,0:T(8,128)(...) custom-call(bf16[2,512]{1,0:T(2,128)(2,1)S(1)} %collective-permute-d, ...), custom_call_target="tpu_custom_call", output_to_operand_aliasing={{0}: (5, {}), {1}: (6, {}), {2}: (7, {}), {3}: (8, {}), {4}... | custom-call | tf_op jit(solution)/shard_map/pallas_call | solution.py:47
  7.9 0.6 %shard_map.112 = (f32[2048,128]{1,0:T(8,128)S(1)}, f32[512,128]{1,0:T(8,128)S(1)}, bf16[384,512]{1,0:T(8,128)(2,1)S(1)}, f32[32,128]{1,0:T(8,128)S(1)}, bf16[16,512]{1,0:T(8,128)(2,1)S(1)}) custom-call(bf16[256,384]{1,0:T(8,128)(2,1)S(1)} %get-tuple-element.64.refs_0_, bf16[384,2048]{1,0:T(8,128)(2,1)S(1)} %get-tuple-element.65.refs_1_, ...), custom_call_target="tpu_custom_call" | custom-call | tf_op jit(solution)/shard_map/pallas_call | solution.py:47
  8.6 0.4 shard_map.113.refs_4_.refs_1_
  9.0 1.3 %collective-permute-done.1.refs_0_ = bf16[3360,128]{1,0:T(8,128)(2,1)S(1)} collective-permute-done((bf16[3360,128]{1,0:T(8,128)(2,1)S(1)}, bf16[3360,128]{1,0:T(8,128)(2,1)S(1)}, u32[]{:S(2)}, u32[]{:S(2)}) %collective-permute-start.1) | collective-permute-done | bytes 860192 | tf_op jit(solution)/shard_map/ppermute | solution.py:484
  10.4 1.6 %collective-permute-start.3 = (bf16[1312,128]{1,0:T(8,128)(2,1)S(1)}, bf16[1312,128]{1,0:T(8,128)(2,1)S(1)}, u32[]{:S(2)}, u32[]{:S(2)}) collective-permute-start(bf16[1312,128]{1,0:T(8,128)(2,1)S(1)} %get-tuple-element.75.refs_3_), channel_id=1, source_target_pairs={{0,16},{1,17},{2,18},{3,19},{4,12},{5,13},{6,14},{7,15},{8,24},{9,... | collective-permute-start | bytes 1007624 | tf_op jit(solution)/shard_map/ppermute | solution.py:484
  12.0 0.4 shard_map.115.refs_1_
  12.4 0.9 %collective-permute-start.2 = (bf16[544,256]{1,0:T(8,128)(2,1)S(1)}, bf16[544,256]{1,0:T(8,128)(2,1)S(1)}, u32[]{:S(2)}, u32[]{:S(2)}) collective-permute-start(bf16[544,256]{1,0:T(8,128)(2,1)S(1)} %shard_map.115.refs_1_), channel_id=1, source_target_pairs={{0,1},{1,0},{2,3},{3,2},{4,6},{5,7},{6,4},{7,5},{8,9},{9,8},{10,11... | collective-permute-start | bytes 835592 | tf_op jit(solution)/shard_map/ppermute | solution.py:484
  13.3 0.4 shard_map.116.refs_1_
  13.7 0.4 shard_map.117.refs_3_.refs_1_
  14.2 3.5 %collective-permute-done.3.refs_0_ = bf16[1312,128]{1,0:T(8,128)(2,1)S(1)} collective-permute-done((bf16[1312,128]{1,0:T(8,128)(2,1)S(1)}, bf16[1312,128]{1,0:T(8,128)(2,1)S(1)}, u32[]{:S(2)}, u32[]{:S(2)}) %collective-permute-start.3) | collective-permute-done | bytes 335904 | tf_op jit(solution)/shard_map/ppermute | solution.py:484
  17.7 1.6 %collective-permute-start.5 = (bf16[800,128]{1,0:T(8,128)(2,1)S(1)}, bf16[800,128]{1,0:T(8,128)(2,1)S(1)}, u32[]{:S(2)}, u32[]{:S(2)}) collective-permute-start(bf16[800,128]{1,0:T(8,128)(2,1)S(1)} %get-tuple-element.78.refs_3_), channel_id=1, source_target_pairs={{0,8},{1,9},{2,10},{3,11},{4,20},{5,21},{6,22},{7,23},{8,0},{9,1},... | collective-permute-start | bytes 614408 | tf_op jit(solution)/shard_map/ppermute | solution.py:484
  19.3 2.5 %collective-permute-done.2.refs_0_ = bf16[544,256]{1,0:T(8,128)(2,1)S(1)} collective-permute-done((bf16[544,256]{1,0:T(8,128)(2,1)S(1)}, bf16[544,256]{1,0:T(8,128)(2,1)S(1)}, u32[]{:S(2)}, u32[]{:S(2)}) %collective-permute-start.2) | collective-permute-done | bytes 278560 | tf_op jit(solution)/shard_map/ppermute | solution.py:484
  21.9 0.9 %collective-permute-start.4 = (bf16[272,256]{1,0:T(8,128)(2,1)S(1)}, bf16[272,256]{1,0:T(8,128)(2,1)S(1)}, u32[]{:S(2)}, u32[]{:S(2)}) collective-permute-start(bf16[272,256]{1,0:T(8,128)(2,1)S(1)} %get-tuple-element.79.refs_3_), channel_id=1, source_target_pairs={{0,2},{1,3},{2,0},{3,1},{4,5},{5,4},{6,7},{7,6},{8,10},{9,11},{10,... | collective-permute-start | bytes 417800 | tf_op jit(solution)/shard_map/ppermute | solution.py:484
  22.8 0.8 %collective-permute-done.5.refs_0_ = bf16[800,128]{1,0:T(8,128)(2,1)S(1)} collective-permute-done((bf16[800,128]{1,0:T(8,128)(2,1)S(1)}, bf16[800,128]{1,0:T(8,128)(2,1)S(1)}, u32[]{:S(2)}, u32[]{:S(2)}) %collective-permute-start.5) | collective-permute-done | bytes 204832 | tf_op jit(solution)/shard_map/ppermute | solution.py:484
  23.7 1.4 %collective-permute-start.7 = (bf16[544,128]{1,0:T(8,128)(2,1)S(1)}, bf16[544,128]{1,0:T(8,128)(2,1)S(1)}, u32[]{:S(2)}, u32[]{:S(2)}) collective-permute-start(bf16[544,128]{1,0:T(8,128)(2,1)S(1)} %get-tuple-element.84.refs_3_), channel_id=1, source_target_pairs={{0,2},{1,3},{2,0},{3,1},{4,5},{5,4},{6,7},{7,6},{8,10},{9,11},{10,... | collective-permute-start | bytes 417800 | tf_op jit(solution)/shard_map/ppermute | solution.py:484
  25.1 5.4 %collective-permute-done.4.refs_0_ = bf16[272,256]{1,0:T(8,128)(2,1)S(1)} collective-permute-done((bf16[272,256]{1,0:T(8,128)(2,1)S(1)}, bf16[272,256]{1,0:T(8,128)(2,1)S(1)}, u32[]{:S(2)}, u32[]{:S(2)}) %collective-permute-start.4) | collective-permute-done | bytes 139296 | tf_op jit(solution)/shard_map/ppermute | solution.py:484
  30.6 1.9 %collective-permute-done.7.refs_0_ = bf16[544,128]{1,0:T(8,128)(2,1)S(1)} collective-permute-done((bf16[544,128]{1,0:T(8,128)(2,1)S(1)}, bf16[544,128]{1,0:T(8,128)(2,1)S(1)}, u32[]{:S(2)}, u32[]{:S(2)}) %collective-permute-start.7) | collective-permute-done | bytes 139296 | tf_op jit(solution)/shard_map/ppermute | solution.py:484
  32.6 4.4 %collective-permute-done.6.refs_0_ = bf16[272,256]{1,0:T(8,128)(2,1)S(1)} collective-permute-done((bf16[272,256]{1,0:T(8,128)(2,1)S(1)}, bf16[272,256]{1,0:T(8,128)(2,1)S(1)}, u32[]{:S(2)}, u32[]{:S(2)}) %collective-permute-start.6) | collective-permute-done | bytes 139296 | tf_op jit(solution)/shard_map/ppermute | solution.py:484
  37.1 0.5 %collective-permute-start.9 = (bf16[272,256]{1,0:T(8,128)(2,1)S(1)}, bf16[272,256]{1,0:T(8,128)(2,1)S(1)}, u32[]{:S(2)}, u32[]{:S(2)}) collective-permute-start(bf16[272,256]{1,0:T(8,128)(2,1)S(1)} %get-tuple-element.91.refs_3_), channel_id=1, source_target_pairs={{0,8},{1,9},{2,10},{3,11},{4,20},{5,21},{6,22},{7,23},{8,0},{9,1},... | collective-permute-start | bytes 417800 | tf_op jit(solution)/shard_map/ppermute | solution.py:484
  37.6 2.0 %shard_map.124 = (bf16[768,512]{1,0:T(8,128)(2,1)}, f32[8,128]{1,0:T(8,128)S(1)}) custom-call(bf16[384,512]{1,0:T(8,128)(2,1)S(1)} %get-tuple-element.69.refs_0_, bf16[16,512]{1,0:T(8,128)(2,1)S(1)} %get-tuple-element.85.refs_1_, bf16[2048,512]{1,0:T(8,128)(2,1)S(1)} %copy-done, bf16[272,256]{1,0:T(8,128)(2,1)S(1)} %get-tuple-element.91.refs_3_), custom_call_target="tpu_custom_call" | custom-call | tf_op jit(solution)/shard_map/pallas_call | solution.py:47
  39.7 2.6 %collective-permute-done.9.refs_3_ = bf16[272,256]{1,0:T(8,128)(2,1)S(1)} collective-permute-done((bf16[272,256]{1,0:T(8,128)(2,1)S(1)}, bf16[272,256]{1,0:T(8,128)(2,1)S(1)}, u32[]{:S(2)}, u32[]{:S(2)}) %collective-permute-start.9) | collective-permute-done | bytes 139296 | tf_op jit(solution)/shard_map/ppermute | solution.py:484
  42.5 2.1 %collective-permute-start.11 = (bf16[256,128]{1,0:T(8,128)(2,1)S(1)}, bf16[256,128]{1,0:T(8,128)(2,1)S(1)}, u32[]{:S(2)}, u32[]{:S(2)}) collective-permute-start(bf16[256,128]{1,0:T(8,128)(2,1)S(1)} %get-tuple-element.98.refs_2_.refs_1_), channel_id=1, source_target_pairs={{0,16},{1,17},{2,18},{3,19},{4,12},{5,13},{6,14},{7,15},{8,24},{9,... | collective-permute-start | bytes 196616 | tf_op jit(solution)/shard_map/ppermute | solution.py:484
  44.6 1.0 %shard_map.126 = (f32[64,512]{1,0:T(8,128)}, f32[8,128]{1,0:T(8,128)S(1)}) custom-call(f32[256,128]{1,0:T(8,128)S(1)} %get-tuple-element.97.refs_0_, bf16[512,256]{1,0:T(8,128)(2,1)S(1)} %copy-done.1, bf16[256,128]{1,0:T(8,128)(2,1)S(1)} %get-tuple-element.98.refs_2_.refs_1_), custom_call_target="tpu_custom_call" | custom-call | tf_op jit(solution)/shard_map/pallas_call | solution.py:47
  45.6 0.6 %collective-permute-done.12.refs_4_ = bf16[256,128]{1,0:T(8,128)(2,1)S(1)} collective-permute-done((bf16[256,128]{1,0:T(8,128)(2,1)S(1)}, bf16[256,128]{1,0:T(8,128)(2,1)S(1)}, u32[]{:S(2)}, u32[]{:S(2)}) %collective-permute-start.12) | collective-permute-done | bytes 65568 | tf_op jit(solution)/shard_map/ppermute | solution.py:495
  46.2 1.3 %collective-permute-done.11.refs_3_ = bf16[256,128]{1,0:T(8,128)(2,1)S(1)} collective-permute-done((bf16[256,128]{1,0:T(8,128)(2,1)S(1)}, bf16[256,128]{1,0:T(8,128)(2,1)S(1)}, u32[]{:S(2)}, u32[]{:S(2)}) %collective-permute-start.11) | collective-permute-done | bytes 65568 | tf_op jit(solution)/shard_map/ppermute | solution.py:484
  47.5 1.0 %shard_map.127 = (f32[512,256]{1,0:T(8,128)}, f32[1,512]{1,0:T(1,128)}, bf16[2,256,256]{2,1,0:T(8,128)(2,1)}, f32[2,256]{1,0:T(2,128)}) custom-call(bf16[832,128]{1,0:T(8,128)(2,1)S(1)} %get-tuple-element.100.refs_0_, bf16[256,128]{1,0:T(8,128)(2,1)S(1)} %get-tuple-element.98.refs_2_.refs_1_, bf16[832,128]{1,0:T(8,128)(2,1)S(1)} %collective-permute-done.10.refs_2_, ...), custom_call_target="tpu_custom_call" | custom-call | tf_op jit(solution)/shard_map/pallas_call | solution.py:47
  (26 shorter events, 1.1 us)
Async XLA Ops:
  1.3 1.6 %copy-start = (bf16[2048,512]{1,0:T(8,128)(2,1)S(1)}, bf16[2048,512]{1,0:T(8,128)(2,1)}, u32[]{:S(2)}) copy-start(bf16[2048,512]{1,0:T(8,128)(2,1)} %refs_2_.1) | copy-start | bytes 6291460
  1.3 1.6 %copy-start.1 = (bf16[512,256]{1,0:T(8,128)(2,1)S(1)}, bf16[512,256]{1,0:T(8,128)(2,1)}, u32[]{:S(2)}) copy-start(bf16[512,256]{1,0:T(8,128)(2,1)} %refs_1_.3) | copy-start | bytes 786436
  1.3 1.9 %copy-start.2 = (bf16[2,1024,256]{2,1,0:T(8,128)(2,1)S(1)}, bf16[2,1024,256]{2,1,0:T(8,128)(2,1)}, u32[]{:S(2)}) copy-start(bf16[2,1024,256]{2,1,0:T(8,128)(2,1)} %refs_4_.3) | copy-start | bytes 3145732
  1.3 2.1 %copy-start.3 = (bf16[768,512]{1,0:T(8,128)(2,1)S(1)}, bf16[768,512]{1,0:T(8,128)(2,1)}, u32[]{:S(2)}) copy-start(bf16[768,512]{1,0:T(8,128)(2,1)} %refs_0_.1) | copy-start | bytes 2359300
  1.4 2.1 %copy-start.4 = (s32[1,2,384]{2,1,0:T(2,128)S(1)}, s32[1,2,384]{2,1,0:T(2,128)}, u32[]{:S(2)}) copy-start(s32[1,2,384]{2,1,0:T(2,128)} %param.7) | copy-start | bytes 9220
  1.4 2.1 %copy-start.5 = (f32[512]{0:T(512)S(1)}, f32[512]{0:T(512)}, u32[]{:S(2)}) copy-start(f32[512]{0:T(512)} %param.9) | copy-start | bytes 6148
  1.4 5.7 %collective-permute-start = (bf16[2,512]{1,0:T(2,128)(2,1)S(1)}, bf16[2,512]{1,0:T(2,128)(2,1)S(1)}, u32[]{:S(2)}, u32[]{:S(2)}) collective-permute-start(bf16[2,512]{1,0:T(2,128)(2,1)S(1)} %shard_map.109), channel_id=1, source_target_pairs={{0,1},{1,2},{2,3},{4,5},{5,6},{6,7},{8,9},{9,10},{10,11},{12,13},{... | collective-permute-start | bytes 6152 | tf_op jit(solution)/shard_map/ppermute | solution.py:473
  7.8 2.5 %collective-permute-start.1 = (bf16[3360,128]{1,0:T(8,128)(2,1)S(1)}, bf16[3360,128]{1,0:T(8,128)(2,1)S(1)}, u32[]{:S(2)}, u32[]{:S(2)}) collective-permute-start(bf16[3360,128]{1,0:T(8,128)(2,1)S(1)} %get-tuple-element.68.refs_5_), channel_id=1, source_target_pairs={{0,4},{1,5},{2,6},{3,7},{4,0},{5,1},{6,2},{7,3},{8,12},{9,13},{10,... | collective-permute-start | bytes 2580488 | tf_op jit(solution)/shard_map/ppermute | solution.py:484
  10.4 7.2 %collective-permute-start.3 = (bf16[1312,128]{1,0:T(8,128)(2,1)S(1)}, bf16[1312,128]{1,0:T(8,128)(2,1)S(1)}, u32[]{:S(2)}, u32[]{:S(2)}) collective-permute-start(bf16[1312,128]{1,0:T(8,128)(2,1)S(1)} %get-tuple-element.75.refs_3_), channel_id=1, source_target_pairs={{0,16},{1,17},{2,18},{3,19},{4,12},{5,13},{6,14},{7,15},{8,24},{9,... | collective-permute-start | bytes 1007624 | tf_op jit(solution)/shard_map/ppermute | solution.py:484
  12.4 9.4 %collective-permute-start.2 = (bf16[544,256]{1,0:T(8,128)(2,1)S(1)}, bf16[544,256]{1,0:T(8,128)(2,1)S(1)}, u32[]{:S(2)}, u32[]{:S(2)}) collective-permute-start(bf16[544,256]{1,0:T(8,128)(2,1)S(1)} %shard_map.115.refs_1_), channel_id=1, source_target_pairs={{0,1},{1,0},{2,3},{3,2},{4,6},{5,7},{6,4},{7,5},{8,9},{9,8},{10,11... | collective-permute-start | bytes 835592 | tf_op jit(solution)/shard_map/ppermute | solution.py:484
  17.7 5.8 %collective-permute-start.5 = (bf16[800,128]{1,0:T(8,128)(2,1)S(1)}, bf16[800,128]{1,0:T(8,128)(2,1)S(1)}, u32[]{:S(2)}, u32[]{:S(2)}) collective-permute-start(bf16[800,128]{1,0:T(8,128)(2,1)S(1)} %get-tuple-element.78.refs_3_), channel_id=1, source_target_pairs={{0,8},{1,9},{2,10},{3,11},{4,20},{5,21},{6,22},{7,23},{8,0},{9,1},... | collective-permute-start | bytes 614408 | tf_op jit(solution)/shard_map/ppermute | solution.py:484
  21.9 8.6 %collective-permute-start.4 = (bf16[272,256]{1,0:T(8,128)(2,1)S(1)}, bf16[272,256]{1,0:T(8,128)(2,1)S(1)}, u32[]{:S(2)}, u32[]{:S(2)}) collective-permute-start(bf16[272,256]{1,0:T(8,128)(2,1)S(1)} %get-tuple-element.79.refs_3_), channel_id=1, source_target_pairs={{0,2},{1,3},{2,0},{3,1},{4,5},{5,4},{6,7},{7,6},{8,10},{9,11},{10,... | collective-permute-start | bytes 417800 | tf_op jit(solution)/shard_map/ppermute | solution.py:484
  23.7 8.8 %collective-permute-start.7 = (bf16[544,128]{1,0:T(8,128)(2,1)S(1)}, bf16[544,128]{1,0:T(8,128)(2,1)S(1)}, u32[]{:S(2)}, u32[]{:S(2)}) collective-permute-start(bf16[544,128]{1,0:T(8,128)(2,1)S(1)} %get-tuple-element.84.refs_3_), channel_id=1, source_target_pairs={{0,2},{1,3},{2,0},{3,1},{4,5},{5,4},{6,7},{7,6},{8,10},{9,11},{10,... | collective-permute-start | bytes 417800 | tf_op jit(solution)/shard_map/ppermute | solution.py:484
  30.6 6.5 %collective-permute-start.6 = (bf16[272,256]{1,0:T(8,128)(2,1)S(1)}, bf16[272,256]{1,0:T(8,128)(2,1)S(1)}, u32[]{:S(2)}, u32[]{:S(2)}) collective-permute-start(bf16[272,256]{1,0:T(8,128)(2,1)S(1)} %get-tuple-element.86.refs_3_), channel_id=1, source_target_pairs={{0,16},{1,17},{2,18},{3,19},{4,12},{5,13},{6,14},{7,15},{8,24},{9,... | collective-permute-start | bytes 417800 | tf_op jit(solution)/shard_map/ppermute | solution.py:484
  32.6 9.7 %collective-permute-start.8 = (bf16[560,128]{1,0:T(8,128)(2,1)S(1)}, bf16[560,128]{1,0:T(8,128)(2,1)S(1)}, u32[]{:S(2)}, u32[]{:S(2)}) collective-permute-start(bf16[560,128]{1,0:T(8,128)(2,1)S(1)} %get-tuple-element.90.refs_2_), channel_id=1, source_target_pairs={{0,1},{1,0},{2,3},{3,2},{4,6},{5,7},{6,4},{7,5},{8,9},{9,8},{10,11... | collective-permute-start | bytes 430088 | tf_op jit(solution)/shard_map/ppermute | solution.py:484
  37.1 5.1 %collective-permute-start.9 = (bf16[272,256]{1,0:T(8,128)(2,1)S(1)}, bf16[272,256]{1,0:T(8,128)(2,1)S(1)}, u32[]{:S(2)}, u32[]{:S(2)}) collective-permute-start(bf16[272,256]{1,0:T(8,128)(2,1)S(1)} %get-tuple-element.91.refs_3_), channel_id=1, source_target_pairs={{0,8},{1,9},{2,10},{3,11},{4,20},{5,21},{6,22},{7,23},{8,0},{9,1},... | collective-permute-start | bytes 417800 | tf_op jit(solution)/shard_map/ppermute | solution.py:484
  42.4 5.2 %collective-permute-start.10 = (bf16[832,128]{1,0:T(8,128)(2,1)S(1)}, bf16[832,128]{1,0:T(8,128)(2,1)S(1)}, u32[]{:S(2)}, u32[]{:S(2)}) collective-permute-start(bf16[832,128]{1,0:T(8,128)(2,1)S(1)} %get-tuple-element.100.refs_0_), channel_id=1, source_target_pairs={{0,4},{1,5},{2,6},{3,7},{4,0},{5,1},{6,2},{7,3},{8,12},{9,13},{10,... | collective-permute-start | bytes 638984 | tf_op jit(solution)/shard_map/ppermute | solution.py:484
  42.5 3.7 %collective-permute-start.12 = (bf16[256,128]{1,0:T(8,128)(2,1)S(1)}, bf16[256,128]{1,0:T(8,128)(2,1)S(1)}, u32[]{:S(2)}, u32[]{:S(2)}) collective-permute-start(bf16[256,128]{1,0:T(8,128)(2,1)S(1)} %get-tuple-element.98.refs_2_.refs_1_), channel_id=1, source_target_pairs={{0,20},{1,21},{2,22},{3,23},{4,8},{5,9},{6,10},{7,11},{8,28},{9,29... | collective-permute-start | bytes 196616 | tf_op jit(solution)/shard_map/ppermute | solution.py:495
  42.5 5.0 %collective-permute-start.11 = (bf16[256,128]{1,0:T(8,128)(2,1)S(1)}, bf16[256,128]{1,0:T(8,128)(2,1)S(1)}, u32[]{:S(2)}, u32[]{:S(2)}) collective-permute-start(bf16[256,128]{1,0:T(8,128)(2,1)S(1)} %get-tuple-element.98.refs_2_.refs_1_), channel_id=1, source_target_pairs={{0,16},{1,17},{2,18},{3,19},{4,12},{5,13},{6,14},{7,15},{8,24},{9,... | collective-permute-start | bytes 196616 | tf_op jit(solution)/shard_map/ppermute | solution.py:484

commit v23 on v20

--- a/solution.py
+++ b/solution.py
@@ -142,7 +142,7 @@
 
 
 def local_kernel(plan, info, feats, weight, bias, codes, books, proj,
-                 unfold, hidden, latent_grad, flipped, own, send, first, part, wide, chosen):
+                 unfold, hidden, latent_grad, flipped, own, send_sums, first, part, wide, chosen):
     rows, channels = feats.shape
     frames = rows // 2
     dz = proj.shape[1]
@@ -172,15 +172,15 @@
     digits = [code_digits(codes[level:level + 1, :], dz, code_rows) for level in range(2)]
     own[0:frames, :] = jnp.where(bit == 1, once, latent).astype(BF16)
     own[frames:, :] = jnp.where(bit == 1, digits[1], digits[0])
-    put_columns(send, at, rows_b, jnp.where(bit == 1, latent, once).astype(BF16))
-    put_columns(send, at + frames, rows_b, jnp.where(bit == 1, digits[0], digits[1]))
+    put_columns(send_sums, 0, rows_b, jnp.where(bit == 1, latent, once).astype(BF16))
+    put_columns(send_sums, frames, rows_b, jnp.where(bit == 1, digits[0], digits[1]))
     for level in range(levels):
         part[at + level * 16 * (dz // LANES):at + (level + 1) * 16 * (dz // LANES), :] = jnp.concatenate(
             [chosen[level, 0:16, j * LANES:(j + 1) * LANES].astype(F32) for j in range(dz // LANES)], 0)
 
 
-def frame_kernel(plan, info, halo, first, part, weight, proj, unfold_in, hidden_in, grad_in, flipped_in, own_in, send_in,
-                 unfold, hidden, latent_grad, flipped, own, send):
+def frame_kernel(plan, info, halo, first, part, weight, proj, unfold_in, hidden_in, grad_in, flipped_in, own_in, sums_in,
+                 unfold, hidden, latent_grad, flipped, own, send_sums, send):
     width = unfold.shape[1]
     half = width // 2
     dz = proj.shape[1]
@@ -216,7 +216,7 @@
         at += count // 2 if halved else count
     rows_b = own.shape[0]
     own[0:16, :] = jnp.where(bit == 1, once, latent).astype(BF16)
-    put_columns(send, at * dz, rows_b, jnp.where(bit == 1, latent, once).astype(BF16))
+    put_columns(send_sums, 0, rows_b, jnp.where(bit == 1, latent, once).astype(BF16))
 
 
 def rest_kernel(plan, info, flipped, unfold, hidden, latent_grad, proj, keep_a, keep_c, hidden_grad, extras, row):
@@ -593,16 +593,16 @@
     rows_b = frames + code_rows
     shared = [shape((frames, width), BF16), shape((frames, channels), BF16), shape((frames, dz), BF16),
               shape((dz, frames), BF16), shape((rows_b, dz), BF16),
-              shape((corr_rows + rows_b * (dz // LANES), LANES), BF16)]
+              shape((rows_b * (dz // LANES), LANES), BF16)]
     *arrays, first, part = call(
         functools.partial(local_kernel, plan),
         shared + [shape((16, channels), F32), shape((corr_rows + 32 * (dz // LANES), LANES), F32)],
         [info, feats, weight, conv_bias[None, :], codes, codebooks, proj],
         scratch=[VMEM((channels // LANES, rows_in + 8, LANES), F32), VMEM((levels, frames, dz), BF16)],
     )
-    unfold, hidden, latent_grad, flipped, own, send = call(
+    unfold, hidden, latent_grad, flipped, own, send_sums, send = call(
         functools.partial(frame_kernel, plan),
-        shared,
+        shared + [shape((corr_rows, LANES), BF16)],
         [info, halo, first, part, weight, proj] + arrays,
         aliases={6 + k: k for k in range(len(shared))},
     )
@@ -624,7 +624,7 @@
 
     size = per_shard + 16
     sums_rows = size * (tm // 2)
-    got_core = got
+    got_core = swapped(send_sums, exchanges[0])
 
     def own_sums(first, after):
         return call(
@@ -635,7 +635,7 @@
 
     def both_sums(first, base, dtype, after):
         return call(
-            functools.partial(sums_kernel, corr_rows, frames, at_codes + first, per_shard),
+            functools.partial(sums_kernel, 0, frames, at_codes + first, per_shard),
             shape((sums_rows, dz), dtype),
             [info, got_core, base, row],
             after=after)

time: 48.7 us -> 48.4 us (level)
  waiting for transfers between devices: 25.6 us -> 24.8 us
  starting transfers between devices: 10.9 us -> 11.4 us
    ppermute x11 -> x12, waiting for transfers between devices: 23.6 us -> 22.8 us  [swapped(): return lax.ppermute(block, ('dp', 'tm'), route)]
    ppermute x11 -> x12, starting transfers between devices: 9.29 us -> 9.8 us  [swapped(): return lax.ppermute(block, ('dp', 'tm'), route)]
  transfers between devices with their start and end apart: 13 -> 14, of which waited for: 11 -> 11; matrix products, arithmetic and copies ran while one was open for 0% -> 0% of each run, Pallas kernels for 17% -> 17%
where the time goes in v23:
time: 48.4 us; the launch traced here: 48.2 us
  waiting for transfers between devices  24.8 us (51%)
  starting transfers between devices  11.4 us (24%)
  Pallas kernels  9.93 us (21%)
  local copies, waits for them, and re-layouts  1.25 us (3%)
  between operations  0.82 us (2%)
    ppermute x12, waiting for transfers between devices, swapped(): return lax.ppermute(block, ('dp', 'tm'), route)  22.8 us
    pallas_call x19, Pallas kernels, call(): pl.pallas_call(kernel, out_shape=shown, in_specs=specs, out_specs=[pl.Blo...  9.93 us
    ppermute x12, starting transfers between devices, swapped(): return lax.ppermute(block, ('dp', 'tm'), route)  9.8 us
    ppermute x1, starting transfers between devices, shifted(): return lax.ppermute(block, axis, route)  1.56 us
    ppermute x1, waiting for transfers between devices, shifted(): return lax.ppermute(block, axis, route)  1.32 us
  transfers between devices with their start and end apart: 14, of which 11 were waited for; matrix products, arithmetic and copies ran while one was open for 0% of the time, Pallas kernels for 17%

profile of v23, /device:TPU:24, one launch (start us, length us, event | category | flops | bytes accessed | tf_op | source)
XLA Modules:
  0.0 48.2 jit_solution(16815120950486091023)
XLA Ops:
  0.6 0.7 %slice.3.refs_0_ = bf16[2,512]{1,0:T(2,128)(2,1)S(1)} slice(bf16[768,512]{1,0:T(8,128)(2,1)} %refs_0_.1), slice={[766:768], [0:512]} | slice | bytes 4096 | tf_op jit(solution)/shard_map/slice | solution.py:588
  1.4 1.6 %collective-permute-start = (bf16[2,512]{1,0:T(2,128)(2,1)S(1)}, bf16[2,512]{1,0:T(2,128)(2,1)S(1)}, u32[]{:S(2)}, u32[]{:S(2)}) collective-permute-start(bf16[2,512]{1,0:T(2,128)(2,1)S(1)} %shard_map.109), channel_id=1, source_target_pairs={{0,1},{1,2},{2,3},{4,5},{5,6},{6,7},{8,9},{9,10},{10,11},{12,13},{... | collective-permute-start | bytes 6152 | tf_op jit(solution)/shard_map/ppermute | solution.py:473
  3.0 0.3 copy-done.2
  3.5 2.3 %shard_map.110 = (bf16[384,2048]{1,0:T(8,128)(2,1)S(1)}, bf16[384,512]{1,0:T(8,128)(2,1)S(1)}, bf16[384,256]{1,0:T(8,128)(2,1)S(1)}, bf16[256,384]{1,0:T(8,128)(...) custom-call(bf16[768,512]{1,0:T(8,128)(2,1)S(1)} %copy-done.3, ...), custom_call_target="tpu_custom_call" | custom-call | tf_op jit(solution)/shard_map/pallas_call | solution.py:47
  5.8 1.3 %collective-permute-done.refs_0_ = bf16[2,512]{1,0:T(2,128)(2,1)S(1)} collective-permute-done((bf16[2,512]{1,0:T(2,128)(2,1)S(1)}, bf16[2,512]{1,0:T(2,128)(2,1)S(1)}, u32[]{:S(2)}, u32[]{:S(2)}) %collective-permute-start) | collective-permute-done | bytes 2080 | tf_op jit(solution)/shard_map/ppermute | solution.py:473
  7.1 0.7 %shard_map.111 = (bf16[384,2048]{1,0:T(8,128)(2,1)S(1)}, bf16[384,512]{1,0:T(8,128)(2,1)S(1)}, bf16[384,256]{1,0:T(8,128)(2,1)S(1)}, bf16[256,384]{1,0:T(8,128)(...) custom-call(bf16[2,512]{1,0:T(2,128)(2,1)S(1)} %collective-permute-d, ...), custom_call_target="tpu_custom_call", output_to_operand_aliasing={{0}: (5, {}), {1}: (6, {}), {2}: (7, {}), {3}: (8, {}), {4}... | custom-call | tf_op jit(solution)/shard_map/pallas_call | solution.py:47
  7.9 0.5 %collective-permute-start.1 = (bf16[800,128]{1,0:T(8,128)(2,1)S(1)}, bf16[800,128]{1,0:T(8,128)(2,1)S(1)}, u32[]{:S(2)}, u32[]{:S(2)}) collective-permute-start(bf16[800,128]{1,0:T(8,128)(2,1)S(1)} %get-tuple-element.71), channel_id=1, source_target_pairs={{0,4},{1,5},{2,6},{3,7},{4,0},{5,1},{6,2},{7,3},{8,12},{9,13},{10,... | collective-permute-start | bytes 614408 | tf_op jit(solution)/shard_map/ppermute | solution.py:484
  8.4 0.6 %shard_map.112 = (f32[2048,128]{1,0:T(8,128)S(1)}, f32[512,128]{1,0:T(8,128)S(1)}, bf16[384,512]{1,0:T(8,128)(2,1)S(1)}, f32[32,128]{1,0:T(8,128)S(1)}, bf16[16,512]{1,0:T(8,128)(2,1)S(1)}) custom-call(bf16[256,384]{1,0:T(8,128)(2,1)S(1)} %get-tuple-element.65.refs_0_, bf16[384,2048]{1,0:T(8,128)(2,1)S(1)} %get-tuple-element.66.refs_1_, ...), custom_call_target="tpu_custom_call" | custom-call | tf_op jit(solution)/shard_map/pallas_call | solution.py:47
  9.0 0.4 shard_map.113.refs_4_.refs_1_
  9.5 0.5 %collective-permute-done.2.refs_0_ = bf16[2560,128]{1,0:T(8,128)(2,1)S(1)} collective-permute-done((bf16[2560,128]{1,0:T(8,128)(2,1)S(1)}, bf16[2560,128]{1,0:T(8,128)(2,1)S(1)}, u32[]{:S(2)}, u32[]{:S(2)}) %collective-permute-start.2) | collective-permute-done | bytes 655392 | tf_op jit(solution)/shard_map/ppermute | solution.py:484
  10.1 1.6 %collective-permute-start.4 = (bf16[1312,128]{1,0:T(8,128)(2,1)S(1)}, bf16[1312,128]{1,0:T(8,128)(2,1)S(1)}, u32[]{:S(2)}, u32[]{:S(2)}) collective-permute-start(bf16[1312,128]{1,0:T(8,128)(2,1)S(1)} %get-tuple-element.77.refs_3_), channel_id=1, source_target_pairs={{0,8},{1,9},{2,10},{3,11},{4,20},{5,21},{6,22},{7,23},{8,0},{9,1},... | collective-permute-start | bytes 1007624 | tf_op jit(solution)/shard_map/ppermute | solution.py:484
  11.7 0.4 shard_map.115.refs_1_
  12.1 0.9 %collective-permute-start.3 = (bf16[544,256]{1,0:T(8,128)(2,1)S(1)}, bf16[544,256]{1,0:T(8,128)(2,1)S(1)}, u32[]{:S(2)}, u32[]{:S(2)}) collective-permute-start(bf16[544,256]{1,0:T(8,128)(2,1)S(1)} %shard_map.115.refs_1_), channel_id=1, source_target_pairs={{0,1},{1,0},{2,3},{3,2},{4,6},{5,7},{6,4},{7,5},{8,9},{9,8},{10,11... | collective-permute-start | bytes 835592 | tf_op jit(solution)/shard_map/ppermute | solution.py:484
  13.0 0.4 shard_map.116.refs_1_
  13.4 0.4 shard_map.117.refs_3_.refs_1_
  13.8 3.5 %collective-permute-done.4.refs_0_ = bf16[1312,128]{1,0:T(8,128)(2,1)S(1)} collective-permute-done((bf16[1312,128]{1,0:T(8,128)(2,1)S(1)}, bf16[1312,128]{1,0:T(8,128)(2,1)S(1)}, u32[]{:S(2)}, u32[]{:S(2)}) %collective-permute-start.4) | collective-permute-done | bytes 335904 | tf_op jit(solution)/shard_map/ppermute | solution.py:484
  17.4 1.6 %collective-permute-start.6 = (bf16[800,128]{1,0:T(8,128)(2,1)S(1)}, bf16[800,128]{1,0:T(8,128)(2,1)S(1)}, u32[]{:S(2)}, u32[]{:S(2)}) collective-permute-start(bf16[800,128]{1,0:T(8,128)(2,1)S(1)} %get-tuple-element.80.refs_3_), channel_id=1, source_target_pairs={{0,16},{1,17},{2,18},{3,19},{4,12},{5,13},{6,14},{7,15},{8,24},{9,... | collective-permute-start | bytes 614408 | tf_op jit(solution)/shard_map/ppermute | solution.py:484
  19.0 2.5 %collective-permute-done.3.refs_0_ = bf16[544,256]{1,0:T(8,128)(2,1)S(1)} collective-permute-done((bf16[544,256]{1,0:T(8,128)(2,1)S(1)}, bf16[544,256]{1,0:T(8,128)(2,1)S(1)}, u32[]{:S(2)}, u32[]{:S(2)}) %collective-permute-start.3) | collective-permute-done | bytes 278560 | tf_op jit(solution)/shard_map/ppermute | solution.py:484
  21.6 0.9 %collective-permute-start.5 = (bf16[272,256]{1,0:T(8,128)(2,1)S(1)}, bf16[272,256]{1,0:T(8,128)(2,1)S(1)}, u32[]{:S(2)}, u32[]{:S(2)}) collective-permute-start(bf16[272,256]{1,0:T(8,128)(2,1)S(1)} %get-tuple-element.81.refs_3_), channel_id=1, source_target_pairs={{0,2},{1,3},{2,0},{3,1},{4,5},{5,4},{6,7},{7,6},{8,10},{9,11},{10,... | collective-permute-start | bytes 417800 | tf_op jit(solution)/shard_map/ppermute | solution.py:484
  22.5 0.7 %collective-permute-done.6.refs_0_ = bf16[800,128]{1,0:T(8,128)(2,1)S(1)} collective-permute-done((bf16[800,128]{1,0:T(8,128)(2,1)S(1)}, bf16[800,128]{1,0:T(8,128)(2,1)S(1)}, u32[]{:S(2)}, u32[]{:S(2)}) %collective-permute-start.6) | collective-permute-done | bytes 204832 | tf_op jit(solution)/shard_map/ppermute | solution.py:484
  23.4 1.4 %collective-permute-start.8 = (bf16[544,128]{1,0:T(8,128)(2,1)S(1)}, bf16[544,128]{1,0:T(8,128)(2,1)S(1)}, u32[]{:S(2)}, u32[]{:S(2)}) collective-permute-start(bf16[544,128]{1,0:T(8,128)(2,1)S(1)} %get-tuple-element.86.refs_3_), channel_id=1, source_target_pairs={{0,2},{1,3},{2,0},{3,1},{4,5},{5,4},{6,7},{7,6},{8,10},{9,11},{10,... | collective-permute-start | bytes 417800 | tf_op jit(solution)/shard_map/ppermute | solution.py:484
  24.8 5.5 %collective-permute-done.5.refs_0_ = bf16[272,256]{1,0:T(8,128)(2,1)S(1)} collective-permute-done((bf16[272,256]{1,0:T(8,128)(2,1)S(1)}, bf16[272,256]{1,0:T(8,128)(2,1)S(1)}, u32[]{:S(2)}, u32[]{:S(2)}) %collective-permute-start.5) | collective-permute-done | bytes 139296 | tf_op jit(solution)/shard_map/ppermute | solution.py:484
  30.4 2.0 %collective-permute-done.8.refs_0_ = bf16[544,128]{1,0:T(8,128)(2,1)S(1)} collective-permute-done((bf16[544,128]{1,0:T(8,128)(2,1)S(1)}, bf16[544,128]{1,0:T(8,128)(2,1)S(1)}, u32[]{:S(2)}, u32[]{:S(2)}) %collective-permute-start.8) | collective-permute-done | bytes 139296 | tf_op jit(solution)/shard_map/ppermute | solution.py:484
  32.5 4.2 %collective-permute-done.7.refs_0_ = bf16[272,256]{1,0:T(8,128)(2,1)S(1)} collective-permute-done((bf16[272,256]{1,0:T(8,128)(2,1)S(1)}, bf16[272,256]{1,0:T(8,128)(2,1)S(1)}, u32[]{:S(2)}, u32[]{:S(2)}) %collective-permute-start.7) | collective-permute-done | bytes 139296 | tf_op jit(solution)/shard_map/ppermute | solution.py:484
  36.8 0.6 %collective-permute-start.10 = (bf16[272,256]{1,0:T(8,128)(2,1)S(1)}, bf16[272,256]{1,0:T(8,128)(2,1)S(1)}, u32[]{:S(2)}, u32[]{:S(2)}) collective-permute-start(bf16[272,256]{1,0:T(8,128)(2,1)S(1)} %get-tuple-element.93.refs_3_), channel_id=1, source_target_pairs={{0,16},{1,17},{2,18},{3,19},{4,12},{5,13},{6,14},{7,15},{8,24},{9,... | collective-permute-start | bytes 417800 | tf_op jit(solution)/shard_map/ppermute | solution.py:484
  37.3 2.0 %shard_map.124 = (bf16[768,512]{1,0:T(8,128)(2,1)}, f32[8,128]{1,0:T(8,128)S(1)}) custom-call(bf16[384,512]{1,0:T(8,128)(2,1)S(1)} %get-tuple-element.70.refs_0_, bf16[16,512]{1,0:T(8,128)(2,1)S(1)} %get-tuple-element.87.refs_1_, bf16[2048,512]{1,0:T(8,128)(2,1)S(1)} %copy-done, bf16[272,256]{1,0:T(8,128)(2,1)S(1)} %get-tuple-element.93.refs_3_), custom_call_target="tpu_custom_call" | custom-call | tf_op jit(solution)/shard_map/pallas_call | solution.py:47
  39.4 2.5 %collective-permute-done.10.refs_3_ = bf16[272,256]{1,0:T(8,128)(2,1)S(1)} collective-permute-done((bf16[272,256]{1,0:T(8,128)(2,1)S(1)}, bf16[272,256]{1,0:T(8,128)(2,1)S(1)}, u32[]{:S(2)}, u32[]{:S(2)}) %collective-permute-start.10) | collective-permute-done | bytes 139296 | tf_op jit(solution)/shard_map/ppermute | solution.py:484
  42.2 2.1 %collective-permute-start.12 = (bf16[256,128]{1,0:T(8,128)(2,1)S(1)}, bf16[256,128]{1,0:T(8,128)(2,1)S(1)}, u32[]{:S(2)}, u32[]{:S(2)}) collective-permute-start(bf16[256,128]{1,0:T(8,128)(2,1)S(1)} %get-tuple-element.100.refs_2_.refs_1_), channel_id=1, source_target_pairs={{0,8},{1,9},{2,10},{3,11},{4,20},{5,21},{6,22},{7,23},{8,0},{9,1},... | collective-permute-start | bytes 196616 | tf_op jit(solution)/shard_map/ppermute | solution.py:484
  44.3 1.0 %shard_map.126 = (f32[64,512]{1,0:T(8,128)}, f32[8,128]{1,0:T(8,128)S(1)}) custom-call(f32[256,128]{1,0:T(8,128)S(1)} %get-tuple-element.99.refs_0_, bf16[512,256]{1,0:T(8,128)(2,1)S(1)} %copy-done.1, bf16[256,128]{1,0:T(8,128)(2,1)S(1)} %get-tuple-element.100.refs_2_.refs_1_), custom_call_target="tpu_custom_call" | custom-call | tf_op jit(solution)/shard_map/pallas_call | solution.py:47
  45.2 0.6 %collective-permute-done.13.refs_4_ = bf16[256,128]{1,0:T(8,128)(2,1)S(1)} collective-permute-done((bf16[256,128]{1,0:T(8,128)(2,1)S(1)}, bf16[256,128]{1,0:T(8,128)(2,1)S(1)}, u32[]{:S(2)}, u32[]{:S(2)}) %collective-permute-start.13) | collective-permute-done | bytes 65568 | tf_op jit(solution)/shard_map/ppermute | solution.py:495
  45.9 1.3 %collective-permute-done.12.refs_3_ = bf16[256,128]{1,0:T(8,128)(2,1)S(1)} collective-permute-done((bf16[256,128]{1,0:T(8,128)(2,1)S(1)}, bf16[256,128]{1,0:T(8,128)(2,1)S(1)}, u32[]{:S(2)}, u32[]{:S(2)}) %collective-permute-start.12) | collective-permute-done | bytes 65568 | tf_op jit(solution)/shard_map/ppermute | solution.py:484
  47.2 1.0 %shard_map.127 = (f32[512,256]{1,0:T(8,128)}, f32[1,512]{1,0:T(1,128)}, bf16[2,256,256]{2,1,0:T(8,128)(2,1)}, f32[2,256]{1,0:T(2,128)}) custom-call(bf16[832,128]{1,0:T(8,128)(2,1)S(1)} %get-tuple-element.102.refs_0_, bf16[256,128]{1,0:T(8,128)(2,1)S(1)} %get-tuple-element.100.refs_2_.refs_1_, bf16[832,128]{1,0:T(8,128)(2,1)S(1)} %collective-permute-done.11.refs_2_, ...), custom_call_target="tpu_custom_call" | custom-call | tf_op jit(solution)/shard_map/pallas_call | solution.py:47
  (28 shorter events, 1.3 us)
Async XLA Ops:
  1.3 1.6 %copy-start = (bf16[2048,512]{1,0:T(8,128)(2,1)S(1)}, bf16[2048,512]{1,0:T(8,128)(2,1)}, u32[]{:S(2)}) copy-start(bf16[2048,512]{1,0:T(8,128)(2,1)} %refs_2_.1) | copy-start | bytes 6291460
  1.3 1.6 %copy-start.1 = (bf16[512,256]{1,0:T(8,128)(2,1)S(1)}, bf16[512,256]{1,0:T(8,128)(2,1)}, u32[]{:S(2)}) copy-start(bf16[512,256]{1,0:T(8,128)(2,1)} %refs_1_.3) | copy-start | bytes 786436
  1.3 1.9 %copy-start.2 = (bf16[2,1024,256]{2,1,0:T(8,128)(2,1)S(1)}, bf16[2,1024,256]{2,1,0:T(8,128)(2,1)}, u32[]{:S(2)}) copy-start(bf16[2,1024,256]{2,1,0:T(8,128)(2,1)} %refs_4_.3) | copy-start | bytes 3145732
  1.3 2.1 %copy-start.3 = (bf16[768,512]{1,0:T(8,128)(2,1)S(1)}, bf16[768,512]{1,0:T(8,128)(2,1)}, u32[]{:S(2)}) copy-start(bf16[768,512]{1,0:T(8,128)(2,1)} %refs_0_.1) | copy-start | bytes 2359300
  1.4 2.1 %copy-start.4 = (s32[1,2,384]{2,1,0:T(2,128)S(1)}, s32[1,2,384]{2,1,0:T(2,128)}, u32[]{:S(2)}) copy-start(s32[1,2,384]{2,1,0:T(2,128)} %param.7) | copy-start | bytes 9220
  1.4 2.1 %copy-start.5 = (f32[512]{0:T(512)S(1)}, f32[512]{0:T(512)}, u32[]{:S(2)}) copy-start(f32[512]{0:T(512)} %param.9) | copy-start | bytes 6148
  1.4 5.7 %collective-permute-start = (bf16[2,512]{1,0:T(2,128)(2,1)S(1)}, bf16[2,512]{1,0:T(2,128)(2,1)S(1)}, u32[]{:S(2)}, u32[]{:S(2)}) collective-permute-start(bf16[2,512]{1,0:T(2,128)(2,1)S(1)} %shard_map.109), channel_id=1, source_target_pairs={{0,1},{1,2},{2,3},{4,5},{5,6},{6,7},{8,9},{9,10},{10,11},{12,13},{... | collective-permute-start | bytes 6152 | tf_op jit(solution)/shard_map/ppermute | solution.py:473
  7.8 2.2 %collective-permute-start.2 = (bf16[2560,128]{1,0:T(8,128)(2,1)S(1)}, bf16[2560,128]{1,0:T(8,128)(2,1)S(1)}, u32[]{:S(2)}, u32[]{:S(2)}) collective-permute-start(bf16[2560,128]{1,0:T(8,128)(2,1)S(1)} %get-tuple-element.69.refs_5_), channel_id=1, source_target_pairs={{0,4},{1,5},{2,6},{3,7},{4,0},{5,1},{6,2},{7,3},{8,12},{9,13},{10,... | collective-permute-start | bytes 1966088 | tf_op jit(solution)/shard_map/ppermute | solution.py:484
  7.9 3.8 %collective-permute-start.1 = (bf16[800,128]{1,0:T(8,128)(2,1)S(1)}, bf16[800,128]{1,0:T(8,128)(2,1)S(1)}, u32[]{:S(2)}, u32[]{:S(2)}) collective-permute-start(bf16[800,128]{1,0:T(8,128)(2,1)S(1)} %get-tuple-element.71), channel_id=1, source_target_pairs={{0,4},{1,5},{2,6},{3,7},{4,0},{5,1},{6,2},{7,3},{8,12},{9,13},{10,... | collective-permute-start | bytes 614408 | tf_op jit(solution)/shard_map/ppermute | solution.py:484
  10.1 7.2 %collective-permute-start.4 = (bf16[1312,128]{1,0:T(8,128)(2,1)S(1)}, bf16[1312,128]{1,0:T(8,128)(2,1)S(1)}, u32[]{:S(2)}, u32[]{:S(2)}) collective-permute-start(bf16[1312,128]{1,0:T(8,128)(2,1)S(1)} %get-tuple-element.77.refs_3_), channel_id=1, source_target_pairs={{0,8},{1,9},{2,10},{3,11},{4,20},{5,21},{6,22},{7,23},{8,0},{9,1},... | collective-permute-start | bytes 1007624 | tf_op jit(solution)/shard_map/ppermute | solution.py:484
  12.1 9.4 %collective-permute-start.3 = (bf16[544,256]{1,0:T(8,128)(2,1)S(1)}, bf16[544,256]{1,0:T(8,128)(2,1)S(1)}, u32[]{:S(2)}, u32[]{:S(2)}) collective-permute-start(bf16[544,256]{1,0:T(8,128)(2,1)S(1)} %shard_map.115.refs_1_), channel_id=1, source_target_pairs={{0,1},{1,0},{2,3},{3,2},{4,6},{5,7},{6,4},{7,5},{8,9},{9,8},{10,11... | collective-permute-start | bytes 835592 | tf_op jit(solution)/shard_map/ppermute | solution.py:484
  17.4 5.8 %collective-permute-start.6 = (bf16[800,128]{1,0:T(8,128)(2,1)S(1)}, bf16[800,128]{1,0:T(8,128)(2,1)S(1)}, u32[]{:S(2)}, u32[]{:S(2)}) collective-permute-start(bf16[800,128]{1,0:T(8,128)(2,1)S(1)} %get-tuple-element.80.refs_3_), channel_id=1, source_target_pairs={{0,16},{1,17},{2,18},{3,19},{4,12},{5,13},{6,14},{7,15},{8,24},{9,... | collective-permute-start | bytes 614408 | tf_op jit(solution)/shard_map/ppermute | solution.py:484
  21.6 8.7 %collective-permute-start.5 = (bf16[272,256]{1,0:T(8,128)(2,1)S(1)}, bf16[272,256]{1,0:T(8,128)(2,1)S(1)}, u32[]{:S(2)}, u32[]{:S(2)}) collective-permute-start(bf16[272,256]{1,0:T(8,128)(2,1)S(1)} %get-tuple-element.81.refs_3_), channel_id=1, source_target_pairs={{0,2},{1,3},{2,0},{3,1},{4,5},{5,4},{6,7},{7,6},{8,10},{9,11},{10,... | collective-permute-start | bytes 417800 | tf_op jit(solution)/shard_map/ppermute | solution.py:484
  23.4 9.0 %collective-permute-start.8 = (bf16[544,128]{1,0:T(8,128)(2,1)S(1)}, bf16[544,128]{1,0:T(8,128)(2,1)S(1)}, u32[]{:S(2)}, u32[]{:S(2)}) collective-permute-start(bf16[544,128]{1,0:T(8,128)(2,1)S(1)} %get-tuple-element.86.refs_3_), channel_id=1, source_target_pairs={{0,2},{1,3},{2,0},{3,1},{4,5},{5,4},{6,7},{7,6},{8,10},{9,11},{10,... | collective-permute-start | bytes 417800 | tf_op jit(solution)/shard_map/ppermute | solution.py:484
  30.3 6.4 %collective-permute-start.7 = (bf16[272,256]{1,0:T(8,128)(2,1)S(1)}, bf16[272,256]{1,0:T(8,128)(2,1)S(1)}, u32[]{:S(2)}, u32[]{:S(2)}) collective-permute-start(bf16[272,256]{1,0:T(8,128)(2,1)S(1)} %get-tuple-element.88.refs_3_), channel_id=1, source_target_pairs={{0,8},{1,9},{2,10},{3,11},{4,20},{5,21},{6,22},{7,23},{8,0},{9,1},... | collective-permute-start | bytes 417800 | tf_op jit(solution)/shard_map/ppermute | solution.py:484
  32.4 9.5 %collective-permute-start.9 = (bf16[560,128]{1,0:T(8,128)(2,1)S(1)}, bf16[560,128]{1,0:T(8,128)(2,1)S(1)}, u32[]{:S(2)}, u32[]{:S(2)}) collective-permute-start(bf16[560,128]{1,0:T(8,128)(2,1)S(1)} %get-tuple-element.92.refs_2_), channel_id=1, source_target_pairs={{0,1},{1,0},{2,3},{3,2},{4,6},{5,7},{6,4},{7,5},{8,9},{9,8},{10,11... | collective-permute-start | bytes 430088 | tf_op jit(solution)/shard_map/ppermute | solution.py:484
  36.8 5.1 %collective-permute-start.10 = (bf16[272,256]{1,0:T(8,128)(2,1)S(1)}, bf16[272,256]{1,0:T(8,128)(2,1)S(1)}, u32[]{:S(2)}, u32[]{:S(2)}) collective-permute-start(bf16[272,256]{1,0:T(8,128)(2,1)S(1)} %get-tuple-element.93.refs_3_), channel_id=1, source_target_pairs={{0,16},{1,17},{2,18},{3,19},{4,12},{5,13},{6,14},{7,15},{8,24},{9,... | collective-permute-start | bytes 417800 | tf_op jit(solution)/shard_map/ppermute | solution.py:484
  42.0 5.2 %collective-permute-start.11 = (bf16[832,128]{1,0:T(8,128)(2,1)S(1)}, bf16[832,128]{1,0:T(8,128)(2,1)S(1)}, u32[]{:S(2)}, u32[]{:S(2)}) collective-permute-start(bf16[832,128]{1,0:T(8,128)(2,1)S(1)} %get-tuple-element.102.refs_0_), channel_id=1, source_target_pairs={{0,4},{1,5},{2,6},{3,7},{4,0},{5,1},{6,2},{7,3},{8,12},{9,13},{10,... | collective-permute-start | bytes 638984 | tf_op jit(solution)/shard_map/ppermute | solution.py:484
  42.1 3.7 %collective-permute-start.13 = (bf16[256,128]{1,0:T(8,128)(2,1)S(1)}, bf16[256,128]{1,0:T(8,128)(2,1)S(1)}, u32[]{:S(2)}, u32[]{:S(2)}) collective-permute-start(bf16[256,128]{1,0:T(8,128)(2,1)S(1)} %get-tuple-element.100.refs_2_.refs_1_), channel_id=1, source_target_pairs={{0,12},{1,13},{2,14},{3,15},{4,16},{5,17},{6,18},{7,19},{8,4},{9,5... | collective-permute-start | bytes 196616 | tf_op jit(solution)/shard_map/ppermute | solution.py:495
  42.2 5.0 %collective-permute-start.12 = (bf16[256,128]{1,0:T(8,128)(2,1)S(1)}, bf16[256,128]{1,0:T(8,128)(2,1)S(1)}, u32[]{:S(2)}, u32[]{:S(2)}) collective-permute-start(bf16[256,128]{1,0:T(8,128)(2,1)S(1)} %get-tuple-element.100.refs_2_.refs_1_), channel_id=1, source_target_pairs={{0,8},{1,9},{2,10},{3,11},{4,20},{5,21},{6,22},{7,23},{8,0},{9,1},... | collective-permute-start | bytes 196616 | tf_op jit(solution)/shard_map/ppermute | solution.py:484

commit v24 on v23

--- a/solution.py
+++ b/solution.py
@@ -438,9 +438,7 @@
         out[...] = taken
 
 
-def out_kernel(total_frames, use_scale, dz, place, inner, extra, info, mine, *refs):
-    parts, (out, bias, means, usage) = refs[:-4], refs[-4:]
-    theirs = parts[1]
+def means_out_kernel(total_frames, use_scale, dz, inner, extra, info, mine, theirs, bias, means, usage):
     scale = 1.0 / total_frames
     top = inner * dz
     value = add_digits(mine[top:top + extra, :].astype(F32), theirs[top:top + extra, :].astype(F32)) * scale
@@ -460,6 +458,11 @@
         numbers.append(count_of(whole[count:, :].astype(F32), count) * use_scale)
     usage[0:1, :] = jnp.where(bit == 1, numbers[1], numbers[0])
     usage[1:2, :] = jnp.where(bit == 1, numbers[0], numbers[1])
+
+
+def proj_out_kernel(total_frames, dz, place, inner, info, *refs):
+    parts, out = refs[:-1], refs[-1]
+    scale = 1.0 / total_frames
     for j, ref in enumerate(parts):
         for k in range(inner):
             start = pl.multiple_of((info[place + j] + k) * LANES, LANES)
@@ -700,11 +703,17 @@
         token=True,
         scratch=[VMEM((LANES, channels), F32)],
     )
-    proj_grad, bias_grad, code_means, code_usage = call(
-        functools.partial(out_kernel, total_frames, book_size / total_frames, dz, at_pieces, now_c, extra),
-        [shape((channels, dz), F32), shape((1, channels), F32), shape((levels, per_shard, dz), BF16),
-         shape((levels, per_shard), F32)],
-        [info, mine] + parts,
+    bias_grad, code_means, code_usage, last = call(
+        functools.partial(means_out_kernel, total_frames, book_size / total_frames, dz, now_c, extra),
+        [shape((1, channels), F32), shape((levels, per_shard, dz), BF16), shape((levels, per_shard), F32)],
+        [info, mine, parts[1]],
+        after=[last],
+        token=True,
+    )
+    proj_grad = call(
+        functools.partial(proj_out_kernel, total_frames, dz, at_pieces, now_c),
+        shape((channels, dz), F32),
+        [info] + parts,
         after=[last],
     )
     return feat_grad, conv_grad, bias_grad[0], proj_grad, code_means, code_usage

time: 48.4 us -> 48.4 us (level)
  waiting for transfers between devices: 24.8 us -> 24 us
  Pallas kernels: 9.93 us -> 10.6 us
    pallas_call x19 -> x20, Pallas kernels: 9.93 us -> 10.6 us  [call(): pl.pallas_call(kernel, out_shape=shown, in_specs=specs, out_specs=[pl.Blo...]
    ppermute x1, waiting for transfers between devices: 0.63 us -> 0.01 us  [crossed(): return lax.ppermute(block, ('dp', 'tm'), route)]
  transfers between devices with their start and end apart: 14 -> 14, of which waited for: 11 -> 10; matrix products, arithmetic and copies ran while one was open for 0% -> 0% of each run, Pallas kernels for 17% -> 18%
where the time goes in v24:
time: 48.4 us; the launch traced here: 48.1 us
  waiting for transfers between devices  24 us (50%)
  starting transfers between devices  11.4 us (24%)
  Pallas kernels  10.6 us (22%)
  local copies, waits for them, and re-layouts  1.25 us (3%)
  between operations  0.82 us (2%)
    ppermute x12, waiting for transfers between devices, swapped(): return lax.ppermute(block, ('dp', 'tm'), route)  22.7 us
    pallas_call x20, Pallas kernels, call(): pl.pallas_call(kernel, out_shape=shown, in_specs=specs, out_specs=[pl.Blo...  10.6 us
    ppermute x12, starting transfers between devices, swapped(): return lax.ppermute(block, ('dp', 'tm'), route)  9.8 us
    ppermute x1, starting transfers between devices, shifted(): return lax.ppermute(block, axis, route)  1.56 us
    ppermute x1, waiting for transfers between devices, shifted(): return lax.ppermute(block, axis, route)  1.32 us
  transfers between devices with their start and end apart: 14, of which 10 were waited for; matrix products, arithmetic and copies ran while one was open for 0% of the time, Pallas kernels for 18%

profile of v24, /device:TPU:24, one launch (start us, length us, event | category | flops | bytes accessed | tf_op | source)
XLA Modules:
  0.0 48.1 jit_solution(1003840082244462177)
XLA Ops:
  0.6 0.7 %slice.3.refs_0_ = bf16[2,512]{1,0:T(2,128)(2,1)S(1)} slice(bf16[768,512]{1,0:T(8,128)(2,1)} %refs_0_.1), slice={[766:768], [0:512]} | slice | bytes 4096 | tf_op jit(solution)/shard_map/slice | solution.py:591
  1.4 1.6 %collective-permute-start = (bf16[2,512]{1,0:T(2,128)(2,1)S(1)}, bf16[2,512]{1,0:T(2,128)(2,1)S(1)}, u32[]{:S(2)}, u32[]{:S(2)}) collective-permute-start(bf16[2,512]{1,0:T(2,128)(2,1)S(1)} %shard_map.109), channel_id=1, source_target_pairs={{0,1},{1,2},{2,3},{4,5},{5,6},{6,7},{8,9},{9,10},{10,11},{12,13},{... | collective-permute-start | bytes 6152 | tf_op jit(solution)/shard_map/ppermute | solution.py:476
  3.0 0.3 copy-done.2
  3.5 2.3 %shard_map.110 = (bf16[384,2048]{1,0:T(8,128)(2,1)S(1)}, bf16[384,512]{1,0:T(8,128)(2,1)S(1)}, bf16[384,256]{1,0:T(8,128)(2,1)S(1)}, bf16[256,384]{1,0:T(8,128)(...) custom-call(bf16[768,512]{1,0:T(8,128)(2,1)S(1)} %copy-done.3, ...), custom_call_target="tpu_custom_call" | custom-call | tf_op jit(solution)/shard_map/pallas_call | solution.py:47
  5.8 1.3 %collective-permute-done.refs_0_ = bf16[2,512]{1,0:T(2,128)(2,1)S(1)} collective-permute-done((bf16[2,512]{1,0:T(2,128)(2,1)S(1)}, bf16[2,512]{1,0:T(2,128)(2,1)S(1)}, u32[]{:S(2)}, u32[]{:S(2)}) %collective-permute-start) | collective-permute-done | bytes 2080 | tf_op jit(solution)/shard_map/ppermute | solution.py:476
  7.1 0.7 %shard_map.111 = (bf16[384,2048]{1,0:T(8,128)(2,1)S(1)}, bf16[384,512]{1,0:T(8,128)(2,1)S(1)}, bf16[384,256]{1,0:T(8,128)(2,1)S(1)}, bf16[256,384]{1,0:T(8,128)(...) custom-call(bf16[2,512]{1,0:T(2,128)(2,1)S(1)} %collective-permute-d, ...), custom_call_target="tpu_custom_call", output_to_operand_aliasing={{0}: (5, {}), {1}: (6, {}), {2}: (7, {}), {3}: (8, {}), {4}... | custom-call | tf_op jit(solution)/shard_map/pallas_call | solution.py:47
  7.9 0.5 %collective-permute-start.1 = (bf16[800,128]{1,0:T(8,128)(2,1)S(1)}, bf16[800,128]{1,0:T(8,128)(2,1)S(1)}, u32[]{:S(2)}, u32[]{:S(2)}) collective-permute-start(bf16[800,128]{1,0:T(8,128)(2,1)S(1)} %get-tuple-element.71), channel_id=1, source_target_pairs={{0,4},{1,5},{2,6},{3,7},{4,0},{5,1},{6,2},{7,3},{8,12},{9,13},{10,... | collective-permute-start | bytes 614408 | tf_op jit(solution)/shard_map/ppermute | solution.py:487
  8.4 0.6 %shard_map.112 = (f32[2048,128]{1,0:T(8,128)S(1)}, f32[512,128]{1,0:T(8,128)S(1)}, bf16[384,512]{1,0:T(8,128)(2,1)S(1)}, f32[32,128]{1,0:T(8,128)S(1)}, bf16[16,512]{1,0:T(8,128)(2,1)S(1)}) custom-call(bf16[256,384]{1,0:T(8,128)(2,1)S(1)} %get-tuple-element.65.refs_0_, bf16[384,2048]{1,0:T(8,128)(2,1)S(1)} %get-tuple-element.66.refs_1_, ...), custom_call_target="tpu_custom_call" | custom-call | tf_op jit(solution)/shard_map/pallas_call | solution.py:47
  9.0 0.4 shard_map.113.refs_4_.refs_1_
  9.5 0.5 %collective-permute-done.2.refs_0_ = bf16[2560,128]{1,0:T(8,128)(2,1)S(1)} collective-permute-done((bf16[2560,128]{1,0:T(8,128)(2,1)S(1)}, bf16[2560,128]{1,0:T(8,128)(2,1)S(1)}, u32[]{:S(2)}, u32[]{:S(2)}) %collective-permute-start.2) | collective-permute-done | bytes 655392 | tf_op jit(solution)/shard_map/ppermute | solution.py:487
  10.1 1.6 %collective-permute-start.4 = (bf16[1312,128]{1,0:T(8,128)(2,1)S(1)}, bf16[1312,128]{1,0:T(8,128)(2,1)S(1)}, u32[]{:S(2)}, u32[]{:S(2)}) collective-permute-start(bf16[1312,128]{1,0:T(8,128)(2,1)S(1)} %get-tuple-element.77.refs_3_), channel_id=1, source_target_pairs={{0,8},{1,9},{2,10},{3,11},{4,20},{5,21},{6,22},{7,23},{8,0},{9,1},... | collective-permute-start | bytes 1007624 | tf_op jit(solution)/shard_map/ppermute | solution.py:487
  11.7 0.4 shard_map.115.refs_1_
  12.1 0.9 %collective-permute-start.3 = (bf16[544,256]{1,0:T(8,128)(2,1)S(1)}, bf16[544,256]{1,0:T(8,128)(2,1)S(1)}, u32[]{:S(2)}, u32[]{:S(2)}) collective-permute-start(bf16[544,256]{1,0:T(8,128)(2,1)S(1)} %shard_map.115.refs_1_), channel_id=1, source_target_pairs={{0,1},{1,0},{2,3},{3,2},{4,6},{5,7},{6,4},{7,5},{8,9},{9,8},{10,11... | collective-permute-start | bytes 835592 | tf_op jit(solution)/shard_map/ppermute | solution.py:487
  13.0 0.4 shard_map.116.refs_1_
  13.4 0.4 shard_map.117.refs_3_.refs_1_
  13.8 3.5 %collective-permute-done.4.refs_0_ = bf16[1312,128]{1,0:T(8,128)(2,1)S(1)} collective-permute-done((bf16[1312,128]{1,0:T(8,128)(2,1)S(1)}, bf16[1312,128]{1,0:T(8,128)(2,1)S(1)}, u32[]{:S(2)}, u32[]{:S(2)}) %collective-permute-start.4) | collective-permute-done | bytes 335904 | tf_op jit(solution)/shard_map/ppermute | solution.py:487
  17.4 1.6 %collective-permute-start.6 = (bf16[800,128]{1,0:T(8,128)(2,1)S(1)}, bf16[800,128]{1,0:T(8,128)(2,1)S(1)}, u32[]{:S(2)}, u32[]{:S(2)}) collective-permute-start(bf16[800,128]{1,0:T(8,128)(2,1)S(1)} %get-tuple-element.80.refs_3_), channel_id=1, source_target_pairs={{0,16},{1,17},{2,18},{3,19},{4,12},{5,13},{6,14},{7,15},{8,24},{9,... | collective-permute-start | bytes 614408 | tf_op jit(solution)/shard_map/ppermute | solution.py:487
  19.0 2.5 %collective-permute-done.3.refs_0_ = bf16[544,256]{1,0:T(8,128)(2,1)S(1)} collective-permute-done((bf16[544,256]{1,0:T(8,128)(2,1)S(1)}, bf16[544,256]{1,0:T(8,128)(2,1)S(1)}, u32[]{:S(2)}, u32[]{:S(2)}) %collective-permute-start.3) | collective-permute-done | bytes 278560 | tf_op jit(solution)/shard_map/ppermute | solution.py:487
  21.6 0.9 %collective-permute-start.5 = (bf16[272,256]{1,0:T(8,128)(2,1)S(1)}, bf16[272,256]{1,0:T(8,128)(2,1)S(1)}, u32[]{:S(2)}, u32[]{:S(2)}) collective-permute-start(bf16[272,256]{1,0:T(8,128)(2,1)S(1)} %get-tuple-element.81.refs_3_), channel_id=1, source_target_pairs={{0,2},{1,3},{2,0},{3,1},{4,5},{5,4},{6,7},{7,6},{8,10},{9,11},{10,... | collective-permute-start | bytes 417800 | tf_op jit(solution)/shard_map/ppermute | solution.py:487
  22.5 0.7 %collective-permute-done.6.refs_0_ = bf16[800,128]{1,0:T(8,128)(2,1)S(1)} collective-permute-done((bf16[800,128]{1,0:T(8,128)(2,1)S(1)}, bf16[800,128]{1,0:T(8,128)(2,1)S(1)}, u32[]{:S(2)}, u32[]{:S(2)}) %collective-permute-start.6) | collective-permute-done | bytes 204832 | tf_op jit(solution)/shard_map/ppermute | solution.py:487
  23.4 1.4 %collective-permute-start.8 = (bf16[544,128]{1,0:T(8,128)(2,1)S(1)}, bf16[544,128]{1,0:T(8,128)(2,1)S(1)}, u32[]{:S(2)}, u32[]{:S(2)}) collective-permute-start(bf16[544,128]{1,0:T(8,128)(2,1)S(1)} %get-tuple-element.86.refs_3_), channel_id=1, source_target_pairs={{0,2},{1,3},{2,0},{3,1},{4,5},{5,4},{6,7},{7,6},{8,10},{9,11},{10,... | collective-permute-start | bytes 417800 | tf_op jit(solution)/shard_map/ppermute | solution.py:487
  24.8 5.5 %collective-permute-done.5.refs_0_ = bf16[272,256]{1,0:T(8,128)(2,1)S(1)} collective-permute-done((bf16[272,256]{1,0:T(8,128)(2,1)S(1)}, bf16[272,256]{1,0:T(8,128)(2,1)S(1)}, u32[]{:S(2)}, u32[]{:S(2)}) %collective-permute-start.5) | collective-permute-done | bytes 139296 | tf_op jit(solution)/shard_map/ppermute | solution.py:487
  30.4 2.0 %collective-permute-done.8.refs_0_ = bf16[544,128]{1,0:T(8,128)(2,1)S(1)} collective-permute-done((bf16[544,128]{1,0:T(8,128)(2,1)S(1)}, bf16[544,128]{1,0:T(8,128)(2,1)S(1)}, u32[]{:S(2)}, u32[]{:S(2)}) %collective-permute-start.8) | collective-permute-done | bytes 139296 | tf_op jit(solution)/shard_map/ppermute | solution.py:487
  32.5 4.2 %collective-permute-done.7.refs_0_ = bf16[272,256]{1,0:T(8,128)(2,1)S(1)} collective-permute-done((bf16[272,256]{1,0:T(8,128)(2,1)S(1)}, bf16[272,256]{1,0:T(8,128)(2,1)S(1)}, u32[]{:S(2)}, u32[]{:S(2)}) %collective-permute-start.7) | collective-permute-done | bytes 139296 | tf_op jit(solution)/shard_map/ppermute | solution.py:487
  36.8 0.6 %collective-permute-start.10 = (bf16[272,256]{1,0:T(8,128)(2,1)S(1)}, bf16[272,256]{1,0:T(8,128)(2,1)S(1)}, u32[]{:S(2)}, u32[]{:S(2)}) collective-permute-start(bf16[272,256]{1,0:T(8,128)(2,1)S(1)} %get-tuple-element.93.refs_3_), channel_id=1, source_target_pairs={{0,16},{1,17},{2,18},{3,19},{4,12},{5,13},{6,14},{7,15},{8,24},{9,... | collective-permute-start | bytes 417800 | tf_op jit(solution)/shard_map/ppermute | solution.py:487
  37.3 2.0 %shard_map.124 = (bf16[768,512]{1,0:T(8,128)(2,1)}, f32[8,128]{1,0:T(8,128)S(1)}) custom-call(bf16[384,512]{1,0:T(8,128)(2,1)S(1)} %get-tuple-element.70.refs_0_, bf16[16,512]{1,0:T(8,128)(2,1)S(1)} %get-tuple-element.87.refs_1_, bf16[2048,512]{1,0:T(8,128)(2,1)S(1)} %copy-done, bf16[272,256]{1,0:T(8,128)(2,1)S(1)} %get-tuple-element.93.refs_3_), custom_call_target="tpu_custom_call" | custom-call | tf_op jit(solution)/shard_map/pallas_call | solution.py:47
  39.4 2.5 %collective-permute-done.10.refs_3_ = bf16[272,256]{1,0:T(8,128)(2,1)S(1)} collective-permute-done((bf16[272,256]{1,0:T(8,128)(2,1)S(1)}, bf16[272,256]{1,0:T(8,128)(2,1)S(1)}, u32[]{:S(2)}, u32[]{:S(2)}) %collective-permute-start.10) | collective-permute-done | bytes 139296 | tf_op jit(solution)/shard_map/ppermute | solution.py:487
  42.2 2.1 %collective-permute-start.12 = (bf16[256,128]{1,0:T(8,128)(2,1)S(1)}, bf16[256,128]{1,0:T(8,128)(2,1)S(1)}, u32[]{:S(2)}, u32[]{:S(2)}) collective-permute-start(bf16[256,128]{1,0:T(8,128)(2,1)S(1)} %get-tuple-element.100.refs_2_.refs_0_), channel_id=1, source_target_pairs={{0,8},{1,9},{2,10},{3,11},{4,20},{5,21},{6,22},{7,23},{8,0},{9,1},... | collective-permute-start | bytes 196616 | tf_op jit(solution)/shard_map/ppermute | solution.py:487
  44.3 1.0 %shard_map.126 = (f32[64,512]{1,0:T(8,128)}, f32[8,128]{1,0:T(8,128)S(1)}) custom-call(f32[256,128]{1,0:T(8,128)S(1)} %get-tuple-element.99.refs_0_, bf16[512,256]{1,0:T(8,128)(2,1)S(1)} %copy-done.1, bf16[256,128]{1,0:T(8,128)(2,1)S(1)} %get-tuple-element.100.refs_2_.refs_0_), custom_call_target="tpu_custom_call" | custom-call | tf_op jit(solution)/shard_map/pallas_call | solution.py:47
  45.2 0.7 %shard_map.127 = (f32[1,512]{1,0:T(1,128)}, bf16[2,256,256]{2,1,0:T(8,128)(2,1)}, f32[2,256]{1,0:T(2,128)}, f32[8,128]{1,0:T(8,128)S(1)}) custom-call(bf16[832,128]{1,0:T(8,128)(2,1)S(1)} %get-tuple-element.102.refs_0_, bf16[832,128]{1,0:T(8,128)(2,1)S(1)} %collective-permute-done.11.refs_1_, f32[8,128]{1,0:T(8,128)S(1)} %get-tuple-element.103.refs_2_), custom_call_target="tpu_custom_call" | custom-call | tf_op jit(solution)/shard_map/pallas_call | solution.py:47
  46.0 1.2 %collective-permute-done.12.refs_2_ = bf16[256,128]{1,0:T(8,128)(2,1)S(1)} collective-permute-done((bf16[256,128]{1,0:T(8,128)(2,1)S(1)}, bf16[256,128]{1,0:T(8,128)(2,1)S(1)}, u32[]{:S(2)}, u32[]{:S(2)}) %collective-permute-start.12) | collective-permute-done | bytes 65568 | tf_op jit(solution)/shard_map/ppermute | solution.py:487
  47.2 0.9 %shard_map.128 = f32[512,256]{1,0:T(8,128)} custom-call(bf16[256,128]{1,0:T(8,128)(2,1)S(1)} %get-tuple-element.100.refs_2_.refs_0_, bf16[832,128]{1,0:T(8,128)(2,1)S(1)} %collective-permute-done.11.refs_1_, bf16[256,128]{1,0:T(8,128)(2,1)S(1)} %collective-permute-done.12.refs_2_, bf16[256,128]{1,0:T(8,128)(2,1)S(1)} %collective-permute-done.13.refs_3_, ...), custom_call_target="tpu_custom_call" | custom-call | tf_op jit(solution)/shard_map/pallas_call | solution.py:47
  (29 shorter events, 1.3 us)
Async XLA Ops:
  1.3 1.6 %copy-start = (bf16[2048,512]{1,0:T(8,128)(2,1)S(1)}, bf16[2048,512]{1,0:T(8,128)(2,1)}, u32[]{:S(2)}) copy-start(bf16[2048,512]{1,0:T(8,128)(2,1)} %refs_2_.1) | copy-start | bytes 6291460
  1.3 1.6 %copy-start.1 = (bf16[512,256]{1,0:T(8,128)(2,1)S(1)}, bf16[512,256]{1,0:T(8,128)(2,1)}, u32[]{:S(2)}) copy-start(bf16[512,256]{1,0:T(8,128)(2,1)} %refs_1_.3) | copy-start | bytes 786436
  1.3 1.9 %copy-start.2 = (bf16[2,1024,256]{2,1,0:T(8,128)(2,1)S(1)}, bf16[2,1024,256]{2,1,0:T(8,128)(2,1)}, u32[]{:S(2)}) copy-start(bf16[2,1024,256]{2,1,0:T(8,128)(2,1)} %refs_4_.3) | copy-start | bytes 3145732
  1.3 2.1 %copy-start.3 = (bf16[768,512]{1,0:T(8,128)(2,1)S(1)}, bf16[768,512]{1,0:T(8,128)(2,1)}, u32[]{:S(2)}) copy-start(bf16[768,512]{1,0:T(8,128)(2,1)} %refs_0_.1) | copy-start | bytes 2359300
  1.4 2.1 %copy-start.4 = (s32[1,2,384]{2,1,0:T(2,128)S(1)}, s32[1,2,384]{2,1,0:T(2,128)}, u32[]{:S(2)}) copy-start(s32[1,2,384]{2,1,0:T(2,128)} %param.7) | copy-start | bytes 9220
  1.4 2.1 %copy-start.5 = (f32[512]{0:T(512)S(1)}, f32[512]{0:T(512)}, u32[]{:S(2)}) copy-start(f32[512]{0:T(512)} %param.9) | copy-start | bytes 6148
  1.4 5.7 %collective-permute-start = (bf16[2,512]{1,0:T(2,128)(2,1)S(1)}, bf16[2,512]{1,0:T(2,128)(2,1)S(1)}, u32[]{:S(2)}, u32[]{:S(2)}) collective-permute-start(bf16[2,512]{1,0:T(2,128)(2,1)S(1)} %shard_map.109), channel_id=1, source_target_pairs={{0,1},{1,2},{2,3},{4,5},{5,6},{6,7},{8,9},{9,10},{10,11},{12,13},{... | collective-permute-start | bytes 6152 | tf_op jit(solution)/shard_map/ppermute | solution.py:476
  7.8 2.2 %collective-permute-start.2 = (bf16[2560,128]{1,0:T(8,128)(2,1)S(1)}, bf16[2560,128]{1,0:T(8,128)(2,1)S(1)}, u32[]{:S(2)}, u32[]{:S(2)}) collective-permute-start(bf16[2560,128]{1,0:T(8,128)(2,1)S(1)} %get-tuple-element.69.refs_5_), channel_id=1, source_target_pairs={{0,4},{1,5},{2,6},{3,7},{4,0},{5,1},{6,2},{7,3},{8,12},{9,13},{10,... | collective-permute-start | bytes 1966088 | tf_op jit(solution)/shard_map/ppermute | solution.py:487
  7.9 3.8 %collective-permute-start.1 = (bf16[800,128]{1,0:T(8,128)(2,1)S(1)}, bf16[800,128]{1,0:T(8,128)(2,1)S(1)}, u32[]{:S(2)}, u32[]{:S(2)}) collective-permute-start(bf16[800,128]{1,0:T(8,128)(2,1)S(1)} %get-tuple-element.71), channel_id=1, source_target_pairs={{0,4},{1,5},{2,6},{3,7},{4,0},{5,1},{6,2},{7,3},{8,12},{9,13},{10,... | collective-permute-start | bytes 614408 | tf_op jit(solution)/shard_map/ppermute | solution.py:487
  10.1 7.2 %collective-permute-start.4 = (bf16[1312,128]{1,0:T(8,128)(2,1)S(1)}, bf16[1312,128]{1,0:T(8,128)(2,1)S(1)}, u32[]{:S(2)}, u32[]{:S(2)}) collective-permute-start(bf16[1312,128]{1,0:T(8,128)(2,1)S(1)} %get-tuple-element.77.refs_3_), channel_id=1, source_target_pairs={{0,8},{1,9},{2,10},{3,11},{4,20},{5,21},{6,22},{7,23},{8,0},{9,1},... | collective-permute-start | bytes 1007624 | tf_op jit(solution)/shard_map/ppermute | solution.py:487
  12.1 9.4 %collective-permute-start.3 = (bf16[544,256]{1,0:T(8,128)(2,1)S(1)}, bf16[544,256]{1,0:T(8,128)(2,1)S(1)}, u32[]{:S(2)}, u32[]{:S(2)}) collective-permute-start(bf16[544,256]{1,0:T(8,128)(2,1)S(1)} %shard_map.115.refs_1_), channel_id=1, source_target_pairs={{0,1},{1,0},{2,3},{3,2},{4,6},{5,7},{6,4},{7,5},{8,9},{9,8},{10,11... | collective-permute-start | bytes 835592 | tf_op jit(solution)/shard_map/ppermute | solution.py:487
  17.4 5.8 %collective-permute-start.6 = (bf16[800,128]{1,0:T(8,128)(2,1)S(1)}, bf16[800,128]{1,0:T(8,128)(2,1)S(1)}, u32[]{:S(2)}, u32[]{:S(2)}) collective-permute-start(bf16[800,128]{1,0:T(8,128)(2,1)S(1)} %get-tuple-element.80.refs_3_), channel_id=1, source_target_pairs={{0,16},{1,17},{2,18},{3,19},{4,12},{5,13},{6,14},{7,15},{8,24},{9,... | collective-permute-start | bytes 614408 | tf_op jit(solution)/shard_map/ppermute | solution.py:487
  21.6 8.7 %collective-permute-start.5 = (bf16[272,256]{1,0:T(8,128)(2,1)S(1)}, bf16[272,256]{1,0:T(8,128)(2,1)S(1)}, u32[]{:S(2)}, u32[]{:S(2)}) collective-permute-start(bf16[272,256]{1,0:T(8,128)(2,1)S(1)} %get-tuple-element.81.refs_3_), channel_id=1, source_target_pairs={{0,2},{1,3},{2,0},{3,1},{4,5},{5,4},{6,7},{7,6},{8,10},{9,11},{10,... | collective-permute-start | bytes 417800 | tf_op jit(solution)/shard_map/ppermute | solution.py:487
  23.4 9.0 %collective-permute-start.8 = (bf16[544,128]{1,0:T(8,128)(2,1)S(1)}, bf16[544,128]{1,0:T(8,128)(2,1)S(1)}, u32[]{:S(2)}, u32[]{:S(2)}) collective-permute-start(bf16[544,128]{1,0:T(8,128)(2,1)S(1)} %get-tuple-element.86.refs_3_), channel_id=1, source_target_pairs={{0,2},{1,3},{2,0},{3,1},{4,5},{5,4},{6,7},{7,6},{8,10},{9,11},{10,... | collective-permute-start | bytes 417800 | tf_op jit(solution)/shard_map/ppermute | solution.py:487
  30.3 6.4 %collective-permute-start.7 = (bf16[272,256]{1,0:T(8,128)(2,1)S(1)}, bf16[272,256]{1,0:T(8,128)(2,1)S(1)}, u32[]{:S(2)}, u32[]{:S(2)}) collective-permute-start(bf16[272,256]{1,0:T(8,128)(2,1)S(1)} %get-tuple-element.88.refs_3_), channel_id=1, source_target_pairs={{0,8},{1,9},{2,10},{3,11},{4,20},{5,21},{6,22},{7,23},{8,0},{9,1},... | collective-permute-start | bytes 417800 | tf_op jit(solution)/shard_map/ppermute | solution.py:487
  32.4 9.5 %collective-permute-start.9 = (bf16[560,128]{1,0:T(8,128)(2,1)S(1)}, bf16[560,128]{1,0:T(8,128)(2,1)S(1)}, u32[]{:S(2)}, u32[]{:S(2)}) collective-permute-start(bf16[560,128]{1,0:T(8,128)(2,1)S(1)} %get-tuple-element.92.refs_2_), channel_id=1, source_target_pairs={{0,1},{1,0},{2,3},{3,2},{4,6},{5,7},{6,4},{7,5},{8,9},{9,8},{10,11... | collective-permute-start | bytes 430088 | tf_op jit(solution)/shard_map/ppermute | solution.py:487
  36.8 5.1 %collective-permute-start.10 = (bf16[272,256]{1,0:T(8,128)(2,1)S(1)}, bf16[272,256]{1,0:T(8,128)(2,1)S(1)}, u32[]{:S(2)}, u32[]{:S(2)}) collective-permute-start(bf16[272,256]{1,0:T(8,128)(2,1)S(1)} %get-tuple-element.93.refs_3_), channel_id=1, source_target_pairs={{0,16},{1,17},{2,18},{3,19},{4,12},{5,13},{6,14},{7,15},{8,24},{9,... | collective-permute-start | bytes 417800 | tf_op jit(solution)/shard_map/ppermute | solution.py:487
  42.0 3.2 %collective-permute-start.11 = (bf16[832,128]{1,0:T(8,128)(2,1)S(1)}, bf16[832,128]{1,0:T(8,128)(2,1)S(1)}, u32[]{:S(2)}, u32[]{:S(2)}) collective-permute-start(bf16[832,128]{1,0:T(8,128)(2,1)S(1)} %get-tuple-element.102.refs_0_), channel_id=1, source_target_pairs={{0,4},{1,5},{2,6},{3,7},{4,0},{5,1},{6,2},{7,3},{8,12},{9,13},{10,... | collective-permute-start | bytes 638984 | tf_op jit(solution)/shard_map/ppermute | solution.py:487
  42.1 3.9 %collective-permute-start.13 = (bf16[256,128]{1,0:T(8,128)(2,1)S(1)}, bf16[256,128]{1,0:T(8,128)(2,1)S(1)}, u32[]{:S(2)}, u32[]{:S(2)}) collective-permute-start(bf16[256,128]{1,0:T(8,128)(2,1)S(1)} %get-tuple-element.100.refs_2_.refs_0_), channel_id=1, source_target_pairs={{0,12},{1,13},{2,14},{3,15},{4,16},{5,17},{6,18},{7,19},{8,4},{9,5... | collective-permute-start | bytes 196616 | tf_op jit(solution)/shard_map/ppermute | solution.py:498
  42.2 5.0 %collective-permute-start.12 = (bf16[256,128]{1,0:T(8,128)(2,1)S(1)}, bf16[256,128]{1,0:T(8,128)(2,1)S(1)}, u32[]{:S(2)}, u32[]{:S(2)}) collective-permute-start(bf16[256,128]{1,0:T(8,128)(2,1)S(1)} %get-tuple-element.100.refs_2_.refs_0_), channel_id=1, source_target_pairs={{0,8},{1,9},{2,10},{3,11},{4,20},{5,21},{6,22},{7,23},{8,0},{9,1},... | collective-permute-start | bytes 196616 | tf_op jit(solution)/shard_map/ppermute | solution.py:487
